TPU v7x, 32 devices: a whole 2x2x4 slice. The times are simulated.
32 devices in a mesh: section: 8 (over z, core), rep: 4 (over y, x).
Axes of the slice: x: 2, y: 2, z: 4, core: 2. Of those that a mesh axis runs over, the one named last changes fastest.
Arguments:
- features: bfloat16 [4096, 256], P(('section', 'rep')), may hold values from -6 to 6
- adj_tiles: bfloat16 [32, 4, 4, 128, 128], P('section', 'rep'), may hold values from -0.125 to 0.125
- adj_src: int32 [32, 4, 4], P('section', 'rep'), may hold values from 0 to 7
- cotangent: bfloat16 [4096, 256], P(('section', 'rep')), may hold values from -1 to 1
- weight: bfloat16 [256, 256], replicated, may hold values from -0.375 to 0.375
- destination: int32 [4096, 1], P(('section', 'rep')), may hold values from 0 to 7; in each aligned block of 128 rows (0 to 127, 128 to 255, ...) at most 32 rows name the same one
Outputs:
- relaid: bfloat16 [8, 4, 8, 32, 256], P('section', 'rep')
- weight_grad: float32 [256, 256], replicated
Inputs may be any that keep to these rules, and one draw needn't show every extreme that they name: `destination`: from the rows of one device, at most 32 go to one section; some device sends exactly 32 to some section.
All inputs are finite; a program needn't handle non-finite values.
Results may differ from a plain program's by a relative error of at most 0.013.
Values may be sent and summed in bfloat16 or wider, within the bound.
No kernel may reach another device: no remote copies, remote signals or barrier semaphores. Data moves between devices by JAX's collectives and lax.ppermute only.
A program may use at most 64 MiB of HBM per device.

v0:
```python
import jax
import jax.numpy as jnp
from jax import lax
from jax.sharding import PartitionSpec as P


def dense_rows(agg, weight):
    agg_b = agg.astype(jnp.bfloat16)
    pre = jnp.dot(agg_b, weight, preferred_element_type=jnp.float32)
    sig = jax.nn.sigmoid(pre)
    output = (pre * sig).astype(jnp.bfloat16)
    factor = sig * (1.0 + pre * (1.0 - sig))
    return (agg_b, output, factor)


def per_device(features, adj_tiles, adj_src, cotangent, weight, destination):
    n_section = lax.axis_size("section")
    rows_here, width = features.shape
    tile = adj_tiles.shape[3]
    depth = adj_tiles.shape[2]
    tiles_local = adj_tiles[:, 0]
    sources = adj_src[:, 0]
    gathered = lax.all_gather(features, "section", axis=0, tiled=True)
    source_blocks = gathered.reshape(-1, tile, width)
    count = rows_here * lax.axis_size("rep")
    many = count // tile

    def one_slot(total, index):
        picked = jnp.take(source_blocks, sources[:, index], axis=0)
        part = jnp.einsum(
            "gab,gbf->gaf", tiles_local[:, index], picked, preferred_element_type=jnp.float32
        )
        return (total + part, None)

    start_total = jnp.zeros((many, tile, width), jnp.float32)
    total, _ = lax.scan(one_slot, start_total, jnp.arange(depth))
    agg = lax.psum_scatter(
        total.reshape(count, width).astype(jnp.bfloat16), "rep", scatter_dimension=0, tiled=True
    ).astype(jnp.float32)
    agg_b, output, factor = dense_rows(agg, weight)
    grad_pre = (cotangent.astype(jnp.float32) * factor).astype(jnp.bfloat16)
    grad_term = lax.dot_general(
        agg_b, grad_pre, (((0,), (0,)), ((), ())), preferred_element_type=jnp.float32
    )
    weight_grad = lax.psum(grad_term, ("section", "rep"))
    slots = max(2, 2 * rows_here // n_section)
    target = destination[:, 0]
    hits = (target[:, None] == jnp.arange(n_section, dtype=jnp.int32)[None, :]).astype(jnp.int32)
    before = jnp.cumsum(hits, axis=0) - hits
    slot = jnp.sum(before * hits, axis=1)
    position = target * slots + slot
    placing = (jnp.arange(n_section * slots, dtype=jnp.int32)[:, None] == position[None, :]).astype(
        jnp.bfloat16
    )
    packed = jnp.dot(placing, output, preferred_element_type=jnp.float32).astype(jnp.bfloat16)
    packed = packed.reshape(n_section, slots, width)
    received = lax.all_to_all(packed, "section", split_axis=0, concat_axis=0, tiled=True)
    relaid = received.reshape(1, 1, n_section, slots, width)
    return (relaid, weight_grad)


def solution(mesh):
    placed = (
        P(("section", "rep"), None),
        P("section", "rep", None, None, None),
        P("section", "rep", None),
        P(("section", "rep"), None),
        P(),
        P(("section", "rep"), None),
    )
    return jax.shard_map(
        per_device,
        mesh=mesh,
        in_specs=placed,
        out_specs=(P("section", "rep", None, None, None), P()),
        check_vma=False,
    )
```

profile of v0, /device:TPU:0, one launch (start us, length us, event | category | flops | bytes accessed | tf_op | source)
XLA Modules:
  0.0 213.9 jit_solution(12501231068709511164)
XLA Ops:
  7.2 0.0 copy-start
  7.2 0.0 reduce-scatter.2.cloned.1.call-start
  7.2 0.0 copy-start.2
  7.2 1.1 copy.11
  8.4 0.0 copy-done.2
  8.4 0.0 copy-start.5
  8.4 16.6 %all_gather.3 = bf16[1024,256]{1,0:T(8,128)(2,1)S(1)} all-gather(bf16[128,256]{1,0:T(8,128)(2,1)S(1)} %copy-done.2), channel_id=1, replica_groups=mesh['section'=8,'rep'=4] {'section'}, dimensions={0}, use_global_device_ids=true | all-gather | bytes 589824 | tf_op jit(solution)/shard_map/all_gather | solution.py:23
  25.0 0.0 copy-done.5
  25.0 0.1 copy.9
  25.1 14.3 %while.11 = (s32[]{:T(128)}, f32[4,128,256]{2,1,0:T(8,128)S(1)}, s32[4]{0:T(128)S(1)}, bf16[4,4,128,128]{3,2,0,1:T(8,128)(2,1)S(1)}, s32[4,4]{0,1:T(4,128)S(1)},...) while((s32[]{:T(128)}, f32[4,128,256]{2,1,0:T(8,128)S(1)}, ...), condition=%wide.region_3.4_spmd.clone, body=%wide.region_2.3_spmd.clone.sunk | while | flops 33948700 | bytes 1970913 | solution.py:36
  25.1 0.6 dynamic_slice.22
  27.6 0.6 gather_fusion
  28.2 0.4 convolution_add_fusion.2
  28.6 0.6 dynamic_slice.22
  31.2 0.6 gather_fusion
  31.8 0.4 convolution_add_fusion.2
  32.2 0.6 dynamic_slice.22
  34.8 0.6 gather_fusion
  35.4 0.4 convolution_add_fusion.2
  35.8 0.6 dynamic_slice.22
  38.4 0.6 gather_fusion
  38.9 0.4 convolution_add_fusion.2
  39.4 0.7 convert_element_type.25
  40.1 0.0 reduce-scatter.2.cloned.1.call-update
  40.1 0.0 copy-start.4
  40.1 0.6 copy-done.4
  40.8 0.1 fusion.11
  40.9 0.2 reduce_window_sum.11
  41.0 0.2 select_reduce_fusion
  41.2 24.2 %reduce-scatter.2.cloned.1.call-done = bf16[128,256]{1,0:T(8,128)(2,1)} async-done(((bf16[512,256]{1,0:T(8,128)(2,1)}), bf16[128,256]{1,0:T(8,128)(2,1)}) %reduce-scatter.2.cloned.1.call-update) | async-done | bytes 65552 | tf_op jit(solution)/shard_map/reduce_scatter | solution.py:37
  65.4 0.0 copy-done
  65.4 1.0 fusion.14
  66.4 0.9 convolution_convert_fusion
  67.3 0.0 copy-start.3
  67.3 0.0 copy-start.6
  67.3 4.7 %all-to-all-start = ((bf16[8,32,256]{2,1,0:T(8,128)(2,1)}), bf16[8,32,256]{2,1,0:T(8,128)(2,1)S(1)}, u32[]{:S(2)}, u32[]{:S(2)}) async-start(bf16[8,32,256]{2,1,0:T(8,128)(2,1)} %bitcast.5), calls=%async_computation.1 | async-start | bytes 262144 | tf_op jit(solution)/shard_map/all_to_all | solution.py:57
  72.0 0.0 all-reduce.2.cloned.1.call-start
  72.1 0.0 copy-done.3
  72.1 0.0 copy-done.6
  72.1 0.9 fusion.7
  73.0 0.0 all-reduce.2.cloned.1.call-update
  73.0 5.8 %all-to-all-done = bf16[8,32,256]{2,1,0:T(8,128)(2,1)S(1)} async-done(((bf16[8,32,256]{2,1,0:T(8,128)(2,1)}), bf16[8,32,256]{2,1,0:T(8,128)(2,1)S(1)}, u32[]{:S(2)}, u32[]{:S(2)}) %all-to-all-start) | async-done | bytes 131104 | tf_op jit(solution)/shard_map/all_to_all | solution.py:57
  78.8 126.5 %all-reduce.2.cloned.1.call-done = f32[256,256]{1,0:T(8,128)} async-done(((f32[256,256]{1,0:T(8,128)}), f32[256,256]{1,0:T(8,128)}) %all-reduce.2.cloned.1.call-update) | async-done | bytes 262160 | tf_op jit(solution)/shard_map/psum | solution.py:45
  205.4 0.0 copy-start.1
  205.4 0.7 copy.20
  206.0 0.3 copy-done.1
  206.3 0.7 copy.21
  (11 shorter events, 0.1 us)
Async XLA Ops:
  7.2 58.3 %copy-start = (bf16[256,256]{1,0:T(8,128)(2,1)S(1)}, bf16[256,256]{1,0:T(8,128)(2,1)}, u32[]{:S(2)}) copy-start(bf16[256,256]{1,0:T(8,128)(2,1)} %param.12) | copy-start | bytes 393220
  7.2 58.2 %reduce-scatter.2.cloned.1.call-start = ((), (), s32[]{:S(2)}) async-start(), calls=%async_computation.2 | async-start | bytes 327680 | tf_op jit(solution)/shard_map/reduce_scatter | solution.py:37
  7.2 1.1 copy-start.2
  8.4 16.6 %copy-start.5 = (s32[4,1,4]{2,1,0:T(1,128)S(1)}, s32[4,1,4]{2,1,0:T(1,128)}, u32[]{:S(2)}) copy-start(s32[4,1,4]{2,1,0:T(1,128)} %param.10) | copy-start | bytes 196
  40.1 0.7 copy-start.4
  67.3 4.8 %copy-start.3 = (bf16[128,256]{1,0:T(8,128)(2,1)S(1)}, bf16[128,256]{1,0:T(8,128)(2,1)}, u32[]{:S(2)}) copy-start(bf16[128,256]{1,0:T(8,128)(2,1)} %reduce-scatter.2.cloned.1.call-done) | copy-start | bytes 196612
  67.3 4.8 %copy-start.6 = (bf16[128,256]{1,0:T(8,128)(2,1)S(1)}, bf16[128,256]{1,0:T(8,128)(2,1)}, u32[]{:S(2)}) copy-start(bf16[128,256]{1,0:T(8,128)(2,1)} %param.11) | copy-start | bytes 196612
  67.3 11.5 %all-to-all-start = ((bf16[8,32,256]{2,1,0:T(8,128)(2,1)}), bf16[8,32,256]{2,1,0:T(8,128)(2,1)S(1)}, u32[]{:S(2)}, u32[]{:S(2)}) async-start(bf16[8,32,256]{2,1,0:T(8,128)(2,1)} %bitcast.5), calls=%async_computation.1 | async-start | bytes 262144 | tf_op jit(solution)/shard_map/all_to_all | solution.py:57
  72.0 133.3 %all-reduce.2.cloned.1.call-start = ((), (), s32[]{:S(2)}) async-start(), calls=%async_computation.3 | async-start | bytes 524288 | tf_op jit(solution)/shard_map/psum | solution.py:45
  205.4 1.0 copy-start.1
Sparse Core Ops, SparseCore 0:
  40.2 25.1 reduce-scatter.1
  79.8 125.4 all-reduce.1
where the time goes:
time: 214 us
  waiting for transfers between devices  157 us (73%)
  blocking collectives  16.6 us (8%)
  between operations  14.1 us (7%)
  local copies, waits for them, and re-layouts  8.18 us (4%)
  loops' own time  7.96 us (4%)
  starting transfers between devices  4.81 us (2%)
  matrix products  4.45 us (2%)
    psum x1, waiting for transfers between devices, per_device(): weight_grad = lax.psum(grad_term, ('section', 'rep'))  127 us
    reduce_scatter x1, waiting for transfers between devices, per_device(): lax.psum_scatter(total.reshape(count, width).astype(jnp.bfloat16), 'rep',...  24.2 us
    all_gather x1, blocking collectives, per_device(): gathered = lax.all_gather(features, 'section', axis=0, tiled=True)  16.6 us
    another operation x1, loops' own time, per_device(): total, _ = lax.scan(one_slot, start_total, jnp.arange(depth))  7.96 us
    all_to_all x1, waiting for transfers between devices, per_device(): lax.all_to_all(packed, 'section', split_axis=0, concat_axis=0, tiled=True)  5.77 us
    all_to_all x1, starting transfers between devices, per_device(): lax.all_to_all(packed, 'section', split_axis=0, concat_axis=0, tiled=True)  4.73 us
  transfers between devices with their start and end apart: 3, of which 3 were waited for; matrix products, arithmetic and copies ran while one was open for 1% of the time, Pallas kernels for 0%

commit v1 on v0

v1 whole, which is shorter than its diff:
```python
import functools

import jax
import jax.numpy as jnp
from jax import lax
from jax.experimental import pallas as pl
from jax.experimental.pallas import tpu as pltpu
from jax.sharding import PartitionSpec as P

VMEM = pl.BlockSpec(memory_space=pltpu.VMEM)
SMEM = pl.BlockSpec(memory_space=pltpu.SMEM)


def partials_kernel(src_ref, tiles_ref, blocks_ref, out_ref):
    many, depth = tiles_ref.shape[0], tiles_ref.shape[1]
    for g in range(many):
        left = jnp.concatenate([tiles_ref[g, k] for k in range(depth)], axis=1)
        right = jnp.concatenate([blocks_ref[src_ref[g, k]] for k in range(depth)], axis=0)
        out_ref[g] = jnp.dot(left, right, preferred_element_type=jnp.float32).astype(jnp.bfloat16)


def partials(sources, tiles, blocks):
    many, depth, tile, _ = tiles.shape
    width = blocks.shape[2]
    return pl.pallas_call(
        partials_kernel,
        out_shape=jax.ShapeDtypeStruct((many, tile, width), jnp.bfloat16),
        in_specs=[SMEM, VMEM, VMEM],
        out_specs=VMEM,
        compiler_params=pltpu.CompilerParams(vmem_limit_bytes=32 * 1024 * 1024),
        name="partials",
    )(sources, tiles, blocks)


def dense_kernel(slots, parts_ref, weight_ref, cot_ref, target_ref, packed_ref, grad_ref):
    rows = cot_ref.shape[0]
    places = packed_ref.shape[0]
    n_section = places // slots
    agg_b = jnp.sum(parts_ref[...].astype(jnp.float32), axis=0).astype(jnp.bfloat16)
    pre = jnp.dot(agg_b, weight_ref[...], preferred_element_type=jnp.float32)
    sig = jax.nn.sigmoid(pre)
    output = (pre * sig).astype(jnp.bfloat16)
    factor = sig * (1.0 + pre * (1.0 - sig))
    grad_pre = (cot_ref[...].astype(jnp.float32) * factor).astype(jnp.bfloat16)
    grad_ref[...] = lax.dot_general(
        agg_b, grad_pre, (((0,), (0,)), ((), ())), preferred_element_type=jnp.float32
    ).astype(grad_ref.dtype)
    target = target_ref[...]
    hits = lax.broadcasted_iota(jnp.int32, (n_section, rows), 0) == target
    hits_f = jnp.where(hits, 1.0, 0.0)
    earlier = lax.broadcasted_iota(jnp.int32, (rows, rows), 0) < lax.broadcasted_iota(
        jnp.int32, (rows, rows), 1
    )
    earlier = jnp.where(earlier, 1.0, 0.0).astype(jnp.bfloat16)
    before = jnp.dot(hits_f.astype(jnp.bfloat16), earlier, preferred_element_type=jnp.float32)
    slot = jnp.sum(before * hits_f, axis=0, keepdims=True).astype(jnp.int32)
    position = target * slots + slot
    placing = lax.broadcasted_iota(jnp.int32, (places, rows), 0) == position
    placing = jnp.where(placing, 1.0, 0.0).astype(jnp.bfloat16)
    packed_ref[...] = jnp.dot(placing, output, preferred_element_type=jnp.float32).astype(
        jnp.bfloat16
    )


def dense(parts, weight, cotangent, target, places, slots):
    width = weight.shape[0]
    return pl.pallas_call(
        functools.partial(dense_kernel, slots),
        out_shape=(
            jax.ShapeDtypeStruct((places, width), jnp.bfloat16),
            jax.ShapeDtypeStruct((width, width), jnp.float32),
        ),
        in_specs=[VMEM] * 4,
        out_specs=(VMEM, VMEM),
        compiler_params=pltpu.CompilerParams(vmem_limit_bytes=32 * 1024 * 1024),
        name="dense",
    )(parts, weight, cotangent, target)


def per_device(features, adj_tiles, adj_src, cotangent, weight, destination):
    n_section, n_rep = lax.axis_size("section"), lax.axis_size("rep")
    both = ("section", "rep")
    devices = n_section * n_rep
    rows_here, width = features.shape
    tile = adj_tiles.shape[3]
    gathered = lax.all_gather(features, "section", axis=0, tiled=True)
    blocks = gathered.reshape(-1, tile, width)
    part = partials(adj_src[:, 0], adj_tiles[:, 0], blocks)
    parts = part.reshape(n_rep, rows_here, width)
    parts = lax.all_to_all(parts, "rep", split_axis=0, concat_axis=0, tiled=True)
    slots = max(2, 2 * rows_here // n_section)
    target = destination.reshape(1, rows_here)
    packed, grad = dense(parts, weight, cotangent, target, n_section * slots, slots)
    packed = packed.reshape(n_section, slots, width)
    received = lax.all_to_all(packed, "section", split_axis=0, concat_axis=0, tiled=True)
    relaid = received.reshape(1, 1, n_section, slots, width)
    chunks = grad.reshape(devices, width * width // devices)
    if width % devices == 0:
        chunks = grad.reshape(devices, width // devices, width)
    terms = lax.all_to_all(chunks, both, split_axis=0, concat_axis=0, tiled=True)
    mine = jnp.sum(terms, axis=0, keepdims=True)
    spread = jnp.broadcast_to(mine, chunks.shape)
    weight_grad = lax.all_to_all(spread, both, split_axis=0, concat_axis=0, tiled=True)
    return (relaid, weight_grad.reshape(width, width))


def solution(mesh):
    placed = (
        P(("section", "rep"), None),
        P("section", "rep", None, None, None),
        P("section", "rep", None),
        P(("section", "rep"), None),
        P(),
        P(("section", "rep"), None),
    )
    return jax.shard_map(
        per_device,
        mesh=mesh,
        in_specs=placed,
        out_specs=(P("section", "rep", None, None, None), P()),
        check_vma=False,
    )
```

time: 214 us -> 71.7 us (0.34)
  waiting for transfers between devices: 157 us -> 17.6 us
  blocking collectives: 16.6 us -> 41.6 us
  between operations: 14.1 us -> 0.69 us
  loops' own time: 7.96 us -> 0 us
  local copies, waits for them, and re-layouts: 8.18 us -> 3.42 us
  matrix products: 4.45 us -> 0 us
    psum x1 -> x0, waiting for transfers between devices: 127 us -> none  [per_device(): weight_grad = lax.psum(grad_term, ('section', 'rep'))]
    all_to_all x0 -> x2, blocking collectives: none -> 24.7 us  [the longest x1 14.8 us: per_device(): lax.all_to_all(chunks, both, split_axis=0, concat_axis=0, tiled=True)]
    reduce_scatter x1 -> x0, waiting for transfers between devices: 24.2 us -> none  [per_device(): lax.psum_scatter(total.reshape(count, width).astype(jnp.bfloat16), 'rep',...]
    all_to_all x0 -> x1, waiting for transfers between devices: none -> 10.9 us  [per_device(): lax.all_to_all(spread, both, split_axis=0, concat_axis=0, tiled=True)]
    another operation x1 -> x0, loops' own time: 7.96 us -> none  [per_device(): total, _ = lax.scan(one_slot, start_total, jnp.arange(depth))]
    dot_general x7 -> x0, matrix products: 4.45 us -> none  [the longest x4 1.67 us: one_slot(): jnp.einsum('gab,gbf->gaf', tiles_local[:, index], picked, preferred_eleme...]
    all_to_all x0 -> x1, starting transfers between devices: none -> 2.59 us  [per_device(): lax.all_to_all(spread, both, split_axis=0, concat_axis=0, tiled=True)]
    dynamic_slice x4 -> x0, local copies, waits for them, and re-layouts: 2.34 us -> none  [per_device(): total, _ = lax.scan(one_slot, start_total, jnp.arange(depth))]
  transfers between devices with their start and end apart: 3 -> 2, of which waited for: 3 -> 2; matrix products, arithmetic and copies ran while one was open for 1% -> 0% of each run, Pallas kernels for 0% -> 0%
where the time goes in v1:
time: 71.7 us; the launch traced here: 71.3 us
  blocking collectives  41.6 us (58%)
  waiting for transfers between devices  17.6 us (25%)
  starting transfers between devices  5.96 us (8%)
  local copies, waits for them, and re-layouts  3.42 us (5%)
  Pallas kernels  1.96 us (3%)
    all_gather x1, blocking collectives, per_device(): gathered = lax.all_gather(features, 'section', axis=0, tiled=True)  16.9 us
    all_to_all x1, blocking collectives, per_device(): lax.all_to_all(chunks, both, split_axis=0, concat_axis=0, tiled=True)  14.8 us
    all_to_all x1, waiting for transfers between devices, per_device(): lax.all_to_all(spread, both, split_axis=0, concat_axis=0, tiled=True)  10.9 us
    all_to_all x1, blocking collectives, per_device(): lax.all_to_all(parts, 'rep', split_axis=0, concat_axis=0, tiled=True)  9.87 us
    all_to_all x1, waiting for transfers between devices, per_device(): lax.all_to_all(packed, 'section', split_axis=0, concat_axis=0, tiled=True)  6.67 us
    all_to_all x1, starting transfers between devices, per_device(): lax.all_to_all(packed, 'section', split_axis=0, concat_axis=0, tiled=True)  3.37 us
    unnamed x12, local copies, waits for them, and re-layouts  2.7 us
    all_to_all x1, starting transfers between devices, per_device(): lax.all_to_all(spread, both, split_axis=0, concat_axis=0, tiled=True)  2.59 us
  transfers between devices with their start and end apart: 2, of which 2 were waited for; matrix products, arithmetic and copies ran while one was open for 0% of the time, Pallas kernels for 0%

profile of v1, /device:TPU:0, one launch (start us, length us, event | category | flops | bytes accessed | tf_op | source)
XLA Modules:
  0.0 71.3 jit_solution(9259226477326422844)
XLA Ops:
  0.6 0.0 copy-start
  0.6 16.9 %all_gather.3 = bf16[1024,256]{1,0:T(8,128)(2,1)S(1)} all-gather(bf16[128,256]{1,0:T(8,128)(2,1)} %param.6), channel_id=1, replica_groups=mesh['section'=8,'rep'=4] {'section'}, dimensions={0}, use_global_device_ids=true | all-gather | bytes 589824 | tf_op jit(solution)/shard_map/all_gather | solution.py:86
  17.6 0.0 copy-start.3
  17.6 0.0 copy-done
  17.6 0.7 copy-done.3
  18.2 0.9 %partials.1 = bf16[4,128,256]{2,1,0:T(8,128)(2,1)S(1)} custom-call(s32[4,4]{1,0:T(4,128)S(1)} %bitcast.11, bf16[4,4,128,128]{3,2,1,0:T(8,128)(2,1)S(1)} %bitcast.9, bf16[8,128,256]{2,1,0:T(8,128)(2,1)S(1)} %bitcast.8), custom_call_target="tpu_custom_call" | custom-call | tf_op jit(solution)/shard_map/partials/pallas_call | solution.py:25
  19.1 0.0 copy-start.1
  19.1 0.0 copy-start.2
  19.2 9.9 %all_to_all.20.parts_ref = bf16[4,128,256]{2,1,0:T(8,128)(2,1)S(1)} all-to-all(bf16[4,128,256]{2,1,0:T(8,128)(2,1)S(1)} %partials.1), channel_id=1, replica_groups=mesh['section'=8,'rep'=4] {'rep'}, dimensions={0} | all-to-all | bytes 524288 | tf_op jit(solution)/shard_map/all_to_all | solution.py:90
  29.0 0.0 copy-start.4
  29.0 0.0 copy-done.1
  29.0 0.0 copy-done.2
  29.0 0.6 copy-done.4
  29.7 1.1 %dense.1 = (bf16[256,256]{1,0:T(8,128)(2,1)}, f32[256,256]{1,0:T(8,128)S(1)}) custom-call(bf16[4,128,256]{2,1,0:T(8,128)(2,1)S(1)} %all_to_all.20.parts_ref, bf16[256,256]{1,0:T(8,128)(2,1)S(1)} %copy-done.1, bf16[128,256]{1,0:T(8,128)(2,1)S(1)} %copy-done.2, s32[1,128]{1,0:T(1,128)S(1)} %bitcast.12), custom_call_target="tpu_custom_call" | custom-call | tf_op jit(solution)/shard_map/dense/pallas_call | solution.py:67
  30.8 14.8 %all_to_all.21 = f32[32,8,256]{2,1,0:T(8,128)S(1)} all-to-all(f32[32,8,256]{2,1,0:T(8,128)S(1)} %bitcast.10), channel_id=1, replica_groups=mesh['section'=8,'rep'=4] {'section','rep'}, dimensions={0} | all-to-all | bytes 524288 | tf_op jit(solution)/shard_map/all_to_all | solution.py:100
  45.6 3.4 %all-to-all-start.1 = ((bf16[8,32,256]{2,1,0:T(8,128)(2,1)}), bf16[8,32,256]{2,1,0:T(8,128)(2,1)S(1)}, u32[]{:S(2)}, u32[]{:S(2)}) async-start(bf16[8,32,256]{2,1,0:T(8,128)(2,1)} %bitcast.4), calls=%async_computation.1 | async-start | bytes 262144 | tf_op jit(solution)/shard_map/all_to_all | solution.py:95
  49.0 6.7 %all-to-all-done.1 = bf16[8,32,256]{2,1,0:T(8,128)(2,1)S(1)} async-done(((bf16[8,32,256]{2,1,0:T(8,128)(2,1)}), bf16[8,32,256]{2,1,0:T(8,128)(2,1)S(1)}, u32[]{:S(2)}, u32[]{:S(2)}) %all-to-all-start.1) | async-done | bytes 131104 | tf_op jit(solution)/shard_map/all_to_all | solution.py:95
  55.7 0.7 %broadcast_in_dim.2 = f32[32,8,256]{2,1,0:T(8,128)} broadcast(f32[8,256]{1,0:T(8,128)S(1)} %reduce_sum.9), dimensions={1,2} | broadcast | bytes 270336 | tf_op jit(solution)/shard_map/broadcast_in_dim | solution.py:102
  56.4 2.6 %all-to-all-start.3 = ((f32[32,8,256]{2,1,0:T(8,128)}), f32[32,8,256]{2,1,0:T(8,128)S(1)}, u32[]{:S(2)}, u32[]{:S(2)}) async-start(f32[32,8,256]{2,1,0:T(8,128)} %broadcast_in_dim.2), calls=%async_computation.3 | async-start | bytes 524288 | tf_op jit(solution)/shard_map/all_to_all | solution.py:103
  59.0 10.9 %all-to-all-done.3 = f32[32,8,256]{2,1,0:T(8,128)S(1)} async-done(((f32[32,8,256]{2,1,0:T(8,128)}), f32[32,8,256]{2,1,0:T(8,128)S(1)}, u32[]{:S(2)}, u32[]{:S(2)}) %all-to-all-start.3) | async-done | bytes 262176 | tf_op jit(solution)/shard_map/all_to_all | solution.py:103
  69.9 0.7 copy.10
  70.6 0.7 copy.11
  (1 shorter events, 0.0 us)
Async XLA Ops:
  0.6 16.9 %copy-start = (bf16[4,1,4,128,128]{4,3,2,1,0:T(8,128)(2,1)S(1)}, bf16[4,1,4,128,128]{4,3,2,1,0:T(8,128)(2,1)}, u32[]{:S(2)}) copy-start(bf16[4,1,4,128,128]{4,3,2,1,0:T(8,128)(2,1)} %param.7) | copy-start | bytes 1572868
  17.6 0.7 copy-start.3
  19.1 9.9 %copy-start.1 = (bf16[256,256]{1,0:T(8,128)(2,1)S(1)}, bf16[256,256]{1,0:T(8,128)(2,1)}, u32[]{:S(2)}) copy-start(bf16[256,256]{1,0:T(8,128)(2,1)} %weight_ref.1) | copy-start | bytes 393220
  19.1 9.9 %copy-start.2 = (bf16[128,256]{1,0:T(8,128)(2,1)S(1)}, bf16[128,256]{1,0:T(8,128)(2,1)}, u32[]{:S(2)}) copy-start(bf16[128,256]{1,0:T(8,128)(2,1)} %cot_ref.1) | copy-start | bytes 196612
  29.0 0.7 copy-start.4
  45.6 10.1 %all-to-all-start.1 = ((bf16[8,32,256]{2,1,0:T(8,128)(2,1)}), bf16[8,32,256]{2,1,0:T(8,128)(2,1)S(1)}, u32[]{:S(2)}, u32[]{:S(2)}) async-start(bf16[8,32,256]{2,1,0:T(8,128)(2,1)} %bitcast.4), calls=%async_computation.1 | async-start | bytes 262144 | tf_op jit(solution)/shard_map/all_to_all | solution.py:95
  56.4 13.5 %all-to-all-start.3 = ((f32[32,8,256]{2,1,0:T(8,128)}), f32[32,8,256]{2,1,0:T(8,128)S(1)}, u32[]{:S(2)}, u32[]{:S(2)}) async-start(f32[32,8,256]{2,1,0:T(8,128)} %broadcast_in_dim.2), calls=%async_computation.3 | async-start | bytes 524288 | tf_op jit(solution)/shard_map/all_to_all | solution.py:103

commit v2 on v1

--- a/solution.py
+++ b/solution.py
@@ -11,32 +11,54 @@
 SMEM = pl.BlockSpec(memory_space=pltpu.SMEM)
 
 
-def partials_kernel(src_ref, tiles_ref, blocks_ref, out_ref):
-    many, depth = tiles_ref.shape[0], tiles_ref.shape[1]
-    for g in range(many):
+def partials_kernel(count, src_ref, tiles_ref, *refs):
+    block_refs, out_refs, held = refs[:count], refs[count:-1], refs[-1]
+    depth = tiles_ref.shape[1]
+    section, rep = lax.axis_index("section"), lax.axis_index("rep")
+    for j in range(count):
+        held[j] = block_refs[j][...]
+    for j, out_ref in enumerate(out_refs):
+        g = rep ^ j
         left = jnp.concatenate([tiles_ref[g, k] for k in range(depth)], axis=1)
-        right = jnp.concatenate([blocks_ref[src_ref[g, k]] for k in range(depth)], axis=0)
-        out_ref[g] = jnp.dot(left, right, preferred_element_type=jnp.float32).astype(jnp.bfloat16)
+        right = jnp.concatenate([held[src_ref[g, k] ^ section] for k in range(depth)], axis=0)
+        out_ref[...] = jnp.dot(left, right, preferred_element_type=jnp.float32).astype(jnp.bfloat16)
 
 
 def partials(sources, tiles, blocks):
-    many, depth, tile, _ = tiles.shape
-    width = blocks.shape[2]
+    many, tile = tiles.shape[0], tiles.shape[2]
+    width = blocks[0].shape[1]
     return pl.pallas_call(
-        partials_kernel,
-        out_shape=jax.ShapeDtypeStruct((many, tile, width), jnp.bfloat16),
-        in_specs=[SMEM, VMEM, VMEM],
-        out_specs=VMEM,
+        functools.partial(partials_kernel, len(blocks)),
+        out_shape=[jax.ShapeDtypeStruct((tile, width), jnp.bfloat16)] * many,
+        in_specs=[SMEM] + [VMEM] * (1 + len(blocks)),
+        out_specs=[VMEM] * many,
+        scratch_shapes=[pltpu.VMEM((len(blocks), tile, width), jnp.bfloat16)],
         compiler_params=pltpu.CompilerParams(vmem_limit_bytes=32 * 1024 * 1024),
         name="partials",
-    )(sources, tiles, blocks)
+    )(sources, tiles, *blocks)
 
 
-def dense_kernel(slots, parts_ref, weight_ref, cot_ref, target_ref, packed_ref, grad_ref):
+def swap(value, axis, j):
+    return lax.ppermute(value, axis, [(i, i ^ j) for i in range(lax.axis_size(axis))])
+
+
+def gather_blocks(features, axis):
+    n = lax.axis_size(axis)
+    blocks = [None] * n
+    blocks[0] = features
+    for j in range(2, n, 2):
+        blocks[j] = swap(features, axis, j)
+    for j in range(0, n, 2):
+        blocks[j + 1] = swap(blocks[j], axis, 1)
+    return blocks
+
+
+def dense_kernel(slots, weight_ref, cot_ref, target_ref, *refs):
+    part_refs, (packed_ref, grad_ref) = refs[:-2], refs[-2:]
     rows = cot_ref.shape[0]
     places = packed_ref.shape[0]
     n_section = places // slots
-    agg_b = jnp.sum(parts_ref[...].astype(jnp.float32), axis=0).astype(jnp.bfloat16)
+    agg_b = sum(ref[...].astype(jnp.float32) for ref in part_refs).astype(jnp.bfloat16)
     pre = jnp.dot(agg_b, weight_ref[...], preferred_element_type=jnp.float32)
     sig = jax.nn.sigmoid(pre)
     output = (pre * sig).astype(jnp.bfloat16)
@@ -68,13 +90,13 @@
         functools.partial(dense_kernel, slots),
         out_shape=(
             jax.ShapeDtypeStruct((places, width), jnp.bfloat16),
-            jax.ShapeDtypeStruct((width, width), jnp.float32),
+            jax.ShapeDtypeStruct((width, width), jnp.bfloat16),
         ),
-        in_specs=[VMEM] * 4,
+        in_specs=[VMEM] * (3 + len(parts)),
         out_specs=(VMEM, VMEM),
         compiler_params=pltpu.CompilerParams(vmem_limit_bytes=32 * 1024 * 1024),
         name="dense",
-    )(parts, weight, cotangent, target)
+    )(weight, cotangent, target, *parts)
 
 
 def per_device(features, adj_tiles, adj_src, cotangent, weight, destination):
@@ -83,11 +105,9 @@
     devices = n_section * n_rep
     rows_here, width = features.shape
     tile = adj_tiles.shape[3]
-    gathered = lax.all_gather(features, "section", axis=0, tiled=True)
-    blocks = gathered.reshape(-1, tile, width)
-    part = partials(adj_src[:, 0], adj_tiles[:, 0], blocks)
-    parts = part.reshape(n_rep, rows_here, width)
-    parts = lax.all_to_all(parts, "rep", split_axis=0, concat_axis=0, tiled=True)
+    blocks = gather_blocks(features.reshape(tile, width), "section")
+    parts = partials(adj_src[:, 0], adj_tiles[:, 0], blocks)
+    parts = [parts[0]] + [swap(parts[j], "rep", j) for j in range(1, n_rep)]
     slots = max(2, 2 * rows_here // n_section)
     target = destination.reshape(1, rows_here)
     packed, grad = dense(parts, weight, cotangent, target, n_section * slots, slots)
@@ -98,10 +118,10 @@
     if width % devices == 0:
         chunks = grad.reshape(devices, width // devices, width)
     terms = lax.all_to_all(chunks, both, split_axis=0, concat_axis=0, tiled=True)
-    mine = jnp.sum(terms, axis=0, keepdims=True)
+    mine = jnp.sum(terms.astype(jnp.float32), axis=0, keepdims=True).astype(jnp.bfloat16)
     spread = jnp.broadcast_to(mine, chunks.shape)
     weight_grad = lax.all_to_all(spread, both, split_axis=0, concat_axis=0, tiled=True)
-    return (relaid, weight_grad.reshape(width, width))
+    return (relaid, weight_grad.reshape(width, width).astype(jnp.float32))
 
 
 def solution(mesh):

time: 71.7 us -> 60.5 us (0.84)
  blocking collectives: 41.6 us -> 10.3 us
  waiting for transfers between devices: 17.6 us -> 27.3 us
  starting transfers between devices: 5.96 us -> 15.2 us
  other arithmetic: 0.04 us -> 0.76 us
    all_gather x1 -> x0, blocking collectives: 16.9 us -> none  [per_device(): gathered = lax.all_gather(features, 'section', axis=0, tiled=True)]
    ppermute x0 -> x10, waiting for transfers between devices: none -> 12.2 us  [swap(): lax.ppermute(value, axis, [(i, i ^ j) for i in range(lax.axis_size(axis))])]
    all_to_all x1 -> x0, blocking collectives: 9.87 us -> none  [per_device(): lax.all_to_all(parts, 'rep', split_axis=0, concat_axis=0, tiled=True)]
    ppermute x0 -> x10, starting transfers between devices: none -> 9.24 us  [swap(): lax.ppermute(value, axis, [(i, i ^ j) for i in range(lax.axis_size(axis))])]
    all_to_all x1, blocking collectives: 14.8 us -> 10.3 us  [per_device(): lax.all_to_all(chunks, both, split_axis=0, concat_axis=0, tiled=True)]
    all_to_all x1, waiting for transfers between devices: 10.9 us -> 8.4 us  [per_device(): lax.all_to_all(spread, both, split_axis=0, concat_axis=0, tiled=True)]
    convert_element_type x0 -> x1, other arithmetic: none -> 0.72 us  [per_device(): return (relaid, weight_grad.reshape(width, width).astype(jnp.float32))]
    unnamed x12 -> x13, local copies, waits for them, and re-layouts: 2.7 us -> 3.2 us
  transfers between devices with their start and end apart: 2 -> 12, of which waited for: 2 -> 9; matrix products, arithmetic and copies ran while one was open for 0% -> 0% of each run, Pallas kernels for 0% -> 0%
where the time goes in v2:
time: 60.5 us; the launch traced here: 60.1 us
  waiting for transfers between devices  27.3 us (45%)
  starting transfers between devices  15.2 us (25%)
  blocking collectives  10.3 us (17%)
  local copies, waits for them, and re-layouts  3.86 us (6%)
  Pallas kernels  2 us (3%)
  other arithmetic  0.76 us (1%)
  between operations  0.7 us (1%)
    ppermute x10, waiting for transfers between devices, swap(): lax.ppermute(value, axis, [(i, i ^ j) for i in range(lax.axis_size(axis))])  12.2 us
    all_to_all x1, blocking collectives, per_device(): lax.all_to_all(chunks, both, split_axis=0, concat_axis=0, tiled=True)  10.3 us
    ppermute x10, starting transfers between devices, swap(): lax.ppermute(value, axis, [(i, i ^ j) for i in range(lax.axis_size(axis))])  9.24 us
    all_to_all x1, waiting for transfers between devices, per_device(): lax.all_to_all(spread, both, split_axis=0, concat_axis=0, tiled=True)  8.4 us
    all_to_all x1, waiting for transfers between devices, per_device(): lax.all_to_all(packed, 'section', split_axis=0, concat_axis=0, tiled=True)  6.67 us
    all_to_all x1, starting transfers between devices, per_device(): lax.all_to_all(packed, 'section', split_axis=0, concat_axis=0, tiled=True)  3.37 us
    unnamed x13, local copies, waits for them, and re-layouts  3.2 us
    all_to_all x1, starting transfers between devices, per_device(): lax.all_to_all(spread, both, split_axis=0, concat_axis=0, tiled=True)  2.58 us
  transfers between devices with their start and end apart: 12, of which 9 were waited for; matrix products, arithmetic and copies ran while one was open for 0% of the time, Pallas kernels for 0%

profile of v2, /device:TPU:0, one launch (start us, length us, event | category | flops | bytes accessed | tf_op | source)
XLA Modules:
  0.0 60.1 jit_solution(14775509578876945952)
XLA Ops:
  0.6 0.0 copy-start.4
  0.6 4.1 %collective-permute-start.3 = (bf16[128,256]{1,0:T(8,128)(2,1)}, bf16[128,256]{1,0:T(8,128)(2,1)S(1)}, u32[]{:S(2)}, u32[]{:S(2)}) collective-permute-start(bf16[128,256]{1,0:T(8,128)(2,1)} %refs_0_.1), channel_id=1, source_target_pairs={{0,16},{4,20},{8,24},{12,28},{16,0},{20,4},{24,8},{28,12},{1,17},{... | collective-permute-start | bytes 196616 | tf_op jit(solution)/shard_map/ppermute | solution.py:42
  4.7 1.6 %collective-permute-start.1 = (bf16[128,256]{1,0:T(8,128)(2,1)}, bf16[128,256]{1,0:T(8,128)(2,1)S(1)}, u32[]{:S(2)}, u32[]{:S(2)}) collective-permute-start(bf16[128,256]{1,0:T(8,128)(2,1)} %refs_0_.1), channel_id=1, source_target_pairs={{0,8},{4,12},{8,0},{12,4},{16,24},{20,28},{24,16},{28,20},{1,9},{5... | collective-permute-start | bytes 196616 | tf_op jit(solution)/shard_map/ppermute | solution.py:42
  6.3 0.0 collective-permute-start.5
  6.3 0.0 collective-permute-start
  6.3 1.7 %collective-permute-done.3.refs_4_ = bf16[128,256]{1,0:T(8,128)(2,1)S(1)} collective-permute-done((bf16[128,256]{1,0:T(8,128)(2,1)}, bf16[128,256]{1,0:T(8,128)(2,1)S(1)}, u32[]{:S(2)}, u32[]{:S(2)}) %collective-permute-start.3) | collective-permute-done | bytes 65568 | tf_op jit(solution)/shard_map/ppermute | solution.py:42
  8.0 0.0 collective-permute-start.4
  8.0 1.2 %collective-permute-done.1.refs_2_ = bf16[128,256]{1,0:T(8,128)(2,1)S(1)} collective-permute-done((bf16[128,256]{1,0:T(8,128)(2,1)}, bf16[128,256]{1,0:T(8,128)(2,1)S(1)}, u32[]{:S(2)}, u32[]{:S(2)}) %collective-permute-start.1) | collective-permute-done | bytes 65568 | tf_op jit(solution)/shard_map/ppermute | solution.py:42
  9.2 0.0 collective-permute-start.2
  9.2 3.4 %collective-permute-done.5.refs_6_ = bf16[128,256]{1,0:T(8,128)(2,1)S(1)} collective-permute-done((bf16[128,256]{1,0:T(8,128)(2,1)}, bf16[128,256]{1,0:T(8,128)(2,1)S(1)}, u32[]{:S(2)}, u32[]{:S(2)}) %collective-permute-start.5) | collective-permute-done | bytes 65568 | tf_op jit(solution)/shard_map/ppermute | solution.py:42
  12.6 0.0 collective-permute-start.6
  12.6 0.0 collective-permute-done.refs_1_
  12.6 0.0 collective-permute-done.4.refs_5_
  12.6 0.0 collective-permute-done.2.refs_3_
  12.6 1.2 %collective-permute-done.6.refs_7_ = bf16[128,256]{1,0:T(8,128)(2,1)S(1)} collective-permute-done((bf16[128,256]{1,0:T(8,128)(2,1)S(1)}, bf16[128,256]{1,0:T(8,128)(2,1)S(1)}, u32[]{:S(2)}, u32[]{:S(2)}) %collective-permute-start.6) | collective-permute-done | bytes 65568 | tf_op jit(solution)/shard_map/ppermute | solution.py:42
  13.8 0.0 copy-done.4
  13.9 0.0 copy-start
  13.9 1.0 %copy-done = bf16[4,1,4,128,128]{4,3,2,1,0:T(8,128)(2,1)S(1)} copy-done((bf16[4,1,4,128,128]{4,3,2,1,0:T(8,128)(2,1)S(1)}, bf16[4,1,4,128,128]{4,3,2,1,0:T(8,128)(2,1)}, u32[]{:S(2)}) %copy-start) | copy-done | bytes 524312
  14.9 0.0 copy-start.2
  14.9 0.8 %copy-done.2 = bf16[128,256]{1,0:T(8,128)(2,1)S(1)} copy-done((bf16[128,256]{1,0:T(8,128)(2,1)S(1)}, bf16[128,256]{1,0:T(8,128)(2,1)}, u32[]{:S(2)}) %copy-start.2) | copy-done | bytes 65560
  15.7 0.0 copy-start.1
  15.7 0.0 copy-start.3
  15.7 0.9 %partials.1 = (bf16[128,256]{1,0:T(8,128)(2,1)S(1)}, bf16[128,256]{1,0:T(8,128)(2,1)S(1)}, bf16[128,256]{1,0:T(8,128)(2,1)S(1)}, bf16[128,256]{1,0:T(8,128)(2,1)S(1)}) custom-call(s32[4,4]{1,0:T(4,128)S(1)} %bitcast.11, bf16[4,4,128,128]{3,2,1,0:T(8,128)(2,1)S(1)} %bitcast.9, bf16[128,256]{1,0:T(8,128)(2,1)S(1)} %copy-done.2, ...), custom_call_target="tpu_custom_call" | custom-call | tf_op jit(solution)/shard_map/partials/pallas_call | solution.py:30
  16.7 1.6 %collective-permute-start.7 = (bf16[128,256]{1,0:T(8,128)(2,1)S(1)}, bf16[128,256]{1,0:T(8,128)(2,1)S(1)}, u32[]{:S(2)}, u32[]{:S(2)}) collective-permute-start(bf16[128,256]{1,0:T(8,128)(2,1)S(1)} %get-tuple-element.9), channel_id=1, source_target_pairs={{0,1},{1,0},{2,3},{3,2},{4,5},{5,4},{6,7},{7,6},{8,9},{9,8},{10,11... | collective-permute-start | bytes 196616 | tf_op jit(solution)/shard_map/ppermute | solution.py:42
  18.2 1.5 %collective-permute-start.8 = (bf16[128,256]{1,0:T(8,128)(2,1)S(1)}, bf16[128,256]{1,0:T(8,128)(2,1)S(1)}, u32[]{:S(2)}, u32[]{:S(2)}) collective-permute-start(bf16[128,256]{1,0:T(8,128)(2,1)S(1)} %get-tuple-element.10), channel_id=1, source_target_pairs={{0,2},{1,3},{2,0},{3,1},{4,6},{5,7},{6,4},{7,5},{8,10},{9,11},{10,... | collective-permute-start | bytes 196616 | tf_op jit(solution)/shard_map/ppermute | solution.py:42
  19.7 0.5 collective-permute-start.9
  20.2 0.8 %collective-permute-done.7.refs_1_ = bf16[128,256]{1,0:T(8,128)(2,1)S(1)} collective-permute-done((bf16[128,256]{1,0:T(8,128)(2,1)S(1)}, bf16[128,256]{1,0:T(8,128)(2,1)S(1)}, u32[]{:S(2)}, u32[]{:S(2)}) %collective-permute-start.7) | collective-permute-done | bytes 65568 | tf_op jit(solution)/shard_map/ppermute | solution.py:42
  21.0 1.5 %collective-permute-done.8.refs_2_ = bf16[128,256]{1,0:T(8,128)(2,1)S(1)} collective-permute-done((bf16[128,256]{1,0:T(8,128)(2,1)S(1)}, bf16[128,256]{1,0:T(8,128)(2,1)S(1)}, u32[]{:S(2)}, u32[]{:S(2)}) %collective-permute-start.8) | collective-permute-done | bytes 65568 | tf_op jit(solution)/shard_map/ppermute | solution.py:42
  22.5 2.4 %collective-permute-done.9.refs_3_ = bf16[128,256]{1,0:T(8,128)(2,1)S(1)} collective-permute-done((bf16[128,256]{1,0:T(8,128)(2,1)S(1)}, bf16[128,256]{1,0:T(8,128)(2,1)S(1)}, u32[]{:S(2)}, u32[]{:S(2)}) %collective-permute-start.9) | collective-permute-done | bytes 65568 | tf_op jit(solution)/shard_map/ppermute | solution.py:42
  24.9 0.0 copy-start.5
  24.9 0.0 copy-done.1
  24.9 0.0 copy-done.3
  24.9 0.6 %copy-done.5 = s32[128,1]{0,1:T(1,128)S(1)} copy-done((s32[128,1]{0,1:T(1,128)S(1)}, s32[128,1]{0,1:T(1,128)}, u32[]{:S(2)}) %copy-start.5) | copy-done | bytes 536
  25.6 1.1 %dense.1 = (bf16[256,256]{1,0:T(8,128)(2,1)}, bf16[256,256]{1,0:T(8,128)(2,1)S(1)}) custom-call(bf16[256,256]{1,0:T(8,128)(2,1)S(1)} %copy-done.1, bf16[128,256]{1,0:T(8,128)(2,1)S(1)} %copy-done.3, s32[1,128]{1,0:T(1,128)S(1)} %bitcast.12, bf16[128,256]{1,0:T(8,128)(2,1)S(1)} %get-tuple-element.8.refs_0_, ...), custom_call_target="tpu_custom_call" | custom-call | tf_op jit(solution)/shard_map/dense/pallas_call | solution.py:89
  26.6 10.3 %all_to_all.15 = bf16[32,8,256]{2,1,0:T(8,128)(2,1)S(1)} all-to-all(bf16[32,8,256]{2,1,0:T(8,128)(2,1)S(1)} %bitcast.10), channel_id=1, replica_groups=mesh['section'=8,'rep'=4] {'section','rep'}, dimensions={0} | all-to-all | bytes 262144 | tf_op jit(solution)/shard_map/all_to_all | solution.py:120
  37.0 3.4 %all-to-all-start = ((bf16[8,32,256]{2,1,0:T(8,128)(2,1)}), bf16[8,32,256]{2,1,0:T(8,128)(2,1)S(1)}, u32[]{:S(2)}, u32[]{:S(2)}) async-start(bf16[8,32,256]{2,1,0:T(8,128)(2,1)} %bitcast.3), calls=%async_computation | async-start | bytes 262144 | tf_op jit(solution)/shard_map/all_to_all | solution.py:115
  40.4 6.7 %all-to-all-done = bf16[8,32,256]{2,1,0:T(8,128)(2,1)S(1)} async-done(((bf16[8,32,256]{2,1,0:T(8,128)(2,1)}), bf16[8,32,256]{2,1,0:T(8,128)(2,1)S(1)}, u32[]{:S(2)}, u32[]{:S(2)}) %all-to-all-start) | async-done | bytes 131104 | tf_op jit(solution)/shard_map/all_to_all | solution.py:115
  47.1 0.7 %broadcast_in_dim.2 = bf16[32,8,256]{2,1,0:T(8,128)(2,1)} broadcast(bf16[8,256]{1,0:T(8,128)(2,1)S(1)} %reduce_sum.12), dimensions={1,2} | broadcast | bytes 135168 | tf_op jit(solution)/shard_map/broadcast_in_dim | solution.py:122
  47.7 2.6 %all-to-all-start.2 = ((bf16[32,8,256]{2,1,0:T(8,128)(2,1)}), bf16[32,8,256]{2,1,0:T(8,128)(2,1)S(1)}, u32[]{:S(2)}, u32[]{:S(2)}) async-start(bf16[32,8,256]{2,1,0:T(8,128)(2,1)} %broadcast_in_dim.2), calls=%async_computation.2 | async-start | bytes 262144 | tf_op jit(solution)/shard_map/all_to_all | solution.py:123
  50.3 8.4 %all-to-all-done.2 = bf16[32,8,256]{2,1,0:T(8,128)(2,1)S(1)} async-done(((bf16[32,8,256]{2,1,0:T(8,128)(2,1)}), bf16[32,8,256]{2,1,0:T(8,128)(2,1)S(1)}, u32[]{:S(2)}, u32[]{:S(2)}) %all-to-all-start.2) | async-done | bytes 131104 | tf_op jit(solution)/shard_map/all_to_all | solution.py:123
  58.7 0.7 %bitcast_convert_fusion = f32[256,256]{1,0:T(8,128)} fusion(bf16[32,8,256]{2,1,0:T(8,128)(2,1)S(1)} %all-to-all-done.2), kind=kLoop, calls=%fused_computation | loop fusion | flops 65536 | bytes 393216 | tf_op jit(solution)/shard_map/convert_element_type | solution.py:124
  59.4 0.7 %copy.9 = bf16[1,1,8,32,256]{4,3,2,1,0:T(8,128)(2,1)} copy(bf16[1,1,8,32,256]{4,3,2,1,0:T(8,128)(2,1)S(1)} %bitcast.13) | data formatting | bytes 262144
  (1 shorter events, 0.0 us)
Async XLA Ops:
  0.6 13.2 %copy-start.4 = (s32[4,1,4]{2,1,0:T(1,128)S(1)}, s32[4,1,4]{2,1,0:T(1,128)}, u32[]{:S(2)}) copy-start(s32[4,1,4]{2,1,0:T(1,128)} %param.8) | copy-start | bytes 196
  0.6 7.4 %collective-permute-start.3 = (bf16[128,256]{1,0:T(8,128)(2,1)}, bf16[128,256]{1,0:T(8,128)(2,1)S(1)}, u32[]{:S(2)}, u32[]{:S(2)}) collective-permute-start(bf16[128,256]{1,0:T(8,128)(2,1)} %refs_0_.1), channel_id=1, source_target_pairs={{0,16},{4,20},{8,24},{12,28},{16,0},{20,4},{24,8},{28,12},{1,17},{... | collective-permute-start | bytes 196616 | tf_op jit(solution)/shard_map/ppermute | solution.py:42
  4.7 4.5 %collective-permute-start.1 = (bf16[128,256]{1,0:T(8,128)(2,1)}, bf16[128,256]{1,0:T(8,128)(2,1)S(1)}, u32[]{:S(2)}, u32[]{:S(2)}) collective-permute-start(bf16[128,256]{1,0:T(8,128)(2,1)} %refs_0_.1), channel_id=1, source_target_pairs={{0,8},{4,12},{8,0},{12,4},{16,24},{20,28},{24,16},{28,20},{1,9},{5... | collective-permute-start | bytes 196616 | tf_op jit(solution)/shard_map/ppermute | solution.py:42
  6.3 6.3 %collective-permute-start.5 = (bf16[128,256]{1,0:T(8,128)(2,1)}, bf16[128,256]{1,0:T(8,128)(2,1)S(1)}, u32[]{:S(2)}, u32[]{:S(2)}) collective-permute-start(bf16[128,256]{1,0:T(8,128)(2,1)} %refs_0_.1), channel_id=1, source_target_pairs={{0,24},{4,28},{8,16},{12,20},{16,8},{20,12},{24,0},{28,4},{1,25},{... | collective-permute-start | bytes 196616 | tf_op jit(solution)/shard_map/ppermute | solution.py:42
  6.3 6.3 %collective-permute-start = (bf16[128,256]{1,0:T(8,128)(2,1)}, bf16[128,256]{1,0:T(8,128)(2,1)S(1)}, u32[]{:S(2)}, u32[]{:S(2)}) collective-permute-start(bf16[128,256]{1,0:T(8,128)(2,1)} %refs_0_.1), channel_id=1, source_target_pairs={{0,4},{4,0},{8,12},{12,8},{16,20},{20,16},{24,28},{28,24},{1,5},{5... | collective-permute-start | bytes 196616 | tf_op jit(solution)/shard_map/ppermute | solution.py:42
  8.0 4.6 %collective-permute-start.4 = (bf16[128,256]{1,0:T(8,128)(2,1)S(1)}, bf16[128,256]{1,0:T(8,128)(2,1)S(1)}, u32[]{:S(2)}, u32[]{:S(2)}) collective-permute-start(bf16[128,256]{1,0:T(8,128)(2,1)S(1)} %collective-permute-done.3.refs_4_), channel_id=1, source_target_pairs={{0,4},{4,0},{8,12},{12,8},{16,20},{20,16},{24,28},{28,24},{1,5},{5... | collective-permute-start | bytes 196616 | tf_op jit(solution)/shard_map/ppermute | solution.py:42
  9.2 3.4 %collective-permute-start.2 = (bf16[128,256]{1,0:T(8,128)(2,1)S(1)}, bf16[128,256]{1,0:T(8,128)(2,1)S(1)}, u32[]{:S(2)}, u32[]{:S(2)}) collective-permute-start(bf16[128,256]{1,0:T(8,128)(2,1)S(1)} %collective-permute-done.1.refs_2_), channel_id=1, source_target_pairs={{0,4},{4,0},{8,12},{12,8},{16,20},{20,16},{24,28},{28,24},{1,5},{5... | collective-permute-start | bytes 196616 | tf_op jit(solution)/shard_map/ppermute | solution.py:42
  12.6 1.3 %collective-permute-start.6 = (bf16[128,256]{1,0:T(8,128)(2,1)S(1)}, bf16[128,256]{1,0:T(8,128)(2,1)S(1)}, u32[]{:S(2)}, u32[]{:S(2)}) collective-permute-start(bf16[128,256]{1,0:T(8,128)(2,1)S(1)} %collective-permute-done.5.refs_6_), channel_id=1, source_target_pairs={{0,4},{4,0},{8,12},{12,8},{16,20},{20,16},{24,28},{28,24},{1,5},{5... | collective-permute-start | bytes 196616 | tf_op jit(solution)/shard_map/ppermute | solution.py:42
  13.9 1.0 %copy-start = (bf16[4,1,4,128,128]{4,3,2,1,0:T(8,128)(2,1)S(1)}, bf16[4,1,4,128,128]{4,3,2,1,0:T(8,128)(2,1)}, u32[]{:S(2)}) copy-start(bf16[4,1,4,128,128]{4,3,2,1,0:T(8,128)(2,1)} %param.7) | copy-start | bytes 1572868
  14.9 0.8 %copy-start.2 = (bf16[128,256]{1,0:T(8,128)(2,1)S(1)}, bf16[128,256]{1,0:T(8,128)(2,1)}, u32[]{:S(2)}) copy-start(bf16[128,256]{1,0:T(8,128)(2,1)} %refs_0_.1) | copy-start | bytes 196612
  15.7 9.2 %copy-start.1 = (bf16[256,256]{1,0:T(8,128)(2,1)S(1)}, bf16[256,256]{1,0:T(8,128)(2,1)}, u32[]{:S(2)}) copy-start(bf16[256,256]{1,0:T(8,128)(2,1)} %weight_ref.1) | copy-start | bytes 393220
  15.7 9.2 %copy-start.3 = (bf16[128,256]{1,0:T(8,128)(2,1)S(1)}, bf16[128,256]{1,0:T(8,128)(2,1)}, u32[]{:S(2)}) copy-start(bf16[128,256]{1,0:T(8,128)(2,1)} %cot_ref.1) | copy-start | bytes 196612
  16.7 4.3 %collective-permute-start.7 = (bf16[128,256]{1,0:T(8,128)(2,1)S(1)}, bf16[128,256]{1,0:T(8,128)(2,1)S(1)}, u32[]{:S(2)}, u32[]{:S(2)}) collective-permute-start(bf16[128,256]{1,0:T(8,128)(2,1)S(1)} %get-tuple-element.9), channel_id=1, source_target_pairs={{0,1},{1,0},{2,3},{3,2},{4,5},{5,4},{6,7},{7,6},{8,9},{9,8},{10,11... | collective-permute-start | bytes 196616 | tf_op jit(solution)/shard_map/ppermute | solution.py:42
  18.2 4.3 %collective-permute-start.8 = (bf16[128,256]{1,0:T(8,128)(2,1)S(1)}, bf16[128,256]{1,0:T(8,128)(2,1)S(1)}, u32[]{:S(2)}, u32[]{:S(2)}) collective-permute-start(bf16[128,256]{1,0:T(8,128)(2,1)S(1)} %get-tuple-element.10), channel_id=1, source_target_pairs={{0,2},{1,3},{2,0},{3,1},{4,6},{5,7},{6,4},{7,5},{8,10},{9,11},{10,... | collective-permute-start | bytes 196616 | tf_op jit(solution)/shard_map/ppermute | solution.py:42
  19.7 5.2 %collective-permute-start.9 = (bf16[128,256]{1,0:T(8,128)(2,1)S(1)}, bf16[128,256]{1,0:T(8,128)(2,1)S(1)}, u32[]{:S(2)}, u32[]{:S(2)}) collective-permute-start(bf16[128,256]{1,0:T(8,128)(2,1)S(1)} %get-tuple-element.11), channel_id=1, source_target_pairs={{0,3},{1,2},{2,1},{3,0},{4,7},{5,6},{6,5},{7,4},{8,11},{9,10},{10,... | collective-permute-start | bytes 196616 | tf_op jit(solution)/shard_map/ppermute | solution.py:42
  24.9 0.7 %copy-start.5 = (s32[128,1]{0,1:T(1,128)S(1)}, s32[128,1]{0,1:T(1,128)}, u32[]{:S(2)}) copy-start(s32[128,1]{0,1:T(1,128)} %param.11) | copy-start | bytes 1540
  37.0 10.1 %all-to-all-start = ((bf16[8,32,256]{2,1,0:T(8,128)(2,1)}), bf16[8,32,256]{2,1,0:T(8,128)(2,1)S(1)}, u32[]{:S(2)}, u32[]{:S(2)}) async-start(bf16[8,32,256]{2,1,0:T(8,128)(2,1)} %bitcast.3), calls=%async_computation | async-start | bytes 262144 | tf_op jit(solution)/shard_map/all_to_all | solution.py:115
  47.7 11.0 %all-to-all-start.2 = ((bf16[32,8,256]{2,1,0:T(8,128)(2,1)}), bf16[32,8,256]{2,1,0:T(8,128)(2,1)S(1)}, u32[]{:S(2)}, u32[]{:S(2)}) async-start(bf16[32,8,256]{2,1,0:T(8,128)(2,1)} %broadcast_in_dim.2), calls=%async_computation.2 | async-start | bytes 262144 | tf_op jit(solution)/shard_map/all_to_all | solution.py:123

commit v3 on v2

v3 whole, which is shorter than its diff:
```python
import functools

import jax
import jax.numpy as jnp
from jax import lax
from jax.experimental import pallas as pl
from jax.experimental.pallas import tpu as pltpu
from jax.sharding import PartitionSpec as P

VMEM = pl.BlockSpec(memory_space=pltpu.VMEM)
LIMIT = pltpu.CompilerParams(vmem_limit_bytes=32 * 1024 * 1024)
SMEM = pl.BlockSpec(memory_space=pltpu.SMEM)


def prepare_kernel(slots, tiles_ref, own_ref, target_ref, wide_ref, held_ref, placing_ref):
    many, depth = tiles_ref.shape[:2]
    for g in range(many):
        wide_ref[g] = jnp.concatenate([tiles_ref[g, k] for k in range(depth)], axis=1)
    held_ref[...] = own_ref[...]
    places, rows = placing_ref.shape
    n_section = places // slots
    target = target_ref[...]
    hits = lax.broadcasted_iota(jnp.int32, (n_section, rows), 0) == target
    hits = jnp.where(hits, 1.0, 0.0)
    earlier = lax.broadcasted_iota(jnp.int32, (rows, rows), 0) < lax.broadcasted_iota(
        jnp.int32, (rows, rows), 1
    )
    earlier = jnp.where(earlier, 1.0, 0.0).astype(jnp.bfloat16)
    before = jnp.dot(hits.astype(jnp.bfloat16), earlier, preferred_element_type=jnp.float32)
    slot = jnp.sum(before * hits, axis=0, keepdims=True).astype(jnp.int32)
    apart = target ^ lax.axis_index("section")
    position = ((apart & 1) * (n_section // 2) + (apart >> 1)) * slots + slot
    placing = lax.broadcasted_iota(jnp.int32, (places, rows), 0) == position
    placing_ref[...] = jnp.where(placing, 1.0, 0.0).astype(jnp.bfloat16)


def prepare(tiles, own, target, places, slots):
    many, depth, tile, _ = tiles.shape
    return pl.pallas_call(
        functools.partial(prepare_kernel, slots),
        out_shape=(
            jax.ShapeDtypeStruct((many, tile, depth * tile), jnp.bfloat16),
            jax.ShapeDtypeStruct(own.shape, jnp.bfloat16),
            jax.ShapeDtypeStruct((places, target.shape[1]), jnp.bfloat16),
        ),
        in_specs=[VMEM] * 3,
        out_specs=(VMEM,) * 3,
        compiler_params=LIMIT,
        cost_estimate=pl.CostEstimate(flops=0, bytes_accessed=2 * tiles.size * 2, transcendentals=0),
        name="prepare",
    )(tiles, own, target)


def partials_kernel(count, src_ref, wide_ref, *refs):
    block_refs, out_refs, held = refs[:count], refs[count:-1], refs[-1]
    depth = src_ref.shape[1]
    section, rep = lax.axis_index("section"), lax.axis_index("rep")
    for j in range(count):
        held[j] = block_refs[j][...]
    for j, out_ref in enumerate(out_refs):
        g = rep ^ j
        right = jnp.concatenate([held[src_ref[g, k] ^ section] for k in range(depth)], axis=0)
        out_ref[...] = jnp.dot(wide_ref[g], right, preferred_element_type=jnp.float32).astype(
            jnp.bfloat16
        )


def partials(sources, wide, blocks):
    many = wide.shape[0]
    tile, width = blocks[0].shape
    return pl.pallas_call(
        functools.partial(partials_kernel, len(blocks)),
        out_shape=[jax.ShapeDtypeStruct((tile, width), jnp.bfloat16)] * many,
        in_specs=[SMEM] + [VMEM] * (1 + len(blocks)),
        out_specs=[VMEM] * many,
        scratch_shapes=[pltpu.VMEM((len(blocks), tile, width), jnp.bfloat16)],
        compiler_params=LIMIT,
        name="partials",
    )(sources, wide, *blocks)


def swap(value, axis, j):
    return lax.ppermute(value, axis, [(i, i ^ j) for i in range(lax.axis_size(axis))])


def swaps_of(values, axis, steps):
    return [swap(value, axis, j) for value, j in zip(values, steps)]


def dense_kernel(n_part, weight_ref, cot_ref, placing_ref, *refs):
    part_refs, packed_ref, term_refs, term = refs[:n_part], refs[n_part], refs[n_part + 1 : -1], refs[-1]
    rep = lax.axis_index("rep")
    agg_b = sum(ref[...].astype(jnp.float32) for ref in part_refs).astype(jnp.bfloat16)
    pre = jnp.dot(agg_b, weight_ref[...], preferred_element_type=jnp.float32)
    sig = jax.nn.sigmoid(pre)
    factor = sig * (1.0 + pre * (1.0 - sig))
    grad_pre = (cot_ref[...].astype(jnp.float32) * factor).astype(jnp.bfloat16)
    whole = lax.dot_general(
        agg_b, grad_pre, (((0,), (0,)), ((), ())), preferred_element_type=jnp.float32
    )
    term[...] = whole.reshape(term.shape)
    for j, ref in enumerate(term_refs):
        ref[...] = term[rep ^ j].astype(jnp.bfloat16)
    output = (pre * sig).astype(jnp.bfloat16)
    packed_ref[...] = jnp.dot(placing_ref[...], output, preferred_element_type=jnp.float32).astype(
        jnp.bfloat16
    )


def dense(parts, weight, cotangent, placing):
    places, width = placing.shape[0], weight.shape[0]
    n_rep = len(parts)
    rows = width // n_rep
    return pl.pallas_call(
        functools.partial(dense_kernel, n_rep),
        out_shape=[jax.ShapeDtypeStruct((places, width), jnp.bfloat16)]
        + [jax.ShapeDtypeStruct((rows, width), jnp.bfloat16)] * n_rep,
        in_specs=[VMEM] * (3 + n_rep),
        out_specs=[VMEM] * (1 + n_rep),
        scratch_shapes=[pltpu.VMEM((n_rep, rows, width), jnp.float32)],
        compiler_params=LIMIT,
        name="dense",
    )(weight, cotangent, placing, *parts)


def add_kernel(*refs):
    total = sum(ref[...].astype(jnp.float32) for ref in refs[:-1])
    refs[-1][...] = total.astype(refs[-1].dtype)


def add(terms):
    return pl.pallas_call(
        add_kernel,
        out_shape=jax.ShapeDtypeStruct(terms[0].shape, jnp.bfloat16),
        in_specs=[VMEM] * len(terms),
        out_specs=VMEM,
        compiler_params=LIMIT,
        name="add",
    )(*terms)


def place_kernel(*refs):
    rep = lax.axis_index("rep")
    for j, ref in enumerate(refs[:-1]):
        refs[-1][rep ^ j] = ref[...].astype(jnp.float32)


def place(chunks):
    rows, width = chunks[0].shape
    return pl.pallas_call(
        place_kernel,
        out_shape=jax.ShapeDtypeStruct((len(chunks), rows, width), jnp.float32),
        in_specs=[VMEM] * len(chunks),
        out_specs=VMEM,
        compiler_params=LIMIT,
        name="place",
    )(*chunks)


def gather_blocks(features, axis, ready):
    n = lax.axis_size(axis)
    blocks = [None] * n
    blocks[0] = features
    for j in range(2, n, 2):
        blocks[j] = swap(features, axis, j)
    blocks[1] = swap(features, axis, 1)
    blocks[2::2], ready = lax.optimization_barrier((blocks[2::2], ready))
    for j in range(2, n, 2):
        blocks[j + 1] = swap(blocks[j], axis, 1)
    return blocks, ready


def pair_kernel(mine_ref, other_ref, *out_refs):
    for j, ref in enumerate(out_refs):
        ref[0] = mine_ref[j]
        ref[1] = other_ref[j]


def pair(mine, other):
    chips = mine.shape[0]
    return pl.pallas_call(
        pair_kernel,
        out_shape=[jax.ShapeDtypeStruct((2,) + mine.shape[1:], jnp.bfloat16)] * chips,
        in_specs=[VMEM] * 2,
        out_specs=[VMEM] * chips,
        compiler_params=LIMIT,
        name="pair",
    )(mine, other)


def unpack_kernel(*refs):
    section = lax.axis_index("section")
    for j, ref in enumerate(refs[:-1]):
        for i in range(2):
            refs[-1][section ^ (2 * j + i)] = ref[i]


def unpack(pairs):
    return pl.pallas_call(
        unpack_kernel,
        out_shape=jax.ShapeDtypeStruct((2 * len(pairs),) + pairs[0].shape[1:], jnp.bfloat16),
        in_specs=[VMEM] * len(pairs),
        out_specs=VMEM,
        compiler_params=LIMIT,
        name="unpack",
    )(*pairs)


def relay(packed, axis):
    chips = packed.shape[0] // 2
    pairs = list(pair(packed[:chips], swap(packed[chips:], axis, 1)))
    return unpack(pairs[:1] + [swap(pairs[j], axis, 2 * j) for j in range(1, chips)])


def per_device(features, adj_tiles, adj_src, cotangent, weight, destination):
    n_section, n_rep = lax.axis_size("section"), lax.axis_size("rep")
    rows_here, width = features.shape
    tile = adj_tiles.shape[3]
    slots = max(2, 2 * rows_here // n_section)
    target = destination.reshape(1, rows_here)
    wide, own, placing = prepare(adj_tiles[:, 0], features, target, n_section * slots, slots)
    blocks, (wide, own, placing) = gather_blocks(features, "section", (wide, own, placing))
    parts = list(partials(adj_src[:, 0], wide, [own] + blocks[1:]))
    across = range(1, n_rep)
    parts = parts[:1] + swaps_of(parts[1:], "rep", across)
    packed, *terms = dense(parts, weight, cotangent, placing)
    received = relay(packed.reshape(n_section, slots, width), "section")
    relaid = received.reshape(1, 1, n_section, slots, width)
    chunk = add(terms[:1] + swaps_of(terms[1:], "rep", across))
    chunk = add([chunk] + [swap(chunk, "section", j) for j in range(2, n_section, 2)])
    chunk = add([chunk, swap(chunk, "section", 1)])
    weight_grad = place([chunk] + [swap(chunk, "rep", j) for j in across])
    return (relaid, weight_grad.reshape(width, width))


def solution(mesh):
    placed = (
        P(("section", "rep"), None),
        P("section", "rep", None, None, None),
        P("section", "rep", None),
        P(("section", "rep"), None),
        P(),
        P(("section", "rep"), None),
    )
    return jax.shard_map(
        per_device,
        mesh=mesh,
        in_specs=placed,
        out_specs=(P("section", "rep", None, None, None), P()),
        check_vma=False,
    )
```

time: 60.5 us -> 49 us (0.81)
  waiting for transfers between devices: 27.3 us -> 16.4 us
  starting transfers between devices: 15.2 us -> 26 us
  blocking collectives: 10.3 us -> 0 us
  local copies, waits for them, and re-layouts: 3.86 us -> 2.56 us
  Pallas kernels: 2 us -> 3.01 us
  other arithmetic: 0.76 us -> 0 us
    ppermute x10 -> x24, starting transfers between devices: 9.24 us -> 26 us  [swap(): lax.ppermute(value, axis, [(i, i ^ j) for i in range(lax.axis_size(axis))])]
    all_to_all x2 -> x0, waiting for transfers between devices: 15.1 us -> none  [the longest x1 8.4 us: per_device(): lax.all_to_all(spread, both, split_axis=0, concat_axis=0, tiled=True)]
    all_to_all x1 -> x0, blocking collectives: 10.3 us -> none  [per_device(): lax.all_to_all(chunks, both, split_axis=0, concat_axis=0, tiled=True)]
    all_to_all x2 -> x0, starting transfers between devices: 5.95 us -> none  [the longest x1 3.37 us: per_device(): lax.all_to_all(packed, 'section', split_axis=0, concat_axis=0, tiled=True)]
    ppermute x10 -> x24, waiting for transfers between devices: 12.2 us -> 16.4 us  [swap(): lax.ppermute(value, axis, [(i, i ^ j) for i in range(lax.axis_size(axis))])]
    pallas_call x1 -> x8, Pallas kernels: 1.08 us -> 2.1 us  [the longest x1 0.73 us: place(): pl.pallas_call(place_kernel, out_shape=jax.ShapeDtypeStruct((len(chunks),...]
    convert_element_type x1 -> x0, other arithmetic: 0.72 us -> none  [per_device(): return (relaid, weight_grad.reshape(width, width).astype(jnp.float32))]
    broadcast_in_dim x1 -> x0, local copies, waits for them, and re-layouts: 0.66 us -> none  [per_device(): spread = jnp.broadcast_to(mine, chunks.shape)]
  transfers between devices with their start and end apart: 12 -> 24, of which waited for: 9 -> 16; matrix products, arithmetic and copies ran while one was open for 0% -> 0% of each run, Pallas kernels for 0% -> 2%
where the time goes in v3:
time: 49 us; the launch traced here: 48.8 us
  starting transfers between devices  26 us (53%)
  waiting for transfers between devices  16.4 us (33%)
  Pallas kernels  3.01 us (6%)
  local copies, waits for them, and re-layouts  2.56 us (5%)
  between operations  0.74 us (2%)
    ppermute x24, starting transfers between devices, swap(): lax.ppermute(value, axis, [(i, i ^ j) for i in range(lax.axis_size(axis))])  26 us
    ppermute x24, waiting for transfers between devices, swap(): lax.ppermute(value, axis, [(i, i ^ j) for i in range(lax.axis_size(axis))])  16.4 us
    unnamed x12, local copies, waits for them, and re-layouts  2.55 us
  transfers between devices with their start and end apart: 24, of which 16 were waited for; matrix products, arithmetic and copies ran while one was open for 0% of the time, Pallas kernels for 2%

profile of v3, /device:TPU:0, one launch (start us, length us, event | category | flops | bytes accessed | tf_op | source)
XLA Modules:
  0.0 48.8 jit_solution(7190885107131589461)
XLA Ops:
  0.6 5.1 %collective-permute-start.2 = (bf16[128,256]{1,0:T(8,128)(2,1)}, bf16[128,256]{1,0:T(8,128)(2,1)S(1)}, u32[]{:S(2)}, u32[]{:S(2)}) collective-permute-start(bf16[128,256]{1,0:T(8,128)(2,1)} %own_ref.1), channel_id=1, source_target_pairs={{0,24},{4,28},{8,16},{12,20},{16,8},{20,12},{24,0},{28,4},{1,25},{... | collective-permute-start | bytes 196616 | tf_op jit(solution)/shard_map/ppermute | solution.py:83
  5.7 0.0 collective-permute-start.1
  5.7 0.6 %collective-permute-start = (bf16[128,256]{1,0:T(8,128)(2,1)}, bf16[128,256]{1,0:T(8,128)(2,1)S(1)}, u32[]{:S(2)}, u32[]{:S(2)}) collective-permute-start(bf16[128,256]{1,0:T(8,128)(2,1)} %own_ref.1), channel_id=1, source_target_pairs={{0,8},{4,12},{8,0},{12,4},{16,24},{20,28},{24,16},{28,20},{1,9},{5... | collective-permute-start | bytes 196616 | tf_op jit(solution)/shard_map/ppermute | solution.py:83
  6.4 0.0 collective-permute-start.3
  6.4 0.7 %copy-done.5 = s32[128,1]{0,1:T(1,128)S(1)} copy-done((s32[128,1]{0,1:T(1,128)S(1)}, s32[128,1]{0,1:T(1,128)}, u32[]{:S(2)}) %copy-start.5) | copy-done | bytes 536
  7.0 1.0 %copy-done = bf16[4,1,4,128,128]{4,3,2,1,0:T(8,128)(2,1)S(1)} copy-done((bf16[4,1,4,128,128]{4,3,2,1,0:T(8,128)(2,1)S(1)}, bf16[4,1,4,128,128]{4,3,2,1,0:T(8,128)(2,1)}, u32[]{:S(2)}) %copy-start) | copy-done | bytes 524312
  8.1 0.8 %copy-done.2 = bf16[128,256]{1,0:T(8,128)(2,1)S(1)} copy-done((bf16[128,256]{1,0:T(8,128)(2,1)S(1)}, bf16[128,256]{1,0:T(8,128)(2,1)}, u32[]{:S(2)}) %copy-start.2) | copy-done | bytes 65560
  8.9 0.2 prepare.1
  9.2 2.4 %collective-permute-done.1.refs_4_ = bf16[128,256]{1,0:T(8,128)(2,1)S(1)} collective-permute-done((bf16[128,256]{1,0:T(8,128)(2,1)}, bf16[128,256]{1,0:T(8,128)(2,1)S(1)}, u32[]{:S(2)}, u32[]{:S(2)}) %collective-permute-start.1) | collective-permute-done | bytes 65568 | tf_op jit(solution)/shard_map/ppermute | solution.py:83
  11.6 0.5 %collective-permute-start.5 = (bf16[128,256]{1,0:T(8,128)(2,1)S(1)}, bf16[128,256]{1,0:T(8,128)(2,1)S(1)}, u32[]{:S(2)}, u32[]{:S(2)}) collective-permute-start(bf16[128,256]{1,0:T(8,128)(2,1)S(1)} %collective-permute-done.1.refs_4_), channel_id=1, source_target_pairs={{0,4},{4,0},{8,12},{12,8},{16,20},{20,16},{24,28},{28,24},{1,5},{5... | collective-permute-start | bytes 196616 | tf_op jit(solution)/shard_map/ppermute | solution.py:83
  12.1 0.1 collective-permute-start.6
  12.1 0.0 collective-permute-done.3.refs_1_
  12.1 0.7 %collective-permute-done.4.refs_3_ = bf16[128,256]{1,0:T(8,128)(2,1)S(1)} collective-permute-done((bf16[128,256]{1,0:T(8,128)(2,1)S(1)}, bf16[128,256]{1,0:T(8,128)(2,1)S(1)}, u32[]{:S(2)}, u32[]{:S(2)}) %collective-permute-start.4) | collective-permute-done | bytes 65568 | tf_op jit(solution)/shard_map/ppermute | solution.py:83
  12.8 0.2 collective-permute-done.5.refs_5_
  13.0 0.4 collective-permute-done.6.refs_7_
  13.3 0.9 %partials.1 = (bf16[128,256]{1,0:T(8,128)(2,1)S(1)}, bf16[128,256]{1,0:T(8,128)(2,1)S(1)}, bf16[128,256]{1,0:T(8,128)(2,1)S(1)}, bf16[128,256]{1,0:T(8,128)(2,1)S(1)}) custom-call(s32[4,4]{1,0:T(4,128)S(1)} %bitcast.9, bf16[4,128,512]{2,1,0:T(8,128)(2,1)S(1)} %get-tuple-element.28.wide_ref, bf16[128,256]{1,0:T(8,128)(2,1)S(1)} %get-tuple-element.29.refs_0_, ...), custom_call_target="tpu_custom_call" | custom-call | tf_op jit(solution)/shard_map/partials/pallas_call | solution.py:71
  14.3 1.6 %collective-permute-start.7 = (bf16[128,256]{1,0:T(8,128)(2,1)S(1)}, bf16[128,256]{1,0:T(8,128)(2,1)S(1)}, u32[]{:S(2)}, u32[]{:S(2)}) collective-permute-start(bf16[128,256]{1,0:T(8,128)(2,1)S(1)} %get-tuple-element.34), channel_id=1, source_target_pairs={{0,1},{1,0},{2,3},{3,2},{4,5},{5,4},{6,7},{7,6},{8,9},{9,8},{10,11... | collective-permute-start | bytes 196616 | tf_op jit(solution)/shard_map/ppermute | solution.py:83
  15.8 1.5 %collective-permute-start.8 = (bf16[128,256]{1,0:T(8,128)(2,1)S(1)}, bf16[128,256]{1,0:T(8,128)(2,1)S(1)}, u32[]{:S(2)}, u32[]{:S(2)}) collective-permute-start(bf16[128,256]{1,0:T(8,128)(2,1)S(1)} %get-tuple-element.35), channel_id=1, source_target_pairs={{0,2},{1,3},{2,0},{3,1},{4,6},{5,7},{6,4},{7,5},{8,10},{9,11},{10,... | collective-permute-start | bytes 196616 | tf_op jit(solution)/shard_map/ppermute | solution.py:83
  17.3 0.5 collective-permute-start.9
  17.8 0.8 %collective-permute-done.7.refs_1_ = bf16[128,256]{1,0:T(8,128)(2,1)S(1)} collective-permute-done((bf16[128,256]{1,0:T(8,128)(2,1)S(1)}, bf16[128,256]{1,0:T(8,128)(2,1)S(1)}, u32[]{:S(2)}, u32[]{:S(2)}) %collective-permute-start.7) | collective-permute-done | bytes 65568 | tf_op jit(solution)/shard_map/ppermute | solution.py:83
  18.6 1.5 %collective-permute-done.8.refs_2_ = bf16[128,256]{1,0:T(8,128)(2,1)S(1)} collective-permute-done((bf16[128,256]{1,0:T(8,128)(2,1)S(1)}, bf16[128,256]{1,0:T(8,128)(2,1)S(1)}, u32[]{:S(2)}, u32[]{:S(2)}) %collective-permute-start.8) | collective-permute-done | bytes 65568 | tf_op jit(solution)/shard_map/ppermute | solution.py:83
  20.1 2.4 %collective-permute-done.9.refs_3_ = bf16[128,256]{1,0:T(8,128)(2,1)S(1)} collective-permute-done((bf16[128,256]{1,0:T(8,128)(2,1)S(1)}, bf16[128,256]{1,0:T(8,128)(2,1)S(1)}, u32[]{:S(2)}, u32[]{:S(2)}) %collective-permute-start.9) | collective-permute-done | bytes 65568 | tf_op jit(solution)/shard_map/ppermute | solution.py:83
  22.5 0.4 dense.1
  22.9 0.6 %collective-permute-start.14 = (bf16[64,256]{1,0:T(8,128)(2,1)S(1)}, bf16[64,256]{1,0:T(8,128)(2,1)S(1)}, u32[]{:S(2)}, u32[]{:S(2)}) collective-permute-start(bf16[64,256]{1,0:T(8,128)(2,1)S(1)} %get-tuple-element.43), channel_id=1, source_target_pairs={{0,1},{1,0},{2,3},{3,2},{4,5},{5,4},{6,7},{7,6},{8,9},{9,8},{10,11... | collective-permute-start | bytes 98312 | tf_op jit(solution)/shard_map/ppermute | solution.py:83
  23.5 0.5 %collective-permute-start.15 = (bf16[64,256]{1,0:T(8,128)(2,1)S(1)}, bf16[64,256]{1,0:T(8,128)(2,1)S(1)}, u32[]{:S(2)}, u32[]{:S(2)}) collective-permute-start(bf16[64,256]{1,0:T(8,128)(2,1)S(1)} %get-tuple-element.44), channel_id=1, source_target_pairs={{0,2},{1,3},{2,0},{3,1},{4,6},{5,7},{6,4},{7,5},{8,10},{9,11},{10,... | collective-permute-start | bytes 98312 | tf_op jit(solution)/shard_map/ppermute | solution.py:83
  24.1 2.4 %collective-permute-start.16 = (bf16[64,256]{1,0:T(8,128)(2,1)S(1)}, bf16[64,256]{1,0:T(8,128)(2,1)S(1)}, u32[]{:S(2)}, u32[]{:S(2)}) collective-permute-start(bf16[64,256]{1,0:T(8,128)(2,1)S(1)} %get-tuple-element.45), channel_id=1, source_target_pairs={{0,3},{1,2},{2,1},{3,0},{4,7},{5,6},{6,5},{7,4},{8,11},{9,10},{10,... | collective-permute-start | bytes 98312 | tf_op jit(solution)/shard_map/ppermute | solution.py:83
  26.5 0.1 collective-permute-start.10
  26.6 0.3 collective-permute-done.14.refs_1_
  26.9 0.5 %collective-permute-done.15.refs_2_ = bf16[64,256]{1,0:T(8,128)(2,1)S(1)} collective-permute-done((bf16[64,256]{1,0:T(8,128)(2,1)S(1)}, bf16[64,256]{1,0:T(8,128)(2,1)S(1)}, u32[]{:S(2)}, u32[]{:S(2)}) %collective-permute-start.15) | collective-permute-done | bytes 32800 | tf_op jit(solution)/shard_map/ppermute | solution.py:83
  27.5 1.4 %collective-permute-done.16.refs_3_ = bf16[64,256]{1,0:T(8,128)(2,1)S(1)} collective-permute-done((bf16[64,256]{1,0:T(8,128)(2,1)S(1)}, bf16[64,256]{1,0:T(8,128)(2,1)S(1)}, u32[]{:S(2)}, u32[]{:S(2)}) %collective-permute-start.16) | collective-permute-done | bytes 32800 | tf_op jit(solution)/shard_map/ppermute | solution.py:83
  28.9 2.8 %collective-permute-start.19 = (bf16[64,256]{1,0:T(8,128)(2,1)S(1)}, bf16[64,256]{1,0:T(8,128)(2,1)S(1)}, u32[]{:S(2)}, u32[]{:S(2)}) collective-permute-start(bf16[64,256]{1,0:T(8,128)(2,1)S(1)} %add.3.refs_0_), channel_id=1, source_target_pairs={{0,24},{4,28},{8,16},{12,20},{16,8},{20,12},{24,0},{28,4},{1,25},{... | collective-permute-start | bytes 98312 | tf_op jit(solution)/shard_map/ppermute | solution.py:83
  31.7 0.0 collective-permute-start.18
  31.7 1.7 %collective-permute-start.17 = (bf16[64,256]{1,0:T(8,128)(2,1)S(1)}, bf16[64,256]{1,0:T(8,128)(2,1)S(1)}, u32[]{:S(2)}, u32[]{:S(2)}) collective-permute-start(bf16[64,256]{1,0:T(8,128)(2,1)S(1)} %add.3.refs_0_), channel_id=1, source_target_pairs={{0,8},{4,12},{8,0},{12,4},{16,24},{20,28},{24,16},{28,20},{1,9},{5... | collective-permute-start | bytes 98312 | tf_op jit(solution)/shard_map/ppermute | solution.py:83
  33.3 1.7 %collective-permute-done.19.refs_3_ = bf16[64,256]{1,0:T(8,128)(2,1)S(1)} collective-permute-done((bf16[64,256]{1,0:T(8,128)(2,1)S(1)}, bf16[64,256]{1,0:T(8,128)(2,1)S(1)}, u32[]{:S(2)}, u32[]{:S(2)}) %collective-permute-start.19) | collective-permute-done | bytes 32800 | tf_op jit(solution)/shard_map/ppermute | solution.py:83
  35.0 1.5 %collective-permute-done.18.refs_2_ = bf16[64,256]{1,0:T(8,128)(2,1)S(1)} collective-permute-done((bf16[64,256]{1,0:T(8,128)(2,1)S(1)}, bf16[64,256]{1,0:T(8,128)(2,1)S(1)}, u32[]{:S(2)}, u32[]{:S(2)}) %collective-permute-start.18) | collective-permute-done | bytes 32800 | tf_op jit(solution)/shard_map/ppermute | solution.py:83
  36.5 0.1 collective-permute-start.20
  36.6 0.8 %collective-permute-start.11 = (bf16[2,32,256]{2,1,0:T(8,128)(2,1)S(1)}, bf16[2,32,256]{2,1,0:T(8,128)(2,1)S(1)}, u32[]{:S(2)}, u32[]{:S(2)}) collective-permute-start(bf16[2,32,256]{2,1,0:T(8,128)(2,1)S(1)} %get-tuple-element.39), channel_id=1, source_target_pairs={{0,8},{4,12},{8,0},{12,4},{16,24},{20,28},{24,16},{28,20},{1,9},{5... | collective-permute-start | bytes 98312 | tf_op jit(solution)/shard_map/ppermute | solution.py:83
  37.5 1.6 %collective-permute-start.12 = (bf16[2,32,256]{2,1,0:T(8,128)(2,1)S(1)}, bf16[2,32,256]{2,1,0:T(8,128)(2,1)S(1)}, u32[]{:S(2)}, u32[]{:S(2)}) collective-permute-start(bf16[2,32,256]{2,1,0:T(8,128)(2,1)S(1)} %get-tuple-element.40), channel_id=1, source_target_pairs={{0,16},{4,20},{8,24},{12,28},{16,0},{20,4},{24,8},{28,12},{1,17},{... | collective-permute-start | bytes 98312 | tf_op jit(solution)/shard_map/ppermute | solution.py:83
  39.0 2.0 %collective-permute-start.13 = (bf16[2,32,256]{2,1,0:T(8,128)(2,1)S(1)}, bf16[2,32,256]{2,1,0:T(8,128)(2,1)S(1)}, u32[]{:S(2)}, u32[]{:S(2)}) collective-permute-start(bf16[2,32,256]{2,1,0:T(8,128)(2,1)S(1)} %get-tuple-element.41), channel_id=1, source_target_pairs={{0,24},{4,28},{8,16},{12,20},{16,8},{20,12},{24,0},{28,4},{1,25},{... | collective-permute-start | bytes 98312 | tf_op jit(solution)/shard_map/ppermute | solution.py:83
  41.1 2.5 %collective-permute-start.23 = (bf16[64,256]{1,0:T(8,128)(2,1)S(1)}, bf16[64,256]{1,0:T(8,128)(2,1)S(1)}, u32[]{:S(2)}, u32[]{:S(2)}) collective-permute-start(bf16[64,256]{1,0:T(8,128)(2,1)S(1)} %add.5.refs_0_), channel_id=1, source_target_pairs={{0,3},{1,2},{2,1},{3,0},{4,7},{5,6},{6,5},{7,4},{8,11},{9,10},{10,... | collective-permute-start | bytes 98312 | tf_op jit(solution)/shard_map/ppermute | solution.py:83
  43.6 0.5 %collective-permute-start.22 = (bf16[64,256]{1,0:T(8,128)(2,1)S(1)}, bf16[64,256]{1,0:T(8,128)(2,1)S(1)}, u32[]{:S(2)}, u32[]{:S(2)}) collective-permute-start(bf16[64,256]{1,0:T(8,128)(2,1)S(1)} %add.5.refs_0_), channel_id=1, source_target_pairs={{0,2},{1,3},{2,0},{3,1},{4,6},{5,7},{6,4},{7,5},{8,10},{9,11},{10,... | collective-permute-start | bytes 98312 | tf_op jit(solution)/shard_map/ppermute | solution.py:83
  44.1 0.5 %collective-permute-start.21 = (bf16[64,256]{1,0:T(8,128)(2,1)S(1)}, bf16[64,256]{1,0:T(8,128)(2,1)S(1)}, u32[]{:S(2)}, u32[]{:S(2)}) collective-permute-start(bf16[64,256]{1,0:T(8,128)(2,1)S(1)} %add.5.refs_0_), channel_id=1, source_target_pairs={{0,1},{1,0},{2,3},{3,2},{4,5},{5,4},{6,7},{7,6},{8,9},{9,8},{10,11... | collective-permute-start | bytes 98312 | tf_op jit(solution)/shard_map/ppermute | solution.py:83
  44.7 0.1 collective-permute-done.13.refs_3_
  44.7 0.7 %unpack.1 = bf16[8,32,256]{2,1,0:T(8,128)(2,1)} custom-call(bf16[2,32,256]{2,1,0:T(8,128)(2,1)S(1)} %get-tuple-element.38.refs_0_, bf16[2,32,256]{2,1,0:T(8,128)(2,1)S(1)} %collective-permute-done.11.refs_1_, bf16[2,32,256]{2,1,0:T(8,128)(2,1)S(1)} %collective-permute-done.12.refs_2_, bf16[2,32,256]{2,1,0:T(8,128)(2,1)S(1)} %collective-permute-done.13.refs_3_), custom_call_target="tpu_custom_call" | custom-call | tf_op jit(solution)/shard_map/unpack/pallas_call | solution.py:199
  45.4 0.7 %collective-permute-done.23.refs_3_ = bf16[64,256]{1,0:T(8,128)(2,1)S(1)} collective-permute-done((bf16[64,256]{1,0:T(8,128)(2,1)S(1)}, bf16[64,256]{1,0:T(8,128)(2,1)S(1)}, u32[]{:S(2)}, u32[]{:S(2)}) %collective-permute-start.23) | collective-permute-done | bytes 32800 | tf_op jit(solution)/shard_map/ppermute | solution.py:83
  46.1 1.4 %collective-permute-done.22.refs_2_ = bf16[64,256]{1,0:T(8,128)(2,1)S(1)} collective-permute-done((bf16[64,256]{1,0:T(8,128)(2,1)S(1)}, bf16[64,256]{1,0:T(8,128)(2,1)S(1)}, u32[]{:S(2)}, u32[]{:S(2)}) %collective-permute-start.22) | collective-permute-done | bytes 32800 | tf_op jit(solution)/shard_map/ppermute | solution.py:83
  47.5 0.5 %collective-permute-done.21.refs_1_ = bf16[64,256]{1,0:T(8,128)(2,1)S(1)} collective-permute-done((bf16[64,256]{1,0:T(8,128)(2,1)S(1)}, bf16[64,256]{1,0:T(8,128)(2,1)S(1)}, u32[]{:S(2)}, u32[]{:S(2)}) %collective-permute-start.21) | collective-permute-done | bytes 32800 | tf_op jit(solution)/shard_map/ppermute | solution.py:83
  48.0 0.7 %place.1 = f32[4,64,256]{2,1,0:T(8,128)} custom-call(bf16[64,256]{1,0:T(8,128)(2,1)S(1)} %add.5.refs_0_, bf16[64,256]{1,0:T(8,128)(2,1)S(1)} %collective-permute-done.21.refs_1_, bf16[64,256]{1,0:T(8,128)(2,1)S(1)} %collective-permute-done.22.refs_2_, bf16[64,256]{1,0:T(8,128)(2,1)S(1)} %collective-permute-done.23.refs_3_), custom_call_target="tpu_custom_call" | custom-call | tf_op jit(solution)/shard_map/place/pallas_call | solution.py:150
  (22 shorter events, 0.1 us)
Async XLA Ops:
  0.6 8.5 %collective-permute-start.2 = (bf16[128,256]{1,0:T(8,128)(2,1)}, bf16[128,256]{1,0:T(8,128)(2,1)S(1)}, u32[]{:S(2)}, u32[]{:S(2)}) collective-permute-start(bf16[128,256]{1,0:T(8,128)(2,1)} %own_ref.1), channel_id=1, source_target_pairs={{0,24},{4,28},{8,16},{12,20},{16,8},{20,12},{24,0},{28,4},{1,25},{... | collective-permute-start | bytes 196616 | tf_op jit(solution)/shard_map/ppermute | solution.py:83
  5.7 5.8 %collective-permute-start.1 = (bf16[128,256]{1,0:T(8,128)(2,1)}, bf16[128,256]{1,0:T(8,128)(2,1)S(1)}, u32[]{:S(2)}, u32[]{:S(2)}) collective-permute-start(bf16[128,256]{1,0:T(8,128)(2,1)} %own_ref.1), channel_id=1, source_target_pairs={{0,16},{4,20},{8,24},{12,28},{16,0},{20,4},{24,8},{28,12},{1,17},{... | collective-permute-start | bytes 196616 | tf_op jit(solution)/shard_map/ppermute | solution.py:83
  5.7 5.8 %collective-permute-start = (bf16[128,256]{1,0:T(8,128)(2,1)}, bf16[128,256]{1,0:T(8,128)(2,1)S(1)}, u32[]{:S(2)}, u32[]{:S(2)}) collective-permute-start(bf16[128,256]{1,0:T(8,128)(2,1)} %own_ref.1), channel_id=1, source_target_pairs={{0,8},{4,12},{8,0},{12,4},{16,24},{20,28},{24,16},{28,20},{1,9},{5... | collective-permute-start | bytes 196616 | tf_op jit(solution)/shard_map/ppermute | solution.py:83
  6.4 5.8 %collective-permute-start.3 = (bf16[128,256]{1,0:T(8,128)(2,1)}, bf16[128,256]{1,0:T(8,128)(2,1)S(1)}, u32[]{:S(2)}, u32[]{:S(2)}) collective-permute-start(bf16[128,256]{1,0:T(8,128)(2,1)} %own_ref.1), channel_id=1, source_target_pairs={{0,4},{4,0},{8,12},{12,8},{16,20},{20,16},{24,28},{28,24},{1,5},{5... | collective-permute-start | bytes 196616 | tf_op jit(solution)/shard_map/ppermute | solution.py:83
  6.4 0.7 %copy-start.5 = (s32[128,1]{0,1:T(1,128)S(1)}, s32[128,1]{0,1:T(1,128)}, u32[]{:S(2)}) copy-start(s32[128,1]{0,1:T(1,128)} %param.11) | copy-start | bytes 1540
  7.0 1.0 %copy-start = (bf16[4,1,4,128,128]{4,3,2,1,0:T(8,128)(2,1)S(1)}, bf16[4,1,4,128,128]{4,3,2,1,0:T(8,128)(2,1)}, u32[]{:S(2)}) copy-start(bf16[4,1,4,128,128]{4,3,2,1,0:T(8,128)(2,1)} %param.7) | copy-start | bytes 1572868
  8.1 0.8 %copy-start.2 = (bf16[128,256]{1,0:T(8,128)(2,1)S(1)}, bf16[128,256]{1,0:T(8,128)(2,1)}, u32[]{:S(2)}) copy-start(bf16[128,256]{1,0:T(8,128)(2,1)} %own_ref.1) | copy-start | bytes 196612
  11.6 1.8 %copy-start.4 = (s32[4,1,4]{2,1,0:T(1,128)S(1)}, s32[4,1,4]{2,1,0:T(1,128)}, u32[]{:S(2)}) copy-start(s32[4,1,4]{2,1,0:T(1,128)} %param.8) | copy-start | bytes 196
  11.6 1.3 %collective-permute-start.4 = (bf16[128,256]{1,0:T(8,128)(2,1)S(1)}, bf16[128,256]{1,0:T(8,128)(2,1)S(1)}, u32[]{:S(2)}, u32[]{:S(2)}) collective-permute-start(bf16[128,256]{1,0:T(8,128)(2,1)S(1)} %collective-permute-done.refs_2_), channel_id=1, source_target_pairs={{0,4},{4,0},{8,12},{12,8},{16,20},{20,16},{24,28},{28,24},{1,5},{5... | collective-permute-start | bytes 196616 | tf_op jit(solution)/shard_map/ppermute | solution.py:83
  11.6 1.4 %collective-permute-start.5 = (bf16[128,256]{1,0:T(8,128)(2,1)S(1)}, bf16[128,256]{1,0:T(8,128)(2,1)S(1)}, u32[]{:S(2)}, u32[]{:S(2)}) collective-permute-start(bf16[128,256]{1,0:T(8,128)(2,1)S(1)} %collective-permute-done.1.refs_4_), channel_id=1, source_target_pairs={{0,4},{4,0},{8,12},{12,8},{16,20},{20,16},{24,28},{28,24},{1,5},{5... | collective-permute-start | bytes 196616 | tf_op jit(solution)/shard_map/ppermute | solution.py:83
  12.1 1.3 %collective-permute-start.6 = (bf16[128,256]{1,0:T(8,128)(2,1)S(1)}, bf16[128,256]{1,0:T(8,128)(2,1)S(1)}, u32[]{:S(2)}, u32[]{:S(2)}) collective-permute-start(bf16[128,256]{1,0:T(8,128)(2,1)S(1)} %collective-permute-done.2.refs_6_), channel_id=1, source_target_pairs={{0,4},{4,0},{8,12},{12,8},{16,20},{20,16},{24,28},{28,24},{1,5},{5... | collective-permute-start | bytes 196616 | tf_op jit(solution)/shard_map/ppermute | solution.py:83
  13.3 9.2 %copy-start.1 = (bf16[256,256]{1,0:T(8,128)(2,1)S(1)}, bf16[256,256]{1,0:T(8,128)(2,1)}, u32[]{:S(2)}) copy-start(bf16[256,256]{1,0:T(8,128)(2,1)} %weight_ref.1) | copy-start | bytes 393220
  13.3 9.2 %copy-start.3 = (bf16[128,256]{1,0:T(8,128)(2,1)S(1)}, bf16[128,256]{1,0:T(8,128)(2,1)}, u32[]{:S(2)}) copy-start(bf16[128,256]{1,0:T(8,128)(2,1)} %cot_ref.1) | copy-start | bytes 196612
  14.3 4.3 %collective-permute-start.7 = (bf16[128,256]{1,0:T(8,128)(2,1)S(1)}, bf16[128,256]{1,0:T(8,128)(2,1)S(1)}, u32[]{:S(2)}, u32[]{:S(2)}) collective-permute-start(bf16[128,256]{1,0:T(8,128)(2,1)S(1)} %get-tuple-element.34), channel_id=1, source_target_pairs={{0,1},{1,0},{2,3},{3,2},{4,5},{5,4},{6,7},{7,6},{8,9},{9,8},{10,11... | collective-permute-start | bytes 196616 | tf_op jit(solution)/shard_map/ppermute | solution.py:83
  15.8 4.3 %collective-permute-start.8 = (bf16[128,256]{1,0:T(8,128)(2,1)S(1)}, bf16[128,256]{1,0:T(8,128)(2,1)S(1)}, u32[]{:S(2)}, u32[]{:S(2)}) collective-permute-start(bf16[128,256]{1,0:T(8,128)(2,1)S(1)} %get-tuple-element.35), channel_id=1, source_target_pairs={{0,2},{1,3},{2,0},{3,1},{4,6},{5,7},{6,4},{7,5},{8,10},{9,11},{10,... | collective-permute-start | bytes 196616 | tf_op jit(solution)/shard_map/ppermute | solution.py:83
  17.3 5.2 %collective-permute-start.9 = (bf16[128,256]{1,0:T(8,128)(2,1)S(1)}, bf16[128,256]{1,0:T(8,128)(2,1)S(1)}, u32[]{:S(2)}, u32[]{:S(2)}) collective-permute-start(bf16[128,256]{1,0:T(8,128)(2,1)S(1)} %get-tuple-element.36), channel_id=1, source_target_pairs={{0,3},{1,2},{2,1},{3,0},{4,7},{5,6},{6,5},{7,4},{8,11},{9,10},{10,... | collective-permute-start | bytes 196616 | tf_op jit(solution)/shard_map/ppermute | solution.py:83
  22.9 4.0 %collective-permute-start.14 = (bf16[64,256]{1,0:T(8,128)(2,1)S(1)}, bf16[64,256]{1,0:T(8,128)(2,1)S(1)}, u32[]{:S(2)}, u32[]{:S(2)}) collective-permute-start(bf16[64,256]{1,0:T(8,128)(2,1)S(1)} %get-tuple-element.43), channel_id=1, source_target_pairs={{0,1},{1,0},{2,3},{3,2},{4,5},{5,4},{6,7},{7,6},{8,9},{9,8},{10,11... | collective-permute-start | bytes 98312 | tf_op jit(solution)/shard_map/ppermute | solution.py:83
  23.5 3.9 %collective-permute-start.15 = (bf16[64,256]{1,0:T(8,128)(2,1)S(1)}, bf16[64,256]{1,0:T(8,128)(2,1)S(1)}, u32[]{:S(2)}, u32[]{:S(2)}) collective-permute-start(bf16[64,256]{1,0:T(8,128)(2,1)S(1)} %get-tuple-element.44), channel_id=1, source_target_pairs={{0,2},{1,3},{2,0},{3,1},{4,6},{5,7},{6,4},{7,5},{8,10},{9,11},{10,... | collective-permute-start | bytes 98312 | tf_op jit(solution)/shard_map/ppermute | solution.py:83
  24.1 4.8 %collective-permute-start.16 = (bf16[64,256]{1,0:T(8,128)(2,1)S(1)}, bf16[64,256]{1,0:T(8,128)(2,1)S(1)}, u32[]{:S(2)}, u32[]{:S(2)}) collective-permute-start(bf16[64,256]{1,0:T(8,128)(2,1)S(1)} %get-tuple-element.45), channel_id=1, source_target_pairs={{0,3},{1,2},{2,1},{3,0},{4,7},{5,6},{6,5},{7,4},{8,11},{9,10},{10,... | collective-permute-start | bytes 98312 | tf_op jit(solution)/shard_map/ppermute | solution.py:83
  26.5 10.1 %collective-permute-start.10 = (bf16[4,32,256]{2,1,0:T(8,128)(2,1)S(1)}, bf16[4,32,256]{2,1,0:T(8,128)(2,1)S(1)}, u32[]{:S(2)}, u32[]{:S(2)}) collective-permute-start(bf16[4,32,256]{2,1,0:T(8,128)(2,1)S(1)} %bitcast.13), channel_id=1, source_target_pairs={{0,4},{4,0},{8,12},{12,8},{16,20},{20,16},{24,28},{28,24},{1,5},{5... | collective-permute-start | bytes 196616 | tf_op jit(solution)/shard_map/ppermute | solution.py:83
  28.9 6.1 %collective-permute-start.19 = (bf16[64,256]{1,0:T(8,128)(2,1)S(1)}, bf16[64,256]{1,0:T(8,128)(2,1)S(1)}, u32[]{:S(2)}, u32[]{:S(2)}) collective-permute-start(bf16[64,256]{1,0:T(8,128)(2,1)S(1)} %add.3.refs_0_), channel_id=1, source_target_pairs={{0,24},{4,28},{8,16},{12,20},{16,8},{20,12},{24,0},{28,4},{1,25},{... | collective-permute-start | bytes 98312 | tf_op jit(solution)/shard_map/ppermute | solution.py:83
  31.7 4.8 %collective-permute-start.18 = (bf16[64,256]{1,0:T(8,128)(2,1)S(1)}, bf16[64,256]{1,0:T(8,128)(2,1)S(1)}, u32[]{:S(2)}, u32[]{:S(2)}) collective-permute-start(bf16[64,256]{1,0:T(8,128)(2,1)S(1)} %add.3.refs_0_), channel_id=1, source_target_pairs={{0,16},{4,20},{8,24},{12,28},{16,0},{20,4},{24,8},{28,12},{1,17},{... | collective-permute-start | bytes 98312 | tf_op jit(solution)/shard_map/ppermute | solution.py:83
  31.7 4.8 %collective-permute-start.17 = (bf16[64,256]{1,0:T(8,128)(2,1)S(1)}, bf16[64,256]{1,0:T(8,128)(2,1)S(1)}, u32[]{:S(2)}, u32[]{:S(2)}) collective-permute-start(bf16[64,256]{1,0:T(8,128)(2,1)S(1)} %add.3.refs_0_), channel_id=1, source_target_pairs={{0,8},{4,12},{8,0},{12,4},{16,24},{20,28},{24,16},{28,20},{1,9},{5... | collective-permute-start | bytes 98312 | tf_op jit(solution)/shard_map/ppermute | solution.py:83
  36.5 4.6 %collective-permute-start.20 = (bf16[64,256]{1,0:T(8,128)(2,1)S(1)}, bf16[64,256]{1,0:T(8,128)(2,1)S(1)}, u32[]{:S(2)}, u32[]{:S(2)}) collective-permute-start(bf16[64,256]{1,0:T(8,128)(2,1)S(1)} %add.4.refs_0_), channel_id=1, source_target_pairs={{0,4},{4,0},{8,12},{12,8},{16,20},{20,16},{24,28},{28,24},{1,5},{5... | collective-permute-start | bytes 98312 | tf_op jit(solution)/shard_map/ppermute | solution.py:83
  36.6 7.5 %collective-permute-start.11 = (bf16[2,32,256]{2,1,0:T(8,128)(2,1)S(1)}, bf16[2,32,256]{2,1,0:T(8,128)(2,1)S(1)}, u32[]{:S(2)}, u32[]{:S(2)}) collective-permute-start(bf16[2,32,256]{2,1,0:T(8,128)(2,1)S(1)} %get-tuple-element.39), channel_id=1, source_target_pairs={{0,8},{4,12},{8,0},{12,4},{16,24},{20,28},{24,16},{28,20},{1,9},{5... | collective-permute-start | bytes 98312 | tf_op jit(solution)/shard_map/ppermute | solution.py:83
  37.5 7.2 %collective-permute-start.12 = (bf16[2,32,256]{2,1,0:T(8,128)(2,1)S(1)}, bf16[2,32,256]{2,1,0:T(8,128)(2,1)S(1)}, u32[]{:S(2)}, u32[]{:S(2)}) collective-permute-start(bf16[2,32,256]{2,1,0:T(8,128)(2,1)S(1)} %get-tuple-element.40), channel_id=1, source_target_pairs={{0,16},{4,20},{8,24},{12,28},{16,0},{20,4},{24,8},{28,12},{1,17},{... | collective-permute-start | bytes 98312 | tf_op jit(solution)/shard_map/ppermute | solution.py:83
  39.0 5.7 %collective-permute-start.13 = (bf16[2,32,256]{2,1,0:T(8,128)(2,1)S(1)}, bf16[2,32,256]{2,1,0:T(8,128)(2,1)S(1)}, u32[]{:S(2)}, u32[]{:S(2)}) collective-permute-start(bf16[2,32,256]{2,1,0:T(8,128)(2,1)S(1)} %get-tuple-element.41), channel_id=1, source_target_pairs={{0,24},{4,28},{8,16},{12,20},{16,8},{20,12},{24,0},{28,4},{1,25},{... | collective-permute-start | bytes 98312 | tf_op jit(solution)/shard_map/ppermute | solution.py:83
  41.1 5.0 %collective-permute-start.23 = (bf16[64,256]{1,0:T(8,128)(2,1)S(1)}, bf16[64,256]{1,0:T(8,128)(2,1)S(1)}, u32[]{:S(2)}, u32[]{:S(2)}) collective-permute-start(bf16[64,256]{1,0:T(8,128)(2,1)S(1)} %add.5.refs_0_), channel_id=1, source_target_pairs={{0,3},{1,2},{2,1},{3,0},{4,7},{5,6},{6,5},{7,4},{8,11},{9,10},{10,... | collective-permute-start | bytes 98312 | tf_op jit(solution)/shard_map/ppermute | solution.py:83
  43.6 3.9 %collective-permute-start.22 = (bf16[64,256]{1,0:T(8,128)(2,1)S(1)}, bf16[64,256]{1,0:T(8,128)(2,1)S(1)}, u32[]{:S(2)}, u32[]{:S(2)}) collective-permute-start(bf16[64,256]{1,0:T(8,128)(2,1)S(1)} %add.5.refs_0_), channel_id=1, source_target_pairs={{0,2},{1,3},{2,0},{3,1},{4,6},{5,7},{6,4},{7,5},{8,10},{9,11},{10,... | collective-permute-start | bytes 98312 | tf_op jit(solution)/shard_map/ppermute | solution.py:83
  44.1 3.9 %collective-permute-start.21 = (bf16[64,256]{1,0:T(8,128)(2,1)S(1)}, bf16[64,256]{1,0:T(8,128)(2,1)S(1)}, u32[]{:S(2)}, u32[]{:S(2)}) collective-permute-start(bf16[64,256]{1,0:T(8,128)(2,1)S(1)} %add.5.refs_0_), channel_id=1, source_target_pairs={{0,1},{1,0},{2,3},{3,2},{4,5},{5,4},{6,7},{7,6},{8,9},{9,8},{10,11... | collective-permute-start | bytes 98312 | tf_op jit(solution)/shard_map/ppermute | solution.py:83

commit v4 on v3

v4 whole, which is shorter than its diff:
```python
import functools

import jax
import jax.numpy as jnp
from jax import lax
from jax.experimental import pallas as pl
from jax.experimental.pallas import tpu as pltpu
from jax.sharding import PartitionSpec as P

VMEM = pl.BlockSpec(memory_space=pltpu.VMEM)
LIMIT = pltpu.CompilerParams(vmem_limit_bytes=32 * 1024 * 1024)
SMEM = pl.BlockSpec(memory_space=pltpu.SMEM)


def across(n):
    return list(range(n - 1, 0, -1))


def prepare_kernel(slots, tiles_ref, own_ref, target_ref, wide_ref, held_ref, placing_ref):
    many, depth = tiles_ref.shape[:2]
    for g in range(many):
        wide_ref[g] = jnp.concatenate([tiles_ref[g, k] for k in range(depth)], axis=1)
    held_ref[...] = own_ref[...]
    places, rows = placing_ref.shape
    n_section = places // slots
    target = target_ref[...]
    hits = lax.broadcasted_iota(jnp.int32, (n_section, rows), 0) == target
    hits = jnp.where(hits, 1.0, 0.0)
    earlier = lax.broadcasted_iota(jnp.int32, (rows, rows), 0) < lax.broadcasted_iota(
        jnp.int32, (rows, rows), 1
    )
    earlier = jnp.where(earlier, 1.0, 0.0).astype(jnp.bfloat16)
    before = jnp.dot(hits.astype(jnp.bfloat16), earlier, preferred_element_type=jnp.float32)
    slot = jnp.sum(before * hits, axis=0, keepdims=True).astype(jnp.int32)
    apart = target ^ lax.axis_index("section")
    position = ((apart & 1) * (n_section // 2) + (apart >> 1)) * slots + slot
    placing = lax.broadcasted_iota(jnp.int32, (places, rows), 0) == position
    placing_ref[...] = jnp.where(placing, 1.0, 0.0).astype(jnp.bfloat16)


def prepare(tiles, own, target, places, slots):
    many, depth, tile, _ = tiles.shape
    return pl.pallas_call(
        functools.partial(prepare_kernel, slots),
        out_shape=(
            jax.ShapeDtypeStruct((many, tile, depth * tile), jnp.bfloat16),
            jax.ShapeDtypeStruct(own.shape, jnp.bfloat16),
            jax.ShapeDtypeStruct((places, target.shape[1]), jnp.bfloat16),
        ),
        in_specs=[VMEM] * 3,
        out_specs=(VMEM,) * 3,
        compiler_params=LIMIT,
        cost_estimate=pl.CostEstimate(flops=0, bytes_accessed=2 * tiles.size * 2, transcendentals=0),
        name="prepare",
    )(tiles, own, target)


def partials_kernel(count, src_ref, wide_ref, *refs):
    block_refs, out_refs, held = refs[:count], refs[count:-1], refs[-1]
    depth = src_ref.shape[1]
    section, rep = lax.axis_index("section"), lax.axis_index("rep")
    for j in range(count):
        held[j] = block_refs[j][...]
    for j, out_ref in zip([0] + across(len(out_refs)), out_refs):
        g = rep ^ j
        right = jnp.concatenate([held[src_ref[g, k] ^ section] for k in range(depth)], axis=0)
        out_ref[...] = jnp.dot(wide_ref[g], right, preferred_element_type=jnp.float32).astype(
            jnp.bfloat16
        )


def partials(sources, wide, blocks):
    many = wide.shape[0]
    tile, width = blocks[0].shape
    return pl.pallas_call(
        functools.partial(partials_kernel, len(blocks)),
        out_shape=[jax.ShapeDtypeStruct((tile, width), jnp.bfloat16)] * many,
        in_specs=[SMEM] + [VMEM] * (1 + len(blocks)),
        out_specs=[VMEM] * many,
        scratch_shapes=[pltpu.VMEM((len(blocks), tile, width), jnp.bfloat16)],
        compiler_params=LIMIT,
        name="partials",
    )(sources, wide, *blocks)


def swap(value, axis, j):
    return lax.ppermute(value, axis, [(i, i ^ j) for i in range(lax.axis_size(axis))])


def tree_sum(terms):
    while len(terms) > 1:
        terms = [terms[i] + terms[i + 1] for i in range(0, len(terms), 2)]
    return terms[0]


def dense_kernel(
    n_part, weight_ref, cot_ref, placing_ref, *refs
):
    part_refs, (same_ref, kept_ref, sent_ref, term) = refs[:n_part], refs[n_part:]
    core = lax.axis_index("section") & 1
    agg_b = tree_sum([ref[...].astype(jnp.float32) for ref in part_refs]).astype(jnp.bfloat16)
    pre = jnp.dot(agg_b, weight_ref[...], preferred_element_type=jnp.float32)
    sig = jax.nn.sigmoid(pre)
    factor = sig * (1.0 + pre * (1.0 - sig))
    grad_pre = (cot_ref[...].astype(jnp.float32) * factor).astype(jnp.bfloat16)
    whole = lax.dot_general(
        agg_b, grad_pre, (((0,), (0,)), ((), ())), preferred_element_type=jnp.float32
    )
    term[...] = whole.reshape(term.shape)
    kept_ref[...] = term[core]
    output = (pre * sig).astype(jnp.bfloat16)
    packed = jnp.dot(placing_ref[...], output, preferred_element_type=jnp.float32)
    half = packed.shape[0] // 2
    same_ref[...] = packed[:half].astype(jnp.bfloat16)
    sent_ref[:half] = packed[half:].astype(jnp.bfloat16)
    sent_ref[half:] = term[1 - core].astype(jnp.bfloat16)


def dense(parts, weight, cotangent, placing):
    places, width = placing.shape[0], weight.shape[0]
    return pl.pallas_call(
        functools.partial(dense_kernel, len(parts)),
        out_shape=(
            jax.ShapeDtypeStruct((places // 2, width), jnp.bfloat16),
            jax.ShapeDtypeStruct((width // 2, width), jnp.float32),
            jax.ShapeDtypeStruct((places // 2 + width // 2, width), jnp.bfloat16),
        ),
        in_specs=[VMEM] * (3 + len(parts)),
        out_specs=(VMEM,) * 3,
        scratch_shapes=[pltpu.VMEM((2, width // 2, width), jnp.float32)],
        compiler_params=LIMIT,
        name="dense",
    )(weight, cotangent, placing, *parts)


def split_kernel(kept_ref, came_ref, own_ref, *refs):
    out_refs, term = refs[:-1], refs[-1]
    rep = lax.axis_index("rep")
    half = kept_ref.shape[0]
    total = kept_ref[...] + came_ref[came_ref.shape[0] - half :].astype(jnp.float32)
    term[...] = total.reshape(term.shape)
    own_ref[...] = term[rep]
    for ref, j in zip(out_refs, across(len(out_refs) + 1)):
        ref[...] = term[rep ^ j].astype(jnp.bfloat16)


def split(kept, came, n_rep):
    half, width = kept.shape
    rows = half // n_rep
    return pl.pallas_call(
        split_kernel,
        out_shape=[jax.ShapeDtypeStruct((rows, width), jnp.float32)]
        + [jax.ShapeDtypeStruct((rows, width), jnp.bfloat16)] * (n_rep - 1),
        in_specs=[VMEM] * 2,
        out_specs=[VMEM] * n_rep,
        scratch_shapes=[pltpu.VMEM((n_rep, rows, width), jnp.float32)],
        compiler_params=LIMIT,
        name="split",
    )(kept, came)


def message_kernel(n_term, slots, same_ref, came_ref, *refs):
    term_refs, out_refs = refs[:n_term], refs[n_term:]
    chunk = sum(ref[...].astype(jnp.float32) for ref in term_refs).astype(jnp.bfloat16)
    for j, ref in zip([0] + across(len(out_refs)), out_refs):
        ref[:slots] = same_ref[j * slots : (j + 1) * slots]
        ref[slots : 2 * slots] = came_ref[j * slots : (j + 1) * slots]
        ref[2 * slots :] = chunk


def message(same, came, terms, slots):
    chips = same.shape[0] // slots
    rows, width = terms[0].shape
    return pl.pallas_call(
        functools.partial(message_kernel, len(terms), slots),
        out_shape=[jax.ShapeDtypeStruct((2 * slots + rows, width), jnp.bfloat16)] * chips,
        in_specs=[VMEM] * (2 + len(terms)),
        out_specs=[VMEM] * chips,
        compiler_params=LIMIT,
        name="message",
    )(same, came, *terms)


def chunk_kernel(start, *refs):
    by_xor = [refs[0]] + [None] * (len(refs) - 2)
    for ref, j in zip(refs[1:-1], across(len(by_xor))):
        by_xor[j] = ref
    total = tree_sum([ref[start:].astype(jnp.float32) for ref in by_xor])
    refs[-1][...] = total.astype(jnp.bfloat16)


def chunk_of(messages, start):
    rows, width = messages[0].shape
    return pl.pallas_call(
        functools.partial(chunk_kernel, start),
        out_shape=jax.ShapeDtypeStruct((rows - start, width), jnp.bfloat16),
        in_specs=[VMEM] * len(messages),
        out_specs=VMEM,
        compiler_params=LIMIT,
        name="chunk",
    )(*messages)


def unpack_kernel(slots, *refs):
    section = lax.axis_index("section")
    for j, ref in zip([0] + across(len(refs) - 1), refs[:-1]):
        refs[-1][section ^ (2 * j)] = ref[:slots]
        refs[-1][section ^ (2 * j + 1)] = ref[slots : 2 * slots]


def unpack(messages, slots):
    width = messages[0].shape[1]
    return pl.pallas_call(
        functools.partial(unpack_kernel, slots),
        out_shape=jax.ShapeDtypeStruct((2 * len(messages), slots, width), jnp.bfloat16),
        in_specs=[VMEM] * len(messages),
        out_specs=VMEM,
        compiler_params=LIMIT,
        name="unpack",
    )(*messages)


def place_kernel(*refs):
    rep = lax.axis_index("rep")
    for j, ref in zip([0] + across(len(refs) - 1), refs[:-1]):
        refs[-1][rep ^ j] = ref[...]


def place(chunks):
    rows, width = chunks[0].shape
    return pl.pallas_call(
        place_kernel,
        out_shape=jax.ShapeDtypeStruct((len(chunks), rows, width), jnp.bfloat16),
        in_specs=[VMEM] * len(chunks),
        out_specs=VMEM,
        compiler_params=LIMIT,
        name="place",
    )(*chunks)


def finish_kernel(own_ref, came_ref, out_ref):
    core = lax.axis_index("section") & 1
    out_ref[core] = own_ref[...].astype(jnp.float32)
    out_ref[1 - core] = came_ref[...].astype(jnp.float32)


def finish(own, came):
    return pl.pallas_call(
        finish_kernel,
        out_shape=jax.ShapeDtypeStruct((2,) + own.shape, jnp.float32),
        in_specs=[VMEM] * 2,
        out_specs=VMEM,
        compiler_params=LIMIT,
        name="finish",
    )(own, came)


def gather_blocks(features, axis, ready):
    n = lax.axis_size(axis)
    blocks = [None] * n
    blocks[0] = features
    for j in range(2, n, 2):
        blocks[j] = swap(features, axis, j)
    blocks[1] = swap(features, axis, 1)
    blocks[2::2], ready = lax.optimization_barrier((blocks[2::2], ready))
    for j in range(2, n, 2):
        blocks[j + 1] = swap(blocks[j], axis, 1)
    return blocks, ready


def per_device(features, adj_tiles, adj_src, cotangent, weight, destination):
    n_section, n_rep = lax.axis_size("section"), lax.axis_size("rep")
    rows_here, width = features.shape
    tile = adj_tiles.shape[3]
    slots = max(2, 2 * rows_here // n_section)
    target = destination.reshape(1, rows_here)
    wide, own, placing = prepare(adj_tiles[:, 0], features, target, n_section * slots, slots)
    blocks, (wide, own, placing) = gather_blocks(features, "section", (wide, own, placing))
    parts = list(partials(adj_src[:, 0], wide, [own] + blocks[1:]))
    others, chips = across(n_rep), across(n_section // 2)
    parts = [swap(part, "rep", j) if j else part for part, j in zip(parts, [0] + others)]
    parts = [parts[0]] + parts[:0:-1]
    same, kept, sent = dense(parts, weight, cotangent, placing)
    came = swap(sent, "section", 1)
    own, *terms = split(kept, came, n_rep)
    terms = [own] + [swap(term, "rep", j) for term, j in zip(terms, others)]
    messages = list(message(same, came, terms, slots))
    messages = messages[:1] + [swap(m, "section", 2 * j) for m, j in zip(messages[1:], chips)]
    chunk = chunk_of(messages, 2 * slots)
    relaid = unpack(messages, slots).reshape(1, 1, n_section, slots, width)
    half = place([chunk] + [swap(chunk, "rep", j) for j in others]).reshape(width // 2, width)
    weight_grad = finish(half, swap(half, "section", 1))
    return (relaid, weight_grad.reshape(width, width))


def solution(mesh):
    placed = (
        P(("section", "rep"), None),
        P("section", "rep", None, None, None),
        P("section", "rep", None),
        P(("section", "rep"), None),
        P(),
        P(("section", "rep"), None),
    )
    return jax.shard_map(
        per_device,
        mesh=mesh,
        in_specs=placed,
        out_specs=(P("section", "rep", None, None, None), P()),
        check_vma=False,
    )
```

time: 49 us -> 47 us (0.959)
  starting transfers between devices: 26 us -> 21.6 us
  waiting for transfers between devices: 16.4 us -> 18.9 us
    ppermute x24 -> x21, starting transfers between devices: 26 us -> 21.6 us  [swap(): lax.ppermute(value, axis, [(i, i ^ j) for i in range(lax.axis_size(axis))])]
    ppermute x24 -> x21, waiting for transfers between devices: 16.4 us -> 18.9 us  [swap(): lax.ppermute(value, axis, [(i, i ^ j) for i in range(lax.axis_size(axis))])]
    pallas_call x6, Pallas kernels: 1.15 us -> 1.9 us  [the longest x1 0.73 us: finish(): pl.pallas_call(finish_kernel, out_shape=jax.ShapeDtypeStruct((2,) + own.s...]
    pallas_call x1, Pallas kernels: 0.73 us -> 0.01 us  [place(): pl.pallas_call(place_kernel, out_shape=jax.ShapeDtypeStruct((len(chunks),...]
  transfers between devices with their start and end apart: 24 -> 21, of which waited for: 16 -> 16; matrix products, arithmetic and copies ran while one was open for 0% -> 0% of each run, Pallas kernels for 2% -> 2%
where the time goes in v4:
time: 47 us; the launch traced here: 46.8 us
  starting transfers between devices  21.6 us (46%)
  waiting for transfers between devices  18.9 us (40%)
  Pallas kernels  3.04 us (6%)
  local copies, waits for them, and re-layouts  2.55 us (5%)
  between operations  0.72 us (2%)
    ppermute x21, starting transfers between devices, swap(): lax.ppermute(value, axis, [(i, i ^ j) for i in range(lax.axis_size(axis))])  21.6 us
    ppermute x21, waiting for transfers between devices, swap(): lax.ppermute(value, axis, [(i, i ^ j) for i in range(lax.axis_size(axis))])  18.9 us
    unnamed x12, local copies, waits for them, and re-layouts  2.55 us
  transfers between devices with their start and end apart: 21, of which 16 were waited for; matrix products, arithmetic and copies ran while one was open for 0% of the time, Pallas kernels for 2%

profile of v4, /device:TPU:0, one launch (start us, length us, event | category | flops | bytes accessed | tf_op | source)
XLA Modules:
  0.0 46.8 jit_solution(5766498260841983287)
XLA Ops:
  0.6 5.1 %collective-permute-start.2 = (bf16[128,256]{1,0:T(8,128)(2,1)}, bf16[128,256]{1,0:T(8,128)(2,1)S(1)}, u32[]{:S(2)}, u32[]{:S(2)}) collective-permute-start(bf16[128,256]{1,0:T(8,128)(2,1)} %own_ref.1), channel_id=1, source_target_pairs={{0,24},{4,28},{8,16},{12,20},{16,8},{20,12},{24,0},{28,4},{1,25},{... | collective-permute-start | bytes 196616 | tf_op jit(solution)/shard_map/ppermute | solution.py:87
  5.7 0.0 collective-permute-start.1
  5.7 0.6 %collective-permute-start = (bf16[128,256]{1,0:T(8,128)(2,1)}, bf16[128,256]{1,0:T(8,128)(2,1)S(1)}, u32[]{:S(2)}, u32[]{:S(2)}) collective-permute-start(bf16[128,256]{1,0:T(8,128)(2,1)} %own_ref.1), channel_id=1, source_target_pairs={{0,8},{4,12},{8,0},{12,4},{16,24},{20,28},{24,16},{28,20},{1,9},{5... | collective-permute-start | bytes 196616 | tf_op jit(solution)/shard_map/ppermute | solution.py:87
  6.4 0.0 collective-permute-start.3
  6.4 0.7 %copy-done.5 = s32[128,1]{0,1:T(1,128)S(1)} copy-done((s32[128,1]{0,1:T(1,128)S(1)}, s32[128,1]{0,1:T(1,128)}, u32[]{:S(2)}) %copy-start.5) | copy-done | bytes 536
  7.0 1.0 %copy-done = bf16[4,1,4,128,128]{4,3,2,1,0:T(8,128)(2,1)S(1)} copy-done((bf16[4,1,4,128,128]{4,3,2,1,0:T(8,128)(2,1)S(1)}, bf16[4,1,4,128,128]{4,3,2,1,0:T(8,128)(2,1)}, u32[]{:S(2)}) %copy-start) | copy-done | bytes 524312
  8.1 0.8 %copy-done.2 = bf16[128,256]{1,0:T(8,128)(2,1)S(1)} copy-done((bf16[128,256]{1,0:T(8,128)(2,1)S(1)}, bf16[128,256]{1,0:T(8,128)(2,1)}, u32[]{:S(2)}) %copy-start.2) | copy-done | bytes 65560
  8.9 0.2 prepare.1
  9.2 0.0 collective-permute-done.2.refs_6_
  9.2 2.4 %collective-permute-done.1.refs_4_ = bf16[128,256]{1,0:T(8,128)(2,1)S(1)} collective-permute-done((bf16[128,256]{1,0:T(8,128)(2,1)}, bf16[128,256]{1,0:T(8,128)(2,1)S(1)}, u32[]{:S(2)}, u32[]{:S(2)}) %collective-permute-start.1) | collective-permute-done | bytes 65568 | tf_op jit(solution)/shard_map/ppermute | solution.py:87
  11.6 0.0 collective-permute-done.refs_2_
  11.6 0.5 %collective-permute-start.5 = (bf16[128,256]{1,0:T(8,128)(2,1)S(1)}, bf16[128,256]{1,0:T(8,128)(2,1)S(1)}, u32[]{:S(2)}, u32[]{:S(2)}) collective-permute-start(bf16[128,256]{1,0:T(8,128)(2,1)S(1)} %collective-permute-done.1.refs_4_), channel_id=1, source_target_pairs={{0,4},{4,0},{8,12},{12,8},{16,20},{20,16},{24,28},{28,24},{1,5},{5... | collective-permute-start | bytes 196616 | tf_op jit(solution)/shard_map/ppermute | solution.py:87
  12.1 0.1 collective-permute-start.6
  12.1 0.0 collective-permute-done.3.refs_1_
  12.1 0.7 %collective-permute-done.4.refs_3_ = bf16[128,256]{1,0:T(8,128)(2,1)S(1)} collective-permute-done((bf16[128,256]{1,0:T(8,128)(2,1)S(1)}, bf16[128,256]{1,0:T(8,128)(2,1)S(1)}, u32[]{:S(2)}, u32[]{:S(2)}) %collective-permute-start.4) | collective-permute-done | bytes 65568 | tf_op jit(solution)/shard_map/ppermute | solution.py:87
  12.8 0.2 collective-permute-done.5.refs_5_
  13.0 0.4 collective-permute-done.6.refs_7_
  13.3 0.9 %partials.1 = (bf16[128,256]{1,0:T(8,128)(2,1)S(1)}, bf16[128,256]{1,0:T(8,128)(2,1)S(1)}, bf16[128,256]{1,0:T(8,128)(2,1)S(1)}, bf16[128,256]{1,0:T(8,128)(2,1)S(1)}) custom-call(s32[4,4]{1,0:T(4,128)S(1)} %bitcast.9, bf16[4,128,512]{2,1,0:T(8,128)(2,1)S(1)} %get-tuple-element.30.wide_ref, bf16[128,256]{1,0:T(8,128)(2,1)S(1)} %get-tuple-element.31.refs_0_, ...), custom_call_target="tpu_custom_call" | custom-call | tf_op jit(solution)/shard_map/partials/pallas_call | solution.py:75
  14.3 1.6 %collective-permute-start.7 = (bf16[128,256]{1,0:T(8,128)(2,1)S(1)}, bf16[128,256]{1,0:T(8,128)(2,1)S(1)}, u32[]{:S(2)}, u32[]{:S(2)}) collective-permute-start(bf16[128,256]{1,0:T(8,128)(2,1)S(1)} %get-tuple-element.36), channel_id=1, source_target_pairs={{0,1},{1,0},{2,3},{3,2},{4,5},{5,4},{6,7},{7,6},{8,9},{9,8},{10,11... | collective-permute-start | bytes 196616 | tf_op jit(solution)/shard_map/ppermute | solution.py:87
  15.8 1.5 %collective-permute-start.8 = (bf16[128,256]{1,0:T(8,128)(2,1)S(1)}, bf16[128,256]{1,0:T(8,128)(2,1)S(1)}, u32[]{:S(2)}, u32[]{:S(2)}) collective-permute-start(bf16[128,256]{1,0:T(8,128)(2,1)S(1)} %get-tuple-element.37), channel_id=1, source_target_pairs={{0,2},{1,3},{2,0},{3,1},{4,6},{5,7},{6,4},{7,5},{8,10},{9,11},{10,... | collective-permute-start | bytes 196616 | tf_op jit(solution)/shard_map/ppermute | solution.py:87
  17.3 0.5 %collective-permute-start.9 = (bf16[128,256]{1,0:T(8,128)(2,1)S(1)}, bf16[128,256]{1,0:T(8,128)(2,1)S(1)}, u32[]{:S(2)}, u32[]{:S(2)}) collective-permute-start(bf16[128,256]{1,0:T(8,128)(2,1)S(1)} %get-tuple-element.38), channel_id=1, source_target_pairs={{0,3},{1,2},{2,1},{3,0},{4,7},{5,6},{6,5},{7,4},{8,11},{9,10},{10,... | collective-permute-start | bytes 196616 | tf_op jit(solution)/shard_map/ppermute | solution.py:87
  17.8 0.8 %collective-permute-done.7.refs_1_ = bf16[128,256]{1,0:T(8,128)(2,1)S(1)} collective-permute-done((bf16[128,256]{1,0:T(8,128)(2,1)S(1)}, bf16[128,256]{1,0:T(8,128)(2,1)S(1)}, u32[]{:S(2)}, u32[]{:S(2)}) %collective-permute-start.7) | collective-permute-done | bytes 65568 | tf_op jit(solution)/shard_map/ppermute | solution.py:87
  18.6 1.5 %collective-permute-done.8.refs_2_ = bf16[128,256]{1,0:T(8,128)(2,1)S(1)} collective-permute-done((bf16[128,256]{1,0:T(8,128)(2,1)S(1)}, bf16[128,256]{1,0:T(8,128)(2,1)S(1)}, u32[]{:S(2)}, u32[]{:S(2)}) %collective-permute-start.8) | collective-permute-done | bytes 65568 | tf_op jit(solution)/shard_map/ppermute | solution.py:87
  20.1 2.4 %collective-permute-done.9.refs_3_ = bf16[128,256]{1,0:T(8,128)(2,1)S(1)} collective-permute-done((bf16[128,256]{1,0:T(8,128)(2,1)S(1)}, bf16[128,256]{1,0:T(8,128)(2,1)S(1)}, u32[]{:S(2)}, u32[]{:S(2)}) %collective-permute-start.9) | collective-permute-done | bytes 65568 | tf_op jit(solution)/shard_map/ppermute | solution.py:87
  22.5 0.4 dense.1
  22.9 0.1 collective-permute-start.10
  23.0 1.3 %collective-permute-done.10.came_ref = bf16[256,256]{1,0:T(8,128)(2,1)S(1)} collective-permute-done((bf16[256,256]{1,0:T(8,128)(2,1)S(1)}, bf16[256,256]{1,0:T(8,128)(2,1)S(1)}, u32[]{:S(2)}, u32[]{:S(2)}) %collective-permute-start.10) | collective-permute-done | bytes 131104 | tf_op jit(solution)/shard_map/ppermute | solution.py:87
  24.4 0.6 %collective-permute-start.11 = (bf16[32,256]{1,0:T(8,128)(2,1)S(1)}, bf16[32,256]{1,0:T(8,128)(2,1)S(1)}, u32[]{:S(2)}, u32[]{:S(2)}) collective-permute-start(bf16[32,256]{1,0:T(8,128)(2,1)S(1)} %get-tuple-element.43), channel_id=1, source_target_pairs={{0,3},{1,2},{2,1},{3,0},{4,7},{5,6},{6,5},{7,4},{8,11},{9,10},{10,... | collective-permute-start | bytes 49160 | tf_op jit(solution)/shard_map/ppermute | solution.py:87
  24.9 1.5 %collective-permute-start.12 = (bf16[32,256]{1,0:T(8,128)(2,1)S(1)}, bf16[32,256]{1,0:T(8,128)(2,1)S(1)}, u32[]{:S(2)}, u32[]{:S(2)}) collective-permute-start(bf16[32,256]{1,0:T(8,128)(2,1)S(1)} %get-tuple-element.44), channel_id=1, source_target_pairs={{0,2},{1,3},{2,0},{3,1},{4,6},{5,7},{6,4},{7,5},{8,10},{9,11},{10,... | collective-permute-start | bytes 49160 | tf_op jit(solution)/shard_map/ppermute | solution.py:87
  26.4 1.5 %collective-permute-start.13 = (bf16[32,256]{1,0:T(8,128)(2,1)S(1)}, bf16[32,256]{1,0:T(8,128)(2,1)S(1)}, u32[]{:S(2)}, u32[]{:S(2)}) collective-permute-start(bf16[32,256]{1,0:T(8,128)(2,1)S(1)} %get-tuple-element.45), channel_id=1, source_target_pairs={{0,1},{1,0},{2,3},{3,2},{4,5},{5,4},{6,7},{7,6},{8,9},{9,8},{10,11... | collective-permute-start | bytes 49160 | tf_op jit(solution)/shard_map/ppermute | solution.py:87
  27.9 1.1 %collective-permute-done.11.refs_1_ = bf16[32,256]{1,0:T(8,128)(2,1)S(1)} collective-permute-done((bf16[32,256]{1,0:T(8,128)(2,1)S(1)}, bf16[32,256]{1,0:T(8,128)(2,1)S(1)}, u32[]{:S(2)}, u32[]{:S(2)}) %collective-permute-start.11) | collective-permute-done | bytes 16416 | tf_op jit(solution)/shard_map/ppermute | solution.py:87
  29.1 1.1 %collective-permute-done.13.refs_3_ = bf16[32,256]{1,0:T(8,128)(2,1)S(1)} collective-permute-done((bf16[32,256]{1,0:T(8,128)(2,1)S(1)}, bf16[32,256]{1,0:T(8,128)(2,1)S(1)}, u32[]{:S(2)}, u32[]{:S(2)}) %collective-permute-start.13) | collective-permute-done | bytes 16416 | tf_op jit(solution)/shard_map/ppermute | solution.py:87
  30.2 2.8 %collective-permute-start.14 = (bf16[96,256]{1,0:T(8,128)(2,1)S(1)}, bf16[96,256]{1,0:T(8,128)(2,1)S(1)}, u32[]{:S(2)}, u32[]{:S(2)}) collective-permute-start(bf16[96,256]{1,0:T(8,128)(2,1)S(1)} %get-tuple-element.47), channel_id=1, source_target_pairs={{0,24},{4,28},{8,16},{12,20},{16,8},{20,12},{24,0},{28,4},{1,25},{... | collective-permute-start | bytes 147464 | tf_op jit(solution)/shard_map/ppermute | solution.py:87
  33.0 0.0 collective-permute-start.15
  33.0 1.7 %collective-permute-start.16 = (bf16[96,256]{1,0:T(8,128)(2,1)S(1)}, bf16[96,256]{1,0:T(8,128)(2,1)S(1)}, u32[]{:S(2)}, u32[]{:S(2)}) collective-permute-start(bf16[96,256]{1,0:T(8,128)(2,1)S(1)} %get-tuple-element.49), channel_id=1, source_target_pairs={{0,8},{4,12},{8,0},{12,4},{16,24},{20,28},{24,16},{28,20},{1,9},{5... | collective-permute-start | bytes 147464 | tf_op jit(solution)/shard_map/ppermute | solution.py:87
  34.7 1.6 %collective-permute-done.14.refs_1_ = bf16[96,256]{1,0:T(8,128)(2,1)S(1)} collective-permute-done((bf16[96,256]{1,0:T(8,128)(2,1)S(1)}, bf16[96,256]{1,0:T(8,128)(2,1)S(1)}, u32[]{:S(2)}, u32[]{:S(2)}) %collective-permute-start.14) | collective-permute-done | bytes 49184 | tf_op jit(solution)/shard_map/ppermute | solution.py:87
  36.3 1.7 %collective-permute-done.15.refs_2_ = bf16[96,256]{1,0:T(8,128)(2,1)S(1)} collective-permute-done((bf16[96,256]{1,0:T(8,128)(2,1)S(1)}, bf16[96,256]{1,0:T(8,128)(2,1)S(1)}, u32[]{:S(2)}, u32[]{:S(2)}) %collective-permute-start.15) | collective-permute-done | bytes 49184 | tf_op jit(solution)/shard_map/ppermute | solution.py:87
  38.0 0.0 collective-permute-done.16.refs_3_
  38.0 1.5 %collective-permute-start.19 = (bf16[32,256]{1,0:T(8,128)(2,1)S(1)}, bf16[32,256]{1,0:T(8,128)(2,1)S(1)}, u32[]{:S(2)}, u32[]{:S(2)}) collective-permute-start(bf16[32,256]{1,0:T(8,128)(2,1)S(1)} %chunk.1.refs_0_), channel_id=1, source_target_pairs={{0,1},{1,0},{2,3},{3,2},{4,5},{5,4},{6,7},{7,6},{8,9},{9,8},{10,11... | collective-permute-start | bytes 49160 | tf_op jit(solution)/shard_map/ppermute | solution.py:87
  39.6 0.5 %collective-permute-start.18 = (bf16[32,256]{1,0:T(8,128)(2,1)S(1)}, bf16[32,256]{1,0:T(8,128)(2,1)S(1)}, u32[]{:S(2)}, u32[]{:S(2)}) collective-permute-start(bf16[32,256]{1,0:T(8,128)(2,1)S(1)} %chunk.1.refs_0_), channel_id=1, source_target_pairs={{0,2},{1,3},{2,0},{3,1},{4,6},{5,7},{6,4},{7,5},{8,10},{9,11},{10,... | collective-permute-start | bytes 49160 | tf_op jit(solution)/shard_map/ppermute | solution.py:87
  40.1 1.5 %collective-permute-start.17 = (bf16[32,256]{1,0:T(8,128)(2,1)S(1)}, bf16[32,256]{1,0:T(8,128)(2,1)S(1)}, u32[]{:S(2)}, u32[]{:S(2)}) collective-permute-start(bf16[32,256]{1,0:T(8,128)(2,1)S(1)} %chunk.1.refs_0_), channel_id=1, source_target_pairs={{0,3},{1,2},{2,1},{3,0},{4,7},{5,6},{6,5},{7,4},{8,11},{9,10},{10,... | collective-permute-start | bytes 49160 | tf_op jit(solution)/shard_map/ppermute | solution.py:87
  41.6 0.2 collective-permute-done.19.refs_3_
  41.8 1.5 %collective-permute-done.18.refs_2_ = bf16[32,256]{1,0:T(8,128)(2,1)S(1)} collective-permute-done((bf16[32,256]{1,0:T(8,128)(2,1)S(1)}, bf16[32,256]{1,0:T(8,128)(2,1)S(1)}, u32[]{:S(2)}, u32[]{:S(2)}) %collective-permute-start.18) | collective-permute-done | bytes 16416 | tf_op jit(solution)/shard_map/ppermute | solution.py:87
  43.3 1.4 %collective-permute-done.17.refs_1_ = bf16[32,256]{1,0:T(8,128)(2,1)S(1)} collective-permute-done((bf16[32,256]{1,0:T(8,128)(2,1)S(1)}, bf16[32,256]{1,0:T(8,128)(2,1)S(1)}, u32[]{:S(2)}, u32[]{:S(2)}) %collective-permute-start.17) | collective-permute-done | bytes 16416 | tf_op jit(solution)/shard_map/ppermute | solution.py:87
  44.7 0.1 collective-permute-start.20
  44.8 0.7 %unpack.1 = bf16[8,32,256]{2,1,0:T(8,128)(2,1)} custom-call(bf16[96,256]{1,0:T(8,128)(2,1)S(1)} %get-tuple-element.46.refs_0_, bf16[96,256]{1,0:T(8,128)(2,1)S(1)} %collective-permute-done.14.refs_1_, bf16[96,256]{1,0:T(8,128)(2,1)S(1)} %collective-permute-done.15.refs_2_, bf16[96,256]{1,0:T(8,128)(2,1)S(1)} %collective-permute-done.16.refs_3_), custom_call_target="tpu_custom_call" | custom-call | tf_op jit(solution)/shard_map/unpack/pallas_call | solution.py:213
  45.5 0.6 %collective-permute-done.20.came_ref = bf16[128,256]{1,0:T(8,128)(2,1)S(1)} collective-permute-done((bf16[128,256]{1,0:T(8,128)(2,1)S(1)}, bf16[128,256]{1,0:T(8,128)(2,1)S(1)}, u32[]{:S(2)}, u32[]{:S(2)}) %collective-permute-start.20) | collective-permute-done | bytes 65568 | tf_op jit(solution)/shard_map/ppermute | solution.py:87
  46.0 0.7 %finish.1 = f32[2,128,256]{2,1,0:T(8,128)} custom-call(bf16[128,256]{1,0:T(8,128)(2,1)S(1)} %bitcast.8, bf16[128,256]{1,0:T(8,128)(2,1)S(1)} %collective-permute-done.20.came_ref), custom_call_target="tpu_custom_call" | custom-call | tf_op jit(solution)/shard_map/finish/pallas_call | solution.py:248
  (15 shorter events, 0.1 us)
Async XLA Ops:
  0.6 8.5 %collective-permute-start.2 = (bf16[128,256]{1,0:T(8,128)(2,1)}, bf16[128,256]{1,0:T(8,128)(2,1)S(1)}, u32[]{:S(2)}, u32[]{:S(2)}) collective-permute-start(bf16[128,256]{1,0:T(8,128)(2,1)} %own_ref.1), channel_id=1, source_target_pairs={{0,24},{4,28},{8,16},{12,20},{16,8},{20,12},{24,0},{28,4},{1,25},{... | collective-permute-start | bytes 196616 | tf_op jit(solution)/shard_map/ppermute | solution.py:87
  5.7 5.8 %collective-permute-start.1 = (bf16[128,256]{1,0:T(8,128)(2,1)}, bf16[128,256]{1,0:T(8,128)(2,1)S(1)}, u32[]{:S(2)}, u32[]{:S(2)}) collective-permute-start(bf16[128,256]{1,0:T(8,128)(2,1)} %own_ref.1), channel_id=1, source_target_pairs={{0,16},{4,20},{8,24},{12,28},{16,0},{20,4},{24,8},{28,12},{1,17},{... | collective-permute-start | bytes 196616 | tf_op jit(solution)/shard_map/ppermute | solution.py:87
  5.7 5.8 %collective-permute-start = (bf16[128,256]{1,0:T(8,128)(2,1)}, bf16[128,256]{1,0:T(8,128)(2,1)S(1)}, u32[]{:S(2)}, u32[]{:S(2)}) collective-permute-start(bf16[128,256]{1,0:T(8,128)(2,1)} %own_ref.1), channel_id=1, source_target_pairs={{0,8},{4,12},{8,0},{12,4},{16,24},{20,28},{24,16},{28,20},{1,9},{5... | collective-permute-start | bytes 196616 | tf_op jit(solution)/shard_map/ppermute | solution.py:87
  6.4 5.8 %collective-permute-start.3 = (bf16[128,256]{1,0:T(8,128)(2,1)}, bf16[128,256]{1,0:T(8,128)(2,1)S(1)}, u32[]{:S(2)}, u32[]{:S(2)}) collective-permute-start(bf16[128,256]{1,0:T(8,128)(2,1)} %own_ref.1), channel_id=1, source_target_pairs={{0,4},{4,0},{8,12},{12,8},{16,20},{20,16},{24,28},{28,24},{1,5},{5... | collective-permute-start | bytes 196616 | tf_op jit(solution)/shard_map/ppermute | solution.py:87
  6.4 0.7 %copy-start.5 = (s32[128,1]{0,1:T(1,128)S(1)}, s32[128,1]{0,1:T(1,128)}, u32[]{:S(2)}) copy-start(s32[128,1]{0,1:T(1,128)} %param.11) | copy-start | bytes 1540
  7.0 1.0 %copy-start = (bf16[4,1,4,128,128]{4,3,2,1,0:T(8,128)(2,1)S(1)}, bf16[4,1,4,128,128]{4,3,2,1,0:T(8,128)(2,1)}, u32[]{:S(2)}) copy-start(bf16[4,1,4,128,128]{4,3,2,1,0:T(8,128)(2,1)} %param.7) | copy-start | bytes 1572868
  8.1 0.8 %copy-start.2 = (bf16[128,256]{1,0:T(8,128)(2,1)S(1)}, bf16[128,256]{1,0:T(8,128)(2,1)}, u32[]{:S(2)}) copy-start(bf16[128,256]{1,0:T(8,128)(2,1)} %own_ref.1) | copy-start | bytes 196612
  11.6 1.8 %copy-start.4 = (s32[4,1,4]{2,1,0:T(1,128)S(1)}, s32[4,1,4]{2,1,0:T(1,128)}, u32[]{:S(2)}) copy-start(s32[4,1,4]{2,1,0:T(1,128)} %param.8) | copy-start | bytes 196
  11.6 1.3 %collective-permute-start.4 = (bf16[128,256]{1,0:T(8,128)(2,1)S(1)}, bf16[128,256]{1,0:T(8,128)(2,1)S(1)}, u32[]{:S(2)}, u32[]{:S(2)}) collective-permute-start(bf16[128,256]{1,0:T(8,128)(2,1)S(1)} %collective-permute-done.refs_2_), channel_id=1, source_target_pairs={{0,4},{4,0},{8,12},{12,8},{16,20},{20,16},{24,28},{28,24},{1,5},{5... | collective-permute-start | bytes 196616 | tf_op jit(solution)/shard_map/ppermute | solution.py:87
  11.6 1.4 %collective-permute-start.5 = (bf16[128,256]{1,0:T(8,128)(2,1)S(1)}, bf16[128,256]{1,0:T(8,128)(2,1)S(1)}, u32[]{:S(2)}, u32[]{:S(2)}) collective-permute-start(bf16[128,256]{1,0:T(8,128)(2,1)S(1)} %collective-permute-done.1.refs_4_), channel_id=1, source_target_pairs={{0,4},{4,0},{8,12},{12,8},{16,20},{20,16},{24,28},{28,24},{1,5},{5... | collective-permute-start | bytes 196616 | tf_op jit(solution)/shard_map/ppermute | solution.py:87
  12.1 1.3 %collective-permute-start.6 = (bf16[128,256]{1,0:T(8,128)(2,1)S(1)}, bf16[128,256]{1,0:T(8,128)(2,1)S(1)}, u32[]{:S(2)}, u32[]{:S(2)}) collective-permute-start(bf16[128,256]{1,0:T(8,128)(2,1)S(1)} %collective-permute-done.2.refs_6_), channel_id=1, source_target_pairs={{0,4},{4,0},{8,12},{12,8},{16,20},{20,16},{24,28},{28,24},{1,5},{5... | collective-permute-start | bytes 196616 | tf_op jit(solution)/shard_map/ppermute | solution.py:87
  13.3 9.2 %copy-start.1 = (bf16[256,256]{1,0:T(8,128)(2,1)S(1)}, bf16[256,256]{1,0:T(8,128)(2,1)}, u32[]{:S(2)}) copy-start(bf16[256,256]{1,0:T(8,128)(2,1)} %weight_ref.1) | copy-start | bytes 393220
  13.3 9.2 %copy-start.3 = (bf16[128,256]{1,0:T(8,128)(2,1)S(1)}, bf16[128,256]{1,0:T(8,128)(2,1)}, u32[]{:S(2)}) copy-start(bf16[128,256]{1,0:T(8,128)(2,1)} %cot_ref.1) | copy-start | bytes 196612
  14.3 4.3 %collective-permute-start.7 = (bf16[128,256]{1,0:T(8,128)(2,1)S(1)}, bf16[128,256]{1,0:T(8,128)(2,1)S(1)}, u32[]{:S(2)}, u32[]{:S(2)}) collective-permute-start(bf16[128,256]{1,0:T(8,128)(2,1)S(1)} %get-tuple-element.36), channel_id=1, source_target_pairs={{0,1},{1,0},{2,3},{3,2},{4,5},{5,4},{6,7},{7,6},{8,9},{9,8},{10,11... | collective-permute-start | bytes 196616 | tf_op jit(solution)/shard_map/ppermute | solution.py:87
  15.8 4.3 %collective-permute-start.8 = (bf16[128,256]{1,0:T(8,128)(2,1)S(1)}, bf16[128,256]{1,0:T(8,128)(2,1)S(1)}, u32[]{:S(2)}, u32[]{:S(2)}) collective-permute-start(bf16[128,256]{1,0:T(8,128)(2,1)S(1)} %get-tuple-element.37), channel_id=1, source_target_pairs={{0,2},{1,3},{2,0},{3,1},{4,6},{5,7},{6,4},{7,5},{8,10},{9,11},{10,... | collective-permute-start | bytes 196616 | tf_op jit(solution)/shard_map/ppermute | solution.py:87
  17.3 5.2 %collective-permute-start.9 = (bf16[128,256]{1,0:T(8,128)(2,1)S(1)}, bf16[128,256]{1,0:T(8,128)(2,1)S(1)}, u32[]{:S(2)}, u32[]{:S(2)}) collective-permute-start(bf16[128,256]{1,0:T(8,128)(2,1)S(1)} %get-tuple-element.38), channel_id=1, source_target_pairs={{0,3},{1,2},{2,1},{3,0},{4,7},{5,6},{6,5},{7,4},{8,11},{9,10},{10,... | collective-permute-start | bytes 196616 | tf_op jit(solution)/shard_map/ppermute | solution.py:87
  22.9 1.4 %collective-permute-start.10 = (bf16[256,256]{1,0:T(8,128)(2,1)S(1)}, bf16[256,256]{1,0:T(8,128)(2,1)S(1)}, u32[]{:S(2)}, u32[]{:S(2)}) collective-permute-start(bf16[256,256]{1,0:T(8,128)(2,1)S(1)} %get-tuple-element.40), channel_id=1, source_target_pairs={{0,4},{4,0},{8,12},{12,8},{16,20},{20,16},{24,28},{28,24},{1,5},{5... | collective-permute-start | bytes 393224 | tf_op jit(solution)/shard_map/ppermute | solution.py:87
  24.4 4.7 %collective-permute-start.11 = (bf16[32,256]{1,0:T(8,128)(2,1)S(1)}, bf16[32,256]{1,0:T(8,128)(2,1)S(1)}, u32[]{:S(2)}, u32[]{:S(2)}) collective-permute-start(bf16[32,256]{1,0:T(8,128)(2,1)S(1)} %get-tuple-element.43), channel_id=1, source_target_pairs={{0,3},{1,2},{2,1},{3,0},{4,7},{5,6},{6,5},{7,4},{8,11},{9,10},{10,... | collective-permute-start | bytes 49160 | tf_op jit(solution)/shard_map/ppermute | solution.py:87
  24.9 4.2 %collective-permute-start.12 = (bf16[32,256]{1,0:T(8,128)(2,1)S(1)}, bf16[32,256]{1,0:T(8,128)(2,1)S(1)}, u32[]{:S(2)}, u32[]{:S(2)}) collective-permute-start(bf16[32,256]{1,0:T(8,128)(2,1)S(1)} %get-tuple-element.44), channel_id=1, source_target_pairs={{0,2},{1,3},{2,0},{3,1},{4,6},{5,7},{6,4},{7,5},{8,10},{9,11},{10,... | collective-permute-start | bytes 49160 | tf_op jit(solution)/shard_map/ppermute | solution.py:87
  26.4 3.7 %collective-permute-start.13 = (bf16[32,256]{1,0:T(8,128)(2,1)S(1)}, bf16[32,256]{1,0:T(8,128)(2,1)S(1)}, u32[]{:S(2)}, u32[]{:S(2)}) collective-permute-start(bf16[32,256]{1,0:T(8,128)(2,1)S(1)} %get-tuple-element.45), channel_id=1, source_target_pairs={{0,1},{1,0},{2,3},{3,2},{4,5},{5,4},{6,7},{7,6},{8,9},{9,8},{10,11... | collective-permute-start | bytes 49160 | tf_op jit(solution)/shard_map/ppermute | solution.py:87
  30.2 6.1 %collective-permute-start.14 = (bf16[96,256]{1,0:T(8,128)(2,1)S(1)}, bf16[96,256]{1,0:T(8,128)(2,1)S(1)}, u32[]{:S(2)}, u32[]{:S(2)}) collective-permute-start(bf16[96,256]{1,0:T(8,128)(2,1)S(1)} %get-tuple-element.47), channel_id=1, source_target_pairs={{0,24},{4,28},{8,16},{12,20},{16,8},{20,12},{24,0},{28,4},{1,25},{... | collective-permute-start | bytes 147464 | tf_op jit(solution)/shard_map/ppermute | solution.py:87
  33.0 5.0 %collective-permute-start.15 = (bf16[96,256]{1,0:T(8,128)(2,1)S(1)}, bf16[96,256]{1,0:T(8,128)(2,1)S(1)}, u32[]{:S(2)}, u32[]{:S(2)}) collective-permute-start(bf16[96,256]{1,0:T(8,128)(2,1)S(1)} %get-tuple-element.48), channel_id=1, source_target_pairs={{0,16},{4,20},{8,24},{12,28},{16,0},{20,4},{24,8},{28,12},{1,17},{... | collective-permute-start | bytes 147464 | tf_op jit(solution)/shard_map/ppermute | solution.py:87
  33.0 5.0 %collective-permute-start.16 = (bf16[96,256]{1,0:T(8,128)(2,1)S(1)}, bf16[96,256]{1,0:T(8,128)(2,1)S(1)}, u32[]{:S(2)}, u32[]{:S(2)}) collective-permute-start(bf16[96,256]{1,0:T(8,128)(2,1)S(1)} %get-tuple-element.49), channel_id=1, source_target_pairs={{0,8},{4,12},{8,0},{12,4},{16,24},{20,28},{24,16},{28,20},{1,9},{5... | collective-permute-start | bytes 147464 | tf_op jit(solution)/shard_map/ppermute | solution.py:87
  38.0 3.8 %collective-permute-start.19 = (bf16[32,256]{1,0:T(8,128)(2,1)S(1)}, bf16[32,256]{1,0:T(8,128)(2,1)S(1)}, u32[]{:S(2)}, u32[]{:S(2)}) collective-permute-start(bf16[32,256]{1,0:T(8,128)(2,1)S(1)} %chunk.1.refs_0_), channel_id=1, source_target_pairs={{0,1},{1,0},{2,3},{3,2},{4,5},{5,4},{6,7},{7,6},{8,9},{9,8},{10,11... | collective-permute-start | bytes 49160 | tf_op jit(solution)/shard_map/ppermute | solution.py:87
  39.6 3.7 %collective-permute-start.18 = (bf16[32,256]{1,0:T(8,128)(2,1)S(1)}, bf16[32,256]{1,0:T(8,128)(2,1)S(1)}, u32[]{:S(2)}, u32[]{:S(2)}) collective-permute-start(bf16[32,256]{1,0:T(8,128)(2,1)S(1)} %chunk.1.refs_0_), channel_id=1, source_target_pairs={{0,2},{1,3},{2,0},{3,1},{4,6},{5,7},{6,4},{7,5},{8,10},{9,11},{10,... | collective-permute-start | bytes 49160 | tf_op jit(solution)/shard_map/ppermute | solution.py:87
  40.1 4.6 %collective-permute-start.17 = (bf16[32,256]{1,0:T(8,128)(2,1)S(1)}, bf16[32,256]{1,0:T(8,128)(2,1)S(1)}, u32[]{:S(2)}, u32[]{:S(2)}) collective-permute-start(bf16[32,256]{1,0:T(8,128)(2,1)S(1)} %chunk.1.refs_0_), channel_id=1, source_target_pairs={{0,3},{1,2},{2,1},{3,0},{4,7},{5,6},{6,5},{7,4},{8,11},{9,10},{10,... | collective-permute-start | bytes 49160 | tf_op jit(solution)/shard_map/ppermute | solution.py:87
  44.7 1.3 %collective-permute-start.20 = (bf16[128,256]{1,0:T(8,128)(2,1)S(1)}, bf16[128,256]{1,0:T(8,128)(2,1)S(1)}, u32[]{:S(2)}, u32[]{:S(2)}) collective-permute-start(bf16[128,256]{1,0:T(8,128)(2,1)S(1)} %bitcast.7), channel_id=1, source_target_pairs={{0,4},{4,0},{8,12},{12,8},{16,20},{20,16},{24,28},{28,24},{1,5},{5... | collective-permute-start | bytes 196616 | tf_op jit(solution)/shard_map/ppermute | solution.py:87

commit v5 on v4

v5 whole, which is shorter than its diff:
```python
import functools

import jax
import jax.numpy as jnp
from jax import lax
from jax.experimental import pallas as pl
from jax.experimental.pallas import tpu as pltpu
from jax.sharding import PartitionSpec as P

VMEM = pl.BlockSpec(memory_space=pltpu.VMEM)
LIMIT = pltpu.CompilerParams(vmem_limit_bytes=32 * 1024 * 1024)
SMEM = pl.BlockSpec(memory_space=pltpu.SMEM)


def across(n):
    return list(range(n - 1, 0, -1))


def prepare_kernel(slots, tiles_ref, own_ref, target_ref, wide_ref, held_ref, placing_ref):
    many, depth = tiles_ref.shape[:2]
    for g in range(many):
        wide_ref[g] = jnp.concatenate([tiles_ref[g, k] for k in range(depth)], axis=1)
    held_ref[...] = own_ref[...]
    places, rows = placing_ref.shape
    n_section = places // slots
    target = target_ref[...]
    hits = lax.broadcasted_iota(jnp.int32, (n_section, rows), 0) == target
    hits = jnp.where(hits, 1.0, 0.0)
    earlier = lax.broadcasted_iota(jnp.int32, (rows, rows), 0) < lax.broadcasted_iota(
        jnp.int32, (rows, rows), 1
    )
    earlier = jnp.where(earlier, 1.0, 0.0).astype(jnp.bfloat16)
    before = jnp.dot(hits.astype(jnp.bfloat16), earlier, preferred_element_type=jnp.float32)
    slot = jnp.sum(before * hits, axis=0, keepdims=True).astype(jnp.int32)
    chip = lax.axis_index("section") & -2
    position = (target ^ chip) * slots + slot
    placing = lax.broadcasted_iota(jnp.int32, (places, rows), 0) == position
    placing_ref[...] = jnp.where(placing, 1.0, 0.0).astype(jnp.bfloat16)


def prepare(tiles, own, target, places, slots):
    many, depth, tile, _ = tiles.shape
    return pl.pallas_call(
        functools.partial(prepare_kernel, slots),
        out_shape=(
            jax.ShapeDtypeStruct((many, tile, depth * tile), jnp.bfloat16),
            jax.ShapeDtypeStruct(own.shape, jnp.bfloat16),
            jax.ShapeDtypeStruct((places, target.shape[1]), jnp.bfloat16),
        ),
        in_specs=[VMEM] * 3,
        out_specs=(VMEM,) * 3,
        compiler_params=LIMIT,
        cost_estimate=pl.CostEstimate(flops=0, bytes_accessed=2 * tiles.size * 2, transcendentals=0),
        name="prepare",
    )(tiles, own, target)


def partials_kernel(count, src_ref, wide_ref, *refs):
    block_refs, out_refs, held = refs[:count], refs[count:-1], refs[-1]
    depth = src_ref.shape[1]
    section, rep = lax.axis_index("section"), lax.axis_index("rep")
    for j in range(count):
        held[j] = block_refs[j][...]
    for j, out_ref in zip([0] + across(len(out_refs)), out_refs):
        g = rep ^ j
        right = jnp.concatenate([held[src_ref[g, k] ^ section] for k in range(depth)], axis=0)
        out_ref[...] = jnp.dot(wide_ref[g], right, preferred_element_type=jnp.float32).astype(
            jnp.bfloat16
        )


def partials(sources, wide, blocks):
    many = wide.shape[0]
    tile, width = blocks[0].shape
    return pl.pallas_call(
        functools.partial(partials_kernel, len(blocks)),
        out_shape=[jax.ShapeDtypeStruct((tile, width), jnp.bfloat16)] * many,
        in_specs=[SMEM] + [VMEM] * (1 + len(blocks)),
        out_specs=[VMEM] * many,
        scratch_shapes=[pltpu.VMEM((len(blocks), tile, width), jnp.bfloat16)],
        compiler_params=LIMIT,
        name="partials",
    )(sources, wide, *blocks)


def swap(value, axis, j):
    return lax.ppermute(value, axis, [(i, i ^ j) for i in range(lax.axis_size(axis))])


def tree_sum(terms):
    while len(terms) > 1:
        terms = [terms[i] + terms[i + 1] for i in range(0, len(terms), 2)]
    return terms[0]


def tree_sum(terms):
    while len(terms) > 1:
        terms = [terms[i] + terms[i + 1] for i in range(0, len(terms), 2)]
    return terms[0]


def dense_kernel(n_part, weight_ref, cot_ref, placing_ref, *refs):
    part_refs, (packed_ref, term_ref, sent_ref) = refs[:n_part], refs[n_part:]
    core = lax.axis_index("section") & 1
    agg_b = tree_sum([ref[...].astype(jnp.float32) for ref in part_refs]).astype(jnp.bfloat16)
    pre = jnp.dot(agg_b, weight_ref[...], preferred_element_type=jnp.float32)
    sig = jax.nn.sigmoid(pre)
    factor = sig * (1.0 + pre * (1.0 - sig))
    grad_pre = (cot_ref[...].astype(jnp.float32) * factor).astype(jnp.bfloat16)
    term = lax.dot_general(
        agg_b, grad_pre, (((0,), (0,)), ((), ())), preferred_element_type=jnp.float32
    )
    term_ref[...] = term
    output = (pre * sig).astype(jnp.bfloat16)
    packed = jnp.dot(placing_ref[...], output, preferred_element_type=jnp.float32)
    packed = packed.astype(jnp.bfloat16)
    packed_ref[...] = packed

    @pl.when(core == 0)
    def _():
        sent_ref[: term.shape[0]] = term.astype(jnp.bfloat16)

    @pl.when(core == 1)
    def _():
        sent_ref[: packed.shape[0]] = packed


def dense(parts, weight, cotangent, placing):
    places, width = placing.shape[0], weight.shape[0]
    return pl.pallas_call(
        functools.partial(dense_kernel, len(parts)),
        out_shape=(
            jax.ShapeDtypeStruct((places, width), jnp.bfloat16),
            jax.ShapeDtypeStruct((width, width), jnp.float32),
            jax.ShapeDtypeStruct((max(places, width), width), jnp.bfloat16),
        ),
        in_specs=[VMEM] * (3 + len(parts)),
        out_specs=(VMEM,) * 3,
        compiler_params=LIMIT,
        name="dense",
    )(weight, cotangent, placing, *parts)


def split_kernel(n_rep, packed_ref, term_ref, came_ref, own_ref, *refs):
    chunk_refs, message_refs, term = refs[: n_rep - 1], refs[n_rep - 1 : -1], refs[-1]
    rep = lax.axis_index("rep")
    width = term_ref.shape[0]
    total = term_ref[...] + came_ref[:width].astype(jnp.float32)
    term[...] = total.reshape(term.shape)
    own_ref[...] = term[rep]
    for ref, j in zip(chunk_refs, across(n_rep)):
        ref[...] = term[rep ^ j].astype(jnp.bfloat16)
    rows = packed_ref.shape[0] // len(message_refs)
    for ref, j in zip(message_refs, [0] + across(len(message_refs))):
        ref[:rows] = packed_ref[j * rows : (j + 1) * rows]
        ref[rows:] = came_ref[j * rows : (j + 1) * rows]


def split(packed, term, came, n_rep, chips):
    places, width = packed.shape
    chunk = (width // n_rep, width)
    return pl.pallas_call(
        functools.partial(split_kernel, n_rep),
        out_shape=[jax.ShapeDtypeStruct(chunk, jnp.float32)]
        + [jax.ShapeDtypeStruct(chunk, jnp.bfloat16)] * (n_rep - 1)
        + [jax.ShapeDtypeStruct((2 * places // chips, width), jnp.bfloat16)] * chips,
        in_specs=[VMEM] * 3,
        out_specs=[VMEM] * (n_rep + chips),
        scratch_shapes=[pltpu.VMEM((n_rep,) + chunk, jnp.float32)],
        compiler_params=LIMIT,
        name="split",
    )(packed, term, came)


def add_kernel(*refs):
    refs[-1][...] = tree_sum([ref[...].astype(jnp.float32) for ref in refs[:-1]]).astype(jnp.bfloat16)


def add(terms):
    return pl.pallas_call(
        add_kernel,
        out_shape=jax.ShapeDtypeStruct(terms[0].shape, jnp.bfloat16),
        in_specs=[VMEM] * len(terms),
        out_specs=VMEM,
        compiler_params=LIMIT,
        name="add",
    )(*terms)


def unpack_kernel(slots, *refs):
    message_refs, out_refs = refs[:-2], refs[-2:]
    chip = lax.axis_index("section") & -2
    for j, ref in zip([0] + across(len(message_refs)), message_refs):
        for source in range(2):
            for core in range(2):
                start = (2 * source + core) * slots
                out_refs[core][chip ^ (2 * j) | source] = ref[start : start + slots]


def unpack(messages, slots):
    width = messages[0].shape[1]
    n_section = 2 * len(messages)
    return pl.pallas_call(
        functools.partial(unpack_kernel, slots),
        out_shape=[jax.ShapeDtypeStruct((n_section, slots, width), jnp.bfloat16)] * 2,
        in_specs=[VMEM] * len(messages),
        out_specs=[VMEM] * 2,
        compiler_params=LIMIT,
        name="unpack",
    )(*messages)


def place_kernel(other_ref, *refs):
    chunk_refs, (whole_ref, sent_ref) = refs[:-2], refs[-2:]
    rep, core = lax.axis_index("rep"), lax.axis_index("section") & 1
    for j, ref in enumerate(chunk_refs):
        whole_ref[rep ^ j] = ref[...]

    @pl.when(core == 0)
    def _():
        sent_ref[: other_ref.shape[0]] = other_ref[...]

    @pl.when(core == 1)
    def _():
        n_rep, rows, _ = whole_ref.shape
        for r in range(n_rep):
            sent_ref[r * rows : (r + 1) * rows] = whole_ref[r]


def place(chunks, other):
    rows, width = chunks[0].shape
    return pl.pallas_call(
        place_kernel,
        out_shape=(
            jax.ShapeDtypeStruct((len(chunks), rows, width), jnp.bfloat16),
            jax.ShapeDtypeStruct((max(len(chunks) * rows, other.shape[0]), width), jnp.bfloat16),
        ),
        in_specs=[VMEM] * (1 + len(chunks)),
        out_specs=(VMEM,) * 2,
        compiler_params=LIMIT,
        name="place",
    )(other, *chunks)


def finish_kernel(whole_ref, mine_ref, came_ref, relaid_ref, grad_ref):
    core = lax.axis_index("section") & 1

    @pl.when(core == 0)
    def _():
        grad_ref[...] = came_ref[: grad_ref.shape[0]].astype(jnp.float32)
        relaid_ref[...] = mine_ref[...]

    @pl.when(core == 1)
    def _():
        grad_ref[...] = whole_ref[...].astype(jnp.float32)
        relaid_ref[...] = came_ref[: relaid_ref.shape[0]]


def finish(whole, mine, came):
    return pl.pallas_call(
        finish_kernel,
        out_shape=(
            jax.ShapeDtypeStruct(mine.shape, jnp.bfloat16),
            jax.ShapeDtypeStruct(whole.shape, jnp.float32),
        ),
        in_specs=[VMEM] * 3,
        out_specs=(VMEM,) * 2,
        compiler_params=LIMIT,
        name="finish",
    )(whole, mine, came)


def swap_on_core(value, core, section_xor, rep_xor):
    n_rep = lax.axis_size("rep")
    pairs = [
        (s * n_rep + r, (s ^ section_xor) * n_rep + (r ^ rep_xor))
        for s in range(core, lax.axis_size("section"), 2)
        for r in range(n_rep)
    ]
    return lax.ppermute(value, ("section", "rep"), pairs)


def gather_blocks(features, axis, ready):
    n = lax.axis_size(axis)
    blocks = [None] * n
    blocks[0] = features
    for j in range(2, n, 2):
        blocks[j] = swap(features, axis, j)
    blocks[1] = swap(features, axis, 1)
    blocks[2], ready = lax.optimization_barrier((blocks[2], ready))
    for j in range(2, n, 2):
        blocks[j + 1] = swap(blocks[j], axis, 1)
    return blocks, ready


def per_device(features, adj_tiles, adj_src, cotangent, weight, destination):
    n_section, n_rep = lax.axis_size("section"), lax.axis_size("rep")
    rows_here, width = features.shape
    tile = adj_tiles.shape[3]
    slots = max(2, 2 * rows_here // n_section)
    target = destination.reshape(1, rows_here)
    wide, own, placing = prepare(adj_tiles[:, 0], features, target, n_section * slots, slots)
    blocks, (wide, own, placing) = gather_blocks(features, "section", (wide, own, placing))
    parts = list(partials(adj_src[:, 0], wide, [own] + blocks[1:]))
    others = across(n_rep)
    parts = [swap(part, "rep", j) if j else part for part, j in zip(parts, [0] + others)]
    packed, term, sent = dense(parts, weight, cotangent, placing)
    came = swap(sent, "section", 1)
    chips = n_section // 2
    own, *rest = split(packed, term, came, n_rep, chips)
    terms, messages = rest[: n_rep - 1], rest[n_rep - 1 :]
    terms = [swap_on_core(t, 1, 0, j) for t, j in zip(terms, others)]
    chunk = add([own] + terms)
    others = across(chips)
    messages = messages[:1] + [swap_on_core(m, 0, 2 * j, 0) for m, j in zip(messages[1:], others)]
    chunk = add([chunk] + [swap_on_core(chunk, 1, 2 * j, 0) for j in range(1, chips)])
    mine, other = unpack(messages, slots)
    chunks = [chunk] + [swap_on_core(chunk, 1, 0, j) for j in range(1, n_rep)]
    whole, sent = place(chunks, other.reshape(n_section * slots, width))
    came = swap(sent, "section", 1)
    relaid, weight_grad = finish(
        whole.reshape(width, width), mine.reshape(n_section * slots, width), came
    )
    return (relaid.reshape(1, 1, n_section, slots, width), weight_grad)


def solution(mesh):
    placed = (
        P(("section", "rep"), None),
        P("section", "rep", None, None, None),
        P("section", "rep", None),
        P(("section", "rep"), None),
        P(),
        P(("section", "rep"), None),
    )
    return jax.shard_map(
        per_device,
        mesh=mesh,
        in_specs=placed,
        out_specs=(P("section", "rep", None, None, None), P()),
        check_vma=False,
    )
```

time: 47 us -> 59.9 us (1.27)
  starting transfers between devices: 21.6 us -> 42.6 us
  waiting for transfers between devices: 18.9 us -> 10.9 us
    ppermute x0 -> x12, starting transfers between devices: none -> 16.1 us  [swap_on_core(): return lax.ppermute(value, ('section', 'rep'), pairs)]
    ppermute x21 -> x12, waiting for transfers between devices: 18.9 us -> 10.7 us  [swap(): lax.ppermute(value, axis, [(i, i ^ j) for i in range(lax.axis_size(axis))])]
    ppermute x21 -> x12, starting transfers between devices: 21.6 us -> 26.5 us  [swap(): lax.ppermute(value, axis, [(i, i ^ j) for i in range(lax.axis_size(axis))])]
  transfers between devices with their start and end apart: 21 -> 24, of which waited for: 16 -> 10; matrix products, arithmetic and copies ran while one was open for 0% -> 0% of each run, Pallas kernels for 2% -> 0%
where the time goes in v5:
time: 59.9 us; the launch traced here: 59.5 us
  starting transfers between devices  42.6 us (71%)
  waiting for transfers between devices  10.9 us (18%)
  local copies, waits for them, and re-layouts  2.55 us (4%)
  Pallas kernels  2.49 us (4%)
  between operations  0.91 us (2%)
    ppermute x12, starting transfers between devices, swap(): lax.ppermute(value, axis, [(i, i ^ j) for i in range(lax.axis_size(axis))])  26.5 us
    ppermute x12, starting transfers between devices, swap_on_core(): return lax.ppermute(value, ('section', 'rep'), pairs)  16.1 us
    ppermute x12, waiting for transfers between devices, swap(): lax.ppermute(value, axis, [(i, i ^ j) for i in range(lax.axis_size(axis))])  10.7 us
    unnamed x12, local copies, waits for them, and re-layouts  2.55 us
  transfers between devices with their start and end apart: 24, of which 10 were waited for; matrix products, arithmetic and copies ran while one was open for 0% of the time, Pallas kernels for 0%

profile of v5, /device:TPU:0, one launch (start us, length us, event | category | flops | bytes accessed | tf_op | source)
XLA Modules:
  0.0 59.5 jit_solution(14788442688952580425)
XLA Ops:
  0.6 3.1 %collective-permute-start = (bf16[128,256]{1,0:T(8,128)(2,1)}, bf16[128,256]{1,0:T(8,128)(2,1)S(1)}, u32[]{:S(2)}, u32[]{:S(2)}) collective-permute-start(bf16[128,256]{1,0:T(8,128)(2,1)} %own_ref.1), channel_id=1, source_target_pairs={{0,8},{4,12},{8,0},{12,4},{16,24},{20,28},{24,16},{28,20},{1,9},{5... | collective-permute-start | bytes 196616 | tf_op jit(solution)/shard_map/ppermute | solution.py:87
  3.7 2.5 %collective-permute-start.5 = (bf16[128,256]{1,0:T(8,128)(2,1)}, bf16[128,256]{1,0:T(8,128)(2,1)S(1)}, u32[]{:S(2)}, u32[]{:S(2)}) collective-permute-start(bf16[128,256]{1,0:T(8,128)(2,1)} %own_ref.1), channel_id=1, source_target_pairs={{0,24},{4,28},{8,16},{12,20},{16,8},{20,12},{24,0},{28,4},{1,25},{... | collective-permute-start | bytes 196616 | tf_op jit(solution)/shard_map/ppermute | solution.py:87
  6.2 0.1 collective-permute-start.3
  6.3 0.0 collective-permute-start.1
  6.3 0.7 %copy-done.5 = s32[128,1]{0,1:T(1,128)S(1)} copy-done((s32[128,1]{0,1:T(1,128)S(1)}, s32[128,1]{0,1:T(1,128)}, u32[]{:S(2)}) %copy-start.5) | copy-done | bytes 536
  7.0 1.0 %copy-done = bf16[4,1,4,128,128]{4,3,2,1,0:T(8,128)(2,1)S(1)} copy-done((bf16[4,1,4,128,128]{4,3,2,1,0:T(8,128)(2,1)S(1)}, bf16[4,1,4,128,128]{4,3,2,1,0:T(8,128)(2,1)}, u32[]{:S(2)}) %copy-start) | copy-done | bytes 524312
  8.0 0.8 %copy-done.2 = bf16[128,256]{1,0:T(8,128)(2,1)S(1)} copy-done((bf16[128,256]{1,0:T(8,128)(2,1)S(1)}, bf16[128,256]{1,0:T(8,128)(2,1)}, u32[]{:S(2)}) %copy-start.2) | copy-done | bytes 65560
  8.9 0.2 prepare.1
  9.1 0.0 collective-permute-done.refs_2_
  9.1 0.0 copy-start.4
  9.1 1.7 %collective-permute-done.5.refs_6_ = bf16[128,256]{1,0:T(8,128)(2,1)S(1)} collective-permute-done((bf16[128,256]{1,0:T(8,128)(2,1)}, bf16[128,256]{1,0:T(8,128)(2,1)S(1)}, u32[]{:S(2)}, u32[]{:S(2)}) %collective-permute-start.5) | collective-permute-done | bytes 65568 | tf_op jit(solution)/shard_map/ppermute | solution.py:87
  10.8 0.0 collective-permute-start.6
  10.8 2.1 %collective-permute-done.3.refs_4_ = bf16[128,256]{1,0:T(8,128)(2,1)S(1)} collective-permute-done((bf16[128,256]{1,0:T(8,128)(2,1)}, bf16[128,256]{1,0:T(8,128)(2,1)S(1)}, u32[]{:S(2)}, u32[]{:S(2)}) %collective-permute-start.3) | collective-permute-done | bytes 65568 | tf_op jit(solution)/shard_map/ppermute | solution.py:87
  12.9 0.0 collective-permute-start.4
  12.9 0.5 collective-permute-start.2
  13.4 0.0 collective-permute-done.1.refs_1_
  13.4 0.7 %collective-permute-done.4.refs_5_ = bf16[128,256]{1,0:T(8,128)(2,1)S(1)} collective-permute-done((bf16[128,256]{1,0:T(8,128)(2,1)S(1)}, bf16[128,256]{1,0:T(8,128)(2,1)S(1)}, u32[]{:S(2)}, u32[]{:S(2)}) %collective-permute-start.4) | collective-permute-done | bytes 65568 | tf_op jit(solution)/shard_map/ppermute | solution.py:87
  14.1 0.2 collective-permute-done.2.refs_3_
  14.3 0.9 %partials.1 = (bf16[128,256]{1,0:T(8,128)(2,1)S(1)}, bf16[128,256]{1,0:T(8,128)(2,1)S(1)}, bf16[128,256]{1,0:T(8,128)(2,1)S(1)}, bf16[128,256]{1,0:T(8,128)(2,1)S(1)}) custom-call(s32[4,4]{1,0:T(4,128)S(1)} %bitcast.11, bf16[4,128,512]{2,1,0:T(8,128)(2,1)S(1)} %get-tuple-element.34.wide_ref, bf16[128,256]{1,0:T(8,128)(2,1)S(1)} %get-tuple-element.35.refs_0_, ...), custom_call_target="tpu_custom_call" | custom-call | tf_op jit(solution)/shard_map/partials/pallas_call | solution.py:75
  15.2 2.5 %collective-permute-start.7 = (bf16[128,256]{1,0:T(8,128)(2,1)S(1)}, bf16[128,256]{1,0:T(8,128)(2,1)S(1)}, u32[]{:S(2)}, u32[]{:S(2)}) collective-permute-start(bf16[128,256]{1,0:T(8,128)(2,1)S(1)} %get-tuple-element.38), channel_id=1, source_target_pairs={{0,3},{1,2},{2,1},{3,0},{4,7},{5,6},{6,5},{7,4},{8,11},{9,10},{10,... | collective-permute-start | bytes 196616 | tf_op jit(solution)/shard_map/ppermute | solution.py:87
  17.7 0.5 collective-permute-start.8
  18.2 0.5 collective-permute-start.9
  18.8 1.8 %collective-permute-done.7.refs_1_ = bf16[128,256]{1,0:T(8,128)(2,1)S(1)} collective-permute-done((bf16[128,256]{1,0:T(8,128)(2,1)S(1)}, bf16[128,256]{1,0:T(8,128)(2,1)S(1)}, u32[]{:S(2)}, u32[]{:S(2)}) %collective-permute-start.7) | collective-permute-done | bytes 65568 | tf_op jit(solution)/shard_map/ppermute | solution.py:87
  20.5 1.5 %collective-permute-done.8.refs_2_ = bf16[128,256]{1,0:T(8,128)(2,1)S(1)} collective-permute-done((bf16[128,256]{1,0:T(8,128)(2,1)S(1)}, bf16[128,256]{1,0:T(8,128)(2,1)S(1)}, u32[]{:S(2)}, u32[]{:S(2)}) %collective-permute-start.8) | collective-permute-done | bytes 65568 | tf_op jit(solution)/shard_map/ppermute | solution.py:87
  22.0 0.5 collective-permute-done.9.refs_3_
  22.5 0.4 dense.1
  22.9 0.1 collective-permute-start.10
  23.0 1.3 %collective-permute-done.10.came_ref = bf16[256,256]{1,0:T(8,128)(2,1)S(1)} collective-permute-done((bf16[256,256]{1,0:T(8,128)(2,1)S(1)}, bf16[256,256]{1,0:T(8,128)(2,1)S(1)}, u32[]{:S(2)}, u32[]{:S(2)}) %collective-permute-start.10) | collective-permute-done | bytes 131104 | tf_op jit(solution)/shard_map/ppermute | solution.py:87
  24.3 0.1 split.1
  24.4 0.7 %collective-permute-start.14 = (bf16[64,256]{1,0:T(8,128)(2,1)S(1)}, bf16[64,256]{1,0:T(8,128)(2,1)S(1)}, u32[]{:S(2)}, u32[]{:S(2)}) collective-permute-start(bf16[64,256]{1,0:T(8,128)(2,1)S(1)} %get-tuple-element.50), channel_id=1, source_target_pairs={{4,7},{5,6},{6,5},{7,4},{12,15},{13,14},{14,13},{15,12},{20,23},{2... | collective-permute-start | bytes 98312 | tf_op jit(solution)/shard_map/ppermute | solution.py:280
  25.1 0.7 %collective-permute-start.15 = (bf16[64,256]{1,0:T(8,128)(2,1)S(1)}, bf16[64,256]{1,0:T(8,128)(2,1)S(1)}, u32[]{:S(2)}, u32[]{:S(2)}) collective-permute-start(bf16[64,256]{1,0:T(8,128)(2,1)S(1)} %get-tuple-element.51), channel_id=1, source_target_pairs={{4,6},{5,7},{6,4},{7,5},{12,14},{13,15},{14,12},{15,13},{20,22},{2... | collective-permute-start | bytes 98312 | tf_op jit(solution)/shard_map/ppermute | solution.py:280
  25.7 0.7 %collective-permute-start.16 = (bf16[64,256]{1,0:T(8,128)(2,1)S(1)}, bf16[64,256]{1,0:T(8,128)(2,1)S(1)}, u32[]{:S(2)}, u32[]{:S(2)}) collective-permute-start(bf16[64,256]{1,0:T(8,128)(2,1)S(1)} %get-tuple-element.52), channel_id=1, source_target_pairs={{4,5},{5,4},{6,7},{7,6},{12,13},{13,12},{14,15},{15,14},{20,21},{2... | collective-permute-start | bytes 98312 | tf_op jit(solution)/shard_map/ppermute | solution.py:280
  26.4 0.0 collective-permute-done.14.refs_1_
  26.4 0.0 collective-permute-done.16.refs_3_
  26.5 0.7 %collective-permute-start.19 = (bf16[64,256]{1,0:T(8,128)(2,1)S(1)}, bf16[64,256]{1,0:T(8,128)(2,1)S(1)}, u32[]{:S(2)}, u32[]{:S(2)}) collective-permute-start(bf16[64,256]{1,0:T(8,128)(2,1)S(1)} %add.2.refs_0_), channel_id=1, source_target_pairs={{4,28},{5,29},{6,30},{7,31},{12,20},{13,21},{14,22},{15,23},{20,12... | collective-permute-start | bytes 98312 | tf_op jit(solution)/shard_map/ppermute | solution.py:280
  27.1 4.3 %collective-permute-start.11 = (bf16[128,256]{1,0:T(8,128)(2,1)S(1)}, bf16[128,256]{1,0:T(8,128)(2,1)S(1)}, u32[]{:S(2)}, u32[]{:S(2)}) collective-permute-start(bf16[128,256]{1,0:T(8,128)(2,1)S(1)} %get-tuple-element.45), channel_id=1, source_target_pairs={{0,24},{1,25},{2,26},{3,27},{8,16},{9,17},{10,18},{11,19},{16,8},{... | collective-permute-start | bytes 196616 | tf_op jit(solution)/shard_map/ppermute | solution.py:280
  31.5 1.9 %collective-permute-start.12 = (bf16[128,256]{1,0:T(8,128)(2,1)S(1)}, bf16[128,256]{1,0:T(8,128)(2,1)S(1)}, u32[]{:S(2)}, u32[]{:S(2)}) collective-permute-start(bf16[128,256]{1,0:T(8,128)(2,1)S(1)} %get-tuple-element.46), channel_id=1, source_target_pairs={{0,16},{1,17},{2,18},{3,19},{8,24},{9,25},{10,26},{11,27},{16,0},{... | collective-permute-start | bytes 196616 | tf_op jit(solution)/shard_map/ppermute | solution.py:280
  33.4 0.7 %collective-permute-start.18 = (bf16[64,256]{1,0:T(8,128)(2,1)S(1)}, bf16[64,256]{1,0:T(8,128)(2,1)S(1)}, u32[]{:S(2)}, u32[]{:S(2)}) collective-permute-start(bf16[64,256]{1,0:T(8,128)(2,1)S(1)} %add.2.refs_0_), channel_id=1, source_target_pairs={{4,20},{5,21},{6,22},{7,23},{12,28},{13,29},{14,30},{15,31},{20,4}... | collective-permute-start | bytes 98312 | tf_op jit(solution)/shard_map/ppermute | solution.py:280
  34.1 0.7 %collective-permute-start.17 = (bf16[64,256]{1,0:T(8,128)(2,1)S(1)}, bf16[64,256]{1,0:T(8,128)(2,1)S(1)}, u32[]{:S(2)}, u32[]{:S(2)}) collective-permute-start(bf16[64,256]{1,0:T(8,128)(2,1)S(1)} %add.2.refs_0_), channel_id=1, source_target_pairs={{4,12},{5,13},{6,14},{7,15},{12,4},{13,5},{14,6},{15,7},{20,28},{2... | collective-permute-start | bytes 98312 | tf_op jit(solution)/shard_map/ppermute | solution.py:280
  34.8 3.9 %collective-permute-start.13 = (bf16[128,256]{1,0:T(8,128)(2,1)S(1)}, bf16[128,256]{1,0:T(8,128)(2,1)S(1)}, u32[]{:S(2)}, u32[]{:S(2)}) collective-permute-start(bf16[128,256]{1,0:T(8,128)(2,1)S(1)} %get-tuple-element.47), channel_id=1, source_target_pairs={{0,8},{1,9},{2,10},{3,11},{8,0},{9,1},{10,2},{11,3},{16,24},{17,25... | collective-permute-start | bytes 196616 | tf_op jit(solution)/shard_map/ppermute | solution.py:280
  38.6 0.0 collective-permute-done.18.refs_2_
  38.7 0.7 %collective-permute-start.22 = (bf16[64,256]{1,0:T(8,128)(2,1)S(1)}, bf16[64,256]{1,0:T(8,128)(2,1)S(1)}, u32[]{:S(2)}, u32[]{:S(2)}) collective-permute-start(bf16[64,256]{1,0:T(8,128)(2,1)S(1)} %add.3.refs_0_), channel_id=1, source_target_pairs={{4,7},{5,6},{6,5},{7,4},{12,15},{13,14},{14,13},{15,12},{20,23},{2... | collective-permute-start | bytes 98312 | tf_op jit(solution)/shard_map/ppermute | solution.py:280
  39.4 0.7 %collective-permute-start.21 = (bf16[64,256]{1,0:T(8,128)(2,1)S(1)}, bf16[64,256]{1,0:T(8,128)(2,1)S(1)}, u32[]{:S(2)}, u32[]{:S(2)}) collective-permute-start(bf16[64,256]{1,0:T(8,128)(2,1)S(1)} %add.3.refs_0_), channel_id=1, source_target_pairs={{4,6},{5,7},{6,4},{7,5},{12,14},{13,15},{14,12},{15,13},{20,22},{2... | collective-permute-start | bytes 98312 | tf_op jit(solution)/shard_map/ppermute | solution.py:280
  40.0 0.7 %collective-permute-start.20 = (bf16[64,256]{1,0:T(8,128)(2,1)S(1)}, bf16[64,256]{1,0:T(8,128)(2,1)S(1)}, u32[]{:S(2)}, u32[]{:S(2)}) collective-permute-start(bf16[64,256]{1,0:T(8,128)(2,1)S(1)} %add.3.refs_0_), channel_id=1, source_target_pairs={{4,5},{5,4},{6,7},{7,6},{12,13},{13,12},{14,15},{15,14},{20,21},{2... | collective-permute-start | bytes 98312 | tf_op jit(solution)/shard_map/ppermute | solution.py:280
  40.7 0.2 collective-permute-done.13.refs_3_
  41.0 16.7 %collective-permute-start.23 = (bf16[256,256]{1,0:T(8,128)(2,1)S(1)}, bf16[256,256]{1,0:T(8,128)(2,1)S(1)}, u32[]{:S(2)}, u32[]{:S(2)}) collective-permute-start(bf16[256,256]{1,0:T(8,128)(2,1)S(1)} %get-tuple-element.55), channel_id=1, source_target_pairs={{0,4},{4,0},{8,12},{12,8},{16,20},{20,16},{24,28},{28,24},{1,5},{5... | collective-permute-start | bytes 393224 | tf_op jit(solution)/shard_map/ppermute | solution.py:87
  57.7 1.0 %collective-permute-done.23.came_ref = bf16[256,256]{1,0:T(8,128)(2,1)S(1)} collective-permute-done((bf16[256,256]{1,0:T(8,128)(2,1)S(1)}, bf16[256,256]{1,0:T(8,128)(2,1)S(1)}, u32[]{:S(2)}, u32[]{:S(2)}) %collective-permute-start.23) | collective-permute-done | bytes 131104 | tf_op jit(solution)/shard_map/ppermute | solution.py:87
  58.7 0.8 %finish.1 = (bf16[256,256]{1,0:T(8,128)(2,1)}, f32[256,256]{1,0:T(8,128)}) custom-call(bf16[256,256]{1,0:T(8,128)(2,1)S(1)} %bitcast.9, bf16[256,256]{1,0:T(8,128)(2,1)S(1)} %bitcast.8, bf16[256,256]{1,0:T(8,128)(2,1)S(1)} %collective-permute-done.23.came_ref), custom_call_target="tpu_custom_call" | custom-call | tf_op jit(solution)/shard_map/finish/pallas_call | solution.py:260
  (21 shorter events, 0.1 us)
Async XLA Ops:
  0.6 8.5 %collective-permute-start = (bf16[128,256]{1,0:T(8,128)(2,1)}, bf16[128,256]{1,0:T(8,128)(2,1)S(1)}, u32[]{:S(2)}, u32[]{:S(2)}) collective-permute-start(bf16[128,256]{1,0:T(8,128)(2,1)} %own_ref.1), channel_id=1, source_target_pairs={{0,8},{4,12},{8,0},{12,4},{16,24},{20,28},{24,16},{28,20},{1,9},{5... | collective-permute-start | bytes 196616 | tf_op jit(solution)/shard_map/ppermute | solution.py:87
  3.7 7.1 %collective-permute-start.5 = (bf16[128,256]{1,0:T(8,128)(2,1)}, bf16[128,256]{1,0:T(8,128)(2,1)S(1)}, u32[]{:S(2)}, u32[]{:S(2)}) collective-permute-start(bf16[128,256]{1,0:T(8,128)(2,1)} %own_ref.1), channel_id=1, source_target_pairs={{0,24},{4,28},{8,16},{12,20},{16,8},{20,12},{24,0},{28,4},{1,25},{... | collective-permute-start | bytes 196616 | tf_op jit(solution)/shard_map/ppermute | solution.py:87
  6.2 6.7 %collective-permute-start.3 = (bf16[128,256]{1,0:T(8,128)(2,1)}, bf16[128,256]{1,0:T(8,128)(2,1)S(1)}, u32[]{:S(2)}, u32[]{:S(2)}) collective-permute-start(bf16[128,256]{1,0:T(8,128)(2,1)} %own_ref.1), channel_id=1, source_target_pairs={{0,16},{4,20},{8,24},{12,28},{16,0},{20,4},{24,8},{28,12},{1,17},{... | collective-permute-start | bytes 196616 | tf_op jit(solution)/shard_map/ppermute | solution.py:87
  6.3 7.1 %collective-permute-start.1 = (bf16[128,256]{1,0:T(8,128)(2,1)}, bf16[128,256]{1,0:T(8,128)(2,1)S(1)}, u32[]{:S(2)}, u32[]{:S(2)}) collective-permute-start(bf16[128,256]{1,0:T(8,128)(2,1)} %own_ref.1), channel_id=1, source_target_pairs={{0,4},{4,0},{8,12},{12,8},{16,20},{20,16},{24,28},{28,24},{1,5},{5... | collective-permute-start | bytes 196616 | tf_op jit(solution)/shard_map/ppermute | solution.py:87
  6.3 0.7 %copy-start.5 = (s32[128,1]{0,1:T(1,128)S(1)}, s32[128,1]{0,1:T(1,128)}, u32[]{:S(2)}) copy-start(s32[128,1]{0,1:T(1,128)} %param.11) | copy-start | bytes 1540
  7.0 1.0 %copy-start = (bf16[4,1,4,128,128]{4,3,2,1,0:T(8,128)(2,1)S(1)}, bf16[4,1,4,128,128]{4,3,2,1,0:T(8,128)(2,1)}, u32[]{:S(2)}) copy-start(bf16[4,1,4,128,128]{4,3,2,1,0:T(8,128)(2,1)} %param.7) | copy-start | bytes 1572868
  8.0 0.8 %copy-start.2 = (bf16[128,256]{1,0:T(8,128)(2,1)S(1)}, bf16[128,256]{1,0:T(8,128)(2,1)}, u32[]{:S(2)}) copy-start(bf16[128,256]{1,0:T(8,128)(2,1)} %own_ref.1) | copy-start | bytes 196612
  9.1 5.2 %copy-start.4 = (s32[4,1,4]{2,1,0:T(1,128)S(1)}, s32[4,1,4]{2,1,0:T(1,128)}, u32[]{:S(2)}) copy-start(s32[4,1,4]{2,1,0:T(1,128)} %param.8) | copy-start | bytes 196
  10.8 2.6 %collective-permute-start.6 = (bf16[128,256]{1,0:T(8,128)(2,1)S(1)}, bf16[128,256]{1,0:T(8,128)(2,1)S(1)}, u32[]{:S(2)}, u32[]{:S(2)}) collective-permute-start(bf16[128,256]{1,0:T(8,128)(2,1)S(1)} %collective-permute-done.5.refs_6_), channel_id=1, source_target_pairs={{0,4},{4,0},{8,12},{12,8},{16,20},{20,16},{24,28},{28,24},{1,5},{5... | collective-permute-start | bytes 196616 | tf_op jit(solution)/shard_map/ppermute | solution.py:87
  12.9 1.3 %collective-permute-start.4 = (bf16[128,256]{1,0:T(8,128)(2,1)S(1)}, bf16[128,256]{1,0:T(8,128)(2,1)S(1)}, u32[]{:S(2)}, u32[]{:S(2)}) collective-permute-start(bf16[128,256]{1,0:T(8,128)(2,1)S(1)} %collective-permute-done.3.refs_4_), channel_id=1, source_target_pairs={{0,4},{4,0},{8,12},{12,8},{16,20},{20,16},{24,28},{28,24},{1,5},{5... | collective-permute-start | bytes 196616 | tf_op jit(solution)/shard_map/ppermute | solution.py:87
  12.9 1.4 %collective-permute-start.2 = (bf16[128,256]{1,0:T(8,128)(2,1)S(1)}, bf16[128,256]{1,0:T(8,128)(2,1)S(1)}, u32[]{:S(2)}, u32[]{:S(2)}) collective-permute-start(bf16[128,256]{1,0:T(8,128)(2,1)S(1)} %collective-permute-done.refs_2_), channel_id=1, source_target_pairs={{0,4},{4,0},{8,12},{12,8},{16,20},{20,16},{24,28},{28,24},{1,5},{5... | collective-permute-start | bytes 196616 | tf_op jit(solution)/shard_map/ppermute | solution.py:87
  14.3 8.2 %copy-start.1 = (bf16[256,256]{1,0:T(8,128)(2,1)S(1)}, bf16[256,256]{1,0:T(8,128)(2,1)}, u32[]{:S(2)}) copy-start(bf16[256,256]{1,0:T(8,128)(2,1)} %weight_ref.1) | copy-start | bytes 393220
  14.3 8.2 %copy-start.3 = (bf16[128,256]{1,0:T(8,128)(2,1)S(1)}, bf16[128,256]{1,0:T(8,128)(2,1)}, u32[]{:S(2)}) copy-start(bf16[128,256]{1,0:T(8,128)(2,1)} %cot_ref.1) | copy-start | bytes 196612
  15.2 5.3 %collective-permute-start.7 = (bf16[128,256]{1,0:T(8,128)(2,1)S(1)}, bf16[128,256]{1,0:T(8,128)(2,1)S(1)}, u32[]{:S(2)}, u32[]{:S(2)}) collective-permute-start(bf16[128,256]{1,0:T(8,128)(2,1)S(1)} %get-tuple-element.38), channel_id=1, source_target_pairs={{0,3},{1,2},{2,1},{3,0},{4,7},{5,6},{6,5},{7,4},{8,11},{9,10},{10,... | collective-permute-start | bytes 196616 | tf_op jit(solution)/shard_map/ppermute | solution.py:87
  17.7 4.3 %collective-permute-start.8 = (bf16[128,256]{1,0:T(8,128)(2,1)S(1)}, bf16[128,256]{1,0:T(8,128)(2,1)S(1)}, u32[]{:S(2)}, u32[]{:S(2)}) collective-permute-start(bf16[128,256]{1,0:T(8,128)(2,1)S(1)} %get-tuple-element.39), channel_id=1, source_target_pairs={{0,2},{1,3},{2,0},{3,1},{4,6},{5,7},{6,4},{7,5},{8,10},{9,11},{10,... | collective-permute-start | bytes 196616 | tf_op jit(solution)/shard_map/ppermute | solution.py:87
  18.2 4.3 %collective-permute-start.9 = (bf16[128,256]{1,0:T(8,128)(2,1)S(1)}, bf16[128,256]{1,0:T(8,128)(2,1)S(1)}, u32[]{:S(2)}, u32[]{:S(2)}) collective-permute-start(bf16[128,256]{1,0:T(8,128)(2,1)S(1)} %get-tuple-element.40), channel_id=1, source_target_pairs={{0,1},{1,0},{2,3},{3,2},{4,5},{5,4},{6,7},{7,6},{8,9},{9,8},{10,11... | collective-permute-start | bytes 196616 | tf_op jit(solution)/shard_map/ppermute | solution.py:87
  22.9 1.4 %collective-permute-start.10 = (bf16[256,256]{1,0:T(8,128)(2,1)S(1)}, bf16[256,256]{1,0:T(8,128)(2,1)S(1)}, u32[]{:S(2)}, u32[]{:S(2)}) collective-permute-start(bf16[256,256]{1,0:T(8,128)(2,1)S(1)} %get-tuple-element.43), channel_id=1, source_target_pairs={{0,4},{4,0},{8,12},{12,8},{16,20},{20,16},{24,28},{28,24},{1,5},{5... | collective-permute-start | bytes 393224 | tf_op jit(solution)/shard_map/ppermute | solution.py:87
  24.4 2.0 %collective-permute-start.14 = (bf16[64,256]{1,0:T(8,128)(2,1)S(1)}, bf16[64,256]{1,0:T(8,128)(2,1)S(1)}, u32[]{:S(2)}, u32[]{:S(2)}) collective-permute-start(bf16[64,256]{1,0:T(8,128)(2,1)S(1)} %get-tuple-element.50), channel_id=1, source_target_pairs={{4,7},{5,6},{6,5},{7,4},{12,15},{13,14},{14,13},{15,12},{20,23},{2... | collective-permute-start | bytes 98312 | tf_op jit(solution)/shard_map/ppermute | solution.py:280
  25.1 1.4 %collective-permute-start.15 = (bf16[64,256]{1,0:T(8,128)(2,1)S(1)}, bf16[64,256]{1,0:T(8,128)(2,1)S(1)}, u32[]{:S(2)}, u32[]{:S(2)}) collective-permute-start(bf16[64,256]{1,0:T(8,128)(2,1)S(1)} %get-tuple-element.51), channel_id=1, source_target_pairs={{4,6},{5,7},{6,4},{7,5},{12,14},{13,15},{14,12},{15,13},{20,22},{2... | collective-permute-start | bytes 98312 | tf_op jit(solution)/shard_map/ppermute | solution.py:280
  25.7 0.7 %collective-permute-start.16 = (bf16[64,256]{1,0:T(8,128)(2,1)S(1)}, bf16[64,256]{1,0:T(8,128)(2,1)S(1)}, u32[]{:S(2)}, u32[]{:S(2)}) collective-permute-start(bf16[64,256]{1,0:T(8,128)(2,1)S(1)} %get-tuple-element.52), channel_id=1, source_target_pairs={{4,5},{5,4},{6,7},{7,6},{12,13},{13,12},{14,15},{15,14},{20,21},{2... | collective-permute-start | bytes 98312 | tf_op jit(solution)/shard_map/ppermute | solution.py:280
  26.5 8.3 %collective-permute-start.19 = (bf16[64,256]{1,0:T(8,128)(2,1)S(1)}, bf16[64,256]{1,0:T(8,128)(2,1)S(1)}, u32[]{:S(2)}, u32[]{:S(2)}) collective-permute-start(bf16[64,256]{1,0:T(8,128)(2,1)S(1)} %add.2.refs_0_), channel_id=1, source_target_pairs={{4,28},{5,29},{6,30},{7,31},{12,20},{13,21},{14,22},{15,23},{20,12... | collective-permute-start | bytes 98312 | tf_op jit(solution)/shard_map/ppermute | solution.py:280
  27.1 12.9 %collective-permute-start.11 = (bf16[128,256]{1,0:T(8,128)(2,1)S(1)}, bf16[128,256]{1,0:T(8,128)(2,1)S(1)}, u32[]{:S(2)}, u32[]{:S(2)}) collective-permute-start(bf16[128,256]{1,0:T(8,128)(2,1)S(1)} %get-tuple-element.45), channel_id=1, source_target_pairs={{0,24},{1,25},{2,26},{3,27},{8,16},{9,17},{10,18},{11,19},{16,8},{... | collective-permute-start | bytes 196616 | tf_op jit(solution)/shard_map/ppermute | solution.py:280
  31.5 9.2 %collective-permute-start.12 = (bf16[128,256]{1,0:T(8,128)(2,1)S(1)}, bf16[128,256]{1,0:T(8,128)(2,1)S(1)}, u32[]{:S(2)}, u32[]{:S(2)}) collective-permute-start(bf16[128,256]{1,0:T(8,128)(2,1)S(1)} %get-tuple-element.46), channel_id=1, source_target_pairs={{0,16},{1,17},{2,18},{3,19},{8,24},{9,25},{10,26},{11,27},{16,0},{... | collective-permute-start | bytes 196616 | tf_op jit(solution)/shard_map/ppermute | solution.py:280
  33.4 5.2 %collective-permute-start.18 = (bf16[64,256]{1,0:T(8,128)(2,1)S(1)}, bf16[64,256]{1,0:T(8,128)(2,1)S(1)}, u32[]{:S(2)}, u32[]{:S(2)}) collective-permute-start(bf16[64,256]{1,0:T(8,128)(2,1)S(1)} %add.2.refs_0_), channel_id=1, source_target_pairs={{4,20},{5,21},{6,22},{7,23},{12,28},{13,29},{14,30},{15,31},{20,4}... | collective-permute-start | bytes 98312 | tf_op jit(solution)/shard_map/ppermute | solution.py:280
  34.1 4.6 %collective-permute-start.17 = (bf16[64,256]{1,0:T(8,128)(2,1)S(1)}, bf16[64,256]{1,0:T(8,128)(2,1)S(1)}, u32[]{:S(2)}, u32[]{:S(2)}) collective-permute-start(bf16[64,256]{1,0:T(8,128)(2,1)S(1)} %add.2.refs_0_), channel_id=1, source_target_pairs={{4,12},{5,13},{6,14},{7,15},{12,4},{13,5},{14,6},{15,7},{20,28},{2... | collective-permute-start | bytes 98312 | tf_op jit(solution)/shard_map/ppermute | solution.py:280
  34.8 6.2 %collective-permute-start.13 = (bf16[128,256]{1,0:T(8,128)(2,1)S(1)}, bf16[128,256]{1,0:T(8,128)(2,1)S(1)}, u32[]{:S(2)}, u32[]{:S(2)}) collective-permute-start(bf16[128,256]{1,0:T(8,128)(2,1)S(1)} %get-tuple-element.47), channel_id=1, source_target_pairs={{0,8},{1,9},{2,10},{3,11},{8,0},{9,1},{10,2},{11,3},{16,24},{17,25... | collective-permute-start | bytes 196616 | tf_op jit(solution)/shard_map/ppermute | solution.py:280
  38.7 2.3 %collective-permute-start.22 = (bf16[64,256]{1,0:T(8,128)(2,1)S(1)}, bf16[64,256]{1,0:T(8,128)(2,1)S(1)}, u32[]{:S(2)}, u32[]{:S(2)}) collective-permute-start(bf16[64,256]{1,0:T(8,128)(2,1)S(1)} %add.3.refs_0_), channel_id=1, source_target_pairs={{4,7},{5,6},{6,5},{7,4},{12,15},{13,14},{14,13},{15,12},{20,23},{2... | collective-permute-start | bytes 98312 | tf_op jit(solution)/shard_map/ppermute | solution.py:280
  39.4 1.6 %collective-permute-start.21 = (bf16[64,256]{1,0:T(8,128)(2,1)S(1)}, bf16[64,256]{1,0:T(8,128)(2,1)S(1)}, u32[]{:S(2)}, u32[]{:S(2)}) collective-permute-start(bf16[64,256]{1,0:T(8,128)(2,1)S(1)} %add.3.refs_0_), channel_id=1, source_target_pairs={{4,6},{5,7},{6,4},{7,5},{12,14},{13,15},{14,12},{15,13},{20,22},{2... | collective-permute-start | bytes 98312 | tf_op jit(solution)/shard_map/ppermute | solution.py:280
  40.0 0.9 %collective-permute-start.20 = (bf16[64,256]{1,0:T(8,128)(2,1)S(1)}, bf16[64,256]{1,0:T(8,128)(2,1)S(1)}, u32[]{:S(2)}, u32[]{:S(2)}) collective-permute-start(bf16[64,256]{1,0:T(8,128)(2,1)S(1)} %add.3.refs_0_), channel_id=1, source_target_pairs={{4,5},{5,4},{6,7},{7,6},{12,13},{13,12},{14,15},{15,14},{20,21},{2... | collective-permute-start | bytes 98312 | tf_op jit(solution)/shard_map/ppermute | solution.py:280
  41.0 17.7 %collective-permute-start.23 = (bf16[256,256]{1,0:T(8,128)(2,1)S(1)}, bf16[256,256]{1,0:T(8,128)(2,1)S(1)}, u32[]{:S(2)}, u32[]{:S(2)}) collective-permute-start(bf16[256,256]{1,0:T(8,128)(2,1)S(1)} %get-tuple-element.55), channel_id=1, source_target_pairs={{0,4},{4,0},{8,12},{12,8},{16,20},{20,16},{24,28},{28,24},{1,5},{5... | collective-permute-start | bytes 393224 | tf_op jit(solution)/shard_map/ppermute | solution.py:87

commit v6 on v5

--- a/solution.py
+++ b/solution.py
@@ -141,73 +141,120 @@
     )(weight, cotangent, placing, *parts)
 
 
-def split_kernel(n_rep, packed_ref, term_ref, came_ref, own_ref, *refs):
-    chunk_refs, message_refs, term = refs[: n_rep - 1], refs[n_rep - 1 : -1], refs[-1]
-    rep = lax.axis_index("rep")
-    width = term_ref.shape[0]
-    total = term_ref[...] + came_ref[:width].astype(jnp.float32)
+def split_kernel(packed_ref, term_ref, came_ref, own_ref, *refs):
+    out_refs, term = refs[:-1], refs[-1]
+    rep, core = lax.axis_index("rep"), lax.axis_index("section") & 1
+    n_rep, chunk = term.shape[:2]
+    total = term_ref[...] + came_ref[: n_rep * chunk].astype(jnp.float32)
     term[...] = total.reshape(term.shape)
     own_ref[...] = term[rep]
-    for ref, j in zip(chunk_refs, across(n_rep)):
-        ref[...] = term[rep ^ j].astype(jnp.bfloat16)
-    rows = packed_ref.shape[0] // len(message_refs)
-    for ref, j in zip(message_refs, [0] + across(len(message_refs))):
-        ref[:rows] = packed_ref[j * rows : (j + 1) * rows]
-        ref[rows:] = came_ref[j * rows : (j + 1) * rows]
+    rows = 2 * packed_ref.shape[0] // lax.axis_size("section")
+
+    @pl.when(core == 1)
+    def _():
+        for ref, j in zip(out_refs, across(len(out_refs) + 1)):
+            ref[:chunk] = term[rep ^ (j % n_rep)].astype(jnp.bfloat16)
+
+    @pl.when(core == 0)
+    def _():
+        for ref, j in zip(out_refs, across(len(out_refs) + 1)):
+            start = j * rows % packed_ref.shape[0]
+            ref[:rows] = packed_ref[start : start + rows]
 
 
 def split(packed, term, came, n_rep, chips):
     places, width = packed.shape
-    chunk = (width // n_rep, width)
-    return pl.pallas_call(
-        functools.partial(split_kernel, n_rep),
-        out_shape=[jax.ShapeDtypeStruct(chunk, jnp.float32)]
-        + [jax.ShapeDtypeStruct(chunk, jnp.bfloat16)] * (n_rep - 1)
-        + [jax.ShapeDtypeStruct((2 * places // chips, width), jnp.bfloat16)] * chips,
+    chunk = width // n_rep
+    out = jax.ShapeDtypeStruct((max(chunk, places // chips), width), jnp.bfloat16)
+    many = max(n_rep, chips)
+    return pl.pallas_call(
+        split_kernel,
+        out_shape=[jax.ShapeDtypeStruct((chunk, width), jnp.float32)] + [out] * (many - 1),
         in_specs=[VMEM] * 3,
-        out_specs=[VMEM] * (n_rep + chips),
-        scratch_shapes=[pltpu.VMEM((n_rep,) + chunk, jnp.float32)],
+        out_specs=[VMEM] * many,
+        scratch_shapes=[pltpu.VMEM((n_rep, chunk, width), jnp.float32)],
         compiler_params=LIMIT,
         name="split",
     )(packed, term, came)
 
 
-def add_kernel(*refs):
-    refs[-1][...] = tree_sum([ref[...].astype(jnp.float32) for ref in refs[:-1]]).astype(jnp.bfloat16)
-
-
-def add(terms):
+def second_kernel(n_rep, packed_ref, came_ref, own_ref, *refs):
+    term_refs, chunk_ref, out_refs = refs[: n_rep - 1], refs[n_rep - 1], refs[n_rep:]
+    core = lax.axis_index("section") & 1
+    chunk = own_ref.shape[0]
+    terms = [own_ref[...]] + [ref[:chunk].astype(jnp.float32) for ref in term_refs]
+    total = tree_sum(terms).astype(jnp.bfloat16)
+    chunk_ref[...] = total
+    rows = packed_ref.shape[0] // (len(out_refs) + 1)
+
+    @pl.when(core == 1)
+    def _():
+        for ref in out_refs:
+            ref[:chunk] = total
+
+    @pl.when(core == 0)
+    def _():
+        for ref, j in zip(out_refs, across(len(out_refs) + 1)):
+            ref[:rows] = came_ref[j * rows : (j + 1) * rows]
+
+
+def second(packed, came, own, terms, chips):
+    places, width = packed.shape
+    chunk = own.shape[0]
+    out = jax.ShapeDtypeStruct((max(chunk, places // chips), width), jnp.bfloat16)
+    return pl.pallas_call(
+        functools.partial(second_kernel, len(terms) + 1),
+        out_shape=[jax.ShapeDtypeStruct((chunk, width), jnp.bfloat16)] + [out] * (chips - 1),
+        in_specs=[VMEM] * (3 + len(terms)),
+        out_specs=[VMEM] * chips,
+        compiler_params=LIMIT,
+        name="second",
+    )(packed, came, own, *terms)
+
+
+def add_kernel(own_ref, *refs):
+    chunk = own_ref.shape[0]
+    by_xor = [own_ref] + list(refs[-2::-1])
+    total = tree_sum([ref[:chunk].astype(jnp.float32) for ref in by_xor])
+    refs[-1][...] = total.astype(jnp.bfloat16)
+
+
+def add(own, others):
     return pl.pallas_call(
         add_kernel,
-        out_shape=jax.ShapeDtypeStruct(terms[0].shape, jnp.bfloat16),
-        in_specs=[VMEM] * len(terms),
+        out_shape=jax.ShapeDtypeStruct(own.shape, jnp.bfloat16),
+        in_specs=[VMEM] * (1 + len(others)),
         out_specs=VMEM,
         compiler_params=LIMIT,
         name="add",
-    )(*terms)
-
-
-def unpack_kernel(slots, *refs):
-    message_refs, out_refs = refs[:-2], refs[-2:]
+    )(own, *others)
+
+
+def unpack_kernel(slots, chips, packed_ref, came_ref, *refs):
+    out_refs = refs[-2:]
     chip = lax.axis_index("section") & -2
-    for j, ref in zip([0] + across(len(message_refs)), message_refs):
-        for source in range(2):
+    sources = (
+        [packed_ref] + list(refs[: chips - 1]),
+        [came_ref] + list(refs[chips - 1 : -2]),
+    )
+    for source in range(2):
+        for ref, j in zip(sources[source], [0] + across(chips)):
             for core in range(2):
-                start = (2 * source + core) * slots
-                out_refs[core][chip ^ (2 * j) | source] = ref[start : start + slots]
-
-
-def unpack(messages, slots):
-    width = messages[0].shape[1]
-    n_section = 2 * len(messages)
-    return pl.pallas_call(
-        functools.partial(unpack_kernel, slots),
-        out_shape=[jax.ShapeDtypeStruct((n_section, slots, width), jnp.bfloat16)] * 2,
-        in_specs=[VMEM] * len(messages),
+                rows = ref[core * slots : (core + 1) * slots]
+                out_refs[core][chip ^ (2 * j) | source] = rows
+
+
+def unpack(packed, came, first, later, slots):
+    width = packed.shape[1]
+    chips = len(first) + 1
+    return pl.pallas_call(
+        functools.partial(unpack_kernel, slots, chips),
+        out_shape=[jax.ShapeDtypeStruct((2 * chips, slots, width), jnp.bfloat16)] * 2,
+        in_specs=[VMEM] * (2 * chips),
         out_specs=[VMEM] * 2,
         compiler_params=LIMIT,
         name="unpack",
-    )(*messages)
+    )(packed, came, *first, *later)
 
 
 def place_kernel(other_ref, *refs):
@@ -270,11 +317,12 @@
     )(whole, mine, came)
 
 
-def swap_on_core(value, core, section_xor, rep_xor):
-    n_rep = lax.axis_size("rep")
+def swap_by_core(value, j):
+    n_section, n_rep = lax.axis_size("section"), lax.axis_size("rep")
+    along, side = 2 * j % n_section, j % n_rep
     pairs = [
-        (s * n_rep + r, (s ^ section_xor) * n_rep + (r ^ rep_xor))
-        for s in range(core, lax.axis_size("section"), 2)
+        (s * n_rep + r, s * n_rep + (r ^ side) if s & 1 else (s ^ along) * n_rep + r)
+        for s in range(n_section)
         for r in range(n_rep)
     ]
     return lax.ppermute(value, ("section", "rep"), pairs)
@@ -307,15 +355,13 @@
     packed, term, sent = dense(parts, weight, cotangent, placing)
     came = swap(sent, "section", 1)
     chips = n_section // 2
-    own, *rest = split(packed, term, came, n_rep, chips)
-    terms, messages = rest[: n_rep - 1], rest[n_rep - 1 :]
-    terms = [swap_on_core(t, 1, 0, j) for t, j in zip(terms, others)]
-    chunk = add([own] + terms)
-    others = across(chips)
-    messages = messages[:1] + [swap_on_core(m, 0, 2 * j, 0) for m, j in zip(messages[1:], others)]
-    chunk = add([chunk] + [swap_on_core(chunk, 1, 2 * j, 0) for j in range(1, chips)])
-    mine, other = unpack(messages, slots)
-    chunks = [chunk] + [swap_on_core(chunk, 1, 0, j) for j in range(1, n_rep)]
+    own, *first = split(packed, term, came, n_rep, chips)
+    first = [swap_by_core(value, j) for value, j in zip(first, across(len(first) + 1))]
+    chunk, *later = second(packed, came, own, first[1 - n_rep :], chips)
+    later = [swap(value, "section", 2 * j) for value, j in zip(later, across(chips))]
+    chunk = add(chunk, later)
+    mine, other = unpack(packed, came, first[1 - chips :], later, slots)
+    chunks = [chunk] + [swap(chunk, "rep", j) for j in range(1, n_rep)]
     whole, sent = place(chunks, other.reshape(n_section * slots, width))
     came = swap(sent, "section", 1)
     relaid, weight_grad = finish(

time: 59.9 us -> 47.6 us (0.79)
  starting transfers between devices: 42.6 us -> 22.4 us
  waiting for transfers between devices: 10.9 us -> 19.3 us
    ppermute x12 -> x3, starting transfers between devices: 16.1 us -> 4.45 us  [swap_by_core(): return lax.ppermute(value, ('section', 'rep'), pairs)]
    ppermute x12 -> x18, starting transfers between devices: 26.5 us -> 17.9 us  [swap(): lax.ppermute(value, axis, [(i, i ^ j) for i in range(lax.axis_size(axis))])]
    ppermute x12 -> x18, waiting for transfers between devices: 10.7 us -> 16.3 us  [swap(): lax.ppermute(value, axis, [(i, i ^ j) for i in range(lax.axis_size(axis))])]
    ppermute x12 -> x3, waiting for transfers between devices: 0.22 us -> 3.04 us  [swap_by_core(): return lax.ppermute(value, ('section', 'rep'), pairs)]
  transfers between devices with their start and end apart: 24 -> 21, of which waited for: 10 -> 16; matrix products, arithmetic and copies ran while one was open for 0% -> 0% of each run, Pallas kernels for 0% -> 1%
where the time goes in v6:
time: 47.6 us; the launch traced here: 47.4 us
  starting transfers between devices  22.4 us (47%)
  waiting for transfers between devices  19.3 us (41%)
  local copies, waits for them, and re-layouts  2.55 us (5%)
  Pallas kernels  2.47 us (5%)
  between operations  0.74 us (2%)
    ppermute x18, starting transfers between devices, swap(): lax.ppermute(value, axis, [(i, i ^ j) for i in range(lax.axis_size(axis))])  17.9 us
    ppermute x18, waiting for transfers between devices, swap(): lax.ppermute(value, axis, [(i, i ^ j) for i in range(lax.axis_size(axis))])  16.3 us
    ppermute x3, starting transfers between devices, swap_by_core(): return lax.ppermute(value, ('section', 'rep'), pairs)  4.45 us
    ppermute x3, waiting for transfers between devices, swap_by_core(): return lax.ppermute(value, ('section', 'rep'), pairs)  3.04 us
    unnamed x12, local copies, waits for them, and re-layouts  2.55 us
  transfers between devices with their start and end apart: 21, of which 16 were waited for; matrix products, arithmetic and copies ran while one was open for 0% of the time, Pallas kernels for 1%

profile of v6, /device:TPU:0, one launch (start us, length us, event | category | flops | bytes accessed | tf_op | source)
XLA Modules:
  0.0 47.4 jit_solution(6058315520366975485)
XLA Ops:
  0.6 3.1 %collective-permute-start = (bf16[128,256]{1,0:T(8,128)(2,1)}, bf16[128,256]{1,0:T(8,128)(2,1)S(1)}, u32[]{:S(2)}, u32[]{:S(2)}) collective-permute-start(bf16[128,256]{1,0:T(8,128)(2,1)} %own_ref.1), channel_id=1, source_target_pairs={{0,8},{4,12},{8,0},{12,4},{16,24},{20,28},{24,16},{28,20},{1,9},{5... | collective-permute-start | bytes 196616 | tf_op jit(solution)/shard_map/ppermute | solution.py:87
  3.7 2.5 %collective-permute-start.5 = (bf16[128,256]{1,0:T(8,128)(2,1)}, bf16[128,256]{1,0:T(8,128)(2,1)S(1)}, u32[]{:S(2)}, u32[]{:S(2)}) collective-permute-start(bf16[128,256]{1,0:T(8,128)(2,1)} %own_ref.1), channel_id=1, source_target_pairs={{0,24},{4,28},{8,16},{12,20},{16,8},{20,12},{24,0},{28,4},{1,25},{... | collective-permute-start | bytes 196616 | tf_op jit(solution)/shard_map/ppermute | solution.py:87
  6.2 0.1 collective-permute-start.3
  6.3 0.0 collective-permute-start.1
  6.3 0.7 %copy-done.5 = s32[128,1]{0,1:T(1,128)S(1)} copy-done((s32[128,1]{0,1:T(1,128)S(1)}, s32[128,1]{0,1:T(1,128)}, u32[]{:S(2)}) %copy-start.5) | copy-done | bytes 536
  7.0 1.0 %copy-done = bf16[4,1,4,128,128]{4,3,2,1,0:T(8,128)(2,1)S(1)} copy-done((bf16[4,1,4,128,128]{4,3,2,1,0:T(8,128)(2,1)S(1)}, bf16[4,1,4,128,128]{4,3,2,1,0:T(8,128)(2,1)}, u32[]{:S(2)}) %copy-start) | copy-done | bytes 524312
  8.0 0.8 %copy-done.2 = bf16[128,256]{1,0:T(8,128)(2,1)S(1)} copy-done((bf16[128,256]{1,0:T(8,128)(2,1)S(1)}, bf16[128,256]{1,0:T(8,128)(2,1)}, u32[]{:S(2)}) %copy-start.2) | copy-done | bytes 65560
  8.9 0.2 prepare.1
  9.1 0.0 collective-permute-done.refs_2_
  9.1 0.0 copy-start.4
  9.1 1.7 %collective-permute-done.5.refs_6_ = bf16[128,256]{1,0:T(8,128)(2,1)S(1)} collective-permute-done((bf16[128,256]{1,0:T(8,128)(2,1)}, bf16[128,256]{1,0:T(8,128)(2,1)S(1)}, u32[]{:S(2)}, u32[]{:S(2)}) %collective-permute-start.5) | collective-permute-done | bytes 65568 | tf_op jit(solution)/shard_map/ppermute | solution.py:87
  10.8 0.0 collective-permute-start.6
  10.8 2.1 %collective-permute-done.3.refs_4_ = bf16[128,256]{1,0:T(8,128)(2,1)S(1)} collective-permute-done((bf16[128,256]{1,0:T(8,128)(2,1)}, bf16[128,256]{1,0:T(8,128)(2,1)S(1)}, u32[]{:S(2)}, u32[]{:S(2)}) %collective-permute-start.3) | collective-permute-done | bytes 65568 | tf_op jit(solution)/shard_map/ppermute | solution.py:87
  12.9 0.0 collective-permute-start.4
  12.9 0.5 %collective-permute-start.2 = (bf16[128,256]{1,0:T(8,128)(2,1)S(1)}, bf16[128,256]{1,0:T(8,128)(2,1)S(1)}, u32[]{:S(2)}, u32[]{:S(2)}) collective-permute-start(bf16[128,256]{1,0:T(8,128)(2,1)S(1)} %collective-permute-done.refs_2_), channel_id=1, source_target_pairs={{0,4},{4,0},{8,12},{12,8},{16,20},{20,16},{24,28},{28,24},{1,5},{5... | collective-permute-start | bytes 196616 | tf_op jit(solution)/shard_map/ppermute | solution.py:87
  13.4 0.0 collective-permute-done.1.refs_1_
  13.4 0.0 collective-permute-done.6.refs_7_
  13.4 0.7 %collective-permute-done.4.refs_5_ = bf16[128,256]{1,0:T(8,128)(2,1)S(1)} collective-permute-done((bf16[128,256]{1,0:T(8,128)(2,1)S(1)}, bf16[128,256]{1,0:T(8,128)(2,1)S(1)}, u32[]{:S(2)}, u32[]{:S(2)}) %collective-permute-start.4) | collective-permute-done | bytes 65568 | tf_op jit(solution)/shard_map/ppermute | solution.py:87
  14.1 0.2 collective-permute-done.2.refs_3_
  14.3 0.9 %partials.1 = (bf16[128,256]{1,0:T(8,128)(2,1)S(1)}, bf16[128,256]{1,0:T(8,128)(2,1)S(1)}, bf16[128,256]{1,0:T(8,128)(2,1)S(1)}, bf16[128,256]{1,0:T(8,128)(2,1)S(1)}) custom-call(s32[4,4]{1,0:T(4,128)S(1)} %bitcast.11, bf16[4,128,512]{2,1,0:T(8,128)(2,1)S(1)} %get-tuple-element.34.wide_ref, bf16[128,256]{1,0:T(8,128)(2,1)S(1)} %get-tuple-element.35.refs_0_, ...), custom_call_target="tpu_custom_call" | custom-call | tf_op jit(solution)/shard_map/partials/pallas_call | solution.py:75
  15.2 2.5 %collective-permute-start.7 = (bf16[128,256]{1,0:T(8,128)(2,1)S(1)}, bf16[128,256]{1,0:T(8,128)(2,1)S(1)}, u32[]{:S(2)}, u32[]{:S(2)}) collective-permute-start(bf16[128,256]{1,0:T(8,128)(2,1)S(1)} %get-tuple-element.38), channel_id=1, source_target_pairs={{0,3},{1,2},{2,1},{3,0},{4,7},{5,6},{6,5},{7,4},{8,11},{9,10},{10,... | collective-permute-start | bytes 196616 | tf_op jit(solution)/shard_map/ppermute | solution.py:87
  17.7 0.5 %collective-permute-start.8 = (bf16[128,256]{1,0:T(8,128)(2,1)S(1)}, bf16[128,256]{1,0:T(8,128)(2,1)S(1)}, u32[]{:S(2)}, u32[]{:S(2)}) collective-permute-start(bf16[128,256]{1,0:T(8,128)(2,1)S(1)} %get-tuple-element.39), channel_id=1, source_target_pairs={{0,2},{1,3},{2,0},{3,1},{4,6},{5,7},{6,4},{7,5},{8,10},{9,11},{10,... | collective-permute-start | bytes 196616 | tf_op jit(solution)/shard_map/ppermute | solution.py:87
  18.2 0.5 %collective-permute-start.9 = (bf16[128,256]{1,0:T(8,128)(2,1)S(1)}, bf16[128,256]{1,0:T(8,128)(2,1)S(1)}, u32[]{:S(2)}, u32[]{:S(2)}) collective-permute-start(bf16[128,256]{1,0:T(8,128)(2,1)S(1)} %get-tuple-element.40), channel_id=1, source_target_pairs={{0,1},{1,0},{2,3},{3,2},{4,5},{5,4},{6,7},{7,6},{8,9},{9,8},{10,11... | collective-permute-start | bytes 196616 | tf_op jit(solution)/shard_map/ppermute | solution.py:87
  18.8 1.8 %collective-permute-done.7.refs_1_ = bf16[128,256]{1,0:T(8,128)(2,1)S(1)} collective-permute-done((bf16[128,256]{1,0:T(8,128)(2,1)S(1)}, bf16[128,256]{1,0:T(8,128)(2,1)S(1)}, u32[]{:S(2)}, u32[]{:S(2)}) %collective-permute-start.7) | collective-permute-done | bytes 65568 | tf_op jit(solution)/shard_map/ppermute | solution.py:87
  20.5 1.5 %collective-permute-done.8.refs_2_ = bf16[128,256]{1,0:T(8,128)(2,1)S(1)} collective-permute-done((bf16[128,256]{1,0:T(8,128)(2,1)S(1)}, bf16[128,256]{1,0:T(8,128)(2,1)S(1)}, u32[]{:S(2)}, u32[]{:S(2)}) %collective-permute-start.8) | collective-permute-done | bytes 65568 | tf_op jit(solution)/shard_map/ppermute | solution.py:87
  22.0 0.5 %collective-permute-done.9.refs_3_ = bf16[128,256]{1,0:T(8,128)(2,1)S(1)} collective-permute-done((bf16[128,256]{1,0:T(8,128)(2,1)S(1)}, bf16[128,256]{1,0:T(8,128)(2,1)S(1)}, u32[]{:S(2)}, u32[]{:S(2)}) %collective-permute-start.9) | collective-permute-done | bytes 65568 | tf_op jit(solution)/shard_map/ppermute | solution.py:87
  22.5 0.4 dense.1
  22.9 0.1 collective-permute-start.10
  23.0 1.3 %collective-permute-done.10.came_ref = bf16[256,256]{1,0:T(8,128)(2,1)S(1)} collective-permute-done((bf16[256,256]{1,0:T(8,128)(2,1)S(1)}, bf16[256,256]{1,0:T(8,128)(2,1)S(1)}, u32[]{:S(2)}, u32[]{:S(2)}) %collective-permute-start.10) | collective-permute-done | bytes 131104 | tf_op jit(solution)/shard_map/ppermute | solution.py:87
  24.4 2.5 %collective-permute-start.11 = (bf16[64,256]{1,0:T(8,128)(2,1)S(1)}, bf16[64,256]{1,0:T(8,128)(2,1)S(1)}, u32[]{:S(2)}, u32[]{:S(2)}) collective-permute-start(bf16[64,256]{1,0:T(8,128)(2,1)S(1)} %get-tuple-element.44), channel_id=1, source_target_pairs={{0,24},{1,25},{2,26},{3,27},{4,7},{5,6},{6,5},{7,4},{8,16},{9,17},... | collective-permute-start | bytes 98312 | tf_op jit(solution)/shard_map/ppermute | solution.py:328
  26.9 2.0 %collective-permute-start.13 = (bf16[64,256]{1,0:T(8,128)(2,1)S(1)}, bf16[64,256]{1,0:T(8,128)(2,1)S(1)}, u32[]{:S(2)}, u32[]{:S(2)}) collective-permute-start(bf16[64,256]{1,0:T(8,128)(2,1)S(1)} %get-tuple-element.46), channel_id=1, source_target_pairs={{0,8},{1,9},{2,10},{3,11},{4,5},{5,4},{6,7},{7,6},{8,0},{9,1},{10,... | collective-permute-start | bytes 98312 | tf_op jit(solution)/shard_map/ppermute | solution.py:328
  28.8 1.3 %collective-permute-done.11.refs_0_ = bf16[64,256]{1,0:T(8,128)(2,1)S(1)} collective-permute-done((bf16[64,256]{1,0:T(8,128)(2,1)S(1)}, bf16[64,256]{1,0:T(8,128)(2,1)S(1)}, u32[]{:S(2)}, u32[]{:S(2)}) %collective-permute-start.11) | collective-permute-done | bytes 32800 | tf_op jit(solution)/shard_map/ppermute | solution.py:328
  30.2 1.7 %collective-permute-done.12.refs_1_ = bf16[64,256]{1,0:T(8,128)(2,1)S(1)} collective-permute-done((bf16[64,256]{1,0:T(8,128)(2,1)S(1)}, bf16[64,256]{1,0:T(8,128)(2,1)S(1)}, u32[]{:S(2)}, u32[]{:S(2)}) %collective-permute-start.12) | collective-permute-done | bytes 32800 | tf_op jit(solution)/shard_map/ppermute | solution.py:328
  31.9 0.0 collective-permute-done.13.refs_2_
  31.9 1.7 %collective-permute-start.14 = (bf16[64,256]{1,0:T(8,128)(2,1)S(1)}, bf16[64,256]{1,0:T(8,128)(2,1)S(1)}, u32[]{:S(2)}, u32[]{:S(2)}) collective-permute-start(bf16[64,256]{1,0:T(8,128)(2,1)S(1)} %get-tuple-element.48), channel_id=1, source_target_pairs={{0,24},{4,28},{8,16},{12,20},{16,8},{20,12},{24,0},{28,4},{1,25},{... | collective-permute-start | bytes 98312 | tf_op jit(solution)/shard_map/ppermute | solution.py:87
  33.6 0.7 %collective-permute-start.15 = (bf16[64,256]{1,0:T(8,128)(2,1)S(1)}, bf16[64,256]{1,0:T(8,128)(2,1)S(1)}, u32[]{:S(2)}, u32[]{:S(2)}) collective-permute-start(bf16[64,256]{1,0:T(8,128)(2,1)S(1)} %get-tuple-element.49), channel_id=1, source_target_pairs={{0,16},{4,20},{8,24},{12,28},{16,0},{20,4},{24,8},{28,12},{1,17},{... | collective-permute-start | bytes 98312 | tf_op jit(solution)/shard_map/ppermute | solution.py:87
  34.3 2.0 %collective-permute-start.16 = (bf16[64,256]{1,0:T(8,128)(2,1)S(1)}, bf16[64,256]{1,0:T(8,128)(2,1)S(1)}, u32[]{:S(2)}, u32[]{:S(2)}) collective-permute-start(bf16[64,256]{1,0:T(8,128)(2,1)S(1)} %get-tuple-element.50), channel_id=1, source_target_pairs={{0,8},{4,12},{8,0},{12,4},{16,24},{20,28},{24,16},{28,20},{1,9},{5... | collective-permute-start | bytes 98312 | tf_op jit(solution)/shard_map/ppermute | solution.py:87
  36.4 1.3 %collective-permute-done.14.refs_3_.refs_0_ = bf16[64,256]{1,0:T(8,128)(2,1)S(1)} collective-permute-done((bf16[64,256]{1,0:T(8,128)(2,1)S(1)}, bf16[64,256]{1,0:T(8,128)(2,1)S(1)}, u32[]{:S(2)}, u32[]{:S(2)}) %collective-permute-start.14) | collective-permute-done | bytes 32800 | tf_op jit(solution)/shard_map/ppermute | solution.py:87
  37.7 1.1 %collective-permute-done.15.refs_4_.refs_1_ = bf16[64,256]{1,0:T(8,128)(2,1)S(1)} collective-permute-done((bf16[64,256]{1,0:T(8,128)(2,1)S(1)}, bf16[64,256]{1,0:T(8,128)(2,1)S(1)}, u32[]{:S(2)}, u32[]{:S(2)}) %collective-permute-start.15) | collective-permute-done | bytes 32800 | tf_op jit(solution)/shard_map/ppermute | solution.py:87
  38.8 1.6 %collective-permute-start.19 = (bf16[64,256]{1,0:T(8,128)(2,1)S(1)}, bf16[64,256]{1,0:T(8,128)(2,1)S(1)}, u32[]{:S(2)}, u32[]{:S(2)}) collective-permute-start(bf16[64,256]{1,0:T(8,128)(2,1)S(1)} %add.1.refs_0_), channel_id=1, source_target_pairs={{0,3},{1,2},{2,1},{3,0},{4,7},{5,6},{6,5},{7,4},{8,11},{9,10},{10,... | collective-permute-start | bytes 98312 | tf_op jit(solution)/shard_map/ppermute | solution.py:87
  40.3 1.0 %collective-permute-start.18 = (bf16[64,256]{1,0:T(8,128)(2,1)S(1)}, bf16[64,256]{1,0:T(8,128)(2,1)S(1)}, u32[]{:S(2)}, u32[]{:S(2)}) collective-permute-start(bf16[64,256]{1,0:T(8,128)(2,1)S(1)} %add.1.refs_0_), channel_id=1, source_target_pairs={{0,2},{1,3},{2,0},{3,1},{4,6},{5,7},{6,4},{7,5},{8,10},{9,11},{10,... | collective-permute-start | bytes 98312 | tf_op jit(solution)/shard_map/ppermute | solution.py:87
  41.3 1.0 %collective-permute-start.17 = (bf16[64,256]{1,0:T(8,128)(2,1)S(1)}, bf16[64,256]{1,0:T(8,128)(2,1)S(1)}, u32[]{:S(2)}, u32[]{:S(2)}) collective-permute-start(bf16[64,256]{1,0:T(8,128)(2,1)S(1)} %add.1.refs_0_), channel_id=1, source_target_pairs={{0,1},{1,0},{2,3},{3,2},{4,5},{5,4},{6,7},{7,6},{8,9},{9,8},{10,11... | collective-permute-start | bytes 98312 | tf_op jit(solution)/shard_map/ppermute | solution.py:87
  42.4 1.3 %collective-permute-done.19.refs_3_ = bf16[64,256]{1,0:T(8,128)(2,1)S(1)} collective-permute-done((bf16[64,256]{1,0:T(8,128)(2,1)S(1)}, bf16[64,256]{1,0:T(8,128)(2,1)S(1)}, u32[]{:S(2)}, u32[]{:S(2)}) %collective-permute-start.19) | collective-permute-done | bytes 32800 | tf_op jit(solution)/shard_map/ppermute | solution.py:87
  43.7 0.6 %collective-permute-done.18.refs_2_ = bf16[64,256]{1,0:T(8,128)(2,1)S(1)} collective-permute-done((bf16[64,256]{1,0:T(8,128)(2,1)S(1)}, bf16[64,256]{1,0:T(8,128)(2,1)S(1)}, u32[]{:S(2)}, u32[]{:S(2)}) %collective-permute-start.18) | collective-permute-done | bytes 32800 | tf_op jit(solution)/shard_map/ppermute | solution.py:87
  44.3 1.0 %collective-permute-done.17.refs_1_ = bf16[64,256]{1,0:T(8,128)(2,1)S(1)} collective-permute-done((bf16[64,256]{1,0:T(8,128)(2,1)S(1)}, bf16[64,256]{1,0:T(8,128)(2,1)S(1)}, u32[]{:S(2)}, u32[]{:S(2)}) %collective-permute-start.17) | collective-permute-done | bytes 32800 | tf_op jit(solution)/shard_map/ppermute | solution.py:87
  45.2 0.1 collective-permute-start.20
  45.3 1.3 %collective-permute-done.20.came_ref = bf16[256,256]{1,0:T(8,128)(2,1)S(1)} collective-permute-done((bf16[256,256]{1,0:T(8,128)(2,1)S(1)}, bf16[256,256]{1,0:T(8,128)(2,1)S(1)}, u32[]{:S(2)}, u32[]{:S(2)}) %collective-permute-start.20) | collective-permute-done | bytes 131104 | tf_op jit(solution)/shard_map/ppermute | solution.py:87
  46.6 0.8 %finish.1 = (bf16[256,256]{1,0:T(8,128)(2,1)}, f32[256,256]{1,0:T(8,128)}) custom-call(bf16[256,256]{1,0:T(8,128)(2,1)S(1)} %bitcast.9, bf16[256,256]{1,0:T(8,128)(2,1)S(1)} %bitcast.8, bf16[256,256]{1,0:T(8,128)(2,1)S(1)} %collective-permute-done.20.came_ref), custom_call_target="tpu_custom_call" | custom-call | tf_op jit(solution)/shard_map/finish/pallas_call | solution.py:307
  (15 shorter events, 0.2 us)
Async XLA Ops:
  0.6 8.5 %collective-permute-start = (bf16[128,256]{1,0:T(8,128)(2,1)}, bf16[128,256]{1,0:T(8,128)(2,1)S(1)}, u32[]{:S(2)}, u32[]{:S(2)}) collective-permute-start(bf16[128,256]{1,0:T(8,128)(2,1)} %own_ref.1), channel_id=1, source_target_pairs={{0,8},{4,12},{8,0},{12,4},{16,24},{20,28},{24,16},{28,20},{1,9},{5... | collective-permute-start | bytes 196616 | tf_op jit(solution)/shard_map/ppermute | solution.py:87
  3.7 7.1 %collective-permute-start.5 = (bf16[128,256]{1,0:T(8,128)(2,1)}, bf16[128,256]{1,0:T(8,128)(2,1)S(1)}, u32[]{:S(2)}, u32[]{:S(2)}) collective-permute-start(bf16[128,256]{1,0:T(8,128)(2,1)} %own_ref.1), channel_id=1, source_target_pairs={{0,24},{4,28},{8,16},{12,20},{16,8},{20,12},{24,0},{28,4},{1,25},{... | collective-permute-start | bytes 196616 | tf_op jit(solution)/shard_map/ppermute | solution.py:87
  6.2 6.7 %collective-permute-start.3 = (bf16[128,256]{1,0:T(8,128)(2,1)}, bf16[128,256]{1,0:T(8,128)(2,1)S(1)}, u32[]{:S(2)}, u32[]{:S(2)}) collective-permute-start(bf16[128,256]{1,0:T(8,128)(2,1)} %own_ref.1), channel_id=1, source_target_pairs={{0,16},{4,20},{8,24},{12,28},{16,0},{20,4},{24,8},{28,12},{1,17},{... | collective-permute-start | bytes 196616 | tf_op jit(solution)/shard_map/ppermute | solution.py:87
  6.3 7.1 %collective-permute-start.1 = (bf16[128,256]{1,0:T(8,128)(2,1)}, bf16[128,256]{1,0:T(8,128)(2,1)S(1)}, u32[]{:S(2)}, u32[]{:S(2)}) collective-permute-start(bf16[128,256]{1,0:T(8,128)(2,1)} %own_ref.1), channel_id=1, source_target_pairs={{0,4},{4,0},{8,12},{12,8},{16,20},{20,16},{24,28},{28,24},{1,5},{5... | collective-permute-start | bytes 196616 | tf_op jit(solution)/shard_map/ppermute | solution.py:87
  6.3 0.7 %copy-start.5 = (s32[128,1]{0,1:T(1,128)S(1)}, s32[128,1]{0,1:T(1,128)}, u32[]{:S(2)}) copy-start(s32[128,1]{0,1:T(1,128)} %param.11) | copy-start | bytes 1540
  7.0 1.0 %copy-start = (bf16[4,1,4,128,128]{4,3,2,1,0:T(8,128)(2,1)S(1)}, bf16[4,1,4,128,128]{4,3,2,1,0:T(8,128)(2,1)}, u32[]{:S(2)}) copy-start(bf16[4,1,4,128,128]{4,3,2,1,0:T(8,128)(2,1)} %param.7) | copy-start | bytes 1572868
  8.0 0.8 %copy-start.2 = (bf16[128,256]{1,0:T(8,128)(2,1)S(1)}, bf16[128,256]{1,0:T(8,128)(2,1)}, u32[]{:S(2)}) copy-start(bf16[128,256]{1,0:T(8,128)(2,1)} %own_ref.1) | copy-start | bytes 196612
  9.1 5.2 %copy-start.4 = (s32[4,1,4]{2,1,0:T(1,128)S(1)}, s32[4,1,4]{2,1,0:T(1,128)}, u32[]{:S(2)}) copy-start(s32[4,1,4]{2,1,0:T(1,128)} %param.8) | copy-start | bytes 196
  10.8 2.6 %collective-permute-start.6 = (bf16[128,256]{1,0:T(8,128)(2,1)S(1)}, bf16[128,256]{1,0:T(8,128)(2,1)S(1)}, u32[]{:S(2)}, u32[]{:S(2)}) collective-permute-start(bf16[128,256]{1,0:T(8,128)(2,1)S(1)} %collective-permute-done.5.refs_6_), channel_id=1, source_target_pairs={{0,4},{4,0},{8,12},{12,8},{16,20},{20,16},{24,28},{28,24},{1,5},{5... | collective-permute-start | bytes 196616 | tf_op jit(solution)/shard_map/ppermute | solution.py:87
  12.9 1.3 %collective-permute-start.4 = (bf16[128,256]{1,0:T(8,128)(2,1)S(1)}, bf16[128,256]{1,0:T(8,128)(2,1)S(1)}, u32[]{:S(2)}, u32[]{:S(2)}) collective-permute-start(bf16[128,256]{1,0:T(8,128)(2,1)S(1)} %collective-permute-done.3.refs_4_), channel_id=1, source_target_pairs={{0,4},{4,0},{8,12},{12,8},{16,20},{20,16},{24,28},{28,24},{1,5},{5... | collective-permute-start | bytes 196616 | tf_op jit(solution)/shard_map/ppermute | solution.py:87
  12.9 1.4 %collective-permute-start.2 = (bf16[128,256]{1,0:T(8,128)(2,1)S(1)}, bf16[128,256]{1,0:T(8,128)(2,1)S(1)}, u32[]{:S(2)}, u32[]{:S(2)}) collective-permute-start(bf16[128,256]{1,0:T(8,128)(2,1)S(1)} %collective-permute-done.refs_2_), channel_id=1, source_target_pairs={{0,4},{4,0},{8,12},{12,8},{16,20},{20,16},{24,28},{28,24},{1,5},{5... | collective-permute-start | bytes 196616 | tf_op jit(solution)/shard_map/ppermute | solution.py:87
  14.3 8.2 %copy-start.1 = (bf16[256,256]{1,0:T(8,128)(2,1)S(1)}, bf16[256,256]{1,0:T(8,128)(2,1)}, u32[]{:S(2)}) copy-start(bf16[256,256]{1,0:T(8,128)(2,1)} %weight_ref.1) | copy-start | bytes 393220
  14.3 8.2 %copy-start.3 = (bf16[128,256]{1,0:T(8,128)(2,1)S(1)}, bf16[128,256]{1,0:T(8,128)(2,1)}, u32[]{:S(2)}) copy-start(bf16[128,256]{1,0:T(8,128)(2,1)} %cot_ref.1) | copy-start | bytes 196612
  15.2 5.3 %collective-permute-start.7 = (bf16[128,256]{1,0:T(8,128)(2,1)S(1)}, bf16[128,256]{1,0:T(8,128)(2,1)S(1)}, u32[]{:S(2)}, u32[]{:S(2)}) collective-permute-start(bf16[128,256]{1,0:T(8,128)(2,1)S(1)} %get-tuple-element.38), channel_id=1, source_target_pairs={{0,3},{1,2},{2,1},{3,0},{4,7},{5,6},{6,5},{7,4},{8,11},{9,10},{10,... | collective-permute-start | bytes 196616 | tf_op jit(solution)/shard_map/ppermute | solution.py:87
  17.7 4.3 %collective-permute-start.8 = (bf16[128,256]{1,0:T(8,128)(2,1)S(1)}, bf16[128,256]{1,0:T(8,128)(2,1)S(1)}, u32[]{:S(2)}, u32[]{:S(2)}) collective-permute-start(bf16[128,256]{1,0:T(8,128)(2,1)S(1)} %get-tuple-element.39), channel_id=1, source_target_pairs={{0,2},{1,3},{2,0},{3,1},{4,6},{5,7},{6,4},{7,5},{8,10},{9,11},{10,... | collective-permute-start | bytes 196616 | tf_op jit(solution)/shard_map/ppermute | solution.py:87
  18.2 4.3 %collective-permute-start.9 = (bf16[128,256]{1,0:T(8,128)(2,1)S(1)}, bf16[128,256]{1,0:T(8,128)(2,1)S(1)}, u32[]{:S(2)}, u32[]{:S(2)}) collective-permute-start(bf16[128,256]{1,0:T(8,128)(2,1)S(1)} %get-tuple-element.40), channel_id=1, source_target_pairs={{0,1},{1,0},{2,3},{3,2},{4,5},{5,4},{6,7},{7,6},{8,9},{9,8},{10,11... | collective-permute-start | bytes 196616 | tf_op jit(solution)/shard_map/ppermute | solution.py:87
  22.9 1.4 %collective-permute-start.10 = (bf16[256,256]{1,0:T(8,128)(2,1)S(1)}, bf16[256,256]{1,0:T(8,128)(2,1)S(1)}, u32[]{:S(2)}, u32[]{:S(2)}) collective-permute-start(bf16[256,256]{1,0:T(8,128)(2,1)S(1)} %get-tuple-element.42), channel_id=1, source_target_pairs={{0,4},{4,0},{8,12},{12,8},{16,20},{20,16},{24,28},{28,24},{1,5},{5... | collective-permute-start | bytes 393224 | tf_op jit(solution)/shard_map/ppermute | solution.py:87
  24.4 5.8 %collective-permute-start.11 = (bf16[64,256]{1,0:T(8,128)(2,1)S(1)}, bf16[64,256]{1,0:T(8,128)(2,1)S(1)}, u32[]{:S(2)}, u32[]{:S(2)}) collective-permute-start(bf16[64,256]{1,0:T(8,128)(2,1)S(1)} %get-tuple-element.44), channel_id=1, source_target_pairs={{0,24},{1,25},{2,26},{3,27},{4,7},{5,6},{6,5},{7,4},{8,16},{9,17},... | collective-permute-start | bytes 98312 | tf_op jit(solution)/shard_map/ppermute | solution.py:328
  26.9 5.0 %collective-permute-start.12 = (bf16[64,256]{1,0:T(8,128)(2,1)S(1)}, bf16[64,256]{1,0:T(8,128)(2,1)S(1)}, u32[]{:S(2)}, u32[]{:S(2)}) collective-permute-start(bf16[64,256]{1,0:T(8,128)(2,1)S(1)} %get-tuple-element.45), channel_id=1, source_target_pairs={{0,16},{1,17},{2,18},{3,19},{4,6},{5,7},{6,4},{7,5},{8,24},{9,25},... | collective-permute-start | bytes 98312 | tf_op jit(solution)/shard_map/ppermute | solution.py:328
  26.9 5.0 %collective-permute-start.13 = (bf16[64,256]{1,0:T(8,128)(2,1)S(1)}, bf16[64,256]{1,0:T(8,128)(2,1)S(1)}, u32[]{:S(2)}, u32[]{:S(2)}) collective-permute-start(bf16[64,256]{1,0:T(8,128)(2,1)S(1)} %get-tuple-element.46), channel_id=1, source_target_pairs={{0,8},{1,9},{2,10},{3,11},{4,5},{5,4},{6,7},{7,6},{8,0},{9,1},{10,... | collective-permute-start | bytes 98312 | tf_op jit(solution)/shard_map/ppermute | solution.py:328
  31.9 5.8 %collective-permute-start.14 = (bf16[64,256]{1,0:T(8,128)(2,1)S(1)}, bf16[64,256]{1,0:T(8,128)(2,1)S(1)}, u32[]{:S(2)}, u32[]{:S(2)}) collective-permute-start(bf16[64,256]{1,0:T(8,128)(2,1)S(1)} %get-tuple-element.48), channel_id=1, source_target_pairs={{0,24},{4,28},{8,16},{12,20},{16,8},{20,12},{24,0},{28,4},{1,25},{... | collective-permute-start | bytes 98312 | tf_op jit(solution)/shard_map/ppermute | solution.py:87
  33.6 5.2 %collective-permute-start.15 = (bf16[64,256]{1,0:T(8,128)(2,1)S(1)}, bf16[64,256]{1,0:T(8,128)(2,1)S(1)}, u32[]{:S(2)}, u32[]{:S(2)}) collective-permute-start(bf16[64,256]{1,0:T(8,128)(2,1)S(1)} %get-tuple-element.49), channel_id=1, source_target_pairs={{0,16},{4,20},{8,24},{12,28},{16,0},{20,4},{24,8},{28,12},{1,17},{... | collective-permute-start | bytes 98312 | tf_op jit(solution)/shard_map/ppermute | solution.py:87
  34.3 4.4 %collective-permute-start.16 = (bf16[64,256]{1,0:T(8,128)(2,1)S(1)}, bf16[64,256]{1,0:T(8,128)(2,1)S(1)}, u32[]{:S(2)}, u32[]{:S(2)}) collective-permute-start(bf16[64,256]{1,0:T(8,128)(2,1)S(1)} %get-tuple-element.50), channel_id=1, source_target_pairs={{0,8},{4,12},{8,0},{12,4},{16,24},{20,28},{24,16},{28,20},{1,9},{5... | collective-permute-start | bytes 98312 | tf_op jit(solution)/shard_map/ppermute | solution.py:87
  38.8 4.9 %collective-permute-start.19 = (bf16[64,256]{1,0:T(8,128)(2,1)S(1)}, bf16[64,256]{1,0:T(8,128)(2,1)S(1)}, u32[]{:S(2)}, u32[]{:S(2)}) collective-permute-start(bf16[64,256]{1,0:T(8,128)(2,1)S(1)} %add.1.refs_0_), channel_id=1, source_target_pairs={{0,3},{1,2},{2,1},{3,0},{4,7},{5,6},{6,5},{7,4},{8,11},{9,10},{10,... | collective-permute-start | bytes 98312 | tf_op jit(solution)/shard_map/ppermute | solution.py:87
  40.3 3.9 %collective-permute-start.18 = (bf16[64,256]{1,0:T(8,128)(2,1)S(1)}, bf16[64,256]{1,0:T(8,128)(2,1)S(1)}, u32[]{:S(2)}, u32[]{:S(2)}) collective-permute-start(bf16[64,256]{1,0:T(8,128)(2,1)S(1)} %add.1.refs_0_), channel_id=1, source_target_pairs={{0,2},{1,3},{2,0},{3,1},{4,6},{5,7},{6,4},{7,5},{8,10},{9,11},{10,... | collective-permute-start | bytes 98312 | tf_op jit(solution)/shard_map/ppermute | solution.py:87
  41.3 3.9 %collective-permute-start.17 = (bf16[64,256]{1,0:T(8,128)(2,1)S(1)}, bf16[64,256]{1,0:T(8,128)(2,1)S(1)}, u32[]{:S(2)}, u32[]{:S(2)}) collective-permute-start(bf16[64,256]{1,0:T(8,128)(2,1)S(1)} %add.1.refs_0_), channel_id=1, source_target_pairs={{0,1},{1,0},{2,3},{3,2},{4,5},{5,4},{6,7},{7,6},{8,9},{9,8},{10,11... | collective-permute-start | bytes 98312 | tf_op jit(solution)/shard_map/ppermute | solution.py:87
  45.2 1.4 %collective-permute-start.20 = (bf16[256,256]{1,0:T(8,128)(2,1)S(1)}, bf16[256,256]{1,0:T(8,128)(2,1)S(1)}, u32[]{:S(2)}, u32[]{:S(2)}) collective-permute-start(bf16[256,256]{1,0:T(8,128)(2,1)S(1)} %get-tuple-element.55), channel_id=1, source_target_pairs={{0,4},{4,0},{8,12},{12,8},{16,20},{20,16},{24,28},{28,24},{1,5},{5... | collective-permute-start | bytes 393224 | tf_op jit(solution)/shard_map/ppermute | solution.py:87

commit v7 on v6

--- a/solution.py
+++ b/solution.py
@@ -317,9 +317,9 @@
     )(whole, mine, came)
 
 
-def swap_by_core(value, j):
+def swap_by_core(value, along, side):
     n_section, n_rep = lax.axis_size("section"), lax.axis_size("rep")
-    along, side = 2 * j % n_section, j % n_rep
+    along, side = 2 * along % n_section, side % n_rep
     pairs = [
         (s * n_rep + r, s * n_rep + (r ^ side) if s & 1 else (s ^ along) * n_rep + r)
         for s in range(n_section)
@@ -335,7 +335,7 @@
     for j in range(2, n, 2):
         blocks[j] = swap(features, axis, j)
     blocks[1] = swap(features, axis, 1)
-    blocks[2], ready = lax.optimization_barrier((blocks[2], ready))
+    blocks[2::2], ready = lax.optimization_barrier((blocks[2::2], ready))
     for j in range(2, n, 2):
         blocks[j + 1] = swap(blocks[j], axis, 1)
     return blocks, ready
@@ -356,12 +356,12 @@
     came = swap(sent, "section", 1)
     chips = n_section // 2
     own, *first = split(packed, term, came, n_rep, chips)
-    first = [swap_by_core(value, j) for value, j in zip(first, across(len(first) + 1))]
+    first = [swap_by_core(value, j, j) for value, j in zip(first, across(len(first) + 1))]
     chunk, *later = second(packed, came, own, first[1 - n_rep :], chips)
     later = [swap(value, "section", 2 * j) for value, j in zip(later, across(chips))]
     chunk = add(chunk, later)
     mine, other = unpack(packed, came, first[1 - chips :], later, slots)
-    chunks = [chunk] + [swap(chunk, "rep", j) for j in range(1, n_rep)]
+    chunks = [chunk] + [swap_by_core(chunk, 0, j) for j in range(1, n_rep)]
     whole, sent = place(chunks, other.reshape(n_section * slots, width))
     came = swap(sent, "section", 1)
     relaid, weight_grad = finish(

time: 47.6 us -> 47.7 us (level)
  waiting for transfers between devices: 19.3 us -> 15.3 us
  starting transfers between devices: 22.4 us -> 26.3 us
    ppermute x18 -> x15, waiting for transfers between devices: 16.3 us -> 12.2 us  [swap(): lax.ppermute(value, axis, [(i, i ^ j) for i in range(lax.axis_size(axis))])]
    ppermute x3 -> x6, starting transfers between devices: 4.45 us -> 6.44 us  [swap_by_core(): return lax.ppermute(value, ('section', 'rep'), pairs)]
    ppermute x18 -> x15, starting transfers between devices: 17.9 us -> 19.9 us  [swap(): lax.ppermute(value, axis, [(i, i ^ j) for i in range(lax.axis_size(axis))])]
    ppermute x3 -> x6, waiting for transfers between devices: 3.04 us -> 3.16 us  [swap_by_core(): return lax.ppermute(value, ('section', 'rep'), pairs)]
  transfers between devices with their start and end apart: 21 -> 21, of which waited for: 16 -> 13; matrix products, arithmetic and copies ran while one was open for 0% -> 0% of each run, Pallas kernels for 1% -> 1%
where the time goes in v7:
time: 47.7 us; the launch traced here: 47.5 us
  starting transfers between devices  26.3 us (55%)
  waiting for transfers between devices  15.3 us (32%)
  local copies, waits for them, and re-layouts  2.55 us (5%)
  Pallas kernels  2.49 us (5%)
  between operations  0.77 us (2%)
    ppermute x15, starting transfers between devices, swap(): lax.ppermute(value, axis, [(i, i ^ j) for i in range(lax.axis_size(axis))])  19.9 us
    ppermute x15, waiting for transfers between devices, swap(): lax.ppermute(value, axis, [(i, i ^ j) for i in range(lax.axis_size(axis))])  12.2 us
    ppermute x6, starting transfers between devices, swap_by_core(): return lax.ppermute(value, ('section', 'rep'), pairs)  6.44 us
    ppermute x6, waiting for transfers between devices, swap_by_core(): return lax.ppermute(value, ('section', 'rep'), pairs)  3.16 us
    unnamed x12, local copies, waits for them, and re-layouts  2.55 us
  transfers between devices with their start and end apart: 21, of which 13 were waited for; matrix products, arithmetic and copies ran while one was open for 0% of the time, Pallas kernels for 1%

profile of v7, /device:TPU:0, one launch (start us, length us, event | category | flops | bytes accessed | tf_op | source)
XLA Modules:
  0.0 47.5 jit_solution(3837679163499053632)
XLA Ops:
  0.6 5.1 %collective-permute-start.2 = (bf16[128,256]{1,0:T(8,128)(2,1)}, bf16[128,256]{1,0:T(8,128)(2,1)S(1)}, u32[]{:S(2)}, u32[]{:S(2)}) collective-permute-start(bf16[128,256]{1,0:T(8,128)(2,1)} %own_ref.1), channel_id=1, source_target_pairs={{0,24},{4,28},{8,16},{12,20},{16,8},{20,12},{24,0},{28,4},{1,25},{... | collective-permute-start | bytes 196616 | tf_op jit(solution)/shard_map/ppermute | solution.py:87
  5.7 0.0 collective-permute-start.1
  5.7 0.6 %collective-permute-start = (bf16[128,256]{1,0:T(8,128)(2,1)}, bf16[128,256]{1,0:T(8,128)(2,1)S(1)}, u32[]{:S(2)}, u32[]{:S(2)}) collective-permute-start(bf16[128,256]{1,0:T(8,128)(2,1)} %own_ref.1), channel_id=1, source_target_pairs={{0,8},{4,12},{8,0},{12,4},{16,24},{20,28},{24,16},{28,20},{1,9},{5... | collective-permute-start | bytes 196616 | tf_op jit(solution)/shard_map/ppermute | solution.py:87
  6.4 0.0 collective-permute-start.3
  6.4 0.7 %copy-done.5 = s32[128,1]{0,1:T(1,128)S(1)} copy-done((s32[128,1]{0,1:T(1,128)S(1)}, s32[128,1]{0,1:T(1,128)}, u32[]{:S(2)}) %copy-start.5) | copy-done | bytes 536
  7.0 1.0 %copy-done = bf16[4,1,4,128,128]{4,3,2,1,0:T(8,128)(2,1)S(1)} copy-done((bf16[4,1,4,128,128]{4,3,2,1,0:T(8,128)(2,1)S(1)}, bf16[4,1,4,128,128]{4,3,2,1,0:T(8,128)(2,1)}, u32[]{:S(2)}) %copy-start) | copy-done | bytes 524312
  8.1 0.8 %copy-done.2 = bf16[128,256]{1,0:T(8,128)(2,1)S(1)} copy-done((bf16[128,256]{1,0:T(8,128)(2,1)S(1)}, bf16[128,256]{1,0:T(8,128)(2,1)}, u32[]{:S(2)}) %copy-start.2) | copy-done | bytes 65560
  8.9 0.2 prepare.1
  9.2 0.0 collective-permute-done.2.refs_6_
  9.2 2.4 %collective-permute-done.1.refs_4_ = bf16[128,256]{1,0:T(8,128)(2,1)S(1)} collective-permute-done((bf16[128,256]{1,0:T(8,128)(2,1)}, bf16[128,256]{1,0:T(8,128)(2,1)S(1)}, u32[]{:S(2)}, u32[]{:S(2)}) %collective-permute-start.1) | collective-permute-done | bytes 65568 | tf_op jit(solution)/shard_map/ppermute | solution.py:87
  11.6 0.0 collective-permute-done.refs_2_
  11.6 0.0 collective-permute-start.4
  11.6 0.5 %collective-permute-start.5 = (bf16[128,256]{1,0:T(8,128)(2,1)S(1)}, bf16[128,256]{1,0:T(8,128)(2,1)S(1)}, u32[]{:S(2)}, u32[]{:S(2)}) collective-permute-start(bf16[128,256]{1,0:T(8,128)(2,1)S(1)} %collective-permute-done.1.refs_4_), channel_id=1, source_target_pairs={{0,4},{4,0},{8,12},{12,8},{16,20},{20,16},{24,28},{28,24},{1,5},{5... | collective-permute-start | bytes 196616 | tf_op jit(solution)/shard_map/ppermute | solution.py:87
  12.1 0.1 collective-permute-start.6
  12.1 0.0 collective-permute-done.3.refs_1_
  12.1 0.7 %collective-permute-done.4.refs_3_ = bf16[128,256]{1,0:T(8,128)(2,1)S(1)} collective-permute-done((bf16[128,256]{1,0:T(8,128)(2,1)S(1)}, bf16[128,256]{1,0:T(8,128)(2,1)S(1)}, u32[]{:S(2)}, u32[]{:S(2)}) %collective-permute-start.4) | collective-permute-done | bytes 65568 | tf_op jit(solution)/shard_map/ppermute | solution.py:87
  12.8 0.2 collective-permute-done.5.refs_5_
  13.0 0.4 collective-permute-done.6.refs_7_
  13.3 0.9 %partials.1 = (bf16[128,256]{1,0:T(8,128)(2,1)S(1)}, bf16[128,256]{1,0:T(8,128)(2,1)S(1)}, bf16[128,256]{1,0:T(8,128)(2,1)S(1)}, bf16[128,256]{1,0:T(8,128)(2,1)S(1)}) custom-call(s32[4,4]{1,0:T(4,128)S(1)} %bitcast.11, bf16[4,128,512]{2,1,0:T(8,128)(2,1)S(1)} %get-tuple-element.36.wide_ref, bf16[128,256]{1,0:T(8,128)(2,1)S(1)} %get-tuple-element.37.refs_0_, ...), custom_call_target="tpu_custom_call" | custom-call | tf_op jit(solution)/shard_map/partials/pallas_call | solution.py:75
  14.3 2.5 %collective-permute-start.7 = (bf16[128,256]{1,0:T(8,128)(2,1)S(1)}, bf16[128,256]{1,0:T(8,128)(2,1)S(1)}, u32[]{:S(2)}, u32[]{:S(2)}) collective-permute-start(bf16[128,256]{1,0:T(8,128)(2,1)S(1)} %get-tuple-element.42), channel_id=1, source_target_pairs={{0,3},{1,2},{2,1},{3,0},{4,7},{5,6},{6,5},{7,4},{8,11},{9,10},{10,... | collective-permute-start | bytes 196616 | tf_op jit(solution)/shard_map/ppermute | solution.py:87
  16.8 0.5 %collective-permute-start.8 = (bf16[128,256]{1,0:T(8,128)(2,1)S(1)}, bf16[128,256]{1,0:T(8,128)(2,1)S(1)}, u32[]{:S(2)}, u32[]{:S(2)}) collective-permute-start(bf16[128,256]{1,0:T(8,128)(2,1)S(1)} %get-tuple-element.43), channel_id=1, source_target_pairs={{0,2},{1,3},{2,0},{3,1},{4,6},{5,7},{6,4},{7,5},{8,10},{9,11},{10,... | collective-permute-start | bytes 196616 | tf_op jit(solution)/shard_map/ppermute | solution.py:87
  17.3 0.5 %collective-permute-start.9 = (bf16[128,256]{1,0:T(8,128)(2,1)S(1)}, bf16[128,256]{1,0:T(8,128)(2,1)S(1)}, u32[]{:S(2)}, u32[]{:S(2)}) collective-permute-start(bf16[128,256]{1,0:T(8,128)(2,1)S(1)} %get-tuple-element.44), channel_id=1, source_target_pairs={{0,1},{1,0},{2,3},{3,2},{4,5},{5,4},{6,7},{7,6},{8,9},{9,8},{10,11... | collective-permute-start | bytes 196616 | tf_op jit(solution)/shard_map/ppermute | solution.py:87
  17.8 1.7 %collective-permute-done.7.refs_1_ = bf16[128,256]{1,0:T(8,128)(2,1)S(1)} collective-permute-done((bf16[128,256]{1,0:T(8,128)(2,1)S(1)}, bf16[128,256]{1,0:T(8,128)(2,1)S(1)}, u32[]{:S(2)}, u32[]{:S(2)}) %collective-permute-start.7) | collective-permute-done | bytes 65568 | tf_op jit(solution)/shard_map/ppermute | solution.py:87
  19.5 1.5 %collective-permute-done.8.refs_2_ = bf16[128,256]{1,0:T(8,128)(2,1)S(1)} collective-permute-done((bf16[128,256]{1,0:T(8,128)(2,1)S(1)}, bf16[128,256]{1,0:T(8,128)(2,1)S(1)}, u32[]{:S(2)}, u32[]{:S(2)}) %collective-permute-start.8) | collective-permute-done | bytes 65568 | tf_op jit(solution)/shard_map/ppermute | solution.py:87
  21.0 0.5 %collective-permute-done.9.refs_3_ = bf16[128,256]{1,0:T(8,128)(2,1)S(1)} collective-permute-done((bf16[128,256]{1,0:T(8,128)(2,1)S(1)}, bf16[128,256]{1,0:T(8,128)(2,1)S(1)}, u32[]{:S(2)}, u32[]{:S(2)}) %collective-permute-start.9) | collective-permute-done | bytes 65568 | tf_op jit(solution)/shard_map/ppermute | solution.py:87
  21.5 0.4 dense.1
  22.0 0.1 collective-permute-start.10
  22.1 1.3 %collective-permute-done.10.came_ref = bf16[256,256]{1,0:T(8,128)(2,1)S(1)} collective-permute-done((bf16[256,256]{1,0:T(8,128)(2,1)S(1)}, bf16[256,256]{1,0:T(8,128)(2,1)S(1)}, u32[]{:S(2)}, u32[]{:S(2)}) %collective-permute-start.10) | collective-permute-done | bytes 131104 | tf_op jit(solution)/shard_map/ppermute | solution.py:87
  23.4 2.8 %collective-permute-start.11 = (bf16[64,256]{1,0:T(8,128)(2,1)S(1)}, bf16[64,256]{1,0:T(8,128)(2,1)S(1)}, u32[]{:S(2)}, u32[]{:S(2)}) collective-permute-start(bf16[64,256]{1,0:T(8,128)(2,1)S(1)} %get-tuple-element.48), channel_id=1, source_target_pairs={{0,24},{1,25},{2,26},{3,27},{4,7},{5,6},{6,5},{7,4},{8,16},{9,17},... | collective-permute-start | bytes 98312 | tf_op jit(solution)/shard_map/ppermute | solution.py:328
  26.2 0.0 collective-permute-start.12
  26.2 1.7 %collective-permute-start.13 = (bf16[64,256]{1,0:T(8,128)(2,1)S(1)}, bf16[64,256]{1,0:T(8,128)(2,1)S(1)}, u32[]{:S(2)}, u32[]{:S(2)}) collective-permute-start(bf16[64,256]{1,0:T(8,128)(2,1)S(1)} %get-tuple-element.50), channel_id=1, source_target_pairs={{0,8},{1,9},{2,10},{3,11},{4,5},{5,4},{6,7},{7,6},{8,0},{9,1},{10,... | collective-permute-start | bytes 98312 | tf_op jit(solution)/shard_map/ppermute | solution.py:328
  27.9 1.3 %collective-permute-done.11.refs_0_ = bf16[64,256]{1,0:T(8,128)(2,1)S(1)} collective-permute-done((bf16[64,256]{1,0:T(8,128)(2,1)S(1)}, bf16[64,256]{1,0:T(8,128)(2,1)S(1)}, u32[]{:S(2)}, u32[]{:S(2)}) %collective-permute-start.11) | collective-permute-done | bytes 32800 | tf_op jit(solution)/shard_map/ppermute | solution.py:328
  29.2 1.8 %collective-permute-done.12.refs_1_ = bf16[64,256]{1,0:T(8,128)(2,1)S(1)} collective-permute-done((bf16[64,256]{1,0:T(8,128)(2,1)S(1)}, bf16[64,256]{1,0:T(8,128)(2,1)S(1)}, u32[]{:S(2)}, u32[]{:S(2)}) %collective-permute-start.12) | collective-permute-done | bytes 32800 | tf_op jit(solution)/shard_map/ppermute | solution.py:328
  31.0 0.0 collective-permute-done.13.refs_2_
  31.1 1.8 %collective-permute-start.14 = (bf16[64,256]{1,0:T(8,128)(2,1)S(1)}, bf16[64,256]{1,0:T(8,128)(2,1)S(1)}, u32[]{:S(2)}, u32[]{:S(2)}) collective-permute-start(bf16[64,256]{1,0:T(8,128)(2,1)S(1)} %get-tuple-element.52), channel_id=1, source_target_pairs={{0,24},{4,28},{8,16},{12,20},{16,8},{20,12},{24,0},{28,4},{1,25},{... | collective-permute-start | bytes 98312 | tf_op jit(solution)/shard_map/ppermute | solution.py:87
  32.9 0.4 collective-permute-start.15
  33.4 2.2 %collective-permute-start.16 = (bf16[64,256]{1,0:T(8,128)(2,1)S(1)}, bf16[64,256]{1,0:T(8,128)(2,1)S(1)}, u32[]{:S(2)}, u32[]{:S(2)}) collective-permute-start(bf16[64,256]{1,0:T(8,128)(2,1)S(1)} %get-tuple-element.54), channel_id=1, source_target_pairs={{0,8},{4,12},{8,0},{12,4},{16,24},{20,28},{24,16},{28,20},{1,9},{5... | collective-permute-start | bytes 98312 | tf_op jit(solution)/shard_map/ppermute | solution.py:87
  35.5 1.3 %collective-permute-done.14.refs_3_.refs_0_ = bf16[64,256]{1,0:T(8,128)(2,1)S(1)} collective-permute-done((bf16[64,256]{1,0:T(8,128)(2,1)S(1)}, bf16[64,256]{1,0:T(8,128)(2,1)S(1)}, u32[]{:S(2)}, u32[]{:S(2)}) %collective-permute-start.14) | collective-permute-done | bytes 32800 | tf_op jit(solution)/shard_map/ppermute | solution.py:87
  36.9 1.2 %collective-permute-done.15.refs_4_.refs_1_ = bf16[64,256]{1,0:T(8,128)(2,1)S(1)} collective-permute-done((bf16[64,256]{1,0:T(8,128)(2,1)S(1)}, bf16[64,256]{1,0:T(8,128)(2,1)S(1)}, u32[]{:S(2)}, u32[]{:S(2)}) %collective-permute-start.15) | collective-permute-done | bytes 32800 | tf_op jit(solution)/shard_map/ppermute | solution.py:87
  38.1 0.0 collective-permute-done.16.refs_5_.refs_2_
  38.1 0.7 %collective-permute-start.19 = (bf16[64,256]{1,0:T(8,128)(2,1)S(1)}, bf16[64,256]{1,0:T(8,128)(2,1)S(1)}, u32[]{:S(2)}, u32[]{:S(2)}) collective-permute-start(bf16[64,256]{1,0:T(8,128)(2,1)S(1)} %add.1.refs_0_), channel_id=1, source_target_pairs={{0,0},{1,1},{2,2},{3,3},{4,7},{5,6},{6,5},{7,4},{8,8},{9,9},{10,10... | collective-permute-start | bytes 98312 | tf_op jit(solution)/shard_map/ppermute | solution.py:328
  38.8 0.7 %collective-permute-start.18 = (bf16[64,256]{1,0:T(8,128)(2,1)S(1)}, bf16[64,256]{1,0:T(8,128)(2,1)S(1)}, u32[]{:S(2)}, u32[]{:S(2)}) collective-permute-start(bf16[64,256]{1,0:T(8,128)(2,1)S(1)} %add.1.refs_0_), channel_id=1, source_target_pairs={{0,0},{1,1},{2,2},{3,3},{4,6},{5,7},{6,4},{7,5},{8,8},{9,9},{10,10... | collective-permute-start | bytes 98312 | tf_op jit(solution)/shard_map/ppermute | solution.py:328
  39.5 0.7 %collective-permute-start.17 = (bf16[64,256]{1,0:T(8,128)(2,1)S(1)}, bf16[64,256]{1,0:T(8,128)(2,1)S(1)}, u32[]{:S(2)}, u32[]{:S(2)}) collective-permute-start(bf16[64,256]{1,0:T(8,128)(2,1)S(1)} %add.1.refs_0_), channel_id=1, source_target_pairs={{0,0},{1,1},{2,2},{3,3},{4,5},{5,4},{6,7},{7,6},{8,8},{9,9},{10,10... | collective-permute-start | bytes 98312 | tf_op jit(solution)/shard_map/ppermute | solution.py:328
  40.2 0.0 collective-permute-done.18.refs_2_
  40.2 0.0 collective-permute-done.17.refs_1_
  40.2 5.5 %collective-permute-start.20 = (bf16[256,256]{1,0:T(8,128)(2,1)S(1)}, bf16[256,256]{1,0:T(8,128)(2,1)S(1)}, u32[]{:S(2)}, u32[]{:S(2)}) collective-permute-start(bf16[256,256]{1,0:T(8,128)(2,1)S(1)} %get-tuple-element.59), channel_id=1, source_target_pairs={{0,4},{4,0},{8,12},{12,8},{16,20},{20,16},{24,28},{28,24},{1,5},{5... | collective-permute-start | bytes 393224 | tf_op jit(solution)/shard_map/ppermute | solution.py:87
  45.7 1.0 %collective-permute-done.20.came_ref = bf16[256,256]{1,0:T(8,128)(2,1)S(1)} collective-permute-done((bf16[256,256]{1,0:T(8,128)(2,1)S(1)}, bf16[256,256]{1,0:T(8,128)(2,1)S(1)}, u32[]{:S(2)}, u32[]{:S(2)}) %collective-permute-start.20) | collective-permute-done | bytes 131104 | tf_op jit(solution)/shard_map/ppermute | solution.py:87
  46.7 0.8 %finish.1 = (bf16[256,256]{1,0:T(8,128)(2,1)}, f32[256,256]{1,0:T(8,128)}) custom-call(bf16[256,256]{1,0:T(8,128)(2,1)S(1)} %bitcast.9, bf16[256,256]{1,0:T(8,128)(2,1)S(1)} %bitcast.8, bf16[256,256]{1,0:T(8,128)(2,1)S(1)} %collective-permute-done.20.came_ref), custom_call_target="tpu_custom_call" | custom-call | tf_op jit(solution)/shard_map/finish/pallas_call | solution.py:307
  (15 shorter events, 0.2 us)
Async XLA Ops:
  0.6 8.5 %collective-permute-start.2 = (bf16[128,256]{1,0:T(8,128)(2,1)}, bf16[128,256]{1,0:T(8,128)(2,1)S(1)}, u32[]{:S(2)}, u32[]{:S(2)}) collective-permute-start(bf16[128,256]{1,0:T(8,128)(2,1)} %own_ref.1), channel_id=1, source_target_pairs={{0,24},{4,28},{8,16},{12,20},{16,8},{20,12},{24,0},{28,4},{1,25},{... | collective-permute-start | bytes 196616 | tf_op jit(solution)/shard_map/ppermute | solution.py:87
  5.7 5.8 %collective-permute-start.1 = (bf16[128,256]{1,0:T(8,128)(2,1)}, bf16[128,256]{1,0:T(8,128)(2,1)S(1)}, u32[]{:S(2)}, u32[]{:S(2)}) collective-permute-start(bf16[128,256]{1,0:T(8,128)(2,1)} %own_ref.1), channel_id=1, source_target_pairs={{0,16},{4,20},{8,24},{12,28},{16,0},{20,4},{24,8},{28,12},{1,17},{... | collective-permute-start | bytes 196616 | tf_op jit(solution)/shard_map/ppermute | solution.py:87
  5.7 5.8 %collective-permute-start = (bf16[128,256]{1,0:T(8,128)(2,1)}, bf16[128,256]{1,0:T(8,128)(2,1)S(1)}, u32[]{:S(2)}, u32[]{:S(2)}) collective-permute-start(bf16[128,256]{1,0:T(8,128)(2,1)} %own_ref.1), channel_id=1, source_target_pairs={{0,8},{4,12},{8,0},{12,4},{16,24},{20,28},{24,16},{28,20},{1,9},{5... | collective-permute-start | bytes 196616 | tf_op jit(solution)/shard_map/ppermute | solution.py:87
  6.4 5.8 %collective-permute-start.3 = (bf16[128,256]{1,0:T(8,128)(2,1)}, bf16[128,256]{1,0:T(8,128)(2,1)S(1)}, u32[]{:S(2)}, u32[]{:S(2)}) collective-permute-start(bf16[128,256]{1,0:T(8,128)(2,1)} %own_ref.1), channel_id=1, source_target_pairs={{0,4},{4,0},{8,12},{12,8},{16,20},{20,16},{24,28},{28,24},{1,5},{5... | collective-permute-start | bytes 196616 | tf_op jit(solution)/shard_map/ppermute | solution.py:87
  6.4 0.7 %copy-start.5 = (s32[128,1]{0,1:T(1,128)S(1)}, s32[128,1]{0,1:T(1,128)}, u32[]{:S(2)}) copy-start(s32[128,1]{0,1:T(1,128)} %param.11) | copy-start | bytes 1540
  7.0 1.0 %copy-start = (bf16[4,1,4,128,128]{4,3,2,1,0:T(8,128)(2,1)S(1)}, bf16[4,1,4,128,128]{4,3,2,1,0:T(8,128)(2,1)}, u32[]{:S(2)}) copy-start(bf16[4,1,4,128,128]{4,3,2,1,0:T(8,128)(2,1)} %param.7) | copy-start | bytes 1572868
  8.1 0.8 %copy-start.2 = (bf16[128,256]{1,0:T(8,128)(2,1)S(1)}, bf16[128,256]{1,0:T(8,128)(2,1)}, u32[]{:S(2)}) copy-start(bf16[128,256]{1,0:T(8,128)(2,1)} %own_ref.1) | copy-start | bytes 196612
  11.6 1.8 %copy-start.4 = (s32[4,1,4]{2,1,0:T(1,128)S(1)}, s32[4,1,4]{2,1,0:T(1,128)}, u32[]{:S(2)}) copy-start(s32[4,1,4]{2,1,0:T(1,128)} %param.8) | copy-start | bytes 196
  11.6 1.3 %collective-permute-start.4 = (bf16[128,256]{1,0:T(8,128)(2,1)S(1)}, bf16[128,256]{1,0:T(8,128)(2,1)S(1)}, u32[]{:S(2)}, u32[]{:S(2)}) collective-permute-start(bf16[128,256]{1,0:T(8,128)(2,1)S(1)} %collective-permute-done.refs_2_), channel_id=1, source_target_pairs={{0,4},{4,0},{8,12},{12,8},{16,20},{20,16},{24,28},{28,24},{1,5},{5... | collective-permute-start | bytes 196616 | tf_op jit(solution)/shard_map/ppermute | solution.py:87
  11.6 1.4 %collective-permute-start.5 = (bf16[128,256]{1,0:T(8,128)(2,1)S(1)}, bf16[128,256]{1,0:T(8,128)(2,1)S(1)}, u32[]{:S(2)}, u32[]{:S(2)}) collective-permute-start(bf16[128,256]{1,0:T(8,128)(2,1)S(1)} %collective-permute-done.1.refs_4_), channel_id=1, source_target_pairs={{0,4},{4,0},{8,12},{12,8},{16,20},{20,16},{24,28},{28,24},{1,5},{5... | collective-permute-start | bytes 196616 | tf_op jit(solution)/shard_map/ppermute | solution.py:87
  12.1 1.3 %collective-permute-start.6 = (bf16[128,256]{1,0:T(8,128)(2,1)S(1)}, bf16[128,256]{1,0:T(8,128)(2,1)S(1)}, u32[]{:S(2)}, u32[]{:S(2)}) collective-permute-start(bf16[128,256]{1,0:T(8,128)(2,1)S(1)} %collective-permute-done.2.refs_6_), channel_id=1, source_target_pairs={{0,4},{4,0},{8,12},{12,8},{16,20},{20,16},{24,28},{28,24},{1,5},{5... | collective-permute-start | bytes 196616 | tf_op jit(solution)/shard_map/ppermute | solution.py:87
  13.3 8.2 %copy-start.1 = (bf16[256,256]{1,0:T(8,128)(2,1)S(1)}, bf16[256,256]{1,0:T(8,128)(2,1)}, u32[]{:S(2)}) copy-start(bf16[256,256]{1,0:T(8,128)(2,1)} %weight_ref.1) | copy-start | bytes 393220
  13.3 8.2 %copy-start.3 = (bf16[128,256]{1,0:T(8,128)(2,1)S(1)}, bf16[128,256]{1,0:T(8,128)(2,1)}, u32[]{:S(2)}) copy-start(bf16[128,256]{1,0:T(8,128)(2,1)} %cot_ref.1) | copy-start | bytes 196612
  14.3 5.3 %collective-permute-start.7 = (bf16[128,256]{1,0:T(8,128)(2,1)S(1)}, bf16[128,256]{1,0:T(8,128)(2,1)S(1)}, u32[]{:S(2)}, u32[]{:S(2)}) collective-permute-start(bf16[128,256]{1,0:T(8,128)(2,1)S(1)} %get-tuple-element.42), channel_id=1, source_target_pairs={{0,3},{1,2},{2,1},{3,0},{4,7},{5,6},{6,5},{7,4},{8,11},{9,10},{10,... | collective-permute-start | bytes 196616 | tf_op jit(solution)/shard_map/ppermute | solution.py:87
  16.8 4.3 %collective-permute-start.8 = (bf16[128,256]{1,0:T(8,128)(2,1)S(1)}, bf16[128,256]{1,0:T(8,128)(2,1)S(1)}, u32[]{:S(2)}, u32[]{:S(2)}) collective-permute-start(bf16[128,256]{1,0:T(8,128)(2,1)S(1)} %get-tuple-element.43), channel_id=1, source_target_pairs={{0,2},{1,3},{2,0},{3,1},{4,6},{5,7},{6,4},{7,5},{8,10},{9,11},{10,... | collective-permute-start | bytes 196616 | tf_op jit(solution)/shard_map/ppermute | solution.py:87
  17.3 4.3 %collective-permute-start.9 = (bf16[128,256]{1,0:T(8,128)(2,1)S(1)}, bf16[128,256]{1,0:T(8,128)(2,1)S(1)}, u32[]{:S(2)}, u32[]{:S(2)}) collective-permute-start(bf16[128,256]{1,0:T(8,128)(2,1)S(1)} %get-tuple-element.44), channel_id=1, source_target_pairs={{0,1},{1,0},{2,3},{3,2},{4,5},{5,4},{6,7},{7,6},{8,9},{9,8},{10,11... | collective-permute-start | bytes 196616 | tf_op jit(solution)/shard_map/ppermute | solution.py:87
  22.0 1.4 %collective-permute-start.10 = (bf16[256,256]{1,0:T(8,128)(2,1)S(1)}, bf16[256,256]{1,0:T(8,128)(2,1)S(1)}, u32[]{:S(2)}, u32[]{:S(2)}) collective-permute-start(bf16[256,256]{1,0:T(8,128)(2,1)S(1)} %get-tuple-element.46), channel_id=1, source_target_pairs={{0,4},{4,0},{8,12},{12,8},{16,20},{20,16},{24,28},{28,24},{1,5},{5... | collective-permute-start | bytes 393224 | tf_op jit(solution)/shard_map/ppermute | solution.py:87
  23.4 5.8 %collective-permute-start.11 = (bf16[64,256]{1,0:T(8,128)(2,1)S(1)}, bf16[64,256]{1,0:T(8,128)(2,1)S(1)}, u32[]{:S(2)}, u32[]{:S(2)}) collective-permute-start(bf16[64,256]{1,0:T(8,128)(2,1)S(1)} %get-tuple-element.48), channel_id=1, source_target_pairs={{0,24},{1,25},{2,26},{3,27},{4,7},{5,6},{6,5},{7,4},{8,16},{9,17},... | collective-permute-start | bytes 98312 | tf_op jit(solution)/shard_map/ppermute | solution.py:328
  26.2 4.8 %collective-permute-start.12 = (bf16[64,256]{1,0:T(8,128)(2,1)S(1)}, bf16[64,256]{1,0:T(8,128)(2,1)S(1)}, u32[]{:S(2)}, u32[]{:S(2)}) collective-permute-start(bf16[64,256]{1,0:T(8,128)(2,1)S(1)} %get-tuple-element.49), channel_id=1, source_target_pairs={{0,16},{1,17},{2,18},{3,19},{4,6},{5,7},{6,4},{7,5},{8,24},{9,25},... | collective-permute-start | bytes 98312 | tf_op jit(solution)/shard_map/ppermute | solution.py:328
  26.2 4.8 %collective-permute-start.13 = (bf16[64,256]{1,0:T(8,128)(2,1)S(1)}, bf16[64,256]{1,0:T(8,128)(2,1)S(1)}, u32[]{:S(2)}, u32[]{:S(2)}) collective-permute-start(bf16[64,256]{1,0:T(8,128)(2,1)S(1)} %get-tuple-element.50), channel_id=1, source_target_pairs={{0,8},{1,9},{2,10},{3,11},{4,5},{5,4},{6,7},{7,6},{8,0},{9,1},{10,... | collective-permute-start | bytes 98312 | tf_op jit(solution)/shard_map/ppermute | solution.py:328
  31.1 5.8 %collective-permute-start.14 = (bf16[64,256]{1,0:T(8,128)(2,1)S(1)}, bf16[64,256]{1,0:T(8,128)(2,1)S(1)}, u32[]{:S(2)}, u32[]{:S(2)}) collective-permute-start(bf16[64,256]{1,0:T(8,128)(2,1)S(1)} %get-tuple-element.52), channel_id=1, source_target_pairs={{0,24},{4,28},{8,16},{12,20},{16,8},{20,12},{24,0},{28,4},{1,25},{... | collective-permute-start | bytes 98312 | tf_op jit(solution)/shard_map/ppermute | solution.py:87
  32.9 5.2 %collective-permute-start.15 = (bf16[64,256]{1,0:T(8,128)(2,1)S(1)}, bf16[64,256]{1,0:T(8,128)(2,1)S(1)}, u32[]{:S(2)}, u32[]{:S(2)}) collective-permute-start(bf16[64,256]{1,0:T(8,128)(2,1)S(1)} %get-tuple-element.53), channel_id=1, source_target_pairs={{0,16},{4,20},{8,24},{12,28},{16,0},{20,4},{24,8},{28,12},{1,17},{... | collective-permute-start | bytes 98312 | tf_op jit(solution)/shard_map/ppermute | solution.py:87
  33.4 4.7 %collective-permute-start.16 = (bf16[64,256]{1,0:T(8,128)(2,1)S(1)}, bf16[64,256]{1,0:T(8,128)(2,1)S(1)}, u32[]{:S(2)}, u32[]{:S(2)}) collective-permute-start(bf16[64,256]{1,0:T(8,128)(2,1)S(1)} %get-tuple-element.54), channel_id=1, source_target_pairs={{0,8},{4,12},{8,0},{12,4},{16,24},{20,28},{24,16},{28,20},{1,9},{5... | collective-permute-start | bytes 98312 | tf_op jit(solution)/shard_map/ppermute | solution.py:87
  38.1 2.1 %collective-permute-start.19 = (bf16[64,256]{1,0:T(8,128)(2,1)S(1)}, bf16[64,256]{1,0:T(8,128)(2,1)S(1)}, u32[]{:S(2)}, u32[]{:S(2)}) collective-permute-start(bf16[64,256]{1,0:T(8,128)(2,1)S(1)} %add.1.refs_0_), channel_id=1, source_target_pairs={{0,0},{1,1},{2,2},{3,3},{4,7},{5,6},{6,5},{7,4},{8,8},{9,9},{10,10... | collective-permute-start | bytes 98312 | tf_op jit(solution)/shard_map/ppermute | solution.py:328
  38.8 1.4 %collective-permute-start.18 = (bf16[64,256]{1,0:T(8,128)(2,1)S(1)}, bf16[64,256]{1,0:T(8,128)(2,1)S(1)}, u32[]{:S(2)}, u32[]{:S(2)}) collective-permute-start(bf16[64,256]{1,0:T(8,128)(2,1)S(1)} %add.1.refs_0_), channel_id=1, source_target_pairs={{0,0},{1,1},{2,2},{3,3},{4,6},{5,7},{6,4},{7,5},{8,8},{9,9},{10,10... | collective-permute-start | bytes 98312 | tf_op jit(solution)/shard_map/ppermute | solution.py:328
  39.5 0.7 %collective-permute-start.17 = (bf16[64,256]{1,0:T(8,128)(2,1)S(1)}, bf16[64,256]{1,0:T(8,128)(2,1)S(1)}, u32[]{:S(2)}, u32[]{:S(2)}) collective-permute-start(bf16[64,256]{1,0:T(8,128)(2,1)S(1)} %add.1.refs_0_), channel_id=1, source_target_pairs={{0,0},{1,1},{2,2},{3,3},{4,5},{5,4},{6,7},{7,6},{8,8},{9,9},{10,10... | collective-permute-start | bytes 98312 | tf_op jit(solution)/shard_map/ppermute | solution.py:328
  40.2 6.5 %collective-permute-start.20 = (bf16[256,256]{1,0:T(8,128)(2,1)S(1)}, bf16[256,256]{1,0:T(8,128)(2,1)S(1)}, u32[]{:S(2)}, u32[]{:S(2)}) collective-permute-start(bf16[256,256]{1,0:T(8,128)(2,1)S(1)} %get-tuple-element.59), channel_id=1, source_target_pairs={{0,4},{4,0},{8,12},{12,8},{16,20},{20,16},{24,28},{28,24},{1,5},{5... | collective-permute-start | bytes 393224 | tf_op jit(solution)/shard_map/ppermute | solution.py:87

commit v8 on v5

--- a/solution.py
+++ b/solution.py
@@ -141,105 +141,96 @@
     )(weight, cotangent, placing, *parts)
 
 
-def split_kernel(n_rep, packed_ref, term_ref, came_ref, own_ref, *refs):
-    chunk_refs, message_refs, term = refs[: n_rep - 1], refs[n_rep - 1 : -1], refs[-1]
-    rep = lax.axis_index("rep")
+def split_kernel(packed_ref, term_ref, came_ref, *out_refs):
+    core = lax.axis_index("section") & 1
     width = term_ref.shape[0]
-    total = term_ref[...] + came_ref[:width].astype(jnp.float32)
-    term[...] = total.reshape(term.shape)
-    own_ref[...] = term[rep]
-    for ref, j in zip(chunk_refs, across(n_rep)):
-        ref[...] = term[rep ^ j].astype(jnp.bfloat16)
-    rows = packed_ref.shape[0] // len(message_refs)
-    for ref, j in zip(message_refs, [0] + across(len(message_refs))):
-        ref[:rows] = packed_ref[j * rows : (j + 1) * rows]
-        ref[rows:] = came_ref[j * rows : (j + 1) * rows]
+    rows = 2 * packed_ref.shape[0] // lax.axis_size("section")
+
+    @pl.when(core == 1)
+    def _():
+        total = (term_ref[...] + came_ref[:width].astype(jnp.float32)).astype(jnp.bfloat16)
+        for ref in out_refs:
+            ref[:width] = total
+
+    @pl.when(core == 0)
+    def _():
+        for ref, j in zip(out_refs, [0] + across(len(out_refs))):
+            start = j * rows % packed_ref.shape[0]
+            ref[:rows] = packed_ref[start : start + rows]
+            ref[rows : 2 * rows] = came_ref[start : start + rows]
 
 
 def split(packed, term, came, n_rep, chips):
     places, width = packed.shape
-    chunk = (width // n_rep, width)
-    return pl.pallas_call(
-        functools.partial(split_kernel, n_rep),
-        out_shape=[jax.ShapeDtypeStruct(chunk, jnp.float32)]
-        + [jax.ShapeDtypeStruct(chunk, jnp.bfloat16)] * (n_rep - 1)
-        + [jax.ShapeDtypeStruct((2 * places // chips, width), jnp.bfloat16)] * chips,
+    many = max(n_rep, chips)
+    return pl.pallas_call(
+        split_kernel,
+        out_shape=[jax.ShapeDtypeStruct((max(width, 2 * places // chips), width), jnp.bfloat16)] * many,
         in_specs=[VMEM] * 3,
-        out_specs=[VMEM] * (n_rep + chips),
-        scratch_shapes=[pltpu.VMEM((n_rep,) + chunk, jnp.float32)],
+        out_specs=[VMEM] * many,
         compiler_params=LIMIT,
         name="split",
     )(packed, term, came)
 
 
-def add_kernel(*refs):
-    refs[-1][...] = tree_sum([ref[...].astype(jnp.float32) for ref in refs[:-1]]).astype(jnp.bfloat16)
-
-
-def add(terms):
-    return pl.pallas_call(
-        add_kernel,
-        out_shape=jax.ShapeDtypeStruct(terms[0].shape, jnp.bfloat16),
-        in_specs=[VMEM] * len(terms),
+def middle_kernel(n_rep, slots, *refs):
+    values, total_ref, out_refs = refs[:-3], refs[-3], refs[-2:]
+    section = lax.axis_index("section")
+    chips = lax.axis_size("section") // 2
+    by_xor = [values[0]] + list(values[:0:-1])
+    width = total_ref.shape[0]
+
+    @pl.when(section & 1 == 1)
+    def _():
+        total = tree_sum([ref[:width].astype(jnp.float32) for ref in by_xor[:n_rep]])
+        total_ref[...] = total.astype(jnp.bfloat16)
+
+    @pl.when(section & 1 == 0)
+    def _():
+        total_ref[...] = jnp.zeros_like(total_ref)
+        for j in range(chips):
+            for source in range(2):
+                for core in range(2):
+                    start = (2 * source + core) * slots
+                    out_refs[core][section ^ (2 * j + source)] = by_xor[j][start : start + slots]
+
+
+def middle(values, n_rep, n_section, slots):
+    width = values[0].shape[1]
+    rows = jax.ShapeDtypeStruct((n_section, slots, width), jnp.bfloat16)
+    return pl.pallas_call(
+        functools.partial(middle_kernel, n_rep, slots),
+        out_shape=(jax.ShapeDtypeStruct((width, width), jnp.bfloat16), rows, rows),
+        in_specs=[VMEM] * len(values),
+        out_specs=(VMEM,) * 3,
+        compiler_params=LIMIT,
+        name="middle",
+    )(*values)
+
+
+def place_kernel(other_ref, *refs):
+    core = lax.axis_index("section") & 1
+
+    @pl.when(core == 0)
+    def _():
+        refs[-1][: other_ref.shape[0]] = other_ref[...]
+
+    @pl.when(core == 1)
+    def _():
+        total = tree_sum([ref[...].astype(jnp.float32) for ref in refs[:-1]])
+        refs[-1][: total.shape[0]] = total.astype(jnp.bfloat16)
+
+
+def place(other, terms):
+    width = terms[0].shape[0]
+    return pl.pallas_call(
+        place_kernel,
+        out_shape=jax.ShapeDtypeStruct((max(width, other.shape[0]), width), jnp.bfloat16),
+        in_specs=[VMEM] * (1 + len(terms)),
         out_specs=VMEM,
         compiler_params=LIMIT,
-        name="add",
-    )(*terms)
-
-
-def unpack_kernel(slots, *refs):
-    message_refs, out_refs = refs[:-2], refs[-2:]
-    chip = lax.axis_index("section") & -2
-    for j, ref in zip([0] + across(len(message_refs)), message_refs):
-        for source in range(2):
-            for core in range(2):
-                start = (2 * source + core) * slots
-                out_refs[core][chip ^ (2 * j) | source] = ref[start : start + slots]
-
-
-def unpack(messages, slots):
-    width = messages[0].shape[1]
-    n_section = 2 * len(messages)
-    return pl.pallas_call(
-        functools.partial(unpack_kernel, slots),
-        out_shape=[jax.ShapeDtypeStruct((n_section, slots, width), jnp.bfloat16)] * 2,
-        in_specs=[VMEM] * len(messages),
-        out_specs=[VMEM] * 2,
-        compiler_params=LIMIT,
-        name="unpack",
-    )(*messages)
-
-
-def place_kernel(other_ref, *refs):
-    chunk_refs, (whole_ref, sent_ref) = refs[:-2], refs[-2:]
-    rep, core = lax.axis_index("rep"), lax.axis_index("section") & 1
-    for j, ref in enumerate(chunk_refs):
-        whole_ref[rep ^ j] = ref[...]
-
-    @pl.when(core == 0)
-    def _():
-        sent_ref[: other_ref.shape[0]] = other_ref[...]
-
-    @pl.when(core == 1)
-    def _():
-        n_rep, rows, _ = whole_ref.shape
-        for r in range(n_rep):
-            sent_ref[r * rows : (r + 1) * rows] = whole_ref[r]
-
-
-def place(chunks, other):
-    rows, width = chunks[0].shape
-    return pl.pallas_call(
-        place_kernel,
-        out_shape=(
-            jax.ShapeDtypeStruct((len(chunks), rows, width), jnp.bfloat16),
-            jax.ShapeDtypeStruct((max(len(chunks) * rows, other.shape[0]), width), jnp.bfloat16),
-        ),
-        in_specs=[VMEM] * (1 + len(chunks)),
-        out_specs=(VMEM,) * 2,
-        compiler_params=LIMIT,
         name="place",
-    )(other, *chunks)
+    )(other, *terms)
 
 
 def finish_kernel(whole_ref, mine_ref, came_ref, relaid_ref, grad_ref):
@@ -252,7 +243,7 @@
 
     @pl.when(core == 1)
     def _():
-        grad_ref[...] = whole_ref[...].astype(jnp.float32)
+        grad_ref[...] = whole_ref[: grad_ref.shape[0]].astype(jnp.float32)
         relaid_ref[...] = came_ref[: relaid_ref.shape[0]]
 
 
@@ -261,7 +252,7 @@
         finish_kernel,
         out_shape=(
             jax.ShapeDtypeStruct(mine.shape, jnp.bfloat16),
-            jax.ShapeDtypeStruct(whole.shape, jnp.float32),
+            jax.ShapeDtypeStruct((whole.shape[1],) * 2, jnp.float32),
         ),
         in_specs=[VMEM] * 3,
         out_specs=(VMEM,) * 2,
@@ -270,13 +261,13 @@
     )(whole, mine, came)
 
 
-def swap_on_core(value, core, section_xor, rep_xor):
-    n_rep = lax.axis_size("rep")
-    pairs = [
-        (s * n_rep + r, (s ^ section_xor) * n_rep + (r ^ rep_xor))
-        for s in range(core, lax.axis_size("section"), 2)
-        for r in range(n_rep)
-    ]
+def swap_by_core(value, first, second):
+    n_section, n_rep = lax.axis_size("section"), lax.axis_size("rep")
+    pairs = []
+    for s in range(n_section):
+        chip, rep = second if s & 1 else first
+        for r in range(n_rep):
+            pairs.append((s * n_rep + r, (s ^ 2 * chip % n_section) * n_rep + (r ^ rep % n_rep)))
     return lax.ppermute(value, ("section", "rep"), pairs)
 
 
@@ -287,7 +278,7 @@
     for j in range(2, n, 2):
         blocks[j] = swap(features, axis, j)
     blocks[1] = swap(features, axis, 1)
-    blocks[2], ready = lax.optimization_barrier((blocks[2], ready))
+    blocks[2::2], ready = lax.optimization_barrier((blocks[2::2], ready))
     for j in range(2, n, 2):
         blocks[j + 1] = swap(blocks[j], axis, 1)
     return blocks, ready
@@ -307,20 +298,14 @@
     packed, term, sent = dense(parts, weight, cotangent, placing)
     came = swap(sent, "section", 1)
     chips = n_section // 2
-    own, *rest = split(packed, term, came, n_rep, chips)
-    terms, messages = rest[: n_rep - 1], rest[n_rep - 1 :]
-    terms = [swap_on_core(t, 1, 0, j) for t, j in zip(terms, others)]
-    chunk = add([own] + terms)
-    others = across(chips)
-    messages = messages[:1] + [swap_on_core(m, 0, 2 * j, 0) for m, j in zip(messages[1:], others)]
-    chunk = add([chunk] + [swap_on_core(chunk, 1, 2 * j, 0) for j in range(1, chips)])
-    mine, other = unpack(messages, slots)
-    chunks = [chunk] + [swap_on_core(chunk, 1, 0, j) for j in range(1, n_rep)]
-    whole, sent = place(chunks, other.reshape(n_section * slots, width))
+    own, *values = split(packed, term, came, n_rep, chips)
+    steps = across(len(values) + 1)
+    values = [own] + [swap_by_core(v, (j, 0), (0, j)) for v, j in zip(values, steps)]
+    total, mine, other = middle(values, n_rep, n_section, slots)
+    terms = [total] + [swap_by_core(total, (0, 1 + j % 2), (j, 0)) for j in range(1, chips)]
+    sent = place(other.reshape(n_section * slots, width), terms)
     came = swap(sent, "section", 1)
-    relaid, weight_grad = finish(
-        whole.reshape(width, width), mine.reshape(n_section * slots, width), came
-    )
+    relaid, weight_grad = finish(sent, mine.reshape(n_section * slots, width), came)
     return (relaid.reshape(1, 1, n_section, slots, width), weight_grad)
 
 

time: 59.9 us -> 44.6 us (0.74)
  the two profiles are of different devices: /device:TPU:0 before, /device:TPU:27 now
where the time goes in v8:
time: 44.6 us; the launch traced here: 44.4 us
  starting transfers between devices  23.6 us (53%)
  waiting for transfers between devices  15.1 us (34%)
  local copies, waits for them, and re-layouts  2.55 us (6%)
  Pallas kernels  2.5 us (6%)
  between operations  0.74 us (2%)
    ppermute x12, starting transfers between devices, swap(): lax.ppermute(value, axis, [(i, i ^ j) for i in range(lax.axis_size(axis))])  17.2 us
    ppermute x6, waiting for transfers between devices, swap_by_core(): return lax.ppermute(value, ('section', 'rep'), pairs)  8.57 us
    ppermute x12, waiting for transfers between devices, swap(): lax.ppermute(value, axis, [(i, i ^ j) for i in range(lax.axis_size(axis))])  6.49 us
    ppermute x6, starting transfers between devices, swap_by_core(): return lax.ppermute(value, ('section', 'rep'), pairs)  6.33 us
    unnamed x12, local copies, waits for them, and re-layouts  2.55 us
    pallas_call x1, Pallas kernels, partials(): pl.pallas_call(functools.partial(partials_kernel, len(blocks)), out_shape...  0.91 us
  transfers between devices with their start and end apart: 18, of which 11 were waited for; matrix products, arithmetic and copies ran while one was open for 0% of the time, Pallas kernels for 0%

profile of v8, /device:TPU:27, one launch (start us, length us, event | category | flops | bytes accessed | tf_op | source)
XLA Modules:
  0.0 44.4 jit_solution(18316102736045181433)
XLA Ops:
  0.6 0.1 collective-permute-start.2
  0.7 1.3 %collective-permute-start.1 = (bf16[128,256]{1,0:T(8,128)(2,1)}, bf16[128,256]{1,0:T(8,128)(2,1)S(1)}, u32[]{:S(2)}, u32[]{:S(2)}) collective-permute-start(bf16[128,256]{1,0:T(8,128)(2,1)} %own_ref.1), channel_id=1, source_target_pairs={{0,16},{4,20},{8,24},{12,28},{16,0},{20,4},{24,8},{28,12},{1,17},{... | collective-permute-start | bytes 196616 | tf_op jit(solution)/shard_map/ppermute | solution.py:87
  2.0 2.2 %collective-permute-start = (bf16[128,256]{1,0:T(8,128)(2,1)}, bf16[128,256]{1,0:T(8,128)(2,1)S(1)}, u32[]{:S(2)}, u32[]{:S(2)}) collective-permute-start(bf16[128,256]{1,0:T(8,128)(2,1)} %own_ref.1), channel_id=1, source_target_pairs={{0,8},{4,12},{8,0},{12,4},{16,24},{20,28},{24,16},{28,20},{1,9},{5... | collective-permute-start | bytes 196616 | tf_op jit(solution)/shard_map/ppermute | solution.py:87
  4.2 1.5 %collective-permute-start.3 = (bf16[128,256]{1,0:T(8,128)(2,1)}, bf16[128,256]{1,0:T(8,128)(2,1)S(1)}, u32[]{:S(2)}, u32[]{:S(2)}) collective-permute-start(bf16[128,256]{1,0:T(8,128)(2,1)} %own_ref.1), channel_id=1, source_target_pairs={{0,4},{4,0},{8,12},{12,8},{16,20},{20,16},{24,28},{28,24},{1,5},{5... | collective-permute-start | bytes 196616 | tf_op jit(solution)/shard_map/ppermute | solution.py:87
  5.8 0.7 %copy-done.5 = s32[128,1]{0,1:T(1,128)S(1)} copy-done((s32[128,1]{0,1:T(1,128)S(1)}, s32[128,1]{0,1:T(1,128)}, u32[]{:S(2)}) %copy-start.5) | copy-done | bytes 536
  6.4 1.0 %copy-done = bf16[4,1,4,128,128]{4,3,2,1,0:T(8,128)(2,1)S(1)} copy-done((bf16[4,1,4,128,128]{4,3,2,1,0:T(8,128)(2,1)S(1)}, bf16[4,1,4,128,128]{4,3,2,1,0:T(8,128)(2,1)}, u32[]{:S(2)}) %copy-start) | copy-done | bytes 524312
  7.5 0.8 %copy-done.2 = bf16[128,256]{1,0:T(8,128)(2,1)S(1)} copy-done((bf16[128,256]{1,0:T(8,128)(2,1)S(1)}, bf16[128,256]{1,0:T(8,128)(2,1)}, u32[]{:S(2)}) %copy-start.2) | copy-done | bytes 65560
  8.3 0.2 prepare.1
  8.5 0.0 collective-permute-done.2.refs_6_
  8.5 0.0 collective-permute-done.1.refs_4_
  8.5 0.0 collective-permute-done.refs_2_
  8.6 0.0 copy-start.4
  8.6 1.3 %collective-permute-start.4 = (bf16[128,256]{1,0:T(8,128)(2,1)S(1)}, bf16[128,256]{1,0:T(8,128)(2,1)S(1)}, u32[]{:S(2)}, u32[]{:S(2)}) collective-permute-start(bf16[128,256]{1,0:T(8,128)(2,1)S(1)} %collective-permute-done.refs_2_), channel_id=1, source_target_pairs={{0,4},{4,0},{8,12},{12,8},{16,20},{20,16},{24,28},{28,24},{1,5},{5... | collective-permute-start | bytes 196616 | tf_op jit(solution)/shard_map/ppermute | solution.py:87
  9.9 0.1 collective-permute-start.5
  10.0 0.4 collective-permute-start.6
  10.4 0.0 collective-permute-done.3.refs_1_
  10.4 0.4 collective-permute-done.4.refs_3_
  10.8 0.4 collective-permute-done.5.refs_5_
  11.2 0.2 collective-permute-done.6.refs_7_
  11.3 0.0 copy-done.4
  11.3 0.9 %partials.1 = (bf16[128,256]{1,0:T(8,128)(2,1)S(1)}, bf16[128,256]{1,0:T(8,128)(2,1)S(1)}, bf16[128,256]{1,0:T(8,128)(2,1)S(1)}, bf16[128,256]{1,0:T(8,128)(2,1)S(1)}) custom-call(s32[4,4]{1,0:T(4,128)S(1)} %bitcast.9, bf16[4,128,512]{2,1,0:T(8,128)(2,1)S(1)} %get-tuple-element.31.wide_ref, bf16[128,256]{1,0:T(8,128)(2,1)S(1)} %get-tuple-element.32.refs_0_, ...), custom_call_target="tpu_custom_call" | custom-call | tf_op jit(solution)/shard_map/partials/pallas_call | solution.py:75
  12.2 1.3 %collective-permute-start.7 = (bf16[128,256]{1,0:T(8,128)(2,1)S(1)}, bf16[128,256]{1,0:T(8,128)(2,1)S(1)}, u32[]{:S(2)}, u32[]{:S(2)}) collective-permute-start(bf16[128,256]{1,0:T(8,128)(2,1)S(1)} %get-tuple-element.37), channel_id=1, source_target_pairs={{0,3},{1,2},{2,1},{3,0},{4,7},{5,6},{6,5},{7,4},{8,11},{9,10},{10,... | collective-permute-start | bytes 196616 | tf_op jit(solution)/shard_map/ppermute | solution.py:87
  13.5 0.2 collective-permute-start.8
  13.8 1.2 %collective-permute-start.9 = (bf16[128,256]{1,0:T(8,128)(2,1)S(1)}, bf16[128,256]{1,0:T(8,128)(2,1)S(1)}, u32[]{:S(2)}, u32[]{:S(2)}) collective-permute-start(bf16[128,256]{1,0:T(8,128)(2,1)S(1)} %get-tuple-element.39), channel_id=1, source_target_pairs={{0,1},{1,0},{2,3},{3,2},{4,5},{5,4},{6,7},{7,6},{8,9},{9,8},{10,11... | collective-permute-start | bytes 196616 | tf_op jit(solution)/shard_map/ppermute | solution.py:87
  15.0 1.4 %collective-permute-done.7.refs_1_ = bf16[128,256]{1,0:T(8,128)(2,1)S(1)} collective-permute-done((bf16[128,256]{1,0:T(8,128)(2,1)S(1)}, bf16[128,256]{1,0:T(8,128)(2,1)S(1)}, u32[]{:S(2)}, u32[]{:S(2)}) %collective-permute-start.7) | collective-permute-done | bytes 65568 | tf_op jit(solution)/shard_map/ppermute | solution.py:87
  16.4 2.2 %collective-permute-done.8.refs_2_ = bf16[128,256]{1,0:T(8,128)(2,1)S(1)} collective-permute-done((bf16[128,256]{1,0:T(8,128)(2,1)S(1)}, bf16[128,256]{1,0:T(8,128)(2,1)S(1)}, u32[]{:S(2)}, u32[]{:S(2)}) %collective-permute-start.8) | collective-permute-done | bytes 65568 | tf_op jit(solution)/shard_map/ppermute | solution.py:87
  18.6 0.0 collective-permute-done.9.refs_3_
  18.6 0.0 copy-done.1
  18.6 0.4 dense.1
  19.0 0.7 %collective-permute-start.10 = (bf16[256,256]{1,0:T(8,128)(2,1)S(1)}, bf16[256,256]{1,0:T(8,128)(2,1)S(1)}, u32[]{:S(2)}, u32[]{:S(2)}) collective-permute-start(bf16[256,256]{1,0:T(8,128)(2,1)S(1)} %get-tuple-element.42), channel_id=1, source_target_pairs={{0,4},{4,0},{8,12},{12,8},{16,20},{20,16},{24,28},{28,24},{1,5},{5... | collective-permute-start | bytes 393224 | tf_op jit(solution)/shard_map/ppermute | solution.py:87
  19.7 1.0 %collective-permute-done.10.came_ref = bf16[256,256]{1,0:T(8,128)(2,1)S(1)} collective-permute-done((bf16[256,256]{1,0:T(8,128)(2,1)S(1)}, bf16[256,256]{1,0:T(8,128)(2,1)S(1)}, u32[]{:S(2)}, u32[]{:S(2)}) %collective-permute-start.10) | collective-permute-done | bytes 131104 | tf_op jit(solution)/shard_map/ppermute | solution.py:87
  20.7 2.0 %collective-permute-start.11 = (bf16[256,256]{1,0:T(8,128)(2,1)S(1)}, bf16[256,256]{1,0:T(8,128)(2,1)S(1)}, u32[]{:S(2)}, u32[]{:S(2)}) collective-permute-start(bf16[256,256]{1,0:T(8,128)(2,1)S(1)} %get-tuple-element.44), channel_id=1, source_target_pairs={{0,24},{1,25},{2,26},{3,27},{4,7},{5,6},{6,5},{7,4},{8,16},{9,17},... | collective-permute-start | bytes 393224 | tf_op jit(solution)/shard_map/ppermute | solution.py:271
  22.7 0.2 collective-permute-start.12
  22.9 0.5 %collective-permute-start.13 = (bf16[256,256]{1,0:T(8,128)(2,1)S(1)}, bf16[256,256]{1,0:T(8,128)(2,1)S(1)}, u32[]{:S(2)}, u32[]{:S(2)}) collective-permute-start(bf16[256,256]{1,0:T(8,128)(2,1)S(1)} %get-tuple-element.46), channel_id=1, source_target_pairs={{0,8},{1,9},{2,10},{3,11},{4,5},{5,4},{6,7},{7,6},{8,0},{9,1},{10,... | collective-permute-start | bytes 393224 | tf_op jit(solution)/shard_map/ppermute | solution.py:271
  23.4 2.1 %collective-permute-done.11.refs_1_ = bf16[256,256]{1,0:T(8,128)(2,1)S(1)} collective-permute-done((bf16[256,256]{1,0:T(8,128)(2,1)S(1)}, bf16[256,256]{1,0:T(8,128)(2,1)S(1)}, u32[]{:S(2)}, u32[]{:S(2)}) %collective-permute-start.11) | collective-permute-done | bytes 131104 | tf_op jit(solution)/shard_map/ppermute | solution.py:271
  25.5 1.7 %collective-permute-done.12.refs_2_ = bf16[256,256]{1,0:T(8,128)(2,1)S(1)} collective-permute-done((bf16[256,256]{1,0:T(8,128)(2,1)S(1)}, bf16[256,256]{1,0:T(8,128)(2,1)S(1)}, u32[]{:S(2)}, u32[]{:S(2)}) %collective-permute-start.12) | collective-permute-done | bytes 131104 | tf_op jit(solution)/shard_map/ppermute | solution.py:271
  27.2 0.0 collective-permute-done.13.refs_3_
  27.2 0.1 middle.1
  27.3 0.9 %collective-permute-start.16 = (bf16[256,256]{1,0:T(8,128)(2,1)S(1)}, bf16[256,256]{1,0:T(8,128)(2,1)S(1)}, u32[]{:S(2)}, u32[]{:S(2)}) collective-permute-start(bf16[256,256]{1,0:T(8,128)(2,1)S(1)} %get-tuple-element.48.refs_0_), channel_id=1, source_target_pairs={{0,2},{1,3},{2,0},{3,1},{4,28},{5,29},{6,30},{7,31},{8,10},{9,11},... | collective-permute-start | bytes 393224 | tf_op jit(solution)/shard_map/ppermute | solution.py:271
  28.2 0.1 collective-permute-start.15
  28.3 2.6 %collective-permute-start.14 = (bf16[256,256]{1,0:T(8,128)(2,1)S(1)}, bf16[256,256]{1,0:T(8,128)(2,1)S(1)}, u32[]{:S(2)}, u32[]{:S(2)}) collective-permute-start(bf16[256,256]{1,0:T(8,128)(2,1)S(1)} %get-tuple-element.48.refs_0_), channel_id=1, source_target_pairs={{0,2},{1,3},{2,0},{3,1},{4,12},{5,13},{6,14},{7,15},{8,10},{9,11},... | collective-permute-start | bytes 393224 | tf_op jit(solution)/shard_map/ppermute | solution.py:271
  30.9 2.3 %collective-permute-done.16.refs_3_ = bf16[256,256]{1,0:T(8,128)(2,1)S(1)} collective-permute-done((bf16[256,256]{1,0:T(8,128)(2,1)S(1)}, bf16[256,256]{1,0:T(8,128)(2,1)S(1)}, u32[]{:S(2)}, u32[]{:S(2)}) %collective-permute-start.16) | collective-permute-done | bytes 131104 | tf_op jit(solution)/shard_map/ppermute | solution.py:271
  33.2 2.5 %collective-permute-done.15.refs_2_ = bf16[256,256]{1,0:T(8,128)(2,1)S(1)} collective-permute-done((bf16[256,256]{1,0:T(8,128)(2,1)S(1)}, bf16[256,256]{1,0:T(8,128)(2,1)S(1)}, u32[]{:S(2)}, u32[]{:S(2)}) %collective-permute-start.15) | collective-permute-done | bytes 131104 | tf_op jit(solution)/shard_map/ppermute | solution.py:271
  35.7 0.0 collective-permute-done.14.refs_1_
  35.7 0.1 place.1.whole_ref
  35.8 6.9 %collective-permute-start.17 = (bf16[256,256]{1,0:T(8,128)(2,1)S(1)}, bf16[256,256]{1,0:T(8,128)(2,1)S(1)}, u32[]{:S(2)}, u32[]{:S(2)}) collective-permute-start(bf16[256,256]{1,0:T(8,128)(2,1)S(1)} %place.1.whole_ref), channel_id=1, source_target_pairs={{0,4},{4,0},{8,12},{12,8},{16,20},{20,16},{24,28},{28,24},{1,5},{5... | collective-permute-start | bytes 393224 | tf_op jit(solution)/shard_map/ppermute | solution.py:87
  42.6 1.0 %collective-permute-done.17.came_ref = bf16[256,256]{1,0:T(8,128)(2,1)S(1)} collective-permute-done((bf16[256,256]{1,0:T(8,128)(2,1)S(1)}, bf16[256,256]{1,0:T(8,128)(2,1)S(1)}, u32[]{:S(2)}, u32[]{:S(2)}) %collective-permute-start.17) | collective-permute-done | bytes 131104 | tf_op jit(solution)/shard_map/ppermute | solution.py:87
  43.6 0.8 %finish.1 = (bf16[256,256]{1,0:T(8,128)(2,1)}, f32[256,256]{1,0:T(8,128)}) custom-call(bf16[256,256]{1,0:T(8,128)(2,1)S(1)} %place.1.whole_ref, bf16[256,256]{1,0:T(8,128)(2,1)S(1)} %bitcast.7, bf16[256,256]{1,0:T(8,128)(2,1)S(1)} %collective-permute-done.17.came_ref), custom_call_target="tpu_custom_call" | custom-call | tf_op jit(solution)/shard_map/finish/pallas_call | solution.py:251
  (7 shorter events, 0.0 us)
Async XLA Ops:
  0.6 7.9 %collective-permute-start.2 = (bf16[128,256]{1,0:T(8,128)(2,1)}, bf16[128,256]{1,0:T(8,128)(2,1)S(1)}, u32[]{:S(2)}, u32[]{:S(2)}) collective-permute-start(bf16[128,256]{1,0:T(8,128)(2,1)} %own_ref.1), channel_id=1, source_target_pairs={{0,24},{4,28},{8,16},{12,20},{16,8},{20,12},{24,0},{28,4},{1,25},{... | collective-permute-start | bytes 196616 | tf_op jit(solution)/shard_map/ppermute | solution.py:87
  0.7 7.8 %collective-permute-start.1 = (bf16[128,256]{1,0:T(8,128)(2,1)}, bf16[128,256]{1,0:T(8,128)(2,1)S(1)}, u32[]{:S(2)}, u32[]{:S(2)}) collective-permute-start(bf16[128,256]{1,0:T(8,128)(2,1)} %own_ref.1), channel_id=1, source_target_pairs={{0,16},{4,20},{8,24},{12,28},{16,0},{20,4},{24,8},{28,12},{1,17},{... | collective-permute-start | bytes 196616 | tf_op jit(solution)/shard_map/ppermute | solution.py:87
  2.0 6.5 %collective-permute-start = (bf16[128,256]{1,0:T(8,128)(2,1)}, bf16[128,256]{1,0:T(8,128)(2,1)S(1)}, u32[]{:S(2)}, u32[]{:S(2)}) collective-permute-start(bf16[128,256]{1,0:T(8,128)(2,1)} %own_ref.1), channel_id=1, source_target_pairs={{0,8},{4,12},{8,0},{12,4},{16,24},{20,28},{24,16},{28,20},{1,9},{5... | collective-permute-start | bytes 196616 | tf_op jit(solution)/shard_map/ppermute | solution.py:87
  4.2 6.2 %collective-permute-start.3 = (bf16[128,256]{1,0:T(8,128)(2,1)}, bf16[128,256]{1,0:T(8,128)(2,1)S(1)}, u32[]{:S(2)}, u32[]{:S(2)}) collective-permute-start(bf16[128,256]{1,0:T(8,128)(2,1)} %own_ref.1), channel_id=1, source_target_pairs={{0,4},{4,0},{8,12},{12,8},{16,20},{20,16},{24,28},{28,24},{1,5},{5... | collective-permute-start | bytes 196616 | tf_op jit(solution)/shard_map/ppermute | solution.py:87
  5.8 0.7 %copy-start.5 = (s32[128,1]{0,1:T(1,128)S(1)}, s32[128,1]{0,1:T(1,128)}, u32[]{:S(2)}) copy-start(s32[128,1]{0,1:T(1,128)} %param.11) | copy-start | bytes 1540
  6.4 1.0 %copy-start = (bf16[4,1,4,128,128]{4,3,2,1,0:T(8,128)(2,1)S(1)}, bf16[4,1,4,128,128]{4,3,2,1,0:T(8,128)(2,1)}, u32[]{:S(2)}) copy-start(bf16[4,1,4,128,128]{4,3,2,1,0:T(8,128)(2,1)} %param.7) | copy-start | bytes 1572868
  7.5 0.8 %copy-start.2 = (bf16[128,256]{1,0:T(8,128)(2,1)S(1)}, bf16[128,256]{1,0:T(8,128)(2,1)}, u32[]{:S(2)}) copy-start(bf16[128,256]{1,0:T(8,128)(2,1)} %own_ref.1) | copy-start | bytes 196612
  8.6 2.8 %copy-start.4 = (s32[4,1,4]{2,1,0:T(1,128)S(1)}, s32[4,1,4]{2,1,0:T(1,128)}, u32[]{:S(2)}) copy-start(s32[4,1,4]{2,1,0:T(1,128)} %param.8) | copy-start | bytes 196
  8.6 2.2 %collective-permute-start.4 = (bf16[128,256]{1,0:T(8,128)(2,1)S(1)}, bf16[128,256]{1,0:T(8,128)(2,1)S(1)}, u32[]{:S(2)}, u32[]{:S(2)}) collective-permute-start(bf16[128,256]{1,0:T(8,128)(2,1)S(1)} %collective-permute-done.refs_2_), channel_id=1, source_target_pairs={{0,4},{4,0},{8,12},{12,8},{16,20},{20,16},{24,28},{28,24},{1,5},{5... | collective-permute-start | bytes 196616 | tf_op jit(solution)/shard_map/ppermute | solution.py:87
  9.9 1.3 %collective-permute-start.5 = (bf16[128,256]{1,0:T(8,128)(2,1)S(1)}, bf16[128,256]{1,0:T(8,128)(2,1)S(1)}, u32[]{:S(2)}, u32[]{:S(2)}) collective-permute-start(bf16[128,256]{1,0:T(8,128)(2,1)S(1)} %collective-permute-done.1.refs_4_), channel_id=1, source_target_pairs={{0,4},{4,0},{8,12},{12,8},{16,20},{20,16},{24,28},{28,24},{1,5},{5... | collective-permute-start | bytes 196616 | tf_op jit(solution)/shard_map/ppermute | solution.py:87
  10.0 1.3 %collective-permute-start.6 = (bf16[128,256]{1,0:T(8,128)(2,1)S(1)}, bf16[128,256]{1,0:T(8,128)(2,1)S(1)}, u32[]{:S(2)}, u32[]{:S(2)}) collective-permute-start(bf16[128,256]{1,0:T(8,128)(2,1)S(1)} %collective-permute-done.2.refs_6_), channel_id=1, source_target_pairs={{0,4},{4,0},{8,12},{12,8},{16,20},{20,16},{24,28},{28,24},{1,5},{5... | collective-permute-start | bytes 196616 | tf_op jit(solution)/shard_map/ppermute | solution.py:87
  11.3 7.2 %copy-start.1 = (bf16[256,256]{1,0:T(8,128)(2,1)S(1)}, bf16[256,256]{1,0:T(8,128)(2,1)}, u32[]{:S(2)}) copy-start(bf16[256,256]{1,0:T(8,128)(2,1)} %weight_ref.1) | copy-start | bytes 393220
  11.3 7.2 %copy-start.3 = (bf16[128,256]{1,0:T(8,128)(2,1)S(1)}, bf16[128,256]{1,0:T(8,128)(2,1)}, u32[]{:S(2)}) copy-start(bf16[128,256]{1,0:T(8,128)(2,1)} %cot_ref.1) | copy-start | bytes 196612
  12.2 4.1 %collective-permute-start.7 = (bf16[128,256]{1,0:T(8,128)(2,1)S(1)}, bf16[128,256]{1,0:T(8,128)(2,1)S(1)}, u32[]{:S(2)}, u32[]{:S(2)}) collective-permute-start(bf16[128,256]{1,0:T(8,128)(2,1)S(1)} %get-tuple-element.37), channel_id=1, source_target_pairs={{0,3},{1,2},{2,1},{3,0},{4,7},{5,6},{6,5},{7,4},{8,11},{9,10},{10,... | collective-permute-start | bytes 196616 | tf_op jit(solution)/shard_map/ppermute | solution.py:87
  13.5 5.0 %collective-permute-start.8 = (bf16[128,256]{1,0:T(8,128)(2,1)S(1)}, bf16[128,256]{1,0:T(8,128)(2,1)S(1)}, u32[]{:S(2)}, u32[]{:S(2)}) collective-permute-start(bf16[128,256]{1,0:T(8,128)(2,1)S(1)} %get-tuple-element.38), channel_id=1, source_target_pairs={{0,2},{1,3},{2,0},{3,1},{4,6},{5,7},{6,4},{7,5},{8,10},{9,11},{10,... | collective-permute-start | bytes 196616 | tf_op jit(solution)/shard_map/ppermute | solution.py:87
  13.8 4.8 %collective-permute-start.9 = (bf16[128,256]{1,0:T(8,128)(2,1)S(1)}, bf16[128,256]{1,0:T(8,128)(2,1)S(1)}, u32[]{:S(2)}, u32[]{:S(2)}) collective-permute-start(bf16[128,256]{1,0:T(8,128)(2,1)S(1)} %get-tuple-element.39), channel_id=1, source_target_pairs={{0,1},{1,0},{2,3},{3,2},{4,5},{5,4},{6,7},{7,6},{8,9},{9,8},{10,11... | collective-permute-start | bytes 196616 | tf_op jit(solution)/shard_map/ppermute | solution.py:87
  19.0 1.7 %collective-permute-start.10 = (bf16[256,256]{1,0:T(8,128)(2,1)S(1)}, bf16[256,256]{1,0:T(8,128)(2,1)S(1)}, u32[]{:S(2)}, u32[]{:S(2)}) collective-permute-start(bf16[256,256]{1,0:T(8,128)(2,1)S(1)} %get-tuple-element.42), channel_id=1, source_target_pairs={{0,4},{4,0},{8,12},{12,8},{16,20},{20,16},{24,28},{28,24},{1,5},{5... | collective-permute-start | bytes 393224 | tf_op jit(solution)/shard_map/ppermute | solution.py:87
  20.7 4.8 %collective-permute-start.11 = (bf16[256,256]{1,0:T(8,128)(2,1)S(1)}, bf16[256,256]{1,0:T(8,128)(2,1)S(1)}, u32[]{:S(2)}, u32[]{:S(2)}) collective-permute-start(bf16[256,256]{1,0:T(8,128)(2,1)S(1)} %get-tuple-element.44), channel_id=1, source_target_pairs={{0,24},{1,25},{2,26},{3,27},{4,7},{5,6},{6,5},{7,4},{8,16},{9,17},... | collective-permute-start | bytes 393224 | tf_op jit(solution)/shard_map/ppermute | solution.py:271
  22.7 4.5 %collective-permute-start.12 = (bf16[256,256]{1,0:T(8,128)(2,1)S(1)}, bf16[256,256]{1,0:T(8,128)(2,1)S(1)}, u32[]{:S(2)}, u32[]{:S(2)}) collective-permute-start(bf16[256,256]{1,0:T(8,128)(2,1)S(1)} %get-tuple-element.45), channel_id=1, source_target_pairs={{0,16},{1,17},{2,18},{3,19},{4,6},{5,7},{6,4},{7,5},{8,24},{9,25},... | collective-permute-start | bytes 393224 | tf_op jit(solution)/shard_map/ppermute | solution.py:271
  22.9 4.3 %collective-permute-start.13 = (bf16[256,256]{1,0:T(8,128)(2,1)S(1)}, bf16[256,256]{1,0:T(8,128)(2,1)S(1)}, u32[]{:S(2)}, u32[]{:S(2)}) collective-permute-start(bf16[256,256]{1,0:T(8,128)(2,1)S(1)} %get-tuple-element.46), channel_id=1, source_target_pairs={{0,8},{1,9},{2,10},{3,11},{4,5},{5,4},{6,7},{7,6},{8,0},{9,1},{10,... | collective-permute-start | bytes 393224 | tf_op jit(solution)/shard_map/ppermute | solution.py:271
  27.3 5.9 %collective-permute-start.16 = (bf16[256,256]{1,0:T(8,128)(2,1)S(1)}, bf16[256,256]{1,0:T(8,128)(2,1)S(1)}, u32[]{:S(2)}, u32[]{:S(2)}) collective-permute-start(bf16[256,256]{1,0:T(8,128)(2,1)S(1)} %get-tuple-element.48.refs_0_), channel_id=1, source_target_pairs={{0,2},{1,3},{2,0},{3,1},{4,28},{5,29},{6,30},{7,31},{8,10},{9,11},... | collective-permute-start | bytes 393224 | tf_op jit(solution)/shard_map/ppermute | solution.py:271
  28.2 7.5 %collective-permute-start.15 = (bf16[256,256]{1,0:T(8,128)(2,1)S(1)}, bf16[256,256]{1,0:T(8,128)(2,1)S(1)}, u32[]{:S(2)}, u32[]{:S(2)}) collective-permute-start(bf16[256,256]{1,0:T(8,128)(2,1)S(1)} %get-tuple-element.48.refs_0_), channel_id=1, source_target_pairs={{0,1},{1,0},{2,3},{3,2},{4,20},{5,21},{6,22},{7,23},{8,9},{9,8},{1... | collective-permute-start | bytes 393224 | tf_op jit(solution)/shard_map/ppermute | solution.py:271
  28.3 7.4 %collective-permute-start.14 = (bf16[256,256]{1,0:T(8,128)(2,1)S(1)}, bf16[256,256]{1,0:T(8,128)(2,1)S(1)}, u32[]{:S(2)}, u32[]{:S(2)}) collective-permute-start(bf16[256,256]{1,0:T(8,128)(2,1)S(1)} %get-tuple-element.48.refs_0_), channel_id=1, source_target_pairs={{0,2},{1,3},{2,0},{3,1},{4,12},{5,13},{6,14},{7,15},{8,10},{9,11},... | collective-permute-start | bytes 393224 | tf_op jit(solution)/shard_map/ppermute | solution.py:271
  35.8 7.9 %collective-permute-start.17 = (bf16[256,256]{1,0:T(8,128)(2,1)S(1)}, bf16[256,256]{1,0:T(8,128)(2,1)S(1)}, u32[]{:S(2)}, u32[]{:S(2)}) collective-permute-start(bf16[256,256]{1,0:T(8,128)(2,1)S(1)} %place.1.whole_ref), channel_id=1, source_target_pairs={{0,4},{4,0},{8,12},{12,8},{16,20},{20,16},{24,28},{28,24},{1,5},{5... | collective-permute-start | bytes 393224 | tf_op jit(solution)/shard_map/ppermute | solution.py:87

commit v9 on v4

--- a/solution.py
+++ b/solution.py
@@ -93,9 +93,7 @@
     return terms[0]
 
 
-def dense_kernel(
-    n_part, weight_ref, cot_ref, placing_ref, *refs
-):
+def dense_kernel(n_part, weight_ref, cot_ref, placing_ref, *refs):
     part_refs, (same_ref, kept_ref, sent_ref, term) = refs[:n_part], refs[n_part:]
     core = lax.axis_index("section") & 1
     agg_b = tree_sum([ref[...].astype(jnp.float32) for ref in part_refs]).astype(jnp.bfloat16)
@@ -133,109 +131,80 @@
     )(weight, cotangent, placing, *parts)
 
 
-def split_kernel(kept_ref, came_ref, own_ref, *refs):
-    out_refs, term = refs[:-1], refs[-1]
-    rep = lax.axis_index("rep")
-    half = kept_ref.shape[0]
-    total = kept_ref[...] + came_ref[came_ref.shape[0] - half :].astype(jnp.float32)
-    term[...] = total.reshape(term.shape)
-    own_ref[...] = term[rep]
+def write_messages(slots, same_ref, came_ref, half, out_refs):
     for ref, j in zip(out_refs, across(len(out_refs) + 1)):
-        ref[...] = term[rep ^ j].astype(jnp.bfloat16)
-
-
-def split(kept, came, n_rep):
-    half, width = kept.shape
-    rows = half // n_rep
-    return pl.pallas_call(
-        split_kernel,
-        out_shape=[jax.ShapeDtypeStruct((rows, width), jnp.float32)]
-        + [jax.ShapeDtypeStruct((rows, width), jnp.bfloat16)] * (n_rep - 1),
-        in_specs=[VMEM] * 2,
-        out_specs=[VMEM] * n_rep,
-        scratch_shapes=[pltpu.VMEM((n_rep, rows, width), jnp.float32)],
-        compiler_params=LIMIT,
-        name="split",
-    )(kept, came)
-
-
-def message_kernel(n_term, slots, same_ref, came_ref, *refs):
-    term_refs, out_refs = refs[:n_term], refs[n_term:]
-    chunk = sum(ref[...].astype(jnp.float32) for ref in term_refs).astype(jnp.bfloat16)
-    for j, ref in zip([0] + across(len(out_refs)), out_refs):
-        ref[:slots] = same_ref[j * slots : (j + 1) * slots]
-        ref[slots : 2 * slots] = came_ref[j * slots : (j + 1) * slots]
-        ref[2 * slots :] = chunk
-
-
-def message(same, came, terms, slots):
-    chips = same.shape[0] // slots
-    rows, width = terms[0].shape
-    return pl.pallas_call(
-        functools.partial(message_kernel, len(terms), slots),
-        out_shape=[jax.ShapeDtypeStruct((2 * slots + rows, width), jnp.bfloat16)] * chips,
-        in_specs=[VMEM] * (2 + len(terms)),
-        out_specs=[VMEM] * chips,
-        compiler_params=LIMIT,
-        name="message",
-    )(same, came, *terms)
-
-
-def chunk_kernel(start, *refs):
-    by_xor = [refs[0]] + [None] * (len(refs) - 2)
-    for ref, j in zip(refs[1:-1], across(len(by_xor))):
-        by_xor[j] = ref
-    total = tree_sum([ref[start:].astype(jnp.float32) for ref in by_xor])
-    refs[-1][...] = total.astype(jnp.bfloat16)
-
-
-def chunk_of(messages, start):
-    rows, width = messages[0].shape
-    return pl.pallas_call(
-        functools.partial(chunk_kernel, start),
-        out_shape=jax.ShapeDtypeStruct((rows - start, width), jnp.bfloat16),
-        in_specs=[VMEM] * len(messages),
+        start = j * slots % same_ref.shape[0]
+        ref[:slots] = same_ref[start : start + slots]
+        ref[slots : 2 * slots] = came_ref[start : start + slots]
+        ref[2 * slots :] = half
+
+
+def sum_halves(half_ref, slots, own_ref, message_refs, counts):
+    by_xor = [own_ref[...].astype(jnp.float32)]
+    by_xor += [ref[2 * slots :].astype(jnp.float32) for ref in message_refs[::-1]]
+    for core in range(2):
+
+        @pl.when(lax.axis_index("section") & 1 == core)
+        def _():
+            half_ref[...] = tree_sum(by_xor[: counts[core]]).astype(jnp.bfloat16)
+
+
+def first_kernel(slots, same_ref, kept_ref, came_ref, half_ref, *out_refs):
+    rows = kept_ref.shape[0]
+    half = kept_ref[...] + came_ref[came_ref.shape[0] - rows :].astype(jnp.float32)
+    half_ref[...] = half.astype(jnp.bfloat16)
+    write_messages(slots, same_ref, came_ref, half_ref[...], out_refs)
+
+
+def second_kernel(slots, counts, many, same_ref, came_ref, own_ref, *refs):
+    message_refs, half_ref, out_refs = refs[:many], refs[many], refs[many + 1 :]
+    sum_halves(half_ref, slots, own_ref, message_refs, counts)
+    write_messages(slots, same_ref, came_ref, half_ref[...], out_refs)
+
+
+def third_kernel(slots, counts, own_ref, *refs):
+    sum_halves(refs[-1], slots, own_ref, refs[:-1], counts)
+
+
+def call_halves(kernel, name, operands, half, slots, many):
+    shapes = [jax.ShapeDtypeStruct(half, jnp.bfloat16)]
+    shapes += [jax.ShapeDtypeStruct((2 * slots + half[0], half[1]), jnp.bfloat16)] * many
+    return pl.pallas_call(
+        kernel,
+        out_shape=shapes,
+        in_specs=[VMEM] * len(operands),
+        out_specs=[VMEM] * len(shapes),
+        compiler_params=LIMIT,
+        name=name,
+    )(*operands)
+
+
+def unpack_kernel(slots, same_ref, came_ref, *refs):
+    many = len(refs) // 2
+    section = lax.axis_index("section")
+    chips = lax.axis_size("section") // 2
+    refs[-1][section] = same_ref[:slots]
+    refs[-1][section ^ 1] = came_ref[:slots]
+    for core in range(2):
+
+        @pl.when(section & 1 == core)
+        def _():
+            for ref, j in zip(refs[core * many : (core + 1) * many], across(many + 1)):
+                if j < chips:
+                    refs[-1][section ^ (2 * j)] = ref[:slots]
+                    refs[-1][section ^ (2 * j + 1)] = ref[slots : 2 * slots]
+
+
+def unpack(same, came, first, second, n_section, slots):
+    width = same.shape[1]
+    return pl.pallas_call(
+        functools.partial(unpack_kernel, slots),
+        out_shape=jax.ShapeDtypeStruct((n_section, slots, width), jnp.bfloat16),
+        in_specs=[VMEM] * (2 + len(first) + len(second)),
         out_specs=VMEM,
         compiler_params=LIMIT,
-        name="chunk",
-    )(*messages)
-
-
-def unpack_kernel(slots, *refs):
-    section = lax.axis_index("section")
-    for j, ref in zip([0] + across(len(refs) - 1), refs[:-1]):
-        refs[-1][section ^ (2 * j)] = ref[:slots]
-        refs[-1][section ^ (2 * j + 1)] = ref[slots : 2 * slots]
-
-
-def unpack(messages, slots):
-    width = messages[0].shape[1]
-    return pl.pallas_call(
-        functools.partial(unpack_kernel, slots),
-        out_shape=jax.ShapeDtypeStruct((2 * len(messages), slots, width), jnp.bfloat16),
-        in_specs=[VMEM] * len(messages),
-        out_specs=VMEM,
-        compiler_params=LIMIT,
         name="unpack",
-    )(*messages)
-
-
-def place_kernel(*refs):
-    rep = lax.axis_index("rep")
-    for j, ref in zip([0] + across(len(refs) - 1), refs[:-1]):
-        refs[-1][rep ^ j] = ref[...]
-
-
-def place(chunks):
-    rows, width = chunks[0].shape
-    return pl.pallas_call(
-        place_kernel,
-        out_shape=jax.ShapeDtypeStruct((len(chunks), rows, width), jnp.bfloat16),
-        in_specs=[VMEM] * len(chunks),
-        out_specs=VMEM,
-        compiler_params=LIMIT,
-        name="place",
-    )(*chunks)
+    )(same, came, *first, *second)
 
 
 def finish_kernel(own_ref, came_ref, out_ref):
@@ -253,6 +222,16 @@
         compiler_params=LIMIT,
         name="finish",
     )(own, came)
+
+
+def swap_by_core(value, first, second):
+    n_section, n_rep = lax.axis_size("section"), lax.axis_size("rep")
+    pairs = []
+    for s in range(n_section):
+        chip, rep = second if s & 1 else first
+        for r in range(n_rep):
+            pairs.append((s * n_rep + r, (s ^ 2 * chip % n_section) * n_rep + (r ^ rep % n_rep)))
+    return lax.ppermute(value, ("section", "rep"), pairs)
 
 
 def gather_blocks(features, axis, ready):
@@ -277,20 +256,32 @@
     wide, own, placing = prepare(adj_tiles[:, 0], features, target, n_section * slots, slots)
     blocks, (wide, own, placing) = gather_blocks(features, "section", (wide, own, placing))
     parts = list(partials(adj_src[:, 0], wide, [own] + blocks[1:]))
-    others, chips = across(n_rep), across(n_section // 2)
+    others = across(n_rep)
     parts = [swap(part, "rep", j) if j else part for part, j in zip(parts, [0] + others)]
-    parts = [parts[0]] + parts[:0:-1]
     same, kept, sent = dense(parts, weight, cotangent, placing)
     came = swap(sent, "section", 1)
-    own, *terms = split(kept, came, n_rep)
-    terms = [own] + [swap(term, "rep", j) for term, j in zip(terms, others)]
-    messages = list(message(same, came, terms, slots))
-    messages = messages[:1] + [swap(m, "section", 2 * j) for m, j in zip(messages[1:], chips)]
-    chunk = chunk_of(messages, 2 * slots)
-    relaid = unpack(messages, slots).reshape(1, 1, n_section, slots, width)
-    half = place([chunk] + [swap(chunk, "rep", j) for j in others]).reshape(width // 2, width)
+    chips = n_section // 2
+    steps = across(max(n_rep, chips))
+    half_shape = (width // 2, width)
+    half, *first = call_halves(
+        functools.partial(first_kernel, slots), "first", [same, kept, came], half_shape, slots, len(steps)
+    )
+    first = [swap_by_core(m, (j, 0), (0, j)) for m, j in zip(first, steps)]
+    half, *second = call_halves(
+        functools.partial(second_kernel, slots, (chips, n_rep), len(steps)),
+        "second",
+        [same, came, half, *first],
+        half_shape,
+        slots,
+        len(steps),
+    )
+    second = [swap_by_core(m, (0, j), (j, 0)) for m, j in zip(second, steps)]
+    (half,) = call_halves(
+        functools.partial(third_kernel, slots, (n_rep, chips)), "third", [half, *second], half_shape, slots, 0
+    )
+    relaid = unpack(same, came, first, second, n_section, slots)
     weight_grad = finish(half, swap(half, "section", 1))
-    return (relaid, weight_grad.reshape(width, width))
+    return (relaid.reshape(1, 1, n_section, slots, width), weight_grad.reshape(width, width))
 
 
 def solution(mesh):

time: 47 us -> 41.4 us (0.88)
  starting transfers between devices: 21.6 us -> 18 us
  waiting for transfers between devices: 18.9 us -> 16.7 us
    ppermute x21 -> x12, starting transfers between devices: 21.6 us -> 10 us  [swap(): lax.ppermute(value, axis, [(i, i ^ j) for i in range(lax.axis_size(axis))])]
    ppermute x21 -> x12, waiting for transfers between devices: 18.9 us -> 9.2 us  [swap(): lax.ppermute(value, axis, [(i, i ^ j) for i in range(lax.axis_size(axis))])]
    ppermute x0 -> x6, starting transfers between devices: none -> 8.01 us  [swap_by_core(): return lax.ppermute(value, ('section', 'rep'), pairs)]
    ppermute x0 -> x6, waiting for transfers between devices: none -> 7.5 us  [swap_by_core(): return lax.ppermute(value, ('section', 'rep'), pairs)]
  transfers between devices with their start and end apart: 21 -> 18, of which waited for: 16 -> 14; matrix products, arithmetic and copies ran while one was open for 0% -> 0% of each run, Pallas kernels for 2% -> 2%
where the time goes in v9:
time: 41.4 us; the launch traced here: 41.1 us
  starting transfers between devices  18 us (43%)
  waiting for transfers between devices  16.7 us (40%)
  Pallas kernels  3.13 us (8%)
  local copies, waits for them, and re-layouts  2.55 us (6%)
  between operations  0.72 us (2%)
    ppermute x12, starting transfers between devices, swap(): lax.ppermute(value, axis, [(i, i ^ j) for i in range(lax.axis_size(axis))])  10 us
    ppermute x12, waiting for transfers between devices, swap(): lax.ppermute(value, axis, [(i, i ^ j) for i in range(lax.axis_size(axis))])  9.2 us
    ppermute x6, starting transfers between devices, swap_by_core(): return lax.ppermute(value, ('section', 'rep'), pairs)  8.01 us
    ppermute x6, waiting for transfers between devices, swap_by_core(): return lax.ppermute(value, ('section', 'rep'), pairs)  7.5 us
    unnamed x12, local copies, waits for them, and re-layouts  2.55 us
    pallas_call x1, Pallas kernels, partials(): pl.pallas_call(functools.partial(partials_kernel, len(blocks)), out_shape...  0.91 us
  transfers between devices with their start and end apart: 18, of which 14 were waited for; matrix products, arithmetic and copies ran while one was open for 0% of the time, Pallas kernels for 2%

profile of v9, /device:TPU:0, one launch (start us, length us, event | category | flops | bytes accessed | tf_op | source)
XLA Modules:
  0.0 41.1 jit_solution(17869901550072061061)
XLA Ops:
  0.6 5.1 %collective-permute-start.2 = (bf16[128,256]{1,0:T(8,128)(2,1)}, bf16[128,256]{1,0:T(8,128)(2,1)S(1)}, u32[]{:S(2)}, u32[]{:S(2)}) collective-permute-start(bf16[128,256]{1,0:T(8,128)(2,1)} %own_ref.1), channel_id=1, source_target_pairs={{0,24},{4,28},{8,16},{12,20},{16,8},{20,12},{24,0},{28,4},{1,25},{... | collective-permute-start | bytes 196616 | tf_op jit(solution)/shard_map/ppermute | solution.py:87
  5.7 0.0 collective-permute-start.1
  5.7 0.6 %collective-permute-start = (bf16[128,256]{1,0:T(8,128)(2,1)}, bf16[128,256]{1,0:T(8,128)(2,1)S(1)}, u32[]{:S(2)}, u32[]{:S(2)}) collective-permute-start(bf16[128,256]{1,0:T(8,128)(2,1)} %own_ref.1), channel_id=1, source_target_pairs={{0,8},{4,12},{8,0},{12,4},{16,24},{20,28},{24,16},{28,20},{1,9},{5... | collective-permute-start | bytes 196616 | tf_op jit(solution)/shard_map/ppermute | solution.py:87
  6.4 0.0 collective-permute-start.3
  6.4 0.7 %copy-done.5 = s32[128,1]{0,1:T(1,128)S(1)} copy-done((s32[128,1]{0,1:T(1,128)S(1)}, s32[128,1]{0,1:T(1,128)}, u32[]{:S(2)}) %copy-start.5) | copy-done | bytes 536
  7.0 1.0 %copy-done = bf16[4,1,4,128,128]{4,3,2,1,0:T(8,128)(2,1)S(1)} copy-done((bf16[4,1,4,128,128]{4,3,2,1,0:T(8,128)(2,1)S(1)}, bf16[4,1,4,128,128]{4,3,2,1,0:T(8,128)(2,1)}, u32[]{:S(2)}) %copy-start) | copy-done | bytes 524312
  8.1 0.8 %copy-done.2 = bf16[128,256]{1,0:T(8,128)(2,1)S(1)} copy-done((bf16[128,256]{1,0:T(8,128)(2,1)S(1)}, bf16[128,256]{1,0:T(8,128)(2,1)}, u32[]{:S(2)}) %copy-start.2) | copy-done | bytes 65560
  8.9 0.2 prepare.1
  9.2 0.0 collective-permute-done.2.refs_6_
  9.2 2.4 %collective-permute-done.1.refs_4_ = bf16[128,256]{1,0:T(8,128)(2,1)S(1)} collective-permute-done((bf16[128,256]{1,0:T(8,128)(2,1)}, bf16[128,256]{1,0:T(8,128)(2,1)S(1)}, u32[]{:S(2)}, u32[]{:S(2)}) %collective-permute-start.1) | collective-permute-done | bytes 65568 | tf_op jit(solution)/shard_map/ppermute | solution.py:87
  11.6 0.0 collective-permute-done.refs_2_
  11.6 0.0 collective-permute-start.4
  11.6 0.5 %collective-permute-start.5 = (bf16[128,256]{1,0:T(8,128)(2,1)S(1)}, bf16[128,256]{1,0:T(8,128)(2,1)S(1)}, u32[]{:S(2)}, u32[]{:S(2)}) collective-permute-start(bf16[128,256]{1,0:T(8,128)(2,1)S(1)} %collective-permute-done.1.refs_4_), channel_id=1, source_target_pairs={{0,4},{4,0},{8,12},{12,8},{16,20},{20,16},{24,28},{28,24},{1,5},{5... | collective-permute-start | bytes 196616 | tf_op jit(solution)/shard_map/ppermute | solution.py:87
  12.1 0.1 collective-permute-start.6
  12.1 0.0 collective-permute-done.3.refs_1_
  12.1 0.7 %collective-permute-done.4.refs_3_ = bf16[128,256]{1,0:T(8,128)(2,1)S(1)} collective-permute-done((bf16[128,256]{1,0:T(8,128)(2,1)S(1)}, bf16[128,256]{1,0:T(8,128)(2,1)S(1)}, u32[]{:S(2)}, u32[]{:S(2)}) %collective-permute-start.4) | collective-permute-done | bytes 65568 | tf_op jit(solution)/shard_map/ppermute | solution.py:87
  12.8 0.2 collective-permute-done.5.refs_5_
  13.0 0.4 collective-permute-done.6.refs_7_
  13.3 0.0 copy-done.4
  13.3 0.9 %partials.1 = (bf16[128,256]{1,0:T(8,128)(2,1)S(1)}, bf16[128,256]{1,0:T(8,128)(2,1)S(1)}, bf16[128,256]{1,0:T(8,128)(2,1)S(1)}, bf16[128,256]{1,0:T(8,128)(2,1)S(1)}) custom-call(s32[4,4]{1,0:T(4,128)S(1)} %bitcast.6, bf16[4,128,512]{2,1,0:T(8,128)(2,1)S(1)} %get-tuple-element.30.wide_ref, bf16[128,256]{1,0:T(8,128)(2,1)S(1)} %get-tuple-element.31.refs_0_, ...), custom_call_target="tpu_custom_call" | custom-call | tf_op jit(solution)/shard_map/partials/pallas_call | solution.py:75
  14.3 2.5 %collective-permute-start.7 = (bf16[128,256]{1,0:T(8,128)(2,1)S(1)}, bf16[128,256]{1,0:T(8,128)(2,1)S(1)}, u32[]{:S(2)}, u32[]{:S(2)}) collective-permute-start(bf16[128,256]{1,0:T(8,128)(2,1)S(1)} %get-tuple-element.36), channel_id=1, source_target_pairs={{0,3},{1,2},{2,1},{3,0},{4,7},{5,6},{6,5},{7,4},{8,11},{9,10},{10,... | collective-permute-start | bytes 196616 | tf_op jit(solution)/shard_map/ppermute | solution.py:87
  16.8 0.5 %collective-permute-start.8 = (bf16[128,256]{1,0:T(8,128)(2,1)S(1)}, bf16[128,256]{1,0:T(8,128)(2,1)S(1)}, u32[]{:S(2)}, u32[]{:S(2)}) collective-permute-start(bf16[128,256]{1,0:T(8,128)(2,1)S(1)} %get-tuple-element.37), channel_id=1, source_target_pairs={{0,2},{1,3},{2,0},{3,1},{4,6},{5,7},{6,4},{7,5},{8,10},{9,11},{10,... | collective-permute-start | bytes 196616 | tf_op jit(solution)/shard_map/ppermute | solution.py:87
  17.3 0.5 %collective-permute-start.9 = (bf16[128,256]{1,0:T(8,128)(2,1)S(1)}, bf16[128,256]{1,0:T(8,128)(2,1)S(1)}, u32[]{:S(2)}, u32[]{:S(2)}) collective-permute-start(bf16[128,256]{1,0:T(8,128)(2,1)S(1)} %get-tuple-element.38), channel_id=1, source_target_pairs={{0,1},{1,0},{2,3},{3,2},{4,5},{5,4},{6,7},{7,6},{8,9},{9,8},{10,11... | collective-permute-start | bytes 196616 | tf_op jit(solution)/shard_map/ppermute | solution.py:87
  17.8 1.7 %collective-permute-done.7.refs_1_ = bf16[128,256]{1,0:T(8,128)(2,1)S(1)} collective-permute-done((bf16[128,256]{1,0:T(8,128)(2,1)S(1)}, bf16[128,256]{1,0:T(8,128)(2,1)S(1)}, u32[]{:S(2)}, u32[]{:S(2)}) %collective-permute-start.7) | collective-permute-done | bytes 65568 | tf_op jit(solution)/shard_map/ppermute | solution.py:87
  19.5 1.5 %collective-permute-done.8.refs_2_ = bf16[128,256]{1,0:T(8,128)(2,1)S(1)} collective-permute-done((bf16[128,256]{1,0:T(8,128)(2,1)S(1)}, bf16[128,256]{1,0:T(8,128)(2,1)S(1)}, u32[]{:S(2)}, u32[]{:S(2)}) %collective-permute-start.8) | collective-permute-done | bytes 65568 | tf_op jit(solution)/shard_map/ppermute | solution.py:87
  21.0 0.5 %collective-permute-done.9.refs_3_ = bf16[128,256]{1,0:T(8,128)(2,1)S(1)} collective-permute-done((bf16[128,256]{1,0:T(8,128)(2,1)S(1)}, bf16[128,256]{1,0:T(8,128)(2,1)S(1)}, u32[]{:S(2)}, u32[]{:S(2)}) %collective-permute-start.9) | collective-permute-done | bytes 65568 | tf_op jit(solution)/shard_map/ppermute | solution.py:87
  21.5 0.0 copy-done.1
  21.5 0.0 copy-done.3
  21.5 0.4 %dense.1 = (bf16[128,256]{1,0:T(8,128)(2,1)S(1)}, f32[128,256]{1,0:T(8,128)S(1)}, bf16[256,256]{1,0:T(8,128)(2,1)S(1)}) custom-call(bf16[256,256]{1,0:T(8,128)(2,1)S(1)} %copy-done.1, bf16[128,256]{1,0:T(8,128)(2,1)S(1)} %copy-done.3, bf16[256,128]{1,0:T(8,128)(2,1)S(1)} %get-tuple-element.29.placing_ref, bf16[128,256]{1,0:T(8,128)(2,1)S(1)} %get-tuple-element.35.refs_0_, ...), custom_call_target="tpu_custom_call" | custom-call | tf_op jit(solution)/shard_map/dense/pallas_call | solution.py:119
  22.0 0.1 collective-permute-start.10
  22.1 1.3 %collective-permute-done.10.came_ref = bf16[256,256]{1,0:T(8,128)(2,1)S(1)} collective-permute-done((bf16[256,256]{1,0:T(8,128)(2,1)S(1)}, bf16[256,256]{1,0:T(8,128)(2,1)S(1)}, u32[]{:S(2)}, u32[]{:S(2)}) %collective-permute-start.10) | collective-permute-done | bytes 131104 | tf_op jit(solution)/shard_map/ppermute | solution.py:87
  23.4 2.8 %collective-permute-start.11 = (bf16[192,256]{1,0:T(8,128)(2,1)S(1)}, bf16[192,256]{1,0:T(8,128)(2,1)S(1)}, u32[]{:S(2)}, u32[]{:S(2)}) collective-permute-start(bf16[192,256]{1,0:T(8,128)(2,1)S(1)} %get-tuple-element.42), channel_id=1, source_target_pairs={{0,24},{1,25},{2,26},{3,27},{4,7},{5,6},{6,5},{7,4},{8,16},{9,17},... | collective-permute-start | bytes 294920 | tf_op jit(solution)/shard_map/ppermute | solution.py:234
  26.2 0.0 collective-permute-start.12
  26.2 1.7 %collective-permute-start.13 = (bf16[192,256]{1,0:T(8,128)(2,1)S(1)}, bf16[192,256]{1,0:T(8,128)(2,1)S(1)}, u32[]{:S(2)}, u32[]{:S(2)}) collective-permute-start(bf16[192,256]{1,0:T(8,128)(2,1)S(1)} %get-tuple-element.44), channel_id=1, source_target_pairs={{0,8},{1,9},{2,10},{3,11},{4,5},{5,4},{6,7},{7,6},{8,0},{9,1},{10,... | collective-permute-start | bytes 294920 | tf_op jit(solution)/shard_map/ppermute | solution.py:234
  27.9 2.0 %collective-permute-done.11.refs_0_ = bf16[192,256]{1,0:T(8,128)(2,1)S(1)} collective-permute-done((bf16[192,256]{1,0:T(8,128)(2,1)S(1)}, bf16[192,256]{1,0:T(8,128)(2,1)S(1)}, u32[]{:S(2)}, u32[]{:S(2)}) %collective-permute-start.11) | collective-permute-done | bytes 98336 | tf_op jit(solution)/shard_map/ppermute | solution.py:234
  29.9 2.1 %collective-permute-done.12.refs_1_ = bf16[192,256]{1,0:T(8,128)(2,1)S(1)} collective-permute-done((bf16[192,256]{1,0:T(8,128)(2,1)S(1)}, bf16[192,256]{1,0:T(8,128)(2,1)S(1)}, u32[]{:S(2)}, u32[]{:S(2)}) %collective-permute-start.12) | collective-permute-done | bytes 98336 | tf_op jit(solution)/shard_map/ppermute | solution.py:234
  32.0 0.0 collective-permute-done.13.refs_2_
  32.0 0.1 second.1
  32.1 1.6 %collective-permute-start.14 = (bf16[192,256]{1,0:T(8,128)(2,1)S(1)}, bf16[192,256]{1,0:T(8,128)(2,1)S(1)}, u32[]{:S(2)}, u32[]{:S(2)}) collective-permute-start(bf16[192,256]{1,0:T(8,128)(2,1)S(1)} %get-tuple-element.46), channel_id=1, source_target_pairs={{0,3},{1,2},{2,1},{3,0},{4,28},{5,29},{6,30},{7,31},{8,11},{9,10},... | collective-permute-start | bytes 294920 | tf_op jit(solution)/shard_map/ppermute | solution.py:234
  33.7 0.8 %collective-permute-start.15 = (bf16[192,256]{1,0:T(8,128)(2,1)S(1)}, bf16[192,256]{1,0:T(8,128)(2,1)S(1)}, u32[]{:S(2)}, u32[]{:S(2)}) collective-permute-start(bf16[192,256]{1,0:T(8,128)(2,1)S(1)} %get-tuple-element.47), channel_id=1, source_target_pairs={{0,2},{1,3},{2,0},{3,1},{4,20},{5,21},{6,22},{7,23},{8,10},{9,11},... | collective-permute-start | bytes 294920 | tf_op jit(solution)/shard_map/ppermute | solution.py:234
  34.4 1.2 %collective-permute-start.16 = (bf16[192,256]{1,0:T(8,128)(2,1)S(1)}, bf16[192,256]{1,0:T(8,128)(2,1)S(1)}, u32[]{:S(2)}, u32[]{:S(2)}) collective-permute-start(bf16[192,256]{1,0:T(8,128)(2,1)S(1)} %get-tuple-element.48), channel_id=1, source_target_pairs={{0,1},{1,0},{2,3},{3,2},{4,12},{5,13},{6,14},{7,15},{8,9},{9,8},{1... | collective-permute-start | bytes 294920 | tf_op jit(solution)/shard_map/ppermute | solution.py:234
  35.7 2.1 %collective-permute-done.14.refs_3_.refs_0_ = bf16[192,256]{1,0:T(8,128)(2,1)S(1)} collective-permute-done((bf16[192,256]{1,0:T(8,128)(2,1)S(1)}, bf16[192,256]{1,0:T(8,128)(2,1)S(1)}, u32[]{:S(2)}, u32[]{:S(2)}) %collective-permute-start.14) | collective-permute-done | bytes 98336 | tf_op jit(solution)/shard_map/ppermute | solution.py:234
  37.7 1.0 %collective-permute-done.15.refs_4_.refs_1_ = bf16[192,256]{1,0:T(8,128)(2,1)S(1)} collective-permute-done((bf16[192,256]{1,0:T(8,128)(2,1)S(1)}, bf16[192,256]{1,0:T(8,128)(2,1)S(1)}, u32[]{:S(2)}, u32[]{:S(2)}) %collective-permute-start.15) | collective-permute-done | bytes 98336 | tf_op jit(solution)/shard_map/ppermute | solution.py:234
  38.7 0.3 collective-permute-done.16.refs_5_.refs_2_
  39.1 0.1 collective-permute-start.17
  39.2 0.7 %unpack.1 = bf16[8,32,256]{2,1,0:T(8,128)(2,1)} custom-call(bf16[128,256]{1,0:T(8,128)(2,1)S(1)} %get-tuple-element.39.same_ref, bf16[256,256]{1,0:T(8,128)(2,1)S(1)} %collective-permute-done.10.came_ref, bf16[192,256]{1,0:T(8,128)(2,1)S(1)} %collective-permute-done.11.refs_0_, bf16[192,256]{1,0:T(8,128)(2,1)S(1)} %collective-permute-done.12.refs_1_, ...), custom_call_target="tpu_custom_call" | custom-call | tf_op jit(solution)/shard_map/unpack/pallas_call | solution.py:200
  39.8 0.6 %collective-permute-done.17.came_ref = bf16[128,256]{1,0:T(8,128)(2,1)S(1)} collective-permute-done((bf16[128,256]{1,0:T(8,128)(2,1)S(1)}, bf16[128,256]{1,0:T(8,128)(2,1)S(1)}, u32[]{:S(2)}, u32[]{:S(2)}) %collective-permute-start.17) | collective-permute-done | bytes 65568 | tf_op jit(solution)/shard_map/ppermute | solution.py:87
  40.4 0.7 %finish.1 = f32[2,128,256]{2,1,0:T(8,128)} custom-call(bf16[128,256]{1,0:T(8,128)(2,1)S(1)} %third.1.own_ref, bf16[128,256]{1,0:T(8,128)(2,1)S(1)} %collective-permute-done.17.came_ref), custom_call_target="tpu_custom_call" | custom-call | tf_op jit(solution)/shard_map/finish/pallas_call | solution.py:217
  (8 shorter events, 0.1 us)
Async XLA Ops:
  0.6 8.5 %collective-permute-start.2 = (bf16[128,256]{1,0:T(8,128)(2,1)}, bf16[128,256]{1,0:T(8,128)(2,1)S(1)}, u32[]{:S(2)}, u32[]{:S(2)}) collective-permute-start(bf16[128,256]{1,0:T(8,128)(2,1)} %own_ref.1), channel_id=1, source_target_pairs={{0,24},{4,28},{8,16},{12,20},{16,8},{20,12},{24,0},{28,4},{1,25},{... | collective-permute-start | bytes 196616 | tf_op jit(solution)/shard_map/ppermute | solution.py:87
  5.7 5.8 %collective-permute-start.1 = (bf16[128,256]{1,0:T(8,128)(2,1)}, bf16[128,256]{1,0:T(8,128)(2,1)S(1)}, u32[]{:S(2)}, u32[]{:S(2)}) collective-permute-start(bf16[128,256]{1,0:T(8,128)(2,1)} %own_ref.1), channel_id=1, source_target_pairs={{0,16},{4,20},{8,24},{12,28},{16,0},{20,4},{24,8},{28,12},{1,17},{... | collective-permute-start | bytes 196616 | tf_op jit(solution)/shard_map/ppermute | solution.py:87
  5.7 5.8 %collective-permute-start = (bf16[128,256]{1,0:T(8,128)(2,1)}, bf16[128,256]{1,0:T(8,128)(2,1)S(1)}, u32[]{:S(2)}, u32[]{:S(2)}) collective-permute-start(bf16[128,256]{1,0:T(8,128)(2,1)} %own_ref.1), channel_id=1, source_target_pairs={{0,8},{4,12},{8,0},{12,4},{16,24},{20,28},{24,16},{28,20},{1,9},{5... | collective-permute-start | bytes 196616 | tf_op jit(solution)/shard_map/ppermute | solution.py:87
  6.4 5.8 %collective-permute-start.3 = (bf16[128,256]{1,0:T(8,128)(2,1)}, bf16[128,256]{1,0:T(8,128)(2,1)S(1)}, u32[]{:S(2)}, u32[]{:S(2)}) collective-permute-start(bf16[128,256]{1,0:T(8,128)(2,1)} %own_ref.1), channel_id=1, source_target_pairs={{0,4},{4,0},{8,12},{12,8},{16,20},{20,16},{24,28},{28,24},{1,5},{5... | collective-permute-start | bytes 196616 | tf_op jit(solution)/shard_map/ppermute | solution.py:87
  6.4 0.7 %copy-start.5 = (s32[128,1]{0,1:T(1,128)S(1)}, s32[128,1]{0,1:T(1,128)}, u32[]{:S(2)}) copy-start(s32[128,1]{0,1:T(1,128)} %param.11) | copy-start | bytes 1540
  7.0 1.0 %copy-start = (bf16[4,1,4,128,128]{4,3,2,1,0:T(8,128)(2,1)S(1)}, bf16[4,1,4,128,128]{4,3,2,1,0:T(8,128)(2,1)}, u32[]{:S(2)}) copy-start(bf16[4,1,4,128,128]{4,3,2,1,0:T(8,128)(2,1)} %param.7) | copy-start | bytes 1572868
  8.1 0.8 %copy-start.2 = (bf16[128,256]{1,0:T(8,128)(2,1)S(1)}, bf16[128,256]{1,0:T(8,128)(2,1)}, u32[]{:S(2)}) copy-start(bf16[128,256]{1,0:T(8,128)(2,1)} %own_ref.1) | copy-start | bytes 196612
  11.6 1.8 %copy-start.4 = (s32[4,1,4]{2,1,0:T(1,128)S(1)}, s32[4,1,4]{2,1,0:T(1,128)}, u32[]{:S(2)}) copy-start(s32[4,1,4]{2,1,0:T(1,128)} %param.8) | copy-start | bytes 196
  11.6 1.3 %collective-permute-start.4 = (bf16[128,256]{1,0:T(8,128)(2,1)S(1)}, bf16[128,256]{1,0:T(8,128)(2,1)S(1)}, u32[]{:S(2)}, u32[]{:S(2)}) collective-permute-start(bf16[128,256]{1,0:T(8,128)(2,1)S(1)} %collective-permute-done.refs_2_), channel_id=1, source_target_pairs={{0,4},{4,0},{8,12},{12,8},{16,20},{20,16},{24,28},{28,24},{1,5},{5... | collective-permute-start | bytes 196616 | tf_op jit(solution)/shard_map/ppermute | solution.py:87
  11.6 1.4 %collective-permute-start.5 = (bf16[128,256]{1,0:T(8,128)(2,1)S(1)}, bf16[128,256]{1,0:T(8,128)(2,1)S(1)}, u32[]{:S(2)}, u32[]{:S(2)}) collective-permute-start(bf16[128,256]{1,0:T(8,128)(2,1)S(1)} %collective-permute-done.1.refs_4_), channel_id=1, source_target_pairs={{0,4},{4,0},{8,12},{12,8},{16,20},{20,16},{24,28},{28,24},{1,5},{5... | collective-permute-start | bytes 196616 | tf_op jit(solution)/shard_map/ppermute | solution.py:87
  12.1 1.3 %collective-permute-start.6 = (bf16[128,256]{1,0:T(8,128)(2,1)S(1)}, bf16[128,256]{1,0:T(8,128)(2,1)S(1)}, u32[]{:S(2)}, u32[]{:S(2)}) collective-permute-start(bf16[128,256]{1,0:T(8,128)(2,1)S(1)} %collective-permute-done.2.refs_6_), channel_id=1, source_target_pairs={{0,4},{4,0},{8,12},{12,8},{16,20},{20,16},{24,28},{28,24},{1,5},{5... | collective-permute-start | bytes 196616 | tf_op jit(solution)/shard_map/ppermute | solution.py:87
  13.3 8.2 %copy-start.1 = (bf16[256,256]{1,0:T(8,128)(2,1)S(1)}, bf16[256,256]{1,0:T(8,128)(2,1)}, u32[]{:S(2)}) copy-start(bf16[256,256]{1,0:T(8,128)(2,1)} %weight_ref.1) | copy-start | bytes 393220
  13.3 8.2 %copy-start.3 = (bf16[128,256]{1,0:T(8,128)(2,1)S(1)}, bf16[128,256]{1,0:T(8,128)(2,1)}, u32[]{:S(2)}) copy-start(bf16[128,256]{1,0:T(8,128)(2,1)} %cot_ref.1) | copy-start | bytes 196612
  14.3 5.3 %collective-permute-start.7 = (bf16[128,256]{1,0:T(8,128)(2,1)S(1)}, bf16[128,256]{1,0:T(8,128)(2,1)S(1)}, u32[]{:S(2)}, u32[]{:S(2)}) collective-permute-start(bf16[128,256]{1,0:T(8,128)(2,1)S(1)} %get-tuple-element.36), channel_id=1, source_target_pairs={{0,3},{1,2},{2,1},{3,0},{4,7},{5,6},{6,5},{7,4},{8,11},{9,10},{10,... | collective-permute-start | bytes 196616 | tf_op jit(solution)/shard_map/ppermute | solution.py:87
  16.8 4.3 %collective-permute-start.8 = (bf16[128,256]{1,0:T(8,128)(2,1)S(1)}, bf16[128,256]{1,0:T(8,128)(2,1)S(1)}, u32[]{:S(2)}, u32[]{:S(2)}) collective-permute-start(bf16[128,256]{1,0:T(8,128)(2,1)S(1)} %get-tuple-element.37), channel_id=1, source_target_pairs={{0,2},{1,3},{2,0},{3,1},{4,6},{5,7},{6,4},{7,5},{8,10},{9,11},{10,... | collective-permute-start | bytes 196616 | tf_op jit(solution)/shard_map/ppermute | solution.py:87
  17.3 4.3 %collective-permute-start.9 = (bf16[128,256]{1,0:T(8,128)(2,1)S(1)}, bf16[128,256]{1,0:T(8,128)(2,1)S(1)}, u32[]{:S(2)}, u32[]{:S(2)}) collective-permute-start(bf16[128,256]{1,0:T(8,128)(2,1)S(1)} %get-tuple-element.38), channel_id=1, source_target_pairs={{0,1},{1,0},{2,3},{3,2},{4,5},{5,4},{6,7},{7,6},{8,9},{9,8},{10,11... | collective-permute-start | bytes 196616 | tf_op jit(solution)/shard_map/ppermute | solution.py:87
  22.0 1.4 %collective-permute-start.10 = (bf16[256,256]{1,0:T(8,128)(2,1)S(1)}, bf16[256,256]{1,0:T(8,128)(2,1)S(1)}, u32[]{:S(2)}, u32[]{:S(2)}) collective-permute-start(bf16[256,256]{1,0:T(8,128)(2,1)S(1)} %get-tuple-element.40), channel_id=1, source_target_pairs={{0,4},{4,0},{8,12},{12,8},{16,20},{20,16},{24,28},{28,24},{1,5},{5... | collective-permute-start | bytes 393224 | tf_op jit(solution)/shard_map/ppermute | solution.py:87
  23.4 6.5 %collective-permute-start.11 = (bf16[192,256]{1,0:T(8,128)(2,1)S(1)}, bf16[192,256]{1,0:T(8,128)(2,1)S(1)}, u32[]{:S(2)}, u32[]{:S(2)}) collective-permute-start(bf16[192,256]{1,0:T(8,128)(2,1)S(1)} %get-tuple-element.42), channel_id=1, source_target_pairs={{0,24},{1,25},{2,26},{3,27},{4,7},{5,6},{6,5},{7,4},{8,16},{9,17},... | collective-permute-start | bytes 294920 | tf_op jit(solution)/shard_map/ppermute | solution.py:234
  26.2 5.8 %collective-permute-start.12 = (bf16[192,256]{1,0:T(8,128)(2,1)S(1)}, bf16[192,256]{1,0:T(8,128)(2,1)S(1)}, u32[]{:S(2)}, u32[]{:S(2)}) collective-permute-start(bf16[192,256]{1,0:T(8,128)(2,1)S(1)} %get-tuple-element.43), channel_id=1, source_target_pairs={{0,16},{1,17},{2,18},{3,19},{4,6},{5,7},{6,4},{7,5},{8,24},{9,25},... | collective-permute-start | bytes 294920 | tf_op jit(solution)/shard_map/ppermute | solution.py:234
  26.2 5.8 %collective-permute-start.13 = (bf16[192,256]{1,0:T(8,128)(2,1)S(1)}, bf16[192,256]{1,0:T(8,128)(2,1)S(1)}, u32[]{:S(2)}, u32[]{:S(2)}) collective-permute-start(bf16[192,256]{1,0:T(8,128)(2,1)S(1)} %get-tuple-element.44), channel_id=1, source_target_pairs={{0,8},{1,9},{2,10},{3,11},{4,5},{5,4},{6,7},{7,6},{8,0},{9,1},{10,... | collective-permute-start | bytes 294920 | tf_op jit(solution)/shard_map/ppermute | solution.py:234
  32.1 5.6 %collective-permute-start.14 = (bf16[192,256]{1,0:T(8,128)(2,1)S(1)}, bf16[192,256]{1,0:T(8,128)(2,1)S(1)}, u32[]{:S(2)}, u32[]{:S(2)}) collective-permute-start(bf16[192,256]{1,0:T(8,128)(2,1)S(1)} %get-tuple-element.46), channel_id=1, source_target_pairs={{0,3},{1,2},{2,1},{3,0},{4,28},{5,29},{6,30},{7,31},{8,11},{9,10},... | collective-permute-start | bytes 294920 | tf_op jit(solution)/shard_map/ppermute | solution.py:234
  33.7 5.1 %collective-permute-start.15 = (bf16[192,256]{1,0:T(8,128)(2,1)S(1)}, bf16[192,256]{1,0:T(8,128)(2,1)S(1)}, u32[]{:S(2)}, u32[]{:S(2)}) collective-permute-start(bf16[192,256]{1,0:T(8,128)(2,1)S(1)} %get-tuple-element.47), channel_id=1, source_target_pairs={{0,2},{1,3},{2,0},{3,1},{4,20},{5,21},{6,22},{7,23},{8,10},{9,11},... | collective-permute-start | bytes 294920 | tf_op jit(solution)/shard_map/ppermute | solution.py:234
  34.4 4.6 %collective-permute-start.16 = (bf16[192,256]{1,0:T(8,128)(2,1)S(1)}, bf16[192,256]{1,0:T(8,128)(2,1)S(1)}, u32[]{:S(2)}, u32[]{:S(2)}) collective-permute-start(bf16[192,256]{1,0:T(8,128)(2,1)S(1)} %get-tuple-element.48), channel_id=1, source_target_pairs={{0,1},{1,0},{2,3},{3,2},{4,12},{5,13},{6,14},{7,15},{8,9},{9,8},{1... | collective-permute-start | bytes 294920 | tf_op jit(solution)/shard_map/ppermute | solution.py:234
  39.1 1.3 %collective-permute-start.17 = (bf16[128,256]{1,0:T(8,128)(2,1)S(1)}, bf16[128,256]{1,0:T(8,128)(2,1)S(1)}, u32[]{:S(2)}, u32[]{:S(2)}) collective-permute-start(bf16[128,256]{1,0:T(8,128)(2,1)S(1)} %third.1.own_ref), channel_id=1, source_target_pairs={{0,4},{4,0},{8,12},{12,8},{16,20},{20,16},{24,28},{28,24},{1,5},{5... | collective-permute-start | bytes 196616 | tf_op jit(solution)/shard_map/ppermute | solution.py:87

commit v10 on v9

--- a/solution.py
+++ b/solution.py
@@ -9,11 +9,16 @@
 
 VMEM = pl.BlockSpec(memory_space=pltpu.VMEM)
 LIMIT = pltpu.CompilerParams(vmem_limit_bytes=32 * 1024 * 1024)
-SMEM = pl.BlockSpec(memory_space=pltpu.SMEM)
+HBM = pl.BlockSpec(memory_space=pltpu.HBM)
 
 
 def across(n):
     return list(range(n - 1, 0, -1))
+
+
+def turned(n):
+    first, *rest = across(n)
+    return [first] + rest[::-1]
 
 
 def prepare_kernel(slots, tiles_ref, own_ref, target_ref, wide_ref, held_ref, placing_ref):
@@ -61,8 +66,9 @@
     section, rep = lax.axis_index("section"), lax.axis_index("rep")
     for j in range(count):
         held[j] = block_refs[j][...]
-    for j, out_ref in zip([0] + across(len(out_refs)), out_refs):
-        g = rep ^ j
+    steps = zip([0] + across(len(out_refs)), [0] + turned(len(out_refs)))
+    for (j, j_turned), out_ref in zip(steps, out_refs):
+        g = rep ^ jnp.where(section & 1 == 0, j, j_turned)
         right = jnp.concatenate([held[src_ref[g, k] ^ section] for k in range(depth)], axis=0)
         out_ref[...] = jnp.dot(wide_ref[g], right, preferred_element_type=jnp.float32).astype(
             jnp.bfloat16
@@ -75,7 +81,7 @@
     return pl.pallas_call(
         functools.partial(partials_kernel, len(blocks)),
         out_shape=[jax.ShapeDtypeStruct((tile, width), jnp.bfloat16)] * many,
-        in_specs=[SMEM] + [VMEM] * (1 + len(blocks)),
+        in_specs=[VMEM] * (2 + len(blocks)),
         out_specs=[VMEM] * many,
         scratch_shapes=[pltpu.VMEM((len(blocks), tile, width), jnp.bfloat16)],
         compiler_params=LIMIT,
@@ -179,32 +185,40 @@
     )(*operands)
 
 
-def unpack_kernel(slots, same_ref, came_ref, *refs):
-    many = len(refs) // 2
+def store_kernel(core, slots, same_ref, came_ref, *refs):
+    message_refs, (out_ref, rows, sem) = refs[:-3], refs[-3:]
     section = lax.axis_index("section")
     chips = lax.axis_size("section") // 2
-    refs[-1][section] = same_ref[:slots]
-    refs[-1][section ^ 1] = came_ref[:slots]
-    for core in range(2):
-
-        @pl.when(section & 1 == core)
-        def _():
-            for ref, j in zip(refs[core * many : (core + 1) * many], across(many + 1)):
-                if j < chips:
-                    refs[-1][section ^ (2 * j)] = ref[:slots]
-                    refs[-1][section ^ (2 * j + 1)] = ref[slots : 2 * slots]
-
-
-def unpack(same, came, first, second, n_section, slots):
-    width = same.shape[1]
-    return pl.pallas_call(
-        functools.partial(unpack_kernel, slots),
-        out_shape=jax.ShapeDtypeStruct((n_section, slots, width), jnp.bfloat16),
-        in_specs=[VMEM] * (2 + len(first) + len(second)),
-        out_specs=VMEM,
-        compiler_params=LIMIT,
-        name="unpack",
-    )(same, came, *first, *second)
+
+    @pl.when(section & 1 == core)
+    def _():
+        rows[section] = same_ref[:slots]
+        rows[section ^ 1] = came_ref[:slots]
+        for ref, j in zip(message_refs, across(len(message_refs) + 1)):
+            if j < chips:
+                rows[section ^ (2 * j)] = ref[:slots]
+                rows[section ^ (2 * j + 1)] = ref[slots : 2 * slots]
+        copy = pltpu.make_async_copy(rows, out_ref, sem)
+        copy.start()
+        copy.wait()
+
+
+def store(core, same, came, messages, n_section, slots, base=None):
+    shape = (n_section, slots, same.shape[1])
+    operands = [same, came, *messages]
+    kernel, first, specs = functools.partial(store_kernel, core, slots), [], []
+    if base is not None:
+        kernel, first, specs = lambda _, *refs: store_kernel(core, slots, *refs), [base], [HBM]
+    return pl.pallas_call(
+        kernel,
+        out_shape=jax.ShapeDtypeStruct(shape, jnp.bfloat16),
+        in_specs=specs + [VMEM] * len(operands),
+        out_specs=HBM,
+        scratch_shapes=[pltpu.VMEM(shape, jnp.bfloat16), pltpu.SemaphoreType.DMA],
+        input_output_aliases={0: 0} if first else {},
+        compiler_params=LIMIT,
+        name="store",
+    )(*first, *operands)
 
 
 def finish_kernel(own_ref, came_ref, out_ref):
@@ -257,7 +271,8 @@
     blocks, (wide, own, placing) = gather_blocks(features, "section", (wide, own, placing))
     parts = list(partials(adj_src[:, 0], wide, [own] + blocks[1:]))
     others = across(n_rep)
-    parts = [swap(part, "rep", j) if j else part for part, j in zip(parts, [0] + others)]
+    steps = zip(others, turned(n_rep))
+    parts = parts[:1] + [swap_by_core(p, (0, j), (0, k)) for p, (j, k) in zip(parts[1:], steps)]
     same, kept, sent = dense(parts, weight, cotangent, placing)
     came = swap(sent, "section", 1)
     chips = n_section // 2
@@ -267,6 +282,7 @@
         functools.partial(first_kernel, slots), "first", [same, kept, came], half_shape, slots, len(steps)
     )
     first = [swap_by_core(m, (j, 0), (0, j)) for m, j in zip(first, steps)]
+    relaid = store(0, same, came, first, n_section, slots)
     half, *second = call_halves(
         functools.partial(second_kernel, slots, (chips, n_rep), len(steps)),
         "second",
@@ -279,7 +295,8 @@
     (half,) = call_halves(
         functools.partial(third_kernel, slots, (n_rep, chips)), "third", [half, *second], half_shape, slots, 0
     )
-    relaid = unpack(same, came, first, second, n_section, slots)
+    relaid = store(1, same, came, second, n_section, slots, relaid)
+    half, relaid = lax.optimization_barrier((half, relaid))
     weight_grad = finish(half, swap(half, "section", 1))
     return (relaid.reshape(1, 1, n_section, slots, width), weight_grad.reshape(width, width))
 

time: 41.4 us -> 41.2 us (level)
  Pallas kernels: 3.13 us -> 2.65 us
    ppermute x6 -> x9, starting transfers between devices: 8.01 us -> 11.6 us  [swap_by_core(): return lax.ppermute(value, ('section', 'rep'), pairs)]
    ppermute x12 -> x9, starting transfers between devices: 10 us -> 6.48 us  [swap(): lax.ppermute(value, axis, [(i, i ^ j) for i in range(lax.axis_size(axis))])]
    ppermute x6 -> x9, waiting for transfers between devices: 7.5 us -> 10.8 us  [swap_by_core(): return lax.ppermute(value, ('section', 'rep'), pairs)]
    ppermute x12 -> x9, waiting for transfers between devices: 9.2 us -> 6.16 us  [swap(): lax.ppermute(value, axis, [(i, i ^ j) for i in range(lax.axis_size(axis))])]
    pallas_call x1, Pallas kernels: 0.91 us -> 0.43 us  [partials(): pl.pallas_call(functools.partial(partials_kernel, len(blocks)), out_shape...]
where the time goes in v10:
time: 41.2 us; the launch traced here: 41 us
  starting transfers between devices  18 us (44%)
  waiting for transfers between devices  17 us (41%)
  Pallas kernels  2.65 us (6%)
  local copies, waits for them, and re-layouts  2.55 us (6%)
  between operations  0.73 us (2%)
    ppermute x9, starting transfers between devices, swap_by_core(): return lax.ppermute(value, ('section', 'rep'), pairs)  11.6 us
    ppermute x9, waiting for transfers between devices, swap_by_core(): return lax.ppermute(value, ('section', 'rep'), pairs)  10.8 us
    ppermute x9, starting transfers between devices, swap(): lax.ppermute(value, axis, [(i, i ^ j) for i in range(lax.axis_size(axis))])  6.48 us
    ppermute x9, waiting for transfers between devices, swap(): lax.ppermute(value, axis, [(i, i ^ j) for i in range(lax.axis_size(axis))])  6.16 us
    unnamed x12, local copies, waits for them, and re-layouts  2.55 us
  transfers between devices with their start and end apart: 18, of which 14 were waited for; matrix products, arithmetic and copies ran while one was open for 0% of the time, Pallas kernels for 2%

profile of v10, /device:TPU:0, one launch (start us, length us, event | category | flops | bytes accessed | tf_op | source)
XLA Modules:
  0.0 41.0 jit_solution(13643632017571705608)
XLA Ops:
  0.6 5.1 %collective-permute-start.2 = (bf16[128,256]{1,0:T(8,128)(2,1)}, bf16[128,256]{1,0:T(8,128)(2,1)S(1)}, u32[]{:S(2)}, u32[]{:S(2)}) collective-permute-start(bf16[128,256]{1,0:T(8,128)(2,1)} %own_ref.1), channel_id=1, source_target_pairs={{0,24},{4,28},{8,16},{12,20},{16,8},{20,12},{24,0},{28,4},{1,25},{... | collective-permute-start | bytes 196616 | tf_op jit(solution)/shard_map/ppermute | solution.py:93
  5.7 0.0 collective-permute-start.1
  5.7 0.6 %collective-permute-start = (bf16[128,256]{1,0:T(8,128)(2,1)}, bf16[128,256]{1,0:T(8,128)(2,1)S(1)}, u32[]{:S(2)}, u32[]{:S(2)}) collective-permute-start(bf16[128,256]{1,0:T(8,128)(2,1)} %own_ref.1), channel_id=1, source_target_pairs={{0,8},{4,12},{8,0},{12,4},{16,24},{20,28},{24,16},{28,20},{1,9},{5... | collective-permute-start | bytes 196616 | tf_op jit(solution)/shard_map/ppermute | solution.py:93
  6.4 0.0 collective-permute-start.3
  6.4 0.7 %copy-done.5 = s32[128,1]{0,1:T(1,128)S(1)} copy-done((s32[128,1]{0,1:T(1,128)S(1)}, s32[128,1]{0,1:T(1,128)}, u32[]{:S(2)}) %copy-start.5) | copy-done | bytes 536
  7.0 1.0 %copy-done = bf16[4,1,4,128,128]{4,3,2,1,0:T(8,128)(2,1)S(1)} copy-done((bf16[4,1,4,128,128]{4,3,2,1,0:T(8,128)(2,1)S(1)}, bf16[4,1,4,128,128]{4,3,2,1,0:T(8,128)(2,1)}, u32[]{:S(2)}) %copy-start) | copy-done | bytes 524312
  8.1 0.8 %copy-done.2 = bf16[128,256]{1,0:T(8,128)(2,1)S(1)} copy-done((bf16[128,256]{1,0:T(8,128)(2,1)S(1)}, bf16[128,256]{1,0:T(8,128)(2,1)}, u32[]{:S(2)}) %copy-start.2) | copy-done | bytes 65560
  8.9 0.2 prepare.1
  9.2 0.0 collective-permute-done.2.refs_6_
  9.2 2.4 %collective-permute-done.1.refs_4_ = bf16[128,256]{1,0:T(8,128)(2,1)S(1)} collective-permute-done((bf16[128,256]{1,0:T(8,128)(2,1)}, bf16[128,256]{1,0:T(8,128)(2,1)S(1)}, u32[]{:S(2)}, u32[]{:S(2)}) %collective-permute-start.1) | collective-permute-done | bytes 65568 | tf_op jit(solution)/shard_map/ppermute | solution.py:93
  11.6 0.0 collective-permute-done.refs_2_
  11.6 0.0 collective-permute-start.4
  11.6 0.5 %collective-permute-start.5 = (bf16[128,256]{1,0:T(8,128)(2,1)S(1)}, bf16[128,256]{1,0:T(8,128)(2,1)S(1)}, u32[]{:S(2)}, u32[]{:S(2)}) collective-permute-start(bf16[128,256]{1,0:T(8,128)(2,1)S(1)} %collective-permute-done.1.refs_4_), channel_id=1, source_target_pairs={{0,4},{4,0},{8,12},{12,8},{16,20},{20,16},{24,28},{28,24},{1,5},{5... | collective-permute-start | bytes 196616 | tf_op jit(solution)/shard_map/ppermute | solution.py:93
  12.1 0.1 collective-permute-start.6
  12.1 0.0 collective-permute-done.3.refs_1_
  12.1 0.7 %collective-permute-done.4.refs_3_ = bf16[128,256]{1,0:T(8,128)(2,1)S(1)} collective-permute-done((bf16[128,256]{1,0:T(8,128)(2,1)S(1)}, bf16[128,256]{1,0:T(8,128)(2,1)S(1)}, u32[]{:S(2)}, u32[]{:S(2)}) %collective-permute-start.4) | collective-permute-done | bytes 65568 | tf_op jit(solution)/shard_map/ppermute | solution.py:93
  12.8 0.2 collective-permute-done.5.refs_5_
  13.0 0.4 collective-permute-done.6.refs_7_
  13.3 0.0 copy-done.4
  13.3 0.4 %partials.1 = (bf16[128,256]{1,0:T(8,128)(2,1)S(1)}, bf16[128,256]{1,0:T(8,128)(2,1)S(1)}, bf16[128,256]{1,0:T(8,128)(2,1)S(1)}, bf16[128,256]{1,0:T(8,128)(2,1)S(1)}) custom-call(s32[4,4]{1,0:T(4,128)S(1)} %bitcast.6, bf16[4,128,512]{2,1,0:T(8,128)(2,1)S(1)} %get-tuple-element.32.wide_ref, bf16[128,256]{1,0:T(8,128)(2,1)S(1)} %get-tuple-element.33.refs_0_, ...), custom_call_target="tpu_custom_call" | custom-call | tf_op jit(solution)/shard_map/partials/pallas_call | solution.py:81
  13.8 2.5 %collective-permute-start.7 = (bf16[128,256]{1,0:T(8,128)(2,1)S(1)}, bf16[128,256]{1,0:T(8,128)(2,1)S(1)}, u32[]{:S(2)}, u32[]{:S(2)}) collective-permute-start(bf16[128,256]{1,0:T(8,128)(2,1)S(1)} %get-tuple-element.38), channel_id=1, source_target_pairs={{0,3},{1,2},{2,1},{3,0},{4,7},{5,6},{6,5},{7,4},{8,11},{9,10},{10,... | collective-permute-start | bytes 196616 | tf_op jit(solution)/shard_map/ppermute | solution.py:248
  16.3 0.5 %collective-permute-start.8 = (bf16[128,256]{1,0:T(8,128)(2,1)S(1)}, bf16[128,256]{1,0:T(8,128)(2,1)S(1)}, u32[]{:S(2)}, u32[]{:S(2)}) collective-permute-start(bf16[128,256]{1,0:T(8,128)(2,1)S(1)} %get-tuple-element.39), channel_id=1, source_target_pairs={{0,2},{1,3},{2,0},{3,1},{4,5},{5,4},{6,7},{7,6},{8,10},{9,11},{10,... | collective-permute-start | bytes 196616 | tf_op jit(solution)/shard_map/ppermute | solution.py:248
  16.8 0.5 %collective-permute-start.9 = (bf16[128,256]{1,0:T(8,128)(2,1)S(1)}, bf16[128,256]{1,0:T(8,128)(2,1)S(1)}, u32[]{:S(2)}, u32[]{:S(2)}) collective-permute-start(bf16[128,256]{1,0:T(8,128)(2,1)S(1)} %get-tuple-element.40), channel_id=1, source_target_pairs={{0,1},{1,0},{2,3},{3,2},{4,6},{5,7},{6,4},{7,5},{8,9},{9,8},{10,11... | collective-permute-start | bytes 196616 | tf_op jit(solution)/shard_map/ppermute | solution.py:248
  17.3 2.1 %collective-permute-done.7.refs_1_ = bf16[128,256]{1,0:T(8,128)(2,1)S(1)} collective-permute-done((bf16[128,256]{1,0:T(8,128)(2,1)S(1)}, bf16[128,256]{1,0:T(8,128)(2,1)S(1)}, u32[]{:S(2)}, u32[]{:S(2)}) %collective-permute-start.7) | collective-permute-done | bytes 65568 | tf_op jit(solution)/shard_map/ppermute | solution.py:248
  19.4 1.2 %collective-permute-done.8.refs_2_ = bf16[128,256]{1,0:T(8,128)(2,1)S(1)} collective-permute-done((bf16[128,256]{1,0:T(8,128)(2,1)S(1)}, bf16[128,256]{1,0:T(8,128)(2,1)S(1)}, u32[]{:S(2)}, u32[]{:S(2)}) %collective-permute-start.8) | collective-permute-done | bytes 65568 | tf_op jit(solution)/shard_map/ppermute | solution.py:248
  20.6 0.4 %collective-permute-done.9.refs_3_ = bf16[128,256]{1,0:T(8,128)(2,1)S(1)} collective-permute-done((bf16[128,256]{1,0:T(8,128)(2,1)S(1)}, bf16[128,256]{1,0:T(8,128)(2,1)S(1)}, u32[]{:S(2)}, u32[]{:S(2)}) %collective-permute-start.9) | collective-permute-done | bytes 65568 | tf_op jit(solution)/shard_map/ppermute | solution.py:248
  21.1 0.0 copy-done.3
  21.1 0.4 %dense.1 = (bf16[128,256]{1,0:T(8,128)(2,1)S(1)}, f32[128,256]{1,0:T(8,128)S(1)}, bf16[256,256]{1,0:T(8,128)(2,1)S(1)}) custom-call(bf16[256,256]{1,0:T(8,128)(2,1)S(1)} %copy-done.1, bf16[128,256]{1,0:T(8,128)(2,1)S(1)} %copy-done.3, bf16[256,128]{1,0:T(8,128)(2,1)S(1)} %get-tuple-element.31.placing_ref, bf16[128,256]{1,0:T(8,128)(2,1)S(1)} %get-tuple-element.37.refs_0_, ...), custom_call_target="tpu_custom_call" | custom-call | tf_op jit(solution)/shard_map/dense/pallas_call | solution.py:125
  21.5 0.1 collective-permute-start.10
  21.6 1.3 %collective-permute-done.10.came_ref.refs_1_ = bf16[256,256]{1,0:T(8,128)(2,1)S(1)} collective-permute-done((bf16[256,256]{1,0:T(8,128)(2,1)S(1)}, bf16[256,256]{1,0:T(8,128)(2,1)S(1)}, u32[]{:S(2)}, u32[]{:S(2)}) %collective-permute-start.10) | collective-permute-done | bytes 131104 | tf_op jit(solution)/shard_map/ppermute | solution.py:93
  23.0 2.8 %collective-permute-start.11 = (bf16[192,256]{1,0:T(8,128)(2,1)S(1)}, bf16[192,256]{1,0:T(8,128)(2,1)S(1)}, u32[]{:S(2)}, u32[]{:S(2)}) collective-permute-start(bf16[192,256]{1,0:T(8,128)(2,1)S(1)} %get-tuple-element.45), channel_id=1, source_target_pairs={{0,24},{1,25},{2,26},{3,27},{4,7},{5,6},{6,5},{7,4},{8,16},{9,17},... | collective-permute-start | bytes 294920 | tf_op jit(solution)/shard_map/ppermute | solution.py:248
  25.7 0.0 collective-permute-start.12
  25.7 1.7 %collective-permute-start.13 = (bf16[192,256]{1,0:T(8,128)(2,1)S(1)}, bf16[192,256]{1,0:T(8,128)(2,1)S(1)}, u32[]{:S(2)}, u32[]{:S(2)}) collective-permute-start(bf16[192,256]{1,0:T(8,128)(2,1)S(1)} %get-tuple-element.47), channel_id=1, source_target_pairs={{0,8},{1,9},{2,10},{3,11},{4,5},{5,4},{6,7},{7,6},{8,0},{9,1},{10,... | collective-permute-start | bytes 294920 | tf_op jit(solution)/shard_map/ppermute | solution.py:248
  27.4 2.0 %collective-permute-done.11.refs_0_ = bf16[192,256]{1,0:T(8,128)(2,1)S(1)} collective-permute-done((bf16[192,256]{1,0:T(8,128)(2,1)S(1)}, bf16[192,256]{1,0:T(8,128)(2,1)S(1)}, u32[]{:S(2)}, u32[]{:S(2)}) %collective-permute-start.11) | collective-permute-done | bytes 98336 | tf_op jit(solution)/shard_map/ppermute | solution.py:248
  29.4 2.1 %collective-permute-done.12.refs_1_ = bf16[192,256]{1,0:T(8,128)(2,1)S(1)} collective-permute-done((bf16[192,256]{1,0:T(8,128)(2,1)S(1)}, bf16[192,256]{1,0:T(8,128)(2,1)S(1)}, u32[]{:S(2)}, u32[]{:S(2)}) %collective-permute-start.12) | collective-permute-done | bytes 98336 | tf_op jit(solution)/shard_map/ppermute | solution.py:248
  31.5 0.0 collective-permute-done.13.refs_2_
  31.5 0.1 second.1
  31.6 1.8 %collective-permute-start.14 = (bf16[192,256]{1,0:T(8,128)(2,1)S(1)}, bf16[192,256]{1,0:T(8,128)(2,1)S(1)}, u32[]{:S(2)}, u32[]{:S(2)}) collective-permute-start(bf16[192,256]{1,0:T(8,128)(2,1)S(1)} %get-tuple-element.49), channel_id=1, source_target_pairs={{0,3},{1,2},{2,1},{3,0},{4,28},{5,29},{6,30},{7,31},{8,11},{9,10},... | collective-permute-start | bytes 294920 | tf_op jit(solution)/shard_map/ppermute | solution.py:248
  33.4 0.8 %collective-permute-start.15 = (bf16[192,256]{1,0:T(8,128)(2,1)S(1)}, bf16[192,256]{1,0:T(8,128)(2,1)S(1)}, u32[]{:S(2)}, u32[]{:S(2)}) collective-permute-start(bf16[192,256]{1,0:T(8,128)(2,1)S(1)} %get-tuple-element.50), channel_id=1, source_target_pairs={{0,2},{1,3},{2,0},{3,1},{4,20},{5,21},{6,22},{7,23},{8,10},{9,11},... | collective-permute-start | bytes 294920 | tf_op jit(solution)/shard_map/ppermute | solution.py:248
  34.2 0.9 %collective-permute-start.16 = (bf16[192,256]{1,0:T(8,128)(2,1)S(1)}, bf16[192,256]{1,0:T(8,128)(2,1)S(1)}, u32[]{:S(2)}, u32[]{:S(2)}) collective-permute-start(bf16[192,256]{1,0:T(8,128)(2,1)S(1)} %get-tuple-element.51), channel_id=1, source_target_pairs={{0,1},{1,0},{2,3},{3,2},{4,12},{5,13},{6,14},{7,15},{8,9},{9,8},{1... | collective-permute-start | bytes 294920 | tf_op jit(solution)/shard_map/ppermute | solution.py:248
  35.2 0.7 %store.2._ = bf16[8,32,256]{2,1,0:T(8,128)(2,1)} custom-call(bf16[128,256]{1,0:T(8,128)(2,1)S(1)} %get-tuple-element.41.same_ref.refs_0_, bf16[256,256]{1,0:T(8,128)(2,1)S(1)} %collective-permute-done.10.came_ref.refs_1_, bf16[192,256]{1,0:T(8,128)(2,1)S(1)} %collective-permute-done.11.refs_0_, bf16[192,256]{1,0:T(8,128)(2,1)S(1)} %collective-permute-done.12.refs_1_, ...), custom_call_target="tpu_custom_call" | custom-call | tf_op jit(solution)/shard_map/store/pallas_call | solution.py:212
  35.9 1.4 %collective-permute-done.14.refs_0_.refs_2_ = bf16[192,256]{1,0:T(8,128)(2,1)S(1)} collective-permute-done((bf16[192,256]{1,0:T(8,128)(2,1)S(1)}, bf16[192,256]{1,0:T(8,128)(2,1)S(1)}, u32[]{:S(2)}, u32[]{:S(2)}) %collective-permute-start.14) | collective-permute-done | bytes 98336 | tf_op jit(solution)/shard_map/ppermute | solution.py:248
  37.2 1.0 %collective-permute-done.15.refs_1_.refs_3_ = bf16[192,256]{1,0:T(8,128)(2,1)S(1)} collective-permute-done((bf16[192,256]{1,0:T(8,128)(2,1)S(1)}, bf16[192,256]{1,0:T(8,128)(2,1)S(1)}, u32[]{:S(2)}, u32[]{:S(2)}) %collective-permute-start.15) | collective-permute-done | bytes 98336 | tf_op jit(solution)/shard_map/ppermute | solution.py:248
  38.2 0.6 %collective-permute-done.16.refs_2_.refs_4_ = bf16[192,256]{1,0:T(8,128)(2,1)S(1)} collective-permute-done((bf16[192,256]{1,0:T(8,128)(2,1)S(1)}, bf16[192,256]{1,0:T(8,128)(2,1)S(1)}, u32[]{:S(2)}, u32[]{:S(2)}) %collective-permute-start.16) | collective-permute-done | bytes 98336 | tf_op jit(solution)/shard_map/ppermute | solution.py:248
  38.9 0.1 third.1.own_ref
  38.9 0.1 collective-permute-start.17
  39.0 1.2 %collective-permute-done.17.came_ref = bf16[128,256]{1,0:T(8,128)(2,1)S(1)} collective-permute-done((bf16[128,256]{1,0:T(8,128)(2,1)S(1)}, bf16[128,256]{1,0:T(8,128)(2,1)S(1)}, u32[]{:S(2)}, u32[]{:S(2)}) %collective-permute-start.17) | collective-permute-done | bytes 65568 | tf_op jit(solution)/shard_map/ppermute | solution.py:93
  40.2 0.7 %finish.1 = f32[2,128,256]{2,1,0:T(8,128)} custom-call(bf16[128,256]{1,0:T(8,128)(2,1)S(1)} %third.1.own_ref, bf16[128,256]{1,0:T(8,128)(2,1)S(1)} %collective-permute-done.17.came_ref), custom_call_target="tpu_custom_call" | custom-call | tf_op jit(solution)/shard_map/finish/pallas_call | solution.py:231
  (9 shorter events, 0.1 us)
Async XLA Ops:
  0.6 8.5 %collective-permute-start.2 = (bf16[128,256]{1,0:T(8,128)(2,1)}, bf16[128,256]{1,0:T(8,128)(2,1)S(1)}, u32[]{:S(2)}, u32[]{:S(2)}) collective-permute-start(bf16[128,256]{1,0:T(8,128)(2,1)} %own_ref.1), channel_id=1, source_target_pairs={{0,24},{4,28},{8,16},{12,20},{16,8},{20,12},{24,0},{28,4},{1,25},{... | collective-permute-start | bytes 196616 | tf_op jit(solution)/shard_map/ppermute | solution.py:93
  5.7 5.8 %collective-permute-start.1 = (bf16[128,256]{1,0:T(8,128)(2,1)}, bf16[128,256]{1,0:T(8,128)(2,1)S(1)}, u32[]{:S(2)}, u32[]{:S(2)}) collective-permute-start(bf16[128,256]{1,0:T(8,128)(2,1)} %own_ref.1), channel_id=1, source_target_pairs={{0,16},{4,20},{8,24},{12,28},{16,0},{20,4},{24,8},{28,12},{1,17},{... | collective-permute-start | bytes 196616 | tf_op jit(solution)/shard_map/ppermute | solution.py:93
  5.7 5.8 %collective-permute-start = (bf16[128,256]{1,0:T(8,128)(2,1)}, bf16[128,256]{1,0:T(8,128)(2,1)S(1)}, u32[]{:S(2)}, u32[]{:S(2)}) collective-permute-start(bf16[128,256]{1,0:T(8,128)(2,1)} %own_ref.1), channel_id=1, source_target_pairs={{0,8},{4,12},{8,0},{12,4},{16,24},{20,28},{24,16},{28,20},{1,9},{5... | collective-permute-start | bytes 196616 | tf_op jit(solution)/shard_map/ppermute | solution.py:93
  6.4 5.8 %collective-permute-start.3 = (bf16[128,256]{1,0:T(8,128)(2,1)}, bf16[128,256]{1,0:T(8,128)(2,1)S(1)}, u32[]{:S(2)}, u32[]{:S(2)}) collective-permute-start(bf16[128,256]{1,0:T(8,128)(2,1)} %own_ref.1), channel_id=1, source_target_pairs={{0,4},{4,0},{8,12},{12,8},{16,20},{20,16},{24,28},{28,24},{1,5},{5... | collective-permute-start | bytes 196616 | tf_op jit(solution)/shard_map/ppermute | solution.py:93
  6.4 0.7 %copy-start.5 = (s32[128,1]{0,1:T(1,128)S(1)}, s32[128,1]{0,1:T(1,128)}, u32[]{:S(2)}) copy-start(s32[128,1]{0,1:T(1,128)} %param.11) | copy-start | bytes 1540
  7.0 1.0 %copy-start = (bf16[4,1,4,128,128]{4,3,2,1,0:T(8,128)(2,1)S(1)}, bf16[4,1,4,128,128]{4,3,2,1,0:T(8,128)(2,1)}, u32[]{:S(2)}) copy-start(bf16[4,1,4,128,128]{4,3,2,1,0:T(8,128)(2,1)} %param.7) | copy-start | bytes 1572868
  8.1 0.8 %copy-start.2 = (bf16[128,256]{1,0:T(8,128)(2,1)S(1)}, bf16[128,256]{1,0:T(8,128)(2,1)}, u32[]{:S(2)}) copy-start(bf16[128,256]{1,0:T(8,128)(2,1)} %own_ref.1) | copy-start | bytes 196612
  11.6 1.8 %copy-start.4 = (s32[4,1,4]{2,1,0:T(1,128)S(1)}, s32[4,1,4]{2,1,0:T(1,128)}, u32[]{:S(2)}) copy-start(s32[4,1,4]{2,1,0:T(1,128)} %param.8) | copy-start | bytes 196
  11.6 1.3 %collective-permute-start.4 = (bf16[128,256]{1,0:T(8,128)(2,1)S(1)}, bf16[128,256]{1,0:T(8,128)(2,1)S(1)}, u32[]{:S(2)}, u32[]{:S(2)}) collective-permute-start(bf16[128,256]{1,0:T(8,128)(2,1)S(1)} %collective-permute-done.refs_2_), channel_id=1, source_target_pairs={{0,4},{4,0},{8,12},{12,8},{16,20},{20,16},{24,28},{28,24},{1,5},{5... | collective-permute-start | bytes 196616 | tf_op jit(solution)/shard_map/ppermute | solution.py:93
  11.6 1.4 %collective-permute-start.5 = (bf16[128,256]{1,0:T(8,128)(2,1)S(1)}, bf16[128,256]{1,0:T(8,128)(2,1)S(1)}, u32[]{:S(2)}, u32[]{:S(2)}) collective-permute-start(bf16[128,256]{1,0:T(8,128)(2,1)S(1)} %collective-permute-done.1.refs_4_), channel_id=1, source_target_pairs={{0,4},{4,0},{8,12},{12,8},{16,20},{20,16},{24,28},{28,24},{1,5},{5... | collective-permute-start | bytes 196616 | tf_op jit(solution)/shard_map/ppermute | solution.py:93
  12.1 1.3 %collective-permute-start.6 = (bf16[128,256]{1,0:T(8,128)(2,1)S(1)}, bf16[128,256]{1,0:T(8,128)(2,1)S(1)}, u32[]{:S(2)}, u32[]{:S(2)}) collective-permute-start(bf16[128,256]{1,0:T(8,128)(2,1)S(1)} %collective-permute-done.2.refs_6_), channel_id=1, source_target_pairs={{0,4},{4,0},{8,12},{12,8},{16,20},{20,16},{24,28},{28,24},{1,5},{5... | collective-permute-start | bytes 196616 | tf_op jit(solution)/shard_map/ppermute | solution.py:93
  13.3 7.7 %copy-start.1 = (bf16[256,256]{1,0:T(8,128)(2,1)S(1)}, bf16[256,256]{1,0:T(8,128)(2,1)}, u32[]{:S(2)}) copy-start(bf16[256,256]{1,0:T(8,128)(2,1)} %weight_ref.1) | copy-start | bytes 393220
  13.3 7.7 %copy-start.3 = (bf16[128,256]{1,0:T(8,128)(2,1)S(1)}, bf16[128,256]{1,0:T(8,128)(2,1)}, u32[]{:S(2)}) copy-start(bf16[128,256]{1,0:T(8,128)(2,1)} %cot_ref.1) | copy-start | bytes 196612
  13.8 5.6 %collective-permute-start.7 = (bf16[128,256]{1,0:T(8,128)(2,1)S(1)}, bf16[128,256]{1,0:T(8,128)(2,1)S(1)}, u32[]{:S(2)}, u32[]{:S(2)}) collective-permute-start(bf16[128,256]{1,0:T(8,128)(2,1)S(1)} %get-tuple-element.38), channel_id=1, source_target_pairs={{0,3},{1,2},{2,1},{3,0},{4,7},{5,6},{6,5},{7,4},{8,11},{9,10},{10,... | collective-permute-start | bytes 196616 | tf_op jit(solution)/shard_map/ppermute | solution.py:248
  16.3 4.3 %collective-permute-start.8 = (bf16[128,256]{1,0:T(8,128)(2,1)S(1)}, bf16[128,256]{1,0:T(8,128)(2,1)S(1)}, u32[]{:S(2)}, u32[]{:S(2)}) collective-permute-start(bf16[128,256]{1,0:T(8,128)(2,1)S(1)} %get-tuple-element.39), channel_id=1, source_target_pairs={{0,2},{1,3},{2,0},{3,1},{4,5},{5,4},{6,7},{7,6},{8,10},{9,11},{10,... | collective-permute-start | bytes 196616 | tf_op jit(solution)/shard_map/ppermute | solution.py:248
  16.8 4.3 %collective-permute-start.9 = (bf16[128,256]{1,0:T(8,128)(2,1)S(1)}, bf16[128,256]{1,0:T(8,128)(2,1)S(1)}, u32[]{:S(2)}, u32[]{:S(2)}) collective-permute-start(bf16[128,256]{1,0:T(8,128)(2,1)S(1)} %get-tuple-element.40), channel_id=1, source_target_pairs={{0,1},{1,0},{2,3},{3,2},{4,6},{5,7},{6,4},{7,5},{8,9},{9,8},{10,11... | collective-permute-start | bytes 196616 | tf_op jit(solution)/shard_map/ppermute | solution.py:248
  21.5 1.4 %collective-permute-start.10 = (bf16[256,256]{1,0:T(8,128)(2,1)S(1)}, bf16[256,256]{1,0:T(8,128)(2,1)S(1)}, u32[]{:S(2)}, u32[]{:S(2)}) collective-permute-start(bf16[256,256]{1,0:T(8,128)(2,1)S(1)} %get-tuple-element.42), channel_id=1, source_target_pairs={{0,4},{4,0},{8,12},{12,8},{16,20},{20,16},{24,28},{28,24},{1,5},{5... | collective-permute-start | bytes 393224 | tf_op jit(solution)/shard_map/ppermute | solution.py:93
  23.0 6.5 %collective-permute-start.11 = (bf16[192,256]{1,0:T(8,128)(2,1)S(1)}, bf16[192,256]{1,0:T(8,128)(2,1)S(1)}, u32[]{:S(2)}, u32[]{:S(2)}) collective-permute-start(bf16[192,256]{1,0:T(8,128)(2,1)S(1)} %get-tuple-element.45), channel_id=1, source_target_pairs={{0,24},{1,25},{2,26},{3,27},{4,7},{5,6},{6,5},{7,4},{8,16},{9,17},... | collective-permute-start | bytes 294920 | tf_op jit(solution)/shard_map/ppermute | solution.py:248
  25.7 5.8 %collective-permute-start.12 = (bf16[192,256]{1,0:T(8,128)(2,1)S(1)}, bf16[192,256]{1,0:T(8,128)(2,1)S(1)}, u32[]{:S(2)}, u32[]{:S(2)}) collective-permute-start(bf16[192,256]{1,0:T(8,128)(2,1)S(1)} %get-tuple-element.46), channel_id=1, source_target_pairs={{0,16},{1,17},{2,18},{3,19},{4,6},{5,7},{6,4},{7,5},{8,24},{9,25},... | collective-permute-start | bytes 294920 | tf_op jit(solution)/shard_map/ppermute | solution.py:248
  25.7 5.8 %collective-permute-start.13 = (bf16[192,256]{1,0:T(8,128)(2,1)S(1)}, bf16[192,256]{1,0:T(8,128)(2,1)S(1)}, u32[]{:S(2)}, u32[]{:S(2)}) collective-permute-start(bf16[192,256]{1,0:T(8,128)(2,1)S(1)} %get-tuple-element.47), channel_id=1, source_target_pairs={{0,8},{1,9},{2,10},{3,11},{4,5},{5,4},{6,7},{7,6},{8,0},{9,1},{10,... | collective-permute-start | bytes 294920 | tf_op jit(solution)/shard_map/ppermute | solution.py:248
  31.6 5.6 %collective-permute-start.14 = (bf16[192,256]{1,0:T(8,128)(2,1)S(1)}, bf16[192,256]{1,0:T(8,128)(2,1)S(1)}, u32[]{:S(2)}, u32[]{:S(2)}) collective-permute-start(bf16[192,256]{1,0:T(8,128)(2,1)S(1)} %get-tuple-element.49), channel_id=1, source_target_pairs={{0,3},{1,2},{2,1},{3,0},{4,28},{5,29},{6,30},{7,31},{8,11},{9,10},... | collective-permute-start | bytes 294920 | tf_op jit(solution)/shard_map/ppermute | solution.py:248
  33.4 4.9 %collective-permute-start.15 = (bf16[192,256]{1,0:T(8,128)(2,1)S(1)}, bf16[192,256]{1,0:T(8,128)(2,1)S(1)}, u32[]{:S(2)}, u32[]{:S(2)}) collective-permute-start(bf16[192,256]{1,0:T(8,128)(2,1)S(1)} %get-tuple-element.50), channel_id=1, source_target_pairs={{0,2},{1,3},{2,0},{3,1},{4,20},{5,21},{6,22},{7,23},{8,10},{9,11},... | collective-permute-start | bytes 294920 | tf_op jit(solution)/shard_map/ppermute | solution.py:248
  34.2 4.6 %collective-permute-start.16 = (bf16[192,256]{1,0:T(8,128)(2,1)S(1)}, bf16[192,256]{1,0:T(8,128)(2,1)S(1)}, u32[]{:S(2)}, u32[]{:S(2)}) collective-permute-start(bf16[192,256]{1,0:T(8,128)(2,1)S(1)} %get-tuple-element.51), channel_id=1, source_target_pairs={{0,1},{1,0},{2,3},{3,2},{4,12},{5,13},{6,14},{7,15},{8,9},{9,8},{1... | collective-permute-start | bytes 294920 | tf_op jit(solution)/shard_map/ppermute | solution.py:248
  38.9 1.3 %collective-permute-start.17 = (bf16[128,256]{1,0:T(8,128)(2,1)S(1)}, bf16[128,256]{1,0:T(8,128)(2,1)S(1)}, u32[]{:S(2)}, u32[]{:S(2)}) collective-permute-start(bf16[128,256]{1,0:T(8,128)(2,1)S(1)} %third.1.own_ref), channel_id=1, source_target_pairs={{0,4},{4,0},{8,12},{12,8},{16,20},{20,16},{24,28},{28,24},{1,5},{5... | collective-permute-start | bytes 196616 | tf_op jit(solution)/shard_map/ppermute | solution.py:93

commit v11 on v10

--- a/solution.py
+++ b/solution.py
@@ -185,57 +185,75 @@
     )(*operands)
 
 
-def store_kernel(core, slots, same_ref, came_ref, *refs):
-    message_refs, (out_ref, rows, sem) = refs[:-3], refs[-3:]
+def fill_rows(rows, slots, same_ref, came_ref, message_refs):
     section = lax.axis_index("section")
     chips = lax.axis_size("section") // 2
-
-    @pl.when(section & 1 == core)
+    rows[section] = same_ref[:slots]
+    rows[section ^ 1] = came_ref[:slots]
+    for ref, j in zip(message_refs, across(len(message_refs) + 1)):
+        if j < chips:
+            rows[section ^ (2 * j)] = ref[:slots]
+            rows[section ^ (2 * j + 1)] = ref[slots : 2 * slots]
+
+
+def store_kernel(slots, same_ref, came_ref, *refs):
+    message_refs, (out_ref, rows, sem) = refs[:-3], refs[-3:]
+
+    @pl.when(lax.axis_index("section") & 1 == 1)
     def _():
-        rows[section] = same_ref[:slots]
-        rows[section ^ 1] = came_ref[:slots]
-        for ref, j in zip(message_refs, across(len(message_refs) + 1)):
-            if j < chips:
-                rows[section ^ (2 * j)] = ref[:slots]
-                rows[section ^ (2 * j + 1)] = ref[slots : 2 * slots]
+        fill_rows(rows, slots, same_ref, came_ref, message_refs)
         copy = pltpu.make_async_copy(rows, out_ref, sem)
         copy.start()
         copy.wait()
 
 
-def store(core, same, came, messages, n_section, slots, base=None):
+def store(same, came, messages, n_section, slots):
     shape = (n_section, slots, same.shape[1])
     operands = [same, came, *messages]
-    kernel, first, specs = functools.partial(store_kernel, core, slots), [], []
-    if base is not None:
-        kernel, first, specs = lambda _, *refs: store_kernel(core, slots, *refs), [base], [HBM]
-    return pl.pallas_call(
-        kernel,
+    return pl.pallas_call(
+        functools.partial(store_kernel, slots),
         out_shape=jax.ShapeDtypeStruct(shape, jnp.bfloat16),
-        in_specs=specs + [VMEM] * len(operands),
+        in_specs=[VMEM] * len(operands),
         out_specs=HBM,
         scratch_shapes=[pltpu.VMEM(shape, jnp.bfloat16), pltpu.SemaphoreType.DMA],
-        input_output_aliases={0: 0} if first else {},
         compiler_params=LIMIT,
         name="store",
-    )(*first, *operands)
-
-
-def finish_kernel(own_ref, came_ref, out_ref):
+    )(*operands)
+
+
+def finish_kernel(slots, base_ref, own_ref, other_ref, same_ref, came_ref, *refs):
+    message_refs, (relaid_ref, grad_ref, rows, sem) = refs[:-4], refs[-4:]
     core = lax.axis_index("section") & 1
-    out_ref[core] = own_ref[...].astype(jnp.float32)
-    out_ref[1 - core] = came_ref[...].astype(jnp.float32)
-
-
-def finish(own, came):
-    return pl.pallas_call(
-        finish_kernel,
-        out_shape=jax.ShapeDtypeStruct((2,) + own.shape, jnp.float32),
-        in_specs=[VMEM] * 2,
-        out_specs=VMEM,
+    copy = pltpu.make_async_copy(rows, relaid_ref, sem)
+
+    @pl.when(core == 0)
+    def _():
+        fill_rows(rows, slots, same_ref, came_ref, message_refs)
+        copy.start()
+
+    grad_ref[core] = own_ref[...].astype(jnp.float32)
+    grad_ref[1 - core] = other_ref[...].astype(jnp.float32)
+
+    @pl.when(core == 0)
+    def _():
+        copy.wait()
+
+
+def finish(relaid, own, other, same, came, messages, slots):
+    operands = [relaid, own, other, same, came, *messages]
+    return pl.pallas_call(
+        functools.partial(finish_kernel, slots),
+        out_shape=(
+            jax.ShapeDtypeStruct(relaid.shape, jnp.bfloat16),
+            jax.ShapeDtypeStruct((2,) + own.shape, jnp.float32),
+        ),
+        in_specs=[HBM] + [VMEM] * (len(operands) - 1),
+        out_specs=(HBM, VMEM),
+        scratch_shapes=[pltpu.VMEM(relaid.shape, jnp.bfloat16), pltpu.SemaphoreType.DMA],
+        input_output_aliases={0: 0},
         compiler_params=LIMIT,
         name="finish",
-    )(own, came)
+    )(*operands)
 
 
 def swap_by_core(value, first, second):
@@ -281,23 +299,22 @@
     half, *first = call_halves(
         functools.partial(first_kernel, slots), "first", [same, kept, came], half_shape, slots, len(steps)
     )
-    first = [swap_by_core(m, (j, 0), (0, j)) for m, j in zip(first, steps)]
-    relaid = store(0, same, came, first, n_section, slots)
+    first = [swap_by_core(m, (0, j), (j, 0)) for m, j in zip(first, steps)]
+    relaid = store(same, came, first, n_section, slots)
     half, *second = call_halves(
-        functools.partial(second_kernel, slots, (chips, n_rep), len(steps)),
+        functools.partial(second_kernel, slots, (n_rep, chips), len(steps)),
         "second",
         [same, came, half, *first],
         half_shape,
         slots,
         len(steps),
     )
-    second = [swap_by_core(m, (0, j), (j, 0)) for m, j in zip(second, steps)]
+    second = [swap_by_core(m, (j, 0), (0, j)) for m, j in zip(second, steps)]
     (half,) = call_halves(
-        functools.partial(third_kernel, slots, (n_rep, chips)), "third", [half, *second], half_shape, slots, 0
-    )
-    relaid = store(1, same, came, second, n_section, slots, relaid)
-    half, relaid = lax.optimization_barrier((half, relaid))
-    weight_grad = finish(half, swap(half, "section", 1))
+        functools.partial(third_kernel, slots, (chips, n_rep)), "third", [half, *second], half_shape, slots, 0
+    )
+    other = swap(half, "section", 1)
+    relaid, weight_grad = finish(relaid, half, other, same, came, second, slots)
     return (relaid.reshape(1, 1, n_section, slots, width), weight_grad.reshape(width, width))
 
 

time: 41.2 us -> 41.8 us (1.015)
  waiting for transfers between devices: 17 us -> 17.6 us
    ppermute x9, waiting for transfers between devices: 10.8 us -> 11.5 us  [swap_by_core(): return lax.ppermute(value, ('section', 'rep'), pairs)]
    pallas_call x3 -> x2, Pallas kernels: 1.41 us -> 1.4 us  [the longest x1 1.37 us: finish(): pl.pallas_call(functools.partial(finish_kernel, slots), out_shape=(jax.Sh...]
  transfers between devices with their start and end apart: 18 -> 18, of which waited for: 14 -> 14; matrix products, arithmetic and copies ran while one was open for 0% -> 0% of each run, Pallas kernels for 2% -> 1%
where the time goes in v11:
time: 41.8 us; the launch traced here: 41.6 us
  starting transfers between devices  18 us (43%)
  waiting for transfers between devices  17.6 us (42%)
  Pallas kernels  2.63 us (6%)
  local copies, waits for them, and re-layouts  2.55 us (6%)
  between operations  0.72 us (2%)
    ppermute x9, starting transfers between devices, swap_by_core(): return lax.ppermute(value, ('section', 'rep'), pairs)  11.6 us
    ppermute x9, waiting for transfers between devices, swap_by_core(): return lax.ppermute(value, ('section', 'rep'), pairs)  11.5 us
    ppermute x9, starting transfers between devices, swap(): lax.ppermute(value, axis, [(i, i ^ j) for i in range(lax.axis_size(axis))])  6.48 us
    ppermute x9, waiting for transfers between devices, swap(): lax.ppermute(value, axis, [(i, i ^ j) for i in range(lax.axis_size(axis))])  6.12 us
    unnamed x12, local copies, waits for them, and re-layouts  2.55 us
    pallas_call x1, Pallas kernels, finish(): pl.pallas_call(functools.partial(finish_kernel, slots), out_shape=(jax.Sh...  1.37 us
  transfers between devices with their start and end apart: 18, of which 14 were waited for; matrix products, arithmetic and copies ran while one was open for 0% of the time, Pallas kernels for 1%

profile of v11, /device:TPU:0, one launch (start us, length us, event | category | flops | bytes accessed | tf_op | source)
XLA Modules:
  0.0 41.6 jit_solution(17944674028774395017)
XLA Ops:
  0.6 5.1 %collective-permute-start.2 = (bf16[128,256]{1,0:T(8,128)(2,1)}, bf16[128,256]{1,0:T(8,128)(2,1)S(1)}, u32[]{:S(2)}, u32[]{:S(2)}) collective-permute-start(bf16[128,256]{1,0:T(8,128)(2,1)} %own_ref.1), channel_id=1, source_target_pairs={{0,24},{4,28},{8,16},{12,20},{16,8},{20,12},{24,0},{28,4},{1,25},{... | collective-permute-start | bytes 196616 | tf_op jit(solution)/shard_map/ppermute | solution.py:93
  5.7 0.0 collective-permute-start.1
  5.7 0.6 %collective-permute-start = (bf16[128,256]{1,0:T(8,128)(2,1)}, bf16[128,256]{1,0:T(8,128)(2,1)S(1)}, u32[]{:S(2)}, u32[]{:S(2)}) collective-permute-start(bf16[128,256]{1,0:T(8,128)(2,1)} %own_ref.1), channel_id=1, source_target_pairs={{0,8},{4,12},{8,0},{12,4},{16,24},{20,28},{24,16},{28,20},{1,9},{5... | collective-permute-start | bytes 196616 | tf_op jit(solution)/shard_map/ppermute | solution.py:93
  6.4 0.0 collective-permute-start.3
  6.4 0.0 copy-start.5
  6.4 0.7 %copy-done.5 = s32[128,1]{0,1:T(1,128)S(1)} copy-done((s32[128,1]{0,1:T(1,128)S(1)}, s32[128,1]{0,1:T(1,128)}, u32[]{:S(2)}) %copy-start.5) | copy-done | bytes 536
  7.0 1.0 %copy-done = bf16[4,1,4,128,128]{4,3,2,1,0:T(8,128)(2,1)S(1)} copy-done((bf16[4,1,4,128,128]{4,3,2,1,0:T(8,128)(2,1)S(1)}, bf16[4,1,4,128,128]{4,3,2,1,0:T(8,128)(2,1)}, u32[]{:S(2)}) %copy-start) | copy-done | bytes 524312
  8.1 0.8 %copy-done.2 = bf16[128,256]{1,0:T(8,128)(2,1)S(1)} copy-done((bf16[128,256]{1,0:T(8,128)(2,1)S(1)}, bf16[128,256]{1,0:T(8,128)(2,1)}, u32[]{:S(2)}) %copy-start.2) | copy-done | bytes 65560
  8.9 0.2 prepare.1
  9.2 0.0 collective-permute-done.2.refs_6_
  9.2 2.4 %collective-permute-done.1.refs_4_ = bf16[128,256]{1,0:T(8,128)(2,1)S(1)} collective-permute-done((bf16[128,256]{1,0:T(8,128)(2,1)}, bf16[128,256]{1,0:T(8,128)(2,1)S(1)}, u32[]{:S(2)}, u32[]{:S(2)}) %collective-permute-start.1) | collective-permute-done | bytes 65568 | tf_op jit(solution)/shard_map/ppermute | solution.py:93
  11.6 0.0 collective-permute-done.refs_2_
  11.6 0.0 collective-permute-start.4
  11.6 0.5 %collective-permute-start.5 = (bf16[128,256]{1,0:T(8,128)(2,1)S(1)}, bf16[128,256]{1,0:T(8,128)(2,1)S(1)}, u32[]{:S(2)}, u32[]{:S(2)}) collective-permute-start(bf16[128,256]{1,0:T(8,128)(2,1)S(1)} %collective-permute-done.1.refs_4_), channel_id=1, source_target_pairs={{0,4},{4,0},{8,12},{12,8},{16,20},{20,16},{24,28},{28,24},{1,5},{5... | collective-permute-start | bytes 196616 | tf_op jit(solution)/shard_map/ppermute | solution.py:93
  12.1 0.1 collective-permute-start.6
  12.1 0.0 collective-permute-done.3.refs_1_
  12.1 0.7 %collective-permute-done.4.refs_3_ = bf16[128,256]{1,0:T(8,128)(2,1)S(1)} collective-permute-done((bf16[128,256]{1,0:T(8,128)(2,1)S(1)}, bf16[128,256]{1,0:T(8,128)(2,1)S(1)}, u32[]{:S(2)}, u32[]{:S(2)}) %collective-permute-start.4) | collective-permute-done | bytes 65568 | tf_op jit(solution)/shard_map/ppermute | solution.py:93
  12.8 0.2 collective-permute-done.5.refs_5_
  13.0 0.4 collective-permute-done.6.refs_7_
  13.3 0.0 copy-done.4
  13.3 0.4 %partials.1 = (bf16[128,256]{1,0:T(8,128)(2,1)S(1)}, bf16[128,256]{1,0:T(8,128)(2,1)S(1)}, bf16[128,256]{1,0:T(8,128)(2,1)S(1)}, bf16[128,256]{1,0:T(8,128)(2,1)S(1)}) custom-call(s32[4,4]{1,0:T(4,128)S(1)} %bitcast.6, bf16[4,128,512]{2,1,0:T(8,128)(2,1)S(1)} %get-tuple-element.32.wide_ref, bf16[128,256]{1,0:T(8,128)(2,1)S(1)} %get-tuple-element.33.refs_0_, ...), custom_call_target="tpu_custom_call" | custom-call | tf_op jit(solution)/shard_map/partials/pallas_call | solution.py:81
  13.8 2.5 %collective-permute-start.7 = (bf16[128,256]{1,0:T(8,128)(2,1)S(1)}, bf16[128,256]{1,0:T(8,128)(2,1)S(1)}, u32[]{:S(2)}, u32[]{:S(2)}) collective-permute-start(bf16[128,256]{1,0:T(8,128)(2,1)S(1)} %get-tuple-element.38), channel_id=1, source_target_pairs={{0,3},{1,2},{2,1},{3,0},{4,7},{5,6},{6,5},{7,4},{8,11},{9,10},{10,... | collective-permute-start | bytes 196616 | tf_op jit(solution)/shard_map/ppermute | solution.py:266
  16.3 0.5 %collective-permute-start.8 = (bf16[128,256]{1,0:T(8,128)(2,1)S(1)}, bf16[128,256]{1,0:T(8,128)(2,1)S(1)}, u32[]{:S(2)}, u32[]{:S(2)}) collective-permute-start(bf16[128,256]{1,0:T(8,128)(2,1)S(1)} %get-tuple-element.39), channel_id=1, source_target_pairs={{0,2},{1,3},{2,0},{3,1},{4,5},{5,4},{6,7},{7,6},{8,10},{9,11},{10,... | collective-permute-start | bytes 196616 | tf_op jit(solution)/shard_map/ppermute | solution.py:266
  16.8 0.5 %collective-permute-start.9 = (bf16[128,256]{1,0:T(8,128)(2,1)S(1)}, bf16[128,256]{1,0:T(8,128)(2,1)S(1)}, u32[]{:S(2)}, u32[]{:S(2)}) collective-permute-start(bf16[128,256]{1,0:T(8,128)(2,1)S(1)} %get-tuple-element.40), channel_id=1, source_target_pairs={{0,1},{1,0},{2,3},{3,2},{4,6},{5,7},{6,4},{7,5},{8,9},{9,8},{10,11... | collective-permute-start | bytes 196616 | tf_op jit(solution)/shard_map/ppermute | solution.py:266
  17.3 2.1 %collective-permute-done.7.refs_1_ = bf16[128,256]{1,0:T(8,128)(2,1)S(1)} collective-permute-done((bf16[128,256]{1,0:T(8,128)(2,1)S(1)}, bf16[128,256]{1,0:T(8,128)(2,1)S(1)}, u32[]{:S(2)}, u32[]{:S(2)}) %collective-permute-start.7) | collective-permute-done | bytes 65568 | tf_op jit(solution)/shard_map/ppermute | solution.py:266
  19.4 1.2 %collective-permute-done.8.refs_2_ = bf16[128,256]{1,0:T(8,128)(2,1)S(1)} collective-permute-done((bf16[128,256]{1,0:T(8,128)(2,1)S(1)}, bf16[128,256]{1,0:T(8,128)(2,1)S(1)}, u32[]{:S(2)}, u32[]{:S(2)}) %collective-permute-start.8) | collective-permute-done | bytes 65568 | tf_op jit(solution)/shard_map/ppermute | solution.py:266
  20.6 0.4 %collective-permute-done.9.refs_3_ = bf16[128,256]{1,0:T(8,128)(2,1)S(1)} collective-permute-done((bf16[128,256]{1,0:T(8,128)(2,1)S(1)}, bf16[128,256]{1,0:T(8,128)(2,1)S(1)}, u32[]{:S(2)}, u32[]{:S(2)}) %collective-permute-start.9) | collective-permute-done | bytes 65568 | tf_op jit(solution)/shard_map/ppermute | solution.py:266
  21.0 0.0 copy-done.1
  21.1 0.0 copy-done.3
  21.1 0.4 %dense.1 = (bf16[128,256]{1,0:T(8,128)(2,1)S(1)}, f32[128,256]{1,0:T(8,128)S(1)}, bf16[256,256]{1,0:T(8,128)(2,1)S(1)}) custom-call(bf16[256,256]{1,0:T(8,128)(2,1)S(1)} %copy-done.1, bf16[128,256]{1,0:T(8,128)(2,1)S(1)} %copy-done.3, bf16[256,128]{1,0:T(8,128)(2,1)S(1)} %get-tuple-element.31.placing_ref, bf16[128,256]{1,0:T(8,128)(2,1)S(1)} %get-tuple-element.37.refs_0_, ...), custom_call_target="tpu_custom_call" | custom-call | tf_op jit(solution)/shard_map/dense/pallas_call | solution.py:125
  21.5 0.1 collective-permute-start.10
  21.6 1.3 %collective-permute-done.10.came_ref = bf16[256,256]{1,0:T(8,128)(2,1)S(1)} collective-permute-done((bf16[256,256]{1,0:T(8,128)(2,1)S(1)}, bf16[256,256]{1,0:T(8,128)(2,1)S(1)}, u32[]{:S(2)}, u32[]{:S(2)}) %collective-permute-start.10) | collective-permute-done | bytes 131104 | tf_op jit(solution)/shard_map/ppermute | solution.py:93
  23.0 1.8 %collective-permute-start.11 = (bf16[192,256]{1,0:T(8,128)(2,1)S(1)}, bf16[192,256]{1,0:T(8,128)(2,1)S(1)}, u32[]{:S(2)}, u32[]{:S(2)}) collective-permute-start(bf16[192,256]{1,0:T(8,128)(2,1)S(1)} %get-tuple-element.44), channel_id=1, source_target_pairs={{0,3},{1,2},{2,1},{3,0},{4,28},{5,29},{6,30},{7,31},{8,11},{9,10},... | collective-permute-start | bytes 294920 | tf_op jit(solution)/shard_map/ppermute | solution.py:266
  24.7 0.8 %collective-permute-start.12 = (bf16[192,256]{1,0:T(8,128)(2,1)S(1)}, bf16[192,256]{1,0:T(8,128)(2,1)S(1)}, u32[]{:S(2)}, u32[]{:S(2)}) collective-permute-start(bf16[192,256]{1,0:T(8,128)(2,1)S(1)} %get-tuple-element.45), channel_id=1, source_target_pairs={{0,2},{1,3},{2,0},{3,1},{4,20},{5,21},{6,22},{7,23},{8,10},{9,11},... | collective-permute-start | bytes 294920 | tf_op jit(solution)/shard_map/ppermute | solution.py:266
  25.6 0.9 %collective-permute-start.13 = (bf16[192,256]{1,0:T(8,128)(2,1)S(1)}, bf16[192,256]{1,0:T(8,128)(2,1)S(1)}, u32[]{:S(2)}, u32[]{:S(2)}) collective-permute-start(bf16[192,256]{1,0:T(8,128)(2,1)S(1)} %get-tuple-element.46), channel_id=1, source_target_pairs={{0,1},{1,0},{2,3},{3,2},{4,12},{5,13},{6,14},{7,15},{8,9},{9,8},{1... | collective-permute-start | bytes 294920 | tf_op jit(solution)/shard_map/ppermute | solution.py:266
  26.5 2.1 %collective-permute-done.11.refs_0_ = bf16[192,256]{1,0:T(8,128)(2,1)S(1)} collective-permute-done((bf16[192,256]{1,0:T(8,128)(2,1)S(1)}, bf16[192,256]{1,0:T(8,128)(2,1)S(1)}, u32[]{:S(2)}, u32[]{:S(2)}) %collective-permute-start.11) | collective-permute-done | bytes 98336 | tf_op jit(solution)/shard_map/ppermute | solution.py:266
  28.6 1.0 %collective-permute-done.12.refs_1_ = bf16[192,256]{1,0:T(8,128)(2,1)S(1)} collective-permute-done((bf16[192,256]{1,0:T(8,128)(2,1)S(1)}, bf16[192,256]{1,0:T(8,128)(2,1)S(1)}, u32[]{:S(2)}, u32[]{:S(2)}) %collective-permute-start.12) | collective-permute-done | bytes 98336 | tf_op jit(solution)/shard_map/ppermute | solution.py:266
  29.6 0.6 %collective-permute-done.13.refs_2_ = bf16[192,256]{1,0:T(8,128)(2,1)S(1)} collective-permute-done((bf16[192,256]{1,0:T(8,128)(2,1)S(1)}, bf16[192,256]{1,0:T(8,128)(2,1)S(1)}, u32[]{:S(2)}, u32[]{:S(2)}) %collective-permute-start.13) | collective-permute-done | bytes 98336 | tf_op jit(solution)/shard_map/ppermute | solution.py:266
  30.2 0.1 second.1
  30.2 2.8 %collective-permute-start.14 = (bf16[192,256]{1,0:T(8,128)(2,1)S(1)}, bf16[192,256]{1,0:T(8,128)(2,1)S(1)}, u32[]{:S(2)}, u32[]{:S(2)}) collective-permute-start(bf16[192,256]{1,0:T(8,128)(2,1)S(1)} %get-tuple-element.49), channel_id=1, source_target_pairs={{0,24},{1,25},{2,26},{3,27},{4,7},{5,6},{6,5},{7,4},{8,16},{9,17},... | collective-permute-start | bytes 294920 | tf_op jit(solution)/shard_map/ppermute | solution.py:266
  33.0 0.0 collective-permute-start.15
  33.0 1.7 %collective-permute-start.16 = (bf16[192,256]{1,0:T(8,128)(2,1)S(1)}, bf16[192,256]{1,0:T(8,128)(2,1)S(1)}, u32[]{:S(2)}, u32[]{:S(2)}) collective-permute-start(bf16[192,256]{1,0:T(8,128)(2,1)S(1)} %get-tuple-element.51), channel_id=1, source_target_pairs={{0,8},{1,9},{2,10},{3,11},{4,5},{5,4},{6,7},{7,6},{8,0},{9,1},{10,... | collective-permute-start | bytes 294920 | tf_op jit(solution)/shard_map/ppermute | solution.py:266
  34.7 2.0 %collective-permute-done.14.refs_0_ = bf16[192,256]{1,0:T(8,128)(2,1)S(1)} collective-permute-done((bf16[192,256]{1,0:T(8,128)(2,1)S(1)}, bf16[192,256]{1,0:T(8,128)(2,1)S(1)}, u32[]{:S(2)}, u32[]{:S(2)}) %collective-permute-start.14) | collective-permute-done | bytes 98336 | tf_op jit(solution)/shard_map/ppermute | solution.py:266
  36.7 2.1 %collective-permute-done.15.refs_1_ = bf16[192,256]{1,0:T(8,128)(2,1)S(1)} collective-permute-done((bf16[192,256]{1,0:T(8,128)(2,1)S(1)}, bf16[192,256]{1,0:T(8,128)(2,1)S(1)}, u32[]{:S(2)}, u32[]{:S(2)}) %collective-permute-start.15) | collective-permute-done | bytes 98336 | tf_op jit(solution)/shard_map/ppermute | solution.py:266
  38.8 0.0 collective-permute-done.16.refs_2_
  38.9 0.1 collective-permute-start.17
  39.0 1.2 %collective-permute-done.17.other_ref = bf16[128,256]{1,0:T(8,128)(2,1)S(1)} collective-permute-done((bf16[128,256]{1,0:T(8,128)(2,1)S(1)}, bf16[128,256]{1,0:T(8,128)(2,1)S(1)}, u32[]{:S(2)}, u32[]{:S(2)}) %collective-permute-start.17) | collective-permute-done | bytes 65568 | tf_op jit(solution)/shard_map/ppermute | solution.py:93
  40.2 1.4 %finish.1 = (bf16[8,32,256]{2,1,0:T(8,128)(2,1)}, f32[2,128,256]{2,1,0:T(8,128)}) custom-call(bf16[8,32,256]{2,1,0:T(8,128)(2,1)} %store.1.base_ref, bf16[128,256]{1,0:T(8,128)(2,1)S(1)} %third.1.own_ref, bf16[128,256]{1,0:T(8,128)(2,1)S(1)} %collective-permute-done.17.other_ref, ...), custom_call_target="tpu_custom_call", output_to_operand_aliasing={{0}: (0, {})} | custom-call | tf_op jit(solution)/shard_map/finish/pallas_call | solution.py:244
  (8 shorter events, 0.1 us)
Async XLA Ops:
  0.6 8.5 %collective-permute-start.2 = (bf16[128,256]{1,0:T(8,128)(2,1)}, bf16[128,256]{1,0:T(8,128)(2,1)S(1)}, u32[]{:S(2)}, u32[]{:S(2)}) collective-permute-start(bf16[128,256]{1,0:T(8,128)(2,1)} %own_ref.1), channel_id=1, source_target_pairs={{0,24},{4,28},{8,16},{12,20},{16,8},{20,12},{24,0},{28,4},{1,25},{... | collective-permute-start | bytes 196616 | tf_op jit(solution)/shard_map/ppermute | solution.py:93
  5.7 5.8 %collective-permute-start.1 = (bf16[128,256]{1,0:T(8,128)(2,1)}, bf16[128,256]{1,0:T(8,128)(2,1)S(1)}, u32[]{:S(2)}, u32[]{:S(2)}) collective-permute-start(bf16[128,256]{1,0:T(8,128)(2,1)} %own_ref.1), channel_id=1, source_target_pairs={{0,16},{4,20},{8,24},{12,28},{16,0},{20,4},{24,8},{28,12},{1,17},{... | collective-permute-start | bytes 196616 | tf_op jit(solution)/shard_map/ppermute | solution.py:93
  5.7 5.8 %collective-permute-start = (bf16[128,256]{1,0:T(8,128)(2,1)}, bf16[128,256]{1,0:T(8,128)(2,1)S(1)}, u32[]{:S(2)}, u32[]{:S(2)}) collective-permute-start(bf16[128,256]{1,0:T(8,128)(2,1)} %own_ref.1), channel_id=1, source_target_pairs={{0,8},{4,12},{8,0},{12,4},{16,24},{20,28},{24,16},{28,20},{1,9},{5... | collective-permute-start | bytes 196616 | tf_op jit(solution)/shard_map/ppermute | solution.py:93
  6.4 5.8 %collective-permute-start.3 = (bf16[128,256]{1,0:T(8,128)(2,1)}, bf16[128,256]{1,0:T(8,128)(2,1)S(1)}, u32[]{:S(2)}, u32[]{:S(2)}) collective-permute-start(bf16[128,256]{1,0:T(8,128)(2,1)} %own_ref.1), channel_id=1, source_target_pairs={{0,4},{4,0},{8,12},{12,8},{16,20},{20,16},{24,28},{28,24},{1,5},{5... | collective-permute-start | bytes 196616 | tf_op jit(solution)/shard_map/ppermute | solution.py:93
  6.4 0.7 %copy-start.5 = (s32[128,1]{0,1:T(1,128)S(1)}, s32[128,1]{0,1:T(1,128)}, u32[]{:S(2)}) copy-start(s32[128,1]{0,1:T(1,128)} %param.11) | copy-start | bytes 1540
  7.0 1.0 %copy-start = (bf16[4,1,4,128,128]{4,3,2,1,0:T(8,128)(2,1)S(1)}, bf16[4,1,4,128,128]{4,3,2,1,0:T(8,128)(2,1)}, u32[]{:S(2)}) copy-start(bf16[4,1,4,128,128]{4,3,2,1,0:T(8,128)(2,1)} %param.7) | copy-start | bytes 1572868
  8.1 0.8 %copy-start.2 = (bf16[128,256]{1,0:T(8,128)(2,1)S(1)}, bf16[128,256]{1,0:T(8,128)(2,1)}, u32[]{:S(2)}) copy-start(bf16[128,256]{1,0:T(8,128)(2,1)} %own_ref.1) | copy-start | bytes 196612
  11.6 1.8 %copy-start.4 = (s32[4,1,4]{2,1,0:T(1,128)S(1)}, s32[4,1,4]{2,1,0:T(1,128)}, u32[]{:S(2)}) copy-start(s32[4,1,4]{2,1,0:T(1,128)} %param.8) | copy-start | bytes 196
  11.6 1.3 %collective-permute-start.4 = (bf16[128,256]{1,0:T(8,128)(2,1)S(1)}, bf16[128,256]{1,0:T(8,128)(2,1)S(1)}, u32[]{:S(2)}, u32[]{:S(2)}) collective-permute-start(bf16[128,256]{1,0:T(8,128)(2,1)S(1)} %collective-permute-done.refs_2_), channel_id=1, source_target_pairs={{0,4},{4,0},{8,12},{12,8},{16,20},{20,16},{24,28},{28,24},{1,5},{5... | collective-permute-start | bytes 196616 | tf_op jit(solution)/shard_map/ppermute | solution.py:93
  11.6 1.4 %collective-permute-start.5 = (bf16[128,256]{1,0:T(8,128)(2,1)S(1)}, bf16[128,256]{1,0:T(8,128)(2,1)S(1)}, u32[]{:S(2)}, u32[]{:S(2)}) collective-permute-start(bf16[128,256]{1,0:T(8,128)(2,1)S(1)} %collective-permute-done.1.refs_4_), channel_id=1, source_target_pairs={{0,4},{4,0},{8,12},{12,8},{16,20},{20,16},{24,28},{28,24},{1,5},{5... | collective-permute-start | bytes 196616 | tf_op jit(solution)/shard_map/ppermute | solution.py:93
  12.1 1.3 %collective-permute-start.6 = (bf16[128,256]{1,0:T(8,128)(2,1)S(1)}, bf16[128,256]{1,0:T(8,128)(2,1)S(1)}, u32[]{:S(2)}, u32[]{:S(2)}) collective-permute-start(bf16[128,256]{1,0:T(8,128)(2,1)S(1)} %collective-permute-done.2.refs_6_), channel_id=1, source_target_pairs={{0,4},{4,0},{8,12},{12,8},{16,20},{20,16},{24,28},{28,24},{1,5},{5... | collective-permute-start | bytes 196616 | tf_op jit(solution)/shard_map/ppermute | solution.py:93
  13.3 7.7 %copy-start.1 = (bf16[256,256]{1,0:T(8,128)(2,1)S(1)}, bf16[256,256]{1,0:T(8,128)(2,1)}, u32[]{:S(2)}) copy-start(bf16[256,256]{1,0:T(8,128)(2,1)} %weight_ref.1) | copy-start | bytes 393220
  13.3 7.7 %copy-start.3 = (bf16[128,256]{1,0:T(8,128)(2,1)S(1)}, bf16[128,256]{1,0:T(8,128)(2,1)}, u32[]{:S(2)}) copy-start(bf16[128,256]{1,0:T(8,128)(2,1)} %cot_ref.1) | copy-start | bytes 196612
  13.8 5.6 %collective-permute-start.7 = (bf16[128,256]{1,0:T(8,128)(2,1)S(1)}, bf16[128,256]{1,0:T(8,128)(2,1)S(1)}, u32[]{:S(2)}, u32[]{:S(2)}) collective-permute-start(bf16[128,256]{1,0:T(8,128)(2,1)S(1)} %get-tuple-element.38), channel_id=1, source_target_pairs={{0,3},{1,2},{2,1},{3,0},{4,7},{5,6},{6,5},{7,4},{8,11},{9,10},{10,... | collective-permute-start | bytes 196616 | tf_op jit(solution)/shard_map/ppermute | solution.py:266
  16.3 4.3 %collective-permute-start.8 = (bf16[128,256]{1,0:T(8,128)(2,1)S(1)}, bf16[128,256]{1,0:T(8,128)(2,1)S(1)}, u32[]{:S(2)}, u32[]{:S(2)}) collective-permute-start(bf16[128,256]{1,0:T(8,128)(2,1)S(1)} %get-tuple-element.39), channel_id=1, source_target_pairs={{0,2},{1,3},{2,0},{3,1},{4,5},{5,4},{6,7},{7,6},{8,10},{9,11},{10,... | collective-permute-start | bytes 196616 | tf_op jit(solution)/shard_map/ppermute | solution.py:266
  16.8 4.3 %collective-permute-start.9 = (bf16[128,256]{1,0:T(8,128)(2,1)S(1)}, bf16[128,256]{1,0:T(8,128)(2,1)S(1)}, u32[]{:S(2)}, u32[]{:S(2)}) collective-permute-start(bf16[128,256]{1,0:T(8,128)(2,1)S(1)} %get-tuple-element.40), channel_id=1, source_target_pairs={{0,1},{1,0},{2,3},{3,2},{4,6},{5,7},{6,4},{7,5},{8,9},{9,8},{10,11... | collective-permute-start | bytes 196616 | tf_op jit(solution)/shard_map/ppermute | solution.py:266
  21.5 1.4 %collective-permute-start.10 = (bf16[256,256]{1,0:T(8,128)(2,1)S(1)}, bf16[256,256]{1,0:T(8,128)(2,1)S(1)}, u32[]{:S(2)}, u32[]{:S(2)}) collective-permute-start(bf16[256,256]{1,0:T(8,128)(2,1)S(1)} %get-tuple-element.42), channel_id=1, source_target_pairs={{0,4},{4,0},{8,12},{12,8},{16,20},{20,16},{24,28},{28,24},{1,5},{5... | collective-permute-start | bytes 393224 | tf_op jit(solution)/shard_map/ppermute | solution.py:93
  23.0 5.6 %collective-permute-start.11 = (bf16[192,256]{1,0:T(8,128)(2,1)S(1)}, bf16[192,256]{1,0:T(8,128)(2,1)S(1)}, u32[]{:S(2)}, u32[]{:S(2)}) collective-permute-start(bf16[192,256]{1,0:T(8,128)(2,1)S(1)} %get-tuple-element.44), channel_id=1, source_target_pairs={{0,3},{1,2},{2,1},{3,0},{4,28},{5,29},{6,30},{7,31},{8,11},{9,10},... | collective-permute-start | bytes 294920 | tf_op jit(solution)/shard_map/ppermute | solution.py:266
  24.7 4.9 %collective-permute-start.12 = (bf16[192,256]{1,0:T(8,128)(2,1)S(1)}, bf16[192,256]{1,0:T(8,128)(2,1)S(1)}, u32[]{:S(2)}, u32[]{:S(2)}) collective-permute-start(bf16[192,256]{1,0:T(8,128)(2,1)S(1)} %get-tuple-element.45), channel_id=1, source_target_pairs={{0,2},{1,3},{2,0},{3,1},{4,20},{5,21},{6,22},{7,23},{8,10},{9,11},... | collective-permute-start | bytes 294920 | tf_op jit(solution)/shard_map/ppermute | solution.py:266
  25.6 4.6 %collective-permute-start.13 = (bf16[192,256]{1,0:T(8,128)(2,1)S(1)}, bf16[192,256]{1,0:T(8,128)(2,1)S(1)}, u32[]{:S(2)}, u32[]{:S(2)}) collective-permute-start(bf16[192,256]{1,0:T(8,128)(2,1)S(1)} %get-tuple-element.46), channel_id=1, source_target_pairs={{0,1},{1,0},{2,3},{3,2},{4,12},{5,13},{6,14},{7,15},{8,9},{9,8},{1... | collective-permute-start | bytes 294920 | tf_op jit(solution)/shard_map/ppermute | solution.py:266
  30.2 6.5 %collective-permute-start.14 = (bf16[192,256]{1,0:T(8,128)(2,1)S(1)}, bf16[192,256]{1,0:T(8,128)(2,1)S(1)}, u32[]{:S(2)}, u32[]{:S(2)}) collective-permute-start(bf16[192,256]{1,0:T(8,128)(2,1)S(1)} %get-tuple-element.49), channel_id=1, source_target_pairs={{0,24},{1,25},{2,26},{3,27},{4,7},{5,6},{6,5},{7,4},{8,16},{9,17},... | collective-permute-start | bytes 294920 | tf_op jit(solution)/shard_map/ppermute | solution.py:266
  33.0 5.8 %collective-permute-start.15 = (bf16[192,256]{1,0:T(8,128)(2,1)S(1)}, bf16[192,256]{1,0:T(8,128)(2,1)S(1)}, u32[]{:S(2)}, u32[]{:S(2)}) collective-permute-start(bf16[192,256]{1,0:T(8,128)(2,1)S(1)} %get-tuple-element.50), channel_id=1, source_target_pairs={{0,16},{1,17},{2,18},{3,19},{4,6},{5,7},{6,4},{7,5},{8,24},{9,25},... | collective-permute-start | bytes 294920 | tf_op jit(solution)/shard_map/ppermute | solution.py:266
  33.0 5.8 %collective-permute-start.16 = (bf16[192,256]{1,0:T(8,128)(2,1)S(1)}, bf16[192,256]{1,0:T(8,128)(2,1)S(1)}, u32[]{:S(2)}, u32[]{:S(2)}) collective-permute-start(bf16[192,256]{1,0:T(8,128)(2,1)S(1)} %get-tuple-element.51), channel_id=1, source_target_pairs={{0,8},{1,9},{2,10},{3,11},{4,5},{5,4},{6,7},{7,6},{8,0},{9,1},{10,... | collective-permute-start | bytes 294920 | tf_op jit(solution)/shard_map/ppermute | solution.py:266
  38.9 1.3 %collective-permute-start.17 = (bf16[128,256]{1,0:T(8,128)(2,1)S(1)}, bf16[128,256]{1,0:T(8,128)(2,1)S(1)}, u32[]{:S(2)}, u32[]{:S(2)}) collective-permute-start(bf16[128,256]{1,0:T(8,128)(2,1)S(1)} %third.1.own_ref), channel_id=1, source_target_pairs={{0,4},{4,0},{8,12},{12,8},{16,20},{20,16},{24,28},{28,24},{1,5},{5... | collective-permute-start | bytes 196616 | tf_op jit(solution)/shard_map/ppermute | solution.py:93

commit v12 on v10

--- a/solution.py
+++ b/solution.py
@@ -14,11 +14,6 @@
 
 def across(n):
     return list(range(n - 1, 0, -1))
-
-
-def turned(n):
-    first, *rest = across(n)
-    return [first] + rest[::-1]
 
 
 def prepare_kernel(slots, tiles_ref, own_ref, target_ref, wide_ref, held_ref, placing_ref):
@@ -66,9 +61,8 @@
     section, rep = lax.axis_index("section"), lax.axis_index("rep")
     for j in range(count):
         held[j] = block_refs[j][...]
-    steps = zip([0] + across(len(out_refs)), [0] + turned(len(out_refs)))
-    for (j, j_turned), out_ref in zip(steps, out_refs):
-        g = rep ^ jnp.where(section & 1 == 0, j, j_turned)
+    for j, out_ref in zip([0] + across(len(out_refs)), out_refs):
+        g = rep ^ j
         right = jnp.concatenate([held[src_ref[g, k] ^ section] for k in range(depth)], axis=0)
         out_ref[...] = jnp.dot(wide_ref[g], right, preferred_element_type=jnp.float32).astype(
             jnp.bfloat16
@@ -252,10 +246,13 @@
     n = lax.axis_size(axis)
     blocks = [None] * n
     blocks[0] = features
-    for j in range(2, n, 2):
+    order = sorted(range(2, n, 2), key=lambda j: (j & 4, -(j & 2)))
+    for j in order:
         blocks[j] = swap(features, axis, j)
     blocks[1] = swap(features, axis, 1)
-    blocks[2::2], ready = lax.optimization_barrier((blocks[2::2], ready))
+    came, ready = lax.optimization_barrier(([blocks[j] for j in order], ready))
+    for j, block in zip(order, came):
+        blocks[j] = block
     for j in range(2, n, 2):
         blocks[j + 1] = swap(blocks[j], axis, 1)
     return blocks, ready
@@ -271,8 +268,7 @@
     blocks, (wide, own, placing) = gather_blocks(features, "section", (wide, own, placing))
     parts = list(partials(adj_src[:, 0], wide, [own] + blocks[1:]))
     others = across(n_rep)
-    steps = zip(others, turned(n_rep))
-    parts = parts[:1] + [swap_by_core(p, (0, j), (0, k)) for p, (j, k) in zip(parts[1:], steps)]
+    parts = parts[:1] + [swap(part, "rep", j) for part, j in zip(parts[1:], others)]
     same, kept, sent = dense(parts, weight, cotangent, placing)
     came = swap(sent, "section", 1)
     chips = n_section // 2

time: 41.2 us -> 41.5 us (level)
  waiting for transfers between devices: 17 us -> 17.5 us
    ppermute x9 -> x12, waiting for transfers between devices: 6.16 us -> 9.72 us  [swap(): lax.ppermute(value, axis, [(i, i ^ j) for i in range(lax.axis_size(axis))])]
    ppermute x9 -> x6, starting transfers between devices: 11.6 us -> 8.01 us  [swap_by_core(): return lax.ppermute(value, ('section', 'rep'), pairs)]
    ppermute x9 -> x12, starting transfers between devices: 6.48 us -> 9.89 us  [swap(): lax.ppermute(value, axis, [(i, i ^ j) for i in range(lax.axis_size(axis))])]
    ppermute x9 -> x6, waiting for transfers between devices: 10.8 us -> 7.76 us  [swap_by_core(): return lax.ppermute(value, ('section', 'rep'), pairs)]
  transfers between devices with their start and end apart: 18 -> 18, of which waited for: 14 -> 15; matrix products, arithmetic and copies ran while one was open for 0% -> 0% of each run, Pallas kernels for 2% -> 2%
where the time goes in v12:
time: 41.5 us; the launch traced here: 41.3 us
  starting transfers between devices  17.9 us (43%)
  waiting for transfers between devices  17.5 us (42%)
  Pallas kernels  2.65 us (6%)
  local copies, waits for them, and re-layouts  2.55 us (6%)
  between operations  0.73 us (2%)
    ppermute x12, starting transfers between devices, swap(): lax.ppermute(value, axis, [(i, i ^ j) for i in range(lax.axis_size(axis))])  9.89 us
    ppermute x12, waiting for transfers between devices, swap(): lax.ppermute(value, axis, [(i, i ^ j) for i in range(lax.axis_size(axis))])  9.72 us
    ppermute x6, starting transfers between devices, swap_by_core(): return lax.ppermute(value, ('section', 'rep'), pairs)  8.01 us
    ppermute x6, waiting for transfers between devices, swap_by_core(): return lax.ppermute(value, ('section', 'rep'), pairs)  7.76 us
    unnamed x12, local copies, waits for them, and re-layouts  2.55 us
  transfers between devices with their start and end apart: 18, of which 15 were waited for; matrix products, arithmetic and copies ran while one was open for 0% of the time, Pallas kernels for 2%

profile of v12, /device:TPU:0, one launch (start us, length us, event | category | flops | bytes accessed | tf_op | source)
XLA Modules:
  0.0 41.3 jit_solution(16798209551644876862)
XLA Ops:
  0.6 4.1 %collective-permute-start.2 = (bf16[128,256]{1,0:T(8,128)(2,1)}, bf16[128,256]{1,0:T(8,128)(2,1)S(1)}, u32[]{:S(2)}, u32[]{:S(2)}) collective-permute-start(bf16[128,256]{1,0:T(8,128)(2,1)} %own_ref.1), channel_id=1, source_target_pairs={{0,16},{4,20},{8,24},{12,28},{16,0},{20,4},{24,8},{28,12},{1,17},{... | collective-permute-start | bytes 196616 | tf_op jit(solution)/shard_map/ppermute | solution.py:87
  4.7 1.3 %collective-permute-start.1 = (bf16[128,256]{1,0:T(8,128)(2,1)}, bf16[128,256]{1,0:T(8,128)(2,1)S(1)}, u32[]{:S(2)}, u32[]{:S(2)}) collective-permute-start(bf16[128,256]{1,0:T(8,128)(2,1)} %own_ref.1), channel_id=1, source_target_pairs={{0,24},{4,28},{8,16},{12,20},{16,8},{20,12},{24,0},{28,4},{1,25},{... | collective-permute-start | bytes 196616 | tf_op jit(solution)/shard_map/ppermute | solution.py:87
  6.1 0.2 collective-permute-start
  6.3 0.0 collective-permute-start.3
  6.3 0.7 %copy-done.5 = s32[128,1]{0,1:T(1,128)S(1)} copy-done((s32[128,1]{0,1:T(1,128)S(1)}, s32[128,1]{0,1:T(1,128)}, u32[]{:S(2)}) %copy-start.5) | copy-done | bytes 536
  7.0 1.0 %copy-done = bf16[4,1,4,128,128]{4,3,2,1,0:T(8,128)(2,1)S(1)} copy-done((bf16[4,1,4,128,128]{4,3,2,1,0:T(8,128)(2,1)S(1)}, bf16[4,1,4,128,128]{4,3,2,1,0:T(8,128)(2,1)}, u32[]{:S(2)}) %copy-start) | copy-done | bytes 524312
  8.0 0.8 %copy-done.2 = bf16[128,256]{1,0:T(8,128)(2,1)S(1)} copy-done((bf16[128,256]{1,0:T(8,128)(2,1)S(1)}, bf16[128,256]{1,0:T(8,128)(2,1)}, u32[]{:S(2)}) %copy-start.2) | copy-done | bytes 65560
  8.9 0.2 prepare.1
  9.1 0.0 collective-permute-done.2.refs_4_
  9.1 2.1 %collective-permute-done.1.refs_6_ = bf16[128,256]{1,0:T(8,128)(2,1)S(1)} collective-permute-done((bf16[128,256]{1,0:T(8,128)(2,1)}, bf16[128,256]{1,0:T(8,128)(2,1)S(1)}, u32[]{:S(2)}, u32[]{:S(2)}) %collective-permute-start.1) | collective-permute-done | bytes 65568 | tf_op jit(solution)/shard_map/ppermute | solution.py:87
  11.2 0.1 collective-permute-done.refs_2_
  11.3 0.0 collective-permute-start.4
  11.3 0.5 %collective-permute-start.5 = (bf16[128,256]{1,0:T(8,128)(2,1)S(1)}, bf16[128,256]{1,0:T(8,128)(2,1)S(1)}, u32[]{:S(2)}, u32[]{:S(2)}) collective-permute-start(bf16[128,256]{1,0:T(8,128)(2,1)S(1)} %collective-permute-done.2.refs_4_), channel_id=1, source_target_pairs={{0,4},{4,0},{8,12},{12,8},{16,20},{20,16},{24,28},{28,24},{1,5},{5... | collective-permute-start | bytes 196616 | tf_op jit(solution)/shard_map/ppermute | solution.py:87
  11.8 0.0 collective-permute-start.6
  11.8 0.0 collective-permute-done.3.refs_1_
  11.8 0.7 %collective-permute-done.4.refs_3_ = bf16[128,256]{1,0:T(8,128)(2,1)S(1)} collective-permute-done((bf16[128,256]{1,0:T(8,128)(2,1)S(1)}, bf16[128,256]{1,0:T(8,128)(2,1)S(1)}, u32[]{:S(2)}, u32[]{:S(2)}) %collective-permute-start.4) | collective-permute-done | bytes 65568 | tf_op jit(solution)/shard_map/ppermute | solution.py:87
  12.5 0.2 collective-permute-done.5.refs_5_
  12.7 0.4 collective-permute-done.6.refs_7_
  13.0 0.0 copy-done.4
  13.0 0.4 %partials.1 = (bf16[128,256]{1,0:T(8,128)(2,1)S(1)}, bf16[128,256]{1,0:T(8,128)(2,1)S(1)}, bf16[128,256]{1,0:T(8,128)(2,1)S(1)}, bf16[128,256]{1,0:T(8,128)(2,1)S(1)}) custom-call(s32[4,4]{1,0:T(4,128)S(1)} %bitcast.6, bf16[4,128,512]{2,1,0:T(8,128)(2,1)S(1)} %get-tuple-element.32.wide_ref, bf16[128,256]{1,0:T(8,128)(2,1)S(1)} %get-tuple-element.33.refs_0_, ...), custom_call_target="tpu_custom_call" | custom-call | tf_op jit(solution)/shard_map/partials/pallas_call | solution.py:75
  13.5 2.5 %collective-permute-start.7 = (bf16[128,256]{1,0:T(8,128)(2,1)S(1)}, bf16[128,256]{1,0:T(8,128)(2,1)S(1)}, u32[]{:S(2)}, u32[]{:S(2)}) collective-permute-start(bf16[128,256]{1,0:T(8,128)(2,1)S(1)} %get-tuple-element.38), channel_id=1, source_target_pairs={{0,3},{1,2},{2,1},{3,0},{4,7},{5,6},{6,5},{7,4},{8,11},{9,10},{10,... | collective-permute-start | bytes 196616 | tf_op jit(solution)/shard_map/ppermute | solution.py:87
  16.0 0.5 %collective-permute-start.8 = (bf16[128,256]{1,0:T(8,128)(2,1)S(1)}, bf16[128,256]{1,0:T(8,128)(2,1)S(1)}, u32[]{:S(2)}, u32[]{:S(2)}) collective-permute-start(bf16[128,256]{1,0:T(8,128)(2,1)S(1)} %get-tuple-element.39), channel_id=1, source_target_pairs={{0,2},{1,3},{2,0},{3,1},{4,6},{5,7},{6,4},{7,5},{8,10},{9,11},{10,... | collective-permute-start | bytes 196616 | tf_op jit(solution)/shard_map/ppermute | solution.py:87
  16.5 0.5 %collective-permute-start.9 = (bf16[128,256]{1,0:T(8,128)(2,1)S(1)}, bf16[128,256]{1,0:T(8,128)(2,1)S(1)}, u32[]{:S(2)}, u32[]{:S(2)}) collective-permute-start(bf16[128,256]{1,0:T(8,128)(2,1)S(1)} %get-tuple-element.40), channel_id=1, source_target_pairs={{0,1},{1,0},{2,3},{3,2},{4,5},{5,4},{6,7},{7,6},{8,9},{9,8},{10,11... | collective-permute-start | bytes 196616 | tf_op jit(solution)/shard_map/ppermute | solution.py:87
  17.0 1.7 %collective-permute-done.7.refs_1_ = bf16[128,256]{1,0:T(8,128)(2,1)S(1)} collective-permute-done((bf16[128,256]{1,0:T(8,128)(2,1)S(1)}, bf16[128,256]{1,0:T(8,128)(2,1)S(1)}, u32[]{:S(2)}, u32[]{:S(2)}) %collective-permute-start.7) | collective-permute-done | bytes 65568 | tf_op jit(solution)/shard_map/ppermute | solution.py:87
  18.7 1.5 %collective-permute-done.8.refs_2_ = bf16[128,256]{1,0:T(8,128)(2,1)S(1)} collective-permute-done((bf16[128,256]{1,0:T(8,128)(2,1)S(1)}, bf16[128,256]{1,0:T(8,128)(2,1)S(1)}, u32[]{:S(2)}, u32[]{:S(2)}) %collective-permute-start.8) | collective-permute-done | bytes 65568 | tf_op jit(solution)/shard_map/ppermute | solution.py:87
  20.2 0.5 %collective-permute-done.9.refs_3_ = bf16[128,256]{1,0:T(8,128)(2,1)S(1)} collective-permute-done((bf16[128,256]{1,0:T(8,128)(2,1)S(1)}, bf16[128,256]{1,0:T(8,128)(2,1)S(1)}, u32[]{:S(2)}, u32[]{:S(2)}) %collective-permute-start.9) | collective-permute-done | bytes 65568 | tf_op jit(solution)/shard_map/ppermute | solution.py:87
  20.7 0.0 copy-done.3
  20.8 0.4 %dense.1 = (bf16[128,256]{1,0:T(8,128)(2,1)S(1)}, f32[128,256]{1,0:T(8,128)S(1)}, bf16[256,256]{1,0:T(8,128)(2,1)S(1)}) custom-call(bf16[256,256]{1,0:T(8,128)(2,1)S(1)} %copy-done.1, bf16[128,256]{1,0:T(8,128)(2,1)S(1)} %copy-done.3, bf16[256,128]{1,0:T(8,128)(2,1)S(1)} %get-tuple-element.31.placing_ref, bf16[128,256]{1,0:T(8,128)(2,1)S(1)} %get-tuple-element.37.refs_0_, ...), custom_call_target="tpu_custom_call" | custom-call | tf_op jit(solution)/shard_map/dense/pallas_call | solution.py:119
  21.2 0.1 collective-permute-start.10
  21.3 1.3 %collective-permute-done.10.came_ref.refs_1_ = bf16[256,256]{1,0:T(8,128)(2,1)S(1)} collective-permute-done((bf16[256,256]{1,0:T(8,128)(2,1)S(1)}, bf16[256,256]{1,0:T(8,128)(2,1)S(1)}, u32[]{:S(2)}, u32[]{:S(2)}) %collective-permute-start.10) | collective-permute-done | bytes 131104 | tf_op jit(solution)/shard_map/ppermute | solution.py:87
  22.6 3.1 %collective-permute-start.11 = (bf16[192,256]{1,0:T(8,128)(2,1)S(1)}, bf16[192,256]{1,0:T(8,128)(2,1)S(1)}, u32[]{:S(2)}, u32[]{:S(2)}) collective-permute-start(bf16[192,256]{1,0:T(8,128)(2,1)S(1)} %get-tuple-element.45), channel_id=1, source_target_pairs={{0,24},{1,25},{2,26},{3,27},{4,7},{5,6},{6,5},{7,4},{8,16},{9,17},... | collective-permute-start | bytes 294920 | tf_op jit(solution)/shard_map/ppermute | solution.py:242
  25.7 0.0 collective-permute-start.12
  25.7 1.4 %collective-permute-start.13 = (bf16[192,256]{1,0:T(8,128)(2,1)S(1)}, bf16[192,256]{1,0:T(8,128)(2,1)S(1)}, u32[]{:S(2)}, u32[]{:S(2)}) collective-permute-start(bf16[192,256]{1,0:T(8,128)(2,1)S(1)} %get-tuple-element.47), channel_id=1, source_target_pairs={{0,8},{1,9},{2,10},{3,11},{4,5},{5,4},{6,7},{7,6},{8,0},{9,1},{10,... | collective-permute-start | bytes 294920 | tf_op jit(solution)/shard_map/ppermute | solution.py:242
  27.1 2.0 %collective-permute-done.11.refs_0_ = bf16[192,256]{1,0:T(8,128)(2,1)S(1)} collective-permute-done((bf16[192,256]{1,0:T(8,128)(2,1)S(1)}, bf16[192,256]{1,0:T(8,128)(2,1)S(1)}, u32[]{:S(2)}, u32[]{:S(2)}) %collective-permute-start.11) | collective-permute-done | bytes 98336 | tf_op jit(solution)/shard_map/ppermute | solution.py:242
  29.1 2.8 %collective-permute-done.12.refs_1_ = bf16[192,256]{1,0:T(8,128)(2,1)S(1)} collective-permute-done((bf16[192,256]{1,0:T(8,128)(2,1)S(1)}, bf16[192,256]{1,0:T(8,128)(2,1)S(1)}, u32[]{:S(2)}, u32[]{:S(2)}) %collective-permute-start.12) | collective-permute-done | bytes 98336 | tf_op jit(solution)/shard_map/ppermute | solution.py:242
  32.0 0.0 collective-permute-done.13.refs_2_
  32.0 0.1 second.1
  32.0 1.6 %collective-permute-start.14 = (bf16[192,256]{1,0:T(8,128)(2,1)S(1)}, bf16[192,256]{1,0:T(8,128)(2,1)S(1)}, u32[]{:S(2)}, u32[]{:S(2)}) collective-permute-start(bf16[192,256]{1,0:T(8,128)(2,1)S(1)} %get-tuple-element.49), channel_id=1, source_target_pairs={{0,3},{1,2},{2,1},{3,0},{4,28},{5,29},{6,30},{7,31},{8,11},{9,10},... | collective-permute-start | bytes 294920 | tf_op jit(solution)/shard_map/ppermute | solution.py:242
  33.6 0.8 %collective-permute-start.15 = (bf16[192,256]{1,0:T(8,128)(2,1)S(1)}, bf16[192,256]{1,0:T(8,128)(2,1)S(1)}, u32[]{:S(2)}, u32[]{:S(2)}) collective-permute-start(bf16[192,256]{1,0:T(8,128)(2,1)S(1)} %get-tuple-element.50), channel_id=1, source_target_pairs={{0,2},{1,3},{2,0},{3,1},{4,20},{5,21},{6,22},{7,23},{8,10},{9,11},... | collective-permute-start | bytes 294920 | tf_op jit(solution)/shard_map/ppermute | solution.py:242
  34.4 1.2 %collective-permute-start.16 = (bf16[192,256]{1,0:T(8,128)(2,1)S(1)}, bf16[192,256]{1,0:T(8,128)(2,1)S(1)}, u32[]{:S(2)}, u32[]{:S(2)}) collective-permute-start(bf16[192,256]{1,0:T(8,128)(2,1)S(1)} %get-tuple-element.51), channel_id=1, source_target_pairs={{0,1},{1,0},{2,3},{3,2},{4,12},{5,13},{6,14},{7,15},{8,9},{9,8},{1... | collective-permute-start | bytes 294920 | tf_op jit(solution)/shard_map/ppermute | solution.py:242
  35.6 0.7 %store.2._ = bf16[8,32,256]{2,1,0:T(8,128)(2,1)} custom-call(bf16[128,256]{1,0:T(8,128)(2,1)S(1)} %get-tuple-element.41.same_ref.refs_0_, bf16[256,256]{1,0:T(8,128)(2,1)S(1)} %collective-permute-done.10.came_ref.refs_1_, bf16[192,256]{1,0:T(8,128)(2,1)S(1)} %collective-permute-done.11.refs_0_, bf16[192,256]{1,0:T(8,128)(2,1)S(1)} %collective-permute-done.12.refs_1_, ...), custom_call_target="tpu_custom_call" | custom-call | tf_op jit(solution)/shard_map/store/pallas_call | solution.py:206
  36.3 1.4 %collective-permute-done.14.refs_0_.refs_2_ = bf16[192,256]{1,0:T(8,128)(2,1)S(1)} collective-permute-done((bf16[192,256]{1,0:T(8,128)(2,1)S(1)}, bf16[192,256]{1,0:T(8,128)(2,1)S(1)}, u32[]{:S(2)}, u32[]{:S(2)}) %collective-permute-start.14) | collective-permute-done | bytes 98336 | tf_op jit(solution)/shard_map/ppermute | solution.py:242
  37.7 1.0 %collective-permute-done.15.refs_1_.refs_3_ = bf16[192,256]{1,0:T(8,128)(2,1)S(1)} collective-permute-done((bf16[192,256]{1,0:T(8,128)(2,1)S(1)}, bf16[192,256]{1,0:T(8,128)(2,1)S(1)}, u32[]{:S(2)}, u32[]{:S(2)}) %collective-permute-start.15) | collective-permute-done | bytes 98336 | tf_op jit(solution)/shard_map/ppermute | solution.py:242
  38.7 0.5 %collective-permute-done.16.refs_2_.refs_4_ = bf16[192,256]{1,0:T(8,128)(2,1)S(1)} collective-permute-done((bf16[192,256]{1,0:T(8,128)(2,1)S(1)}, bf16[192,256]{1,0:T(8,128)(2,1)S(1)}, u32[]{:S(2)}, u32[]{:S(2)}) %collective-permute-start.16) | collective-permute-done | bytes 98336 | tf_op jit(solution)/shard_map/ppermute | solution.py:242
  39.2 0.1 third.1.own_ref
  39.3 0.1 collective-permute-start.17
  39.3 1.2 %collective-permute-done.17.came_ref = bf16[128,256]{1,0:T(8,128)(2,1)S(1)} collective-permute-done((bf16[128,256]{1,0:T(8,128)(2,1)S(1)}, bf16[128,256]{1,0:T(8,128)(2,1)S(1)}, u32[]{:S(2)}, u32[]{:S(2)}) %collective-permute-start.17) | collective-permute-done | bytes 65568 | tf_op jit(solution)/shard_map/ppermute | solution.py:87
  40.6 0.7 %finish.1 = f32[2,128,256]{2,1,0:T(8,128)} custom-call(bf16[128,256]{1,0:T(8,128)(2,1)S(1)} %third.1.own_ref, bf16[128,256]{1,0:T(8,128)(2,1)S(1)} %collective-permute-done.17.came_ref), custom_call_target="tpu_custom_call" | custom-call | tf_op jit(solution)/shard_map/finish/pallas_call | solution.py:225
  (9 shorter events, 0.1 us)
Async XLA Ops:
  0.6 8.5 %collective-permute-start.2 = (bf16[128,256]{1,0:T(8,128)(2,1)}, bf16[128,256]{1,0:T(8,128)(2,1)S(1)}, u32[]{:S(2)}, u32[]{:S(2)}) collective-permute-start(bf16[128,256]{1,0:T(8,128)(2,1)} %own_ref.1), channel_id=1, source_target_pairs={{0,16},{4,20},{8,24},{12,28},{16,0},{20,4},{24,8},{28,12},{1,17},{... | collective-permute-start | bytes 196616 | tf_op jit(solution)/shard_map/ppermute | solution.py:87
  4.7 6.4 %collective-permute-start.1 = (bf16[128,256]{1,0:T(8,128)(2,1)}, bf16[128,256]{1,0:T(8,128)(2,1)S(1)}, u32[]{:S(2)}, u32[]{:S(2)}) collective-permute-start(bf16[128,256]{1,0:T(8,128)(2,1)} %own_ref.1), channel_id=1, source_target_pairs={{0,24},{4,28},{8,16},{12,20},{16,8},{20,12},{24,0},{28,4},{1,25},{... | collective-permute-start | bytes 196616 | tf_op jit(solution)/shard_map/ppermute | solution.py:87
  6.1 5.2 %collective-permute-start = (bf16[128,256]{1,0:T(8,128)(2,1)}, bf16[128,256]{1,0:T(8,128)(2,1)S(1)}, u32[]{:S(2)}, u32[]{:S(2)}) collective-permute-start(bf16[128,256]{1,0:T(8,128)(2,1)} %own_ref.1), channel_id=1, source_target_pairs={{0,8},{4,12},{8,0},{12,4},{16,24},{20,28},{24,16},{28,20},{1,9},{5... | collective-permute-start | bytes 196616 | tf_op jit(solution)/shard_map/ppermute | solution.py:87
  6.3 5.5 %collective-permute-start.3 = (bf16[128,256]{1,0:T(8,128)(2,1)}, bf16[128,256]{1,0:T(8,128)(2,1)S(1)}, u32[]{:S(2)}, u32[]{:S(2)}) collective-permute-start(bf16[128,256]{1,0:T(8,128)(2,1)} %own_ref.1), channel_id=1, source_target_pairs={{0,4},{4,0},{8,12},{12,8},{16,20},{20,16},{24,28},{28,24},{1,5},{5... | collective-permute-start | bytes 196616 | tf_op jit(solution)/shard_map/ppermute | solution.py:87
  6.3 0.7 %copy-start.5 = (s32[128,1]{0,1:T(1,128)S(1)}, s32[128,1]{0,1:T(1,128)}, u32[]{:S(2)}) copy-start(s32[128,1]{0,1:T(1,128)} %param.11) | copy-start | bytes 1540
  7.0 1.0 %copy-start = (bf16[4,1,4,128,128]{4,3,2,1,0:T(8,128)(2,1)S(1)}, bf16[4,1,4,128,128]{4,3,2,1,0:T(8,128)(2,1)}, u32[]{:S(2)}) copy-start(bf16[4,1,4,128,128]{4,3,2,1,0:T(8,128)(2,1)} %param.7) | copy-start | bytes 1572868
  8.0 0.8 %copy-start.2 = (bf16[128,256]{1,0:T(8,128)(2,1)S(1)}, bf16[128,256]{1,0:T(8,128)(2,1)}, u32[]{:S(2)}) copy-start(bf16[128,256]{1,0:T(8,128)(2,1)} %own_ref.1) | copy-start | bytes 196612
  11.3 1.8 %copy-start.4 = (s32[4,1,4]{2,1,0:T(1,128)S(1)}, s32[4,1,4]{2,1,0:T(1,128)}, u32[]{:S(2)}) copy-start(s32[4,1,4]{2,1,0:T(1,128)} %param.8) | copy-start | bytes 196
  11.3 1.3 %collective-permute-start.4 = (bf16[128,256]{1,0:T(8,128)(2,1)S(1)}, bf16[128,256]{1,0:T(8,128)(2,1)S(1)}, u32[]{:S(2)}, u32[]{:S(2)}) collective-permute-start(bf16[128,256]{1,0:T(8,128)(2,1)S(1)} %collective-permute-done.refs_2_), channel_id=1, source_target_pairs={{0,4},{4,0},{8,12},{12,8},{16,20},{20,16},{24,28},{28,24},{1,5},{5... | collective-permute-start | bytes 196616 | tf_op jit(solution)/shard_map/ppermute | solution.py:87
  11.3 1.4 %collective-permute-start.5 = (bf16[128,256]{1,0:T(8,128)(2,1)S(1)}, bf16[128,256]{1,0:T(8,128)(2,1)S(1)}, u32[]{:S(2)}, u32[]{:S(2)}) collective-permute-start(bf16[128,256]{1,0:T(8,128)(2,1)S(1)} %collective-permute-done.2.refs_4_), channel_id=1, source_target_pairs={{0,4},{4,0},{8,12},{12,8},{16,20},{20,16},{24,28},{28,24},{1,5},{5... | collective-permute-start | bytes 196616 | tf_op jit(solution)/shard_map/ppermute | solution.py:87
  11.8 1.3 %collective-permute-start.6 = (bf16[128,256]{1,0:T(8,128)(2,1)S(1)}, bf16[128,256]{1,0:T(8,128)(2,1)S(1)}, u32[]{:S(2)}, u32[]{:S(2)}) collective-permute-start(bf16[128,256]{1,0:T(8,128)(2,1)S(1)} %collective-permute-done.1.refs_6_), channel_id=1, source_target_pairs={{0,4},{4,0},{8,12},{12,8},{16,20},{20,16},{24,28},{28,24},{1,5},{5... | collective-permute-start | bytes 196616 | tf_op jit(solution)/shard_map/ppermute | solution.py:87
  13.0 7.7 %copy-start.1 = (bf16[256,256]{1,0:T(8,128)(2,1)S(1)}, bf16[256,256]{1,0:T(8,128)(2,1)}, u32[]{:S(2)}) copy-start(bf16[256,256]{1,0:T(8,128)(2,1)} %weight_ref.1) | copy-start | bytes 393220
  13.0 7.7 %copy-start.3 = (bf16[128,256]{1,0:T(8,128)(2,1)S(1)}, bf16[128,256]{1,0:T(8,128)(2,1)}, u32[]{:S(2)}) copy-start(bf16[128,256]{1,0:T(8,128)(2,1)} %cot_ref.1) | copy-start | bytes 196612
  13.5 5.3 %collective-permute-start.7 = (bf16[128,256]{1,0:T(8,128)(2,1)S(1)}, bf16[128,256]{1,0:T(8,128)(2,1)S(1)}, u32[]{:S(2)}, u32[]{:S(2)}) collective-permute-start(bf16[128,256]{1,0:T(8,128)(2,1)S(1)} %get-tuple-element.38), channel_id=1, source_target_pairs={{0,3},{1,2},{2,1},{3,0},{4,7},{5,6},{6,5},{7,4},{8,11},{9,10},{10,... | collective-permute-start | bytes 196616 | tf_op jit(solution)/shard_map/ppermute | solution.py:87
  16.0 4.3 %collective-permute-start.8 = (bf16[128,256]{1,0:T(8,128)(2,1)S(1)}, bf16[128,256]{1,0:T(8,128)(2,1)S(1)}, u32[]{:S(2)}, u32[]{:S(2)}) collective-permute-start(bf16[128,256]{1,0:T(8,128)(2,1)S(1)} %get-tuple-element.39), channel_id=1, source_target_pairs={{0,2},{1,3},{2,0},{3,1},{4,6},{5,7},{6,4},{7,5},{8,10},{9,11},{10,... | collective-permute-start | bytes 196616 | tf_op jit(solution)/shard_map/ppermute | solution.py:87
  16.5 4.3 %collective-permute-start.9 = (bf16[128,256]{1,0:T(8,128)(2,1)S(1)}, bf16[128,256]{1,0:T(8,128)(2,1)S(1)}, u32[]{:S(2)}, u32[]{:S(2)}) collective-permute-start(bf16[128,256]{1,0:T(8,128)(2,1)S(1)} %get-tuple-element.40), channel_id=1, source_target_pairs={{0,1},{1,0},{2,3},{3,2},{4,5},{5,4},{6,7},{7,6},{8,9},{9,8},{10,11... | collective-permute-start | bytes 196616 | tf_op jit(solution)/shard_map/ppermute | solution.py:87
  21.2 1.4 %collective-permute-start.10 = (bf16[256,256]{1,0:T(8,128)(2,1)S(1)}, bf16[256,256]{1,0:T(8,128)(2,1)S(1)}, u32[]{:S(2)}, u32[]{:S(2)}) collective-permute-start(bf16[256,256]{1,0:T(8,128)(2,1)S(1)} %get-tuple-element.42), channel_id=1, source_target_pairs={{0,4},{4,0},{8,12},{12,8},{16,20},{20,16},{24,28},{28,24},{1,5},{5... | collective-permute-start | bytes 393224 | tf_op jit(solution)/shard_map/ppermute | solution.py:87
  22.6 6.5 %collective-permute-start.11 = (bf16[192,256]{1,0:T(8,128)(2,1)S(1)}, bf16[192,256]{1,0:T(8,128)(2,1)S(1)}, u32[]{:S(2)}, u32[]{:S(2)}) collective-permute-start(bf16[192,256]{1,0:T(8,128)(2,1)S(1)} %get-tuple-element.45), channel_id=1, source_target_pairs={{0,24},{1,25},{2,26},{3,27},{4,7},{5,6},{6,5},{7,4},{8,16},{9,17},... | collective-permute-start | bytes 294920 | tf_op jit(solution)/shard_map/ppermute | solution.py:242
  25.7 6.3 %collective-permute-start.12 = (bf16[192,256]{1,0:T(8,128)(2,1)S(1)}, bf16[192,256]{1,0:T(8,128)(2,1)S(1)}, u32[]{:S(2)}, u32[]{:S(2)}) collective-permute-start(bf16[192,256]{1,0:T(8,128)(2,1)S(1)} %get-tuple-element.46), channel_id=1, source_target_pairs={{0,16},{1,17},{2,18},{3,19},{4,6},{5,7},{6,4},{7,5},{8,24},{9,25},... | collective-permute-start | bytes 294920 | tf_op jit(solution)/shard_map/ppermute | solution.py:242
  25.7 6.3 %collective-permute-start.13 = (bf16[192,256]{1,0:T(8,128)(2,1)S(1)}, bf16[192,256]{1,0:T(8,128)(2,1)S(1)}, u32[]{:S(2)}, u32[]{:S(2)}) collective-permute-start(bf16[192,256]{1,0:T(8,128)(2,1)S(1)} %get-tuple-element.47), channel_id=1, source_target_pairs={{0,8},{1,9},{2,10},{3,11},{4,5},{5,4},{6,7},{7,6},{8,0},{9,1},{10,... | collective-permute-start | bytes 294920 | tf_op jit(solution)/shard_map/ppermute | solution.py:242
  32.0 5.6 %collective-permute-start.14 = (bf16[192,256]{1,0:T(8,128)(2,1)S(1)}, bf16[192,256]{1,0:T(8,128)(2,1)S(1)}, u32[]{:S(2)}, u32[]{:S(2)}) collective-permute-start(bf16[192,256]{1,0:T(8,128)(2,1)S(1)} %get-tuple-element.49), channel_id=1, source_target_pairs={{0,3},{1,2},{2,1},{3,0},{4,28},{5,29},{6,30},{7,31},{8,11},{9,10},... | collective-permute-start | bytes 294920 | tf_op jit(solution)/shard_map/ppermute | solution.py:242
  33.6 5.1 %collective-permute-start.15 = (bf16[192,256]{1,0:T(8,128)(2,1)S(1)}, bf16[192,256]{1,0:T(8,128)(2,1)S(1)}, u32[]{:S(2)}, u32[]{:S(2)}) collective-permute-start(bf16[192,256]{1,0:T(8,128)(2,1)S(1)} %get-tuple-element.50), channel_id=1, source_target_pairs={{0,2},{1,3},{2,0},{3,1},{4,20},{5,21},{6,22},{7,23},{8,10},{9,11},... | collective-permute-start | bytes 294920 | tf_op jit(solution)/shard_map/ppermute | solution.py:242
  34.4 4.8 %collective-permute-start.16 = (bf16[192,256]{1,0:T(8,128)(2,1)S(1)}, bf16[192,256]{1,0:T(8,128)(2,1)S(1)}, u32[]{:S(2)}, u32[]{:S(2)}) collective-permute-start(bf16[192,256]{1,0:T(8,128)(2,1)S(1)} %get-tuple-element.51), channel_id=1, source_target_pairs={{0,1},{1,0},{2,3},{3,2},{4,12},{5,13},{6,14},{7,15},{8,9},{9,8},{1... | collective-permute-start | bytes 294920 | tf_op jit(solution)/shard_map/ppermute | solution.py:242
  39.3 1.3 %collective-permute-start.17 = (bf16[128,256]{1,0:T(8,128)(2,1)S(1)}, bf16[128,256]{1,0:T(8,128)(2,1)S(1)}, u32[]{:S(2)}, u32[]{:S(2)}) collective-permute-start(bf16[128,256]{1,0:T(8,128)(2,1)S(1)} %third.1.own_ref), channel_id=1, source_target_pairs={{0,4},{4,0},{8,12},{12,8},{16,20},{20,16},{24,28},{28,24},{1,5},{5... | collective-permute-start | bytes 196616 | tf_op jit(solution)/shard_map/ppermute | solution.py:87

commit v13 on v12

--- a/solution.py
+++ b/solution.py
@@ -14,6 +14,10 @@
 
 def across(n):
     return list(range(n - 1, 0, -1))
+
+
+def place_of_chip():
+    return lax.axis_index("section") >> 1, lax.axis_size("section") // 2
 
 
 def prepare_kernel(slots, tiles_ref, own_ref, target_ref, wide_ref, held_ref, placing_ref):
@@ -32,8 +36,11 @@
     earlier = jnp.where(earlier, 1.0, 0.0).astype(jnp.bfloat16)
     before = jnp.dot(hits.astype(jnp.bfloat16), earlier, preferred_element_type=jnp.float32)
     slot = jnp.sum(before * hits, axis=0, keepdims=True).astype(jnp.int32)
-    apart = target ^ lax.axis_index("section")
-    position = ((apart & 1) * (n_section // 2) + (apart >> 1)) * slots + slot
+    chip, chips = place_of_chip()
+    apart = (target >> 1) - chip
+    apart = jnp.where(apart < 0, apart + chips, apart)
+    other_core = (target ^ lax.axis_index("section")) & 1
+    position = (other_core * chips + apart) * slots + slot
     placing = lax.broadcasted_iota(jnp.int32, (places, rows), 0) == position
     placing_ref[...] = jnp.where(placing, 1.0, 0.0).astype(jnp.bfloat16)
 
@@ -132,21 +139,30 @@
 
 
 def write_messages(slots, same_ref, came_ref, half, out_refs):
-    for ref, j in zip(out_refs, across(len(out_refs) + 1)):
-        start = j * slots % same_ref.shape[0]
+    for i, ref in enumerate(out_refs):
+        start = (i + 1) * slots % same_ref.shape[0]
         ref[:slots] = same_ref[start : start + slots]
         ref[slots : 2 * slots] = came_ref[start : start + slots]
         ref[2 * slots :] = half
 
 
-def sum_halves(half_ref, slots, own_ref, message_refs, counts):
-    by_xor = [own_ref[...].astype(jnp.float32)]
-    by_xor += [ref[2 * slots :].astype(jnp.float32) for ref in message_refs[::-1]]
-    for core in range(2):
-
-        @pl.when(lax.axis_index("section") & 1 == core)
-        def _():
-            half_ref[...] = tree_sum(by_xor[: counts[core]]).astype(jnp.bfloat16)
+def sum_halves(half_ref, held, slots, own_ref, message_refs, core_along, n_rep):
+    chip, chips = place_of_chip()
+    core = lax.axis_index("section") & 1
+
+    @pl.when(core == core_along)
+    def _():
+        held[chip] = own_ref[...]
+        for i, ref in enumerate(message_refs[: chips - 1]):
+            held[(chip + chips - i - 1) % chips] = ref[2 * slots :]
+        total = tree_sum([held[c].astype(jnp.float32) for c in range(chips)])
+        half_ref[...] = total.astype(jnp.bfloat16)
+
+    @pl.when(core != core_along)
+    def _():
+        by_xor = [own_ref[...].astype(jnp.float32)]
+        by_xor += [ref[2 * slots :].astype(jnp.float32) for ref in message_refs[::-1]]
+        half_ref[...] = tree_sum(by_xor[:n_rep]).astype(jnp.bfloat16)
 
 
 def first_kernel(slots, same_ref, kept_ref, came_ref, half_ref, *out_refs):
@@ -156,17 +172,17 @@
     write_messages(slots, same_ref, came_ref, half_ref[...], out_refs)
 
 
-def second_kernel(slots, counts, many, same_ref, came_ref, own_ref, *refs):
-    message_refs, half_ref, out_refs = refs[:many], refs[many], refs[many + 1 :]
-    sum_halves(half_ref, slots, own_ref, message_refs, counts)
+def second_kernel(slots, n_rep, many, same_ref, came_ref, own_ref, *refs):
+    message_refs, half_ref, out_refs, held = refs[:many], refs[many], refs[many + 1 : -1], refs[-1]
+    sum_halves(half_ref, held, slots, own_ref, message_refs, 0, n_rep)
     write_messages(slots, same_ref, came_ref, half_ref[...], out_refs)
 
 
-def third_kernel(slots, counts, own_ref, *refs):
-    sum_halves(refs[-1], slots, own_ref, refs[:-1], counts)
-
-
-def call_halves(kernel, name, operands, half, slots, many):
+def third_kernel(slots, n_rep, own_ref, *refs):
+    sum_halves(refs[-2], refs[-1], slots, own_ref, refs[:-2], 1, n_rep)
+
+
+def call_halves(kernel, name, operands, half, slots, many, held=()):
     shapes = [jax.ShapeDtypeStruct(half, jnp.bfloat16)]
     shapes += [jax.ShapeDtypeStruct((2 * slots + half[0], half[1]), jnp.bfloat16)] * many
     return pl.pallas_call(
@@ -174,6 +190,7 @@
         out_shape=shapes,
         in_specs=[VMEM] * len(operands),
         out_specs=[VMEM] * len(shapes),
+        scratch_shapes=[pltpu.VMEM(shape, jnp.bfloat16) for shape in held],
         compiler_params=LIMIT,
         name=name,
     )(*operands)
@@ -182,16 +199,16 @@
 def store_kernel(core, slots, same_ref, came_ref, *refs):
     message_refs, (out_ref, rows, sem) = refs[:-3], refs[-3:]
     section = lax.axis_index("section")
-    chips = lax.axis_size("section") // 2
+    chip, chips = place_of_chip()
 
     @pl.when(section & 1 == core)
     def _():
         rows[section] = same_ref[:slots]
         rows[section ^ 1] = came_ref[:slots]
-        for ref, j in zip(message_refs, across(len(message_refs) + 1)):
-            if j < chips:
-                rows[section ^ (2 * j)] = ref[:slots]
-                rows[section ^ (2 * j + 1)] = ref[slots : 2 * slots]
+        for i, ref in enumerate(message_refs[: chips - 1]):
+            source = 2 * ((chip + chips - i - 1) % chips)
+            rows[source + core] = ref[:slots]
+            rows[source + 1 - core] = ref[slots : 2 * slots]
         copy = pltpu.make_async_copy(rows, out_ref, sem)
         copy.start()
         copy.wait()
@@ -232,13 +249,14 @@
     )(own, came)
 
 
-def swap_by_core(value, first, second):
+def exchange(value, core_along, shift, j):
     n_section, n_rep = lax.axis_size("section"), lax.axis_size("rep")
     pairs = []
     for s in range(n_section):
-        chip, rep = second if s & 1 else first
+        along = s & 1 == core_along
+        to = (s + 2 * shift) % n_section if along else s
         for r in range(n_rep):
-            pairs.append((s * n_rep + r, (s ^ 2 * chip % n_section) * n_rep + (r ^ rep % n_rep)))
+            pairs.append((s * n_rep + r, to * n_rep + (r if along else r ^ j % n_rep)))
     return lax.ppermute(value, ("section", "rep"), pairs)
 
 
@@ -274,22 +292,24 @@
     chips = n_section // 2
     steps = across(max(n_rep, chips))
     half_shape = (width // 2, width)
+    held = [(chips,) + half_shape]
     half, *first = call_halves(
         functools.partial(first_kernel, slots), "first", [same, kept, came], half_shape, slots, len(steps)
     )
-    first = [swap_by_core(m, (j, 0), (0, j)) for m, j in zip(first, steps)]
+    first = [exchange(m, 0, i + 1, j) for i, (m, j) in enumerate(zip(first, steps))]
     relaid = store(0, same, came, first, n_section, slots)
     half, *second = call_halves(
-        functools.partial(second_kernel, slots, (chips, n_rep), len(steps)),
+        functools.partial(second_kernel, slots, n_rep, len(steps)),
         "second",
         [same, came, half, *first],
         half_shape,
         slots,
         len(steps),
-    )
-    second = [swap_by_core(m, (0, j), (j, 0)) for m, j in zip(second, steps)]
+        held,
+    )
+    second = [exchange(m, 1, i + 1, j) for i, (m, j) in enumerate(zip(second, steps))]
     (half,) = call_halves(
-        functools.partial(third_kernel, slots, (n_rep, chips)), "third", [half, *second], half_shape, slots, 0
+        functools.partial(third_kernel, slots, n_rep), "third", [half, *second], half_shape, slots, 0, held
     )
     relaid = store(1, same, came, second, n_section, slots, relaid)
     half, relaid = lax.optimization_barrier((half, relaid))

time: 41.5 us -> 40.6 us (0.978)
  waiting for transfers between devices: 17.5 us -> 15.4 us
  starting transfers between devices: 17.9 us -> 19.1 us
    ppermute x6, waiting for transfers between devices: 7.76 us -> 5.67 us  [exchange(): return lax.ppermute(value, ('section', 'rep'), pairs)]
    ppermute x6, starting transfers between devices: 8.01 us -> 9.2 us  [exchange(): return lax.ppermute(value, ('section', 'rep'), pairs)]
  transfers between devices with their start and end apart: 18 -> 18, of which waited for: 15 -> 16; matrix products, arithmetic and copies ran while one was open for 0% -> 0% of each run, Pallas kernels for 2% -> 2%
where the time goes in v13:
time: 40.6 us; the launch traced here: 40.4 us
  starting transfers between devices  19.1 us (47%)
  waiting for transfers between devices  15.4 us (38%)
  Pallas kernels  2.67 us (7%)
  local copies, waits for them, and re-layouts  2.55 us (6%)
  between operations  0.73 us (2%)
    ppermute x12, starting transfers between devices, swap(): lax.ppermute(value, axis, [(i, i ^ j) for i in range(lax.axis_size(axis))])  9.89 us
    ppermute x12, waiting for transfers between devices, swap(): lax.ppermute(value, axis, [(i, i ^ j) for i in range(lax.axis_size(axis))])  9.72 us
    ppermute x6, starting transfers between devices, exchange(): return lax.ppermute(value, ('section', 'rep'), pairs)  9.2 us
    ppermute x6, waiting for transfers between devices, exchange(): return lax.ppermute(value, ('section', 'rep'), pairs)  5.67 us
    unnamed x12, local copies, waits for them, and re-layouts  2.55 us
  transfers between devices with their start and end apart: 18, of which 16 were waited for; matrix products, arithmetic and copies ran while one was open for 0% of the time, Pallas kernels for 2%

profile of v13, /device:TPU:0, one launch (start us, length us, event | category | flops | bytes accessed | tf_op | source)
XLA Modules:
  0.0 40.4 jit_solution(3152796964993778789)
XLA Ops:
  0.6 4.1 %collective-permute-start.2 = (bf16[128,256]{1,0:T(8,128)(2,1)}, bf16[128,256]{1,0:T(8,128)(2,1)S(1)}, u32[]{:S(2)}, u32[]{:S(2)}) collective-permute-start(bf16[128,256]{1,0:T(8,128)(2,1)} %own_ref.1), channel_id=1, source_target_pairs={{0,16},{4,20},{8,24},{12,28},{16,0},{20,4},{24,8},{28,12},{1,17},{... | collective-permute-start | bytes 196616 | tf_op jit(solution)/shard_map/ppermute | solution.py:94
  4.7 1.3 %collective-permute-start.1 = (bf16[128,256]{1,0:T(8,128)(2,1)}, bf16[128,256]{1,0:T(8,128)(2,1)S(1)}, u32[]{:S(2)}, u32[]{:S(2)}) collective-permute-start(bf16[128,256]{1,0:T(8,128)(2,1)} %own_ref.1), channel_id=1, source_target_pairs={{0,24},{4,28},{8,16},{12,20},{16,8},{20,12},{24,0},{28,4},{1,25},{... | collective-permute-start | bytes 196616 | tf_op jit(solution)/shard_map/ppermute | solution.py:94
  6.1 0.2 collective-permute-start
  6.3 0.0 collective-permute-start.3
  6.3 0.7 %copy-done.5 = s32[128,1]{0,1:T(1,128)S(1)} copy-done((s32[128,1]{0,1:T(1,128)S(1)}, s32[128,1]{0,1:T(1,128)}, u32[]{:S(2)}) %copy-start.5) | copy-done | bytes 536
  7.0 1.0 %copy-done = bf16[4,1,4,128,128]{4,3,2,1,0:T(8,128)(2,1)S(1)} copy-done((bf16[4,1,4,128,128]{4,3,2,1,0:T(8,128)(2,1)S(1)}, bf16[4,1,4,128,128]{4,3,2,1,0:T(8,128)(2,1)}, u32[]{:S(2)}) %copy-start) | copy-done | bytes 524312
  8.0 0.8 %copy-done.2 = bf16[128,256]{1,0:T(8,128)(2,1)S(1)} copy-done((bf16[128,256]{1,0:T(8,128)(2,1)S(1)}, bf16[128,256]{1,0:T(8,128)(2,1)}, u32[]{:S(2)}) %copy-start.2) | copy-done | bytes 65560
  8.9 0.2 prepare.1
  9.1 0.0 collective-permute-done.2.refs_4_
  9.1 2.1 %collective-permute-done.1.refs_6_ = bf16[128,256]{1,0:T(8,128)(2,1)S(1)} collective-permute-done((bf16[128,256]{1,0:T(8,128)(2,1)}, bf16[128,256]{1,0:T(8,128)(2,1)S(1)}, u32[]{:S(2)}, u32[]{:S(2)}) %collective-permute-start.1) | collective-permute-done | bytes 65568 | tf_op jit(solution)/shard_map/ppermute | solution.py:94
  11.2 0.1 collective-permute-done.refs_2_
  11.3 0.0 collective-permute-start.4
  11.3 0.5 %collective-permute-start.5 = (bf16[128,256]{1,0:T(8,128)(2,1)S(1)}, bf16[128,256]{1,0:T(8,128)(2,1)S(1)}, u32[]{:S(2)}, u32[]{:S(2)}) collective-permute-start(bf16[128,256]{1,0:T(8,128)(2,1)S(1)} %collective-permute-done.2.refs_4_), channel_id=1, source_target_pairs={{0,4},{4,0},{8,12},{12,8},{16,20},{20,16},{24,28},{28,24},{1,5},{5... | collective-permute-start | bytes 196616 | tf_op jit(solution)/shard_map/ppermute | solution.py:94
  11.8 0.0 collective-permute-start.6
  11.8 0.0 collective-permute-done.3.refs_1_
  11.8 0.7 %collective-permute-done.4.refs_3_ = bf16[128,256]{1,0:T(8,128)(2,1)S(1)} collective-permute-done((bf16[128,256]{1,0:T(8,128)(2,1)S(1)}, bf16[128,256]{1,0:T(8,128)(2,1)S(1)}, u32[]{:S(2)}, u32[]{:S(2)}) %collective-permute-start.4) | collective-permute-done | bytes 65568 | tf_op jit(solution)/shard_map/ppermute | solution.py:94
  12.5 0.2 collective-permute-done.5.refs_5_
  12.7 0.4 collective-permute-done.6.refs_7_
  13.0 0.0 copy-done.4
  13.0 0.4 %partials.1 = (bf16[128,256]{1,0:T(8,128)(2,1)S(1)}, bf16[128,256]{1,0:T(8,128)(2,1)S(1)}, bf16[128,256]{1,0:T(8,128)(2,1)S(1)}, bf16[128,256]{1,0:T(8,128)(2,1)S(1)}) custom-call(s32[4,4]{1,0:T(4,128)S(1)} %bitcast.6, bf16[4,128,512]{2,1,0:T(8,128)(2,1)S(1)} %get-tuple-element.32.wide_ref, bf16[128,256]{1,0:T(8,128)(2,1)S(1)} %get-tuple-element.33.refs_0_, ...), custom_call_target="tpu_custom_call" | custom-call | tf_op jit(solution)/shard_map/partials/pallas_call | solution.py:82
  13.5 2.5 %collective-permute-start.7 = (bf16[128,256]{1,0:T(8,128)(2,1)S(1)}, bf16[128,256]{1,0:T(8,128)(2,1)S(1)}, u32[]{:S(2)}, u32[]{:S(2)}) collective-permute-start(bf16[128,256]{1,0:T(8,128)(2,1)S(1)} %get-tuple-element.38), channel_id=1, source_target_pairs={{0,3},{1,2},{2,1},{3,0},{4,7},{5,6},{6,5},{7,4},{8,11},{9,10},{10,... | collective-permute-start | bytes 196616 | tf_op jit(solution)/shard_map/ppermute | solution.py:94
  16.0 0.5 %collective-permute-start.8 = (bf16[128,256]{1,0:T(8,128)(2,1)S(1)}, bf16[128,256]{1,0:T(8,128)(2,1)S(1)}, u32[]{:S(2)}, u32[]{:S(2)}) collective-permute-start(bf16[128,256]{1,0:T(8,128)(2,1)S(1)} %get-tuple-element.39), channel_id=1, source_target_pairs={{0,2},{1,3},{2,0},{3,1},{4,6},{5,7},{6,4},{7,5},{8,10},{9,11},{10,... | collective-permute-start | bytes 196616 | tf_op jit(solution)/shard_map/ppermute | solution.py:94
  16.5 0.5 %collective-permute-start.9 = (bf16[128,256]{1,0:T(8,128)(2,1)S(1)}, bf16[128,256]{1,0:T(8,128)(2,1)S(1)}, u32[]{:S(2)}, u32[]{:S(2)}) collective-permute-start(bf16[128,256]{1,0:T(8,128)(2,1)S(1)} %get-tuple-element.40), channel_id=1, source_target_pairs={{0,1},{1,0},{2,3},{3,2},{4,5},{5,4},{6,7},{7,6},{8,9},{9,8},{10,11... | collective-permute-start | bytes 196616 | tf_op jit(solution)/shard_map/ppermute | solution.py:94
  17.0 1.7 %collective-permute-done.7.refs_1_ = bf16[128,256]{1,0:T(8,128)(2,1)S(1)} collective-permute-done((bf16[128,256]{1,0:T(8,128)(2,1)S(1)}, bf16[128,256]{1,0:T(8,128)(2,1)S(1)}, u32[]{:S(2)}, u32[]{:S(2)}) %collective-permute-start.7) | collective-permute-done | bytes 65568 | tf_op jit(solution)/shard_map/ppermute | solution.py:94
  18.7 1.5 %collective-permute-done.8.refs_2_ = bf16[128,256]{1,0:T(8,128)(2,1)S(1)} collective-permute-done((bf16[128,256]{1,0:T(8,128)(2,1)S(1)}, bf16[128,256]{1,0:T(8,128)(2,1)S(1)}, u32[]{:S(2)}, u32[]{:S(2)}) %collective-permute-start.8) | collective-permute-done | bytes 65568 | tf_op jit(solution)/shard_map/ppermute | solution.py:94
  20.2 0.5 %collective-permute-done.9.refs_3_ = bf16[128,256]{1,0:T(8,128)(2,1)S(1)} collective-permute-done((bf16[128,256]{1,0:T(8,128)(2,1)S(1)}, bf16[128,256]{1,0:T(8,128)(2,1)S(1)}, u32[]{:S(2)}, u32[]{:S(2)}) %collective-permute-start.9) | collective-permute-done | bytes 65568 | tf_op jit(solution)/shard_map/ppermute | solution.py:94
  20.7 0.0 copy-done.3
  20.8 0.4 %dense.1 = (bf16[128,256]{1,0:T(8,128)(2,1)S(1)}, f32[128,256]{1,0:T(8,128)S(1)}, bf16[256,256]{1,0:T(8,128)(2,1)S(1)}) custom-call(bf16[256,256]{1,0:T(8,128)(2,1)S(1)} %copy-done.1, bf16[128,256]{1,0:T(8,128)(2,1)S(1)} %copy-done.3, bf16[256,128]{1,0:T(8,128)(2,1)S(1)} %get-tuple-element.31.placing_ref, bf16[128,256]{1,0:T(8,128)(2,1)S(1)} %get-tuple-element.37.refs_0_, ...), custom_call_target="tpu_custom_call" | custom-call | tf_op jit(solution)/shard_map/dense/pallas_call | solution.py:126
  21.2 0.1 collective-permute-start.10
  21.3 1.3 %collective-permute-done.10.came_ref.refs_1_ = bf16[256,256]{1,0:T(8,128)(2,1)S(1)} collective-permute-done((bf16[256,256]{1,0:T(8,128)(2,1)S(1)}, bf16[256,256]{1,0:T(8,128)(2,1)S(1)}, u32[]{:S(2)}, u32[]{:S(2)}) %collective-permute-start.10) | collective-permute-done | bytes 131104 | tf_op jit(solution)/shard_map/ppermute | solution.py:94
  22.6 1.0 %collective-permute-start.11 = (bf16[192,256]{1,0:T(8,128)(2,1)S(1)}, bf16[192,256]{1,0:T(8,128)(2,1)S(1)}, u32[]{:S(2)}, u32[]{:S(2)}) collective-permute-start(bf16[192,256]{1,0:T(8,128)(2,1)S(1)} %get-tuple-element.45), channel_id=1, source_target_pairs={{0,8},{1,9},{2,10},{3,11},{4,7},{5,6},{6,5},{7,4},{8,16},{9,17},{1... | collective-permute-start | bytes 294920 | tf_op jit(solution)/shard_map/ppermute | solution.py:260
  23.6 2.6 %collective-permute-start.12 = (bf16[192,256]{1,0:T(8,128)(2,1)S(1)}, bf16[192,256]{1,0:T(8,128)(2,1)S(1)}, u32[]{:S(2)}, u32[]{:S(2)}) collective-permute-start(bf16[192,256]{1,0:T(8,128)(2,1)S(1)} %get-tuple-element.46), channel_id=1, source_target_pairs={{0,16},{1,17},{2,18},{3,19},{4,6},{5,7},{6,4},{7,5},{8,24},{9,25},... | collective-permute-start | bytes 294920 | tf_op jit(solution)/shard_map/ppermute | solution.py:260
  26.3 2.0 %collective-permute-start.13 = (bf16[192,256]{1,0:T(8,128)(2,1)S(1)}, bf16[192,256]{1,0:T(8,128)(2,1)S(1)}, u32[]{:S(2)}, u32[]{:S(2)}) collective-permute-start(bf16[192,256]{1,0:T(8,128)(2,1)S(1)} %get-tuple-element.47), channel_id=1, source_target_pairs={{0,24},{1,25},{2,26},{3,27},{4,5},{5,4},{6,7},{7,6},{8,0},{9,1},{1... | collective-permute-start | bytes 294920 | tf_op jit(solution)/shard_map/ppermute | solution.py:260
  28.3 0.9 %collective-permute-done.11.refs_0_ = bf16[192,256]{1,0:T(8,128)(2,1)S(1)} collective-permute-done((bf16[192,256]{1,0:T(8,128)(2,1)S(1)}, bf16[192,256]{1,0:T(8,128)(2,1)S(1)}, u32[]{:S(2)}, u32[]{:S(2)}) %collective-permute-start.11) | collective-permute-done | bytes 98336 | tf_op jit(solution)/shard_map/ppermute | solution.py:260
  29.2 2.0 %collective-permute-done.12.refs_1_ = bf16[192,256]{1,0:T(8,128)(2,1)S(1)} collective-permute-done((bf16[192,256]{1,0:T(8,128)(2,1)S(1)}, bf16[192,256]{1,0:T(8,128)(2,1)S(1)}, u32[]{:S(2)}, u32[]{:S(2)}) %collective-permute-start.12) | collective-permute-done | bytes 98336 | tf_op jit(solution)/shard_map/ppermute | solution.py:260
  31.2 0.1 collective-permute-done.13.refs_2_
  31.4 0.1 second.1
  31.5 1.4 %collective-permute-start.14 = (bf16[192,256]{1,0:T(8,128)(2,1)S(1)}, bf16[192,256]{1,0:T(8,128)(2,1)S(1)}, u32[]{:S(2)}, u32[]{:S(2)}) collective-permute-start(bf16[192,256]{1,0:T(8,128)(2,1)S(1)} %get-tuple-element.49), channel_id=1, source_target_pairs={{0,3},{1,2},{2,1},{3,0},{4,12},{5,13},{6,14},{7,15},{8,11},{9,10},... | collective-permute-start | bytes 294920 | tf_op jit(solution)/shard_map/ppermute | solution.py:260
  32.9 0.8 %collective-permute-start.15 = (bf16[192,256]{1,0:T(8,128)(2,1)S(1)}, bf16[192,256]{1,0:T(8,128)(2,1)S(1)}, u32[]{:S(2)}, u32[]{:S(2)}) collective-permute-start(bf16[192,256]{1,0:T(8,128)(2,1)S(1)} %get-tuple-element.50), channel_id=1, source_target_pairs={{0,2},{1,3},{2,0},{3,1},{4,20},{5,21},{6,22},{7,23},{8,10},{9,11},... | collective-permute-start | bytes 294920 | tf_op jit(solution)/shard_map/ppermute | solution.py:260
  33.7 1.3 %collective-permute-start.16 = (bf16[192,256]{1,0:T(8,128)(2,1)S(1)}, bf16[192,256]{1,0:T(8,128)(2,1)S(1)}, u32[]{:S(2)}, u32[]{:S(2)}) collective-permute-start(bf16[192,256]{1,0:T(8,128)(2,1)S(1)} %get-tuple-element.51), channel_id=1, source_target_pairs={{0,1},{1,0},{2,3},{3,2},{4,28},{5,29},{6,30},{7,31},{8,9},{9,8},{1... | collective-permute-start | bytes 294920 | tf_op jit(solution)/shard_map/ppermute | solution.py:260
  35.0 0.7 %store.2._ = bf16[8,32,256]{2,1,0:T(8,128)(2,1)} custom-call(bf16[128,256]{1,0:T(8,128)(2,1)S(1)} %get-tuple-element.41.same_ref.refs_0_, bf16[256,256]{1,0:T(8,128)(2,1)S(1)} %collective-permute-done.10.came_ref.refs_1_, bf16[192,256]{1,0:T(8,128)(2,1)S(1)} %collective-permute-done.11.refs_0_, bf16[192,256]{1,0:T(8,128)(2,1)S(1)} %collective-permute-done.12.refs_1_, ...), custom_call_target="tpu_custom_call" | custom-call | tf_op jit(solution)/shard_map/store/pallas_call | solution.py:223
  35.7 1.4 %collective-permute-done.14.refs_0_.refs_2_ = bf16[192,256]{1,0:T(8,128)(2,1)S(1)} collective-permute-done((bf16[192,256]{1,0:T(8,128)(2,1)S(1)}, bf16[192,256]{1,0:T(8,128)(2,1)S(1)}, u32[]{:S(2)}, u32[]{:S(2)}) %collective-permute-start.14) | collective-permute-done | bytes 98336 | tf_op jit(solution)/shard_map/ppermute | solution.py:260
  37.1 1.0 %collective-permute-done.15.refs_1_.refs_3_ = bf16[192,256]{1,0:T(8,128)(2,1)S(1)} collective-permute-done((bf16[192,256]{1,0:T(8,128)(2,1)S(1)}, bf16[192,256]{1,0:T(8,128)(2,1)S(1)}, u32[]{:S(2)}, u32[]{:S(2)}) %collective-permute-start.15) | collective-permute-done | bytes 98336 | tf_op jit(solution)/shard_map/ppermute | solution.py:260
  38.1 0.2 collective-permute-done.16.refs_2_.refs_4_
  38.3 0.1 third.1.own_ref
  38.4 0.1 collective-permute-start.17
  38.5 1.2 %collective-permute-done.17.came_ref = bf16[128,256]{1,0:T(8,128)(2,1)S(1)} collective-permute-done((bf16[128,256]{1,0:T(8,128)(2,1)S(1)}, bf16[128,256]{1,0:T(8,128)(2,1)S(1)}, u32[]{:S(2)}, u32[]{:S(2)}) %collective-permute-start.17) | collective-permute-done | bytes 65568 | tf_op jit(solution)/shard_map/ppermute | solution.py:94
  39.7 0.7 %finish.1 = f32[2,128,256]{2,1,0:T(8,128)} custom-call(bf16[128,256]{1,0:T(8,128)(2,1)S(1)} %third.1.own_ref, bf16[128,256]{1,0:T(8,128)(2,1)S(1)} %collective-permute-done.17.came_ref), custom_call_target="tpu_custom_call" | custom-call | tf_op jit(solution)/shard_map/finish/pallas_call | solution.py:242
  (9 shorter events, 0.1 us)
Async XLA Ops:
  0.6 8.5 %collective-permute-start.2 = (bf16[128,256]{1,0:T(8,128)(2,1)}, bf16[128,256]{1,0:T(8,128)(2,1)S(1)}, u32[]{:S(2)}, u32[]{:S(2)}) collective-permute-start(bf16[128,256]{1,0:T(8,128)(2,1)} %own_ref.1), channel_id=1, source_target_pairs={{0,16},{4,20},{8,24},{12,28},{16,0},{20,4},{24,8},{28,12},{1,17},{... | collective-permute-start | bytes 196616 | tf_op jit(solution)/shard_map/ppermute | solution.py:94
  4.7 6.4 %collective-permute-start.1 = (bf16[128,256]{1,0:T(8,128)(2,1)}, bf16[128,256]{1,0:T(8,128)(2,1)S(1)}, u32[]{:S(2)}, u32[]{:S(2)}) collective-permute-start(bf16[128,256]{1,0:T(8,128)(2,1)} %own_ref.1), channel_id=1, source_target_pairs={{0,24},{4,28},{8,16},{12,20},{16,8},{20,12},{24,0},{28,4},{1,25},{... | collective-permute-start | bytes 196616 | tf_op jit(solution)/shard_map/ppermute | solution.py:94
  6.1 5.2 %collective-permute-start = (bf16[128,256]{1,0:T(8,128)(2,1)}, bf16[128,256]{1,0:T(8,128)(2,1)S(1)}, u32[]{:S(2)}, u32[]{:S(2)}) collective-permute-start(bf16[128,256]{1,0:T(8,128)(2,1)} %own_ref.1), channel_id=1, source_target_pairs={{0,8},{4,12},{8,0},{12,4},{16,24},{20,28},{24,16},{28,20},{1,9},{5... | collective-permute-start | bytes 196616 | tf_op jit(solution)/shard_map/ppermute | solution.py:94
  6.3 5.5 %collective-permute-start.3 = (bf16[128,256]{1,0:T(8,128)(2,1)}, bf16[128,256]{1,0:T(8,128)(2,1)S(1)}, u32[]{:S(2)}, u32[]{:S(2)}) collective-permute-start(bf16[128,256]{1,0:T(8,128)(2,1)} %own_ref.1), channel_id=1, source_target_pairs={{0,4},{4,0},{8,12},{12,8},{16,20},{20,16},{24,28},{28,24},{1,5},{5... | collective-permute-start | bytes 196616 | tf_op jit(solution)/shard_map/ppermute | solution.py:94
  6.3 0.7 %copy-start.5 = (s32[128,1]{0,1:T(1,128)S(1)}, s32[128,1]{0,1:T(1,128)}, u32[]{:S(2)}) copy-start(s32[128,1]{0,1:T(1,128)} %param.11) | copy-start | bytes 1540
  7.0 1.0 %copy-start = (bf16[4,1,4,128,128]{4,3,2,1,0:T(8,128)(2,1)S(1)}, bf16[4,1,4,128,128]{4,3,2,1,0:T(8,128)(2,1)}, u32[]{:S(2)}) copy-start(bf16[4,1,4,128,128]{4,3,2,1,0:T(8,128)(2,1)} %param.7) | copy-start | bytes 1572868
  8.0 0.8 %copy-start.2 = (bf16[128,256]{1,0:T(8,128)(2,1)S(1)}, bf16[128,256]{1,0:T(8,128)(2,1)}, u32[]{:S(2)}) copy-start(bf16[128,256]{1,0:T(8,128)(2,1)} %own_ref.1) | copy-start | bytes 196612
  11.3 1.8 %copy-start.4 = (s32[4,1,4]{2,1,0:T(1,128)S(1)}, s32[4,1,4]{2,1,0:T(1,128)}, u32[]{:S(2)}) copy-start(s32[4,1,4]{2,1,0:T(1,128)} %param.8) | copy-start | bytes 196
  11.3 1.3 %collective-permute-start.4 = (bf16[128,256]{1,0:T(8,128)(2,1)S(1)}, bf16[128,256]{1,0:T(8,128)(2,1)S(1)}, u32[]{:S(2)}, u32[]{:S(2)}) collective-permute-start(bf16[128,256]{1,0:T(8,128)(2,1)S(1)} %collective-permute-done.refs_2_), channel_id=1, source_target_pairs={{0,4},{4,0},{8,12},{12,8},{16,20},{20,16},{24,28},{28,24},{1,5},{5... | collective-permute-start | bytes 196616 | tf_op jit(solution)/shard_map/ppermute | solution.py:94
  11.3 1.4 %collective-permute-start.5 = (bf16[128,256]{1,0:T(8,128)(2,1)S(1)}, bf16[128,256]{1,0:T(8,128)(2,1)S(1)}, u32[]{:S(2)}, u32[]{:S(2)}) collective-permute-start(bf16[128,256]{1,0:T(8,128)(2,1)S(1)} %collective-permute-done.2.refs_4_), channel_id=1, source_target_pairs={{0,4},{4,0},{8,12},{12,8},{16,20},{20,16},{24,28},{28,24},{1,5},{5... | collective-permute-start | bytes 196616 | tf_op jit(solution)/shard_map/ppermute | solution.py:94
  11.8 1.3 %collective-permute-start.6 = (bf16[128,256]{1,0:T(8,128)(2,1)S(1)}, bf16[128,256]{1,0:T(8,128)(2,1)S(1)}, u32[]{:S(2)}, u32[]{:S(2)}) collective-permute-start(bf16[128,256]{1,0:T(8,128)(2,1)S(1)} %collective-permute-done.1.refs_6_), channel_id=1, source_target_pairs={{0,4},{4,0},{8,12},{12,8},{16,20},{20,16},{24,28},{28,24},{1,5},{5... | collective-permute-start | bytes 196616 | tf_op jit(solution)/shard_map/ppermute | solution.py:94
  13.0 7.7 %copy-start.1 = (bf16[256,256]{1,0:T(8,128)(2,1)S(1)}, bf16[256,256]{1,0:T(8,128)(2,1)}, u32[]{:S(2)}) copy-start(bf16[256,256]{1,0:T(8,128)(2,1)} %weight_ref.1) | copy-start | bytes 393220
  13.0 7.7 %copy-start.3 = (bf16[128,256]{1,0:T(8,128)(2,1)S(1)}, bf16[128,256]{1,0:T(8,128)(2,1)}, u32[]{:S(2)}) copy-start(bf16[128,256]{1,0:T(8,128)(2,1)} %cot_ref.1) | copy-start | bytes 196612
  13.5 5.3 %collective-permute-start.7 = (bf16[128,256]{1,0:T(8,128)(2,1)S(1)}, bf16[128,256]{1,0:T(8,128)(2,1)S(1)}, u32[]{:S(2)}, u32[]{:S(2)}) collective-permute-start(bf16[128,256]{1,0:T(8,128)(2,1)S(1)} %get-tuple-element.38), channel_id=1, source_target_pairs={{0,3},{1,2},{2,1},{3,0},{4,7},{5,6},{6,5},{7,4},{8,11},{9,10},{10,... | collective-permute-start | bytes 196616 | tf_op jit(solution)/shard_map/ppermute | solution.py:94
  16.0 4.3 %collective-permute-start.8 = (bf16[128,256]{1,0:T(8,128)(2,1)S(1)}, bf16[128,256]{1,0:T(8,128)(2,1)S(1)}, u32[]{:S(2)}, u32[]{:S(2)}) collective-permute-start(bf16[128,256]{1,0:T(8,128)(2,1)S(1)} %get-tuple-element.39), channel_id=1, source_target_pairs={{0,2},{1,3},{2,0},{3,1},{4,6},{5,7},{6,4},{7,5},{8,10},{9,11},{10,... | collective-permute-start | bytes 196616 | tf_op jit(solution)/shard_map/ppermute | solution.py:94
  16.5 4.3 %collective-permute-start.9 = (bf16[128,256]{1,0:T(8,128)(2,1)S(1)}, bf16[128,256]{1,0:T(8,128)(2,1)S(1)}, u32[]{:S(2)}, u32[]{:S(2)}) collective-permute-start(bf16[128,256]{1,0:T(8,128)(2,1)S(1)} %get-tuple-element.40), channel_id=1, source_target_pairs={{0,1},{1,0},{2,3},{3,2},{4,5},{5,4},{6,7},{7,6},{8,9},{9,8},{10,11... | collective-permute-start | bytes 196616 | tf_op jit(solution)/shard_map/ppermute | solution.py:94
  21.2 1.4 %collective-permute-start.10 = (bf16[256,256]{1,0:T(8,128)(2,1)S(1)}, bf16[256,256]{1,0:T(8,128)(2,1)S(1)}, u32[]{:S(2)}, u32[]{:S(2)}) collective-permute-start(bf16[256,256]{1,0:T(8,128)(2,1)S(1)} %get-tuple-element.42), channel_id=1, source_target_pairs={{0,4},{4,0},{8,12},{12,8},{16,20},{20,16},{24,28},{28,24},{1,5},{5... | collective-permute-start | bytes 393224 | tf_op jit(solution)/shard_map/ppermute | solution.py:94
  22.6 6.6 %collective-permute-start.11 = (bf16[192,256]{1,0:T(8,128)(2,1)S(1)}, bf16[192,256]{1,0:T(8,128)(2,1)S(1)}, u32[]{:S(2)}, u32[]{:S(2)}) collective-permute-start(bf16[192,256]{1,0:T(8,128)(2,1)S(1)} %get-tuple-element.45), channel_id=1, source_target_pairs={{0,8},{1,9},{2,10},{3,11},{4,7},{5,6},{6,5},{7,4},{8,16},{9,17},{1... | collective-permute-start | bytes 294920 | tf_op jit(solution)/shard_map/ppermute | solution.py:260
  23.6 7.6 %collective-permute-start.12 = (bf16[192,256]{1,0:T(8,128)(2,1)S(1)}, bf16[192,256]{1,0:T(8,128)(2,1)S(1)}, u32[]{:S(2)}, u32[]{:S(2)}) collective-permute-start(bf16[192,256]{1,0:T(8,128)(2,1)S(1)} %get-tuple-element.46), channel_id=1, source_target_pairs={{0,16},{1,17},{2,18},{3,19},{4,6},{5,7},{6,4},{7,5},{8,24},{9,25},... | collective-permute-start | bytes 294920 | tf_op jit(solution)/shard_map/ppermute | solution.py:260
  26.3 5.1 %collective-permute-start.13 = (bf16[192,256]{1,0:T(8,128)(2,1)S(1)}, bf16[192,256]{1,0:T(8,128)(2,1)S(1)}, u32[]{:S(2)}, u32[]{:S(2)}) collective-permute-start(bf16[192,256]{1,0:T(8,128)(2,1)S(1)} %get-tuple-element.47), channel_id=1, source_target_pairs={{0,24},{1,25},{2,26},{3,27},{4,5},{5,4},{6,7},{7,6},{8,0},{9,1},{1... | collective-permute-start | bytes 294920 | tf_op jit(solution)/shard_map/ppermute | solution.py:260
  31.5 5.6 %collective-permute-start.14 = (bf16[192,256]{1,0:T(8,128)(2,1)S(1)}, bf16[192,256]{1,0:T(8,128)(2,1)S(1)}, u32[]{:S(2)}, u32[]{:S(2)}) collective-permute-start(bf16[192,256]{1,0:T(8,128)(2,1)S(1)} %get-tuple-element.49), channel_id=1, source_target_pairs={{0,3},{1,2},{2,1},{3,0},{4,12},{5,13},{6,14},{7,15},{8,11},{9,10},... | collective-permute-start | bytes 294920 | tf_op jit(solution)/shard_map/ppermute | solution.py:260
  32.9 5.2 %collective-permute-start.15 = (bf16[192,256]{1,0:T(8,128)(2,1)S(1)}, bf16[192,256]{1,0:T(8,128)(2,1)S(1)}, u32[]{:S(2)}, u32[]{:S(2)}) collective-permute-start(bf16[192,256]{1,0:T(8,128)(2,1)S(1)} %get-tuple-element.50), channel_id=1, source_target_pairs={{0,2},{1,3},{2,0},{3,1},{4,20},{5,21},{6,22},{7,23},{8,10},{9,11},... | collective-permute-start | bytes 294920 | tf_op jit(solution)/shard_map/ppermute | solution.py:260
  33.7 4.6 %collective-permute-start.16 = (bf16[192,256]{1,0:T(8,128)(2,1)S(1)}, bf16[192,256]{1,0:T(8,128)(2,1)S(1)}, u32[]{:S(2)}, u32[]{:S(2)}) collective-permute-start(bf16[192,256]{1,0:T(8,128)(2,1)S(1)} %get-tuple-element.51), channel_id=1, source_target_pairs={{0,1},{1,0},{2,3},{3,2},{4,28},{5,29},{6,30},{7,31},{8,9},{9,8},{1... | collective-permute-start | bytes 294920 | tf_op jit(solution)/shard_map/ppermute | solution.py:260
  38.4 1.3 %collective-permute-start.17 = (bf16[128,256]{1,0:T(8,128)(2,1)S(1)}, bf16[128,256]{1,0:T(8,128)(2,1)S(1)}, u32[]{:S(2)}, u32[]{:S(2)}) collective-permute-start(bf16[128,256]{1,0:T(8,128)(2,1)S(1)} %third.1.own_ref), channel_id=1, source_target_pairs={{0,4},{4,0},{8,12},{12,8},{16,20},{20,16},{24,28},{28,24},{1,5},{5... | collective-permute-start | bytes 196616 | tf_op jit(solution)/shard_map/ppermute | solution.py:94

commit v14 on v13

--- a/solution.py
+++ b/solution.py
@@ -146,25 +146,6 @@
         ref[2 * slots :] = half
 
 
-def sum_halves(half_ref, held, slots, own_ref, message_refs, core_along, n_rep):
-    chip, chips = place_of_chip()
-    core = lax.axis_index("section") & 1
-
-    @pl.when(core == core_along)
-    def _():
-        held[chip] = own_ref[...]
-        for i, ref in enumerate(message_refs[: chips - 1]):
-            held[(chip + chips - i - 1) % chips] = ref[2 * slots :]
-        total = tree_sum([held[c].astype(jnp.float32) for c in range(chips)])
-        half_ref[...] = total.astype(jnp.bfloat16)
-
-    @pl.when(core != core_along)
-    def _():
-        by_xor = [own_ref[...].astype(jnp.float32)]
-        by_xor += [ref[2 * slots :].astype(jnp.float32) for ref in message_refs[::-1]]
-        half_ref[...] = tree_sum(by_xor[:n_rep]).astype(jnp.bfloat16)
-
-
 def first_kernel(slots, same_ref, kept_ref, came_ref, half_ref, *out_refs):
     rows = kept_ref.shape[0]
     half = kept_ref[...] + came_ref[came_ref.shape[0] - rows :].astype(jnp.float32)
@@ -172,14 +153,18 @@
     write_messages(slots, same_ref, came_ref, half_ref[...], out_refs)
 
 
-def second_kernel(slots, n_rep, many, same_ref, came_ref, own_ref, *refs):
-    message_refs, half_ref, out_refs, held = refs[:many], refs[many], refs[many + 1 : -1], refs[-1]
-    sum_halves(half_ref, held, slots, own_ref, message_refs, 0, n_rep)
-    write_messages(slots, same_ref, came_ref, half_ref[...], out_refs)
-
-
-def third_kernel(slots, n_rep, own_ref, *refs):
-    sum_halves(refs[-2], refs[-1], slots, own_ref, refs[:-2], 1, n_rep)
+def second_kernel(slots, own_ref, *refs):
+    message_refs, half_ref, held = refs[:-2], refs[-2], refs[-1]
+    chip, chips = place_of_chip()
+    held[chip] = own_ref[...]
+    for i, ref in enumerate(message_refs):
+        held[(chip + chips - i - 1) % chips] = ref[2 * slots :]
+    total = tree_sum([held[c].astype(jnp.float32) for c in range(chips)])
+    half_ref[...] = total.astype(jnp.bfloat16)
+
+
+def third_kernel(*refs):
+    refs[-1][...] = tree_sum([ref[...].astype(jnp.float32) for ref in refs[:-1]]).astype(jnp.bfloat16)
 
 
 def call_halves(kernel, name, operands, half, slots, many, held=()):
@@ -196,40 +181,33 @@
     )(*operands)
 
 
-def store_kernel(core, slots, same_ref, came_ref, *refs):
+def store_kernel(slots, same_ref, came_ref, *refs):
     message_refs, (out_ref, rows, sem) = refs[:-3], refs[-3:]
     section = lax.axis_index("section")
+    core = section & 1
     chip, chips = place_of_chip()
-
-    @pl.when(section & 1 == core)
-    def _():
-        rows[section] = same_ref[:slots]
-        rows[section ^ 1] = came_ref[:slots]
-        for i, ref in enumerate(message_refs[: chips - 1]):
-            source = 2 * ((chip + chips - i - 1) % chips)
-            rows[source + core] = ref[:slots]
-            rows[source + 1 - core] = ref[slots : 2 * slots]
-        copy = pltpu.make_async_copy(rows, out_ref, sem)
-        copy.start()
-        copy.wait()
-
-
-def store(core, same, came, messages, n_section, slots, base=None):
+    rows[section] = same_ref[:slots]
+    rows[section ^ 1] = came_ref[:slots]
+    for i, ref in enumerate(message_refs):
+        source = 2 * ((chip + chips - i - 1) % chips)
+        rows[source + core] = ref[:slots]
+        rows[source + 1 - core] = ref[slots : 2 * slots]
+    copy = pltpu.make_async_copy(rows, out_ref, sem)
+    copy.start()
+    copy.wait()
+
+
+def store(same, came, messages, n_section, slots):
     shape = (n_section, slots, same.shape[1])
-    operands = [same, came, *messages]
-    kernel, first, specs = functools.partial(store_kernel, core, slots), [], []
-    if base is not None:
-        kernel, first, specs = lambda _, *refs: store_kernel(core, slots, *refs), [base], [HBM]
-    return pl.pallas_call(
-        kernel,
+    return pl.pallas_call(
+        functools.partial(store_kernel, slots),
         out_shape=jax.ShapeDtypeStruct(shape, jnp.bfloat16),
-        in_specs=specs + [VMEM] * len(operands),
+        in_specs=[VMEM] * (2 + len(messages)),
         out_specs=HBM,
         scratch_shapes=[pltpu.VMEM(shape, jnp.bfloat16), pltpu.SemaphoreType.DMA],
-        input_output_aliases={0: 0} if first else {},
         compiler_params=LIMIT,
         name="store",
-    )(*first, *operands)
+    )(same, came, *messages)
 
 
 def finish_kernel(own_ref, came_ref, out_ref):
@@ -249,15 +227,9 @@
     )(own, came)
 
 
-def exchange(value, core_along, shift, j):
-    n_section, n_rep = lax.axis_size("section"), lax.axis_size("rep")
-    pairs = []
-    for s in range(n_section):
-        along = s & 1 == core_along
-        to = (s + 2 * shift) % n_section if along else s
-        for r in range(n_rep):
-            pairs.append((s * n_rep + r, to * n_rep + (r if along else r ^ j % n_rep)))
-    return lax.ppermute(value, ("section", "rep"), pairs)
+def send_along(value, axis, shift):
+    n = lax.axis_size(axis)
+    return lax.ppermute(value, axis, [(s, (s + 2 * shift) % n) for s in range(n)])
 
 
 def gather_blocks(features, axis, ready):
@@ -290,28 +262,17 @@
     same, kept, sent = dense(parts, weight, cotangent, placing)
     came = swap(sent, "section", 1)
     chips = n_section // 2
-    steps = across(max(n_rep, chips))
     half_shape = (width // 2, width)
+    half, *messages = call_halves(
+        functools.partial(first_kernel, slots), "first", [same, kept, came], half_shape, slots, chips - 1
+    )
+    messages = [send_along(m, "section", i + 1) for i, m in enumerate(messages)]
+    relaid = store(same, came, messages, n_section, slots)
+    second = functools.partial(second_kernel, slots)
     held = [(chips,) + half_shape]
-    half, *first = call_halves(
-        functools.partial(first_kernel, slots), "first", [same, kept, came], half_shape, slots, len(steps)
-    )
-    first = [exchange(m, 0, i + 1, j) for i, (m, j) in enumerate(zip(first, steps))]
-    relaid = store(0, same, came, first, n_section, slots)
-    half, *second = call_halves(
-        functools.partial(second_kernel, slots, n_rep, len(steps)),
-        "second",
-        [same, came, half, *first],
-        half_shape,
-        slots,
-        len(steps),
-        held,
-    )
-    second = [exchange(m, 1, i + 1, j) for i, (m, j) in enumerate(zip(second, steps))]
-    (half,) = call_halves(
-        functools.partial(third_kernel, slots, n_rep), "third", [half, *second], half_shape, slots, 0, held
-    )
-    relaid = store(1, same, came, second, n_section, slots, relaid)
+    (half,) = call_halves(second, "second", [half, *messages], half_shape, slots, 0, held)
+    halves = [half] + [swap(half, "rep", j) for j in range(1, n_rep)]
+    (half,) = call_halves(third_kernel, "third", halves, half_shape, slots, 0)
     half, relaid = lax.optimization_barrier((half, relaid))
     weight_grad = finish(half, swap(half, "section", 1))
     return (relaid.reshape(1, 1, n_section, slots, width), weight_grad.reshape(width, width))

time: 40.6 us -> 42.6 us (1.049)
  waiting for transfers between devices: 15.4 us -> 17.4 us
    ppermute x12 -> x15, starting transfers between devices: 9.89 us -> 13.4 us  [swap(): lax.ppermute(value, axis, [(i, i ^ j) for i in range(lax.axis_size(axis))])]
    ppermute x6 -> x3, starting transfers between devices: 9.2 us -> 5.66 us  [send_along(): lax.ppermute(value, axis, [(s, (s + 2 * shift) % n) for s in range(n)])]
    ppermute x12 -> x15, waiting for transfers between devices: 9.72 us -> 12.1 us  [swap(): lax.ppermute(value, axis, [(i, i ^ j) for i in range(lax.axis_size(axis))])]
    ppermute x6 -> x3, waiting for transfers between devices: 5.67 us -> 5.36 us  [send_along(): lax.ppermute(value, axis, [(s, (s + 2 * shift) % n) for s in range(n)])]
  transfers between devices with their start and end apart: 18 -> 18, of which waited for: 16 -> 15; matrix products, arithmetic and copies ran while one was open for 0% -> 0% of each run, Pallas kernels for 2% -> 2%
where the time goes in v14:
time: 42.6 us; the launch traced here: 42.4 us
  starting transfers between devices  19.1 us (45%)
  waiting for transfers between devices  17.4 us (41%)
  Pallas kernels  2.63 us (6%)
  local copies, waits for them, and re-layouts  2.55 us (6%)
  between operations  0.72 us (2%)
    ppermute x15, starting transfers between devices, swap(): lax.ppermute(value, axis, [(i, i ^ j) for i in range(lax.axis_size(axis))])  13.4 us
    ppermute x15, waiting for transfers between devices, swap(): lax.ppermute(value, axis, [(i, i ^ j) for i in range(lax.axis_size(axis))])  12.1 us
    ppermute x3, starting transfers between devices, send_along(): lax.ppermute(value, axis, [(s, (s + 2 * shift) % n) for s in range(n)])  5.66 us
    ppermute x3, waiting for transfers between devices, send_along(): lax.ppermute(value, axis, [(s, (s + 2 * shift) % n) for s in range(n)])  5.36 us
    unnamed x12, local copies, waits for them, and re-layouts  2.55 us
  transfers between devices with their start and end apart: 18, of which 15 were waited for; matrix products, arithmetic and copies ran while one was open for 0% of the time, Pallas kernels for 2%

profile of v14, /device:TPU:0, one launch (start us, length us, event | category | flops | bytes accessed | tf_op | source)
XLA Modules:
  0.0 42.4 jit_solution(5086047210149660382)
XLA Ops:
  0.6 4.1 %collective-permute-start.2 = (bf16[128,256]{1,0:T(8,128)(2,1)}, bf16[128,256]{1,0:T(8,128)(2,1)S(1)}, u32[]{:S(2)}, u32[]{:S(2)}) collective-permute-start(bf16[128,256]{1,0:T(8,128)(2,1)} %own_ref.1), channel_id=1, source_target_pairs={{0,16},{4,20},{8,24},{12,28},{16,0},{20,4},{24,8},{28,12},{1,17},{... | collective-permute-start | bytes 196616 | tf_op jit(solution)/shard_map/ppermute | solution.py:94
  4.7 1.3 %collective-permute-start.1 = (bf16[128,256]{1,0:T(8,128)(2,1)}, bf16[128,256]{1,0:T(8,128)(2,1)S(1)}, u32[]{:S(2)}, u32[]{:S(2)}) collective-permute-start(bf16[128,256]{1,0:T(8,128)(2,1)} %own_ref.1), channel_id=1, source_target_pairs={{0,24},{4,28},{8,16},{12,20},{16,8},{20,12},{24,0},{28,4},{1,25},{... | collective-permute-start | bytes 196616 | tf_op jit(solution)/shard_map/ppermute | solution.py:94
  6.1 0.2 collective-permute-start
  6.3 0.0 collective-permute-start.3
  6.3 0.7 %copy-done.5 = s32[128,1]{0,1:T(1,128)S(1)} copy-done((s32[128,1]{0,1:T(1,128)S(1)}, s32[128,1]{0,1:T(1,128)}, u32[]{:S(2)}) %copy-start.5) | copy-done | bytes 536
  7.0 1.0 %copy-done = bf16[4,1,4,128,128]{4,3,2,1,0:T(8,128)(2,1)S(1)} copy-done((bf16[4,1,4,128,128]{4,3,2,1,0:T(8,128)(2,1)S(1)}, bf16[4,1,4,128,128]{4,3,2,1,0:T(8,128)(2,1)}, u32[]{:S(2)}) %copy-start) | copy-done | bytes 524312
  8.0 0.8 %copy-done.2 = bf16[128,256]{1,0:T(8,128)(2,1)S(1)} copy-done((bf16[128,256]{1,0:T(8,128)(2,1)S(1)}, bf16[128,256]{1,0:T(8,128)(2,1)}, u32[]{:S(2)}) %copy-start.2) | copy-done | bytes 65560
  8.9 0.2 prepare.1
  9.1 0.0 collective-permute-done.2.refs_4_
  9.1 2.1 %collective-permute-done.1.refs_6_ = bf16[128,256]{1,0:T(8,128)(2,1)S(1)} collective-permute-done((bf16[128,256]{1,0:T(8,128)(2,1)}, bf16[128,256]{1,0:T(8,128)(2,1)S(1)}, u32[]{:S(2)}, u32[]{:S(2)}) %collective-permute-start.1) | collective-permute-done | bytes 65568 | tf_op jit(solution)/shard_map/ppermute | solution.py:94
  11.2 0.1 collective-permute-done.refs_2_
  11.3 0.0 collective-permute-start.4
  11.3 0.5 %collective-permute-start.5 = (bf16[128,256]{1,0:T(8,128)(2,1)S(1)}, bf16[128,256]{1,0:T(8,128)(2,1)S(1)}, u32[]{:S(2)}, u32[]{:S(2)}) collective-permute-start(bf16[128,256]{1,0:T(8,128)(2,1)S(1)} %collective-permute-done.2.refs_4_), channel_id=1, source_target_pairs={{0,4},{4,0},{8,12},{12,8},{16,20},{20,16},{24,28},{28,24},{1,5},{5... | collective-permute-start | bytes 196616 | tf_op jit(solution)/shard_map/ppermute | solution.py:94
  11.8 0.0 collective-permute-start.6
  11.8 0.0 collective-permute-done.3.refs_1_
  11.8 0.7 %collective-permute-done.4.refs_3_ = bf16[128,256]{1,0:T(8,128)(2,1)S(1)} collective-permute-done((bf16[128,256]{1,0:T(8,128)(2,1)S(1)}, bf16[128,256]{1,0:T(8,128)(2,1)S(1)}, u32[]{:S(2)}, u32[]{:S(2)}) %collective-permute-start.4) | collective-permute-done | bytes 65568 | tf_op jit(solution)/shard_map/ppermute | solution.py:94
  12.5 0.2 collective-permute-done.5.refs_5_
  12.7 0.4 collective-permute-done.6.refs_7_
  13.0 0.0 copy-done.4
  13.0 0.4 %partials.1 = (bf16[128,256]{1,0:T(8,128)(2,1)S(1)}, bf16[128,256]{1,0:T(8,128)(2,1)S(1)}, bf16[128,256]{1,0:T(8,128)(2,1)S(1)}, bf16[128,256]{1,0:T(8,128)(2,1)S(1)}) custom-call(s32[4,4]{1,0:T(4,128)S(1)} %bitcast.6, bf16[4,128,512]{2,1,0:T(8,128)(2,1)S(1)} %get-tuple-element.28.wide_ref, bf16[128,256]{1,0:T(8,128)(2,1)S(1)} %get-tuple-element.29.refs_0_, ...), custom_call_target="tpu_custom_call" | custom-call | tf_op jit(solution)/shard_map/partials/pallas_call | solution.py:82
  13.5 2.5 %collective-permute-start.7 = (bf16[128,256]{1,0:T(8,128)(2,1)S(1)}, bf16[128,256]{1,0:T(8,128)(2,1)S(1)}, u32[]{:S(2)}, u32[]{:S(2)}) collective-permute-start(bf16[128,256]{1,0:T(8,128)(2,1)S(1)} %get-tuple-element.34), channel_id=1, source_target_pairs={{0,3},{1,2},{2,1},{3,0},{4,7},{5,6},{6,5},{7,4},{8,11},{9,10},{10,... | collective-permute-start | bytes 196616 | tf_op jit(solution)/shard_map/ppermute | solution.py:94
  16.0 0.5 %collective-permute-start.8 = (bf16[128,256]{1,0:T(8,128)(2,1)S(1)}, bf16[128,256]{1,0:T(8,128)(2,1)S(1)}, u32[]{:S(2)}, u32[]{:S(2)}) collective-permute-start(bf16[128,256]{1,0:T(8,128)(2,1)S(1)} %get-tuple-element.35), channel_id=1, source_target_pairs={{0,2},{1,3},{2,0},{3,1},{4,6},{5,7},{6,4},{7,5},{8,10},{9,11},{10,... | collective-permute-start | bytes 196616 | tf_op jit(solution)/shard_map/ppermute | solution.py:94
  16.5 0.5 %collective-permute-start.9 = (bf16[128,256]{1,0:T(8,128)(2,1)S(1)}, bf16[128,256]{1,0:T(8,128)(2,1)S(1)}, u32[]{:S(2)}, u32[]{:S(2)}) collective-permute-start(bf16[128,256]{1,0:T(8,128)(2,1)S(1)} %get-tuple-element.36), channel_id=1, source_target_pairs={{0,1},{1,0},{2,3},{3,2},{4,5},{5,4},{6,7},{7,6},{8,9},{9,8},{10,11... | collective-permute-start | bytes 196616 | tf_op jit(solution)/shard_map/ppermute | solution.py:94
  17.0 1.7 %collective-permute-done.7.refs_1_ = bf16[128,256]{1,0:T(8,128)(2,1)S(1)} collective-permute-done((bf16[128,256]{1,0:T(8,128)(2,1)S(1)}, bf16[128,256]{1,0:T(8,128)(2,1)S(1)}, u32[]{:S(2)}, u32[]{:S(2)}) %collective-permute-start.7) | collective-permute-done | bytes 65568 | tf_op jit(solution)/shard_map/ppermute | solution.py:94
  18.7 1.5 %collective-permute-done.8.refs_2_ = bf16[128,256]{1,0:T(8,128)(2,1)S(1)} collective-permute-done((bf16[128,256]{1,0:T(8,128)(2,1)S(1)}, bf16[128,256]{1,0:T(8,128)(2,1)S(1)}, u32[]{:S(2)}, u32[]{:S(2)}) %collective-permute-start.8) | collective-permute-done | bytes 65568 | tf_op jit(solution)/shard_map/ppermute | solution.py:94
  20.2 0.5 %collective-permute-done.9.refs_3_ = bf16[128,256]{1,0:T(8,128)(2,1)S(1)} collective-permute-done((bf16[128,256]{1,0:T(8,128)(2,1)S(1)}, bf16[128,256]{1,0:T(8,128)(2,1)S(1)}, u32[]{:S(2)}, u32[]{:S(2)}) %collective-permute-start.9) | collective-permute-done | bytes 65568 | tf_op jit(solution)/shard_map/ppermute | solution.py:94
  20.7 0.0 copy-done.1
  20.7 0.0 copy-done.3
  20.8 0.4 %dense.1 = (bf16[128,256]{1,0:T(8,128)(2,1)S(1)}, f32[128,256]{1,0:T(8,128)S(1)}, bf16[256,256]{1,0:T(8,128)(2,1)S(1)}) custom-call(bf16[256,256]{1,0:T(8,128)(2,1)S(1)} %copy-done.1, bf16[128,256]{1,0:T(8,128)(2,1)S(1)} %copy-done.3, bf16[256,128]{1,0:T(8,128)(2,1)S(1)} %get-tuple-element.27.placing_ref, bf16[128,256]{1,0:T(8,128)(2,1)S(1)} %get-tuple-element.33.refs_0_, ...), custom_call_target="tpu_custom_call" | custom-call | tf_op jit(solution)/shard_map/dense/pallas_call | solution.py:126
  21.2 0.1 collective-permute-start.10
  21.3 1.3 %collective-permute-done.10.came_ref = bf16[256,256]{1,0:T(8,128)(2,1)S(1)} collective-permute-done((bf16[256,256]{1,0:T(8,128)(2,1)S(1)}, bf16[256,256]{1,0:T(8,128)(2,1)S(1)}, u32[]{:S(2)}, u32[]{:S(2)}) %collective-permute-start.10) | collective-permute-done | bytes 131104 | tf_op jit(solution)/shard_map/ppermute | solution.py:94
  22.6 1.0 %collective-permute-start.11 = (bf16[192,256]{1,0:T(8,128)(2,1)S(1)}, bf16[192,256]{1,0:T(8,128)(2,1)S(1)}, u32[]{:S(2)}, u32[]{:S(2)}) collective-permute-start(bf16[192,256]{1,0:T(8,128)(2,1)S(1)} %get-tuple-element.41), channel_id=1, source_target_pairs={{0,8},{4,12},{8,16},{12,20},{16,24},{20,28},{24,0},{28,4},{1,9},{5... | collective-permute-start | bytes 294920 | tf_op jit(solution)/shard_map/ppermute | solution.py:232
  23.6 2.6 %collective-permute-start.12 = (bf16[192,256]{1,0:T(8,128)(2,1)S(1)}, bf16[192,256]{1,0:T(8,128)(2,1)S(1)}, u32[]{:S(2)}, u32[]{:S(2)}) collective-permute-start(bf16[192,256]{1,0:T(8,128)(2,1)S(1)} %get-tuple-element.42), channel_id=1, source_target_pairs={{0,16},{4,20},{8,24},{12,28},{16,0},{20,4},{24,8},{28,12},{1,17},{... | collective-permute-start | bytes 294920 | tf_op jit(solution)/shard_map/ppermute | solution.py:232
  26.3 2.0 %collective-permute-start.13 = (bf16[192,256]{1,0:T(8,128)(2,1)S(1)}, bf16[192,256]{1,0:T(8,128)(2,1)S(1)}, u32[]{:S(2)}, u32[]{:S(2)}) collective-permute-start(bf16[192,256]{1,0:T(8,128)(2,1)S(1)} %get-tuple-element.43), channel_id=1, source_target_pairs={{0,24},{4,28},{8,0},{12,4},{16,8},{20,12},{24,16},{28,20},{1,25},{... | collective-permute-start | bytes 294920 | tf_op jit(solution)/shard_map/ppermute | solution.py:232
  28.3 1.8 %collective-permute-done.11.refs_0_ = bf16[192,256]{1,0:T(8,128)(2,1)S(1)} collective-permute-done((bf16[192,256]{1,0:T(8,128)(2,1)S(1)}, bf16[192,256]{1,0:T(8,128)(2,1)S(1)}, u32[]{:S(2)}, u32[]{:S(2)}) %collective-permute-start.11) | collective-permute-done | bytes 98336 | tf_op jit(solution)/shard_map/ppermute | solution.py:232
  30.1 3.5 %collective-permute-done.12.refs_1_ = bf16[192,256]{1,0:T(8,128)(2,1)S(1)} collective-permute-done((bf16[192,256]{1,0:T(8,128)(2,1)S(1)}, bf16[192,256]{1,0:T(8,128)(2,1)S(1)}, u32[]{:S(2)}, u32[]{:S(2)}) %collective-permute-start.12) | collective-permute-done | bytes 98336 | tf_op jit(solution)/shard_map/ppermute | solution.py:232
  33.7 0.0 collective-permute-done.13.refs_2_
  33.7 0.1 second.1.refs_0_
  33.8 1.6 %collective-permute-start.16 = (bf16[128,256]{1,0:T(8,128)(2,1)S(1)}, bf16[128,256]{1,0:T(8,128)(2,1)S(1)}, u32[]{:S(2)}, u32[]{:S(2)}) collective-permute-start(bf16[128,256]{1,0:T(8,128)(2,1)S(1)} %second.1.refs_0_), channel_id=1, source_target_pairs={{0,3},{1,2},{2,1},{3,0},{4,7},{5,6},{6,5},{7,4},{8,11},{9,10},{10,... | collective-permute-start | bytes 196616 | tf_op jit(solution)/shard_map/ppermute | solution.py:94
  35.3 0.8 %collective-permute-start.15 = (bf16[128,256]{1,0:T(8,128)(2,1)S(1)}, bf16[128,256]{1,0:T(8,128)(2,1)S(1)}, u32[]{:S(2)}, u32[]{:S(2)}) collective-permute-start(bf16[128,256]{1,0:T(8,128)(2,1)S(1)} %second.1.refs_0_), channel_id=1, source_target_pairs={{0,2},{1,3},{2,0},{3,1},{4,6},{5,7},{6,4},{7,5},{8,10},{9,11},{10,... | collective-permute-start | bytes 196616 | tf_op jit(solution)/shard_map/ppermute | solution.py:94
  36.1 1.2 %collective-permute-start.14 = (bf16[128,256]{1,0:T(8,128)(2,1)S(1)}, bf16[128,256]{1,0:T(8,128)(2,1)S(1)}, u32[]{:S(2)}, u32[]{:S(2)}) collective-permute-start(bf16[128,256]{1,0:T(8,128)(2,1)S(1)} %second.1.refs_0_), channel_id=1, source_target_pairs={{0,1},{1,0},{2,3},{3,2},{4,5},{5,4},{6,7},{7,6},{8,9},{9,8},{10,11... | collective-permute-start | bytes 196616 | tf_op jit(solution)/shard_map/ppermute | solution.py:94
  37.3 0.7 %store.1 = bf16[8,32,256]{2,1,0:T(8,128)(2,1)} custom-call(bf16[128,256]{1,0:T(8,128)(2,1)S(1)} %get-tuple-element.37.same_ref, bf16[256,256]{1,0:T(8,128)(2,1)S(1)} %collective-permute-done.10.came_ref, bf16[192,256]{1,0:T(8,128)(2,1)S(1)} %collective-permute-done.11.refs_0_, bf16[192,256]{1,0:T(8,128)(2,1)S(1)} %collective-permute-done.12.refs_1_, ...), custom_call_target="tpu_custom_call" | custom-call | tf_op jit(solution)/shard_map/store/pallas_call | solution.py:202
  38.0 1.7 %collective-permute-done.16.refs_3_ = bf16[128,256]{1,0:T(8,128)(2,1)S(1)} collective-permute-done((bf16[128,256]{1,0:T(8,128)(2,1)S(1)}, bf16[128,256]{1,0:T(8,128)(2,1)S(1)}, u32[]{:S(2)}, u32[]{:S(2)}) %collective-permute-start.16) | collective-permute-done | bytes 65568 | tf_op jit(solution)/shard_map/ppermute | solution.py:94
  39.7 0.3 collective-permute-done.15.refs_2_
  40.0 0.4 collective-permute-done.14.refs_1_
  40.4 0.1 collective-permute-start.17
  40.5 1.2 %collective-permute-done.17.came_ref = bf16[128,256]{1,0:T(8,128)(2,1)S(1)} collective-permute-done((bf16[128,256]{1,0:T(8,128)(2,1)S(1)}, bf16[128,256]{1,0:T(8,128)(2,1)S(1)}, u32[]{:S(2)}, u32[]{:S(2)}) %collective-permute-start.17) | collective-permute-done | bytes 65568 | tf_op jit(solution)/shard_map/ppermute | solution.py:94
  41.7 0.7 %finish.1 = f32[2,128,256]{2,1,0:T(8,128)} custom-call(bf16[128,256]{1,0:T(8,128)(2,1)S(1)} %third.1.own_ref, bf16[128,256]{1,0:T(8,128)(2,1)S(1)} %collective-permute-done.17.came_ref), custom_call_target="tpu_custom_call" | custom-call | tf_op jit(solution)/shard_map/finish/pallas_call | solution.py:220
  (8 shorter events, 0.1 us)
Async XLA Ops:
  0.6 8.5 %collective-permute-start.2 = (bf16[128,256]{1,0:T(8,128)(2,1)}, bf16[128,256]{1,0:T(8,128)(2,1)S(1)}, u32[]{:S(2)}, u32[]{:S(2)}) collective-permute-start(bf16[128,256]{1,0:T(8,128)(2,1)} %own_ref.1), channel_id=1, source_target_pairs={{0,16},{4,20},{8,24},{12,28},{16,0},{20,4},{24,8},{28,12},{1,17},{... | collective-permute-start | bytes 196616 | tf_op jit(solution)/shard_map/ppermute | solution.py:94
  4.7 6.4 %collective-permute-start.1 = (bf16[128,256]{1,0:T(8,128)(2,1)}, bf16[128,256]{1,0:T(8,128)(2,1)S(1)}, u32[]{:S(2)}, u32[]{:S(2)}) collective-permute-start(bf16[128,256]{1,0:T(8,128)(2,1)} %own_ref.1), channel_id=1, source_target_pairs={{0,24},{4,28},{8,16},{12,20},{16,8},{20,12},{24,0},{28,4},{1,25},{... | collective-permute-start | bytes 196616 | tf_op jit(solution)/shard_map/ppermute | solution.py:94
  6.1 5.2 %collective-permute-start = (bf16[128,256]{1,0:T(8,128)(2,1)}, bf16[128,256]{1,0:T(8,128)(2,1)S(1)}, u32[]{:S(2)}, u32[]{:S(2)}) collective-permute-start(bf16[128,256]{1,0:T(8,128)(2,1)} %own_ref.1), channel_id=1, source_target_pairs={{0,8},{4,12},{8,0},{12,4},{16,24},{20,28},{24,16},{28,20},{1,9},{5... | collective-permute-start | bytes 196616 | tf_op jit(solution)/shard_map/ppermute | solution.py:94
  6.3 5.5 %collective-permute-start.3 = (bf16[128,256]{1,0:T(8,128)(2,1)}, bf16[128,256]{1,0:T(8,128)(2,1)S(1)}, u32[]{:S(2)}, u32[]{:S(2)}) collective-permute-start(bf16[128,256]{1,0:T(8,128)(2,1)} %own_ref.1), channel_id=1, source_target_pairs={{0,4},{4,0},{8,12},{12,8},{16,20},{20,16},{24,28},{28,24},{1,5},{5... | collective-permute-start | bytes 196616 | tf_op jit(solution)/shard_map/ppermute | solution.py:94
  6.3 0.7 %copy-start.5 = (s32[128,1]{0,1:T(1,128)S(1)}, s32[128,1]{0,1:T(1,128)}, u32[]{:S(2)}) copy-start(s32[128,1]{0,1:T(1,128)} %param.11) | copy-start | bytes 1540
  7.0 1.0 %copy-start = (bf16[4,1,4,128,128]{4,3,2,1,0:T(8,128)(2,1)S(1)}, bf16[4,1,4,128,128]{4,3,2,1,0:T(8,128)(2,1)}, u32[]{:S(2)}) copy-start(bf16[4,1,4,128,128]{4,3,2,1,0:T(8,128)(2,1)} %param.7) | copy-start | bytes 1572868
  8.0 0.8 %copy-start.2 = (bf16[128,256]{1,0:T(8,128)(2,1)S(1)}, bf16[128,256]{1,0:T(8,128)(2,1)}, u32[]{:S(2)}) copy-start(bf16[128,256]{1,0:T(8,128)(2,1)} %own_ref.1) | copy-start | bytes 196612
  11.3 1.8 %copy-start.4 = (s32[4,1,4]{2,1,0:T(1,128)S(1)}, s32[4,1,4]{2,1,0:T(1,128)}, u32[]{:S(2)}) copy-start(s32[4,1,4]{2,1,0:T(1,128)} %param.8) | copy-start | bytes 196
  11.3 1.3 %collective-permute-start.4 = (bf16[128,256]{1,0:T(8,128)(2,1)S(1)}, bf16[128,256]{1,0:T(8,128)(2,1)S(1)}, u32[]{:S(2)}, u32[]{:S(2)}) collective-permute-start(bf16[128,256]{1,0:T(8,128)(2,1)S(1)} %collective-permute-done.refs_2_), channel_id=1, source_target_pairs={{0,4},{4,0},{8,12},{12,8},{16,20},{20,16},{24,28},{28,24},{1,5},{5... | collective-permute-start | bytes 196616 | tf_op jit(solution)/shard_map/ppermute | solution.py:94
  11.3 1.4 %collective-permute-start.5 = (bf16[128,256]{1,0:T(8,128)(2,1)S(1)}, bf16[128,256]{1,0:T(8,128)(2,1)S(1)}, u32[]{:S(2)}, u32[]{:S(2)}) collective-permute-start(bf16[128,256]{1,0:T(8,128)(2,1)S(1)} %collective-permute-done.2.refs_4_), channel_id=1, source_target_pairs={{0,4},{4,0},{8,12},{12,8},{16,20},{20,16},{24,28},{28,24},{1,5},{5... | collective-permute-start | bytes 196616 | tf_op jit(solution)/shard_map/ppermute | solution.py:94
  11.8 1.3 %collective-permute-start.6 = (bf16[128,256]{1,0:T(8,128)(2,1)S(1)}, bf16[128,256]{1,0:T(8,128)(2,1)S(1)}, u32[]{:S(2)}, u32[]{:S(2)}) collective-permute-start(bf16[128,256]{1,0:T(8,128)(2,1)S(1)} %collective-permute-done.1.refs_6_), channel_id=1, source_target_pairs={{0,4},{4,0},{8,12},{12,8},{16,20},{20,16},{24,28},{28,24},{1,5},{5... | collective-permute-start | bytes 196616 | tf_op jit(solution)/shard_map/ppermute | solution.py:94
  13.0 7.7 %copy-start.1 = (bf16[256,256]{1,0:T(8,128)(2,1)S(1)}, bf16[256,256]{1,0:T(8,128)(2,1)}, u32[]{:S(2)}) copy-start(bf16[256,256]{1,0:T(8,128)(2,1)} %weight_ref.1) | copy-start | bytes 393220
  13.0 7.7 %copy-start.3 = (bf16[128,256]{1,0:T(8,128)(2,1)S(1)}, bf16[128,256]{1,0:T(8,128)(2,1)}, u32[]{:S(2)}) copy-start(bf16[128,256]{1,0:T(8,128)(2,1)} %cot_ref.1) | copy-start | bytes 196612
  13.5 5.3 %collective-permute-start.7 = (bf16[128,256]{1,0:T(8,128)(2,1)S(1)}, bf16[128,256]{1,0:T(8,128)(2,1)S(1)}, u32[]{:S(2)}, u32[]{:S(2)}) collective-permute-start(bf16[128,256]{1,0:T(8,128)(2,1)S(1)} %get-tuple-element.34), channel_id=1, source_target_pairs={{0,3},{1,2},{2,1},{3,0},{4,7},{5,6},{6,5},{7,4},{8,11},{9,10},{10,... | collective-permute-start | bytes 196616 | tf_op jit(solution)/shard_map/ppermute | solution.py:94
  16.0 4.3 %collective-permute-start.8 = (bf16[128,256]{1,0:T(8,128)(2,1)S(1)}, bf16[128,256]{1,0:T(8,128)(2,1)S(1)}, u32[]{:S(2)}, u32[]{:S(2)}) collective-permute-start(bf16[128,256]{1,0:T(8,128)(2,1)S(1)} %get-tuple-element.35), channel_id=1, source_target_pairs={{0,2},{1,3},{2,0},{3,1},{4,6},{5,7},{6,4},{7,5},{8,10},{9,11},{10,... | collective-permute-start | bytes 196616 | tf_op jit(solution)/shard_map/ppermute | solution.py:94
  16.5 4.3 %collective-permute-start.9 = (bf16[128,256]{1,0:T(8,128)(2,1)S(1)}, bf16[128,256]{1,0:T(8,128)(2,1)S(1)}, u32[]{:S(2)}, u32[]{:S(2)}) collective-permute-start(bf16[128,256]{1,0:T(8,128)(2,1)S(1)} %get-tuple-element.36), channel_id=1, source_target_pairs={{0,1},{1,0},{2,3},{3,2},{4,5},{5,4},{6,7},{7,6},{8,9},{9,8},{10,11... | collective-permute-start | bytes 196616 | tf_op jit(solution)/shard_map/ppermute | solution.py:94
  21.2 1.4 %collective-permute-start.10 = (bf16[256,256]{1,0:T(8,128)(2,1)S(1)}, bf16[256,256]{1,0:T(8,128)(2,1)S(1)}, u32[]{:S(2)}, u32[]{:S(2)}) collective-permute-start(bf16[256,256]{1,0:T(8,128)(2,1)S(1)} %get-tuple-element.39), channel_id=1, source_target_pairs={{0,4},{4,0},{8,12},{12,8},{16,20},{20,16},{24,28},{28,24},{1,5},{5... | collective-permute-start | bytes 393224 | tf_op jit(solution)/shard_map/ppermute | solution.py:94
  22.6 7.5 %collective-permute-start.11 = (bf16[192,256]{1,0:T(8,128)(2,1)S(1)}, bf16[192,256]{1,0:T(8,128)(2,1)S(1)}, u32[]{:S(2)}, u32[]{:S(2)}) collective-permute-start(bf16[192,256]{1,0:T(8,128)(2,1)S(1)} %get-tuple-element.41), channel_id=1, source_target_pairs={{0,8},{4,12},{8,16},{12,20},{16,24},{20,28},{24,0},{28,4},{1,9},{5... | collective-permute-start | bytes 294920 | tf_op jit(solution)/shard_map/ppermute | solution.py:232
  23.6 10.0 %collective-permute-start.12 = (bf16[192,256]{1,0:T(8,128)(2,1)S(1)}, bf16[192,256]{1,0:T(8,128)(2,1)S(1)}, u32[]{:S(2)}, u32[]{:S(2)}) collective-permute-start(bf16[192,256]{1,0:T(8,128)(2,1)S(1)} %get-tuple-element.42), channel_id=1, source_target_pairs={{0,16},{4,20},{8,24},{12,28},{16,0},{20,4},{24,8},{28,12},{1,17},{... | collective-permute-start | bytes 294920 | tf_op jit(solution)/shard_map/ppermute | solution.py:232
  26.3 7.4 %collective-permute-start.13 = (bf16[192,256]{1,0:T(8,128)(2,1)S(1)}, bf16[192,256]{1,0:T(8,128)(2,1)S(1)}, u32[]{:S(2)}, u32[]{:S(2)}) collective-permute-start(bf16[192,256]{1,0:T(8,128)(2,1)S(1)} %get-tuple-element.43), channel_id=1, source_target_pairs={{0,24},{4,28},{8,0},{12,4},{16,8},{20,12},{24,16},{28,20},{1,25},{... | collective-permute-start | bytes 294920 | tf_op jit(solution)/shard_map/ppermute | solution.py:232
  33.8 5.9 %collective-permute-start.16 = (bf16[128,256]{1,0:T(8,128)(2,1)S(1)}, bf16[128,256]{1,0:T(8,128)(2,1)S(1)}, u32[]{:S(2)}, u32[]{:S(2)}) collective-permute-start(bf16[128,256]{1,0:T(8,128)(2,1)S(1)} %second.1.refs_0_), channel_id=1, source_target_pairs={{0,3},{1,2},{2,1},{3,0},{4,7},{5,6},{6,5},{7,4},{8,11},{9,10},{10,... | collective-permute-start | bytes 196616 | tf_op jit(solution)/shard_map/ppermute | solution.py:94
  35.3 4.7 %collective-permute-start.15 = (bf16[128,256]{1,0:T(8,128)(2,1)S(1)}, bf16[128,256]{1,0:T(8,128)(2,1)S(1)}, u32[]{:S(2)}, u32[]{:S(2)}) collective-permute-start(bf16[128,256]{1,0:T(8,128)(2,1)S(1)} %second.1.refs_0_), channel_id=1, source_target_pairs={{0,2},{1,3},{2,0},{3,1},{4,6},{5,7},{6,4},{7,5},{8,10},{9,11},{10,... | collective-permute-start | bytes 196616 | tf_op jit(solution)/shard_map/ppermute | solution.py:94
  36.1 4.3 %collective-permute-start.14 = (bf16[128,256]{1,0:T(8,128)(2,1)S(1)}, bf16[128,256]{1,0:T(8,128)(2,1)S(1)}, u32[]{:S(2)}, u32[]{:S(2)}) collective-permute-start(bf16[128,256]{1,0:T(8,128)(2,1)S(1)} %second.1.refs_0_), channel_id=1, source_target_pairs={{0,1},{1,0},{2,3},{3,2},{4,5},{5,4},{6,7},{7,6},{8,9},{9,8},{10,11... | collective-permute-start | bytes 196616 | tf_op jit(solution)/shard_map/ppermute | solution.py:94
  40.4 1.3 %collective-permute-start.17 = (bf16[128,256]{1,0:T(8,128)(2,1)S(1)}, bf16[128,256]{1,0:T(8,128)(2,1)S(1)}, u32[]{:S(2)}, u32[]{:S(2)}) collective-permute-start(bf16[128,256]{1,0:T(8,128)(2,1)S(1)} %third.1.own_ref), channel_id=1, source_target_pairs={{0,4},{4,0},{8,12},{12,8},{16,20},{20,16},{24,28},{28,24},{1,5},{5... | collective-permute-start | bytes 196616 | tf_op jit(solution)/shard_map/ppermute | solution.py:94

commit v15 on v13

--- a/solution.py
+++ b/solution.py
@@ -100,91 +100,122 @@
     return terms[0]
 
 
-def dense_kernel(n_part, weight_ref, cot_ref, placing_ref, *refs):
-    part_refs, (same_ref, kept_ref, sent_ref, term) = refs[:n_part], refs[n_part:]
+def parts_of(width, slots):
+    low = (width - 2 * slots) // 2 // 16 * 16
+    return low, width - low
+
+
+def dense_kernel(n_part, slots, weight_ref, cot_ref, placing_ref, *refs):
+    part_refs, (same_ref, term_ref, sent_ref) = refs[:n_part], refs[n_part:]
     core = lax.axis_index("section") & 1
     agg_b = tree_sum([ref[...].astype(jnp.float32) for ref in part_refs]).astype(jnp.bfloat16)
     pre = jnp.dot(agg_b, weight_ref[...], preferred_element_type=jnp.float32)
     sig = jax.nn.sigmoid(pre)
     factor = sig * (1.0 + pre * (1.0 - sig))
     grad_pre = (cot_ref[...].astype(jnp.float32) * factor).astype(jnp.bfloat16)
-    whole = lax.dot_general(
+    term = lax.dot_general(
         agg_b, grad_pre, (((0,), (0,)), ((), ())), preferred_element_type=jnp.float32
     )
-    term[...] = whole.reshape(term.shape)
-    kept_ref[...] = term[core]
+    term_ref[...] = term
     output = (pre * sig).astype(jnp.bfloat16)
     packed = jnp.dot(placing_ref[...], output, preferred_element_type=jnp.float32)
     half = packed.shape[0] // 2
     same_ref[...] = packed[:half].astype(jnp.bfloat16)
     sent_ref[:half] = packed[half:].astype(jnp.bfloat16)
-    sent_ref[half:] = term[1 - core].astype(jnp.bfloat16)
-
-
-def dense(parts, weight, cotangent, placing):
+    low, high = parts_of(term.shape[0], slots)
+
+    @pl.when(core == 0)
+    def _():
+        sent_ref[half:] = term[low:].astype(jnp.bfloat16)
+
+    @pl.when(core == 1)
+    def _():
+        sent_ref[half : half + low] = term[:low].astype(jnp.bfloat16)
+
+
+def dense(parts, weight, cotangent, placing, slots):
     places, width = placing.shape[0], weight.shape[0]
     return pl.pallas_call(
-        functools.partial(dense_kernel, len(parts)),
+        functools.partial(dense_kernel, len(parts), slots),
         out_shape=(
             jax.ShapeDtypeStruct((places // 2, width), jnp.bfloat16),
-            jax.ShapeDtypeStruct((width // 2, width), jnp.float32),
-            jax.ShapeDtypeStruct((places // 2 + width // 2, width), jnp.bfloat16),
+            jax.ShapeDtypeStruct((width, width), jnp.float32),
+            jax.ShapeDtypeStruct((places // 2 + parts_of(width, slots)[1], width), jnp.bfloat16),
         ),
         in_specs=[VMEM] * (3 + len(parts)),
         out_specs=(VMEM,) * 3,
-        scratch_shapes=[pltpu.VMEM((2, width // 2, width), jnp.float32)],
         compiler_params=LIMIT,
         name="dense",
     )(weight, cotangent, placing, *parts)
 
 
-def write_messages(slots, same_ref, came_ref, half, out_refs):
-    for i, ref in enumerate(out_refs):
-        start = (i + 1) * slots % same_ref.shape[0]
-        ref[:slots] = same_ref[start : start + slots]
-        ref[slots : 2 * slots] = came_ref[start : start + slots]
-        ref[2 * slots :] = half
-
-
-def sum_halves(half_ref, held, slots, own_ref, message_refs, core_along, n_rep):
+def write_messages(core_along, slots, rows, same_ref, came_ref, half_ref, out_refs):
+    core = lax.axis_index("section") & 1
+
+    @pl.when(core == core_along)
+    def _():
+        for i, ref in enumerate(out_refs):
+            start = (i + 1) * slots % same_ref.shape[0]
+            ref[:slots] = same_ref[start : start + slots]
+            ref[slots : 2 * slots] = came_ref[start : start + slots]
+            ref[2 * slots : 2 * slots + rows[core_along]] = half_ref[: rows[core_along]]
+
+    @pl.when(core != core_along)
+    def _():
+        for ref in out_refs:
+            ref[: rows[1 - core_along]] = half_ref[: rows[1 - core_along]]
+
+
+def sum_parts(core_along, slots, rows, half_ref, held, own_ref, message_refs, n_rep):
     chip, chips = place_of_chip()
     core = lax.axis_index("section") & 1
 
     @pl.when(core == core_along)
     def _():
-        held[chip] = own_ref[...]
+        many = rows[core_along]
+        held[chip, :many] = own_ref[:many]
         for i, ref in enumerate(message_refs[: chips - 1]):
-            held[(chip + chips - i - 1) % chips] = ref[2 * slots :]
-        total = tree_sum([held[c].astype(jnp.float32) for c in range(chips)])
-        half_ref[...] = total.astype(jnp.bfloat16)
+            held[(chip + chips - i - 1) % chips, :many] = ref[2 * slots : 2 * slots + many]
+        total = tree_sum([held[c, :many].astype(jnp.float32) for c in range(chips)])
+        half_ref[:many] = total.astype(jnp.bfloat16)
 
     @pl.when(core != core_along)
     def _():
-        by_xor = [own_ref[...].astype(jnp.float32)]
-        by_xor += [ref[2 * slots :].astype(jnp.float32) for ref in message_refs[::-1]]
-        half_ref[...] = tree_sum(by_xor[:n_rep]).astype(jnp.bfloat16)
-
-
-def first_kernel(slots, same_ref, kept_ref, came_ref, half_ref, *out_refs):
-    rows = kept_ref.shape[0]
-    half = kept_ref[...] + came_ref[came_ref.shape[0] - rows :].astype(jnp.float32)
-    half_ref[...] = half.astype(jnp.bfloat16)
-    write_messages(slots, same_ref, came_ref, half_ref[...], out_refs)
-
-
-def second_kernel(slots, n_rep, many, same_ref, came_ref, own_ref, *refs):
+        many = rows[1 - core_along]
+        by_xor = [ref[:many].astype(jnp.float32) for ref in [own_ref] + list(message_refs[::-1])]
+        half_ref[:many] = tree_sum(by_xor[:n_rep]).astype(jnp.bfloat16)
+
+
+def first_kernel(slots, rows, same_ref, term_ref, came_ref, half_ref, *out_refs):
+    core = lax.axis_index("section") & 1
+    start = same_ref.shape[0]
+
+    @pl.when(core == 0)
+    def _():
+        other = came_ref[start : start + rows[0]].astype(jnp.float32)
+        half_ref[: rows[0]] = (term_ref[: rows[0]] + other).astype(jnp.bfloat16)
+
+    @pl.when(core == 1)
+    def _():
+        other = came_ref[start:].astype(jnp.float32)
+        half_ref[...] = (term_ref[rows[0] :] + other).astype(jnp.bfloat16)
+
+    write_messages(0, slots, rows, same_ref, came_ref, half_ref, out_refs)
+
+
+def second_kernel(slots, rows, n_rep, many, same_ref, came_ref, own_ref, *refs):
     message_refs, half_ref, out_refs, held = refs[:many], refs[many], refs[many + 1 : -1], refs[-1]
-    sum_halves(half_ref, held, slots, own_ref, message_refs, 0, n_rep)
-    write_messages(slots, same_ref, came_ref, half_ref[...], out_refs)
-
-
-def third_kernel(slots, n_rep, own_ref, *refs):
-    sum_halves(refs[-2], refs[-1], slots, own_ref, refs[:-2], 1, n_rep)
-
-
-def call_halves(kernel, name, operands, half, slots, many, held=()):
+    sum_parts(0, slots, rows, half_ref, held, own_ref, message_refs, n_rep)
+    write_messages(1, slots, rows, same_ref, came_ref, half_ref, out_refs)
+
+
+def third_kernel(slots, rows, n_rep, own_ref, *refs):
+    sum_parts(1, slots, rows, refs[-2], refs[-1], own_ref, refs[:-2], n_rep)
+
+
+def call_parts(kernel, name, operands, half, message, many, held=()):
     shapes = [jax.ShapeDtypeStruct(half, jnp.bfloat16)]
-    shapes += [jax.ShapeDtypeStruct((2 * slots + half[0], half[1]), jnp.bfloat16)] * many
+    shapes += [jax.ShapeDtypeStruct(message, jnp.bfloat16)] * many
     return pl.pallas_call(
         kernel,
         out_shape=shapes,
@@ -232,16 +263,26 @@
     )(*first, *operands)
 
 
-def finish_kernel(own_ref, came_ref, out_ref):
-    core = lax.axis_index("section") & 1
-    out_ref[core] = own_ref[...].astype(jnp.float32)
-    out_ref[1 - core] = came_ref[...].astype(jnp.float32)
-
-
-def finish(own, came):
-    return pl.pallas_call(
-        finish_kernel,
-        out_shape=jax.ShapeDtypeStruct((2,) + own.shape, jnp.float32),
+def finish_kernel(rows, own_ref, came_ref, out_ref):
+    core = lax.axis_index("section") & 1
+    low, high = rows
+
+    @pl.when(core == 0)
+    def _():
+        out_ref[:low] = own_ref[:low].astype(jnp.float32)
+        out_ref[low:] = came_ref[...].astype(jnp.float32)
+
+    @pl.when(core == 1)
+    def _():
+        out_ref[:low] = came_ref[:low].astype(jnp.float32)
+        out_ref[low:] = own_ref[...].astype(jnp.float32)
+
+
+def finish(own, came, rows):
+    width = own.shape[1]
+    return pl.pallas_call(
+        functools.partial(finish_kernel, rows),
+        out_shape=jax.ShapeDtypeStruct((width, width), jnp.float32),
         in_specs=[VMEM] * 2,
         out_specs=VMEM,
         compiler_params=LIMIT,
@@ -287,34 +328,32 @@
     parts = list(partials(adj_src[:, 0], wide, [own] + blocks[1:]))
     others = across(n_rep)
     parts = parts[:1] + [swap(part, "rep", j) for part, j in zip(parts[1:], others)]
-    same, kept, sent = dense(parts, weight, cotangent, placing)
+    same, term, sent = dense(parts, weight, cotangent, placing, slots)
     came = swap(sent, "section", 1)
     chips = n_section // 2
     steps = across(max(n_rep, chips))
-    half_shape = (width // 2, width)
-    held = [(chips,) + half_shape]
-    half, *first = call_halves(
-        functools.partial(first_kernel, slots), "first", [same, kept, came], half_shape, slots, len(steps)
+    many = len(steps)
+    rows = parts_of(width, slots)
+    part = (rows[1], width)
+    held = [(chips,) + part]
+    message = (max(rows[1], 2 * slots + rows[0]), width)
+    operands = [same, term, came]
+    half, *first = call_parts(
+        functools.partial(first_kernel, slots, rows), "first", operands, part, message, many
     )
     first = [exchange(m, 0, i + 1, j) for i, (m, j) in enumerate(zip(first, steps))]
     relaid = store(0, same, came, first, n_section, slots)
-    half, *second = call_halves(
-        functools.partial(second_kernel, slots, n_rep, len(steps)),
-        "second",
-        [same, came, half, *first],
-        half_shape,
-        slots,
-        len(steps),
-        held,
-    )
+    message = (2 * slots + rows[1], width)
+    second = functools.partial(second_kernel, slots, rows, n_rep, many)
+    operands = [same, came, half, *first]
+    half, *second = call_parts(second, "second", operands, part, message, many, held)
     second = [exchange(m, 1, i + 1, j) for i, (m, j) in enumerate(zip(second, steps))]
-    (half,) = call_halves(
-        functools.partial(third_kernel, slots, n_rep), "third", [half, *second], half_shape, slots, 0, held
-    )
+    third = functools.partial(third_kernel, slots, rows, n_rep)
+    (half,) = call_parts(third, "third", [half, *second], part, part, 0, held)
     relaid = store(1, same, came, second, n_section, slots, relaid)
     half, relaid = lax.optimization_barrier((half, relaid))
-    weight_grad = finish(half, swap(half, "section", 1))
-    return (relaid.reshape(1, 1, n_section, slots, width), weight_grad.reshape(width, width))
+    weight_grad = finish(half, swap(half, "section", 1), rows)
+    return (relaid.reshape(1, 1, n_section, slots, width), weight_grad)
 
 
 def solution(mesh):

time: 40.6 us -> 40.6 us (level)
  no operation moved by 1% of the time
where the time goes in v15:
time: 40.6 us; the launch traced here: 40.4 us
  starting transfers between devices  19.1 us (47%)
  waiting for transfers between devices  15.4 us (38%)
  Pallas kernels  2.62 us (6%)
  local copies, waits for them, and re-layouts  2.55 us (6%)
  between operations  0.74 us (2%)
    ppermute x12, starting transfers between devices, swap(): lax.ppermute(value, axis, [(i, i ^ j) for i in range(lax.axis_size(axis))])  9.89 us
    ppermute x12, waiting for transfers between devices, swap(): lax.ppermute(value, axis, [(i, i ^ j) for i in range(lax.axis_size(axis))])  9.76 us
    ppermute x6, starting transfers between devices, exchange(): return lax.ppermute(value, ('section', 'rep'), pairs)  9.2 us
    ppermute x6, waiting for transfers between devices, exchange(): return lax.ppermute(value, ('section', 'rep'), pairs)  5.64 us
    unnamed x12, local copies, waits for them, and re-layouts  2.55 us
  transfers between devices with their start and end apart: 18, of which 16 were waited for; matrix products, arithmetic and copies ran while one was open for 0% of the time, Pallas kernels for 2%

profile of v15, /device:TPU:0, one launch (start us, length us, event | category | flops | bytes accessed | tf_op | source)
XLA Modules:
  0.0 40.4 jit_solution(12734146126782280267)
XLA Ops:
  0.6 4.1 %collective-permute-start.2 = (bf16[128,256]{1,0:T(8,128)(2,1)}, bf16[128,256]{1,0:T(8,128)(2,1)S(1)}, u32[]{:S(2)}, u32[]{:S(2)}) collective-permute-start(bf16[128,256]{1,0:T(8,128)(2,1)} %own_ref.1), channel_id=1, source_target_pairs={{0,16},{4,20},{8,24},{12,28},{16,0},{20,4},{24,8},{28,12},{1,17},{... | collective-permute-start | bytes 196616 | tf_op jit(solution)/shard_map/ppermute | solution.py:94
  4.7 1.3 %collective-permute-start.1 = (bf16[128,256]{1,0:T(8,128)(2,1)}, bf16[128,256]{1,0:T(8,128)(2,1)S(1)}, u32[]{:S(2)}, u32[]{:S(2)}) collective-permute-start(bf16[128,256]{1,0:T(8,128)(2,1)} %own_ref.1), channel_id=1, source_target_pairs={{0,24},{4,28},{8,16},{12,20},{16,8},{20,12},{24,0},{28,4},{1,25},{... | collective-permute-start | bytes 196616 | tf_op jit(solution)/shard_map/ppermute | solution.py:94
  6.1 0.2 collective-permute-start
  6.3 0.0 collective-permute-start.3
  6.3 0.7 %copy-done.5 = s32[128,1]{0,1:T(1,128)S(1)} copy-done((s32[128,1]{0,1:T(1,128)S(1)}, s32[128,1]{0,1:T(1,128)}, u32[]{:S(2)}) %copy-start.5) | copy-done | bytes 536
  7.0 1.0 %copy-done = bf16[4,1,4,128,128]{4,3,2,1,0:T(8,128)(2,1)S(1)} copy-done((bf16[4,1,4,128,128]{4,3,2,1,0:T(8,128)(2,1)S(1)}, bf16[4,1,4,128,128]{4,3,2,1,0:T(8,128)(2,1)}, u32[]{:S(2)}) %copy-start) | copy-done | bytes 524312
  8.0 0.8 %copy-done.2 = bf16[128,256]{1,0:T(8,128)(2,1)S(1)} copy-done((bf16[128,256]{1,0:T(8,128)(2,1)S(1)}, bf16[128,256]{1,0:T(8,128)(2,1)}, u32[]{:S(2)}) %copy-start.2) | copy-done | bytes 65560
  8.9 0.2 prepare.1
  9.1 0.0 collective-permute-done.2.refs_4_
  9.1 2.1 %collective-permute-done.1.refs_6_ = bf16[128,256]{1,0:T(8,128)(2,1)S(1)} collective-permute-done((bf16[128,256]{1,0:T(8,128)(2,1)}, bf16[128,256]{1,0:T(8,128)(2,1)S(1)}, u32[]{:S(2)}, u32[]{:S(2)}) %collective-permute-start.1) | collective-permute-done | bytes 65568 | tf_op jit(solution)/shard_map/ppermute | solution.py:94
  11.2 0.1 collective-permute-done.refs_2_
  11.3 0.0 collective-permute-start.4
  11.3 0.5 %collective-permute-start.5 = (bf16[128,256]{1,0:T(8,128)(2,1)S(1)}, bf16[128,256]{1,0:T(8,128)(2,1)S(1)}, u32[]{:S(2)}, u32[]{:S(2)}) collective-permute-start(bf16[128,256]{1,0:T(8,128)(2,1)S(1)} %collective-permute-done.2.refs_4_), channel_id=1, source_target_pairs={{0,4},{4,0},{8,12},{12,8},{16,20},{20,16},{24,28},{28,24},{1,5},{5... | collective-permute-start | bytes 196616 | tf_op jit(solution)/shard_map/ppermute | solution.py:94
  11.8 0.0 collective-permute-start.6
  11.8 0.0 collective-permute-done.3.refs_1_
  11.8 0.7 %collective-permute-done.4.refs_3_ = bf16[128,256]{1,0:T(8,128)(2,1)S(1)} collective-permute-done((bf16[128,256]{1,0:T(8,128)(2,1)S(1)}, bf16[128,256]{1,0:T(8,128)(2,1)S(1)}, u32[]{:S(2)}, u32[]{:S(2)}) %collective-permute-start.4) | collective-permute-done | bytes 65568 | tf_op jit(solution)/shard_map/ppermute | solution.py:94
  12.5 0.2 collective-permute-done.5.refs_5_
  12.7 0.4 collective-permute-done.6.refs_7_
  13.0 0.0 copy-done.4
  13.0 0.4 %partials.1 = (bf16[128,256]{1,0:T(8,128)(2,1)S(1)}, bf16[128,256]{1,0:T(8,128)(2,1)S(1)}, bf16[128,256]{1,0:T(8,128)(2,1)S(1)}, bf16[128,256]{1,0:T(8,128)(2,1)S(1)}) custom-call(s32[4,4]{1,0:T(4,128)S(1)} %bitcast.5, bf16[4,128,512]{2,1,0:T(8,128)(2,1)S(1)} %get-tuple-element.32.wide_ref, bf16[128,256]{1,0:T(8,128)(2,1)S(1)} %get-tuple-element.33.refs_0_, ...), custom_call_target="tpu_custom_call" | custom-call | tf_op jit(solution)/shard_map/partials/pallas_call | solution.py:82
  13.5 2.5 %collective-permute-start.7 = (bf16[128,256]{1,0:T(8,128)(2,1)S(1)}, bf16[128,256]{1,0:T(8,128)(2,1)S(1)}, u32[]{:S(2)}, u32[]{:S(2)}) collective-permute-start(bf16[128,256]{1,0:T(8,128)(2,1)S(1)} %get-tuple-element.38), channel_id=1, source_target_pairs={{0,3},{1,2},{2,1},{3,0},{4,7},{5,6},{6,5},{7,4},{8,11},{9,10},{10,... | collective-permute-start | bytes 196616 | tf_op jit(solution)/shard_map/ppermute | solution.py:94
  16.0 0.5 %collective-permute-start.8 = (bf16[128,256]{1,0:T(8,128)(2,1)S(1)}, bf16[128,256]{1,0:T(8,128)(2,1)S(1)}, u32[]{:S(2)}, u32[]{:S(2)}) collective-permute-start(bf16[128,256]{1,0:T(8,128)(2,1)S(1)} %get-tuple-element.39), channel_id=1, source_target_pairs={{0,2},{1,3},{2,0},{3,1},{4,6},{5,7},{6,4},{7,5},{8,10},{9,11},{10,... | collective-permute-start | bytes 196616 | tf_op jit(solution)/shard_map/ppermute | solution.py:94
  16.5 0.5 %collective-permute-start.9 = (bf16[128,256]{1,0:T(8,128)(2,1)S(1)}, bf16[128,256]{1,0:T(8,128)(2,1)S(1)}, u32[]{:S(2)}, u32[]{:S(2)}) collective-permute-start(bf16[128,256]{1,0:T(8,128)(2,1)S(1)} %get-tuple-element.40), channel_id=1, source_target_pairs={{0,1},{1,0},{2,3},{3,2},{4,5},{5,4},{6,7},{7,6},{8,9},{9,8},{10,11... | collective-permute-start | bytes 196616 | tf_op jit(solution)/shard_map/ppermute | solution.py:94
  17.0 1.7 %collective-permute-done.7.refs_1_ = bf16[128,256]{1,0:T(8,128)(2,1)S(1)} collective-permute-done((bf16[128,256]{1,0:T(8,128)(2,1)S(1)}, bf16[128,256]{1,0:T(8,128)(2,1)S(1)}, u32[]{:S(2)}, u32[]{:S(2)}) %collective-permute-start.7) | collective-permute-done | bytes 65568 | tf_op jit(solution)/shard_map/ppermute | solution.py:94
  18.7 1.5 %collective-permute-done.8.refs_2_ = bf16[128,256]{1,0:T(8,128)(2,1)S(1)} collective-permute-done((bf16[128,256]{1,0:T(8,128)(2,1)S(1)}, bf16[128,256]{1,0:T(8,128)(2,1)S(1)}, u32[]{:S(2)}, u32[]{:S(2)}) %collective-permute-start.8) | collective-permute-done | bytes 65568 | tf_op jit(solution)/shard_map/ppermute | solution.py:94
  20.2 0.5 %collective-permute-done.9.refs_3_ = bf16[128,256]{1,0:T(8,128)(2,1)S(1)} collective-permute-done((bf16[128,256]{1,0:T(8,128)(2,1)S(1)}, bf16[128,256]{1,0:T(8,128)(2,1)S(1)}, u32[]{:S(2)}, u32[]{:S(2)}) %collective-permute-start.9) | collective-permute-done | bytes 65568 | tf_op jit(solution)/shard_map/ppermute | solution.py:94
  20.7 0.0 copy-done.1
  20.7 0.0 copy-done.3
  20.8 0.4 %dense.1 = (bf16[128,256]{1,0:T(8,128)(2,1)S(1)}, f32[256,256]{1,0:T(8,128)S(1)}, bf16[288,256]{1,0:T(8,128)(2,1)S(1)}) custom-call(bf16[256,256]{1,0:T(8,128)(2,1)S(1)} %copy-done.1, bf16[128,256]{1,0:T(8,128)(2,1)S(1)} %copy-done.3, bf16[256,128]{1,0:T(8,128)(2,1)S(1)} %get-tuple-element.31.placing_ref, bf16[128,256]{1,0:T(8,128)(2,1)S(1)} %get-tuple-element.37.refs_0_, ...), custom_call_target="tpu_custom_call" | custom-call | tf_op jit(solution)/shard_map/dense/pallas_call | solution.py:138
  21.2 0.1 collective-permute-start.10
  21.3 1.4 %collective-permute-done.10.came_ref.refs_1_ = bf16[288,256]{1,0:T(8,128)(2,1)S(1)} collective-permute-done((bf16[288,256]{1,0:T(8,128)(2,1)S(1)}, bf16[288,256]{1,0:T(8,128)(2,1)S(1)}, u32[]{:S(2)}, u32[]{:S(2)}) %collective-permute-start.10) | collective-permute-done | bytes 147488 | tf_op jit(solution)/shard_map/ppermute | solution.py:94
  22.7 1.0 %collective-permute-start.11 = (bf16[160,256]{1,0:T(8,128)(2,1)S(1)}, bf16[160,256]{1,0:T(8,128)(2,1)S(1)}, u32[]{:S(2)}, u32[]{:S(2)}) collective-permute-start(bf16[160,256]{1,0:T(8,128)(2,1)S(1)} %get-tuple-element.45), channel_id=1, source_target_pairs={{0,8},{1,9},{2,10},{3,11},{4,7},{5,6},{6,5},{7,4},{8,16},{9,17},{1... | collective-permute-start | bytes 245768 | tf_op jit(solution)/shard_map/ppermute | solution.py:301
  23.6 2.6 %collective-permute-start.12 = (bf16[160,256]{1,0:T(8,128)(2,1)S(1)}, bf16[160,256]{1,0:T(8,128)(2,1)S(1)}, u32[]{:S(2)}, u32[]{:S(2)}) collective-permute-start(bf16[160,256]{1,0:T(8,128)(2,1)S(1)} %get-tuple-element.46), channel_id=1, source_target_pairs={{0,16},{1,17},{2,18},{3,19},{4,6},{5,7},{6,4},{7,5},{8,24},{9,25},... | collective-permute-start | bytes 245768 | tf_op jit(solution)/shard_map/ppermute | solution.py:301
  26.3 2.0 %collective-permute-start.13 = (bf16[160,256]{1,0:T(8,128)(2,1)S(1)}, bf16[160,256]{1,0:T(8,128)(2,1)S(1)}, u32[]{:S(2)}, u32[]{:S(2)}) collective-permute-start(bf16[160,256]{1,0:T(8,128)(2,1)S(1)} %get-tuple-element.47), channel_id=1, source_target_pairs={{0,24},{1,25},{2,26},{3,27},{4,5},{5,4},{6,7},{7,6},{8,0},{9,1},{1... | collective-permute-start | bytes 245768 | tf_op jit(solution)/shard_map/ppermute | solution.py:301
  28.3 0.7 %collective-permute-done.11.refs_0_ = bf16[160,256]{1,0:T(8,128)(2,1)S(1)} collective-permute-done((bf16[160,256]{1,0:T(8,128)(2,1)S(1)}, bf16[160,256]{1,0:T(8,128)(2,1)S(1)}, u32[]{:S(2)}, u32[]{:S(2)}) %collective-permute-start.11) | collective-permute-done | bytes 81952 | tf_op jit(solution)/shard_map/ppermute | solution.py:301
  29.0 0.8 %collective-permute-done.12.refs_1_ = bf16[160,256]{1,0:T(8,128)(2,1)S(1)} collective-permute-done((bf16[160,256]{1,0:T(8,128)(2,1)S(1)}, bf16[160,256]{1,0:T(8,128)(2,1)S(1)}, u32[]{:S(2)}, u32[]{:S(2)}) %collective-permute-start.12) | collective-permute-done | bytes 81952 | tf_op jit(solution)/shard_map/ppermute | solution.py:301
  29.8 1.3 %collective-permute-done.13.refs_2_ = bf16[160,256]{1,0:T(8,128)(2,1)S(1)} collective-permute-done((bf16[160,256]{1,0:T(8,128)(2,1)S(1)}, bf16[160,256]{1,0:T(8,128)(2,1)S(1)}, u32[]{:S(2)}, u32[]{:S(2)}) %collective-permute-start.13) | collective-permute-done | bytes 81952 | tf_op jit(solution)/shard_map/ppermute | solution.py:301
  31.2 0.1 second.1
  31.2 1.2 %collective-permute-start.14 = (bf16[224,256]{1,0:T(8,128)(2,1)S(1)}, bf16[224,256]{1,0:T(8,128)(2,1)S(1)}, u32[]{:S(2)}, u32[]{:S(2)}) collective-permute-start(bf16[224,256]{1,0:T(8,128)(2,1)S(1)} %get-tuple-element.49), channel_id=1, source_target_pairs={{0,3},{1,2},{2,1},{3,0},{4,12},{5,13},{6,14},{7,15},{8,11},{9,10},... | collective-permute-start | bytes 344072 | tf_op jit(solution)/shard_map/ppermute | solution.py:301
  32.5 1.0 %collective-permute-start.15 = (bf16[224,256]{1,0:T(8,128)(2,1)S(1)}, bf16[224,256]{1,0:T(8,128)(2,1)S(1)}, u32[]{:S(2)}, u32[]{:S(2)}) collective-permute-start(bf16[224,256]{1,0:T(8,128)(2,1)S(1)} %get-tuple-element.50), channel_id=1, source_target_pairs={{0,2},{1,3},{2,0},{3,1},{4,20},{5,21},{6,22},{7,23},{8,10},{9,11},... | collective-permute-start | bytes 344072 | tf_op jit(solution)/shard_map/ppermute | solution.py:301
  33.5 1.3 %collective-permute-start.16 = (bf16[224,256]{1,0:T(8,128)(2,1)S(1)}, bf16[224,256]{1,0:T(8,128)(2,1)S(1)}, u32[]{:S(2)}, u32[]{:S(2)}) collective-permute-start(bf16[224,256]{1,0:T(8,128)(2,1)S(1)} %get-tuple-element.51), channel_id=1, source_target_pairs={{0,1},{1,0},{2,3},{3,2},{4,28},{5,29},{6,30},{7,31},{8,9},{9,8},{1... | collective-permute-start | bytes 344072 | tf_op jit(solution)/shard_map/ppermute | solution.py:301
  34.8 0.7 %store.2._ = bf16[8,32,256]{2,1,0:T(8,128)(2,1)} custom-call(bf16[128,256]{1,0:T(8,128)(2,1)S(1)} %get-tuple-element.41.same_ref.refs_0_, bf16[288,256]{1,0:T(8,128)(2,1)S(1)} %collective-permute-done.10.came_ref.refs_1_, bf16[160,256]{1,0:T(8,128)(2,1)S(1)} %collective-permute-done.11.refs_0_, bf16[160,256]{1,0:T(8,128)(2,1)S(1)} %collective-permute-done.12.refs_1_, ...), custom_call_target="tpu_custom_call" | custom-call | tf_op jit(solution)/shard_map/store/pallas_call | solution.py:254
  35.5 1.6 %collective-permute-done.14.refs_0_.refs_2_ = bf16[224,256]{1,0:T(8,128)(2,1)S(1)} collective-permute-done((bf16[224,256]{1,0:T(8,128)(2,1)S(1)}, bf16[224,256]{1,0:T(8,128)(2,1)S(1)}, u32[]{:S(2)}, u32[]{:S(2)}) %collective-permute-start.14) | collective-permute-done | bytes 114720 | tf_op jit(solution)/shard_map/ppermute | solution.py:301
  37.1 1.1 %collective-permute-done.15.refs_1_.refs_3_ = bf16[224,256]{1,0:T(8,128)(2,1)S(1)} collective-permute-done((bf16[224,256]{1,0:T(8,128)(2,1)S(1)}, bf16[224,256]{1,0:T(8,128)(2,1)S(1)}, u32[]{:S(2)}, u32[]{:S(2)}) %collective-permute-start.15) | collective-permute-done | bytes 114720 | tf_op jit(solution)/shard_map/ppermute | solution.py:301
  38.2 0.1 collective-permute-done.16.refs_2_.refs_4_
  38.3 0.1 collective-permute-start.17
  38.4 1.3 %collective-permute-done.17.came_ref = bf16[160,256]{1,0:T(8,128)(2,1)S(1)} collective-permute-done((bf16[160,256]{1,0:T(8,128)(2,1)S(1)}, bf16[160,256]{1,0:T(8,128)(2,1)S(1)}, u32[]{:S(2)}, u32[]{:S(2)}) %collective-permute-start.17) | collective-permute-done | bytes 81952 | tf_op jit(solution)/shard_map/ppermute | solution.py:94
  39.7 0.7 %finish.1 = f32[256,256]{1,0:T(8,128)} custom-call(bf16[160,256]{1,0:T(8,128)(2,1)S(1)} %third.1.own_ref, bf16[160,256]{1,0:T(8,128)(2,1)S(1)} %collective-permute-done.17.came_ref), custom_call_target="tpu_custom_call" | custom-call | tf_op jit(solution)/shard_map/finish/pallas_call | solution.py:283
  (9 shorter events, 0.1 us)
Async XLA Ops:
  0.6 8.5 %collective-permute-start.2 = (bf16[128,256]{1,0:T(8,128)(2,1)}, bf16[128,256]{1,0:T(8,128)(2,1)S(1)}, u32[]{:S(2)}, u32[]{:S(2)}) collective-permute-start(bf16[128,256]{1,0:T(8,128)(2,1)} %own_ref.1), channel_id=1, source_target_pairs={{0,16},{4,20},{8,24},{12,28},{16,0},{20,4},{24,8},{28,12},{1,17},{... | collective-permute-start | bytes 196616 | tf_op jit(solution)/shard_map/ppermute | solution.py:94
  4.7 6.4 %collective-permute-start.1 = (bf16[128,256]{1,0:T(8,128)(2,1)}, bf16[128,256]{1,0:T(8,128)(2,1)S(1)}, u32[]{:S(2)}, u32[]{:S(2)}) collective-permute-start(bf16[128,256]{1,0:T(8,128)(2,1)} %own_ref.1), channel_id=1, source_target_pairs={{0,24},{4,28},{8,16},{12,20},{16,8},{20,12},{24,0},{28,4},{1,25},{... | collective-permute-start | bytes 196616 | tf_op jit(solution)/shard_map/ppermute | solution.py:94
  6.1 5.2 %collective-permute-start = (bf16[128,256]{1,0:T(8,128)(2,1)}, bf16[128,256]{1,0:T(8,128)(2,1)S(1)}, u32[]{:S(2)}, u32[]{:S(2)}) collective-permute-start(bf16[128,256]{1,0:T(8,128)(2,1)} %own_ref.1), channel_id=1, source_target_pairs={{0,8},{4,12},{8,0},{12,4},{16,24},{20,28},{24,16},{28,20},{1,9},{5... | collective-permute-start | bytes 196616 | tf_op jit(solution)/shard_map/ppermute | solution.py:94
  6.3 5.5 %collective-permute-start.3 = (bf16[128,256]{1,0:T(8,128)(2,1)}, bf16[128,256]{1,0:T(8,128)(2,1)S(1)}, u32[]{:S(2)}, u32[]{:S(2)}) collective-permute-start(bf16[128,256]{1,0:T(8,128)(2,1)} %own_ref.1), channel_id=1, source_target_pairs={{0,4},{4,0},{8,12},{12,8},{16,20},{20,16},{24,28},{28,24},{1,5},{5... | collective-permute-start | bytes 196616 | tf_op jit(solution)/shard_map/ppermute | solution.py:94
  6.3 0.7 %copy-start.5 = (s32[128,1]{0,1:T(1,128)S(1)}, s32[128,1]{0,1:T(1,128)}, u32[]{:S(2)}) copy-start(s32[128,1]{0,1:T(1,128)} %param.11) | copy-start | bytes 1540
  7.0 1.0 %copy-start = (bf16[4,1,4,128,128]{4,3,2,1,0:T(8,128)(2,1)S(1)}, bf16[4,1,4,128,128]{4,3,2,1,0:T(8,128)(2,1)}, u32[]{:S(2)}) copy-start(bf16[4,1,4,128,128]{4,3,2,1,0:T(8,128)(2,1)} %param.7) | copy-start | bytes 1572868
  8.0 0.8 %copy-start.2 = (bf16[128,256]{1,0:T(8,128)(2,1)S(1)}, bf16[128,256]{1,0:T(8,128)(2,1)}, u32[]{:S(2)}) copy-start(bf16[128,256]{1,0:T(8,128)(2,1)} %own_ref.1) | copy-start | bytes 196612
  11.3 1.8 %copy-start.4 = (s32[4,1,4]{2,1,0:T(1,128)S(1)}, s32[4,1,4]{2,1,0:T(1,128)}, u32[]{:S(2)}) copy-start(s32[4,1,4]{2,1,0:T(1,128)} %param.8) | copy-start | bytes 196
  11.3 1.3 %collective-permute-start.4 = (bf16[128,256]{1,0:T(8,128)(2,1)S(1)}, bf16[128,256]{1,0:T(8,128)(2,1)S(1)}, u32[]{:S(2)}, u32[]{:S(2)}) collective-permute-start(bf16[128,256]{1,0:T(8,128)(2,1)S(1)} %collective-permute-done.refs_2_), channel_id=1, source_target_pairs={{0,4},{4,0},{8,12},{12,8},{16,20},{20,16},{24,28},{28,24},{1,5},{5... | collective-permute-start | bytes 196616 | tf_op jit(solution)/shard_map/ppermute | solution.py:94
  11.3 1.4 %collective-permute-start.5 = (bf16[128,256]{1,0:T(8,128)(2,1)S(1)}, bf16[128,256]{1,0:T(8,128)(2,1)S(1)}, u32[]{:S(2)}, u32[]{:S(2)}) collective-permute-start(bf16[128,256]{1,0:T(8,128)(2,1)S(1)} %collective-permute-done.2.refs_4_), channel_id=1, source_target_pairs={{0,4},{4,0},{8,12},{12,8},{16,20},{20,16},{24,28},{28,24},{1,5},{5... | collective-permute-start | bytes 196616 | tf_op jit(solution)/shard_map/ppermute | solution.py:94
  11.8 1.3 %collective-permute-start.6 = (bf16[128,256]{1,0:T(8,128)(2,1)S(1)}, bf16[128,256]{1,0:T(8,128)(2,1)S(1)}, u32[]{:S(2)}, u32[]{:S(2)}) collective-permute-start(bf16[128,256]{1,0:T(8,128)(2,1)S(1)} %collective-permute-done.1.refs_6_), channel_id=1, source_target_pairs={{0,4},{4,0},{8,12},{12,8},{16,20},{20,16},{24,28},{28,24},{1,5},{5... | collective-permute-start | bytes 196616 | tf_op jit(solution)/shard_map/ppermute | solution.py:94
  13.0 7.7 %copy-start.1 = (bf16[256,256]{1,0:T(8,128)(2,1)S(1)}, bf16[256,256]{1,0:T(8,128)(2,1)}, u32[]{:S(2)}) copy-start(bf16[256,256]{1,0:T(8,128)(2,1)} %weight_ref.1) | copy-start | bytes 393220
  13.0 7.7 %copy-start.3 = (bf16[128,256]{1,0:T(8,128)(2,1)S(1)}, bf16[128,256]{1,0:T(8,128)(2,1)}, u32[]{:S(2)}) copy-start(bf16[128,256]{1,0:T(8,128)(2,1)} %cot_ref.1) | copy-start | bytes 196612
  13.5 5.3 %collective-permute-start.7 = (bf16[128,256]{1,0:T(8,128)(2,1)S(1)}, bf16[128,256]{1,0:T(8,128)(2,1)S(1)}, u32[]{:S(2)}, u32[]{:S(2)}) collective-permute-start(bf16[128,256]{1,0:T(8,128)(2,1)S(1)} %get-tuple-element.38), channel_id=1, source_target_pairs={{0,3},{1,2},{2,1},{3,0},{4,7},{5,6},{6,5},{7,4},{8,11},{9,10},{10,... | collective-permute-start | bytes 196616 | tf_op jit(solution)/shard_map/ppermute | solution.py:94
  16.0 4.3 %collective-permute-start.8 = (bf16[128,256]{1,0:T(8,128)(2,1)S(1)}, bf16[128,256]{1,0:T(8,128)(2,1)S(1)}, u32[]{:S(2)}, u32[]{:S(2)}) collective-permute-start(bf16[128,256]{1,0:T(8,128)(2,1)S(1)} %get-tuple-element.39), channel_id=1, source_target_pairs={{0,2},{1,3},{2,0},{3,1},{4,6},{5,7},{6,4},{7,5},{8,10},{9,11},{10,... | collective-permute-start | bytes 196616 | tf_op jit(solution)/shard_map/ppermute | solution.py:94
  16.5 4.3 %collective-permute-start.9 = (bf16[128,256]{1,0:T(8,128)(2,1)S(1)}, bf16[128,256]{1,0:T(8,128)(2,1)S(1)}, u32[]{:S(2)}, u32[]{:S(2)}) collective-permute-start(bf16[128,256]{1,0:T(8,128)(2,1)S(1)} %get-tuple-element.40), channel_id=1, source_target_pairs={{0,1},{1,0},{2,3},{3,2},{4,5},{5,4},{6,7},{7,6},{8,9},{9,8},{10,11... | collective-permute-start | bytes 196616 | tf_op jit(solution)/shard_map/ppermute | solution.py:94
  21.2 1.4 %collective-permute-start.10 = (bf16[288,256]{1,0:T(8,128)(2,1)S(1)}, bf16[288,256]{1,0:T(8,128)(2,1)S(1)}, u32[]{:S(2)}, u32[]{:S(2)}) collective-permute-start(bf16[288,256]{1,0:T(8,128)(2,1)S(1)} %get-tuple-element.42), channel_id=1, source_target_pairs={{0,4},{4,0},{8,12},{12,8},{16,20},{20,16},{24,28},{28,24},{1,5},{5... | collective-permute-start | bytes 442376 | tf_op jit(solution)/shard_map/ppermute | solution.py:94
  22.7 6.4 %collective-permute-start.11 = (bf16[160,256]{1,0:T(8,128)(2,1)S(1)}, bf16[160,256]{1,0:T(8,128)(2,1)S(1)}, u32[]{:S(2)}, u32[]{:S(2)}) collective-permute-start(bf16[160,256]{1,0:T(8,128)(2,1)S(1)} %get-tuple-element.45), channel_id=1, source_target_pairs={{0,8},{1,9},{2,10},{3,11},{4,7},{5,6},{6,5},{7,4},{8,16},{9,17},{1... | collective-permute-start | bytes 245768 | tf_op jit(solution)/shard_map/ppermute | solution.py:301
  23.6 6.2 %collective-permute-start.12 = (bf16[160,256]{1,0:T(8,128)(2,1)S(1)}, bf16[160,256]{1,0:T(8,128)(2,1)S(1)}, u32[]{:S(2)}, u32[]{:S(2)}) collective-permute-start(bf16[160,256]{1,0:T(8,128)(2,1)S(1)} %get-tuple-element.46), channel_id=1, source_target_pairs={{0,16},{1,17},{2,18},{3,19},{4,6},{5,7},{6,4},{7,5},{8,24},{9,25},... | collective-permute-start | bytes 245768 | tf_op jit(solution)/shard_map/ppermute | solution.py:301
  26.3 4.9 %collective-permute-start.13 = (bf16[160,256]{1,0:T(8,128)(2,1)S(1)}, bf16[160,256]{1,0:T(8,128)(2,1)S(1)}, u32[]{:S(2)}, u32[]{:S(2)}) collective-permute-start(bf16[160,256]{1,0:T(8,128)(2,1)S(1)} %get-tuple-element.47), channel_id=1, source_target_pairs={{0,24},{1,25},{2,26},{3,27},{4,5},{5,4},{6,7},{7,6},{8,0},{9,1},{1... | collective-permute-start | bytes 245768 | tf_op jit(solution)/shard_map/ppermute | solution.py:301
  31.2 5.8 %collective-permute-start.14 = (bf16[224,256]{1,0:T(8,128)(2,1)S(1)}, bf16[224,256]{1,0:T(8,128)(2,1)S(1)}, u32[]{:S(2)}, u32[]{:S(2)}) collective-permute-start(bf16[224,256]{1,0:T(8,128)(2,1)S(1)} %get-tuple-element.49), channel_id=1, source_target_pairs={{0,3},{1,2},{2,1},{3,0},{4,12},{5,13},{6,14},{7,15},{8,11},{9,10},... | collective-permute-start | bytes 344072 | tf_op jit(solution)/shard_map/ppermute | solution.py:301
  32.5 5.7 %collective-permute-start.15 = (bf16[224,256]{1,0:T(8,128)(2,1)S(1)}, bf16[224,256]{1,0:T(8,128)(2,1)S(1)}, u32[]{:S(2)}, u32[]{:S(2)}) collective-permute-start(bf16[224,256]{1,0:T(8,128)(2,1)S(1)} %get-tuple-element.50), channel_id=1, source_target_pairs={{0,2},{1,3},{2,0},{3,1},{4,20},{5,21},{6,22},{7,23},{8,10},{9,11},... | collective-permute-start | bytes 344072 | tf_op jit(solution)/shard_map/ppermute | solution.py:301
  33.5 4.8 %collective-permute-start.16 = (bf16[224,256]{1,0:T(8,128)(2,1)S(1)}, bf16[224,256]{1,0:T(8,128)(2,1)S(1)}, u32[]{:S(2)}, u32[]{:S(2)}) collective-permute-start(bf16[224,256]{1,0:T(8,128)(2,1)S(1)} %get-tuple-element.51), channel_id=1, source_target_pairs={{0,1},{1,0},{2,3},{3,2},{4,28},{5,29},{6,30},{7,31},{8,9},{9,8},{1... | collective-permute-start | bytes 344072 | tf_op jit(solution)/shard_map/ppermute | solution.py:301
  38.3 1.3 %collective-permute-start.17 = (bf16[160,256]{1,0:T(8,128)(2,1)S(1)}, bf16[160,256]{1,0:T(8,128)(2,1)S(1)}, u32[]{:S(2)}, u32[]{:S(2)}) collective-permute-start(bf16[160,256]{1,0:T(8,128)(2,1)S(1)} %third.1.own_ref), channel_id=1, source_target_pairs={{0,4},{4,0},{8,12},{12,8},{16,20},{20,16},{24,28},{28,24},{1,5},{5... | collective-permute-start | bytes 245768 | tf_op jit(solution)/shard_map/ppermute | solution.py:94

commit v16 on v13

--- a/solution.py
+++ b/solution.py
@@ -232,21 +232,27 @@
     )(*first, *operands)
 
 
-def finish_kernel(own_ref, came_ref, out_ref):
+def half_kernel(mine, half_ref, *refs):
+    out_ref, wide, sem = refs[-3:]
     core = lax.axis_index("section") & 1
-    out_ref[core] = own_ref[...].astype(jnp.float32)
-    out_ref[1 - core] = came_ref[...].astype(jnp.float32)
-
-
-def finish(own, came):
-    return pl.pallas_call(
-        finish_kernel,
-        out_shape=jax.ShapeDtypeStruct((2,) + own.shape, jnp.float32),
-        in_specs=[VMEM] * 2,
-        out_specs=VMEM,
-        compiler_params=LIMIT,
-        name="finish",
-    )(own, came)
+    wide[...] = half_ref[...].astype(jnp.float32)
+    copy = pltpu.make_async_copy(wide, out_ref.at[core if mine else 1 - core], sem)
+    copy.start()
+    copy.wait()
+
+
+def store_half(mine, half, base=None):
+    operands = [half] if base is None else [half, base]
+    return pl.pallas_call(
+        functools.partial(half_kernel, mine),
+        out_shape=jax.ShapeDtypeStruct((2,) + half.shape, jnp.float32),
+        in_specs=[VMEM, HBM][: len(operands)],
+        out_specs=HBM,
+        scratch_shapes=[pltpu.VMEM(half.shape, jnp.float32), pltpu.SemaphoreType.DMA],
+        input_output_aliases={} if base is None else {1: 0},
+        compiler_params=LIMIT,
+        name="store_half",
+    )(*operands)
 
 
 def exchange(value, core_along, shift, j):
@@ -264,14 +270,12 @@
     n = lax.axis_size(axis)
     blocks = [None] * n
     blocks[0] = features
-    order = sorted(range(2, n, 2), key=lambda j: (j & 4, -(j & 2)))
-    for j in order:
+    far = n // 2 & -2
+    for j in sorted(range(2, n, 2), key=lambda j: (j & 4, -(j & 2))):
         blocks[j] = swap(features, axis, j)
     blocks[1] = swap(features, axis, 1)
-    came, ready = lax.optimization_barrier(([blocks[j] for j in order], ready))
-    for j, block in zip(order, came):
-        blocks[j] = block
-    for j in range(2, n, 2):
+    blocks[far], ready = lax.optimization_barrier((blocks[far], ready))
+    for j in sorted(range(2, n, 2), key=lambda j: -j):
         blocks[j + 1] = swap(blocks[j], axis, 1)
     return blocks, ready
 
@@ -313,7 +317,7 @@
     )
     relaid = store(1, same, came, second, n_section, slots, relaid)
     half, relaid = lax.optimization_barrier((half, relaid))
-    weight_grad = finish(half, swap(half, "section", 1))
+    weight_grad = store_half(False, swap(half, "section", 1), store_half(True, half))
     return (relaid.reshape(1, 1, n_section, slots, width), weight_grad.reshape(width, width))
 
 

time: 40.6 us -> 40.6 us (level)
  waiting for transfers between devices: 15.4 us -> 14.6 us
  Pallas kernels: 2.67 us -> 3.29 us
    ppermute x12, waiting for transfers between devices: 9.72 us -> 8.94 us  [swap(): lax.ppermute(value, axis, [(i, i ^ j) for i in range(lax.axis_size(axis))])]
    pallas_call x1 -> x2, Pallas kernels: 0.73 us -> 1.35 us  [store_half(): pl.pallas_call(functools.partial(half_kernel, mine), out_shape=jax.ShapeD...]
  transfers between devices with their start and end apart: 18 -> 18, of which waited for: 16 -> 16; matrix products, arithmetic and copies ran while one was open for 0% -> 0% of each run, Pallas kernels for 2% -> 4%
where the time goes in v16:
time: 40.6 us; the launch traced here: 40.4 us
  starting transfers between devices  19.2 us (47%)
  waiting for transfers between devices  14.6 us (36%)
  Pallas kernels  3.29 us (8%)
  local copies, waits for them, and re-layouts  2.55 us (6%)
  between operations  0.74 us (2%)
    ppermute x12, starting transfers between devices, swap(): lax.ppermute(value, axis, [(i, i ^ j) for i in range(lax.axis_size(axis))])  9.89 us
    ppermute x6, starting transfers between devices, exchange(): return lax.ppermute(value, ('section', 'rep'), pairs)  9.28 us
    ppermute x12, waiting for transfers between devices, swap(): lax.ppermute(value, axis, [(i, i ^ j) for i in range(lax.axis_size(axis))])  8.94 us
    ppermute x6, waiting for transfers between devices, exchange(): return lax.ppermute(value, ('section', 'rep'), pairs)  5.66 us
    unnamed x12, local copies, waits for them, and re-layouts  2.55 us
    pallas_call x2, Pallas kernels, store_half(): pl.pallas_call(functools.partial(half_kernel, mine), out_shape=jax.ShapeD...  1.35 us
  transfers between devices with their start and end apart: 18, of which 16 were waited for; matrix products, arithmetic and copies ran while one was open for 0% of the time, Pallas kernels for 4%

profile of v16, /device:TPU:0, one launch (start us, length us, event | category | flops | bytes accessed | tf_op | source)
XLA Modules:
  0.0 40.4 jit_solution(8640369623052867626)
XLA Ops:
  0.6 4.1 %collective-permute-start = (bf16[128,256]{1,0:T(8,128)(2,1)}, bf16[128,256]{1,0:T(8,128)(2,1)S(1)}, u32[]{:S(2)}, u32[]{:S(2)}) collective-permute-start(bf16[128,256]{1,0:T(8,128)(2,1)} %own_ref.1), channel_id=1, source_target_pairs={{0,16},{4,20},{8,24},{12,28},{16,0},{20,4},{24,8},{28,12},{1,17},{... | collective-permute-start | bytes 196616 | tf_op jit(solution)/shard_map/ppermute | solution.py:94
  4.7 1.3 %collective-permute-start.5 = (bf16[128,256]{1,0:T(8,128)(2,1)}, bf16[128,256]{1,0:T(8,128)(2,1)S(1)}, u32[]{:S(2)}, u32[]{:S(2)}) collective-permute-start(bf16[128,256]{1,0:T(8,128)(2,1)} %own_ref.1), channel_id=1, source_target_pairs={{0,24},{4,28},{8,16},{12,20},{16,8},{20,12},{24,0},{28,4},{1,25},{... | collective-permute-start | bytes 196616 | tf_op jit(solution)/shard_map/ppermute | solution.py:94
  6.1 0.2 collective-permute-start.2
  6.3 0.0 collective-permute-start.1
  6.3 0.7 %copy-done.5 = s32[128,1]{0,1:T(1,128)S(1)} copy-done((s32[128,1]{0,1:T(1,128)S(1)}, s32[128,1]{0,1:T(1,128)}, u32[]{:S(2)}) %copy-start.5) | copy-done | bytes 536
  7.0 1.0 %copy-done = bf16[4,1,4,128,128]{4,3,2,1,0:T(8,128)(2,1)S(1)} copy-done((bf16[4,1,4,128,128]{4,3,2,1,0:T(8,128)(2,1)S(1)}, bf16[4,1,4,128,128]{4,3,2,1,0:T(8,128)(2,1)}, u32[]{:S(2)}) %copy-start) | copy-done | bytes 524312
  8.0 0.8 %copy-done.2 = bf16[128,256]{1,0:T(8,128)(2,1)S(1)} copy-done((bf16[128,256]{1,0:T(8,128)(2,1)S(1)}, bf16[128,256]{1,0:T(8,128)(2,1)}, u32[]{:S(2)}) %copy-start.2) | copy-done | bytes 65560
  8.9 0.2 prepare.1
  9.1 0.0 collective-permute-done.refs_4_
  9.1 0.0 copy-start.4
  9.1 2.1 %collective-permute-done.5.refs_6_ = bf16[128,256]{1,0:T(8,128)(2,1)S(1)} collective-permute-done((bf16[128,256]{1,0:T(8,128)(2,1)}, bf16[128,256]{1,0:T(8,128)(2,1)S(1)}, u32[]{:S(2)}, u32[]{:S(2)}) %collective-permute-start.5) | collective-permute-done | bytes 65568 | tf_op jit(solution)/shard_map/ppermute | solution.py:94
  11.2 0.0 collective-permute-start.6
  11.2 0.1 collective-permute-done.2.refs_2_
  11.3 0.4 %collective-permute-start.3 = (bf16[128,256]{1,0:T(8,128)(2,1)S(1)}, bf16[128,256]{1,0:T(8,128)(2,1)S(1)}, u32[]{:S(2)}, u32[]{:S(2)}) collective-permute-start(bf16[128,256]{1,0:T(8,128)(2,1)S(1)} %collective-permute-done.2.refs_2_), channel_id=1, source_target_pairs={{0,4},{4,0},{8,12},{12,8},{16,20},{20,16},{24,28},{28,24},{1,5},{5... | collective-permute-start | bytes 196616 | tf_op jit(solution)/shard_map/ppermute | solution.py:94
  11.7 0.1 collective-permute-start.4
  11.8 0.0 collective-permute-done.1.refs_1_
  11.8 0.6 %collective-permute-done.6.refs_7_ = bf16[128,256]{1,0:T(8,128)(2,1)S(1)} collective-permute-done((bf16[128,256]{1,0:T(8,128)(2,1)S(1)}, bf16[128,256]{1,0:T(8,128)(2,1)S(1)}, u32[]{:S(2)}, u32[]{:S(2)}) %collective-permute-start.6) | collective-permute-done | bytes 65568 | tf_op jit(solution)/shard_map/ppermute | solution.py:94
  12.4 0.2 collective-permute-done.3.refs_3_
  12.6 0.4 collective-permute-done.4.refs_5_
  12.9 0.4 %partials.1 = (bf16[128,256]{1,0:T(8,128)(2,1)S(1)}, bf16[128,256]{1,0:T(8,128)(2,1)S(1)}, bf16[128,256]{1,0:T(8,128)(2,1)S(1)}, bf16[128,256]{1,0:T(8,128)(2,1)S(1)}) custom-call(s32[4,4]{1,0:T(4,128)S(1)} %bitcast.6, bf16[4,128,512]{2,1,0:T(8,128)(2,1)S(1)} %get-tuple-element.30.wide_ref, bf16[128,256]{1,0:T(8,128)(2,1)S(1)} %get-tuple-element.31.refs_0_, ...), custom_call_target="tpu_custom_call" | custom-call | tf_op jit(solution)/shard_map/partials/pallas_call | solution.py:82
  13.4 2.5 %collective-permute-start.7 = (bf16[128,256]{1,0:T(8,128)(2,1)S(1)}, bf16[128,256]{1,0:T(8,128)(2,1)S(1)}, u32[]{:S(2)}, u32[]{:S(2)}) collective-permute-start(bf16[128,256]{1,0:T(8,128)(2,1)S(1)} %get-tuple-element.34), channel_id=1, source_target_pairs={{0,3},{1,2},{2,1},{3,0},{4,7},{5,6},{6,5},{7,4},{8,11},{9,10},{10,... | collective-permute-start | bytes 196616 | tf_op jit(solution)/shard_map/ppermute | solution.py:94
  15.9 0.5 %collective-permute-start.8 = (bf16[128,256]{1,0:T(8,128)(2,1)S(1)}, bf16[128,256]{1,0:T(8,128)(2,1)S(1)}, u32[]{:S(2)}, u32[]{:S(2)}) collective-permute-start(bf16[128,256]{1,0:T(8,128)(2,1)S(1)} %get-tuple-element.35), channel_id=1, source_target_pairs={{0,2},{1,3},{2,0},{3,1},{4,6},{5,7},{6,4},{7,5},{8,10},{9,11},{10,... | collective-permute-start | bytes 196616 | tf_op jit(solution)/shard_map/ppermute | solution.py:94
  16.4 0.5 %collective-permute-start.9 = (bf16[128,256]{1,0:T(8,128)(2,1)S(1)}, bf16[128,256]{1,0:T(8,128)(2,1)S(1)}, u32[]{:S(2)}, u32[]{:S(2)}) collective-permute-start(bf16[128,256]{1,0:T(8,128)(2,1)S(1)} %get-tuple-element.36), channel_id=1, source_target_pairs={{0,1},{1,0},{2,3},{3,2},{4,5},{5,4},{6,7},{7,6},{8,9},{9,8},{10,11... | collective-permute-start | bytes 196616 | tf_op jit(solution)/shard_map/ppermute | solution.py:94
  16.9 1.7 %collective-permute-done.7.refs_1_ = bf16[128,256]{1,0:T(8,128)(2,1)S(1)} collective-permute-done((bf16[128,256]{1,0:T(8,128)(2,1)S(1)}, bf16[128,256]{1,0:T(8,128)(2,1)S(1)}, u32[]{:S(2)}, u32[]{:S(2)}) %collective-permute-start.7) | collective-permute-done | bytes 65568 | tf_op jit(solution)/shard_map/ppermute | solution.py:94
  18.6 1.5 %collective-permute-done.8.refs_2_ = bf16[128,256]{1,0:T(8,128)(2,1)S(1)} collective-permute-done((bf16[128,256]{1,0:T(8,128)(2,1)S(1)}, bf16[128,256]{1,0:T(8,128)(2,1)S(1)}, u32[]{:S(2)}, u32[]{:S(2)}) %collective-permute-start.8) | collective-permute-done | bytes 65568 | tf_op jit(solution)/shard_map/ppermute | solution.py:94
  20.2 0.5 %collective-permute-done.9.refs_3_ = bf16[128,256]{1,0:T(8,128)(2,1)S(1)} collective-permute-done((bf16[128,256]{1,0:T(8,128)(2,1)S(1)}, bf16[128,256]{1,0:T(8,128)(2,1)S(1)}, u32[]{:S(2)}, u32[]{:S(2)}) %collective-permute-start.9) | collective-permute-done | bytes 65568 | tf_op jit(solution)/shard_map/ppermute | solution.py:94
  20.7 0.4 %dense.1 = (bf16[128,256]{1,0:T(8,128)(2,1)S(1)}, f32[128,256]{1,0:T(8,128)S(1)}, bf16[256,256]{1,0:T(8,128)(2,1)S(1)}) custom-call(bf16[256,256]{1,0:T(8,128)(2,1)S(1)} %copy-done.1, bf16[128,256]{1,0:T(8,128)(2,1)S(1)} %copy-done.3, bf16[256,128]{1,0:T(8,128)(2,1)S(1)} %get-tuple-element.29.placing_ref, bf16[128,256]{1,0:T(8,128)(2,1)S(1)} %get-tuple-element.33.refs_0_, ...), custom_call_target="tpu_custom_call" | custom-call | tf_op jit(solution)/shard_map/dense/pallas_call | solution.py:126
  21.1 0.1 collective-permute-start.10
  21.2 1.3 %collective-permute-done.10.came_ref.refs_1_ = bf16[256,256]{1,0:T(8,128)(2,1)S(1)} collective-permute-done((bf16[256,256]{1,0:T(8,128)(2,1)S(1)}, bf16[256,256]{1,0:T(8,128)(2,1)S(1)}, u32[]{:S(2)}, u32[]{:S(2)}) %collective-permute-start.10) | collective-permute-done | bytes 131104 | tf_op jit(solution)/shard_map/ppermute | solution.py:94
  22.6 1.1 %collective-permute-start.11 = (bf16[192,256]{1,0:T(8,128)(2,1)S(1)}, bf16[192,256]{1,0:T(8,128)(2,1)S(1)}, u32[]{:S(2)}, u32[]{:S(2)}) collective-permute-start(bf16[192,256]{1,0:T(8,128)(2,1)S(1)} %get-tuple-element.41), channel_id=1, source_target_pairs={{0,8},{1,9},{2,10},{3,11},{4,7},{5,6},{6,5},{7,4},{8,16},{9,17},{1... | collective-permute-start | bytes 294920 | tf_op jit(solution)/shard_map/ppermute | solution.py:266
  23.6 2.3 %collective-permute-start.12 = (bf16[192,256]{1,0:T(8,128)(2,1)S(1)}, bf16[192,256]{1,0:T(8,128)(2,1)S(1)}, u32[]{:S(2)}, u32[]{:S(2)}) collective-permute-start(bf16[192,256]{1,0:T(8,128)(2,1)S(1)} %get-tuple-element.42), channel_id=1, source_target_pairs={{0,16},{1,17},{2,18},{3,19},{4,6},{5,7},{6,4},{7,5},{8,24},{9,25},... | collective-permute-start | bytes 294920 | tf_op jit(solution)/shard_map/ppermute | solution.py:266
  25.9 2.4 %collective-permute-start.13 = (bf16[192,256]{1,0:T(8,128)(2,1)S(1)}, bf16[192,256]{1,0:T(8,128)(2,1)S(1)}, u32[]{:S(2)}, u32[]{:S(2)}) collective-permute-start(bf16[192,256]{1,0:T(8,128)(2,1)S(1)} %get-tuple-element.43), channel_id=1, source_target_pairs={{0,24},{1,25},{2,26},{3,27},{4,5},{5,4},{6,7},{7,6},{8,0},{9,1},{1... | collective-permute-start | bytes 294920 | tf_op jit(solution)/shard_map/ppermute | solution.py:266
  28.3 0.8 %collective-permute-done.11.refs_0_ = bf16[192,256]{1,0:T(8,128)(2,1)S(1)} collective-permute-done((bf16[192,256]{1,0:T(8,128)(2,1)S(1)}, bf16[192,256]{1,0:T(8,128)(2,1)S(1)}, u32[]{:S(2)}, u32[]{:S(2)}) %collective-permute-start.11) | collective-permute-done | bytes 98336 | tf_op jit(solution)/shard_map/ppermute | solution.py:266
  29.1 2.0 %collective-permute-done.12.refs_1_ = bf16[192,256]{1,0:T(8,128)(2,1)S(1)} collective-permute-done((bf16[192,256]{1,0:T(8,128)(2,1)S(1)}, bf16[192,256]{1,0:T(8,128)(2,1)S(1)}, u32[]{:S(2)}, u32[]{:S(2)}) %collective-permute-start.12) | collective-permute-done | bytes 98336 | tf_op jit(solution)/shard_map/ppermute | solution.py:266
  31.1 0.2 collective-permute-done.13.refs_2_
  31.4 0.1 second.1
  31.5 1.3 %collective-permute-start.14 = (bf16[192,256]{1,0:T(8,128)(2,1)S(1)}, bf16[192,256]{1,0:T(8,128)(2,1)S(1)}, u32[]{:S(2)}, u32[]{:S(2)}) collective-permute-start(bf16[192,256]{1,0:T(8,128)(2,1)S(1)} %get-tuple-element.45), channel_id=1, source_target_pairs={{0,3},{1,2},{2,1},{3,0},{4,12},{5,13},{6,14},{7,15},{8,11},{9,10},... | collective-permute-start | bytes 294920 | tf_op jit(solution)/shard_map/ppermute | solution.py:266
  32.8 0.9 %collective-permute-start.15 = (bf16[192,256]{1,0:T(8,128)(2,1)S(1)}, bf16[192,256]{1,0:T(8,128)(2,1)S(1)}, u32[]{:S(2)}, u32[]{:S(2)}) collective-permute-start(bf16[192,256]{1,0:T(8,128)(2,1)S(1)} %get-tuple-element.46), channel_id=1, source_target_pairs={{0,2},{1,3},{2,0},{3,1},{4,20},{5,21},{6,22},{7,23},{8,10},{9,11},... | collective-permute-start | bytes 294920 | tf_op jit(solution)/shard_map/ppermute | solution.py:266
  33.7 1.3 %collective-permute-start.16 = (bf16[192,256]{1,0:T(8,128)(2,1)S(1)}, bf16[192,256]{1,0:T(8,128)(2,1)S(1)}, u32[]{:S(2)}, u32[]{:S(2)}) collective-permute-start(bf16[192,256]{1,0:T(8,128)(2,1)S(1)} %get-tuple-element.47), channel_id=1, source_target_pairs={{0,1},{1,0},{2,3},{3,2},{4,28},{5,29},{6,30},{7,31},{8,9},{9,8},{1... | collective-permute-start | bytes 294920 | tf_op jit(solution)/shard_map/ppermute | solution.py:266
  35.0 0.7 %store.2._ = bf16[8,32,256]{2,1,0:T(8,128)(2,1)} custom-call(bf16[128,256]{1,0:T(8,128)(2,1)S(1)} %get-tuple-element.37.same_ref.refs_0_, bf16[256,256]{1,0:T(8,128)(2,1)S(1)} %collective-permute-done.10.came_ref.refs_1_, bf16[192,256]{1,0:T(8,128)(2,1)S(1)} %collective-permute-done.11.refs_0_, bf16[192,256]{1,0:T(8,128)(2,1)S(1)} %collective-permute-done.12.refs_1_, ...), custom_call_target="tpu_custom_call" | custom-call | tf_op jit(solution)/shard_map/store/pallas_call | solution.py:223
  35.7 1.4 %collective-permute-done.14.refs_0_.refs_2_ = bf16[192,256]{1,0:T(8,128)(2,1)S(1)} collective-permute-done((bf16[192,256]{1,0:T(8,128)(2,1)S(1)}, bf16[192,256]{1,0:T(8,128)(2,1)S(1)}, u32[]{:S(2)}, u32[]{:S(2)}) %collective-permute-start.14) | collective-permute-done | bytes 98336 | tf_op jit(solution)/shard_map/ppermute | solution.py:266
  37.1 1.0 %collective-permute-done.15.refs_1_.refs_3_ = bf16[192,256]{1,0:T(8,128)(2,1)S(1)} collective-permute-done((bf16[192,256]{1,0:T(8,128)(2,1)S(1)}, bf16[192,256]{1,0:T(8,128)(2,1)S(1)}, u32[]{:S(2)}, u32[]{:S(2)}) %collective-permute-start.15) | collective-permute-done | bytes 98336 | tf_op jit(solution)/shard_map/ppermute | solution.py:266
  38.1 0.2 collective-permute-done.16.refs_2_.refs_4_
  38.3 0.1 third.1.half_ref
  38.4 0.1 collective-permute-start.17
  38.4 0.7 %store_half.2.refs_0_ = f32[2,128,256]{2,1,0:T(8,128)} custom-call(bf16[128,256]{1,0:T(8,128)(2,1)S(1)} %third.1.half_ref), custom_call_target="tpu_custom_call" | custom-call | tf_op jit(solution)/shard_map/store_half/pallas_call | solution.py:246
  39.1 0.6 %collective-permute-done.17.half_ref = bf16[128,256]{1,0:T(8,128)(2,1)S(1)} collective-permute-done((bf16[128,256]{1,0:T(8,128)(2,1)S(1)}, bf16[128,256]{1,0:T(8,128)(2,1)S(1)}, u32[]{:S(2)}, u32[]{:S(2)}) %collective-permute-start.17) | collective-permute-done | bytes 65568 | tf_op jit(solution)/shard_map/ppermute | solution.py:94
  39.7 0.7 %store_half.3 = f32[2,128,256]{2,1,0:T(8,128)} custom-call(bf16[128,256]{1,0:T(8,128)(2,1)S(1)} %collective-permute-done.17.half_ref, f32[2,128,256]{2,1,0:T(8,128)} %store_half.2.refs_0_), custom_call_target="tpu_custom_call", output_to_operand_aliasing={{}: (1, {})} | custom-call | tf_op jit(solution)/shard_map/store_half/pallas_call | solution.py:246
  (10 shorter events, 0.1 us)
Async XLA Ops:
  0.6 8.5 %collective-permute-start = (bf16[128,256]{1,0:T(8,128)(2,1)}, bf16[128,256]{1,0:T(8,128)(2,1)S(1)}, u32[]{:S(2)}, u32[]{:S(2)}) collective-permute-start(bf16[128,256]{1,0:T(8,128)(2,1)} %own_ref.1), channel_id=1, source_target_pairs={{0,16},{4,20},{8,24},{12,28},{16,0},{20,4},{24,8},{28,12},{1,17},{... | collective-permute-start | bytes 196616 | tf_op jit(solution)/shard_map/ppermute | solution.py:94
  4.7 6.4 %collective-permute-start.5 = (bf16[128,256]{1,0:T(8,128)(2,1)}, bf16[128,256]{1,0:T(8,128)(2,1)S(1)}, u32[]{:S(2)}, u32[]{:S(2)}) collective-permute-start(bf16[128,256]{1,0:T(8,128)(2,1)} %own_ref.1), channel_id=1, source_target_pairs={{0,24},{4,28},{8,16},{12,20},{16,8},{20,12},{24,0},{28,4},{1,25},{... | collective-permute-start | bytes 196616 | tf_op jit(solution)/shard_map/ppermute | solution.py:94
  6.1 5.2 %collective-permute-start.2 = (bf16[128,256]{1,0:T(8,128)(2,1)}, bf16[128,256]{1,0:T(8,128)(2,1)S(1)}, u32[]{:S(2)}, u32[]{:S(2)}) collective-permute-start(bf16[128,256]{1,0:T(8,128)(2,1)} %own_ref.1), channel_id=1, source_target_pairs={{0,8},{4,12},{8,0},{12,4},{16,24},{20,28},{24,16},{28,20},{1,9},{5... | collective-permute-start | bytes 196616 | tf_op jit(solution)/shard_map/ppermute | solution.py:94
  6.3 5.5 %collective-permute-start.1 = (bf16[128,256]{1,0:T(8,128)(2,1)}, bf16[128,256]{1,0:T(8,128)(2,1)S(1)}, u32[]{:S(2)}, u32[]{:S(2)}) collective-permute-start(bf16[128,256]{1,0:T(8,128)(2,1)} %own_ref.1), channel_id=1, source_target_pairs={{0,4},{4,0},{8,12},{12,8},{16,20},{20,16},{24,28},{28,24},{1,5},{5... | collective-permute-start | bytes 196616 | tf_op jit(solution)/shard_map/ppermute | solution.py:94
  6.3 0.7 %copy-start.5 = (s32[128,1]{0,1:T(1,128)S(1)}, s32[128,1]{0,1:T(1,128)}, u32[]{:S(2)}) copy-start(s32[128,1]{0,1:T(1,128)} %param.11) | copy-start | bytes 1540
  7.0 1.0 %copy-start = (bf16[4,1,4,128,128]{4,3,2,1,0:T(8,128)(2,1)S(1)}, bf16[4,1,4,128,128]{4,3,2,1,0:T(8,128)(2,1)}, u32[]{:S(2)}) copy-start(bf16[4,1,4,128,128]{4,3,2,1,0:T(8,128)(2,1)} %param.7) | copy-start | bytes 1572868
  8.0 0.8 %copy-start.2 = (bf16[128,256]{1,0:T(8,128)(2,1)S(1)}, bf16[128,256]{1,0:T(8,128)(2,1)}, u32[]{:S(2)}) copy-start(bf16[128,256]{1,0:T(8,128)(2,1)} %own_ref.1) | copy-start | bytes 196612
  9.1 3.8 %copy-start.4 = (s32[4,1,4]{2,1,0:T(1,128)S(1)}, s32[4,1,4]{2,1,0:T(1,128)}, u32[]{:S(2)}) copy-start(s32[4,1,4]{2,1,0:T(1,128)} %param.8) | copy-start | bytes 196
  11.2 1.3 %collective-permute-start.6 = (bf16[128,256]{1,0:T(8,128)(2,1)S(1)}, bf16[128,256]{1,0:T(8,128)(2,1)S(1)}, u32[]{:S(2)}, u32[]{:S(2)}) collective-permute-start(bf16[128,256]{1,0:T(8,128)(2,1)S(1)} %collective-permute-done.5.refs_6_), channel_id=1, source_target_pairs={{0,4},{4,0},{8,12},{12,8},{16,20},{20,16},{24,28},{28,24},{1,5},{5... | collective-permute-start | bytes 196616 | tf_op jit(solution)/shard_map/ppermute | solution.py:94
  11.3 1.3 %collective-permute-start.3 = (bf16[128,256]{1,0:T(8,128)(2,1)S(1)}, bf16[128,256]{1,0:T(8,128)(2,1)S(1)}, u32[]{:S(2)}, u32[]{:S(2)}) collective-permute-start(bf16[128,256]{1,0:T(8,128)(2,1)S(1)} %collective-permute-done.2.refs_2_), channel_id=1, source_target_pairs={{0,4},{4,0},{8,12},{12,8},{16,20},{20,16},{24,28},{28,24},{1,5},{5... | collective-permute-start | bytes 196616 | tf_op jit(solution)/shard_map/ppermute | solution.py:94
  11.7 1.3 %collective-permute-start.4 = (bf16[128,256]{1,0:T(8,128)(2,1)S(1)}, bf16[128,256]{1,0:T(8,128)(2,1)S(1)}, u32[]{:S(2)}, u32[]{:S(2)}) collective-permute-start(bf16[128,256]{1,0:T(8,128)(2,1)S(1)} %collective-permute-done.refs_4_), channel_id=1, source_target_pairs={{0,4},{4,0},{8,12},{12,8},{16,20},{20,16},{24,28},{28,24},{1,5},{5... | collective-permute-start | bytes 196616 | tf_op jit(solution)/shard_map/ppermute | solution.py:94
  12.9 7.7 %copy-start.1 = (bf16[256,256]{1,0:T(8,128)(2,1)S(1)}, bf16[256,256]{1,0:T(8,128)(2,1)}, u32[]{:S(2)}) copy-start(bf16[256,256]{1,0:T(8,128)(2,1)} %weight_ref.1) | copy-start | bytes 393220
  12.9 7.7 %copy-start.3 = (bf16[128,256]{1,0:T(8,128)(2,1)S(1)}, bf16[128,256]{1,0:T(8,128)(2,1)}, u32[]{:S(2)}) copy-start(bf16[128,256]{1,0:T(8,128)(2,1)} %cot_ref.1) | copy-start | bytes 196612
  13.4 5.3 %collective-permute-start.7 = (bf16[128,256]{1,0:T(8,128)(2,1)S(1)}, bf16[128,256]{1,0:T(8,128)(2,1)S(1)}, u32[]{:S(2)}, u32[]{:S(2)}) collective-permute-start(bf16[128,256]{1,0:T(8,128)(2,1)S(1)} %get-tuple-element.34), channel_id=1, source_target_pairs={{0,3},{1,2},{2,1},{3,0},{4,7},{5,6},{6,5},{7,4},{8,11},{9,10},{10,... | collective-permute-start | bytes 196616 | tf_op jit(solution)/shard_map/ppermute | solution.py:94
  15.9 4.3 %collective-permute-start.8 = (bf16[128,256]{1,0:T(8,128)(2,1)S(1)}, bf16[128,256]{1,0:T(8,128)(2,1)S(1)}, u32[]{:S(2)}, u32[]{:S(2)}) collective-permute-start(bf16[128,256]{1,0:T(8,128)(2,1)S(1)} %get-tuple-element.35), channel_id=1, source_target_pairs={{0,2},{1,3},{2,0},{3,1},{4,6},{5,7},{6,4},{7,5},{8,10},{9,11},{10,... | collective-permute-start | bytes 196616 | tf_op jit(solution)/shard_map/ppermute | solution.py:94
  16.4 4.3 %collective-permute-start.9 = (bf16[128,256]{1,0:T(8,128)(2,1)S(1)}, bf16[128,256]{1,0:T(8,128)(2,1)S(1)}, u32[]{:S(2)}, u32[]{:S(2)}) collective-permute-start(bf16[128,256]{1,0:T(8,128)(2,1)S(1)} %get-tuple-element.36), channel_id=1, source_target_pairs={{0,1},{1,0},{2,3},{3,2},{4,5},{5,4},{6,7},{7,6},{8,9},{9,8},{10,11... | collective-permute-start | bytes 196616 | tf_op jit(solution)/shard_map/ppermute | solution.py:94
  21.1 1.4 %collective-permute-start.10 = (bf16[256,256]{1,0:T(8,128)(2,1)S(1)}, bf16[256,256]{1,0:T(8,128)(2,1)S(1)}, u32[]{:S(2)}, u32[]{:S(2)}) collective-permute-start(bf16[256,256]{1,0:T(8,128)(2,1)S(1)} %get-tuple-element.38), channel_id=1, source_target_pairs={{0,4},{4,0},{8,12},{12,8},{16,20},{20,16},{24,28},{28,24},{1,5},{5... | collective-permute-start | bytes 393224 | tf_op jit(solution)/shard_map/ppermute | solution.py:94
  22.6 6.6 %collective-permute-start.11 = (bf16[192,256]{1,0:T(8,128)(2,1)S(1)}, bf16[192,256]{1,0:T(8,128)(2,1)S(1)}, u32[]{:S(2)}, u32[]{:S(2)}) collective-permute-start(bf16[192,256]{1,0:T(8,128)(2,1)S(1)} %get-tuple-element.41), channel_id=1, source_target_pairs={{0,8},{1,9},{2,10},{3,11},{4,7},{5,6},{6,5},{7,4},{8,16},{9,17},{1... | collective-permute-start | bytes 294920 | tf_op jit(solution)/shard_map/ppermute | solution.py:266
  23.6 7.5 %collective-permute-start.12 = (bf16[192,256]{1,0:T(8,128)(2,1)S(1)}, bf16[192,256]{1,0:T(8,128)(2,1)S(1)}, u32[]{:S(2)}, u32[]{:S(2)}) collective-permute-start(bf16[192,256]{1,0:T(8,128)(2,1)S(1)} %get-tuple-element.42), channel_id=1, source_target_pairs={{0,16},{1,17},{2,18},{3,19},{4,6},{5,7},{6,4},{7,5},{8,24},{9,25},... | collective-permute-start | bytes 294920 | tf_op jit(solution)/shard_map/ppermute | solution.py:266
  25.9 5.5 %collective-permute-start.13 = (bf16[192,256]{1,0:T(8,128)(2,1)S(1)}, bf16[192,256]{1,0:T(8,128)(2,1)S(1)}, u32[]{:S(2)}, u32[]{:S(2)}) collective-permute-start(bf16[192,256]{1,0:T(8,128)(2,1)S(1)} %get-tuple-element.43), channel_id=1, source_target_pairs={{0,24},{1,25},{2,26},{3,27},{4,5},{5,4},{6,7},{7,6},{8,0},{9,1},{1... | collective-permute-start | bytes 294920 | tf_op jit(solution)/shard_map/ppermute | solution.py:266
  31.5 5.6 %collective-permute-start.14 = (bf16[192,256]{1,0:T(8,128)(2,1)S(1)}, bf16[192,256]{1,0:T(8,128)(2,1)S(1)}, u32[]{:S(2)}, u32[]{:S(2)}) collective-permute-start(bf16[192,256]{1,0:T(8,128)(2,1)S(1)} %get-tuple-element.45), channel_id=1, source_target_pairs={{0,3},{1,2},{2,1},{3,0},{4,12},{5,13},{6,14},{7,15},{8,11},{9,10},... | collective-permute-start | bytes 294920 | tf_op jit(solution)/shard_map/ppermute | solution.py:266
  32.8 5.3 %collective-permute-start.15 = (bf16[192,256]{1,0:T(8,128)(2,1)S(1)}, bf16[192,256]{1,0:T(8,128)(2,1)S(1)}, u32[]{:S(2)}, u32[]{:S(2)}) collective-permute-start(bf16[192,256]{1,0:T(8,128)(2,1)S(1)} %get-tuple-element.46), channel_id=1, source_target_pairs={{0,2},{1,3},{2,0},{3,1},{4,20},{5,21},{6,22},{7,23},{8,10},{9,11},... | collective-permute-start | bytes 294920 | tf_op jit(solution)/shard_map/ppermute | solution.py:266
  33.7 4.6 %collective-permute-start.16 = (bf16[192,256]{1,0:T(8,128)(2,1)S(1)}, bf16[192,256]{1,0:T(8,128)(2,1)S(1)}, u32[]{:S(2)}, u32[]{:S(2)}) collective-permute-start(bf16[192,256]{1,0:T(8,128)(2,1)S(1)} %get-tuple-element.47), channel_id=1, source_target_pairs={{0,1},{1,0},{2,3},{3,2},{4,28},{5,29},{6,30},{7,31},{8,9},{9,8},{1... | collective-permute-start | bytes 294920 | tf_op jit(solution)/shard_map/ppermute | solution.py:266
  38.4 1.3 %collective-permute-start.17 = (bf16[128,256]{1,0:T(8,128)(2,1)S(1)}, bf16[128,256]{1,0:T(8,128)(2,1)S(1)}, u32[]{:S(2)}, u32[]{:S(2)}) collective-permute-start(bf16[128,256]{1,0:T(8,128)(2,1)S(1)} %third.1.half_ref), channel_id=1, source_target_pairs={{0,4},{4,0},{8,12},{12,8},{16,20},{20,16},{24,28},{28,24},{1,5},{5... | collective-permute-start | bytes 196616 | tf_op jit(solution)/shard_map/ppermute | solution.py:94

commit v17 on v13

--- a/solution.py
+++ b/solution.py
@@ -14,6 +14,11 @@
 
 def across(n):
     return list(range(n - 1, 0, -1))
+
+
+def orders(n):
+    near = list(range(1, n - 1))
+    return list(zip([n - 1] + near, near + [n - 1]))
 
 
 def place_of_chip():
@@ -68,8 +73,8 @@
     section, rep = lax.axis_index("section"), lax.axis_index("rep")
     for j in range(count):
         held[j] = block_refs[j][...]
-    for j, out_ref in zip([0] + across(len(out_refs)), out_refs):
-        g = rep ^ j
+    for (j, k), out_ref in zip([(0, 0)] + orders(len(out_refs)), out_refs):
+        g = rep ^ jnp.where(section & 1 == 0, j, k)
         right = jnp.concatenate([held[src_ref[g, k] ^ section] for k in range(depth)], axis=0)
         out_ref[...] = jnp.dot(wide_ref[g], right, preferred_element_type=jnp.float32).astype(
             jnp.bfloat16
@@ -247,6 +252,15 @@
         compiler_params=LIMIT,
         name="finish",
     )(own, came)
+
+
+def swap_rep(value, first, second):
+    n_section, n_rep = lax.axis_size("section"), lax.axis_size("rep")
+    pairs = []
+    for s in range(n_section):
+        j = second if s & 1 else first
+        pairs += [(s * n_rep + r, s * n_rep + (r ^ j)) for r in range(n_rep)]
+    return lax.ppermute(value, ("section", "rep"), pairs)
 
 
 def exchange(value, core_along, shift, j):
@@ -285,8 +299,7 @@
     wide, own, placing = prepare(adj_tiles[:, 0], features, target, n_section * slots, slots)
     blocks, (wide, own, placing) = gather_blocks(features, "section", (wide, own, placing))
     parts = list(partials(adj_src[:, 0], wide, [own] + blocks[1:]))
-    others = across(n_rep)
-    parts = parts[:1] + [swap(part, "rep", j) for part, j in zip(parts[1:], others)]
+    parts = parts[:1] + [swap_rep(part, *step) for part, step in zip(parts[1:], orders(n_rep))]
     same, kept, sent = dense(parts, weight, cotangent, placing)
     came = swap(sent, "section", 1)
     chips = n_section // 2

time: 40.6 us -> 41.6 us (1.025)
  waiting for transfers between devices: 15.4 us -> 16.3 us
    ppermute x0 -> x3, waiting for transfers between devices: none -> 4.24 us  [swap_rep(): return lax.ppermute(value, ('section', 'rep'), pairs)]
    ppermute x12 -> x9, waiting for transfers between devices: 9.72 us -> 6 us  [swap(): lax.ppermute(value, axis, [(i, i ^ j) for i in range(lax.axis_size(axis))])]
    ppermute x0 -> x3, starting transfers between devices: none -> 3.55 us  [swap_rep(): return lax.ppermute(value, ('section', 'rep'), pairs)]
    ppermute x12 -> x9, starting transfers between devices: 9.89 us -> 6.34 us  [swap(): lax.ppermute(value, axis, [(i, i ^ j) for i in range(lax.axis_size(axis))])]
    ppermute x6, waiting for transfers between devices: 5.67 us -> 6.1 us  [exchange(): return lax.ppermute(value, ('section', 'rep'), pairs)]
where the time goes in v17:
time: 41.6 us; the launch traced here: 41.4 us
  starting transfers between devices  19.1 us (46%)
  waiting for transfers between devices  16.3 us (39%)
  Pallas kernels  2.67 us (6%)
  local copies, waits for them, and re-layouts  2.55 us (6%)
  between operations  0.73 us (2%)
    ppermute x6, starting transfers between devices, exchange(): return lax.ppermute(value, ('section', 'rep'), pairs)  9.2 us
    ppermute x9, starting transfers between devices, swap(): lax.ppermute(value, axis, [(i, i ^ j) for i in range(lax.axis_size(axis))])  6.34 us
    ppermute x6, waiting for transfers between devices, exchange(): return lax.ppermute(value, ('section', 'rep'), pairs)  6.1 us
    ppermute x9, waiting for transfers between devices, swap(): lax.ppermute(value, axis, [(i, i ^ j) for i in range(lax.axis_size(axis))])  6 us
    ppermute x3, waiting for transfers between devices, swap_rep(): return lax.ppermute(value, ('section', 'rep'), pairs)  4.24 us
    ppermute x3, starting transfers between devices, swap_rep(): return lax.ppermute(value, ('section', 'rep'), pairs)  3.55 us
    unnamed x12, local copies, waits for them, and re-layouts  2.55 us
  transfers between devices with their start and end apart: 18, of which 16 were waited for; matrix products, arithmetic and copies ran while one was open for 0% of the time, Pallas kernels for 2%

profile of v17, /device:TPU:0, one launch (start us, length us, event | category | flops | bytes accessed | tf_op | source)
XLA Modules:
  0.0 41.4 jit_solution(10415644312804662484)
XLA Ops:
  0.6 4.1 %collective-permute-start.2 = (bf16[128,256]{1,0:T(8,128)(2,1)}, bf16[128,256]{1,0:T(8,128)(2,1)S(1)}, u32[]{:S(2)}, u32[]{:S(2)}) collective-permute-start(bf16[128,256]{1,0:T(8,128)(2,1)} %own_ref.1), channel_id=1, source_target_pairs={{0,16},{4,20},{8,24},{12,28},{16,0},{20,4},{24,8},{28,12},{1,17},{... | collective-permute-start | bytes 196616 | tf_op jit(solution)/shard_map/ppermute | solution.py:99
  4.7 1.3 %collective-permute-start.1 = (bf16[128,256]{1,0:T(8,128)(2,1)}, bf16[128,256]{1,0:T(8,128)(2,1)S(1)}, u32[]{:S(2)}, u32[]{:S(2)}) collective-permute-start(bf16[128,256]{1,0:T(8,128)(2,1)} %own_ref.1), channel_id=1, source_target_pairs={{0,24},{4,28},{8,16},{12,20},{16,8},{20,12},{24,0},{28,4},{1,25},{... | collective-permute-start | bytes 196616 | tf_op jit(solution)/shard_map/ppermute | solution.py:99
  6.1 0.2 collective-permute-start
  6.3 0.0 collective-permute-start.3
  6.3 0.7 %copy-done.5 = s32[128,1]{0,1:T(1,128)S(1)} copy-done((s32[128,1]{0,1:T(1,128)S(1)}, s32[128,1]{0,1:T(1,128)}, u32[]{:S(2)}) %copy-start.5) | copy-done | bytes 536
  7.0 1.0 %copy-done = bf16[4,1,4,128,128]{4,3,2,1,0:T(8,128)(2,1)S(1)} copy-done((bf16[4,1,4,128,128]{4,3,2,1,0:T(8,128)(2,1)S(1)}, bf16[4,1,4,128,128]{4,3,2,1,0:T(8,128)(2,1)}, u32[]{:S(2)}) %copy-start) | copy-done | bytes 524312
  8.0 0.8 %copy-done.2 = bf16[128,256]{1,0:T(8,128)(2,1)S(1)} copy-done((bf16[128,256]{1,0:T(8,128)(2,1)S(1)}, bf16[128,256]{1,0:T(8,128)(2,1)}, u32[]{:S(2)}) %copy-start.2) | copy-done | bytes 65560
  8.9 0.2 prepare.1
  9.1 0.0 collective-permute-done.2.refs_4_
  9.1 2.1 %collective-permute-done.1.refs_6_ = bf16[128,256]{1,0:T(8,128)(2,1)S(1)} collective-permute-done((bf16[128,256]{1,0:T(8,128)(2,1)}, bf16[128,256]{1,0:T(8,128)(2,1)S(1)}, u32[]{:S(2)}, u32[]{:S(2)}) %collective-permute-start.1) | collective-permute-done | bytes 65568 | tf_op jit(solution)/shard_map/ppermute | solution.py:99
  11.2 0.1 collective-permute-done.refs_2_
  11.3 0.0 collective-permute-start.4
  11.3 0.5 %collective-permute-start.5 = (bf16[128,256]{1,0:T(8,128)(2,1)S(1)}, bf16[128,256]{1,0:T(8,128)(2,1)S(1)}, u32[]{:S(2)}, u32[]{:S(2)}) collective-permute-start(bf16[128,256]{1,0:T(8,128)(2,1)S(1)} %collective-permute-done.2.refs_4_), channel_id=1, source_target_pairs={{0,4},{4,0},{8,12},{12,8},{16,20},{20,16},{24,28},{28,24},{1,5},{5... | collective-permute-start | bytes 196616 | tf_op jit(solution)/shard_map/ppermute | solution.py:99
  11.8 0.0 collective-permute-start.6
  11.8 0.0 collective-permute-done.3.refs_1_
  11.8 0.7 %collective-permute-done.4.refs_3_ = bf16[128,256]{1,0:T(8,128)(2,1)S(1)} collective-permute-done((bf16[128,256]{1,0:T(8,128)(2,1)S(1)}, bf16[128,256]{1,0:T(8,128)(2,1)S(1)}, u32[]{:S(2)}, u32[]{:S(2)}) %collective-permute-start.4) | collective-permute-done | bytes 65568 | tf_op jit(solution)/shard_map/ppermute | solution.py:99
  12.5 0.2 collective-permute-done.5.refs_5_
  12.7 0.4 collective-permute-done.6.refs_7_
  13.0 0.0 copy-done.4
  13.0 0.4 %partials.1 = (bf16[128,256]{1,0:T(8,128)(2,1)S(1)}, bf16[128,256]{1,0:T(8,128)(2,1)S(1)}, bf16[128,256]{1,0:T(8,128)(2,1)S(1)}, bf16[128,256]{1,0:T(8,128)(2,1)S(1)}) custom-call(s32[4,4]{1,0:T(4,128)S(1)} %bitcast.6, bf16[4,128,512]{2,1,0:T(8,128)(2,1)S(1)} %get-tuple-element.32.wide_ref, bf16[128,256]{1,0:T(8,128)(2,1)S(1)} %get-tuple-element.33.refs_0_, ...), custom_call_target="tpu_custom_call" | custom-call | tf_op jit(solution)/shard_map/partials/pallas_call | solution.py:87
  13.5 2.5 %collective-permute-start.7 = (bf16[128,256]{1,0:T(8,128)(2,1)S(1)}, bf16[128,256]{1,0:T(8,128)(2,1)S(1)}, u32[]{:S(2)}, u32[]{:S(2)}) collective-permute-start(bf16[128,256]{1,0:T(8,128)(2,1)S(1)} %get-tuple-element.38), channel_id=1, source_target_pairs={{0,3},{1,2},{2,1},{3,0},{4,5},{5,4},{6,7},{7,6},{8,11},{9,10},{10,... | collective-permute-start | bytes 196616 | tf_op jit(solution)/shard_map/ppermute | solution.py:263
  16.0 0.5 %collective-permute-start.8 = (bf16[128,256]{1,0:T(8,128)(2,1)S(1)}, bf16[128,256]{1,0:T(8,128)(2,1)S(1)}, u32[]{:S(2)}, u32[]{:S(2)}) collective-permute-start(bf16[128,256]{1,0:T(8,128)(2,1)S(1)} %get-tuple-element.39), channel_id=1, source_target_pairs={{0,1},{1,0},{2,3},{3,2},{4,6},{5,7},{6,4},{7,5},{8,9},{9,8},{10,11... | collective-permute-start | bytes 196616 | tf_op jit(solution)/shard_map/ppermute | solution.py:263
  16.5 0.5 %collective-permute-start.9 = (bf16[128,256]{1,0:T(8,128)(2,1)S(1)}, bf16[128,256]{1,0:T(8,128)(2,1)S(1)}, u32[]{:S(2)}, u32[]{:S(2)}) collective-permute-start(bf16[128,256]{1,0:T(8,128)(2,1)S(1)} %get-tuple-element.40), channel_id=1, source_target_pairs={{0,2},{1,3},{2,0},{3,1},{4,7},{5,6},{6,5},{7,4},{8,10},{9,11},{10,... | collective-permute-start | bytes 196616 | tf_op jit(solution)/shard_map/ppermute | solution.py:263
  17.0 1.8 %collective-permute-done.7.refs_1_ = bf16[128,256]{1,0:T(8,128)(2,1)S(1)} collective-permute-done((bf16[128,256]{1,0:T(8,128)(2,1)S(1)}, bf16[128,256]{1,0:T(8,128)(2,1)S(1)}, u32[]{:S(2)}, u32[]{:S(2)}) %collective-permute-start.7) | collective-permute-done | bytes 65568 | tf_op jit(solution)/shard_map/ppermute | solution.py:263
  18.8 1.4 %collective-permute-done.8.refs_2_ = bf16[128,256]{1,0:T(8,128)(2,1)S(1)} collective-permute-done((bf16[128,256]{1,0:T(8,128)(2,1)S(1)}, bf16[128,256]{1,0:T(8,128)(2,1)S(1)}, u32[]{:S(2)}, u32[]{:S(2)}) %collective-permute-start.8) | collective-permute-done | bytes 65568 | tf_op jit(solution)/shard_map/ppermute | solution.py:263
  20.2 1.0 %collective-permute-done.9.refs_3_ = bf16[128,256]{1,0:T(8,128)(2,1)S(1)} collective-permute-done((bf16[128,256]{1,0:T(8,128)(2,1)S(1)}, bf16[128,256]{1,0:T(8,128)(2,1)S(1)}, u32[]{:S(2)}, u32[]{:S(2)}) %collective-permute-start.9) | collective-permute-done | bytes 65568 | tf_op jit(solution)/shard_map/ppermute | solution.py:263
  21.3 0.0 copy-done.3
  21.3 0.4 %dense.1 = (bf16[128,256]{1,0:T(8,128)(2,1)S(1)}, f32[128,256]{1,0:T(8,128)S(1)}, bf16[256,256]{1,0:T(8,128)(2,1)S(1)}) custom-call(bf16[256,256]{1,0:T(8,128)(2,1)S(1)} %copy-done.1, bf16[128,256]{1,0:T(8,128)(2,1)S(1)} %copy-done.3, bf16[256,128]{1,0:T(8,128)(2,1)S(1)} %get-tuple-element.31.placing_ref, bf16[128,256]{1,0:T(8,128)(2,1)S(1)} %get-tuple-element.37.refs_0_, ...), custom_call_target="tpu_custom_call" | custom-call | tf_op jit(solution)/shard_map/dense/pallas_call | solution.py:131
  21.7 0.1 collective-permute-start.10
  21.8 1.3 %collective-permute-done.10.came_ref.refs_1_ = bf16[256,256]{1,0:T(8,128)(2,1)S(1)} collective-permute-done((bf16[256,256]{1,0:T(8,128)(2,1)S(1)}, bf16[256,256]{1,0:T(8,128)(2,1)S(1)}, u32[]{:S(2)}, u32[]{:S(2)}) %collective-permute-start.10) | collective-permute-done | bytes 131104 | tf_op jit(solution)/shard_map/ppermute | solution.py:99
  23.2 1.0 %collective-permute-start.11 = (bf16[192,256]{1,0:T(8,128)(2,1)S(1)}, bf16[192,256]{1,0:T(8,128)(2,1)S(1)}, u32[]{:S(2)}, u32[]{:S(2)}) collective-permute-start(bf16[192,256]{1,0:T(8,128)(2,1)S(1)} %get-tuple-element.45), channel_id=1, source_target_pairs={{0,8},{1,9},{2,10},{3,11},{4,7},{5,6},{6,5},{7,4},{8,16},{9,17},{1... | collective-permute-start | bytes 294920 | tf_op jit(solution)/shard_map/ppermute | solution.py:274
  24.1 2.6 %collective-permute-start.12 = (bf16[192,256]{1,0:T(8,128)(2,1)S(1)}, bf16[192,256]{1,0:T(8,128)(2,1)S(1)}, u32[]{:S(2)}, u32[]{:S(2)}) collective-permute-start(bf16[192,256]{1,0:T(8,128)(2,1)S(1)} %get-tuple-element.46), channel_id=1, source_target_pairs={{0,16},{1,17},{2,18},{3,19},{4,6},{5,7},{6,4},{7,5},{8,24},{9,25},... | collective-permute-start | bytes 294920 | tf_op jit(solution)/shard_map/ppermute | solution.py:274
  26.8 2.1 %collective-permute-start.13 = (bf16[192,256]{1,0:T(8,128)(2,1)S(1)}, bf16[192,256]{1,0:T(8,128)(2,1)S(1)}, u32[]{:S(2)}, u32[]{:S(2)}) collective-permute-start(bf16[192,256]{1,0:T(8,128)(2,1)S(1)} %get-tuple-element.47), channel_id=1, source_target_pairs={{0,24},{1,25},{2,26},{3,27},{4,5},{5,4},{6,7},{7,6},{8,0},{9,1},{1... | collective-permute-start | bytes 294920 | tf_op jit(solution)/shard_map/ppermute | solution.py:274
  28.8 0.9 %collective-permute-done.11.refs_0_ = bf16[192,256]{1,0:T(8,128)(2,1)S(1)} collective-permute-done((bf16[192,256]{1,0:T(8,128)(2,1)S(1)}, bf16[192,256]{1,0:T(8,128)(2,1)S(1)}, u32[]{:S(2)}, u32[]{:S(2)}) %collective-permute-start.11) | collective-permute-done | bytes 98336 | tf_op jit(solution)/shard_map/ppermute | solution.py:274
  29.7 2.0 %collective-permute-done.12.refs_1_ = bf16[192,256]{1,0:T(8,128)(2,1)S(1)} collective-permute-done((bf16[192,256]{1,0:T(8,128)(2,1)S(1)}, bf16[192,256]{1,0:T(8,128)(2,1)S(1)}, u32[]{:S(2)}, u32[]{:S(2)}) %collective-permute-start.12) | collective-permute-done | bytes 98336 | tf_op jit(solution)/shard_map/ppermute | solution.py:274
  31.7 0.3 collective-permute-done.13.refs_2_
  32.0 0.1 second.1
  32.1 0.9 %collective-permute-start.14 = (bf16[192,256]{1,0:T(8,128)(2,1)S(1)}, bf16[192,256]{1,0:T(8,128)(2,1)S(1)}, u32[]{:S(2)}, u32[]{:S(2)}) collective-permute-start(bf16[192,256]{1,0:T(8,128)(2,1)S(1)} %get-tuple-element.49), channel_id=1, source_target_pairs={{0,3},{1,2},{2,1},{3,0},{4,12},{5,13},{6,14},{7,15},{8,11},{9,10},... | collective-permute-start | bytes 294920 | tf_op jit(solution)/shard_map/ppermute | solution.py:274
  33.0 1.6 %collective-permute-start.15 = (bf16[192,256]{1,0:T(8,128)(2,1)S(1)}, bf16[192,256]{1,0:T(8,128)(2,1)S(1)}, u32[]{:S(2)}, u32[]{:S(2)}) collective-permute-start(bf16[192,256]{1,0:T(8,128)(2,1)S(1)} %get-tuple-element.50), channel_id=1, source_target_pairs={{0,2},{1,3},{2,0},{3,1},{4,20},{5,21},{6,22},{7,23},{8,10},{9,11},... | collective-permute-start | bytes 294920 | tf_op jit(solution)/shard_map/ppermute | solution.py:274
  34.6 1.0 %collective-permute-start.16 = (bf16[192,256]{1,0:T(8,128)(2,1)S(1)}, bf16[192,256]{1,0:T(8,128)(2,1)S(1)}, u32[]{:S(2)}, u32[]{:S(2)}) collective-permute-start(bf16[192,256]{1,0:T(8,128)(2,1)S(1)} %get-tuple-element.51), channel_id=1, source_target_pairs={{0,1},{1,0},{2,3},{3,2},{4,28},{5,29},{6,30},{7,31},{8,9},{9,8},{1... | collective-permute-start | bytes 294920 | tf_op jit(solution)/shard_map/ppermute | solution.py:274
  35.6 0.7 %store.2._ = bf16[8,32,256]{2,1,0:T(8,128)(2,1)} custom-call(bf16[128,256]{1,0:T(8,128)(2,1)S(1)} %get-tuple-element.41.same_ref.refs_0_, bf16[256,256]{1,0:T(8,128)(2,1)S(1)} %collective-permute-done.10.came_ref.refs_1_, bf16[192,256]{1,0:T(8,128)(2,1)S(1)} %collective-permute-done.11.refs_0_, bf16[192,256]{1,0:T(8,128)(2,1)S(1)} %collective-permute-done.12.refs_1_, ...), custom_call_target="tpu_custom_call" | custom-call | tf_op jit(solution)/shard_map/store/pallas_call | solution.py:228
  36.3 1.4 %collective-permute-done.14.refs_0_.refs_2_ = bf16[192,256]{1,0:T(8,128)(2,1)S(1)} collective-permute-done((bf16[192,256]{1,0:T(8,128)(2,1)S(1)}, bf16[192,256]{1,0:T(8,128)(2,1)S(1)}, u32[]{:S(2)}, u32[]{:S(2)}) %collective-permute-start.14) | collective-permute-done | bytes 98336 | tf_op jit(solution)/shard_map/ppermute | solution.py:274
  37.8 0.9 %collective-permute-done.15.refs_1_.refs_3_ = bf16[192,256]{1,0:T(8,128)(2,1)S(1)} collective-permute-done((bf16[192,256]{1,0:T(8,128)(2,1)S(1)}, bf16[192,256]{1,0:T(8,128)(2,1)S(1)}, u32[]{:S(2)}, u32[]{:S(2)}) %collective-permute-start.15) | collective-permute-done | bytes 98336 | tf_op jit(solution)/shard_map/ppermute | solution.py:274
  38.6 0.6 %collective-permute-done.16.refs_2_.refs_4_ = bf16[192,256]{1,0:T(8,128)(2,1)S(1)} collective-permute-done((bf16[192,256]{1,0:T(8,128)(2,1)S(1)}, bf16[192,256]{1,0:T(8,128)(2,1)S(1)}, u32[]{:S(2)}, u32[]{:S(2)}) %collective-permute-start.16) | collective-permute-done | bytes 98336 | tf_op jit(solution)/shard_map/ppermute | solution.py:274
  39.3 0.1 third.1.own_ref
  39.3 0.1 collective-permute-start.17
  39.4 1.2 %collective-permute-done.17.came_ref = bf16[128,256]{1,0:T(8,128)(2,1)S(1)} collective-permute-done((bf16[128,256]{1,0:T(8,128)(2,1)S(1)}, bf16[128,256]{1,0:T(8,128)(2,1)S(1)}, u32[]{:S(2)}, u32[]{:S(2)}) %collective-permute-start.17) | collective-permute-done | bytes 65568 | tf_op jit(solution)/shard_map/ppermute | solution.py:99
  40.6 0.7 %finish.1 = f32[2,128,256]{2,1,0:T(8,128)} custom-call(bf16[128,256]{1,0:T(8,128)(2,1)S(1)} %third.1.own_ref, bf16[128,256]{1,0:T(8,128)(2,1)S(1)} %collective-permute-done.17.came_ref), custom_call_target="tpu_custom_call" | custom-call | tf_op jit(solution)/shard_map/finish/pallas_call | solution.py:247
  (9 shorter events, 0.1 us)
Async XLA Ops:
  0.6 8.5 %collective-permute-start.2 = (bf16[128,256]{1,0:T(8,128)(2,1)}, bf16[128,256]{1,0:T(8,128)(2,1)S(1)}, u32[]{:S(2)}, u32[]{:S(2)}) collective-permute-start(bf16[128,256]{1,0:T(8,128)(2,1)} %own_ref.1), channel_id=1, source_target_pairs={{0,16},{4,20},{8,24},{12,28},{16,0},{20,4},{24,8},{28,12},{1,17},{... | collective-permute-start | bytes 196616 | tf_op jit(solution)/shard_map/ppermute | solution.py:99
  4.7 6.4 %collective-permute-start.1 = (bf16[128,256]{1,0:T(8,128)(2,1)}, bf16[128,256]{1,0:T(8,128)(2,1)S(1)}, u32[]{:S(2)}, u32[]{:S(2)}) collective-permute-start(bf16[128,256]{1,0:T(8,128)(2,1)} %own_ref.1), channel_id=1, source_target_pairs={{0,24},{4,28},{8,16},{12,20},{16,8},{20,12},{24,0},{28,4},{1,25},{... | collective-permute-start | bytes 196616 | tf_op jit(solution)/shard_map/ppermute | solution.py:99
  6.1 5.2 %collective-permute-start = (bf16[128,256]{1,0:T(8,128)(2,1)}, bf16[128,256]{1,0:T(8,128)(2,1)S(1)}, u32[]{:S(2)}, u32[]{:S(2)}) collective-permute-start(bf16[128,256]{1,0:T(8,128)(2,1)} %own_ref.1), channel_id=1, source_target_pairs={{0,8},{4,12},{8,0},{12,4},{16,24},{20,28},{24,16},{28,20},{1,9},{5... | collective-permute-start | bytes 196616 | tf_op jit(solution)/shard_map/ppermute | solution.py:99
  6.3 5.5 %collective-permute-start.3 = (bf16[128,256]{1,0:T(8,128)(2,1)}, bf16[128,256]{1,0:T(8,128)(2,1)S(1)}, u32[]{:S(2)}, u32[]{:S(2)}) collective-permute-start(bf16[128,256]{1,0:T(8,128)(2,1)} %own_ref.1), channel_id=1, source_target_pairs={{0,4},{4,0},{8,12},{12,8},{16,20},{20,16},{24,28},{28,24},{1,5},{5... | collective-permute-start | bytes 196616 | tf_op jit(solution)/shard_map/ppermute | solution.py:99
  6.3 0.7 %copy-start.5 = (s32[128,1]{0,1:T(1,128)S(1)}, s32[128,1]{0,1:T(1,128)}, u32[]{:S(2)}) copy-start(s32[128,1]{0,1:T(1,128)} %param.11) | copy-start | bytes 1540
  7.0 1.0 %copy-start = (bf16[4,1,4,128,128]{4,3,2,1,0:T(8,128)(2,1)S(1)}, bf16[4,1,4,128,128]{4,3,2,1,0:T(8,128)(2,1)}, u32[]{:S(2)}) copy-start(bf16[4,1,4,128,128]{4,3,2,1,0:T(8,128)(2,1)} %param.7) | copy-start | bytes 1572868
  8.0 0.8 %copy-start.2 = (bf16[128,256]{1,0:T(8,128)(2,1)S(1)}, bf16[128,256]{1,0:T(8,128)(2,1)}, u32[]{:S(2)}) copy-start(bf16[128,256]{1,0:T(8,128)(2,1)} %own_ref.1) | copy-start | bytes 196612
  11.3 1.8 %copy-start.4 = (s32[4,1,4]{2,1,0:T(1,128)S(1)}, s32[4,1,4]{2,1,0:T(1,128)}, u32[]{:S(2)}) copy-start(s32[4,1,4]{2,1,0:T(1,128)} %param.8) | copy-start | bytes 196
  11.3 1.3 %collective-permute-start.4 = (bf16[128,256]{1,0:T(8,128)(2,1)S(1)}, bf16[128,256]{1,0:T(8,128)(2,1)S(1)}, u32[]{:S(2)}, u32[]{:S(2)}) collective-permute-start(bf16[128,256]{1,0:T(8,128)(2,1)S(1)} %collective-permute-done.refs_2_), channel_id=1, source_target_pairs={{0,4},{4,0},{8,12},{12,8},{16,20},{20,16},{24,28},{28,24},{1,5},{5... | collective-permute-start | bytes 196616 | tf_op jit(solution)/shard_map/ppermute | solution.py:99
  11.3 1.4 %collective-permute-start.5 = (bf16[128,256]{1,0:T(8,128)(2,1)S(1)}, bf16[128,256]{1,0:T(8,128)(2,1)S(1)}, u32[]{:S(2)}, u32[]{:S(2)}) collective-permute-start(bf16[128,256]{1,0:T(8,128)(2,1)S(1)} %collective-permute-done.2.refs_4_), channel_id=1, source_target_pairs={{0,4},{4,0},{8,12},{12,8},{16,20},{20,16},{24,28},{28,24},{1,5},{5... | collective-permute-start | bytes 196616 | tf_op jit(solution)/shard_map/ppermute | solution.py:99
  11.8 1.3 %collective-permute-start.6 = (bf16[128,256]{1,0:T(8,128)(2,1)S(1)}, bf16[128,256]{1,0:T(8,128)(2,1)S(1)}, u32[]{:S(2)}, u32[]{:S(2)}) collective-permute-start(bf16[128,256]{1,0:T(8,128)(2,1)S(1)} %collective-permute-done.1.refs_6_), channel_id=1, source_target_pairs={{0,4},{4,0},{8,12},{12,8},{16,20},{20,16},{24,28},{28,24},{1,5},{5... | collective-permute-start | bytes 196616 | tf_op jit(solution)/shard_map/ppermute | solution.py:99
  13.0 8.2 %copy-start.1 = (bf16[256,256]{1,0:T(8,128)(2,1)S(1)}, bf16[256,256]{1,0:T(8,128)(2,1)}, u32[]{:S(2)}) copy-start(bf16[256,256]{1,0:T(8,128)(2,1)} %weight_ref.1) | copy-start | bytes 393220
  13.0 8.2 %copy-start.3 = (bf16[128,256]{1,0:T(8,128)(2,1)S(1)}, bf16[128,256]{1,0:T(8,128)(2,1)}, u32[]{:S(2)}) copy-start(bf16[128,256]{1,0:T(8,128)(2,1)} %cot_ref.1) | copy-start | bytes 196612
  13.5 5.3 %collective-permute-start.7 = (bf16[128,256]{1,0:T(8,128)(2,1)S(1)}, bf16[128,256]{1,0:T(8,128)(2,1)S(1)}, u32[]{:S(2)}, u32[]{:S(2)}) collective-permute-start(bf16[128,256]{1,0:T(8,128)(2,1)S(1)} %get-tuple-element.38), channel_id=1, source_target_pairs={{0,3},{1,2},{2,1},{3,0},{4,5},{5,4},{6,7},{7,6},{8,11},{9,10},{10,... | collective-permute-start | bytes 196616 | tf_op jit(solution)/shard_map/ppermute | solution.py:263
  16.0 4.3 %collective-permute-start.8 = (bf16[128,256]{1,0:T(8,128)(2,1)S(1)}, bf16[128,256]{1,0:T(8,128)(2,1)S(1)}, u32[]{:S(2)}, u32[]{:S(2)}) collective-permute-start(bf16[128,256]{1,0:T(8,128)(2,1)S(1)} %get-tuple-element.39), channel_id=1, source_target_pairs={{0,1},{1,0},{2,3},{3,2},{4,6},{5,7},{6,4},{7,5},{8,9},{9,8},{10,11... | collective-permute-start | bytes 196616 | tf_op jit(solution)/shard_map/ppermute | solution.py:263
  16.5 4.7 %collective-permute-start.9 = (bf16[128,256]{1,0:T(8,128)(2,1)S(1)}, bf16[128,256]{1,0:T(8,128)(2,1)S(1)}, u32[]{:S(2)}, u32[]{:S(2)}) collective-permute-start(bf16[128,256]{1,0:T(8,128)(2,1)S(1)} %get-tuple-element.40), channel_id=1, source_target_pairs={{0,2},{1,3},{2,0},{3,1},{4,7},{5,6},{6,5},{7,4},{8,10},{9,11},{10,... | collective-permute-start | bytes 196616 | tf_op jit(solution)/shard_map/ppermute | solution.py:263
  21.7 1.4 %collective-permute-start.10 = (bf16[256,256]{1,0:T(8,128)(2,1)S(1)}, bf16[256,256]{1,0:T(8,128)(2,1)S(1)}, u32[]{:S(2)}, u32[]{:S(2)}) collective-permute-start(bf16[256,256]{1,0:T(8,128)(2,1)S(1)} %get-tuple-element.42), channel_id=1, source_target_pairs={{0,4},{4,0},{8,12},{12,8},{16,20},{20,16},{24,28},{28,24},{1,5},{5... | collective-permute-start | bytes 393224 | tf_op jit(solution)/shard_map/ppermute | solution.py:99
  23.2 6.6 %collective-permute-start.11 = (bf16[192,256]{1,0:T(8,128)(2,1)S(1)}, bf16[192,256]{1,0:T(8,128)(2,1)S(1)}, u32[]{:S(2)}, u32[]{:S(2)}) collective-permute-start(bf16[192,256]{1,0:T(8,128)(2,1)S(1)} %get-tuple-element.45), channel_id=1, source_target_pairs={{0,8},{1,9},{2,10},{3,11},{4,7},{5,6},{6,5},{7,4},{8,16},{9,17},{1... | collective-permute-start | bytes 294920 | tf_op jit(solution)/shard_map/ppermute | solution.py:274
  24.1 7.6 %collective-permute-start.12 = (bf16[192,256]{1,0:T(8,128)(2,1)S(1)}, bf16[192,256]{1,0:T(8,128)(2,1)S(1)}, u32[]{:S(2)}, u32[]{:S(2)}) collective-permute-start(bf16[192,256]{1,0:T(8,128)(2,1)S(1)} %get-tuple-element.46), channel_id=1, source_target_pairs={{0,16},{1,17},{2,18},{3,19},{4,6},{5,7},{6,4},{7,5},{8,24},{9,25},... | collective-permute-start | bytes 294920 | tf_op jit(solution)/shard_map/ppermute | solution.py:274
  26.8 5.2 %collective-permute-start.13 = (bf16[192,256]{1,0:T(8,128)(2,1)S(1)}, bf16[192,256]{1,0:T(8,128)(2,1)S(1)}, u32[]{:S(2)}, u32[]{:S(2)}) collective-permute-start(bf16[192,256]{1,0:T(8,128)(2,1)S(1)} %get-tuple-element.47), channel_id=1, source_target_pairs={{0,24},{1,25},{2,26},{3,27},{4,5},{5,4},{6,7},{7,6},{8,0},{9,1},{1... | collective-permute-start | bytes 294920 | tf_op jit(solution)/shard_map/ppermute | solution.py:274
  32.1 5.7 %collective-permute-start.14 = (bf16[192,256]{1,0:T(8,128)(2,1)S(1)}, bf16[192,256]{1,0:T(8,128)(2,1)S(1)}, u32[]{:S(2)}, u32[]{:S(2)}) collective-permute-start(bf16[192,256]{1,0:T(8,128)(2,1)S(1)} %get-tuple-element.49), channel_id=1, source_target_pairs={{0,3},{1,2},{2,1},{3,0},{4,12},{5,13},{6,14},{7,15},{8,11},{9,10},... | collective-permute-start | bytes 294920 | tf_op jit(solution)/shard_map/ppermute | solution.py:274
  33.0 5.7 %collective-permute-start.15 = (bf16[192,256]{1,0:T(8,128)(2,1)S(1)}, bf16[192,256]{1,0:T(8,128)(2,1)S(1)}, u32[]{:S(2)}, u32[]{:S(2)}) collective-permute-start(bf16[192,256]{1,0:T(8,128)(2,1)S(1)} %get-tuple-element.50), channel_id=1, source_target_pairs={{0,2},{1,3},{2,0},{3,1},{4,20},{5,21},{6,22},{7,23},{8,10},{9,11},... | collective-permute-start | bytes 294920 | tf_op jit(solution)/shard_map/ppermute | solution.py:274
  34.6 4.6 %collective-permute-start.16 = (bf16[192,256]{1,0:T(8,128)(2,1)S(1)}, bf16[192,256]{1,0:T(8,128)(2,1)S(1)}, u32[]{:S(2)}, u32[]{:S(2)}) collective-permute-start(bf16[192,256]{1,0:T(8,128)(2,1)S(1)} %get-tuple-element.51), channel_id=1, source_target_pairs={{0,1},{1,0},{2,3},{3,2},{4,28},{5,29},{6,30},{7,31},{8,9},{9,8},{1... | collective-permute-start | bytes 294920 | tf_op jit(solution)/shard_map/ppermute | solution.py:274
  39.3 1.3 %collective-permute-start.17 = (bf16[128,256]{1,0:T(8,128)(2,1)S(1)}, bf16[128,256]{1,0:T(8,128)(2,1)S(1)}, u32[]{:S(2)}, u32[]{:S(2)}) collective-permute-start(bf16[128,256]{1,0:T(8,128)(2,1)S(1)} %third.1.own_ref), channel_id=1, source_target_pairs={{0,4},{4,0},{8,12},{12,8},{16,20},{20,16},{24,28},{28,24},{1,5},{5... | collective-permute-start | bytes 196616 | tf_op jit(solution)/shard_map/ppermute | solution.py:99

commit v18 on v13

--- a/solution.py
+++ b/solution.py
@@ -264,13 +264,10 @@
     n = lax.axis_size(axis)
     blocks = [None] * n
     blocks[0] = features
-    order = sorted(range(2, n, 2), key=lambda j: (j & 4, -(j & 2)))
-    for j in order:
+    for j in range(2, n, 2):
         blocks[j] = swap(features, axis, j)
     blocks[1] = swap(features, axis, 1)
-    came, ready = lax.optimization_barrier(([blocks[j] for j in order], ready))
-    for j, block in zip(order, came):
-        blocks[j] = block
+    blocks[2::2], ready = lax.optimization_barrier((blocks[2::2], ready))
     for j in range(2, n, 2):
         blocks[j + 1] = swap(blocks[j], axis, 1)
     return blocks, ready

time: 40.6 us -> 41.2 us (1.015)
  waiting for transfers between devices: 15.4 us -> 16.9 us
  starting transfers between devices: 19.1 us -> 18.1 us
    ppermute x6, waiting for transfers between devices: 5.67 us -> 7.04 us  [exchange(): return lax.ppermute(value, ('section', 'rep'), pairs)]
    ppermute x6, starting transfers between devices: 9.2 us -> 8.09 us  [exchange(): return lax.ppermute(value, ('section', 'rep'), pairs)]
  transfers between devices with their start and end apart: 18 -> 18, of which waited for: 16 -> 15; matrix products, arithmetic and copies ran while one was open for 0% -> 0% of each run, Pallas kernels for 2% -> 2%
where the time goes in v18:
time: 41.2 us; the launch traced here: 41 us
  starting transfers between devices  18.1 us (44%)
  waiting for transfers between devices  16.9 us (41%)
  Pallas kernels  2.67 us (6%)
  local copies, waits for them, and re-layouts  2.55 us (6%)
  between operations  0.73 us (2%)
    ppermute x12, starting transfers between devices, swap(): lax.ppermute(value, axis, [(i, i ^ j) for i in range(lax.axis_size(axis))])  10 us
    ppermute x12, waiting for transfers between devices, swap(): lax.ppermute(value, axis, [(i, i ^ j) for i in range(lax.axis_size(axis))])  9.88 us
    ppermute x6, starting transfers between devices, exchange(): return lax.ppermute(value, ('section', 'rep'), pairs)  8.09 us
    ppermute x6, waiting for transfers between devices, exchange(): return lax.ppermute(value, ('section', 'rep'), pairs)  7.04 us
    unnamed x12, local copies, waits for them, and re-layouts  2.55 us
  transfers between devices with their start and end apart: 18, of which 15 were waited for; matrix products, arithmetic and copies ran while one was open for 0% of the time, Pallas kernels for 2%

profile of v18, /device:TPU:0, one launch (start us, length us, event | category | flops | bytes accessed | tf_op | source)
XLA Modules:
  0.0 41.0 jit_solution(815450948767555783)
XLA Ops:
  0.6 5.1 %collective-permute-start.2 = (bf16[128,256]{1,0:T(8,128)(2,1)}, bf16[128,256]{1,0:T(8,128)(2,1)S(1)}, u32[]{:S(2)}, u32[]{:S(2)}) collective-permute-start(bf16[128,256]{1,0:T(8,128)(2,1)} %own_ref.1), channel_id=1, source_target_pairs={{0,24},{4,28},{8,16},{12,20},{16,8},{20,12},{24,0},{28,4},{1,25},{... | collective-permute-start | bytes 196616 | tf_op jit(solution)/shard_map/ppermute | solution.py:94
  5.7 0.0 collective-permute-start.1
  5.7 0.6 %collective-permute-start = (bf16[128,256]{1,0:T(8,128)(2,1)}, bf16[128,256]{1,0:T(8,128)(2,1)S(1)}, u32[]{:S(2)}, u32[]{:S(2)}) collective-permute-start(bf16[128,256]{1,0:T(8,128)(2,1)} %own_ref.1), channel_id=1, source_target_pairs={{0,8},{4,12},{8,0},{12,4},{16,24},{20,28},{24,16},{28,20},{1,9},{5... | collective-permute-start | bytes 196616 | tf_op jit(solution)/shard_map/ppermute | solution.py:94
  6.4 0.0 collective-permute-start.3
  6.4 0.7 %copy-done.5 = s32[128,1]{0,1:T(1,128)S(1)} copy-done((s32[128,1]{0,1:T(1,128)S(1)}, s32[128,1]{0,1:T(1,128)}, u32[]{:S(2)}) %copy-start.5) | copy-done | bytes 536
  7.0 1.0 %copy-done = bf16[4,1,4,128,128]{4,3,2,1,0:T(8,128)(2,1)S(1)} copy-done((bf16[4,1,4,128,128]{4,3,2,1,0:T(8,128)(2,1)S(1)}, bf16[4,1,4,128,128]{4,3,2,1,0:T(8,128)(2,1)}, u32[]{:S(2)}) %copy-start) | copy-done | bytes 524312
  8.1 0.8 %copy-done.2 = bf16[128,256]{1,0:T(8,128)(2,1)S(1)} copy-done((bf16[128,256]{1,0:T(8,128)(2,1)S(1)}, bf16[128,256]{1,0:T(8,128)(2,1)}, u32[]{:S(2)}) %copy-start.2) | copy-done | bytes 65560
  8.9 0.2 prepare.1
  9.2 0.0 collective-permute-done.2.refs_6_
  9.2 2.4 %collective-permute-done.1.refs_4_ = bf16[128,256]{1,0:T(8,128)(2,1)S(1)} collective-permute-done((bf16[128,256]{1,0:T(8,128)(2,1)}, bf16[128,256]{1,0:T(8,128)(2,1)S(1)}, u32[]{:S(2)}, u32[]{:S(2)}) %collective-permute-start.1) | collective-permute-done | bytes 65568 | tf_op jit(solution)/shard_map/ppermute | solution.py:94
  11.6 0.0 collective-permute-done.refs_2_
  11.6 0.0 collective-permute-start.4
  11.6 0.5 %collective-permute-start.5 = (bf16[128,256]{1,0:T(8,128)(2,1)S(1)}, bf16[128,256]{1,0:T(8,128)(2,1)S(1)}, u32[]{:S(2)}, u32[]{:S(2)}) collective-permute-start(bf16[128,256]{1,0:T(8,128)(2,1)S(1)} %collective-permute-done.1.refs_4_), channel_id=1, source_target_pairs={{0,4},{4,0},{8,12},{12,8},{16,20},{20,16},{24,28},{28,24},{1,5},{5... | collective-permute-start | bytes 196616 | tf_op jit(solution)/shard_map/ppermute | solution.py:94
  12.1 0.1 collective-permute-start.6
  12.1 0.0 collective-permute-done.3.refs_1_
  12.1 0.7 %collective-permute-done.4.refs_3_ = bf16[128,256]{1,0:T(8,128)(2,1)S(1)} collective-permute-done((bf16[128,256]{1,0:T(8,128)(2,1)S(1)}, bf16[128,256]{1,0:T(8,128)(2,1)S(1)}, u32[]{:S(2)}, u32[]{:S(2)}) %collective-permute-start.4) | collective-permute-done | bytes 65568 | tf_op jit(solution)/shard_map/ppermute | solution.py:94
  12.8 0.2 collective-permute-done.5.refs_5_
  13.0 0.4 collective-permute-done.6.refs_7_
  13.3 0.0 copy-done.4
  13.3 0.4 %partials.1 = (bf16[128,256]{1,0:T(8,128)(2,1)S(1)}, bf16[128,256]{1,0:T(8,128)(2,1)S(1)}, bf16[128,256]{1,0:T(8,128)(2,1)S(1)}, bf16[128,256]{1,0:T(8,128)(2,1)S(1)}) custom-call(s32[4,4]{1,0:T(4,128)S(1)} %bitcast.6, bf16[4,128,512]{2,1,0:T(8,128)(2,1)S(1)} %get-tuple-element.32.wide_ref, bf16[128,256]{1,0:T(8,128)(2,1)S(1)} %get-tuple-element.33.refs_0_, ...), custom_call_target="tpu_custom_call" | custom-call | tf_op jit(solution)/shard_map/partials/pallas_call | solution.py:82
  13.8 2.5 %collective-permute-start.7 = (bf16[128,256]{1,0:T(8,128)(2,1)S(1)}, bf16[128,256]{1,0:T(8,128)(2,1)S(1)}, u32[]{:S(2)}, u32[]{:S(2)}) collective-permute-start(bf16[128,256]{1,0:T(8,128)(2,1)S(1)} %get-tuple-element.38), channel_id=1, source_target_pairs={{0,3},{1,2},{2,1},{3,0},{4,7},{5,6},{6,5},{7,4},{8,11},{9,10},{10,... | collective-permute-start | bytes 196616 | tf_op jit(solution)/shard_map/ppermute | solution.py:94
  16.3 0.5 %collective-permute-start.8 = (bf16[128,256]{1,0:T(8,128)(2,1)S(1)}, bf16[128,256]{1,0:T(8,128)(2,1)S(1)}, u32[]{:S(2)}, u32[]{:S(2)}) collective-permute-start(bf16[128,256]{1,0:T(8,128)(2,1)S(1)} %get-tuple-element.39), channel_id=1, source_target_pairs={{0,2},{1,3},{2,0},{3,1},{4,6},{5,7},{6,4},{7,5},{8,10},{9,11},{10,... | collective-permute-start | bytes 196616 | tf_op jit(solution)/shard_map/ppermute | solution.py:94
  16.8 0.5 %collective-permute-start.9 = (bf16[128,256]{1,0:T(8,128)(2,1)S(1)}, bf16[128,256]{1,0:T(8,128)(2,1)S(1)}, u32[]{:S(2)}, u32[]{:S(2)}) collective-permute-start(bf16[128,256]{1,0:T(8,128)(2,1)S(1)} %get-tuple-element.40), channel_id=1, source_target_pairs={{0,1},{1,0},{2,3},{3,2},{4,5},{5,4},{6,7},{7,6},{8,9},{9,8},{10,11... | collective-permute-start | bytes 196616 | tf_op jit(solution)/shard_map/ppermute | solution.py:94
  17.3 1.7 %collective-permute-done.7.refs_1_ = bf16[128,256]{1,0:T(8,128)(2,1)S(1)} collective-permute-done((bf16[128,256]{1,0:T(8,128)(2,1)S(1)}, bf16[128,256]{1,0:T(8,128)(2,1)S(1)}, u32[]{:S(2)}, u32[]{:S(2)}) %collective-permute-start.7) | collective-permute-done | bytes 65568 | tf_op jit(solution)/shard_map/ppermute | solution.py:94
  19.0 1.5 %collective-permute-done.8.refs_2_ = bf16[128,256]{1,0:T(8,128)(2,1)S(1)} collective-permute-done((bf16[128,256]{1,0:T(8,128)(2,1)S(1)}, bf16[128,256]{1,0:T(8,128)(2,1)S(1)}, u32[]{:S(2)}, u32[]{:S(2)}) %collective-permute-start.8) | collective-permute-done | bytes 65568 | tf_op jit(solution)/shard_map/ppermute | solution.py:94
  20.5 0.5 %collective-permute-done.9.refs_3_ = bf16[128,256]{1,0:T(8,128)(2,1)S(1)} collective-permute-done((bf16[128,256]{1,0:T(8,128)(2,1)S(1)}, bf16[128,256]{1,0:T(8,128)(2,1)S(1)}, u32[]{:S(2)}, u32[]{:S(2)}) %collective-permute-start.9) | collective-permute-done | bytes 65568 | tf_op jit(solution)/shard_map/ppermute | solution.py:94
  21.1 0.0 copy-done.1
  21.1 0.4 %dense.1 = (bf16[128,256]{1,0:T(8,128)(2,1)S(1)}, f32[128,256]{1,0:T(8,128)S(1)}, bf16[256,256]{1,0:T(8,128)(2,1)S(1)}) custom-call(bf16[256,256]{1,0:T(8,128)(2,1)S(1)} %copy-done.1, bf16[128,256]{1,0:T(8,128)(2,1)S(1)} %copy-done.3, bf16[256,128]{1,0:T(8,128)(2,1)S(1)} %get-tuple-element.31.placing_ref, bf16[128,256]{1,0:T(8,128)(2,1)S(1)} %get-tuple-element.37.refs_0_, ...), custom_call_target="tpu_custom_call" | custom-call | tf_op jit(solution)/shard_map/dense/pallas_call | solution.py:126
  21.5 0.1 collective-permute-start.10
  21.6 1.3 %collective-permute-done.10.came_ref.refs_1_ = bf16[256,256]{1,0:T(8,128)(2,1)S(1)} collective-permute-done((bf16[256,256]{1,0:T(8,128)(2,1)S(1)}, bf16[256,256]{1,0:T(8,128)(2,1)S(1)}, u32[]{:S(2)}, u32[]{:S(2)}) %collective-permute-start.10) | collective-permute-done | bytes 131104 | tf_op jit(solution)/shard_map/ppermute | solution.py:94
  23.0 1.1 %collective-permute-start.11 = (bf16[192,256]{1,0:T(8,128)(2,1)S(1)}, bf16[192,256]{1,0:T(8,128)(2,1)S(1)}, u32[]{:S(2)}, u32[]{:S(2)}) collective-permute-start(bf16[192,256]{1,0:T(8,128)(2,1)S(1)} %get-tuple-element.45), channel_id=1, source_target_pairs={{0,8},{1,9},{2,10},{3,11},{4,7},{5,6},{6,5},{7,4},{8,16},{9,17},{1... | collective-permute-start | bytes 294920 | tf_op jit(solution)/shard_map/ppermute | solution.py:260
  24.1 2.2 %collective-permute-start.12 = (bf16[192,256]{1,0:T(8,128)(2,1)S(1)}, bf16[192,256]{1,0:T(8,128)(2,1)S(1)}, u32[]{:S(2)}, u32[]{:S(2)}) collective-permute-start(bf16[192,256]{1,0:T(8,128)(2,1)S(1)} %get-tuple-element.46), channel_id=1, source_target_pairs={{0,16},{1,17},{2,18},{3,19},{4,6},{5,7},{6,4},{7,5},{8,24},{9,25},... | collective-permute-start | bytes 294920 | tf_op jit(solution)/shard_map/ppermute | solution.py:260
  26.3 1.2 %collective-permute-start.13 = (bf16[192,256]{1,0:T(8,128)(2,1)S(1)}, bf16[192,256]{1,0:T(8,128)(2,1)S(1)}, u32[]{:S(2)}, u32[]{:S(2)}) collective-permute-start(bf16[192,256]{1,0:T(8,128)(2,1)S(1)} %get-tuple-element.47), channel_id=1, source_target_pairs={{0,24},{1,25},{2,26},{3,27},{4,5},{5,4},{6,7},{7,6},{8,0},{9,1},{1... | collective-permute-start | bytes 294920 | tf_op jit(solution)/shard_map/ppermute | solution.py:260
  27.5 2.0 %collective-permute-done.11.refs_0_ = bf16[192,256]{1,0:T(8,128)(2,1)S(1)} collective-permute-done((bf16[192,256]{1,0:T(8,128)(2,1)S(1)}, bf16[192,256]{1,0:T(8,128)(2,1)S(1)}, u32[]{:S(2)}, u32[]{:S(2)}) %collective-permute-start.11) | collective-permute-done | bytes 98336 | tf_op jit(solution)/shard_map/ppermute | solution.py:260
  29.5 2.1 %collective-permute-done.12.refs_1_ = bf16[192,256]{1,0:T(8,128)(2,1)S(1)} collective-permute-done((bf16[192,256]{1,0:T(8,128)(2,1)S(1)}, bf16[192,256]{1,0:T(8,128)(2,1)S(1)}, u32[]{:S(2)}, u32[]{:S(2)}) %collective-permute-start.12) | collective-permute-done | bytes 98336 | tf_op jit(solution)/shard_map/ppermute | solution.py:260
  31.6 0.2 collective-permute-done.13.refs_2_
  31.9 0.1 second.1
  32.0 1.5 %collective-permute-start.14 = (bf16[192,256]{1,0:T(8,128)(2,1)S(1)}, bf16[192,256]{1,0:T(8,128)(2,1)S(1)}, u32[]{:S(2)}, u32[]{:S(2)}) collective-permute-start(bf16[192,256]{1,0:T(8,128)(2,1)S(1)} %get-tuple-element.49), channel_id=1, source_target_pairs={{0,3},{1,2},{2,1},{3,0},{4,12},{5,13},{6,14},{7,15},{8,11},{9,10},... | collective-permute-start | bytes 294920 | tf_op jit(solution)/shard_map/ppermute | solution.py:260
  33.5 0.8 %collective-permute-start.15 = (bf16[192,256]{1,0:T(8,128)(2,1)S(1)}, bf16[192,256]{1,0:T(8,128)(2,1)S(1)}, u32[]{:S(2)}, u32[]{:S(2)}) collective-permute-start(bf16[192,256]{1,0:T(8,128)(2,1)S(1)} %get-tuple-element.50), channel_id=1, source_target_pairs={{0,2},{1,3},{2,0},{3,1},{4,20},{5,21},{6,22},{7,23},{8,10},{9,11},... | collective-permute-start | bytes 294920 | tf_op jit(solution)/shard_map/ppermute | solution.py:260
  34.3 1.2 %collective-permute-start.16 = (bf16[192,256]{1,0:T(8,128)(2,1)S(1)}, bf16[192,256]{1,0:T(8,128)(2,1)S(1)}, u32[]{:S(2)}, u32[]{:S(2)}) collective-permute-start(bf16[192,256]{1,0:T(8,128)(2,1)S(1)} %get-tuple-element.51), channel_id=1, source_target_pairs={{0,1},{1,0},{2,3},{3,2},{4,28},{5,29},{6,30},{7,31},{8,9},{9,8},{1... | collective-permute-start | bytes 294920 | tf_op jit(solution)/shard_map/ppermute | solution.py:260
  35.5 0.7 %store.2._ = bf16[8,32,256]{2,1,0:T(8,128)(2,1)} custom-call(bf16[128,256]{1,0:T(8,128)(2,1)S(1)} %get-tuple-element.41.same_ref.refs_0_, bf16[256,256]{1,0:T(8,128)(2,1)S(1)} %collective-permute-done.10.came_ref.refs_1_, bf16[192,256]{1,0:T(8,128)(2,1)S(1)} %collective-permute-done.11.refs_0_, bf16[192,256]{1,0:T(8,128)(2,1)S(1)} %collective-permute-done.12.refs_1_, ...), custom_call_target="tpu_custom_call" | custom-call | tf_op jit(solution)/shard_map/store/pallas_call | solution.py:223
  36.2 1.4 %collective-permute-done.14.refs_0_.refs_2_ = bf16[192,256]{1,0:T(8,128)(2,1)S(1)} collective-permute-done((bf16[192,256]{1,0:T(8,128)(2,1)S(1)}, bf16[192,256]{1,0:T(8,128)(2,1)S(1)}, u32[]{:S(2)}, u32[]{:S(2)}) %collective-permute-start.14) | collective-permute-done | bytes 98336 | tf_op jit(solution)/shard_map/ppermute | solution.py:260
  37.6 1.0 %collective-permute-done.15.refs_1_.refs_3_ = bf16[192,256]{1,0:T(8,128)(2,1)S(1)} collective-permute-done((bf16[192,256]{1,0:T(8,128)(2,1)S(1)}, bf16[192,256]{1,0:T(8,128)(2,1)S(1)}, u32[]{:S(2)}, u32[]{:S(2)}) %collective-permute-start.15) | collective-permute-done | bytes 98336 | tf_op jit(solution)/shard_map/ppermute | solution.py:260
  38.6 0.3 collective-permute-done.16.refs_2_.refs_4_
  38.9 0.1 third.1.own_ref
  39.0 0.1 collective-permute-start.17
  39.0 1.2 %collective-permute-done.17.came_ref = bf16[128,256]{1,0:T(8,128)(2,1)S(1)} collective-permute-done((bf16[128,256]{1,0:T(8,128)(2,1)S(1)}, bf16[128,256]{1,0:T(8,128)(2,1)S(1)}, u32[]{:S(2)}, u32[]{:S(2)}) %collective-permute-start.17) | collective-permute-done | bytes 65568 | tf_op jit(solution)/shard_map/ppermute | solution.py:94
  40.3 0.7 %finish.1 = f32[2,128,256]{2,1,0:T(8,128)} custom-call(bf16[128,256]{1,0:T(8,128)(2,1)S(1)} %third.1.own_ref, bf16[128,256]{1,0:T(8,128)(2,1)S(1)} %collective-permute-done.17.came_ref), custom_call_target="tpu_custom_call" | custom-call | tf_op jit(solution)/shard_map/finish/pallas_call | solution.py:242
  (9 shorter events, 0.1 us)
Async XLA Ops:
  0.6 8.5 %collective-permute-start.2 = (bf16[128,256]{1,0:T(8,128)(2,1)}, bf16[128,256]{1,0:T(8,128)(2,1)S(1)}, u32[]{:S(2)}, u32[]{:S(2)}) collective-permute-start(bf16[128,256]{1,0:T(8,128)(2,1)} %own_ref.1), channel_id=1, source_target_pairs={{0,24},{4,28},{8,16},{12,20},{16,8},{20,12},{24,0},{28,4},{1,25},{... | collective-permute-start | bytes 196616 | tf_op jit(solution)/shard_map/ppermute | solution.py:94
  5.7 5.8 %collective-permute-start.1 = (bf16[128,256]{1,0:T(8,128)(2,1)}, bf16[128,256]{1,0:T(8,128)(2,1)S(1)}, u32[]{:S(2)}, u32[]{:S(2)}) collective-permute-start(bf16[128,256]{1,0:T(8,128)(2,1)} %own_ref.1), channel_id=1, source_target_pairs={{0,16},{4,20},{8,24},{12,28},{16,0},{20,4},{24,8},{28,12},{1,17},{... | collective-permute-start | bytes 196616 | tf_op jit(solution)/shard_map/ppermute | solution.py:94
  5.7 5.8 %collective-permute-start = (bf16[128,256]{1,0:T(8,128)(2,1)}, bf16[128,256]{1,0:T(8,128)(2,1)S(1)}, u32[]{:S(2)}, u32[]{:S(2)}) collective-permute-start(bf16[128,256]{1,0:T(8,128)(2,1)} %own_ref.1), channel_id=1, source_target_pairs={{0,8},{4,12},{8,0},{12,4},{16,24},{20,28},{24,16},{28,20},{1,9},{5... | collective-permute-start | bytes 196616 | tf_op jit(solution)/shard_map/ppermute | solution.py:94
  6.4 5.8 %collective-permute-start.3 = (bf16[128,256]{1,0:T(8,128)(2,1)}, bf16[128,256]{1,0:T(8,128)(2,1)S(1)}, u32[]{:S(2)}, u32[]{:S(2)}) collective-permute-start(bf16[128,256]{1,0:T(8,128)(2,1)} %own_ref.1), channel_id=1, source_target_pairs={{0,4},{4,0},{8,12},{12,8},{16,20},{20,16},{24,28},{28,24},{1,5},{5... | collective-permute-start | bytes 196616 | tf_op jit(solution)/shard_map/ppermute | solution.py:94
  6.4 0.7 %copy-start.5 = (s32[128,1]{0,1:T(1,128)S(1)}, s32[128,1]{0,1:T(1,128)}, u32[]{:S(2)}) copy-start(s32[128,1]{0,1:T(1,128)} %param.11) | copy-start | bytes 1540
  7.0 1.0 %copy-start = (bf16[4,1,4,128,128]{4,3,2,1,0:T(8,128)(2,1)S(1)}, bf16[4,1,4,128,128]{4,3,2,1,0:T(8,128)(2,1)}, u32[]{:S(2)}) copy-start(bf16[4,1,4,128,128]{4,3,2,1,0:T(8,128)(2,1)} %param.7) | copy-start | bytes 1572868
  8.1 0.8 %copy-start.2 = (bf16[128,256]{1,0:T(8,128)(2,1)S(1)}, bf16[128,256]{1,0:T(8,128)(2,1)}, u32[]{:S(2)}) copy-start(bf16[128,256]{1,0:T(8,128)(2,1)} %own_ref.1) | copy-start | bytes 196612
  11.6 1.8 %copy-start.4 = (s32[4,1,4]{2,1,0:T(1,128)S(1)}, s32[4,1,4]{2,1,0:T(1,128)}, u32[]{:S(2)}) copy-start(s32[4,1,4]{2,1,0:T(1,128)} %param.8) | copy-start | bytes 196
  11.6 1.3 %collective-permute-start.4 = (bf16[128,256]{1,0:T(8,128)(2,1)S(1)}, bf16[128,256]{1,0:T(8,128)(2,1)S(1)}, u32[]{:S(2)}, u32[]{:S(2)}) collective-permute-start(bf16[128,256]{1,0:T(8,128)(2,1)S(1)} %collective-permute-done.refs_2_), channel_id=1, source_target_pairs={{0,4},{4,0},{8,12},{12,8},{16,20},{20,16},{24,28},{28,24},{1,5},{5... | collective-permute-start | bytes 196616 | tf_op jit(solution)/shard_map/ppermute | solution.py:94
  11.6 1.4 %collective-permute-start.5 = (bf16[128,256]{1,0:T(8,128)(2,1)S(1)}, bf16[128,256]{1,0:T(8,128)(2,1)S(1)}, u32[]{:S(2)}, u32[]{:S(2)}) collective-permute-start(bf16[128,256]{1,0:T(8,128)(2,1)S(1)} %collective-permute-done.1.refs_4_), channel_id=1, source_target_pairs={{0,4},{4,0},{8,12},{12,8},{16,20},{20,16},{24,28},{28,24},{1,5},{5... | collective-permute-start | bytes 196616 | tf_op jit(solution)/shard_map/ppermute | solution.py:94
  12.1 1.3 %collective-permute-start.6 = (bf16[128,256]{1,0:T(8,128)(2,1)S(1)}, bf16[128,256]{1,0:T(8,128)(2,1)S(1)}, u32[]{:S(2)}, u32[]{:S(2)}) collective-permute-start(bf16[128,256]{1,0:T(8,128)(2,1)S(1)} %collective-permute-done.2.refs_6_), channel_id=1, source_target_pairs={{0,4},{4,0},{8,12},{12,8},{16,20},{20,16},{24,28},{28,24},{1,5},{5... | collective-permute-start | bytes 196616 | tf_op jit(solution)/shard_map/ppermute | solution.py:94
  13.3 7.7 %copy-start.1 = (bf16[256,256]{1,0:T(8,128)(2,1)S(1)}, bf16[256,256]{1,0:T(8,128)(2,1)}, u32[]{:S(2)}) copy-start(bf16[256,256]{1,0:T(8,128)(2,1)} %weight_ref.1) | copy-start | bytes 393220
  13.3 7.7 %copy-start.3 = (bf16[128,256]{1,0:T(8,128)(2,1)S(1)}, bf16[128,256]{1,0:T(8,128)(2,1)}, u32[]{:S(2)}) copy-start(bf16[128,256]{1,0:T(8,128)(2,1)} %cot_ref.1) | copy-start | bytes 196612
  13.8 5.3 %collective-permute-start.7 = (bf16[128,256]{1,0:T(8,128)(2,1)S(1)}, bf16[128,256]{1,0:T(8,128)(2,1)S(1)}, u32[]{:S(2)}, u32[]{:S(2)}) collective-permute-start(bf16[128,256]{1,0:T(8,128)(2,1)S(1)} %get-tuple-element.38), channel_id=1, source_target_pairs={{0,3},{1,2},{2,1},{3,0},{4,7},{5,6},{6,5},{7,4},{8,11},{9,10},{10,... | collective-permute-start | bytes 196616 | tf_op jit(solution)/shard_map/ppermute | solution.py:94
  16.3 4.3 %collective-permute-start.8 = (bf16[128,256]{1,0:T(8,128)(2,1)S(1)}, bf16[128,256]{1,0:T(8,128)(2,1)S(1)}, u32[]{:S(2)}, u32[]{:S(2)}) collective-permute-start(bf16[128,256]{1,0:T(8,128)(2,1)S(1)} %get-tuple-element.39), channel_id=1, source_target_pairs={{0,2},{1,3},{2,0},{3,1},{4,6},{5,7},{6,4},{7,5},{8,10},{9,11},{10,... | collective-permute-start | bytes 196616 | tf_op jit(solution)/shard_map/ppermute | solution.py:94
  16.8 4.3 %collective-permute-start.9 = (bf16[128,256]{1,0:T(8,128)(2,1)S(1)}, bf16[128,256]{1,0:T(8,128)(2,1)S(1)}, u32[]{:S(2)}, u32[]{:S(2)}) collective-permute-start(bf16[128,256]{1,0:T(8,128)(2,1)S(1)} %get-tuple-element.40), channel_id=1, source_target_pairs={{0,1},{1,0},{2,3},{3,2},{4,5},{5,4},{6,7},{7,6},{8,9},{9,8},{10,11... | collective-permute-start | bytes 196616 | tf_op jit(solution)/shard_map/ppermute | solution.py:94
  21.5 1.4 %collective-permute-start.10 = (bf16[256,256]{1,0:T(8,128)(2,1)S(1)}, bf16[256,256]{1,0:T(8,128)(2,1)S(1)}, u32[]{:S(2)}, u32[]{:S(2)}) collective-permute-start(bf16[256,256]{1,0:T(8,128)(2,1)S(1)} %get-tuple-element.42), channel_id=1, source_target_pairs={{0,4},{4,0},{8,12},{12,8},{16,20},{20,16},{24,28},{28,24},{1,5},{5... | collective-permute-start | bytes 393224 | tf_op jit(solution)/shard_map/ppermute | solution.py:94
  23.0 6.6 %collective-permute-start.11 = (bf16[192,256]{1,0:T(8,128)(2,1)S(1)}, bf16[192,256]{1,0:T(8,128)(2,1)S(1)}, u32[]{:S(2)}, u32[]{:S(2)}) collective-permute-start(bf16[192,256]{1,0:T(8,128)(2,1)S(1)} %get-tuple-element.45), channel_id=1, source_target_pairs={{0,8},{1,9},{2,10},{3,11},{4,7},{5,6},{6,5},{7,4},{8,16},{9,17},{1... | collective-permute-start | bytes 294920 | tf_op jit(solution)/shard_map/ppermute | solution.py:260
  24.1 7.5 %collective-permute-start.12 = (bf16[192,256]{1,0:T(8,128)(2,1)S(1)}, bf16[192,256]{1,0:T(8,128)(2,1)S(1)}, u32[]{:S(2)}, u32[]{:S(2)}) collective-permute-start(bf16[192,256]{1,0:T(8,128)(2,1)S(1)} %get-tuple-element.46), channel_id=1, source_target_pairs={{0,16},{1,17},{2,18},{3,19},{4,6},{5,7},{6,4},{7,5},{8,24},{9,25},... | collective-permute-start | bytes 294920 | tf_op jit(solution)/shard_map/ppermute | solution.py:260
  26.3 5.6 %collective-permute-start.13 = (bf16[192,256]{1,0:T(8,128)(2,1)S(1)}, bf16[192,256]{1,0:T(8,128)(2,1)S(1)}, u32[]{:S(2)}, u32[]{:S(2)}) collective-permute-start(bf16[192,256]{1,0:T(8,128)(2,1)S(1)} %get-tuple-element.47), channel_id=1, source_target_pairs={{0,24},{1,25},{2,26},{3,27},{4,5},{5,4},{6,7},{7,6},{8,0},{9,1},{1... | collective-permute-start | bytes 294920 | tf_op jit(solution)/shard_map/ppermute | solution.py:260
  32.0 5.6 %collective-permute-start.14 = (bf16[192,256]{1,0:T(8,128)(2,1)S(1)}, bf16[192,256]{1,0:T(8,128)(2,1)S(1)}, u32[]{:S(2)}, u32[]{:S(2)}) collective-permute-start(bf16[192,256]{1,0:T(8,128)(2,1)S(1)} %get-tuple-element.49), channel_id=1, source_target_pairs={{0,3},{1,2},{2,1},{3,0},{4,12},{5,13},{6,14},{7,15},{8,11},{9,10},... | collective-permute-start | bytes 294920 | tf_op jit(solution)/shard_map/ppermute | solution.py:260
  33.5 5.1 %collective-permute-start.15 = (bf16[192,256]{1,0:T(8,128)(2,1)S(1)}, bf16[192,256]{1,0:T(8,128)(2,1)S(1)}, u32[]{:S(2)}, u32[]{:S(2)}) collective-permute-start(bf16[192,256]{1,0:T(8,128)(2,1)S(1)} %get-tuple-element.50), channel_id=1, source_target_pairs={{0,2},{1,3},{2,0},{3,1},{4,20},{5,21},{6,22},{7,23},{8,10},{9,11},... | collective-permute-start | bytes 294920 | tf_op jit(solution)/shard_map/ppermute | solution.py:260
  34.3 4.6 %collective-permute-start.16 = (bf16[192,256]{1,0:T(8,128)(2,1)S(1)}, bf16[192,256]{1,0:T(8,128)(2,1)S(1)}, u32[]{:S(2)}, u32[]{:S(2)}) collective-permute-start(bf16[192,256]{1,0:T(8,128)(2,1)S(1)} %get-tuple-element.51), channel_id=1, source_target_pairs={{0,1},{1,0},{2,3},{3,2},{4,28},{5,29},{6,30},{7,31},{8,9},{9,8},{1... | collective-permute-start | bytes 294920 | tf_op jit(solution)/shard_map/ppermute | solution.py:260
  39.0 1.3 %collective-permute-start.17 = (bf16[128,256]{1,0:T(8,128)(2,1)S(1)}, bf16[128,256]{1,0:T(8,128)(2,1)S(1)}, u32[]{:S(2)}, u32[]{:S(2)}) collective-permute-start(bf16[128,256]{1,0:T(8,128)(2,1)S(1)} %third.1.own_ref), channel_id=1, source_target_pairs={{0,4},{4,0},{8,12},{12,8},{16,20},{20,16},{24,28},{28,24},{1,5},{5... | collective-permute-start | bytes 196616 | tf_op jit(solution)/shard_map/ppermute | solution.py:94

commit v19 on v13

--- a/solution.py
+++ b/solution.py
@@ -268,10 +268,11 @@
     for j in order:
         blocks[j] = swap(features, axis, j)
     blocks[1] = swap(features, axis, 1)
-    came, ready = lax.optimization_barrier(([blocks[j] for j in order], ready))
-    for j, block in zip(order, came):
+    blocks[3] = swap(features, axis, 3)
+    came, ready = lax.optimization_barrier(([blocks[j] for j in [3] + order], ready))
+    for j, block in zip([3] + order, came):
         blocks[j] = block
-    for j in range(2, n, 2):
+    for j in range(4, n, 2):
         blocks[j + 1] = swap(blocks[j], axis, 1)
     return blocks, ready
 

time: 40.6 us -> 41.7 us (1.027)
  starting transfers between devices: 19.1 us -> 20 us
    ppermute x12, starting transfers between devices: 9.89 us -> 11.8 us  [swap(): lax.ppermute(value, axis, [(i, i ^ j) for i in range(lax.axis_size(axis))])]
    ppermute x6, waiting for transfers between devices: 5.67 us -> 7.01 us  [exchange(): return lax.ppermute(value, ('section', 'rep'), pairs)]
    ppermute x12, waiting for transfers between devices: 9.72 us -> 8.52 us  [swap(): lax.ppermute(value, axis, [(i, i ^ j) for i in range(lax.axis_size(axis))])]
    ppermute x6, starting transfers between devices: 9.2 us -> 8.2 us  [exchange(): return lax.ppermute(value, ('section', 'rep'), pairs)]
  transfers between devices with their start and end apart: 18 -> 18, of which waited for: 16 -> 15; matrix products, arithmetic and copies ran while one was open for 0% -> 0% of each run, Pallas kernels for 2% -> 2%
where the time goes in v19:
time: 41.7 us; the launch traced here: 41.5 us
  starting transfers between devices  20 us (48%)
  waiting for transfers between devices  15.5 us (37%)
  Pallas kernels  2.67 us (6%)
  local copies, waits for them, and re-layouts  2.55 us (6%)
  between operations  0.73 us (2%)
    ppermute x12, starting transfers between devices, swap(): lax.ppermute(value, axis, [(i, i ^ j) for i in range(lax.axis_size(axis))])  11.8 us
    ppermute x12, waiting for transfers between devices, swap(): lax.ppermute(value, axis, [(i, i ^ j) for i in range(lax.axis_size(axis))])  8.52 us
    ppermute x6, starting transfers between devices, exchange(): return lax.ppermute(value, ('section', 'rep'), pairs)  8.2 us
    ppermute x6, waiting for transfers between devices, exchange(): return lax.ppermute(value, ('section', 'rep'), pairs)  7.01 us
    unnamed x12, local copies, waits for them, and re-layouts  2.55 us
  transfers between devices with their start and end apart: 18, of which 15 were waited for; matrix products, arithmetic and copies ran while one was open for 0% of the time, Pallas kernels for 2%

profile of v19, /device:TPU:0, one launch (start us, length us, event | category | flops | bytes accessed | tf_op | source)
XLA Modules:
  0.0 41.5 jit_solution(18370335598154771972)
XLA Ops:
  0.6 4.1 %collective-permute-start.3 = (bf16[128,256]{1,0:T(8,128)(2,1)}, bf16[128,256]{1,0:T(8,128)(2,1)S(1)}, u32[]{:S(2)}, u32[]{:S(2)}) collective-permute-start(bf16[128,256]{1,0:T(8,128)(2,1)} %own_ref.1), channel_id=1, source_target_pairs={{0,16},{4,20},{8,24},{12,28},{16,0},{20,4},{24,8},{28,12},{1,17},{... | collective-permute-start | bytes 196616 | tf_op jit(solution)/shard_map/ppermute | solution.py:94
  4.7 1.3 %collective-permute-start.2 = (bf16[128,256]{1,0:T(8,128)(2,1)}, bf16[128,256]{1,0:T(8,128)(2,1)S(1)}, u32[]{:S(2)}, u32[]{:S(2)}) collective-permute-start(bf16[128,256]{1,0:T(8,128)(2,1)} %own_ref.1), channel_id=1, source_target_pairs={{0,24},{4,28},{8,16},{12,20},{16,8},{20,12},{24,0},{28,4},{1,25},{... | collective-permute-start | bytes 196616 | tf_op jit(solution)/shard_map/ppermute | solution.py:94
  6.1 0.2 collective-permute-start.1
  6.3 0.4 %collective-permute-start = (bf16[128,256]{1,0:T(8,128)(2,1)}, bf16[128,256]{1,0:T(8,128)(2,1)S(1)}, u32[]{:S(2)}, u32[]{:S(2)}) collective-permute-start(bf16[128,256]{1,0:T(8,128)(2,1)} %own_ref.1), channel_id=1, source_target_pairs={{0,12},{4,8},{8,4},{12,0},{16,28},{20,24},{24,20},{28,16},{1,13},{... | collective-permute-start | bytes 196616 | tf_op jit(solution)/shard_map/ppermute | solution.py:94
  6.7 1.5 %collective-permute-start.4 = (bf16[128,256]{1,0:T(8,128)(2,1)}, bf16[128,256]{1,0:T(8,128)(2,1)S(1)}, u32[]{:S(2)}, u32[]{:S(2)}) collective-permute-start(bf16[128,256]{1,0:T(8,128)(2,1)} %own_ref.1), channel_id=1, source_target_pairs={{0,4},{4,0},{8,12},{12,8},{16,20},{20,16},{24,28},{28,24},{1,5},{5... | collective-permute-start | bytes 196616 | tf_op jit(solution)/shard_map/ppermute | solution.py:94
  8.2 0.7 %copy-done.5 = s32[128,1]{0,1:T(1,128)S(1)} copy-done((s32[128,1]{0,1:T(1,128)S(1)}, s32[128,1]{0,1:T(1,128)}, u32[]{:S(2)}) %copy-start.5) | copy-done | bytes 536
  8.9 1.0 %copy-done = bf16[4,1,4,128,128]{4,3,2,1,0:T(8,128)(2,1)S(1)} copy-done((bf16[4,1,4,128,128]{4,3,2,1,0:T(8,128)(2,1)S(1)}, bf16[4,1,4,128,128]{4,3,2,1,0:T(8,128)(2,1)}, u32[]{:S(2)}) %copy-start) | copy-done | bytes 524312
  9.9 0.8 %copy-done.2 = bf16[128,256]{1,0:T(8,128)(2,1)S(1)} copy-done((bf16[128,256]{1,0:T(8,128)(2,1)S(1)}, bf16[128,256]{1,0:T(8,128)(2,1)}, u32[]{:S(2)}) %copy-start.2) | copy-done | bytes 65560
  10.8 0.2 prepare.1
  11.0 0.0 collective-permute-done.3.refs_4_
  11.0 0.2 collective-permute-done.2.refs_6_
  11.2 0.6 %collective-permute-done.1.refs_2_ = bf16[128,256]{1,0:T(8,128)(2,1)S(1)} collective-permute-done((bf16[128,256]{1,0:T(8,128)(2,1)}, bf16[128,256]{1,0:T(8,128)(2,1)S(1)}, u32[]{:S(2)}, u32[]{:S(2)}) %collective-permute-start.1) | collective-permute-done | bytes 65568 | tf_op jit(solution)/shard_map/ppermute | solution.py:94
  11.8 0.0 collective-permute-done.refs_3_
  11.8 0.5 %collective-permute-start.5 = (bf16[128,256]{1,0:T(8,128)(2,1)S(1)}, bf16[128,256]{1,0:T(8,128)(2,1)S(1)}, u32[]{:S(2)}, u32[]{:S(2)}) collective-permute-start(bf16[128,256]{1,0:T(8,128)(2,1)S(1)} %collective-permute-done.3.refs_4_), channel_id=1, source_target_pairs={{0,4},{4,0},{8,12},{12,8},{16,20},{20,16},{24,28},{28,24},{1,5},{5... | collective-permute-start | bytes 196616 | tf_op jit(solution)/shard_map/ppermute | solution.py:94
  12.3 0.0 collective-permute-start.6
  12.3 0.0 collective-permute-done.4.refs_1_
  12.3 0.9 %collective-permute-done.5.refs_5_ = bf16[128,256]{1,0:T(8,128)(2,1)S(1)} collective-permute-done((bf16[128,256]{1,0:T(8,128)(2,1)S(1)}, bf16[128,256]{1,0:T(8,128)(2,1)S(1)}, u32[]{:S(2)}, u32[]{:S(2)}) %collective-permute-start.5) | collective-permute-done | bytes 65568 | tf_op jit(solution)/shard_map/ppermute | solution.py:94
  13.2 0.4 collective-permute-done.6.refs_7_
  13.5 0.0 copy-done.4
  13.5 0.4 %partials.1 = (bf16[128,256]{1,0:T(8,128)(2,1)S(1)}, bf16[128,256]{1,0:T(8,128)(2,1)S(1)}, bf16[128,256]{1,0:T(8,128)(2,1)S(1)}, bf16[128,256]{1,0:T(8,128)(2,1)S(1)}) custom-call(s32[4,4]{1,0:T(4,128)S(1)} %bitcast.6, bf16[4,128,512]{2,1,0:T(8,128)(2,1)S(1)} %get-tuple-element.33.wide_ref, bf16[128,256]{1,0:T(8,128)(2,1)S(1)} %get-tuple-element.34.refs_0_, ...), custom_call_target="tpu_custom_call" | custom-call | tf_op jit(solution)/shard_map/partials/pallas_call | solution.py:82
  14.0 2.7 %collective-permute-start.7 = (bf16[128,256]{1,0:T(8,128)(2,1)S(1)}, bf16[128,256]{1,0:T(8,128)(2,1)S(1)}, u32[]{:S(2)}, u32[]{:S(2)}) collective-permute-start(bf16[128,256]{1,0:T(8,128)(2,1)S(1)} %get-tuple-element.40), channel_id=1, source_target_pairs={{0,3},{1,2},{2,1},{3,0},{4,7},{5,6},{6,5},{7,4},{8,11},{9,10},{10,... | collective-permute-start | bytes 196616 | tf_op jit(solution)/shard_map/ppermute | solution.py:94
  16.7 0.5 %collective-permute-start.8 = (bf16[128,256]{1,0:T(8,128)(2,1)S(1)}, bf16[128,256]{1,0:T(8,128)(2,1)S(1)}, u32[]{:S(2)}, u32[]{:S(2)}) collective-permute-start(bf16[128,256]{1,0:T(8,128)(2,1)S(1)} %get-tuple-element.41), channel_id=1, source_target_pairs={{0,2},{1,3},{2,0},{3,1},{4,6},{5,7},{6,4},{7,5},{8,10},{9,11},{10,... | collective-permute-start | bytes 196616 | tf_op jit(solution)/shard_map/ppermute | solution.py:94
  17.2 0.3 collective-permute-start.9
  17.5 1.7 %collective-permute-done.7.refs_1_ = bf16[128,256]{1,0:T(8,128)(2,1)S(1)} collective-permute-done((bf16[128,256]{1,0:T(8,128)(2,1)S(1)}, bf16[128,256]{1,0:T(8,128)(2,1)S(1)}, u32[]{:S(2)}, u32[]{:S(2)}) %collective-permute-start.7) | collective-permute-done | bytes 65568 | tf_op jit(solution)/shard_map/ppermute | solution.py:94
  19.2 1.8 %collective-permute-done.8.refs_2_ = bf16[128,256]{1,0:T(8,128)(2,1)S(1)} collective-permute-done((bf16[128,256]{1,0:T(8,128)(2,1)S(1)}, bf16[128,256]{1,0:T(8,128)(2,1)S(1)}, u32[]{:S(2)}, u32[]{:S(2)}) %collective-permute-start.8) | collective-permute-done | bytes 65568 | tf_op jit(solution)/shard_map/ppermute | solution.py:94
  21.0 0.5 %collective-permute-done.9.refs_3_ = bf16[128,256]{1,0:T(8,128)(2,1)S(1)} collective-permute-done((bf16[128,256]{1,0:T(8,128)(2,1)S(1)}, bf16[128,256]{1,0:T(8,128)(2,1)S(1)}, u32[]{:S(2)}, u32[]{:S(2)}) %collective-permute-start.9) | collective-permute-done | bytes 65568 | tf_op jit(solution)/shard_map/ppermute | solution.py:94
  21.5 0.0 copy-done.1
  21.5 0.4 %dense.1 = (bf16[128,256]{1,0:T(8,128)(2,1)S(1)}, f32[128,256]{1,0:T(8,128)S(1)}, bf16[256,256]{1,0:T(8,128)(2,1)S(1)}) custom-call(bf16[256,256]{1,0:T(8,128)(2,1)S(1)} %copy-done.1, bf16[128,256]{1,0:T(8,128)(2,1)S(1)} %copy-done.3, bf16[256,128]{1,0:T(8,128)(2,1)S(1)} %get-tuple-element.32.placing_ref, bf16[128,256]{1,0:T(8,128)(2,1)S(1)} %get-tuple-element.39.refs_0_, ...), custom_call_target="tpu_custom_call" | custom-call | tf_op jit(solution)/shard_map/dense/pallas_call | solution.py:126
  21.9 0.1 collective-permute-start.10
  22.0 1.3 %collective-permute-done.10.came_ref.refs_1_ = bf16[256,256]{1,0:T(8,128)(2,1)S(1)} collective-permute-done((bf16[256,256]{1,0:T(8,128)(2,1)S(1)}, bf16[256,256]{1,0:T(8,128)(2,1)S(1)}, u32[]{:S(2)}, u32[]{:S(2)}) %collective-permute-start.10) | collective-permute-done | bytes 131104 | tf_op jit(solution)/shard_map/ppermute | solution.py:94
  23.4 0.8 %collective-permute-start.11 = (bf16[192,256]{1,0:T(8,128)(2,1)S(1)}, bf16[192,256]{1,0:T(8,128)(2,1)S(1)}, u32[]{:S(2)}, u32[]{:S(2)}) collective-permute-start(bf16[192,256]{1,0:T(8,128)(2,1)S(1)} %get-tuple-element.47), channel_id=1, source_target_pairs={{0,8},{1,9},{2,10},{3,11},{4,7},{5,6},{6,5},{7,4},{8,16},{9,17},{1... | collective-permute-start | bytes 294920 | tf_op jit(solution)/shard_map/ppermute | solution.py:260
  24.1 2.8 %collective-permute-start.12 = (bf16[192,256]{1,0:T(8,128)(2,1)S(1)}, bf16[192,256]{1,0:T(8,128)(2,1)S(1)}, u32[]{:S(2)}, u32[]{:S(2)}) collective-permute-start(bf16[192,256]{1,0:T(8,128)(2,1)S(1)} %get-tuple-element.48), channel_id=1, source_target_pairs={{0,16},{1,17},{2,18},{3,19},{4,6},{5,7},{6,4},{7,5},{8,24},{9,25},... | collective-permute-start | bytes 294920 | tf_op jit(solution)/shard_map/ppermute | solution.py:260
  27.0 1.1 %collective-permute-start.13 = (bf16[192,256]{1,0:T(8,128)(2,1)S(1)}, bf16[192,256]{1,0:T(8,128)(2,1)S(1)}, u32[]{:S(2)}, u32[]{:S(2)}) collective-permute-start(bf16[192,256]{1,0:T(8,128)(2,1)S(1)} %get-tuple-element.49), channel_id=1, source_target_pairs={{0,24},{1,25},{2,26},{3,27},{4,5},{5,4},{6,7},{7,6},{8,0},{9,1},{1... | collective-permute-start | bytes 294920 | tf_op jit(solution)/shard_map/ppermute | solution.py:260
  28.0 1.9 %collective-permute-done.11.refs_0_ = bf16[192,256]{1,0:T(8,128)(2,1)S(1)} collective-permute-done((bf16[192,256]{1,0:T(8,128)(2,1)S(1)}, bf16[192,256]{1,0:T(8,128)(2,1)S(1)}, u32[]{:S(2)}, u32[]{:S(2)}) %collective-permute-start.11) | collective-permute-done | bytes 98336 | tf_op jit(solution)/shard_map/ppermute | solution.py:260
  29.9 1.9 %collective-permute-done.12.refs_1_ = bf16[192,256]{1,0:T(8,128)(2,1)S(1)} collective-permute-done((bf16[192,256]{1,0:T(8,128)(2,1)S(1)}, bf16[192,256]{1,0:T(8,128)(2,1)S(1)}, u32[]{:S(2)}, u32[]{:S(2)}) %collective-permute-start.12) | collective-permute-done | bytes 98336 | tf_op jit(solution)/shard_map/ppermute | solution.py:260
  31.9 0.5 %collective-permute-done.13.refs_2_ = bf16[192,256]{1,0:T(8,128)(2,1)S(1)} collective-permute-done((bf16[192,256]{1,0:T(8,128)(2,1)S(1)}, bf16[192,256]{1,0:T(8,128)(2,1)S(1)}, u32[]{:S(2)}, u32[]{:S(2)}) %collective-permute-start.13) | collective-permute-done | bytes 98336 | tf_op jit(solution)/shard_map/ppermute | solution.py:260
  32.4 0.1 second.1
  32.5 1.5 %collective-permute-start.14 = (bf16[192,256]{1,0:T(8,128)(2,1)S(1)}, bf16[192,256]{1,0:T(8,128)(2,1)S(1)}, u32[]{:S(2)}, u32[]{:S(2)}) collective-permute-start(bf16[192,256]{1,0:T(8,128)(2,1)S(1)} %get-tuple-element.51), channel_id=1, source_target_pairs={{0,3},{1,2},{2,1},{3,0},{4,12},{5,13},{6,14},{7,15},{8,11},{9,10},... | collective-permute-start | bytes 294920 | tf_op jit(solution)/shard_map/ppermute | solution.py:260
  34.0 0.8 %collective-permute-start.15 = (bf16[192,256]{1,0:T(8,128)(2,1)S(1)}, bf16[192,256]{1,0:T(8,128)(2,1)S(1)}, u32[]{:S(2)}, u32[]{:S(2)}) collective-permute-start(bf16[192,256]{1,0:T(8,128)(2,1)S(1)} %get-tuple-element.52), channel_id=1, source_target_pairs={{0,2},{1,3},{2,0},{3,1},{4,20},{5,21},{6,22},{7,23},{8,10},{9,11},... | collective-permute-start | bytes 294920 | tf_op jit(solution)/shard_map/ppermute | solution.py:260
  34.7 1.2 %collective-permute-start.16 = (bf16[192,256]{1,0:T(8,128)(2,1)S(1)}, bf16[192,256]{1,0:T(8,128)(2,1)S(1)}, u32[]{:S(2)}, u32[]{:S(2)}) collective-permute-start(bf16[192,256]{1,0:T(8,128)(2,1)S(1)} %get-tuple-element.53), channel_id=1, source_target_pairs={{0,1},{1,0},{2,3},{3,2},{4,28},{5,29},{6,30},{7,31},{8,9},{9,8},{1... | collective-permute-start | bytes 294920 | tf_op jit(solution)/shard_map/ppermute | solution.py:260
  36.0 0.7 %store.2._ = bf16[8,32,256]{2,1,0:T(8,128)(2,1)} custom-call(bf16[128,256]{1,0:T(8,128)(2,1)S(1)} %get-tuple-element.43.same_ref.refs_0_, bf16[256,256]{1,0:T(8,128)(2,1)S(1)} %collective-permute-done.10.came_ref.refs_1_, bf16[192,256]{1,0:T(8,128)(2,1)S(1)} %collective-permute-done.11.refs_0_, bf16[192,256]{1,0:T(8,128)(2,1)S(1)} %collective-permute-done.12.refs_1_, ...), custom_call_target="tpu_custom_call" | custom-call | tf_op jit(solution)/shard_map/store/pallas_call | solution.py:223
  36.7 1.4 %collective-permute-done.14.refs_0_.refs_2_ = bf16[192,256]{1,0:T(8,128)(2,1)S(1)} collective-permute-done((bf16[192,256]{1,0:T(8,128)(2,1)S(1)}, bf16[192,256]{1,0:T(8,128)(2,1)S(1)}, u32[]{:S(2)}, u32[]{:S(2)}) %collective-permute-start.14) | collective-permute-done | bytes 98336 | tf_op jit(solution)/shard_map/ppermute | solution.py:260
  38.1 1.0 %collective-permute-done.15.refs_1_.refs_3_ = bf16[192,256]{1,0:T(8,128)(2,1)S(1)} collective-permute-done((bf16[192,256]{1,0:T(8,128)(2,1)S(1)}, bf16[192,256]{1,0:T(8,128)(2,1)S(1)}, u32[]{:S(2)}, u32[]{:S(2)}) %collective-permute-start.15) | collective-permute-done | bytes 98336 | tf_op jit(solution)/shard_map/ppermute | solution.py:260
  39.1 0.3 collective-permute-done.16.refs_2_.refs_4_
  39.4 0.1 third.1.own_ref
  39.4 0.1 collective-permute-start.17
  39.5 1.2 %collective-permute-done.17.came_ref = bf16[128,256]{1,0:T(8,128)(2,1)S(1)} collective-permute-done((bf16[128,256]{1,0:T(8,128)(2,1)S(1)}, bf16[128,256]{1,0:T(8,128)(2,1)S(1)}, u32[]{:S(2)}, u32[]{:S(2)}) %collective-permute-start.17) | collective-permute-done | bytes 65568 | tf_op jit(solution)/shard_map/ppermute | solution.py:94
  40.8 0.7 %finish.1 = f32[2,128,256]{2,1,0:T(8,128)} custom-call(bf16[128,256]{1,0:T(8,128)(2,1)S(1)} %third.1.own_ref, bf16[128,256]{1,0:T(8,128)(2,1)S(1)} %collective-permute-done.17.came_ref), custom_call_target="tpu_custom_call" | custom-call | tf_op jit(solution)/shard_map/finish/pallas_call | solution.py:242
  (9 shorter events, 0.1 us)
Async XLA Ops:
  0.6 10.4 %collective-permute-start.3 = (bf16[128,256]{1,0:T(8,128)(2,1)}, bf16[128,256]{1,0:T(8,128)(2,1)S(1)}, u32[]{:S(2)}, u32[]{:S(2)}) collective-permute-start(bf16[128,256]{1,0:T(8,128)(2,1)} %own_ref.1), channel_id=1, source_target_pairs={{0,16},{4,20},{8,24},{12,28},{16,0},{20,4},{24,8},{28,12},{1,17},{... | collective-permute-start | bytes 196616 | tf_op jit(solution)/shard_map/ppermute | solution.py:94
  4.7 6.4 %collective-permute-start.2 = (bf16[128,256]{1,0:T(8,128)(2,1)}, bf16[128,256]{1,0:T(8,128)(2,1)S(1)}, u32[]{:S(2)}, u32[]{:S(2)}) collective-permute-start(bf16[128,256]{1,0:T(8,128)(2,1)} %own_ref.1), channel_id=1, source_target_pairs={{0,24},{4,28},{8,16},{12,20},{16,8},{20,12},{24,0},{28,4},{1,25},{... | collective-permute-start | bytes 196616 | tf_op jit(solution)/shard_map/ppermute | solution.py:94
  6.1 5.7 %collective-permute-start.1 = (bf16[128,256]{1,0:T(8,128)(2,1)}, bf16[128,256]{1,0:T(8,128)(2,1)S(1)}, u32[]{:S(2)}, u32[]{:S(2)}) collective-permute-start(bf16[128,256]{1,0:T(8,128)(2,1)} %own_ref.1), channel_id=1, source_target_pairs={{0,8},{4,12},{8,0},{12,4},{16,24},{20,28},{24,16},{28,20},{1,9},{5... | collective-permute-start | bytes 196616 | tf_op jit(solution)/shard_map/ppermute | solution.py:94
  6.3 5.4 %collective-permute-start = (bf16[128,256]{1,0:T(8,128)(2,1)}, bf16[128,256]{1,0:T(8,128)(2,1)S(1)}, u32[]{:S(2)}, u32[]{:S(2)}) collective-permute-start(bf16[128,256]{1,0:T(8,128)(2,1)} %own_ref.1), channel_id=1, source_target_pairs={{0,12},{4,8},{8,4},{12,0},{16,28},{20,24},{24,20},{28,16},{1,13},{... | collective-permute-start | bytes 196616 | tf_op jit(solution)/shard_map/ppermute | solution.py:94
  6.7 5.6 %collective-permute-start.4 = (bf16[128,256]{1,0:T(8,128)(2,1)}, bf16[128,256]{1,0:T(8,128)(2,1)S(1)}, u32[]{:S(2)}, u32[]{:S(2)}) collective-permute-start(bf16[128,256]{1,0:T(8,128)(2,1)} %own_ref.1), channel_id=1, source_target_pairs={{0,4},{4,0},{8,12},{12,8},{16,20},{20,16},{24,28},{28,24},{1,5},{5... | collective-permute-start | bytes 196616 | tf_op jit(solution)/shard_map/ppermute | solution.py:94
  8.2 0.7 %copy-start.5 = (s32[128,1]{0,1:T(1,128)S(1)}, s32[128,1]{0,1:T(1,128)}, u32[]{:S(2)}) copy-start(s32[128,1]{0,1:T(1,128)} %param.11) | copy-start | bytes 1540
  8.9 1.0 %copy-start = (bf16[4,1,4,128,128]{4,3,2,1,0:T(8,128)(2,1)S(1)}, bf16[4,1,4,128,128]{4,3,2,1,0:T(8,128)(2,1)}, u32[]{:S(2)}) copy-start(bf16[4,1,4,128,128]{4,3,2,1,0:T(8,128)(2,1)} %param.7) | copy-start | bytes 1572868
  9.9 0.8 %copy-start.2 = (bf16[128,256]{1,0:T(8,128)(2,1)S(1)}, bf16[128,256]{1,0:T(8,128)(2,1)}, u32[]{:S(2)}) copy-start(bf16[128,256]{1,0:T(8,128)(2,1)} %own_ref.1) | copy-start | bytes 196612
  11.8 1.8 %copy-start.4 = (s32[4,1,4]{2,1,0:T(1,128)S(1)}, s32[4,1,4]{2,1,0:T(1,128)}, u32[]{:S(2)}) copy-start(s32[4,1,4]{2,1,0:T(1,128)} %param.8) | copy-start | bytes 196
  11.8 1.4 %collective-permute-start.5 = (bf16[128,256]{1,0:T(8,128)(2,1)S(1)}, bf16[128,256]{1,0:T(8,128)(2,1)S(1)}, u32[]{:S(2)}, u32[]{:S(2)}) collective-permute-start(bf16[128,256]{1,0:T(8,128)(2,1)S(1)} %collective-permute-done.3.refs_4_), channel_id=1, source_target_pairs={{0,4},{4,0},{8,12},{12,8},{16,20},{20,16},{24,28},{28,24},{1,5},{5... | collective-permute-start | bytes 196616 | tf_op jit(solution)/shard_map/ppermute | solution.py:94
  12.3 1.3 %collective-permute-start.6 = (bf16[128,256]{1,0:T(8,128)(2,1)S(1)}, bf16[128,256]{1,0:T(8,128)(2,1)S(1)}, u32[]{:S(2)}, u32[]{:S(2)}) collective-permute-start(bf16[128,256]{1,0:T(8,128)(2,1)S(1)} %collective-permute-done.2.refs_6_), channel_id=1, source_target_pairs={{0,4},{4,0},{8,12},{12,8},{16,20},{20,16},{24,28},{28,24},{1,5},{5... | collective-permute-start | bytes 196616 | tf_op jit(solution)/shard_map/ppermute | solution.py:94
  13.5 7.9 %copy-start.1 = (bf16[256,256]{1,0:T(8,128)(2,1)S(1)}, bf16[256,256]{1,0:T(8,128)(2,1)}, u32[]{:S(2)}) copy-start(bf16[256,256]{1,0:T(8,128)(2,1)} %weight_ref.1) | copy-start | bytes 393220
  13.5 7.9 %copy-start.3 = (bf16[128,256]{1,0:T(8,128)(2,1)S(1)}, bf16[128,256]{1,0:T(8,128)(2,1)}, u32[]{:S(2)}) copy-start(bf16[128,256]{1,0:T(8,128)(2,1)} %cot_ref.1) | copy-start | bytes 196612
  14.0 5.2 %collective-permute-start.7 = (bf16[128,256]{1,0:T(8,128)(2,1)S(1)}, bf16[128,256]{1,0:T(8,128)(2,1)S(1)}, u32[]{:S(2)}, u32[]{:S(2)}) collective-permute-start(bf16[128,256]{1,0:T(8,128)(2,1)S(1)} %get-tuple-element.40), channel_id=1, source_target_pairs={{0,3},{1,2},{2,1},{3,0},{4,7},{5,6},{6,5},{7,4},{8,11},{9,10},{10,... | collective-permute-start | bytes 196616 | tf_op jit(solution)/shard_map/ppermute | solution.py:94
  16.7 4.3 %collective-permute-start.8 = (bf16[128,256]{1,0:T(8,128)(2,1)S(1)}, bf16[128,256]{1,0:T(8,128)(2,1)S(1)}, u32[]{:S(2)}, u32[]{:S(2)}) collective-permute-start(bf16[128,256]{1,0:T(8,128)(2,1)S(1)} %get-tuple-element.41), channel_id=1, source_target_pairs={{0,2},{1,3},{2,0},{3,1},{4,6},{5,7},{6,4},{7,5},{8,10},{9,11},{10,... | collective-permute-start | bytes 196616 | tf_op jit(solution)/shard_map/ppermute | solution.py:94
  17.2 4.3 %collective-permute-start.9 = (bf16[128,256]{1,0:T(8,128)(2,1)S(1)}, bf16[128,256]{1,0:T(8,128)(2,1)S(1)}, u32[]{:S(2)}, u32[]{:S(2)}) collective-permute-start(bf16[128,256]{1,0:T(8,128)(2,1)S(1)} %get-tuple-element.42), channel_id=1, source_target_pairs={{0,1},{1,0},{2,3},{3,2},{4,5},{5,4},{6,7},{7,6},{8,9},{9,8},{10,11... | collective-permute-start | bytes 196616 | tf_op jit(solution)/shard_map/ppermute | solution.py:94
  21.9 1.4 %collective-permute-start.10 = (bf16[256,256]{1,0:T(8,128)(2,1)S(1)}, bf16[256,256]{1,0:T(8,128)(2,1)S(1)}, u32[]{:S(2)}, u32[]{:S(2)}) collective-permute-start(bf16[256,256]{1,0:T(8,128)(2,1)S(1)} %get-tuple-element.44), channel_id=1, source_target_pairs={{0,4},{4,0},{8,12},{12,8},{16,20},{20,16},{24,28},{28,24},{1,5},{5... | collective-permute-start | bytes 393224 | tf_op jit(solution)/shard_map/ppermute | solution.py:94
  23.4 6.6 %collective-permute-start.11 = (bf16[192,256]{1,0:T(8,128)(2,1)S(1)}, bf16[192,256]{1,0:T(8,128)(2,1)S(1)}, u32[]{:S(2)}, u32[]{:S(2)}) collective-permute-start(bf16[192,256]{1,0:T(8,128)(2,1)S(1)} %get-tuple-element.47), channel_id=1, source_target_pairs={{0,8},{1,9},{2,10},{3,11},{4,7},{5,6},{6,5},{7,4},{8,16},{9,17},{1... | collective-permute-start | bytes 294920 | tf_op jit(solution)/shard_map/ppermute | solution.py:260
  24.1 7.7 %collective-permute-start.12 = (bf16[192,256]{1,0:T(8,128)(2,1)S(1)}, bf16[192,256]{1,0:T(8,128)(2,1)S(1)}, u32[]{:S(2)}, u32[]{:S(2)}) collective-permute-start(bf16[192,256]{1,0:T(8,128)(2,1)S(1)} %get-tuple-element.48), channel_id=1, source_target_pairs={{0,16},{1,17},{2,18},{3,19},{4,6},{5,7},{6,4},{7,5},{8,24},{9,25},... | collective-permute-start | bytes 294920 | tf_op jit(solution)/shard_map/ppermute | solution.py:260
  27.0 5.4 %collective-permute-start.13 = (bf16[192,256]{1,0:T(8,128)(2,1)S(1)}, bf16[192,256]{1,0:T(8,128)(2,1)S(1)}, u32[]{:S(2)}, u32[]{:S(2)}) collective-permute-start(bf16[192,256]{1,0:T(8,128)(2,1)S(1)} %get-tuple-element.49), channel_id=1, source_target_pairs={{0,24},{1,25},{2,26},{3,27},{4,5},{5,4},{6,7},{7,6},{8,0},{9,1},{1... | collective-permute-start | bytes 294920 | tf_op jit(solution)/shard_map/ppermute | solution.py:260
  32.5 5.6 %collective-permute-start.14 = (bf16[192,256]{1,0:T(8,128)(2,1)S(1)}, bf16[192,256]{1,0:T(8,128)(2,1)S(1)}, u32[]{:S(2)}, u32[]{:S(2)}) collective-permute-start(bf16[192,256]{1,0:T(8,128)(2,1)S(1)} %get-tuple-element.51), channel_id=1, source_target_pairs={{0,3},{1,2},{2,1},{3,0},{4,12},{5,13},{6,14},{7,15},{8,11},{9,10},... | collective-permute-start | bytes 294920 | tf_op jit(solution)/shard_map/ppermute | solution.py:260
  34.0 5.1 %collective-permute-start.15 = (bf16[192,256]{1,0:T(8,128)(2,1)S(1)}, bf16[192,256]{1,0:T(8,128)(2,1)S(1)}, u32[]{:S(2)}, u32[]{:S(2)}) collective-permute-start(bf16[192,256]{1,0:T(8,128)(2,1)S(1)} %get-tuple-element.52), channel_id=1, source_target_pairs={{0,2},{1,3},{2,0},{3,1},{4,20},{5,21},{6,22},{7,23},{8,10},{9,11},... | collective-permute-start | bytes 294920 | tf_op jit(solution)/shard_map/ppermute | solution.py:260
  34.7 4.6 %collective-permute-start.16 = (bf16[192,256]{1,0:T(8,128)(2,1)S(1)}, bf16[192,256]{1,0:T(8,128)(2,1)S(1)}, u32[]{:S(2)}, u32[]{:S(2)}) collective-permute-start(bf16[192,256]{1,0:T(8,128)(2,1)S(1)} %get-tuple-element.53), channel_id=1, source_target_pairs={{0,1},{1,0},{2,3},{3,2},{4,28},{5,29},{6,30},{7,31},{8,9},{9,8},{1... | collective-permute-start | bytes 294920 | tf_op jit(solution)/shard_map/ppermute | solution.py:260
  39.4 1.3 %collective-permute-start.17 = (bf16[128,256]{1,0:T(8,128)(2,1)S(1)}, bf16[128,256]{1,0:T(8,128)(2,1)S(1)}, u32[]{:S(2)}, u32[]{:S(2)}) collective-permute-start(bf16[128,256]{1,0:T(8,128)(2,1)S(1)} %third.1.own_ref), channel_id=1, source_target_pairs={{0,4},{4,0},{8,12},{12,8},{16,20},{20,16},{24,28},{28,24},{1,5},{5... | collective-permute-start | bytes 196616 | tf_op jit(solution)/shard_map/ppermute | solution.py:94

commit v20 on v18

--- a/solution.py
+++ b/solution.py
@@ -264,11 +264,16 @@
     n = lax.axis_size(axis)
     blocks = [None] * n
     blocks[0] = features
-    for j in range(2, n, 2):
+    first, *rest = [n // 2 & -2] + [j for j in range(2, n, 2) if j != n // 2 & -2]
+    for j in rest + [first]:
         blocks[j] = swap(features, axis, j)
     blocks[1] = swap(features, axis, 1)
-    blocks[2::2], ready = lax.optimization_barrier((blocks[2::2], ready))
-    for j in range(2, n, 2):
+    blocks[first], ready = lax.optimization_barrier((blocks[first], ready))
+    blocks[first + 1] = swap(blocks[first], axis, 1)
+    tied = lax.optimization_barrier([blocks[j] for j in rest + [first + 1]])
+    for j, block in zip(rest + [first + 1], tied):
+        blocks[j] = block
+    for j in rest:
         blocks[j + 1] = swap(blocks[j], axis, 1)
     return blocks, ready
 

time: 41.2 us -> 41.1 us (level)
  starting transfers between devices: 18.1 us -> 19.7 us
  waiting for transfers between devices: 16.9 us -> 15.3 us
    ppermute x12, waiting for transfers between devices: 9.88 us -> 8.77 us  [swap(): lax.ppermute(value, axis, [(i, i ^ j) for i in range(lax.axis_size(axis))])]
    ppermute x6, starting transfers between devices: 8.09 us -> 9.19 us  [exchange(): return lax.ppermute(value, ('section', 'rep'), pairs)]
    ppermute x6, waiting for transfers between devices: 7.04 us -> 6.53 us  [exchange(): return lax.ppermute(value, ('section', 'rep'), pairs)]
    ppermute x12, starting transfers between devices: 10 us -> 10.5 us  [swap(): lax.ppermute(value, axis, [(i, i ^ j) for i in range(lax.axis_size(axis))])]
where the time goes in v20:
time: 41.1 us; the launch traced here: 40.9 us
  starting transfers between devices  19.7 us (48%)
  waiting for transfers between devices  15.3 us (37%)
  Pallas kernels  2.66 us (6%)
  local copies, waits for them, and re-layouts  2.55 us (6%)
  between operations  0.74 us (2%)
    ppermute x12, starting transfers between devices, swap(): lax.ppermute(value, axis, [(i, i ^ j) for i in range(lax.axis_size(axis))])  10.5 us
    ppermute x6, starting transfers between devices, exchange(): return lax.ppermute(value, ('section', 'rep'), pairs)  9.19 us
    ppermute x12, waiting for transfers between devices, swap(): lax.ppermute(value, axis, [(i, i ^ j) for i in range(lax.axis_size(axis))])  8.77 us
    ppermute x6, waiting for transfers between devices, exchange(): return lax.ppermute(value, ('section', 'rep'), pairs)  6.53 us
    unnamed x12, local copies, waits for them, and re-layouts  2.55 us
  transfers between devices with their start and end apart: 18, of which 15 were waited for; matrix products, arithmetic and copies ran while one was open for 0% of the time, Pallas kernels for 2%

profile of v20, /device:TPU:0, one launch (start us, length us, event | category | flops | bytes accessed | tf_op | source)
XLA Modules:
  0.0 40.9 jit_solution(10409727685669192483)
XLA Ops:
  0.6 4.1 %collective-permute-start = (bf16[128,256]{1,0:T(8,128)(2,1)}, bf16[128,256]{1,0:T(8,128)(2,1)S(1)}, u32[]{:S(2)}, u32[]{:S(2)}) collective-permute-start(bf16[128,256]{1,0:T(8,128)(2,1)} %own_ref.1), channel_id=1, source_target_pairs={{0,16},{4,20},{8,24},{12,28},{16,0},{20,4},{24,8},{28,12},{1,17},{... | collective-permute-start | bytes 196616 | tf_op jit(solution)/shard_map/ppermute | solution.py:94
  4.7 1.3 %collective-permute-start.3 = (bf16[128,256]{1,0:T(8,128)(2,1)}, bf16[128,256]{1,0:T(8,128)(2,1)S(1)}, u32[]{:S(2)}, u32[]{:S(2)}) collective-permute-start(bf16[128,256]{1,0:T(8,128)(2,1)} %own_ref.1), channel_id=1, source_target_pairs={{0,24},{4,28},{8,16},{12,20},{16,8},{20,12},{24,0},{28,4},{1,25},{... | collective-permute-start | bytes 196616 | tf_op jit(solution)/shard_map/ppermute | solution.py:94
  6.1 0.2 collective-permute-start.2
  6.3 0.7 %copy-done.5 = s32[128,1]{0,1:T(1,128)S(1)} copy-done((s32[128,1]{0,1:T(1,128)S(1)}, s32[128,1]{0,1:T(1,128)}, u32[]{:S(2)}) %copy-start.5) | copy-done | bytes 536
  7.0 1.0 %copy-done = bf16[4,1,4,128,128]{4,3,2,1,0:T(8,128)(2,1)S(1)} copy-done((bf16[4,1,4,128,128]{4,3,2,1,0:T(8,128)(2,1)S(1)}, bf16[4,1,4,128,128]{4,3,2,1,0:T(8,128)(2,1)}, u32[]{:S(2)}) %copy-start) | copy-done | bytes 524312
  8.0 0.8 %copy-done.2 = bf16[128,256]{1,0:T(8,128)(2,1)S(1)} copy-done((bf16[128,256]{1,0:T(8,128)(2,1)S(1)}, bf16[128,256]{1,0:T(8,128)(2,1)}, u32[]{:S(2)}) %copy-start.2) | copy-done | bytes 65560
  8.8 0.2 prepare.1
  9.1 0.0 collective-permute-done.refs_4_
  9.1 0.0 copy-start.4
  9.1 0.1 collective-permute-start.4
  9.2 0.5 %collective-permute-start.1 = (bf16[128,256]{1,0:T(8,128)(2,1)S(1)}, bf16[128,256]{1,0:T(8,128)(2,1)S(1)}, u32[]{:S(2)}, u32[]{:S(2)}) collective-permute-start(bf16[128,256]{1,0:T(8,128)(2,1)S(1)} %copy-done.2), channel_id=1, source_target_pairs={{0,4},{4,0},{8,12},{12,8},{16,20},{20,16},{24,28},{28,24},{1,5},{5... | collective-permute-start | bytes 196616 | tf_op jit(solution)/shard_map/ppermute | solution.py:94
  9.7 1.5 %collective-permute-done.3.refs_6_ = bf16[128,256]{1,0:T(8,128)(2,1)S(1)} collective-permute-done((bf16[128,256]{1,0:T(8,128)(2,1)}, bf16[128,256]{1,0:T(8,128)(2,1)S(1)}, u32[]{:S(2)}, u32[]{:S(2)}) %collective-permute-start.3) | collective-permute-done | bytes 65568 | tf_op jit(solution)/shard_map/ppermute | solution.py:94
  11.2 0.1 collective-permute-done.2.refs_2_
  11.3 0.0 collective-permute-done.4.refs_5_
  11.3 0.0 collective-permute-start.5
  11.3 0.5 %collective-permute-start.6 = (bf16[128,256]{1,0:T(8,128)(2,1)S(1)}, bf16[128,256]{1,0:T(8,128)(2,1)S(1)}, u32[]{:S(2)}, u32[]{:S(2)}) collective-permute-start(bf16[128,256]{1,0:T(8,128)(2,1)S(1)} %collective-permute-done.3.refs_6_), channel_id=1, source_target_pairs={{0,4},{4,0},{8,12},{12,8},{16,20},{20,16},{24,28},{28,24},{1,5},{5... | collective-permute-start | bytes 196616 | tf_op jit(solution)/shard_map/ppermute | solution.py:94
  11.8 0.0 collective-permute-done.1.refs_1_
  11.8 0.7 %collective-permute-done.5.refs_3_ = bf16[128,256]{1,0:T(8,128)(2,1)S(1)} collective-permute-done((bf16[128,256]{1,0:T(8,128)(2,1)S(1)}, bf16[128,256]{1,0:T(8,128)(2,1)S(1)}, u32[]{:S(2)}, u32[]{:S(2)}) %collective-permute-start.5) | collective-permute-done | bytes 65568 | tf_op jit(solution)/shard_map/ppermute | solution.py:94
  12.5 0.2 collective-permute-done.6.refs_7_
  12.7 0.0 copy-done.4
  12.7 0.4 %partials.1 = (bf16[128,256]{1,0:T(8,128)(2,1)S(1)}, bf16[128,256]{1,0:T(8,128)(2,1)S(1)}, bf16[128,256]{1,0:T(8,128)(2,1)S(1)}, bf16[128,256]{1,0:T(8,128)(2,1)S(1)}) custom-call(s32[4,4]{1,0:T(4,128)S(1)} %bitcast.6, bf16[4,128,512]{2,1,0:T(8,128)(2,1)S(1)} %get-tuple-element.33.wide_ref, bf16[128,256]{1,0:T(8,128)(2,1)S(1)} %get-tuple-element.34.refs_0_, ...), custom_call_target="tpu_custom_call" | custom-call | tf_op jit(solution)/shard_map/partials/pallas_call | solution.py:82
  13.1 2.5 %collective-permute-start.7 = (bf16[128,256]{1,0:T(8,128)(2,1)S(1)}, bf16[128,256]{1,0:T(8,128)(2,1)S(1)}, u32[]{:S(2)}, u32[]{:S(2)}) collective-permute-start(bf16[128,256]{1,0:T(8,128)(2,1)S(1)} %get-tuple-element.40), channel_id=1, source_target_pairs={{0,3},{1,2},{2,1},{3,0},{4,7},{5,6},{6,5},{7,4},{8,11},{9,10},{10,... | collective-permute-start | bytes 196616 | tf_op jit(solution)/shard_map/ppermute | solution.py:94
  15.6 0.5 %collective-permute-start.8 = (bf16[128,256]{1,0:T(8,128)(2,1)S(1)}, bf16[128,256]{1,0:T(8,128)(2,1)S(1)}, u32[]{:S(2)}, u32[]{:S(2)}) collective-permute-start(bf16[128,256]{1,0:T(8,128)(2,1)S(1)} %get-tuple-element.41), channel_id=1, source_target_pairs={{0,2},{1,3},{2,0},{3,1},{4,6},{5,7},{6,4},{7,5},{8,10},{9,11},{10,... | collective-permute-start | bytes 196616 | tf_op jit(solution)/shard_map/ppermute | solution.py:94
  16.1 0.6 %collective-permute-start.9 = (bf16[128,256]{1,0:T(8,128)(2,1)S(1)}, bf16[128,256]{1,0:T(8,128)(2,1)S(1)}, u32[]{:S(2)}, u32[]{:S(2)}) collective-permute-start(bf16[128,256]{1,0:T(8,128)(2,1)S(1)} %get-tuple-element.42), channel_id=1, source_target_pairs={{0,1},{1,0},{2,3},{3,2},{4,5},{5,4},{6,7},{7,6},{8,9},{9,8},{10,11... | collective-permute-start | bytes 196616 | tf_op jit(solution)/shard_map/ppermute | solution.py:94
  16.7 1.8 %collective-permute-done.7.refs_1_ = bf16[128,256]{1,0:T(8,128)(2,1)S(1)} collective-permute-done((bf16[128,256]{1,0:T(8,128)(2,1)S(1)}, bf16[128,256]{1,0:T(8,128)(2,1)S(1)}, u32[]{:S(2)}, u32[]{:S(2)}) %collective-permute-start.7) | collective-permute-done | bytes 65568 | tf_op jit(solution)/shard_map/ppermute | solution.py:94
  18.4 1.5 %collective-permute-done.8.refs_2_ = bf16[128,256]{1,0:T(8,128)(2,1)S(1)} collective-permute-done((bf16[128,256]{1,0:T(8,128)(2,1)S(1)}, bf16[128,256]{1,0:T(8,128)(2,1)S(1)}, u32[]{:S(2)}, u32[]{:S(2)}) %collective-permute-start.8) | collective-permute-done | bytes 65568 | tf_op jit(solution)/shard_map/ppermute | solution.py:94
  19.9 0.5 %collective-permute-done.9.refs_3_ = bf16[128,256]{1,0:T(8,128)(2,1)S(1)} collective-permute-done((bf16[128,256]{1,0:T(8,128)(2,1)S(1)}, bf16[128,256]{1,0:T(8,128)(2,1)S(1)}, u32[]{:S(2)}, u32[]{:S(2)}) %collective-permute-start.9) | collective-permute-done | bytes 65568 | tf_op jit(solution)/shard_map/ppermute | solution.py:94
  20.4 0.4 %dense.1 = (bf16[128,256]{1,0:T(8,128)(2,1)S(1)}, f32[128,256]{1,0:T(8,128)S(1)}, bf16[256,256]{1,0:T(8,128)(2,1)S(1)}) custom-call(bf16[256,256]{1,0:T(8,128)(2,1)S(1)} %copy-done.1, bf16[128,256]{1,0:T(8,128)(2,1)S(1)} %copy-done.3, bf16[256,128]{1,0:T(8,128)(2,1)S(1)} %get-tuple-element.32.placing_ref, bf16[128,256]{1,0:T(8,128)(2,1)S(1)} %get-tuple-element.39.refs_0_, ...), custom_call_target="tpu_custom_call" | custom-call | tf_op jit(solution)/shard_map/dense/pallas_call | solution.py:126
  20.8 0.1 collective-permute-start.10
  20.9 1.3 %collective-permute-done.10.came_ref.refs_1_ = bf16[256,256]{1,0:T(8,128)(2,1)S(1)} collective-permute-done((bf16[256,256]{1,0:T(8,128)(2,1)S(1)}, bf16[256,256]{1,0:T(8,128)(2,1)S(1)}, u32[]{:S(2)}, u32[]{:S(2)}) %collective-permute-start.10) | collective-permute-done | bytes 131104 | tf_op jit(solution)/shard_map/ppermute | solution.py:94
  22.3 1.0 %collective-permute-start.11 = (bf16[192,256]{1,0:T(8,128)(2,1)S(1)}, bf16[192,256]{1,0:T(8,128)(2,1)S(1)}, u32[]{:S(2)}, u32[]{:S(2)}) collective-permute-start(bf16[192,256]{1,0:T(8,128)(2,1)S(1)} %get-tuple-element.47), channel_id=1, source_target_pairs={{0,8},{1,9},{2,10},{3,11},{4,7},{5,6},{6,5},{7,4},{8,16},{9,17},{1... | collective-permute-start | bytes 294920 | tf_op jit(solution)/shard_map/ppermute | solution.py:260
  23.3 3.4 %collective-permute-start.12 = (bf16[192,256]{1,0:T(8,128)(2,1)S(1)}, bf16[192,256]{1,0:T(8,128)(2,1)S(1)}, u32[]{:S(2)}, u32[]{:S(2)}) collective-permute-start(bf16[192,256]{1,0:T(8,128)(2,1)S(1)} %get-tuple-element.48), channel_id=1, source_target_pairs={{0,16},{1,17},{2,18},{3,19},{4,6},{5,7},{6,4},{7,5},{8,24},{9,25},... | collective-permute-start | bytes 294920 | tf_op jit(solution)/shard_map/ppermute | solution.py:260
  26.8 1.2 %collective-permute-start.13 = (bf16[192,256]{1,0:T(8,128)(2,1)S(1)}, bf16[192,256]{1,0:T(8,128)(2,1)S(1)}, u32[]{:S(2)}, u32[]{:S(2)}) collective-permute-start(bf16[192,256]{1,0:T(8,128)(2,1)S(1)} %get-tuple-element.49), channel_id=1, source_target_pairs={{0,24},{1,25},{2,26},{3,27},{4,5},{5,4},{6,7},{7,6},{8,0},{9,1},{1... | collective-permute-start | bytes 294920 | tf_op jit(solution)/shard_map/ppermute | solution.py:260
  27.9 0.9 %collective-permute-done.11.refs_0_ = bf16[192,256]{1,0:T(8,128)(2,1)S(1)} collective-permute-done((bf16[192,256]{1,0:T(8,128)(2,1)S(1)}, bf16[192,256]{1,0:T(8,128)(2,1)S(1)}, u32[]{:S(2)}, u32[]{:S(2)}) %collective-permute-start.11) | collective-permute-done | bytes 98336 | tf_op jit(solution)/shard_map/ppermute | solution.py:260
  28.8 2.2 %collective-permute-done.12.refs_1_ = bf16[192,256]{1,0:T(8,128)(2,1)S(1)} collective-permute-done((bf16[192,256]{1,0:T(8,128)(2,1)S(1)}, bf16[192,256]{1,0:T(8,128)(2,1)S(1)}, u32[]{:S(2)}, u32[]{:S(2)}) %collective-permute-start.12) | collective-permute-done | bytes 98336 | tf_op jit(solution)/shard_map/ppermute | solution.py:260
  31.0 0.6 %collective-permute-done.13.refs_2_ = bf16[192,256]{1,0:T(8,128)(2,1)S(1)} collective-permute-done((bf16[192,256]{1,0:T(8,128)(2,1)S(1)}, bf16[192,256]{1,0:T(8,128)(2,1)S(1)}, u32[]{:S(2)}, u32[]{:S(2)}) %collective-permute-start.13) | collective-permute-done | bytes 98336 | tf_op jit(solution)/shard_map/ppermute | solution.py:260
  31.6 0.1 second.1
  31.7 1.5 %collective-permute-start.14 = (bf16[192,256]{1,0:T(8,128)(2,1)S(1)}, bf16[192,256]{1,0:T(8,128)(2,1)S(1)}, u32[]{:S(2)}, u32[]{:S(2)}) collective-permute-start(bf16[192,256]{1,0:T(8,128)(2,1)S(1)} %get-tuple-element.51), channel_id=1, source_target_pairs={{0,3},{1,2},{2,1},{3,0},{4,12},{5,13},{6,14},{7,15},{8,11},{9,10},... | collective-permute-start | bytes 294920 | tf_op jit(solution)/shard_map/ppermute | solution.py:260
  33.2 1.0 %collective-permute-start.15 = (bf16[192,256]{1,0:T(8,128)(2,1)S(1)}, bf16[192,256]{1,0:T(8,128)(2,1)S(1)}, u32[]{:S(2)}, u32[]{:S(2)}) collective-permute-start(bf16[192,256]{1,0:T(8,128)(2,1)S(1)} %get-tuple-element.52), channel_id=1, source_target_pairs={{0,2},{1,3},{2,0},{3,1},{4,20},{5,21},{6,22},{7,23},{8,10},{9,11},... | collective-permute-start | bytes 294920 | tf_op jit(solution)/shard_map/ppermute | solution.py:260
  34.2 1.1 %collective-permute-start.16 = (bf16[192,256]{1,0:T(8,128)(2,1)S(1)}, bf16[192,256]{1,0:T(8,128)(2,1)S(1)}, u32[]{:S(2)}, u32[]{:S(2)}) collective-permute-start(bf16[192,256]{1,0:T(8,128)(2,1)S(1)} %get-tuple-element.53), channel_id=1, source_target_pairs={{0,1},{1,0},{2,3},{3,2},{4,28},{5,29},{6,30},{7,31},{8,9},{9,8},{1... | collective-permute-start | bytes 294920 | tf_op jit(solution)/shard_map/ppermute | solution.py:260
  35.3 0.7 %store.2._ = bf16[8,32,256]{2,1,0:T(8,128)(2,1)} custom-call(bf16[128,256]{1,0:T(8,128)(2,1)S(1)} %get-tuple-element.43.same_ref.refs_0_, bf16[256,256]{1,0:T(8,128)(2,1)S(1)} %collective-permute-done.10.came_ref.refs_1_, bf16[192,256]{1,0:T(8,128)(2,1)S(1)} %collective-permute-done.11.refs_0_, bf16[192,256]{1,0:T(8,128)(2,1)S(1)} %collective-permute-done.12.refs_1_, ...), custom_call_target="tpu_custom_call" | custom-call | tf_op jit(solution)/shard_map/store/pallas_call | solution.py:223
  35.9 1.4 %collective-permute-done.14.refs_0_.refs_2_ = bf16[192,256]{1,0:T(8,128)(2,1)S(1)} collective-permute-done((bf16[192,256]{1,0:T(8,128)(2,1)S(1)}, bf16[192,256]{1,0:T(8,128)(2,1)S(1)}, u32[]{:S(2)}, u32[]{:S(2)}) %collective-permute-start.14) | collective-permute-done | bytes 98336 | tf_op jit(solution)/shard_map/ppermute | solution.py:260
  37.3 1.0 %collective-permute-done.15.refs_1_.refs_3_ = bf16[192,256]{1,0:T(8,128)(2,1)S(1)} collective-permute-done((bf16[192,256]{1,0:T(8,128)(2,1)S(1)}, bf16[192,256]{1,0:T(8,128)(2,1)S(1)}, u32[]{:S(2)}, u32[]{:S(2)}) %collective-permute-start.15) | collective-permute-done | bytes 98336 | tf_op jit(solution)/shard_map/ppermute | solution.py:260
  38.3 0.4 %collective-permute-done.16.refs_2_.refs_4_ = bf16[192,256]{1,0:T(8,128)(2,1)S(1)} collective-permute-done((bf16[192,256]{1,0:T(8,128)(2,1)S(1)}, bf16[192,256]{1,0:T(8,128)(2,1)S(1)}, u32[]{:S(2)}, u32[]{:S(2)}) %collective-permute-start.16) | collective-permute-done | bytes 98336 | tf_op jit(solution)/shard_map/ppermute | solution.py:260
  38.8 0.1 third.1.own_ref
  38.9 0.1 collective-permute-start.17
  38.9 1.2 %collective-permute-done.17.came_ref = bf16[128,256]{1,0:T(8,128)(2,1)S(1)} collective-permute-done((bf16[128,256]{1,0:T(8,128)(2,1)S(1)}, bf16[128,256]{1,0:T(8,128)(2,1)S(1)}, u32[]{:S(2)}, u32[]{:S(2)}) %collective-permute-start.17) | collective-permute-done | bytes 65568 | tf_op jit(solution)/shard_map/ppermute | solution.py:94
  40.2 0.7 %finish.1 = f32[2,128,256]{2,1,0:T(8,128)} custom-call(bf16[128,256]{1,0:T(8,128)(2,1)S(1)} %third.1.own_ref, bf16[128,256]{1,0:T(8,128)(2,1)S(1)} %collective-permute-done.17.came_ref), custom_call_target="tpu_custom_call" | custom-call | tf_op jit(solution)/shard_map/finish/pallas_call | solution.py:242
  (9 shorter events, 0.1 us)
Async XLA Ops:
  0.6 8.4 %collective-permute-start = (bf16[128,256]{1,0:T(8,128)(2,1)}, bf16[128,256]{1,0:T(8,128)(2,1)S(1)}, u32[]{:S(2)}, u32[]{:S(2)}) collective-permute-start(bf16[128,256]{1,0:T(8,128)(2,1)} %own_ref.1), channel_id=1, source_target_pairs={{0,16},{4,20},{8,24},{12,28},{16,0},{20,4},{24,8},{28,12},{1,17},{... | collective-permute-start | bytes 196616 | tf_op jit(solution)/shard_map/ppermute | solution.py:94
  4.7 6.4 %collective-permute-start.3 = (bf16[128,256]{1,0:T(8,128)(2,1)}, bf16[128,256]{1,0:T(8,128)(2,1)S(1)}, u32[]{:S(2)}, u32[]{:S(2)}) collective-permute-start(bf16[128,256]{1,0:T(8,128)(2,1)} %own_ref.1), channel_id=1, source_target_pairs={{0,24},{4,28},{8,16},{12,20},{16,8},{20,12},{24,0},{28,4},{1,25},{... | collective-permute-start | bytes 196616 | tf_op jit(solution)/shard_map/ppermute | solution.py:94
  6.1 5.2 %collective-permute-start.2 = (bf16[128,256]{1,0:T(8,128)(2,1)}, bf16[128,256]{1,0:T(8,128)(2,1)S(1)}, u32[]{:S(2)}, u32[]{:S(2)}) collective-permute-start(bf16[128,256]{1,0:T(8,128)(2,1)} %own_ref.1), channel_id=1, source_target_pairs={{0,8},{4,12},{8,0},{12,4},{16,24},{20,28},{24,16},{28,20},{1,9},{5... | collective-permute-start | bytes 196616 | tf_op jit(solution)/shard_map/ppermute | solution.py:94
  6.3 0.7 %copy-start.5 = (s32[128,1]{0,1:T(1,128)S(1)}, s32[128,1]{0,1:T(1,128)}, u32[]{:S(2)}) copy-start(s32[128,1]{0,1:T(1,128)} %param.11) | copy-start | bytes 1540
  7.0 1.0 %copy-start = (bf16[4,1,4,128,128]{4,3,2,1,0:T(8,128)(2,1)S(1)}, bf16[4,1,4,128,128]{4,3,2,1,0:T(8,128)(2,1)}, u32[]{:S(2)}) copy-start(bf16[4,1,4,128,128]{4,3,2,1,0:T(8,128)(2,1)} %param.7) | copy-start | bytes 1572868
  8.0 0.8 %copy-start.2 = (bf16[128,256]{1,0:T(8,128)(2,1)S(1)}, bf16[128,256]{1,0:T(8,128)(2,1)}, u32[]{:S(2)}) copy-start(bf16[128,256]{1,0:T(8,128)(2,1)} %own_ref.1) | copy-start | bytes 196612
  9.1 3.6 %copy-start.4 = (s32[4,1,4]{2,1,0:T(1,128)S(1)}, s32[4,1,4]{2,1,0:T(1,128)}, u32[]{:S(2)}) copy-start(s32[4,1,4]{2,1,0:T(1,128)} %param.8) | copy-start | bytes 196
  9.1 2.2 %collective-permute-start.4 = (bf16[128,256]{1,0:T(8,128)(2,1)S(1)}, bf16[128,256]{1,0:T(8,128)(2,1)S(1)}, u32[]{:S(2)}, u32[]{:S(2)}) collective-permute-start(bf16[128,256]{1,0:T(8,128)(2,1)S(1)} %collective-permute-done.refs_4_), channel_id=1, source_target_pairs={{0,4},{4,0},{8,12},{12,8},{16,20},{20,16},{24,28},{28,24},{1,5},{5... | collective-permute-start | bytes 196616 | tf_op jit(solution)/shard_map/ppermute | solution.py:94
  9.2 2.6 %collective-permute-start.1 = (bf16[128,256]{1,0:T(8,128)(2,1)S(1)}, bf16[128,256]{1,0:T(8,128)(2,1)S(1)}, u32[]{:S(2)}, u32[]{:S(2)}) collective-permute-start(bf16[128,256]{1,0:T(8,128)(2,1)S(1)} %copy-done.2), channel_id=1, source_target_pairs={{0,4},{4,0},{8,12},{12,8},{16,20},{20,16},{24,28},{28,24},{1,5},{5... | collective-permute-start | bytes 196616 | tf_op jit(solution)/shard_map/ppermute | solution.py:94
  11.3 1.3 %collective-permute-start.5 = (bf16[128,256]{1,0:T(8,128)(2,1)S(1)}, bf16[128,256]{1,0:T(8,128)(2,1)S(1)}, u32[]{:S(2)}, u32[]{:S(2)}) collective-permute-start(bf16[128,256]{1,0:T(8,128)(2,1)S(1)} %collective-permute-done.2.refs_2_), channel_id=1, source_target_pairs={{0,4},{4,0},{8,12},{12,8},{16,20},{20,16},{24,28},{28,24},{1,5},{5... | collective-permute-start | bytes 196616 | tf_op jit(solution)/shard_map/ppermute | solution.py:94
  11.3 1.4 %collective-permute-start.6 = (bf16[128,256]{1,0:T(8,128)(2,1)S(1)}, bf16[128,256]{1,0:T(8,128)(2,1)S(1)}, u32[]{:S(2)}, u32[]{:S(2)}) collective-permute-start(bf16[128,256]{1,0:T(8,128)(2,1)S(1)} %collective-permute-done.3.refs_6_), channel_id=1, source_target_pairs={{0,4},{4,0},{8,12},{12,8},{16,20},{20,16},{24,28},{28,24},{1,5},{5... | collective-permute-start | bytes 196616 | tf_op jit(solution)/shard_map/ppermute | solution.py:94
  12.7 7.7 %copy-start.1 = (bf16[256,256]{1,0:T(8,128)(2,1)S(1)}, bf16[256,256]{1,0:T(8,128)(2,1)}, u32[]{:S(2)}) copy-start(bf16[256,256]{1,0:T(8,128)(2,1)} %weight_ref.1) | copy-start | bytes 393220
  12.7 7.7 %copy-start.3 = (bf16[128,256]{1,0:T(8,128)(2,1)S(1)}, bf16[128,256]{1,0:T(8,128)(2,1)}, u32[]{:S(2)}) copy-start(bf16[128,256]{1,0:T(8,128)(2,1)} %cot_ref.1) | copy-start | bytes 196612
  13.1 5.3 %collective-permute-start.7 = (bf16[128,256]{1,0:T(8,128)(2,1)S(1)}, bf16[128,256]{1,0:T(8,128)(2,1)S(1)}, u32[]{:S(2)}, u32[]{:S(2)}) collective-permute-start(bf16[128,256]{1,0:T(8,128)(2,1)S(1)} %get-tuple-element.40), channel_id=1, source_target_pairs={{0,3},{1,2},{2,1},{3,0},{4,7},{5,6},{6,5},{7,4},{8,11},{9,10},{10,... | collective-permute-start | bytes 196616 | tf_op jit(solution)/shard_map/ppermute | solution.py:94
  15.6 4.3 %collective-permute-start.8 = (bf16[128,256]{1,0:T(8,128)(2,1)S(1)}, bf16[128,256]{1,0:T(8,128)(2,1)S(1)}, u32[]{:S(2)}, u32[]{:S(2)}) collective-permute-start(bf16[128,256]{1,0:T(8,128)(2,1)S(1)} %get-tuple-element.41), channel_id=1, source_target_pairs={{0,2},{1,3},{2,0},{3,1},{4,6},{5,7},{6,4},{7,5},{8,10},{9,11},{10,... | collective-permute-start | bytes 196616 | tf_op jit(solution)/shard_map/ppermute | solution.py:94
  16.1 4.3 %collective-permute-start.9 = (bf16[128,256]{1,0:T(8,128)(2,1)S(1)}, bf16[128,256]{1,0:T(8,128)(2,1)S(1)}, u32[]{:S(2)}, u32[]{:S(2)}) collective-permute-start(bf16[128,256]{1,0:T(8,128)(2,1)S(1)} %get-tuple-element.42), channel_id=1, source_target_pairs={{0,1},{1,0},{2,3},{3,2},{4,5},{5,4},{6,7},{7,6},{8,9},{9,8},{10,11... | collective-permute-start | bytes 196616 | tf_op jit(solution)/shard_map/ppermute | solution.py:94
  20.8 1.4 %collective-permute-start.10 = (bf16[256,256]{1,0:T(8,128)(2,1)S(1)}, bf16[256,256]{1,0:T(8,128)(2,1)S(1)}, u32[]{:S(2)}, u32[]{:S(2)}) collective-permute-start(bf16[256,256]{1,0:T(8,128)(2,1)S(1)} %get-tuple-element.44), channel_id=1, source_target_pairs={{0,4},{4,0},{8,12},{12,8},{16,20},{20,16},{24,28},{28,24},{1,5},{5... | collective-permute-start | bytes 393224 | tf_op jit(solution)/shard_map/ppermute | solution.py:94
  22.3 6.5 %collective-permute-start.11 = (bf16[192,256]{1,0:T(8,128)(2,1)S(1)}, bf16[192,256]{1,0:T(8,128)(2,1)S(1)}, u32[]{:S(2)}, u32[]{:S(2)}) collective-permute-start(bf16[192,256]{1,0:T(8,128)(2,1)S(1)} %get-tuple-element.47), channel_id=1, source_target_pairs={{0,8},{1,9},{2,10},{3,11},{4,7},{5,6},{6,5},{7,4},{8,16},{9,17},{1... | collective-permute-start | bytes 294920 | tf_op jit(solution)/shard_map/ppermute | solution.py:260
  23.3 7.7 %collective-permute-start.12 = (bf16[192,256]{1,0:T(8,128)(2,1)S(1)}, bf16[192,256]{1,0:T(8,128)(2,1)S(1)}, u32[]{:S(2)}, u32[]{:S(2)}) collective-permute-start(bf16[192,256]{1,0:T(8,128)(2,1)S(1)} %get-tuple-element.48), channel_id=1, source_target_pairs={{0,16},{1,17},{2,18},{3,19},{4,6},{5,7},{6,4},{7,5},{8,24},{9,25},... | collective-permute-start | bytes 294920 | tf_op jit(solution)/shard_map/ppermute | solution.py:260
  26.8 4.9 %collective-permute-start.13 = (bf16[192,256]{1,0:T(8,128)(2,1)S(1)}, bf16[192,256]{1,0:T(8,128)(2,1)S(1)}, u32[]{:S(2)}, u32[]{:S(2)}) collective-permute-start(bf16[192,256]{1,0:T(8,128)(2,1)S(1)} %get-tuple-element.49), channel_id=1, source_target_pairs={{0,24},{1,25},{2,26},{3,27},{4,5},{5,4},{6,7},{7,6},{8,0},{9,1},{1... | collective-permute-start | bytes 294920 | tf_op jit(solution)/shard_map/ppermute | solution.py:260
  31.7 5.6 %collective-permute-start.14 = (bf16[192,256]{1,0:T(8,128)(2,1)S(1)}, bf16[192,256]{1,0:T(8,128)(2,1)S(1)}, u32[]{:S(2)}, u32[]{:S(2)}) collective-permute-start(bf16[192,256]{1,0:T(8,128)(2,1)S(1)} %get-tuple-element.51), channel_id=1, source_target_pairs={{0,3},{1,2},{2,1},{3,0},{4,12},{5,13},{6,14},{7,15},{8,11},{9,10},... | collective-permute-start | bytes 294920 | tf_op jit(solution)/shard_map/ppermute | solution.py:260
  33.2 5.1 %collective-permute-start.15 = (bf16[192,256]{1,0:T(8,128)(2,1)S(1)}, bf16[192,256]{1,0:T(8,128)(2,1)S(1)}, u32[]{:S(2)}, u32[]{:S(2)}) collective-permute-start(bf16[192,256]{1,0:T(8,128)(2,1)S(1)} %get-tuple-element.52), channel_id=1, source_target_pairs={{0,2},{1,3},{2,0},{3,1},{4,20},{5,21},{6,22},{7,23},{8,10},{9,11},... | collective-permute-start | bytes 294920 | tf_op jit(solution)/shard_map/ppermute | solution.py:260
  34.2 4.6 %collective-permute-start.16 = (bf16[192,256]{1,0:T(8,128)(2,1)S(1)}, bf16[192,256]{1,0:T(8,128)(2,1)S(1)}, u32[]{:S(2)}, u32[]{:S(2)}) collective-permute-start(bf16[192,256]{1,0:T(8,128)(2,1)S(1)} %get-tuple-element.53), channel_id=1, source_target_pairs={{0,1},{1,0},{2,3},{3,2},{4,28},{5,29},{6,30},{7,31},{8,9},{9,8},{1... | collective-permute-start | bytes 294920 | tf_op jit(solution)/shard_map/ppermute | solution.py:260
  38.9 1.3 %collective-permute-start.17 = (bf16[128,256]{1,0:T(8,128)(2,1)S(1)}, bf16[128,256]{1,0:T(8,128)(2,1)S(1)}, u32[]{:S(2)}, u32[]{:S(2)}) collective-permute-start(bf16[128,256]{1,0:T(8,128)(2,1)S(1)} %third.1.own_ref), channel_id=1, source_target_pairs={{0,4},{4,0},{8,12},{12,8},{16,20},{20,16},{24,28},{28,24},{1,5},{5... | collective-permute-start | bytes 196616 | tf_op jit(solution)/shard_map/ppermute | solution.py:94

commit v21 on v18

--- a/solution.py
+++ b/solution.py
@@ -66,11 +66,12 @@
     block_refs, out_refs, held = refs[:count], refs[count:-1], refs[-1]
     depth = src_ref.shape[1]
     section, rep = lax.axis_index("section"), lax.axis_index("rep")
-    for j in range(count):
-        held[j] = block_refs[j][...]
+    chip, chips = place_of_chip()
+    for i, ref in enumerate(block_refs):
+        held[2 * ((chip + chips - i % chips) % chips) + ((section + i // chips) & 1)] = ref[...]
     for j, out_ref in zip([0] + across(len(out_refs)), out_refs):
         g = rep ^ j
-        right = jnp.concatenate([held[src_ref[g, k] ^ section] for k in range(depth)], axis=0)
+        right = jnp.concatenate([held[src_ref[g, k]] for k in range(depth)], axis=0)
         out_ref[...] = jnp.dot(wide_ref[g], right, preferred_element_type=jnp.float32).astype(
             jnp.bfloat16
         )
@@ -260,17 +261,18 @@
     return lax.ppermute(value, ("section", "rep"), pairs)
 
 
+def send_along(value, axis, shift):
+    n = lax.axis_size(axis)
+    return lax.ppermute(value, axis, [(s, (s + 2 * shift) % n) for s in range(n)])
+
+
 def gather_blocks(features, axis, ready):
-    n = lax.axis_size(axis)
-    blocks = [None] * n
-    blocks[0] = features
-    for j in range(2, n, 2):
-        blocks[j] = swap(features, axis, j)
-    blocks[1] = swap(features, axis, 1)
-    blocks[2::2], ready = lax.optimization_barrier((blocks[2::2], ready))
-    for j in range(2, n, 2):
-        blocks[j + 1] = swap(blocks[j], axis, 1)
-    return blocks, ready
+    chips = lax.axis_size(axis) // 2
+    near = [features] + [send_along(features, axis, i) for i in range(1, chips)]
+    beside = swap(features, axis, 1)
+    came, ready = lax.optimization_barrier((near[:0:-1], ready))
+    near[1:] = came[::-1]
+    return near, [beside] + [swap(block, axis, 1) for block in near[1:]], ready
 
 
 def per_device(features, adj_tiles, adj_src, cotangent, weight, destination):
@@ -280,8 +282,8 @@
     slots = max(2, 2 * rows_here // n_section)
     target = destination.reshape(1, rows_here)
     wide, own, placing = prepare(adj_tiles[:, 0], features, target, n_section * slots, slots)
-    blocks, (wide, own, placing) = gather_blocks(features, "section", (wide, own, placing))
-    parts = list(partials(adj_src[:, 0], wide, [own] + blocks[1:]))
+    near, beside, (wide, own, placing) = gather_blocks(features, "section", (wide, own, placing))
+    parts = list(partials(adj_src[:, 0], wide, [own] + near[1:] + beside))
     others = across(n_rep)
     parts = parts[:1] + [swap(part, "rep", j) for part, j in zip(parts[1:], others)]
     same, kept, sent = dense(parts, weight, cotangent, placing)

time: 41.2 us -> 41.2 us (level)
  starting transfers between devices: 18.1 us -> 18.8 us
  waiting for transfers between devices: 16.9 us -> 16.2 us
    ppermute x0 -> x3, starting transfers between devices: none -> 7.01 us  [send_along(): lax.ppermute(value, axis, [(s, (s + 2 * shift) % n) for s in range(n)])]
    ppermute x12 -> x9, starting transfers between devices: 10 us -> 4.21 us  [swap(): lax.ppermute(value, axis, [(i, i ^ j) for i in range(lax.axis_size(axis))])]
    ppermute x12 -> x9, waiting for transfers between devices: 9.88 us -> 7.59 us  [swap(): lax.ppermute(value, axis, [(i, i ^ j) for i in range(lax.axis_size(axis))])]
    ppermute x0 -> x3, waiting for transfers between devices: none -> 0.8 us  [send_along(): lax.ppermute(value, axis, [(s, (s + 2 * shift) % n) for s in range(n)])]
    ppermute x6, waiting for transfers between devices: 7.04 us -> 7.84 us  [exchange(): return lax.ppermute(value, ('section', 'rep'), pairs)]
    ppermute x6, starting transfers between devices: 8.09 us -> 7.58 us  [exchange(): return lax.ppermute(value, ('section', 'rep'), pairs)]
  transfers between devices with their start and end apart: 18 -> 18, of which waited for: 15 -> 16; matrix products, arithmetic and copies ran while one was open for 0% -> 0% of each run, Pallas kernels for 2% -> 2%
where the time goes in v21:
time: 41.2 us; the launch traced here: 41 us
  starting transfers between devices  18.8 us (46%)
  waiting for transfers between devices  16.2 us (39%)
  Pallas kernels  2.66 us (6%)
  local copies, waits for them, and re-layouts  2.55 us (6%)
  between operations  0.73 us (2%)
    ppermute x6, waiting for transfers between devices, exchange(): return lax.ppermute(value, ('section', 'rep'), pairs)  7.84 us
    ppermute x9, waiting for transfers between devices, swap(): lax.ppermute(value, axis, [(i, i ^ j) for i in range(lax.axis_size(axis))])  7.59 us
    ppermute x6, starting transfers between devices, exchange(): return lax.ppermute(value, ('section', 'rep'), pairs)  7.58 us
    ppermute x3, starting transfers between devices, send_along(): lax.ppermute(value, axis, [(s, (s + 2 * shift) % n) for s in range(n)])  7.01 us
    ppermute x9, starting transfers between devices, swap(): lax.ppermute(value, axis, [(i, i ^ j) for i in range(lax.axis_size(axis))])  4.21 us
    unnamed x12, local copies, waits for them, and re-layouts  2.55 us
  transfers between devices with their start and end apart: 18, of which 16 were waited for; matrix products, arithmetic and copies ran while one was open for 0% of the time, Pallas kernels for 2%

profile of v21, /device:TPU:0, one launch (start us, length us, event | category | flops | bytes accessed | tf_op | source)
XLA Modules:
  0.0 41.0 jit_solution(14640622911838849429)
XLA Ops:
  0.6 3.1 %collective-permute-start.2 = (bf16[128,256]{1,0:T(8,128)(2,1)}, bf16[128,256]{1,0:T(8,128)(2,1)S(1)}, u32[]{:S(2)}, u32[]{:S(2)}) collective-permute-start(bf16[128,256]{1,0:T(8,128)(2,1)} %own_ref.1), channel_id=1, source_target_pairs={{0,8},{4,12},{8,16},{12,20},{16,24},{20,28},{24,0},{28,4},{1,9},{5... | collective-permute-start | bytes 196616 | tf_op jit(solution)/shard_map/ppermute | solution.py:266
  3.7 2.6 %collective-permute-start.1 = (bf16[128,256]{1,0:T(8,128)(2,1)}, bf16[128,256]{1,0:T(8,128)(2,1)S(1)}, u32[]{:S(2)}, u32[]{:S(2)}) collective-permute-start(bf16[128,256]{1,0:T(8,128)(2,1)} %own_ref.1), channel_id=1, source_target_pairs={{0,16},{4,20},{8,24},{12,28},{16,0},{20,4},{24,8},{28,12},{1,17},{... | collective-permute-start | bytes 196616 | tf_op jit(solution)/shard_map/ppermute | solution.py:266
  6.3 1.3 %collective-permute-start = (bf16[128,256]{1,0:T(8,128)(2,1)}, bf16[128,256]{1,0:T(8,128)(2,1)S(1)}, u32[]{:S(2)}, u32[]{:S(2)}) collective-permute-start(bf16[128,256]{1,0:T(8,128)(2,1)} %own_ref.1), channel_id=1, source_target_pairs={{0,24},{4,28},{8,0},{12,4},{16,8},{20,12},{24,16},{28,20},{1,25},{... | collective-permute-start | bytes 196616 | tf_op jit(solution)/shard_map/ppermute | solution.py:266
  7.6 0.0 collective-permute-start.3
  7.7 0.7 %copy-done.5 = s32[128,1]{0,1:T(1,128)S(1)} copy-done((s32[128,1]{0,1:T(1,128)S(1)}, s32[128,1]{0,1:T(1,128)}, u32[]{:S(2)}) %copy-start.5) | copy-done | bytes 536
  8.3 1.0 %copy-done = bf16[4,1,4,128,128]{4,3,2,1,0:T(8,128)(2,1)S(1)} copy-done((bf16[4,1,4,128,128]{4,3,2,1,0:T(8,128)(2,1)S(1)}, bf16[4,1,4,128,128]{4,3,2,1,0:T(8,128)(2,1)}, u32[]{:S(2)}) %copy-start) | copy-done | bytes 524312
  9.3 0.8 %copy-done.2 = bf16[128,256]{1,0:T(8,128)(2,1)S(1)} copy-done((bf16[128,256]{1,0:T(8,128)(2,1)S(1)}, bf16[128,256]{1,0:T(8,128)(2,1)}, u32[]{:S(2)}) %copy-start.2) | copy-done | bytes 65560
  10.2 0.2 prepare.1
  10.4 0.0 collective-permute-done.2.refs_1_
  10.4 0.6 %collective-permute-done.1.refs_2_ = bf16[128,256]{1,0:T(8,128)(2,1)S(1)} collective-permute-done((bf16[128,256]{1,0:T(8,128)(2,1)}, bf16[128,256]{1,0:T(8,128)(2,1)S(1)}, u32[]{:S(2)}, u32[]{:S(2)}) %collective-permute-start.1) | collective-permute-done | bytes 65568 | tf_op jit(solution)/shard_map/ppermute | solution.py:266
  11.0 0.2 collective-permute-done.refs_3_
  11.2 0.0 collective-permute-start.4
  11.2 0.5 %collective-permute-start.5 = (bf16[128,256]{1,0:T(8,128)(2,1)S(1)}, bf16[128,256]{1,0:T(8,128)(2,1)S(1)}, u32[]{:S(2)}, u32[]{:S(2)}) collective-permute-start(bf16[128,256]{1,0:T(8,128)(2,1)S(1)} %collective-permute-done.1.refs_2_), channel_id=1, source_target_pairs={{0,4},{4,0},{8,12},{12,8},{16,20},{20,16},{24,28},{28,24},{1,5},{5... | collective-permute-start | bytes 196616 | tf_op jit(solution)/shard_map/ppermute | solution.py:95
  11.7 0.0 collective-permute-start.6
  11.7 0.0 collective-permute-done.3.refs_4_
  11.7 0.7 %collective-permute-done.4.refs_5_ = bf16[128,256]{1,0:T(8,128)(2,1)S(1)} collective-permute-done((bf16[128,256]{1,0:T(8,128)(2,1)S(1)}, bf16[128,256]{1,0:T(8,128)(2,1)S(1)}, u32[]{:S(2)}, u32[]{:S(2)}) %collective-permute-start.4) | collective-permute-done | bytes 65568 | tf_op jit(solution)/shard_map/ppermute | solution.py:95
  12.5 0.2 collective-permute-done.5.refs_6_
  12.6 0.4 collective-permute-done.6.refs_7_
  13.0 0.0 copy-done.4
  13.0 0.4 %partials.1 = (bf16[128,256]{1,0:T(8,128)(2,1)S(1)}, bf16[128,256]{1,0:T(8,128)(2,1)S(1)}, bf16[128,256]{1,0:T(8,128)(2,1)S(1)}, bf16[128,256]{1,0:T(8,128)(2,1)S(1)}) custom-call(s32[4,4]{1,0:T(4,128)S(1)} %bitcast.6, bf16[4,128,512]{2,1,0:T(8,128)(2,1)S(1)} %get-tuple-element.32.wide_ref, bf16[128,256]{1,0:T(8,128)(2,1)S(1)} %get-tuple-element.33.refs_0_, ...), custom_call_target="tpu_custom_call" | custom-call | tf_op jit(solution)/shard_map/partials/pallas_call | solution.py:83
  13.4 2.5 %collective-permute-start.7 = (bf16[128,256]{1,0:T(8,128)(2,1)S(1)}, bf16[128,256]{1,0:T(8,128)(2,1)S(1)}, u32[]{:S(2)}, u32[]{:S(2)}) collective-permute-start(bf16[128,256]{1,0:T(8,128)(2,1)S(1)} %get-tuple-element.38), channel_id=1, source_target_pairs={{0,3},{1,2},{2,1},{3,0},{4,7},{5,6},{6,5},{7,4},{8,11},{9,10},{10,... | collective-permute-start | bytes 196616 | tf_op jit(solution)/shard_map/ppermute | solution.py:95
  16.0 0.5 %collective-permute-start.8 = (bf16[128,256]{1,0:T(8,128)(2,1)S(1)}, bf16[128,256]{1,0:T(8,128)(2,1)S(1)}, u32[]{:S(2)}, u32[]{:S(2)}) collective-permute-start(bf16[128,256]{1,0:T(8,128)(2,1)S(1)} %get-tuple-element.39), channel_id=1, source_target_pairs={{0,2},{1,3},{2,0},{3,1},{4,6},{5,7},{6,4},{7,5},{8,10},{9,11},{10,... | collective-permute-start | bytes 196616 | tf_op jit(solution)/shard_map/ppermute | solution.py:95
  16.5 0.5 %collective-permute-start.9 = (bf16[128,256]{1,0:T(8,128)(2,1)S(1)}, bf16[128,256]{1,0:T(8,128)(2,1)S(1)}, u32[]{:S(2)}, u32[]{:S(2)}) collective-permute-start(bf16[128,256]{1,0:T(8,128)(2,1)S(1)} %get-tuple-element.40), channel_id=1, source_target_pairs={{0,1},{1,0},{2,3},{3,2},{4,5},{5,4},{6,7},{7,6},{8,9},{9,8},{10,11... | collective-permute-start | bytes 196616 | tf_op jit(solution)/shard_map/ppermute | solution.py:95
  17.0 1.7 %collective-permute-done.7.refs_1_ = bf16[128,256]{1,0:T(8,128)(2,1)S(1)} collective-permute-done((bf16[128,256]{1,0:T(8,128)(2,1)S(1)}, bf16[128,256]{1,0:T(8,128)(2,1)S(1)}, u32[]{:S(2)}, u32[]{:S(2)}) %collective-permute-start.7) | collective-permute-done | bytes 65568 | tf_op jit(solution)/shard_map/ppermute | solution.py:95
  18.7 1.6 %collective-permute-done.8.refs_2_ = bf16[128,256]{1,0:T(8,128)(2,1)S(1)} collective-permute-done((bf16[128,256]{1,0:T(8,128)(2,1)S(1)}, bf16[128,256]{1,0:T(8,128)(2,1)S(1)}, u32[]{:S(2)}, u32[]{:S(2)}) %collective-permute-start.8) | collective-permute-done | bytes 65568 | tf_op jit(solution)/shard_map/ppermute | solution.py:95
  20.2 0.5 %collective-permute-done.9.refs_3_ = bf16[128,256]{1,0:T(8,128)(2,1)S(1)} collective-permute-done((bf16[128,256]{1,0:T(8,128)(2,1)S(1)}, bf16[128,256]{1,0:T(8,128)(2,1)S(1)}, u32[]{:S(2)}, u32[]{:S(2)}) %collective-permute-start.9) | collective-permute-done | bytes 65568 | tf_op jit(solution)/shard_map/ppermute | solution.py:95
  20.7 0.0 copy-done.1
  20.8 0.4 %dense.1 = (bf16[128,256]{1,0:T(8,128)(2,1)S(1)}, f32[128,256]{1,0:T(8,128)S(1)}, bf16[256,256]{1,0:T(8,128)(2,1)S(1)}) custom-call(bf16[256,256]{1,0:T(8,128)(2,1)S(1)} %copy-done.1, bf16[128,256]{1,0:T(8,128)(2,1)S(1)} %copy-done.3, bf16[256,128]{1,0:T(8,128)(2,1)S(1)} %get-tuple-element.31.placing_ref, bf16[128,256]{1,0:T(8,128)(2,1)S(1)} %get-tuple-element.37.refs_0_, ...), custom_call_target="tpu_custom_call" | custom-call | tf_op jit(solution)/shard_map/dense/pallas_call | solution.py:127
  21.2 0.1 collective-permute-start.10
  21.3 1.3 %collective-permute-done.10.came_ref.refs_1_ = bf16[256,256]{1,0:T(8,128)(2,1)S(1)} collective-permute-done((bf16[256,256]{1,0:T(8,128)(2,1)S(1)}, bf16[256,256]{1,0:T(8,128)(2,1)S(1)}, u32[]{:S(2)}, u32[]{:S(2)}) %collective-permute-start.10) | collective-permute-done | bytes 131104 | tf_op jit(solution)/shard_map/ppermute | solution.py:95
  22.6 1.6 %collective-permute-start.11 = (bf16[192,256]{1,0:T(8,128)(2,1)S(1)}, bf16[192,256]{1,0:T(8,128)(2,1)S(1)}, u32[]{:S(2)}, u32[]{:S(2)}) collective-permute-start(bf16[192,256]{1,0:T(8,128)(2,1)S(1)} %get-tuple-element.45), channel_id=1, source_target_pairs={{0,8},{1,9},{2,10},{3,11},{4,7},{5,6},{6,5},{7,4},{8,16},{9,17},{1... | collective-permute-start | bytes 294920 | tf_op jit(solution)/shard_map/ppermute | solution.py:261
  24.3 2.0 %collective-permute-start.12 = (bf16[192,256]{1,0:T(8,128)(2,1)S(1)}, bf16[192,256]{1,0:T(8,128)(2,1)S(1)}, u32[]{:S(2)}, u32[]{:S(2)}) collective-permute-start(bf16[192,256]{1,0:T(8,128)(2,1)S(1)} %get-tuple-element.46), channel_id=1, source_target_pairs={{0,16},{1,17},{2,18},{3,19},{4,6},{5,7},{6,4},{7,5},{8,24},{9,25},... | collective-permute-start | bytes 294920 | tf_op jit(solution)/shard_map/ppermute | solution.py:261
  26.3 0.4 %collective-permute-start.13 = (bf16[192,256]{1,0:T(8,128)(2,1)S(1)}, bf16[192,256]{1,0:T(8,128)(2,1)S(1)}, u32[]{:S(2)}, u32[]{:S(2)}) collective-permute-start(bf16[192,256]{1,0:T(8,128)(2,1)S(1)} %get-tuple-element.47), channel_id=1, source_target_pairs={{0,24},{1,25},{2,26},{3,27},{4,5},{5,4},{6,7},{7,6},{8,0},{9,1},{1... | collective-permute-start | bytes 294920 | tf_op jit(solution)/shard_map/ppermute | solution.py:261
  26.7 2.5 %collective-permute-done.11.refs_0_ = bf16[192,256]{1,0:T(8,128)(2,1)S(1)} collective-permute-done((bf16[192,256]{1,0:T(8,128)(2,1)S(1)}, bf16[192,256]{1,0:T(8,128)(2,1)S(1)}, u32[]{:S(2)}, u32[]{:S(2)}) %collective-permute-start.11) | collective-permute-done | bytes 98336 | tf_op jit(solution)/shard_map/ppermute | solution.py:261
  29.2 2.2 %collective-permute-done.12.refs_1_ = bf16[192,256]{1,0:T(8,128)(2,1)S(1)} collective-permute-done((bf16[192,256]{1,0:T(8,128)(2,1)S(1)}, bf16[192,256]{1,0:T(8,128)(2,1)S(1)}, u32[]{:S(2)}, u32[]{:S(2)}) %collective-permute-start.12) | collective-permute-done | bytes 98336 | tf_op jit(solution)/shard_map/ppermute | solution.py:261
  31.3 0.5 %collective-permute-done.13.refs_2_ = bf16[192,256]{1,0:T(8,128)(2,1)S(1)} collective-permute-done((bf16[192,256]{1,0:T(8,128)(2,1)S(1)}, bf16[192,256]{1,0:T(8,128)(2,1)S(1)}, u32[]{:S(2)}, u32[]{:S(2)}) %collective-permute-start.13) | collective-permute-done | bytes 98336 | tf_op jit(solution)/shard_map/ppermute | solution.py:261
  31.8 0.1 second.1
  31.9 1.6 %collective-permute-start.14 = (bf16[192,256]{1,0:T(8,128)(2,1)S(1)}, bf16[192,256]{1,0:T(8,128)(2,1)S(1)}, u32[]{:S(2)}, u32[]{:S(2)}) collective-permute-start(bf16[192,256]{1,0:T(8,128)(2,1)S(1)} %get-tuple-element.49), channel_id=1, source_target_pairs={{0,3},{1,2},{2,1},{3,0},{4,12},{5,13},{6,14},{7,15},{8,11},{9,10},... | collective-permute-start | bytes 294920 | tf_op jit(solution)/shard_map/ppermute | solution.py:261
  33.5 0.8 %collective-permute-start.15 = (bf16[192,256]{1,0:T(8,128)(2,1)S(1)}, bf16[192,256]{1,0:T(8,128)(2,1)S(1)}, u32[]{:S(2)}, u32[]{:S(2)}) collective-permute-start(bf16[192,256]{1,0:T(8,128)(2,1)S(1)} %get-tuple-element.50), channel_id=1, source_target_pairs={{0,2},{1,3},{2,0},{3,1},{4,20},{5,21},{6,22},{7,23},{8,10},{9,11},... | collective-permute-start | bytes 294920 | tf_op jit(solution)/shard_map/ppermute | solution.py:261
  34.2 1.2 %collective-permute-start.16 = (bf16[192,256]{1,0:T(8,128)(2,1)S(1)}, bf16[192,256]{1,0:T(8,128)(2,1)S(1)}, u32[]{:S(2)}, u32[]{:S(2)}) collective-permute-start(bf16[192,256]{1,0:T(8,128)(2,1)S(1)} %get-tuple-element.51), channel_id=1, source_target_pairs={{0,1},{1,0},{2,3},{3,2},{4,28},{5,29},{6,30},{7,31},{8,9},{9,8},{1... | collective-permute-start | bytes 294920 | tf_op jit(solution)/shard_map/ppermute | solution.py:261
  35.5 0.7 %store.2._ = bf16[8,32,256]{2,1,0:T(8,128)(2,1)} custom-call(bf16[128,256]{1,0:T(8,128)(2,1)S(1)} %get-tuple-element.41.same_ref.refs_0_, bf16[256,256]{1,0:T(8,128)(2,1)S(1)} %collective-permute-done.10.came_ref.refs_1_, bf16[192,256]{1,0:T(8,128)(2,1)S(1)} %collective-permute-done.11.refs_0_, bf16[192,256]{1,0:T(8,128)(2,1)S(1)} %collective-permute-done.12.refs_1_, ...), custom_call_target="tpu_custom_call" | custom-call | tf_op jit(solution)/shard_map/store/pallas_call | solution.py:224
  36.2 1.4 %collective-permute-done.14.refs_0_.refs_2_ = bf16[192,256]{1,0:T(8,128)(2,1)S(1)} collective-permute-done((bf16[192,256]{1,0:T(8,128)(2,1)S(1)}, bf16[192,256]{1,0:T(8,128)(2,1)S(1)}, u32[]{:S(2)}, u32[]{:S(2)}) %collective-permute-start.14) | collective-permute-done | bytes 98336 | tf_op jit(solution)/shard_map/ppermute | solution.py:261
  37.5 1.0 %collective-permute-done.15.refs_1_.refs_3_ = bf16[192,256]{1,0:T(8,128)(2,1)S(1)} collective-permute-done((bf16[192,256]{1,0:T(8,128)(2,1)S(1)}, bf16[192,256]{1,0:T(8,128)(2,1)S(1)}, u32[]{:S(2)}, u32[]{:S(2)}) %collective-permute-start.15) | collective-permute-done | bytes 98336 | tf_op jit(solution)/shard_map/ppermute | solution.py:261
  38.5 0.3 collective-permute-done.16.refs_2_.refs_4_
  38.9 0.1 third.1.own_ref
  38.9 0.1 collective-permute-start.17
  39.0 1.2 %collective-permute-done.17.came_ref = bf16[128,256]{1,0:T(8,128)(2,1)S(1)} collective-permute-done((bf16[128,256]{1,0:T(8,128)(2,1)S(1)}, bf16[128,256]{1,0:T(8,128)(2,1)S(1)}, u32[]{:S(2)}, u32[]{:S(2)}) %collective-permute-start.17) | collective-permute-done | bytes 65568 | tf_op jit(solution)/shard_map/ppermute | solution.py:95
  40.2 0.7 %finish.1 = f32[2,128,256]{2,1,0:T(8,128)} custom-call(bf16[128,256]{1,0:T(8,128)(2,1)S(1)} %third.1.own_ref, bf16[128,256]{1,0:T(8,128)(2,1)S(1)} %collective-permute-done.17.came_ref), custom_call_target="tpu_custom_call" | custom-call | tf_op jit(solution)/shard_map/finish/pallas_call | solution.py:243
  (9 shorter events, 0.1 us)
Async XLA Ops:
  0.6 9.8 %collective-permute-start.2 = (bf16[128,256]{1,0:T(8,128)(2,1)}, bf16[128,256]{1,0:T(8,128)(2,1)S(1)}, u32[]{:S(2)}, u32[]{:S(2)}) collective-permute-start(bf16[128,256]{1,0:T(8,128)(2,1)} %own_ref.1), channel_id=1, source_target_pairs={{0,8},{4,12},{8,16},{12,20},{16,24},{20,28},{24,0},{28,4},{1,9},{5... | collective-permute-start | bytes 196616 | tf_op jit(solution)/shard_map/ppermute | solution.py:266
  3.7 7.3 %collective-permute-start.1 = (bf16[128,256]{1,0:T(8,128)(2,1)}, bf16[128,256]{1,0:T(8,128)(2,1)S(1)}, u32[]{:S(2)}, u32[]{:S(2)}) collective-permute-start(bf16[128,256]{1,0:T(8,128)(2,1)} %own_ref.1), channel_id=1, source_target_pairs={{0,16},{4,20},{8,24},{12,28},{16,0},{20,4},{24,8},{28,12},{1,17},{... | collective-permute-start | bytes 196616 | tf_op jit(solution)/shard_map/ppermute | solution.py:266
  6.3 4.9 %collective-permute-start = (bf16[128,256]{1,0:T(8,128)(2,1)}, bf16[128,256]{1,0:T(8,128)(2,1)S(1)}, u32[]{:S(2)}, u32[]{:S(2)}) collective-permute-start(bf16[128,256]{1,0:T(8,128)(2,1)} %own_ref.1), channel_id=1, source_target_pairs={{0,24},{4,28},{8,0},{12,4},{16,8},{20,12},{24,16},{28,20},{1,25},{... | collective-permute-start | bytes 196616 | tf_op jit(solution)/shard_map/ppermute | solution.py:266
  7.6 4.1 %collective-permute-start.3 = (bf16[128,256]{1,0:T(8,128)(2,1)}, bf16[128,256]{1,0:T(8,128)(2,1)S(1)}, u32[]{:S(2)}, u32[]{:S(2)}) collective-permute-start(bf16[128,256]{1,0:T(8,128)(2,1)} %own_ref.1), channel_id=1, source_target_pairs={{0,4},{4,0},{8,12},{12,8},{16,20},{20,16},{24,28},{28,24},{1,5},{5... | collective-permute-start | bytes 196616 | tf_op jit(solution)/shard_map/ppermute | solution.py:95
  7.6 0.7 %copy-start.5 = (s32[128,1]{0,1:T(1,128)S(1)}, s32[128,1]{0,1:T(1,128)}, u32[]{:S(2)}) copy-start(s32[128,1]{0,1:T(1,128)} %param.11) | copy-start | bytes 1540
  8.3 1.0 %copy-start = (bf16[4,1,4,128,128]{4,3,2,1,0:T(8,128)(2,1)S(1)}, bf16[4,1,4,128,128]{4,3,2,1,0:T(8,128)(2,1)}, u32[]{:S(2)}) copy-start(bf16[4,1,4,128,128]{4,3,2,1,0:T(8,128)(2,1)} %param.7) | copy-start | bytes 1572868
  9.3 0.8 %copy-start.2 = (bf16[128,256]{1,0:T(8,128)(2,1)S(1)}, bf16[128,256]{1,0:T(8,128)(2,1)}, u32[]{:S(2)}) copy-start(bf16[128,256]{1,0:T(8,128)(2,1)} %own_ref.1) | copy-start | bytes 196612
  11.2 1.8 %copy-start.4 = (s32[4,1,4]{2,1,0:T(1,128)S(1)}, s32[4,1,4]{2,1,0:T(1,128)}, u32[]{:S(2)}) copy-start(s32[4,1,4]{2,1,0:T(1,128)} %param.8) | copy-start | bytes 196
  11.2 1.3 %collective-permute-start.4 = (bf16[128,256]{1,0:T(8,128)(2,1)S(1)}, bf16[128,256]{1,0:T(8,128)(2,1)S(1)}, u32[]{:S(2)}, u32[]{:S(2)}) collective-permute-start(bf16[128,256]{1,0:T(8,128)(2,1)S(1)} %collective-permute-done.2.refs_1_), channel_id=1, source_target_pairs={{0,4},{4,0},{8,12},{12,8},{16,20},{20,16},{24,28},{28,24},{1,5},{5... | collective-permute-start | bytes 196616 | tf_op jit(solution)/shard_map/ppermute | solution.py:95
  11.2 1.4 %collective-permute-start.5 = (bf16[128,256]{1,0:T(8,128)(2,1)S(1)}, bf16[128,256]{1,0:T(8,128)(2,1)S(1)}, u32[]{:S(2)}, u32[]{:S(2)}) collective-permute-start(bf16[128,256]{1,0:T(8,128)(2,1)S(1)} %collective-permute-done.1.refs_2_), channel_id=1, source_target_pairs={{0,4},{4,0},{8,12},{12,8},{16,20},{20,16},{24,28},{28,24},{1,5},{5... | collective-permute-start | bytes 196616 | tf_op jit(solution)/shard_map/ppermute | solution.py:95
  11.7 1.3 %collective-permute-start.6 = (bf16[128,256]{1,0:T(8,128)(2,1)S(1)}, bf16[128,256]{1,0:T(8,128)(2,1)S(1)}, u32[]{:S(2)}, u32[]{:S(2)}) collective-permute-start(bf16[128,256]{1,0:T(8,128)(2,1)S(1)} %collective-permute-done.refs_3_), channel_id=1, source_target_pairs={{0,4},{4,0},{8,12},{12,8},{16,20},{20,16},{24,28},{28,24},{1,5},{5... | collective-permute-start | bytes 196616 | tf_op jit(solution)/shard_map/ppermute | solution.py:95
  13.0 7.8 %copy-start.1 = (bf16[256,256]{1,0:T(8,128)(2,1)S(1)}, bf16[256,256]{1,0:T(8,128)(2,1)}, u32[]{:S(2)}) copy-start(bf16[256,256]{1,0:T(8,128)(2,1)} %weight_ref.1) | copy-start | bytes 393220
  13.0 7.8 %copy-start.3 = (bf16[128,256]{1,0:T(8,128)(2,1)S(1)}, bf16[128,256]{1,0:T(8,128)(2,1)}, u32[]{:S(2)}) copy-start(bf16[128,256]{1,0:T(8,128)(2,1)} %cot_ref.1) | copy-start | bytes 196612
  13.4 5.3 %collective-permute-start.7 = (bf16[128,256]{1,0:T(8,128)(2,1)S(1)}, bf16[128,256]{1,0:T(8,128)(2,1)S(1)}, u32[]{:S(2)}, u32[]{:S(2)}) collective-permute-start(bf16[128,256]{1,0:T(8,128)(2,1)S(1)} %get-tuple-element.38), channel_id=1, source_target_pairs={{0,3},{1,2},{2,1},{3,0},{4,7},{5,6},{6,5},{7,4},{8,11},{9,10},{10,... | collective-permute-start | bytes 196616 | tf_op jit(solution)/shard_map/ppermute | solution.py:95
  16.0 4.3 %collective-permute-start.8 = (bf16[128,256]{1,0:T(8,128)(2,1)S(1)}, bf16[128,256]{1,0:T(8,128)(2,1)S(1)}, u32[]{:S(2)}, u32[]{:S(2)}) collective-permute-start(bf16[128,256]{1,0:T(8,128)(2,1)S(1)} %get-tuple-element.39), channel_id=1, source_target_pairs={{0,2},{1,3},{2,0},{3,1},{4,6},{5,7},{6,4},{7,5},{8,10},{9,11},{10,... | collective-permute-start | bytes 196616 | tf_op jit(solution)/shard_map/ppermute | solution.py:95
  16.5 4.3 %collective-permute-start.9 = (bf16[128,256]{1,0:T(8,128)(2,1)S(1)}, bf16[128,256]{1,0:T(8,128)(2,1)S(1)}, u32[]{:S(2)}, u32[]{:S(2)}) collective-permute-start(bf16[128,256]{1,0:T(8,128)(2,1)S(1)} %get-tuple-element.40), channel_id=1, source_target_pairs={{0,1},{1,0},{2,3},{3,2},{4,5},{5,4},{6,7},{7,6},{8,9},{9,8},{10,11... | collective-permute-start | bytes 196616 | tf_op jit(solution)/shard_map/ppermute | solution.py:95
  21.2 1.4 %collective-permute-start.10 = (bf16[256,256]{1,0:T(8,128)(2,1)S(1)}, bf16[256,256]{1,0:T(8,128)(2,1)S(1)}, u32[]{:S(2)}, u32[]{:S(2)}) collective-permute-start(bf16[256,256]{1,0:T(8,128)(2,1)S(1)} %get-tuple-element.42), channel_id=1, source_target_pairs={{0,4},{4,0},{8,12},{12,8},{16,20},{20,16},{24,28},{28,24},{1,5},{5... | collective-permute-start | bytes 393224 | tf_op jit(solution)/shard_map/ppermute | solution.py:95
  22.6 6.5 %collective-permute-start.11 = (bf16[192,256]{1,0:T(8,128)(2,1)S(1)}, bf16[192,256]{1,0:T(8,128)(2,1)S(1)}, u32[]{:S(2)}, u32[]{:S(2)}) collective-permute-start(bf16[192,256]{1,0:T(8,128)(2,1)S(1)} %get-tuple-element.45), channel_id=1, source_target_pairs={{0,8},{1,9},{2,10},{3,11},{4,7},{5,6},{6,5},{7,4},{8,16},{9,17},{1... | collective-permute-start | bytes 294920 | tf_op jit(solution)/shard_map/ppermute | solution.py:261
  24.3 7.1 %collective-permute-start.12 = (bf16[192,256]{1,0:T(8,128)(2,1)S(1)}, bf16[192,256]{1,0:T(8,128)(2,1)S(1)}, u32[]{:S(2)}, u32[]{:S(2)}) collective-permute-start(bf16[192,256]{1,0:T(8,128)(2,1)S(1)} %get-tuple-element.46), channel_id=1, source_target_pairs={{0,16},{1,17},{2,18},{3,19},{4,6},{5,7},{6,4},{7,5},{8,24},{9,25},... | collective-permute-start | bytes 294920 | tf_op jit(solution)/shard_map/ppermute | solution.py:261
  26.3 5.6 %collective-permute-start.13 = (bf16[192,256]{1,0:T(8,128)(2,1)S(1)}, bf16[192,256]{1,0:T(8,128)(2,1)S(1)}, u32[]{:S(2)}, u32[]{:S(2)}) collective-permute-start(bf16[192,256]{1,0:T(8,128)(2,1)S(1)} %get-tuple-element.47), channel_id=1, source_target_pairs={{0,24},{1,25},{2,26},{3,27},{4,5},{5,4},{6,7},{7,6},{8,0},{9,1},{1... | collective-permute-start | bytes 294920 | tf_op jit(solution)/shard_map/ppermute | solution.py:261
  31.9 5.6 %collective-permute-start.14 = (bf16[192,256]{1,0:T(8,128)(2,1)S(1)}, bf16[192,256]{1,0:T(8,128)(2,1)S(1)}, u32[]{:S(2)}, u32[]{:S(2)}) collective-permute-start(bf16[192,256]{1,0:T(8,128)(2,1)S(1)} %get-tuple-element.49), channel_id=1, source_target_pairs={{0,3},{1,2},{2,1},{3,0},{4,12},{5,13},{6,14},{7,15},{8,11},{9,10},... | collective-permute-start | bytes 294920 | tf_op jit(solution)/shard_map/ppermute | solution.py:261
  33.5 5.1 %collective-permute-start.15 = (bf16[192,256]{1,0:T(8,128)(2,1)S(1)}, bf16[192,256]{1,0:T(8,128)(2,1)S(1)}, u32[]{:S(2)}, u32[]{:S(2)}) collective-permute-start(bf16[192,256]{1,0:T(8,128)(2,1)S(1)} %get-tuple-element.50), channel_id=1, source_target_pairs={{0,2},{1,3},{2,0},{3,1},{4,20},{5,21},{6,22},{7,23},{8,10},{9,11},... | collective-permute-start | bytes 294920 | tf_op jit(solution)/shard_map/ppermute | solution.py:261
  34.2 4.6 %collective-permute-start.16 = (bf16[192,256]{1,0:T(8,128)(2,1)S(1)}, bf16[192,256]{1,0:T(8,128)(2,1)S(1)}, u32[]{:S(2)}, u32[]{:S(2)}) collective-permute-start(bf16[192,256]{1,0:T(8,128)(2,1)S(1)} %get-tuple-element.51), channel_id=1, source_target_pairs={{0,1},{1,0},{2,3},{3,2},{4,28},{5,29},{6,30},{7,31},{8,9},{9,8},{1... | collective-permute-start | bytes 294920 | tf_op jit(solution)/shard_map/ppermute | solution.py:261
  38.9 1.3 %collective-permute-start.17 = (bf16[128,256]{1,0:T(8,128)(2,1)S(1)}, bf16[128,256]{1,0:T(8,128)(2,1)S(1)}, u32[]{:S(2)}, u32[]{:S(2)}) collective-permute-start(bf16[128,256]{1,0:T(8,128)(2,1)S(1)} %third.1.own_ref), channel_id=1, source_target_pairs={{0,4},{4,0},{8,12},{12,8},{16,20},{20,16},{24,28},{28,24},{1,5},{5... | collective-permute-start | bytes 196616 | tf_op jit(solution)/shard_map/ppermute | solution.py:95

commit v22 on v21

--- a/solution.py
+++ b/solution.py
@@ -67,8 +67,14 @@
     depth = src_ref.shape[1]
     section, rep = lax.axis_index("section"), lax.axis_index("rep")
     chip, chips = place_of_chip()
+    sources = [chip]
+    for route in routes(chips):
+        source = jnp.int32(0)
+        for c, to in enumerate(route):
+            source = jnp.where(chip == to, c, source)
+        sources.append(source)
     for i, ref in enumerate(block_refs):
-        held[2 * ((chip + chips - i % chips) % chips) + ((section + i // chips) & 1)] = ref[...]
+        held[2 * sources[i % chips] + ((section + i // chips) & 1)] = ref[...]
     for j, out_ref in zip([0] + across(len(out_refs)), out_refs):
         g = rep ^ j
         right = jnp.concatenate([held[src_ref[g, k]] for k in range(depth)], axis=0)
@@ -261,14 +267,20 @@
     return lax.ppermute(value, ("section", "rep"), pairs)
 
 
-def send_along(value, axis, shift):
-    n = lax.axis_size(axis)
-    return lax.ppermute(value, axis, [(s, (s + 2 * shift) % n) for s in range(n)])
+def routes(chips):
+    if chips == 4:
+        return [(1, 3, 0, 2), (3, 2, 1, 0), (2, 0, 3, 1)]
+    return [tuple((c + i) % chips for c in range(chips)) for i in range(1, chips)]
+
+
+def send_along(value, axis, route):
+    pairs = [(s, 2 * route[s // 2] + s % 2) for s in range(lax.axis_size(axis))]
+    return lax.ppermute(value, axis, pairs)
 
 
 def gather_blocks(features, axis, ready):
     chips = lax.axis_size(axis) // 2
-    near = [features] + [send_along(features, axis, i) for i in range(1, chips)]
+    near = [features] + [send_along(features, axis, route) for route in routes(chips)]
     beside = swap(features, axis, 1)
     came, ready = lax.optimization_barrier((near[:0:-1], ready))
     near[1:] = came[::-1]

time: 41.2 us -> 40.6 us (0.985)
  waiting for transfers between devices: 16.2 us -> 13.7 us
  starting transfers between devices: 18.8 us -> 20.8 us
    ppermute x6, waiting for transfers between devices: 7.84 us -> 5.61 us  [exchange(): return lax.ppermute(value, ('section', 'rep'), pairs)]
    ppermute x6, starting transfers between devices: 7.58 us -> 9.4 us  [exchange(): return lax.ppermute(value, ('section', 'rep'), pairs)]
  transfers between devices with their start and end apart: 18 -> 18, of which waited for: 16 -> 15; matrix products, arithmetic and copies ran while one was open for 0% -> 0% of each run, Pallas kernels for 2% -> 2%
where the time goes in v22:
time: 40.6 us; the launch traced here: 40.4 us
  starting transfers between devices  20.8 us (51%)
  waiting for transfers between devices  13.7 us (34%)
  Pallas kernels  2.66 us (7%)
  local copies, waits for them, and re-layouts  2.55 us (6%)
  between operations  0.73 us (2%)
    ppermute x6, starting transfers between devices, exchange(): return lax.ppermute(value, ('section', 'rep'), pairs)  9.4 us
    ppermute x9, waiting for transfers between devices, swap(): lax.ppermute(value, axis, [(i, i ^ j) for i in range(lax.axis_size(axis))])  7.52 us
    ppermute x3, starting transfers between devices, send_along(): return lax.ppermute(value, axis, pairs)  7.13 us
    ppermute x6, waiting for transfers between devices, exchange(): return lax.ppermute(value, ('section', 'rep'), pairs)  5.61 us
    ppermute x9, starting transfers between devices, swap(): lax.ppermute(value, axis, [(i, i ^ j) for i in range(lax.axis_size(axis))])  4.25 us
    unnamed x12, local copies, waits for them, and re-layouts  2.55 us
  transfers between devices with their start and end apart: 18, of which 15 were waited for; matrix products, arithmetic and copies ran while one was open for 0% of the time, Pallas kernels for 2%

profile of v22, /device:TPU:0, one launch (start us, length us, event | category | flops | bytes accessed | tf_op | source)
XLA Modules:
  0.0 40.4 jit_solution(12768527926442104691)
XLA Ops:
  0.6 3.1 %collective-permute-start.2 = (bf16[128,256]{1,0:T(8,128)(2,1)}, bf16[128,256]{1,0:T(8,128)(2,1)S(1)}, u32[]{:S(2)}, u32[]{:S(2)}) collective-permute-start(bf16[128,256]{1,0:T(8,128)(2,1)} %own_ref.1), channel_id=1, source_target_pairs={{0,8},{4,12},{8,24},{12,28},{16,0},{20,4},{24,16},{28,20},{1,9},{5... | collective-permute-start | bytes 196616 | tf_op jit(solution)/shard_map/ppermute | solution.py:278
  3.7 2.5 %collective-permute-start.1 = (bf16[128,256]{1,0:T(8,128)(2,1)}, bf16[128,256]{1,0:T(8,128)(2,1)S(1)}, u32[]{:S(2)}, u32[]{:S(2)}) collective-permute-start(bf16[128,256]{1,0:T(8,128)(2,1)} %own_ref.1), channel_id=1, source_target_pairs={{0,24},{4,28},{8,16},{12,20},{16,8},{20,12},{24,0},{28,4},{1,25},{... | collective-permute-start | bytes 196616 | tf_op jit(solution)/shard_map/ppermute | solution.py:278
  6.2 1.6 %collective-permute-start = (bf16[128,256]{1,0:T(8,128)(2,1)}, bf16[128,256]{1,0:T(8,128)(2,1)S(1)}, u32[]{:S(2)}, u32[]{:S(2)}) collective-permute-start(bf16[128,256]{1,0:T(8,128)(2,1)} %own_ref.1), channel_id=1, source_target_pairs={{0,16},{4,20},{8,0},{12,4},{16,24},{20,28},{24,8},{28,12},{1,17},{... | collective-permute-start | bytes 196616 | tf_op jit(solution)/shard_map/ppermute | solution.py:278
  7.8 0.0 collective-permute-start.3
  7.8 0.7 %copy-done.5 = s32[128,1]{0,1:T(1,128)S(1)} copy-done((s32[128,1]{0,1:T(1,128)S(1)}, s32[128,1]{0,1:T(1,128)}, u32[]{:S(2)}) %copy-start.5) | copy-done | bytes 536
  8.4 1.0 %copy-done = bf16[4,1,4,128,128]{4,3,2,1,0:T(8,128)(2,1)S(1)} copy-done((bf16[4,1,4,128,128]{4,3,2,1,0:T(8,128)(2,1)S(1)}, bf16[4,1,4,128,128]{4,3,2,1,0:T(8,128)(2,1)}, u32[]{:S(2)}) %copy-start) | copy-done | bytes 524312
  9.5 0.8 %copy-done.2 = bf16[128,256]{1,0:T(8,128)(2,1)S(1)} copy-done((bf16[128,256]{1,0:T(8,128)(2,1)S(1)}, bf16[128,256]{1,0:T(8,128)(2,1)}, u32[]{:S(2)}) %copy-start.2) | copy-done | bytes 65560
  10.3 0.2 prepare.1
  10.5 0.0 collective-permute-done.2.refs_1_
  10.5 0.3 collective-permute-done.1.refs_2_
  10.9 0.2 collective-permute-done.refs_3_
  11.1 0.0 collective-permute-start.4
  11.1 0.5 %collective-permute-start.5 = (bf16[128,256]{1,0:T(8,128)(2,1)S(1)}, bf16[128,256]{1,0:T(8,128)(2,1)S(1)}, u32[]{:S(2)}, u32[]{:S(2)}) collective-permute-start(bf16[128,256]{1,0:T(8,128)(2,1)S(1)} %collective-permute-done.1.refs_2_), channel_id=1, source_target_pairs={{0,4},{4,0},{8,12},{12,8},{16,20},{20,16},{24,28},{28,24},{1,5},{5... | collective-permute-start | bytes 196616 | tf_op jit(solution)/shard_map/ppermute | solution.py:101
  11.6 0.0 collective-permute-start.6
  11.7 0.0 collective-permute-done.3.refs_4_
  11.7 0.7 %collective-permute-done.4.refs_5_ = bf16[128,256]{1,0:T(8,128)(2,1)S(1)} collective-permute-done((bf16[128,256]{1,0:T(8,128)(2,1)S(1)}, bf16[128,256]{1,0:T(8,128)(2,1)S(1)}, u32[]{:S(2)}, u32[]{:S(2)}) %collective-permute-start.4) | collective-permute-done | bytes 65568 | tf_op jit(solution)/shard_map/ppermute | solution.py:101
  12.4 0.2 collective-permute-done.5.refs_6_
  12.5 0.4 collective-permute-done.6.refs_7_
  12.9 0.0 copy-done.4
  12.9 0.4 %partials.1 = (bf16[128,256]{1,0:T(8,128)(2,1)S(1)}, bf16[128,256]{1,0:T(8,128)(2,1)S(1)}, bf16[128,256]{1,0:T(8,128)(2,1)S(1)}, bf16[128,256]{1,0:T(8,128)(2,1)S(1)}) custom-call(s32[4,4]{1,0:T(4,128)S(1)} %bitcast.6, bf16[4,128,512]{2,1,0:T(8,128)(2,1)S(1)} %get-tuple-element.32.wide_ref, bf16[128,256]{1,0:T(8,128)(2,1)S(1)} %get-tuple-element.33.refs_0_, ...), custom_call_target="tpu_custom_call" | custom-call | tf_op jit(solution)/shard_map/partials/pallas_call | solution.py:89
  13.3 2.5 %collective-permute-start.7 = (bf16[128,256]{1,0:T(8,128)(2,1)S(1)}, bf16[128,256]{1,0:T(8,128)(2,1)S(1)}, u32[]{:S(2)}, u32[]{:S(2)}) collective-permute-start(bf16[128,256]{1,0:T(8,128)(2,1)S(1)} %get-tuple-element.38), channel_id=1, source_target_pairs={{0,3},{1,2},{2,1},{3,0},{4,7},{5,6},{6,5},{7,4},{8,11},{9,10},{10,... | collective-permute-start | bytes 196616 | tf_op jit(solution)/shard_map/ppermute | solution.py:101
  15.8 0.5 %collective-permute-start.8 = (bf16[128,256]{1,0:T(8,128)(2,1)S(1)}, bf16[128,256]{1,0:T(8,128)(2,1)S(1)}, u32[]{:S(2)}, u32[]{:S(2)}) collective-permute-start(bf16[128,256]{1,0:T(8,128)(2,1)S(1)} %get-tuple-element.39), channel_id=1, source_target_pairs={{0,2},{1,3},{2,0},{3,1},{4,6},{5,7},{6,4},{7,5},{8,10},{9,11},{10,... | collective-permute-start | bytes 196616 | tf_op jit(solution)/shard_map/ppermute | solution.py:101
  16.3 0.5 %collective-permute-start.9 = (bf16[128,256]{1,0:T(8,128)(2,1)S(1)}, bf16[128,256]{1,0:T(8,128)(2,1)S(1)}, u32[]{:S(2)}, u32[]{:S(2)}) collective-permute-start(bf16[128,256]{1,0:T(8,128)(2,1)S(1)} %get-tuple-element.40), channel_id=1, source_target_pairs={{0,1},{1,0},{2,3},{3,2},{4,5},{5,4},{6,7},{7,6},{8,9},{9,8},{10,11... | collective-permute-start | bytes 196616 | tf_op jit(solution)/shard_map/ppermute | solution.py:101
  16.9 1.7 %collective-permute-done.7.refs_1_ = bf16[128,256]{1,0:T(8,128)(2,1)S(1)} collective-permute-done((bf16[128,256]{1,0:T(8,128)(2,1)S(1)}, bf16[128,256]{1,0:T(8,128)(2,1)S(1)}, u32[]{:S(2)}, u32[]{:S(2)}) %collective-permute-start.7) | collective-permute-done | bytes 65568 | tf_op jit(solution)/shard_map/ppermute | solution.py:101
  18.5 1.5 %collective-permute-done.8.refs_2_ = bf16[128,256]{1,0:T(8,128)(2,1)S(1)} collective-permute-done((bf16[128,256]{1,0:T(8,128)(2,1)S(1)}, bf16[128,256]{1,0:T(8,128)(2,1)S(1)}, u32[]{:S(2)}, u32[]{:S(2)}) %collective-permute-start.8) | collective-permute-done | bytes 65568 | tf_op jit(solution)/shard_map/ppermute | solution.py:101
  20.1 0.5 %collective-permute-done.9.refs_3_ = bf16[128,256]{1,0:T(8,128)(2,1)S(1)} collective-permute-done((bf16[128,256]{1,0:T(8,128)(2,1)S(1)}, bf16[128,256]{1,0:T(8,128)(2,1)S(1)}, u32[]{:S(2)}, u32[]{:S(2)}) %collective-permute-start.9) | collective-permute-done | bytes 65568 | tf_op jit(solution)/shard_map/ppermute | solution.py:101
  20.6 0.0 copy-done.1
  20.6 0.4 %dense.1 = (bf16[128,256]{1,0:T(8,128)(2,1)S(1)}, f32[128,256]{1,0:T(8,128)S(1)}, bf16[256,256]{1,0:T(8,128)(2,1)S(1)}) custom-call(bf16[256,256]{1,0:T(8,128)(2,1)S(1)} %copy-done.1, bf16[128,256]{1,0:T(8,128)(2,1)S(1)} %copy-done.3, bf16[256,128]{1,0:T(8,128)(2,1)S(1)} %get-tuple-element.31.placing_ref, bf16[128,256]{1,0:T(8,128)(2,1)S(1)} %get-tuple-element.37.refs_0_, ...), custom_call_target="tpu_custom_call" | custom-call | tf_op jit(solution)/shard_map/dense/pallas_call | solution.py:133
  21.0 0.1 collective-permute-start.10
  21.1 1.3 %collective-permute-done.10.came_ref.refs_1_ = bf16[256,256]{1,0:T(8,128)(2,1)S(1)} collective-permute-done((bf16[256,256]{1,0:T(8,128)(2,1)S(1)}, bf16[256,256]{1,0:T(8,128)(2,1)S(1)}, u32[]{:S(2)}, u32[]{:S(2)}) %collective-permute-start.10) | collective-permute-done | bytes 131104 | tf_op jit(solution)/shard_map/ppermute | solution.py:101
  22.5 1.7 %collective-permute-start.11 = (bf16[192,256]{1,0:T(8,128)(2,1)S(1)}, bf16[192,256]{1,0:T(8,128)(2,1)S(1)}, u32[]{:S(2)}, u32[]{:S(2)}) collective-permute-start(bf16[192,256]{1,0:T(8,128)(2,1)S(1)} %get-tuple-element.45), channel_id=1, source_target_pairs={{0,8},{1,9},{2,10},{3,11},{4,7},{5,6},{6,5},{7,4},{8,16},{9,17},{1... | collective-permute-start | bytes 294920 | tf_op jit(solution)/shard_map/ppermute | solution.py:267
  24.2 2.1 %collective-permute-start.12 = (bf16[192,256]{1,0:T(8,128)(2,1)S(1)}, bf16[192,256]{1,0:T(8,128)(2,1)S(1)}, u32[]{:S(2)}, u32[]{:S(2)}) collective-permute-start(bf16[192,256]{1,0:T(8,128)(2,1)S(1)} %get-tuple-element.46), channel_id=1, source_target_pairs={{0,16},{1,17},{2,18},{3,19},{4,6},{5,7},{6,4},{7,5},{8,24},{9,25},... | collective-permute-start | bytes 294920 | tf_op jit(solution)/shard_map/ppermute | solution.py:267
  26.3 2.1 %collective-permute-start.13 = (bf16[192,256]{1,0:T(8,128)(2,1)S(1)}, bf16[192,256]{1,0:T(8,128)(2,1)S(1)}, u32[]{:S(2)}, u32[]{:S(2)}) collective-permute-start(bf16[192,256]{1,0:T(8,128)(2,1)S(1)} %get-tuple-element.47), channel_id=1, source_target_pairs={{0,24},{1,25},{2,26},{3,27},{4,5},{5,4},{6,7},{7,6},{8,0},{9,1},{1... | collective-permute-start | bytes 294920 | tf_op jit(solution)/shard_map/ppermute | solution.py:267
  28.4 0.6 %collective-permute-done.11.refs_0_ = bf16[192,256]{1,0:T(8,128)(2,1)S(1)} collective-permute-done((bf16[192,256]{1,0:T(8,128)(2,1)S(1)}, bf16[192,256]{1,0:T(8,128)(2,1)S(1)}, u32[]{:S(2)}, u32[]{:S(2)}) %collective-permute-start.11) | collective-permute-done | bytes 98336 | tf_op jit(solution)/shard_map/ppermute | solution.py:267
  29.0 2.1 %collective-permute-done.12.refs_1_ = bf16[192,256]{1,0:T(8,128)(2,1)S(1)} collective-permute-done((bf16[192,256]{1,0:T(8,128)(2,1)S(1)}, bf16[192,256]{1,0:T(8,128)(2,1)S(1)}, u32[]{:S(2)}, u32[]{:S(2)}) %collective-permute-start.12) | collective-permute-done | bytes 98336 | tf_op jit(solution)/shard_map/ppermute | solution.py:267
  31.1 0.0 collective-permute-done.13.refs_2_
  31.1 0.1 second.1
  31.2 1.5 %collective-permute-start.14 = (bf16[192,256]{1,0:T(8,128)(2,1)S(1)}, bf16[192,256]{1,0:T(8,128)(2,1)S(1)}, u32[]{:S(2)}, u32[]{:S(2)}) collective-permute-start(bf16[192,256]{1,0:T(8,128)(2,1)S(1)} %get-tuple-element.49), channel_id=1, source_target_pairs={{0,3},{1,2},{2,1},{3,0},{4,12},{5,13},{6,14},{7,15},{8,11},{9,10},... | collective-permute-start | bytes 294920 | tf_op jit(solution)/shard_map/ppermute | solution.py:267
  32.7 0.8 %collective-permute-start.15 = (bf16[192,256]{1,0:T(8,128)(2,1)S(1)}, bf16[192,256]{1,0:T(8,128)(2,1)S(1)}, u32[]{:S(2)}, u32[]{:S(2)}) collective-permute-start(bf16[192,256]{1,0:T(8,128)(2,1)S(1)} %get-tuple-element.50), channel_id=1, source_target_pairs={{0,2},{1,3},{2,0},{3,1},{4,20},{5,21},{6,22},{7,23},{8,10},{9,11},... | collective-permute-start | bytes 294920 | tf_op jit(solution)/shard_map/ppermute | solution.py:267
  33.5 1.2 %collective-permute-start.16 = (bf16[192,256]{1,0:T(8,128)(2,1)S(1)}, bf16[192,256]{1,0:T(8,128)(2,1)S(1)}, u32[]{:S(2)}, u32[]{:S(2)}) collective-permute-start(bf16[192,256]{1,0:T(8,128)(2,1)S(1)} %get-tuple-element.51), channel_id=1, source_target_pairs={{0,1},{1,0},{2,3},{3,2},{4,28},{5,29},{6,30},{7,31},{8,9},{9,8},{1... | collective-permute-start | bytes 294920 | tf_op jit(solution)/shard_map/ppermute | solution.py:267
  34.7 0.7 %store.2._ = bf16[8,32,256]{2,1,0:T(8,128)(2,1)} custom-call(bf16[128,256]{1,0:T(8,128)(2,1)S(1)} %get-tuple-element.41.same_ref.refs_0_, bf16[256,256]{1,0:T(8,128)(2,1)S(1)} %collective-permute-done.10.came_ref.refs_1_, bf16[192,256]{1,0:T(8,128)(2,1)S(1)} %collective-permute-done.11.refs_0_, bf16[192,256]{1,0:T(8,128)(2,1)S(1)} %collective-permute-done.12.refs_1_, ...), custom_call_target="tpu_custom_call" | custom-call | tf_op jit(solution)/shard_map/store/pallas_call | solution.py:230
  35.4 1.4 %collective-permute-done.14.refs_0_.refs_2_ = bf16[192,256]{1,0:T(8,128)(2,1)S(1)} collective-permute-done((bf16[192,256]{1,0:T(8,128)(2,1)S(1)}, bf16[192,256]{1,0:T(8,128)(2,1)S(1)}, u32[]{:S(2)}, u32[]{:S(2)}) %collective-permute-start.14) | collective-permute-done | bytes 98336 | tf_op jit(solution)/shard_map/ppermute | solution.py:267
  36.8 1.0 %collective-permute-done.15.refs_1_.refs_3_ = bf16[192,256]{1,0:T(8,128)(2,1)S(1)} collective-permute-done((bf16[192,256]{1,0:T(8,128)(2,1)S(1)}, bf16[192,256]{1,0:T(8,128)(2,1)S(1)}, u32[]{:S(2)}, u32[]{:S(2)}) %collective-permute-start.15) | collective-permute-done | bytes 98336 | tf_op jit(solution)/shard_map/ppermute | solution.py:267
  37.8 0.5 %collective-permute-done.16.refs_2_.refs_4_ = bf16[192,256]{1,0:T(8,128)(2,1)S(1)} collective-permute-done((bf16[192,256]{1,0:T(8,128)(2,1)S(1)}, bf16[192,256]{1,0:T(8,128)(2,1)S(1)}, u32[]{:S(2)}, u32[]{:S(2)}) %collective-permute-start.16) | collective-permute-done | bytes 98336 | tf_op jit(solution)/shard_map/ppermute | solution.py:267
  38.3 0.1 third.1.own_ref
  38.4 0.1 collective-permute-start.17
  38.4 1.2 %collective-permute-done.17.came_ref = bf16[128,256]{1,0:T(8,128)(2,1)S(1)} collective-permute-done((bf16[128,256]{1,0:T(8,128)(2,1)S(1)}, bf16[128,256]{1,0:T(8,128)(2,1)S(1)}, u32[]{:S(2)}, u32[]{:S(2)}) %collective-permute-start.17) | collective-permute-done | bytes 65568 | tf_op jit(solution)/shard_map/ppermute | solution.py:101
  39.7 0.7 %finish.1 = f32[2,128,256]{2,1,0:T(8,128)} custom-call(bf16[128,256]{1,0:T(8,128)(2,1)S(1)} %third.1.own_ref, bf16[128,256]{1,0:T(8,128)(2,1)S(1)} %collective-permute-done.17.came_ref), custom_call_target="tpu_custom_call" | custom-call | tf_op jit(solution)/shard_map/finish/pallas_call | solution.py:249
  (9 shorter events, 0.1 us)
Async XLA Ops:
  0.6 9.9 %collective-permute-start.2 = (bf16[128,256]{1,0:T(8,128)(2,1)}, bf16[128,256]{1,0:T(8,128)(2,1)S(1)}, u32[]{:S(2)}, u32[]{:S(2)}) collective-permute-start(bf16[128,256]{1,0:T(8,128)(2,1)} %own_ref.1), channel_id=1, source_target_pairs={{0,8},{4,12},{8,24},{12,28},{16,0},{20,4},{24,16},{28,20},{1,9},{5... | collective-permute-start | bytes 196616 | tf_op jit(solution)/shard_map/ppermute | solution.py:278
  3.7 7.2 %collective-permute-start.1 = (bf16[128,256]{1,0:T(8,128)(2,1)}, bf16[128,256]{1,0:T(8,128)(2,1)S(1)}, u32[]{:S(2)}, u32[]{:S(2)}) collective-permute-start(bf16[128,256]{1,0:T(8,128)(2,1)} %own_ref.1), channel_id=1, source_target_pairs={{0,24},{4,28},{8,16},{12,20},{16,8},{20,12},{24,0},{28,4},{1,25},{... | collective-permute-start | bytes 196616 | tf_op jit(solution)/shard_map/ppermute | solution.py:278
  6.2 4.9 %collective-permute-start = (bf16[128,256]{1,0:T(8,128)(2,1)}, bf16[128,256]{1,0:T(8,128)(2,1)S(1)}, u32[]{:S(2)}, u32[]{:S(2)}) collective-permute-start(bf16[128,256]{1,0:T(8,128)(2,1)} %own_ref.1), channel_id=1, source_target_pairs={{0,16},{4,20},{8,0},{12,4},{16,24},{20,28},{24,8},{28,12},{1,17},{... | collective-permute-start | bytes 196616 | tf_op jit(solution)/shard_map/ppermute | solution.py:278
  7.8 3.9 %collective-permute-start.3 = (bf16[128,256]{1,0:T(8,128)(2,1)}, bf16[128,256]{1,0:T(8,128)(2,1)S(1)}, u32[]{:S(2)}, u32[]{:S(2)}) collective-permute-start(bf16[128,256]{1,0:T(8,128)(2,1)} %own_ref.1), channel_id=1, source_target_pairs={{0,4},{4,0},{8,12},{12,8},{16,20},{20,16},{24,28},{28,24},{1,5},{5... | collective-permute-start | bytes 196616 | tf_op jit(solution)/shard_map/ppermute | solution.py:101
  7.8 0.7 %copy-start.5 = (s32[128,1]{0,1:T(1,128)S(1)}, s32[128,1]{0,1:T(1,128)}, u32[]{:S(2)}) copy-start(s32[128,1]{0,1:T(1,128)} %param.11) | copy-start | bytes 1540
  8.4 1.0 %copy-start = (bf16[4,1,4,128,128]{4,3,2,1,0:T(8,128)(2,1)S(1)}, bf16[4,1,4,128,128]{4,3,2,1,0:T(8,128)(2,1)}, u32[]{:S(2)}) copy-start(bf16[4,1,4,128,128]{4,3,2,1,0:T(8,128)(2,1)} %param.7) | copy-start | bytes 1572868
  9.5 0.8 %copy-start.2 = (bf16[128,256]{1,0:T(8,128)(2,1)S(1)}, bf16[128,256]{1,0:T(8,128)(2,1)}, u32[]{:S(2)}) copy-start(bf16[128,256]{1,0:T(8,128)(2,1)} %own_ref.1) | copy-start | bytes 196612
  11.1 1.8 %copy-start.4 = (s32[4,1,4]{2,1,0:T(1,128)S(1)}, s32[4,1,4]{2,1,0:T(1,128)}, u32[]{:S(2)}) copy-start(s32[4,1,4]{2,1,0:T(1,128)} %param.8) | copy-start | bytes 196
  11.1 1.3 %collective-permute-start.4 = (bf16[128,256]{1,0:T(8,128)(2,1)S(1)}, bf16[128,256]{1,0:T(8,128)(2,1)S(1)}, u32[]{:S(2)}, u32[]{:S(2)}) collective-permute-start(bf16[128,256]{1,0:T(8,128)(2,1)S(1)} %collective-permute-done.2.refs_1_), channel_id=1, source_target_pairs={{0,4},{4,0},{8,12},{12,8},{16,20},{20,16},{24,28},{28,24},{1,5},{5... | collective-permute-start | bytes 196616 | tf_op jit(solution)/shard_map/ppermute | solution.py:101
  11.1 1.4 %collective-permute-start.5 = (bf16[128,256]{1,0:T(8,128)(2,1)S(1)}, bf16[128,256]{1,0:T(8,128)(2,1)S(1)}, u32[]{:S(2)}, u32[]{:S(2)}) collective-permute-start(bf16[128,256]{1,0:T(8,128)(2,1)S(1)} %collective-permute-done.1.refs_2_), channel_id=1, source_target_pairs={{0,4},{4,0},{8,12},{12,8},{16,20},{20,16},{24,28},{28,24},{1,5},{5... | collective-permute-start | bytes 196616 | tf_op jit(solution)/shard_map/ppermute | solution.py:101
  11.6 1.3 %collective-permute-start.6 = (bf16[128,256]{1,0:T(8,128)(2,1)S(1)}, bf16[128,256]{1,0:T(8,128)(2,1)S(1)}, u32[]{:S(2)}, u32[]{:S(2)}) collective-permute-start(bf16[128,256]{1,0:T(8,128)(2,1)S(1)} %collective-permute-done.refs_3_), channel_id=1, source_target_pairs={{0,4},{4,0},{8,12},{12,8},{16,20},{20,16},{24,28},{28,24},{1,5},{5... | collective-permute-start | bytes 196616 | tf_op jit(solution)/shard_map/ppermute | solution.py:101
  12.9 7.7 %copy-start.1 = (bf16[256,256]{1,0:T(8,128)(2,1)S(1)}, bf16[256,256]{1,0:T(8,128)(2,1)}, u32[]{:S(2)}) copy-start(bf16[256,256]{1,0:T(8,128)(2,1)} %weight_ref.1) | copy-start | bytes 393220
  12.9 7.7 %copy-start.3 = (bf16[128,256]{1,0:T(8,128)(2,1)S(1)}, bf16[128,256]{1,0:T(8,128)(2,1)}, u32[]{:S(2)}) copy-start(bf16[128,256]{1,0:T(8,128)(2,1)} %cot_ref.1) | copy-start | bytes 196612
  13.3 5.3 %collective-permute-start.7 = (bf16[128,256]{1,0:T(8,128)(2,1)S(1)}, bf16[128,256]{1,0:T(8,128)(2,1)S(1)}, u32[]{:S(2)}, u32[]{:S(2)}) collective-permute-start(bf16[128,256]{1,0:T(8,128)(2,1)S(1)} %get-tuple-element.38), channel_id=1, source_target_pairs={{0,3},{1,2},{2,1},{3,0},{4,7},{5,6},{6,5},{7,4},{8,11},{9,10},{10,... | collective-permute-start | bytes 196616 | tf_op jit(solution)/shard_map/ppermute | solution.py:101
  15.8 4.3 %collective-permute-start.8 = (bf16[128,256]{1,0:T(8,128)(2,1)S(1)}, bf16[128,256]{1,0:T(8,128)(2,1)S(1)}, u32[]{:S(2)}, u32[]{:S(2)}) collective-permute-start(bf16[128,256]{1,0:T(8,128)(2,1)S(1)} %get-tuple-element.39), channel_id=1, source_target_pairs={{0,2},{1,3},{2,0},{3,1},{4,6},{5,7},{6,4},{7,5},{8,10},{9,11},{10,... | collective-permute-start | bytes 196616 | tf_op jit(solution)/shard_map/ppermute | solution.py:101
  16.3 4.3 %collective-permute-start.9 = (bf16[128,256]{1,0:T(8,128)(2,1)S(1)}, bf16[128,256]{1,0:T(8,128)(2,1)S(1)}, u32[]{:S(2)}, u32[]{:S(2)}) collective-permute-start(bf16[128,256]{1,0:T(8,128)(2,1)S(1)} %get-tuple-element.40), channel_id=1, source_target_pairs={{0,1},{1,0},{2,3},{3,2},{4,5},{5,4},{6,7},{7,6},{8,9},{9,8},{10,11... | collective-permute-start | bytes 196616 | tf_op jit(solution)/shard_map/ppermute | solution.py:101
  21.0 1.4 %collective-permute-start.10 = (bf16[256,256]{1,0:T(8,128)(2,1)S(1)}, bf16[256,256]{1,0:T(8,128)(2,1)S(1)}, u32[]{:S(2)}, u32[]{:S(2)}) collective-permute-start(bf16[256,256]{1,0:T(8,128)(2,1)S(1)} %get-tuple-element.42), channel_id=1, source_target_pairs={{0,4},{4,0},{8,12},{12,8},{16,20},{20,16},{24,28},{28,24},{1,5},{5... | collective-permute-start | bytes 393224 | tf_op jit(solution)/shard_map/ppermute | solution.py:101
  22.5 6.5 %collective-permute-start.11 = (bf16[192,256]{1,0:T(8,128)(2,1)S(1)}, bf16[192,256]{1,0:T(8,128)(2,1)S(1)}, u32[]{:S(2)}, u32[]{:S(2)}) collective-permute-start(bf16[192,256]{1,0:T(8,128)(2,1)S(1)} %get-tuple-element.45), channel_id=1, source_target_pairs={{0,8},{1,9},{2,10},{3,11},{4,7},{5,6},{6,5},{7,4},{8,16},{9,17},{1... | collective-permute-start | bytes 294920 | tf_op jit(solution)/shard_map/ppermute | solution.py:267
  24.2 6.9 %collective-permute-start.12 = (bf16[192,256]{1,0:T(8,128)(2,1)S(1)}, bf16[192,256]{1,0:T(8,128)(2,1)S(1)}, u32[]{:S(2)}, u32[]{:S(2)}) collective-permute-start(bf16[192,256]{1,0:T(8,128)(2,1)S(1)} %get-tuple-element.46), channel_id=1, source_target_pairs={{0,16},{1,17},{2,18},{3,19},{4,6},{5,7},{6,4},{7,5},{8,24},{9,25},... | collective-permute-start | bytes 294920 | tf_op jit(solution)/shard_map/ppermute | solution.py:267
  26.3 4.8 %collective-permute-start.13 = (bf16[192,256]{1,0:T(8,128)(2,1)S(1)}, bf16[192,256]{1,0:T(8,128)(2,1)S(1)}, u32[]{:S(2)}, u32[]{:S(2)}) collective-permute-start(bf16[192,256]{1,0:T(8,128)(2,1)S(1)} %get-tuple-element.47), channel_id=1, source_target_pairs={{0,24},{1,25},{2,26},{3,27},{4,5},{5,4},{6,7},{7,6},{8,0},{9,1},{1... | collective-permute-start | bytes 294920 | tf_op jit(solution)/shard_map/ppermute | solution.py:267
  31.2 5.6 %collective-permute-start.14 = (bf16[192,256]{1,0:T(8,128)(2,1)S(1)}, bf16[192,256]{1,0:T(8,128)(2,1)S(1)}, u32[]{:S(2)}, u32[]{:S(2)}) collective-permute-start(bf16[192,256]{1,0:T(8,128)(2,1)S(1)} %get-tuple-element.49), channel_id=1, source_target_pairs={{0,3},{1,2},{2,1},{3,0},{4,12},{5,13},{6,14},{7,15},{8,11},{9,10},... | collective-permute-start | bytes 294920 | tf_op jit(solution)/shard_map/ppermute | solution.py:267
  32.7 5.1 %collective-permute-start.15 = (bf16[192,256]{1,0:T(8,128)(2,1)S(1)}, bf16[192,256]{1,0:T(8,128)(2,1)S(1)}, u32[]{:S(2)}, u32[]{:S(2)}) collective-permute-start(bf16[192,256]{1,0:T(8,128)(2,1)S(1)} %get-tuple-element.50), channel_id=1, source_target_pairs={{0,2},{1,3},{2,0},{3,1},{4,20},{5,21},{6,22},{7,23},{8,10},{9,11},... | collective-permute-start | bytes 294920 | tf_op jit(solution)/shard_map/ppermute | solution.py:267
  33.5 4.8 %collective-permute-start.16 = (bf16[192,256]{1,0:T(8,128)(2,1)S(1)}, bf16[192,256]{1,0:T(8,128)(2,1)S(1)}, u32[]{:S(2)}, u32[]{:S(2)}) collective-permute-start(bf16[192,256]{1,0:T(8,128)(2,1)S(1)} %get-tuple-element.51), channel_id=1, source_target_pairs={{0,1},{1,0},{2,3},{3,2},{4,28},{5,29},{6,30},{7,31},{8,9},{9,8},{1... | collective-permute-start | bytes 294920 | tf_op jit(solution)/shard_map/ppermute | solution.py:267
  38.4 1.3 %collective-permute-start.17 = (bf16[128,256]{1,0:T(8,128)(2,1)S(1)}, bf16[128,256]{1,0:T(8,128)(2,1)S(1)}, u32[]{:S(2)}, u32[]{:S(2)}) collective-permute-start(bf16[128,256]{1,0:T(8,128)(2,1)S(1)} %third.1.own_ref), channel_id=1, source_target_pairs={{0,4},{4,0},{8,12},{12,8},{16,20},{20,16},{24,28},{28,24},{1,5},{5... | collective-permute-start | bytes 196616 | tf_op jit(solution)/shard_map/ppermute | solution.py:101

commit v23 on v22

--- a/solution.py
+++ b/solution.py
@@ -67,12 +67,7 @@
     depth = src_ref.shape[1]
     section, rep = lax.axis_index("section"), lax.axis_index("rep")
     chip, chips = place_of_chip()
-    sources = [chip]
-    for route in routes(chips):
-        source = jnp.int32(0)
-        for c, to in enumerate(route):
-            source = jnp.where(chip == to, c, source)
-        sources.append(source)
+    sources = [chip] + [source_of(route, chip) for route in routes(chips)]
     for i, ref in enumerate(block_refs):
         held[2 * sources[i % chips] + ((section + i // chips) & 1)] = ref[...]
     for j, out_ref in zip([0] + across(len(out_refs)), out_refs):
@@ -167,9 +162,12 @@
 
     @pl.when(core != core_along)
     def _():
-        by_xor = [own_ref[...].astype(jnp.float32)]
-        by_xor += [ref[2 * slots :].astype(jnp.float32) for ref in message_refs[::-1]]
-        half_ref[...] = tree_sum(by_xor[:n_rep]).astype(jnp.bfloat16)
+        rep = lax.axis_index("rep")
+        held[rep] = own_ref[...]
+        for route, ref in zip(rep_routes(n_rep, 1 + core_along), message_refs):
+            held[source_of(route, rep)] = ref[2 * slots :]
+        total = tree_sum([held[r].astype(jnp.float32) for r in range(n_rep)])
+        half_ref[...] = total.astype(jnp.bfloat16)
 
 
 def first_kernel(slots, same_ref, kept_ref, came_ref, half_ref, *out_refs):
@@ -256,14 +254,15 @@
     )(own, came)
 
 
-def exchange(value, core_along, shift, j):
+def exchange(value, core_along, shift):
     n_section, n_rep = lax.axis_size("section"), lax.axis_size("rep")
+    over = rep_routes(n_rep, 1 + core_along)[(shift - 1) % (n_rep - 1)]
     pairs = []
     for s in range(n_section):
         along = s & 1 == core_along
         to = (s + 2 * shift) % n_section if along else s
         for r in range(n_rep):
-            pairs.append((s * n_rep + r, to * n_rep + (r if along else r ^ j % n_rep)))
+            pairs.append((s * n_rep + r, to * n_rep + (r if along else over[r])))
     return lax.ppermute(value, ("section", "rep"), pairs)
 
 
@@ -273,6 +272,19 @@
     return [tuple((c + i) % chips for c in range(chips)) for i in range(1, chips)]
 
 
+def rep_routes(n, phase):
+    if n == 4 and phase == 2:
+        return [(1, 0, 3, 2), (2, 3, 1, 0), (3, 2, 0, 1)]
+    return [tuple(r ^ j for r in range(n)) for j in across(n)]
+
+
+def source_of(route, place):
+    source = jnp.int32(0)
+    for c, to in enumerate(route):
+        source = jnp.where(place == to, c, source)
+    return source
+
+
 def send_along(value, axis, route):
     pairs = [(s, 2 * route[s // 2] + s % 2) for s in range(lax.axis_size(axis))]
     return lax.ppermute(value, axis, pairs)
@@ -282,8 +294,7 @@
     chips = lax.axis_size(axis) // 2
     near = [features] + [send_along(features, axis, route) for route in routes(chips)]
     beside = swap(features, axis, 1)
-    came, ready = lax.optimization_barrier((near[:0:-1], ready))
-    near[1:] = came[::-1]
+    near[1], ready = lax.optimization_barrier((near[1], ready))
     return near, [beside] + [swap(block, axis, 1) for block in near[1:]], ready
 
 
@@ -303,11 +314,11 @@
     chips = n_section // 2
     steps = across(max(n_rep, chips))
     half_shape = (width // 2, width)
-    held = [(chips,) + half_shape]
+    held = [(max(n_rep, chips),) + half_shape]
     half, *first = call_halves(
         functools.partial(first_kernel, slots), "first", [same, kept, came], half_shape, slots, len(steps)
     )
-    first = [exchange(m, 0, i + 1, j) for i, (m, j) in enumerate(zip(first, steps))]
+    first = [exchange(m, 0, i + 1) for i, m in enumerate(first)]
     relaid = store(0, same, came, first, n_section, slots)
     half, *second = call_halves(
         functools.partial(second_kernel, slots, n_rep, len(steps)),
@@ -318,7 +329,7 @@
         len(steps),
         held,
     )
-    second = [exchange(m, 1, i + 1, j) for i, (m, j) in enumerate(zip(second, steps))]
+    second = [exchange(m, 1, i + 1) for i, m in enumerate(second)]
     (half,) = call_halves(
         functools.partial(third_kernel, slots, n_rep), "third", [half, *second], half_shape, slots, 0, held
     )

time: 40.6 us -> 41.2 us (1.015)
  starting transfers between devices: 20.8 us -> 21.4 us
    ppermute x6, starting transfers between devices: 9.4 us -> 9.85 us  [exchange(): return lax.ppermute(value, ('section', 'rep'), pairs)]
where the time goes in v23:
time: 41.2 us; the launch traced here: 41 us
  starting transfers between devices  21.4 us (52%)
  waiting for transfers between devices  13.6 us (33%)
  Pallas kernels  2.69 us (7%)
  local copies, waits for them, and re-layouts  2.55 us (6%)
  between operations  0.74 us (2%)
    ppermute x6, starting transfers between devices, exchange(): return lax.ppermute(value, ('section', 'rep'), pairs)  9.85 us
    ppermute x9, waiting for transfers between devices, swap(): lax.ppermute(value, axis, [(i, i ^ j) for i in range(lax.axis_size(axis))])  7.3 us
    ppermute x3, starting transfers between devices, send_along(): return lax.ppermute(value, axis, pairs)  7.13 us
    ppermute x6, waiting for transfers between devices, exchange(): return lax.ppermute(value, ('section', 'rep'), pairs)  5.94 us
    ppermute x9, starting transfers between devices, swap(): lax.ppermute(value, axis, [(i, i ^ j) for i in range(lax.axis_size(axis))])  4.46 us
    unnamed x12, local copies, waits for them, and re-layouts  2.55 us
  transfers between devices with their start and end apart: 18, of which 15 were waited for; matrix products, arithmetic and copies ran while one was open for 0% of the time, Pallas kernels for 2%

profile of v23, /device:TPU:0, one launch (start us, length us, event | category | flops | bytes accessed | tf_op | source)
XLA Modules:
  0.0 41.0 jit_solution(2124928655465216352)
XLA Ops:
  0.6 3.1 %collective-permute-start = (bf16[128,256]{1,0:T(8,128)(2,1)}, bf16[128,256]{1,0:T(8,128)(2,1)S(1)}, u32[]{:S(2)}, u32[]{:S(2)}) collective-permute-start(bf16[128,256]{1,0:T(8,128)(2,1)} %own_ref.1), channel_id=1, source_target_pairs={{0,8},{4,12},{8,24},{12,28},{16,0},{20,4},{24,16},{28,20},{1,9},{5... | collective-permute-start | bytes 196616 | tf_op jit(solution)/shard_map/ppermute | solution.py:290
  3.7 2.5 %collective-permute-start.1 = (bf16[128,256]{1,0:T(8,128)(2,1)}, bf16[128,256]{1,0:T(8,128)(2,1)S(1)}, u32[]{:S(2)}, u32[]{:S(2)}) collective-permute-start(bf16[128,256]{1,0:T(8,128)(2,1)} %own_ref.1), channel_id=1, source_target_pairs={{0,24},{4,28},{8,16},{12,20},{16,8},{20,12},{24,0},{28,4},{1,25},{... | collective-permute-start | bytes 196616 | tf_op jit(solution)/shard_map/ppermute | solution.py:290
  6.2 1.6 %collective-permute-start.2 = (bf16[128,256]{1,0:T(8,128)(2,1)}, bf16[128,256]{1,0:T(8,128)(2,1)S(1)}, u32[]{:S(2)}, u32[]{:S(2)}) collective-permute-start(bf16[128,256]{1,0:T(8,128)(2,1)} %own_ref.1), channel_id=1, source_target_pairs={{0,16},{4,20},{8,0},{12,4},{16,24},{20,28},{24,8},{28,12},{1,17},{... | collective-permute-start | bytes 196616 | tf_op jit(solution)/shard_map/ppermute | solution.py:290
  7.8 0.0 collective-permute-start.3
  7.8 0.7 %copy-done.5 = s32[128,1]{0,1:T(1,128)S(1)} copy-done((s32[128,1]{0,1:T(1,128)S(1)}, s32[128,1]{0,1:T(1,128)}, u32[]{:S(2)}) %copy-start.5) | copy-done | bytes 536
  8.4 1.0 %copy-done = bf16[4,1,4,128,128]{4,3,2,1,0:T(8,128)(2,1)S(1)} copy-done((bf16[4,1,4,128,128]{4,3,2,1,0:T(8,128)(2,1)S(1)}, bf16[4,1,4,128,128]{4,3,2,1,0:T(8,128)(2,1)}, u32[]{:S(2)}) %copy-start) | copy-done | bytes 524312
  9.5 0.8 %copy-done.2 = bf16[128,256]{1,0:T(8,128)(2,1)S(1)} copy-done((bf16[128,256]{1,0:T(8,128)(2,1)S(1)}, bf16[128,256]{1,0:T(8,128)(2,1)}, u32[]{:S(2)}) %copy-start.2) | copy-done | bytes 65560
  10.3 0.2 prepare.1
  10.5 0.0 collective-permute-done.refs_1_
  10.5 0.0 copy-start.4
  10.5 0.3 collective-permute-done.1.refs_2_
  10.9 0.3 collective-permute-start.5
  11.1 0.0 collective-permute-done.2.refs_3_
  11.1 0.3 collective-permute-start.6
  11.4 0.3 collective-permute-start.4
  11.6 0.0 collective-permute-done.3.refs_4_
  11.7 0.5 %collective-permute-done.5.refs_6_ = bf16[128,256]{1,0:T(8,128)(2,1)S(1)} collective-permute-done((bf16[128,256]{1,0:T(8,128)(2,1)S(1)}, bf16[128,256]{1,0:T(8,128)(2,1)S(1)}, u32[]{:S(2)}, u32[]{:S(2)}) %collective-permute-start.5) | collective-permute-done | bytes 65568 | tf_op jit(solution)/shard_map/ppermute | solution.py:96
  12.1 0.3 collective-permute-done.6.refs_7_
  12.4 0.3 collective-permute-done.4.refs_5_
  12.6 0.0 copy-done.4
  12.7 0.4 %partials.1 = (bf16[128,256]{1,0:T(8,128)(2,1)S(1)}, bf16[128,256]{1,0:T(8,128)(2,1)S(1)}, bf16[128,256]{1,0:T(8,128)(2,1)S(1)}, bf16[128,256]{1,0:T(8,128)(2,1)S(1)}) custom-call(s32[4,4]{1,0:T(4,128)S(1)} %bitcast.6, bf16[4,128,512]{2,1,0:T(8,128)(2,1)S(1)} %get-tuple-element.30.wide_ref, bf16[128,256]{1,0:T(8,128)(2,1)S(1)} %get-tuple-element.31.refs_0_, ...), custom_call_target="tpu_custom_call" | custom-call | tf_op jit(solution)/shard_map/partials/pallas_call | solution.py:84
  13.1 2.5 %collective-permute-start.7 = (bf16[128,256]{1,0:T(8,128)(2,1)S(1)}, bf16[128,256]{1,0:T(8,128)(2,1)S(1)}, u32[]{:S(2)}, u32[]{:S(2)}) collective-permute-start(bf16[128,256]{1,0:T(8,128)(2,1)S(1)} %get-tuple-element.34), channel_id=1, source_target_pairs={{0,3},{1,2},{2,1},{3,0},{4,7},{5,6},{6,5},{7,4},{8,11},{9,10},{10,... | collective-permute-start | bytes 196616 | tf_op jit(solution)/shard_map/ppermute | solution.py:96
  15.6 0.5 %collective-permute-start.8 = (bf16[128,256]{1,0:T(8,128)(2,1)S(1)}, bf16[128,256]{1,0:T(8,128)(2,1)S(1)}, u32[]{:S(2)}, u32[]{:S(2)}) collective-permute-start(bf16[128,256]{1,0:T(8,128)(2,1)S(1)} %get-tuple-element.35), channel_id=1, source_target_pairs={{0,2},{1,3},{2,0},{3,1},{4,6},{5,7},{6,4},{7,5},{8,10},{9,11},{10,... | collective-permute-start | bytes 196616 | tf_op jit(solution)/shard_map/ppermute | solution.py:96
  16.1 0.5 %collective-permute-start.9 = (bf16[128,256]{1,0:T(8,128)(2,1)S(1)}, bf16[128,256]{1,0:T(8,128)(2,1)S(1)}, u32[]{:S(2)}, u32[]{:S(2)}) collective-permute-start(bf16[128,256]{1,0:T(8,128)(2,1)S(1)} %get-tuple-element.36), channel_id=1, source_target_pairs={{0,1},{1,0},{2,3},{3,2},{4,5},{5,4},{6,7},{7,6},{8,9},{9,8},{10,11... | collective-permute-start | bytes 196616 | tf_op jit(solution)/shard_map/ppermute | solution.py:96
  16.6 1.7 %collective-permute-done.7.refs_1_ = bf16[128,256]{1,0:T(8,128)(2,1)S(1)} collective-permute-done((bf16[128,256]{1,0:T(8,128)(2,1)S(1)}, bf16[128,256]{1,0:T(8,128)(2,1)S(1)}, u32[]{:S(2)}, u32[]{:S(2)}) %collective-permute-start.7) | collective-permute-done | bytes 65568 | tf_op jit(solution)/shard_map/ppermute | solution.py:96
  18.3 1.5 %collective-permute-done.8.refs_2_ = bf16[128,256]{1,0:T(8,128)(2,1)S(1)} collective-permute-done((bf16[128,256]{1,0:T(8,128)(2,1)S(1)}, bf16[128,256]{1,0:T(8,128)(2,1)S(1)}, u32[]{:S(2)}, u32[]{:S(2)}) %collective-permute-start.8) | collective-permute-done | bytes 65568 | tf_op jit(solution)/shard_map/ppermute | solution.py:96
  19.9 0.5 %collective-permute-done.9.refs_3_ = bf16[128,256]{1,0:T(8,128)(2,1)S(1)} collective-permute-done((bf16[128,256]{1,0:T(8,128)(2,1)S(1)}, bf16[128,256]{1,0:T(8,128)(2,1)S(1)}, u32[]{:S(2)}, u32[]{:S(2)}) %collective-permute-start.9) | collective-permute-done | bytes 65568 | tf_op jit(solution)/shard_map/ppermute | solution.py:96
  20.4 0.4 %dense.1 = (bf16[128,256]{1,0:T(8,128)(2,1)S(1)}, f32[128,256]{1,0:T(8,128)S(1)}, bf16[256,256]{1,0:T(8,128)(2,1)S(1)}) custom-call(bf16[256,256]{1,0:T(8,128)(2,1)S(1)} %copy-done.1, bf16[128,256]{1,0:T(8,128)(2,1)S(1)} %copy-done.3, bf16[256,128]{1,0:T(8,128)(2,1)S(1)} %get-tuple-element.29.placing_ref, bf16[128,256]{1,0:T(8,128)(2,1)S(1)} %get-tuple-element.33.refs_0_, ...), custom_call_target="tpu_custom_call" | custom-call | tf_op jit(solution)/shard_map/dense/pallas_call | solution.py:128
  20.8 0.1 collective-permute-start.10
  20.9 1.3 %collective-permute-done.10.came_ref.refs_1_ = bf16[256,256]{1,0:T(8,128)(2,1)S(1)} collective-permute-done((bf16[256,256]{1,0:T(8,128)(2,1)S(1)}, bf16[256,256]{1,0:T(8,128)(2,1)S(1)}, u32[]{:S(2)}, u32[]{:S(2)}) %collective-permute-start.10) | collective-permute-done | bytes 131104 | tf_op jit(solution)/shard_map/ppermute | solution.py:96
  22.3 1.9 %collective-permute-start.11 = (bf16[192,256]{1,0:T(8,128)(2,1)S(1)}, bf16[192,256]{1,0:T(8,128)(2,1)S(1)}, u32[]{:S(2)}, u32[]{:S(2)}) collective-permute-start(bf16[192,256]{1,0:T(8,128)(2,1)S(1)} %get-tuple-element.41), channel_id=1, source_target_pairs={{0,8},{1,9},{2,10},{3,11},{4,7},{5,6},{6,5},{7,4},{8,16},{9,17},{1... | collective-permute-start | bytes 294920 | tf_op jit(solution)/shard_map/ppermute | solution.py:266
  24.2 2.0 %collective-permute-start.12 = (bf16[192,256]{1,0:T(8,128)(2,1)S(1)}, bf16[192,256]{1,0:T(8,128)(2,1)S(1)}, u32[]{:S(2)}, u32[]{:S(2)}) collective-permute-start(bf16[192,256]{1,0:T(8,128)(2,1)S(1)} %get-tuple-element.42), channel_id=1, source_target_pairs={{0,16},{1,17},{2,18},{3,19},{4,6},{5,7},{6,4},{7,5},{8,24},{9,25},... | collective-permute-start | bytes 294920 | tf_op jit(solution)/shard_map/ppermute | solution.py:266
  26.2 2.2 %collective-permute-start.13 = (bf16[192,256]{1,0:T(8,128)(2,1)S(1)}, bf16[192,256]{1,0:T(8,128)(2,1)S(1)}, u32[]{:S(2)}, u32[]{:S(2)}) collective-permute-start(bf16[192,256]{1,0:T(8,128)(2,1)S(1)} %get-tuple-element.43), channel_id=1, source_target_pairs={{0,24},{1,25},{2,26},{3,27},{4,5},{5,4},{6,7},{7,6},{8,0},{9,1},{1... | collective-permute-start | bytes 294920 | tf_op jit(solution)/shard_map/ppermute | solution.py:266
  28.4 0.4 collective-permute-done.11.refs_0_
  28.7 1.0 %collective-permute-done.12.refs_1_ = bf16[192,256]{1,0:T(8,128)(2,1)S(1)} collective-permute-done((bf16[192,256]{1,0:T(8,128)(2,1)S(1)}, bf16[192,256]{1,0:T(8,128)(2,1)S(1)}, u32[]{:S(2)}, u32[]{:S(2)}) %collective-permute-start.12) | collective-permute-done | bytes 98336 | tf_op jit(solution)/shard_map/ppermute | solution.py:266
  29.8 1.2 %collective-permute-done.13.refs_2_ = bf16[192,256]{1,0:T(8,128)(2,1)S(1)} collective-permute-done((bf16[192,256]{1,0:T(8,128)(2,1)S(1)}, bf16[192,256]{1,0:T(8,128)(2,1)S(1)}, u32[]{:S(2)}, u32[]{:S(2)}) %collective-permute-start.13) | collective-permute-done | bytes 98336 | tf_op jit(solution)/shard_map/ppermute | solution.py:266
  30.9 0.1 second.1
  31.0 0.8 %collective-permute-start.14 = (bf16[192,256]{1,0:T(8,128)(2,1)S(1)}, bf16[192,256]{1,0:T(8,128)(2,1)S(1)}, u32[]{:S(2)}, u32[]{:S(2)}) collective-permute-start(bf16[192,256]{1,0:T(8,128)(2,1)S(1)} %get-tuple-element.45), channel_id=1, source_target_pairs={{0,1},{1,0},{2,3},{3,2},{4,12},{5,13},{6,14},{7,15},{8,9},{9,8},{1... | collective-permute-start | bytes 294920 | tf_op jit(solution)/shard_map/ppermute | solution.py:266
  31.9 1.3 %collective-permute-start.15 = (bf16[192,256]{1,0:T(8,128)(2,1)S(1)}, bf16[192,256]{1,0:T(8,128)(2,1)S(1)}, u32[]{:S(2)}, u32[]{:S(2)}) collective-permute-start(bf16[192,256]{1,0:T(8,128)(2,1)S(1)} %get-tuple-element.46), channel_id=1, source_target_pairs={{0,2},{1,3},{2,1},{3,0},{4,20},{5,21},{6,22},{7,23},{8,10},{9,11},... | collective-permute-start | bytes 294920 | tf_op jit(solution)/shard_map/ppermute | solution.py:266
  33.2 1.6 %collective-permute-start.16 = (bf16[192,256]{1,0:T(8,128)(2,1)S(1)}, bf16[192,256]{1,0:T(8,128)(2,1)S(1)}, u32[]{:S(2)}, u32[]{:S(2)}) collective-permute-start(bf16[192,256]{1,0:T(8,128)(2,1)S(1)} %get-tuple-element.47), channel_id=1, source_target_pairs={{0,3},{1,2},{2,0},{3,1},{4,28},{5,29},{6,30},{7,31},{8,11},{9,10},... | collective-permute-start | bytes 294920 | tf_op jit(solution)/shard_map/ppermute | solution.py:266
  34.8 0.7 %store.2._ = bf16[8,32,256]{2,1,0:T(8,128)(2,1)} custom-call(bf16[128,256]{1,0:T(8,128)(2,1)S(1)} %get-tuple-element.37.same_ref.refs_0_, bf16[256,256]{1,0:T(8,128)(2,1)S(1)} %collective-permute-done.10.came_ref.refs_1_, bf16[192,256]{1,0:T(8,128)(2,1)S(1)} %collective-permute-done.11.refs_0_, bf16[192,256]{1,0:T(8,128)(2,1)S(1)} %collective-permute-done.12.refs_1_, ...), custom_call_target="tpu_custom_call" | custom-call | tf_op jit(solution)/shard_map/store/pallas_call | solution.py:228
  35.5 0.2 collective-permute-done.14.refs_0_.refs_2_
  35.7 2.6 %collective-permute-done.15.refs_1_.refs_3_ = bf16[192,256]{1,0:T(8,128)(2,1)S(1)} collective-permute-done((bf16[192,256]{1,0:T(8,128)(2,1)S(1)}, bf16[192,256]{1,0:T(8,128)(2,1)S(1)}, u32[]{:S(2)}, u32[]{:S(2)}) %collective-permute-start.15) | collective-permute-done | bytes 98336 | tf_op jit(solution)/shard_map/ppermute | solution.py:266
  38.3 0.5 %collective-permute-done.16.refs_2_.refs_4_ = bf16[192,256]{1,0:T(8,128)(2,1)S(1)} collective-permute-done((bf16[192,256]{1,0:T(8,128)(2,1)S(1)}, bf16[192,256]{1,0:T(8,128)(2,1)S(1)}, u32[]{:S(2)}, u32[]{:S(2)}) %collective-permute-start.16) | collective-permute-done | bytes 98336 | tf_op jit(solution)/shard_map/ppermute | solution.py:266
  38.8 0.1 third.1.own_ref
  38.9 0.1 collective-permute-start.17
  39.0 1.2 %collective-permute-done.17.came_ref = bf16[128,256]{1,0:T(8,128)(2,1)S(1)} collective-permute-done((bf16[128,256]{1,0:T(8,128)(2,1)S(1)}, bf16[128,256]{1,0:T(8,128)(2,1)S(1)}, u32[]{:S(2)}, u32[]{:S(2)}) %collective-permute-start.17) | collective-permute-done | bytes 65568 | tf_op jit(solution)/shard_map/ppermute | solution.py:96
  40.3 0.7 %finish.1 = f32[2,128,256]{2,1,0:T(8,128)} custom-call(bf16[128,256]{1,0:T(8,128)(2,1)S(1)} %third.1.own_ref, bf16[128,256]{1,0:T(8,128)(2,1)S(1)} %collective-permute-done.17.came_ref), custom_call_target="tpu_custom_call" | custom-call | tf_op jit(solution)/shard_map/finish/pallas_call | solution.py:247
  (9 shorter events, 0.1 us)
Async XLA Ops:
  0.6 9.9 %collective-permute-start = (bf16[128,256]{1,0:T(8,128)(2,1)}, bf16[128,256]{1,0:T(8,128)(2,1)S(1)}, u32[]{:S(2)}, u32[]{:S(2)}) collective-permute-start(bf16[128,256]{1,0:T(8,128)(2,1)} %own_ref.1), channel_id=1, source_target_pairs={{0,8},{4,12},{8,24},{12,28},{16,0},{20,4},{24,16},{28,20},{1,9},{5... | collective-permute-start | bytes 196616 | tf_op jit(solution)/shard_map/ppermute | solution.py:290
  3.7 7.2 %collective-permute-start.1 = (bf16[128,256]{1,0:T(8,128)(2,1)}, bf16[128,256]{1,0:T(8,128)(2,1)S(1)}, u32[]{:S(2)}, u32[]{:S(2)}) collective-permute-start(bf16[128,256]{1,0:T(8,128)(2,1)} %own_ref.1), channel_id=1, source_target_pairs={{0,24},{4,28},{8,16},{12,20},{16,8},{20,12},{24,0},{28,4},{1,25},{... | collective-permute-start | bytes 196616 | tf_op jit(solution)/shard_map/ppermute | solution.py:290
  6.2 5.0 %collective-permute-start.2 = (bf16[128,256]{1,0:T(8,128)(2,1)}, bf16[128,256]{1,0:T(8,128)(2,1)S(1)}, u32[]{:S(2)}, u32[]{:S(2)}) collective-permute-start(bf16[128,256]{1,0:T(8,128)(2,1)} %own_ref.1), channel_id=1, source_target_pairs={{0,16},{4,20},{8,0},{12,4},{16,24},{20,28},{24,8},{28,12},{1,17},{... | collective-permute-start | bytes 196616 | tf_op jit(solution)/shard_map/ppermute | solution.py:290
  7.8 3.9 %collective-permute-start.3 = (bf16[128,256]{1,0:T(8,128)(2,1)}, bf16[128,256]{1,0:T(8,128)(2,1)S(1)}, u32[]{:S(2)}, u32[]{:S(2)}) collective-permute-start(bf16[128,256]{1,0:T(8,128)(2,1)} %own_ref.1), channel_id=1, source_target_pairs={{0,4},{4,0},{8,12},{12,8},{16,20},{20,16},{24,28},{28,24},{1,5},{5... | collective-permute-start | bytes 196616 | tf_op jit(solution)/shard_map/ppermute | solution.py:96
  7.8 0.7 %copy-start.5 = (s32[128,1]{0,1:T(1,128)S(1)}, s32[128,1]{0,1:T(1,128)}, u32[]{:S(2)}) copy-start(s32[128,1]{0,1:T(1,128)} %param.11) | copy-start | bytes 1540
  8.4 1.0 %copy-start = (bf16[4,1,4,128,128]{4,3,2,1,0:T(8,128)(2,1)S(1)}, bf16[4,1,4,128,128]{4,3,2,1,0:T(8,128)(2,1)}, u32[]{:S(2)}) copy-start(bf16[4,1,4,128,128]{4,3,2,1,0:T(8,128)(2,1)} %param.7) | copy-start | bytes 1572868
  9.5 0.8 %copy-start.2 = (bf16[128,256]{1,0:T(8,128)(2,1)S(1)}, bf16[128,256]{1,0:T(8,128)(2,1)}, u32[]{:S(2)}) copy-start(bf16[128,256]{1,0:T(8,128)(2,1)} %own_ref.1) | copy-start | bytes 196612
  10.5 2.1 %copy-start.4 = (s32[4,1,4]{2,1,0:T(1,128)S(1)}, s32[4,1,4]{2,1,0:T(1,128)}, u32[]{:S(2)}) copy-start(s32[4,1,4]{2,1,0:T(1,128)} %param.8) | copy-start | bytes 196
  10.9 1.3 %collective-permute-start.5 = (bf16[128,256]{1,0:T(8,128)(2,1)S(1)}, bf16[128,256]{1,0:T(8,128)(2,1)S(1)}, u32[]{:S(2)}, u32[]{:S(2)}) collective-permute-start(bf16[128,256]{1,0:T(8,128)(2,1)S(1)} %collective-permute-done.1.refs_2_), channel_id=1, source_target_pairs={{0,4},{4,0},{8,12},{12,8},{16,20},{20,16},{24,28},{28,24},{1,5},{5... | collective-permute-start | bytes 196616 | tf_op jit(solution)/shard_map/ppermute | solution.py:96
  11.1 1.3 %collective-permute-start.6 = (bf16[128,256]{1,0:T(8,128)(2,1)S(1)}, bf16[128,256]{1,0:T(8,128)(2,1)S(1)}, u32[]{:S(2)}, u32[]{:S(2)}) collective-permute-start(bf16[128,256]{1,0:T(8,128)(2,1)S(1)} %collective-permute-done.2.refs_3_), channel_id=1, source_target_pairs={{0,4},{4,0},{8,12},{12,8},{16,20},{20,16},{24,28},{28,24},{1,5},{5... | collective-permute-start | bytes 196616 | tf_op jit(solution)/shard_map/ppermute | solution.py:96
  11.4 1.3 %collective-permute-start.4 = (bf16[128,256]{1,0:T(8,128)(2,1)S(1)}, bf16[128,256]{1,0:T(8,128)(2,1)S(1)}, u32[]{:S(2)}, u32[]{:S(2)}) collective-permute-start(bf16[128,256]{1,0:T(8,128)(2,1)S(1)} %collective-permute-done.refs_1_), channel_id=1, source_target_pairs={{0,4},{4,0},{8,12},{12,8},{16,20},{20,16},{24,28},{28,24},{1,5},{5... | collective-permute-start | bytes 196616 | tf_op jit(solution)/shard_map/ppermute | solution.py:96
  12.7 7.7 %copy-start.1 = (bf16[256,256]{1,0:T(8,128)(2,1)S(1)}, bf16[256,256]{1,0:T(8,128)(2,1)}, u32[]{:S(2)}) copy-start(bf16[256,256]{1,0:T(8,128)(2,1)} %weight_ref.1) | copy-start | bytes 393220
  12.7 7.7 %copy-start.3 = (bf16[128,256]{1,0:T(8,128)(2,1)S(1)}, bf16[128,256]{1,0:T(8,128)(2,1)}, u32[]{:S(2)}) copy-start(bf16[128,256]{1,0:T(8,128)(2,1)} %cot_ref.1) | copy-start | bytes 196612
  13.1 5.2 %collective-permute-start.7 = (bf16[128,256]{1,0:T(8,128)(2,1)S(1)}, bf16[128,256]{1,0:T(8,128)(2,1)S(1)}, u32[]{:S(2)}, u32[]{:S(2)}) collective-permute-start(bf16[128,256]{1,0:T(8,128)(2,1)S(1)} %get-tuple-element.34), channel_id=1, source_target_pairs={{0,3},{1,2},{2,1},{3,0},{4,7},{5,6},{6,5},{7,4},{8,11},{9,10},{10,... | collective-permute-start | bytes 196616 | tf_op jit(solution)/shard_map/ppermute | solution.py:96
  15.6 4.3 %collective-permute-start.8 = (bf16[128,256]{1,0:T(8,128)(2,1)S(1)}, bf16[128,256]{1,0:T(8,128)(2,1)S(1)}, u32[]{:S(2)}, u32[]{:S(2)}) collective-permute-start(bf16[128,256]{1,0:T(8,128)(2,1)S(1)} %get-tuple-element.35), channel_id=1, source_target_pairs={{0,2},{1,3},{2,0},{3,1},{4,6},{5,7},{6,4},{7,5},{8,10},{9,11},{10,... | collective-permute-start | bytes 196616 | tf_op jit(solution)/shard_map/ppermute | solution.py:96
  16.1 4.3 %collective-permute-start.9 = (bf16[128,256]{1,0:T(8,128)(2,1)S(1)}, bf16[128,256]{1,0:T(8,128)(2,1)S(1)}, u32[]{:S(2)}, u32[]{:S(2)}) collective-permute-start(bf16[128,256]{1,0:T(8,128)(2,1)S(1)} %get-tuple-element.36), channel_id=1, source_target_pairs={{0,1},{1,0},{2,3},{3,2},{4,5},{5,4},{6,7},{7,6},{8,9},{9,8},{10,11... | collective-permute-start | bytes 196616 | tf_op jit(solution)/shard_map/ppermute | solution.py:96
  20.8 1.4 %collective-permute-start.10 = (bf16[256,256]{1,0:T(8,128)(2,1)S(1)}, bf16[256,256]{1,0:T(8,128)(2,1)S(1)}, u32[]{:S(2)}, u32[]{:S(2)}) collective-permute-start(bf16[256,256]{1,0:T(8,128)(2,1)S(1)} %get-tuple-element.38), channel_id=1, source_target_pairs={{0,4},{4,0},{8,12},{12,8},{16,20},{20,16},{24,28},{28,24},{1,5},{5... | collective-permute-start | bytes 393224 | tf_op jit(solution)/shard_map/ppermute | solution.py:96
  22.3 6.5 %collective-permute-start.11 = (bf16[192,256]{1,0:T(8,128)(2,1)S(1)}, bf16[192,256]{1,0:T(8,128)(2,1)S(1)}, u32[]{:S(2)}, u32[]{:S(2)}) collective-permute-start(bf16[192,256]{1,0:T(8,128)(2,1)S(1)} %get-tuple-element.41), channel_id=1, source_target_pairs={{0,8},{1,9},{2,10},{3,11},{4,7},{5,6},{6,5},{7,4},{8,16},{9,17},{1... | collective-permute-start | bytes 294920 | tf_op jit(solution)/shard_map/ppermute | solution.py:266
  24.2 5.6 %collective-permute-start.12 = (bf16[192,256]{1,0:T(8,128)(2,1)S(1)}, bf16[192,256]{1,0:T(8,128)(2,1)S(1)}, u32[]{:S(2)}, u32[]{:S(2)}) collective-permute-start(bf16[192,256]{1,0:T(8,128)(2,1)S(1)} %get-tuple-element.42), channel_id=1, source_target_pairs={{0,16},{1,17},{2,18},{3,19},{4,6},{5,7},{6,4},{7,5},{8,24},{9,25},... | collective-permute-start | bytes 294920 | tf_op jit(solution)/shard_map/ppermute | solution.py:266
  26.2 4.7 %collective-permute-start.13 = (bf16[192,256]{1,0:T(8,128)(2,1)S(1)}, bf16[192,256]{1,0:T(8,128)(2,1)S(1)}, u32[]{:S(2)}, u32[]{:S(2)}) collective-permute-start(bf16[192,256]{1,0:T(8,128)(2,1)S(1)} %get-tuple-element.43), channel_id=1, source_target_pairs={{0,24},{1,25},{2,26},{3,27},{4,5},{5,4},{6,7},{7,6},{8,0},{9,1},{1... | collective-permute-start | bytes 294920 | tf_op jit(solution)/shard_map/ppermute | solution.py:266
  31.0 4.7 %collective-permute-start.14 = (bf16[192,256]{1,0:T(8,128)(2,1)S(1)}, bf16[192,256]{1,0:T(8,128)(2,1)S(1)}, u32[]{:S(2)}, u32[]{:S(2)}) collective-permute-start(bf16[192,256]{1,0:T(8,128)(2,1)S(1)} %get-tuple-element.45), channel_id=1, source_target_pairs={{0,1},{1,0},{2,3},{3,2},{4,12},{5,13},{6,14},{7,15},{8,9},{9,8},{1... | collective-permute-start | bytes 294920 | tf_op jit(solution)/shard_map/ppermute | solution.py:266
  31.9 6.4 %collective-permute-start.15 = (bf16[192,256]{1,0:T(8,128)(2,1)S(1)}, bf16[192,256]{1,0:T(8,128)(2,1)S(1)}, u32[]{:S(2)}, u32[]{:S(2)}) collective-permute-start(bf16[192,256]{1,0:T(8,128)(2,1)S(1)} %get-tuple-element.46), channel_id=1, source_target_pairs={{0,2},{1,3},{2,1},{3,0},{4,20},{5,21},{6,22},{7,23},{8,10},{9,11},... | collective-permute-start | bytes 294920 | tf_op jit(solution)/shard_map/ppermute | solution.py:266
  33.2 5.7 %collective-permute-start.16 = (bf16[192,256]{1,0:T(8,128)(2,1)S(1)}, bf16[192,256]{1,0:T(8,128)(2,1)S(1)}, u32[]{:S(2)}, u32[]{:S(2)}) collective-permute-start(bf16[192,256]{1,0:T(8,128)(2,1)S(1)} %get-tuple-element.47), channel_id=1, source_target_pairs={{0,3},{1,2},{2,0},{3,1},{4,28},{5,29},{6,30},{7,31},{8,11},{9,10},... | collective-permute-start | bytes 294920 | tf_op jit(solution)/shard_map/ppermute | solution.py:266
  38.9 1.3 %collective-permute-start.17 = (bf16[128,256]{1,0:T(8,128)(2,1)S(1)}, bf16[128,256]{1,0:T(8,128)(2,1)S(1)}, u32[]{:S(2)}, u32[]{:S(2)}) collective-permute-start(bf16[128,256]{1,0:T(8,128)(2,1)S(1)} %third.1.own_ref), channel_id=1, source_target_pairs={{0,4},{4,0},{8,12},{12,8},{16,20},{20,16},{24,28},{28,24},{1,5},{5... | collective-permute-start | bytes 196616 | tf_op jit(solution)/shard_map/ppermute | solution.py:96

commit v24 on v23

--- a/solution.py
+++ b/solution.py
@@ -164,7 +164,7 @@
     def _():
         rep = lax.axis_index("rep")
         held[rep] = own_ref[...]
-        for route, ref in zip(rep_routes(n_rep, 1 + core_along), message_refs):
+        for route, ref in zip(rep_routes(n_rep), message_refs):
             held[source_of(route, rep)] = ref[2 * slots :]
         total = tree_sum([held[r].astype(jnp.float32) for r in range(n_rep)])
         half_ref[...] = total.astype(jnp.bfloat16)
@@ -256,7 +256,7 @@
 
 def exchange(value, core_along, shift):
     n_section, n_rep = lax.axis_size("section"), lax.axis_size("rep")
-    over = rep_routes(n_rep, 1 + core_along)[(shift - 1) % (n_rep - 1)]
+    over = rep_routes(n_rep)[(shift - 1) % (n_rep - 1)]
     pairs = []
     for s in range(n_section):
         along = s & 1 == core_along
@@ -272,9 +272,7 @@
     return [tuple((c + i) % chips for c in range(chips)) for i in range(1, chips)]
 
 
-def rep_routes(n, phase):
-    if n == 4 and phase == 2:
-        return [(1, 0, 3, 2), (2, 3, 1, 0), (3, 2, 0, 1)]
+def rep_routes(n):
     return [tuple(r ^ j for r in range(n)) for j in across(n)]
 
 

time: 41.2 us -> 40.6 us (0.985)
  no operation moved by 1% of the time
where the time goes in v24:
time: 40.6 us; the launch traced here: 40.4 us
  starting transfers between devices  21.2 us (52%)
  waiting for transfers between devices  13.2 us (33%)
  Pallas kernels  2.69 us (7%)
  local copies, waits for them, and re-layouts  2.55 us (6%)
  between operations  0.74 us (2%)
    ppermute x6, starting transfers between devices, exchange(): return lax.ppermute(value, ('section', 'rep'), pairs)  9.63 us
    ppermute x9, waiting for transfers between devices, swap(): lax.ppermute(value, axis, [(i, i ^ j) for i in range(lax.axis_size(axis))])  7.3 us
    ppermute x3, starting transfers between devices, send_along(): return lax.ppermute(value, axis, pairs)  7.13 us
    ppermute x6, waiting for transfers between devices, exchange(): return lax.ppermute(value, ('section', 'rep'), pairs)  5.57 us
    ppermute x9, starting transfers between devices, swap(): lax.ppermute(value, axis, [(i, i ^ j) for i in range(lax.axis_size(axis))])  4.46 us
    unnamed x12, local copies, waits for them, and re-layouts  2.55 us
  transfers between devices with their start and end apart: 18, of which 15 were waited for; matrix products, arithmetic and copies ran while one was open for 0% of the time, Pallas kernels for 2%

profile of v24, /device:TPU:0, one launch (start us, length us, event | category | flops | bytes accessed | tf_op | source)
XLA Modules:
  0.0 40.4 jit_solution(3000054754394077326)
XLA Ops:
  0.6 3.1 %collective-permute-start = (bf16[128,256]{1,0:T(8,128)(2,1)}, bf16[128,256]{1,0:T(8,128)(2,1)S(1)}, u32[]{:S(2)}, u32[]{:S(2)}) collective-permute-start(bf16[128,256]{1,0:T(8,128)(2,1)} %own_ref.1), channel_id=1, source_target_pairs={{0,8},{4,12},{8,24},{12,28},{16,0},{20,4},{24,16},{28,20},{1,9},{5... | collective-permute-start | bytes 196616 | tf_op jit(solution)/shard_map/ppermute | solution.py:288
  3.7 2.5 %collective-permute-start.1 = (bf16[128,256]{1,0:T(8,128)(2,1)}, bf16[128,256]{1,0:T(8,128)(2,1)S(1)}, u32[]{:S(2)}, u32[]{:S(2)}) collective-permute-start(bf16[128,256]{1,0:T(8,128)(2,1)} %own_ref.1), channel_id=1, source_target_pairs={{0,24},{4,28},{8,16},{12,20},{16,8},{20,12},{24,0},{28,4},{1,25},{... | collective-permute-start | bytes 196616 | tf_op jit(solution)/shard_map/ppermute | solution.py:288
  6.2 1.6 %collective-permute-start.2 = (bf16[128,256]{1,0:T(8,128)(2,1)}, bf16[128,256]{1,0:T(8,128)(2,1)S(1)}, u32[]{:S(2)}, u32[]{:S(2)}) collective-permute-start(bf16[128,256]{1,0:T(8,128)(2,1)} %own_ref.1), channel_id=1, source_target_pairs={{0,16},{4,20},{8,0},{12,4},{16,24},{20,28},{24,8},{28,12},{1,17},{... | collective-permute-start | bytes 196616 | tf_op jit(solution)/shard_map/ppermute | solution.py:288
  7.8 0.0 collective-permute-start.3
  7.8 0.7 %copy-done.5 = s32[128,1]{0,1:T(1,128)S(1)} copy-done((s32[128,1]{0,1:T(1,128)S(1)}, s32[128,1]{0,1:T(1,128)}, u32[]{:S(2)}) %copy-start.5) | copy-done | bytes 536
  8.4 1.0 %copy-done = bf16[4,1,4,128,128]{4,3,2,1,0:T(8,128)(2,1)S(1)} copy-done((bf16[4,1,4,128,128]{4,3,2,1,0:T(8,128)(2,1)S(1)}, bf16[4,1,4,128,128]{4,3,2,1,0:T(8,128)(2,1)}, u32[]{:S(2)}) %copy-start) | copy-done | bytes 524312
  9.5 0.8 %copy-done.2 = bf16[128,256]{1,0:T(8,128)(2,1)S(1)} copy-done((bf16[128,256]{1,0:T(8,128)(2,1)S(1)}, bf16[128,256]{1,0:T(8,128)(2,1)}, u32[]{:S(2)}) %copy-start.2) | copy-done | bytes 65560
  10.3 0.2 prepare.1
  10.5 0.0 collective-permute-done.refs_1_
  10.5 0.0 copy-start.4
  10.5 0.3 collective-permute-done.1.refs_2_
  10.9 0.3 collective-permute-start.5
  11.1 0.0 collective-permute-done.2.refs_3_
  11.1 0.3 collective-permute-start.6
  11.4 0.3 collective-permute-start.4
  11.6 0.0 collective-permute-done.3.refs_4_
  11.7 0.5 %collective-permute-done.5.refs_6_ = bf16[128,256]{1,0:T(8,128)(2,1)S(1)} collective-permute-done((bf16[128,256]{1,0:T(8,128)(2,1)S(1)}, bf16[128,256]{1,0:T(8,128)(2,1)S(1)}, u32[]{:S(2)}, u32[]{:S(2)}) %collective-permute-start.5) | collective-permute-done | bytes 65568 | tf_op jit(solution)/shard_map/ppermute | solution.py:96
  12.1 0.3 collective-permute-done.6.refs_7_
  12.4 0.3 collective-permute-done.4.refs_5_
  12.7 0.4 %partials.1 = (bf16[128,256]{1,0:T(8,128)(2,1)S(1)}, bf16[128,256]{1,0:T(8,128)(2,1)S(1)}, bf16[128,256]{1,0:T(8,128)(2,1)S(1)}, bf16[128,256]{1,0:T(8,128)(2,1)S(1)}) custom-call(s32[4,4]{1,0:T(4,128)S(1)} %bitcast.6, bf16[4,128,512]{2,1,0:T(8,128)(2,1)S(1)} %get-tuple-element.30.wide_ref, bf16[128,256]{1,0:T(8,128)(2,1)S(1)} %get-tuple-element.31.refs_0_, ...), custom_call_target="tpu_custom_call" | custom-call | tf_op jit(solution)/shard_map/partials/pallas_call | solution.py:84
  13.1 2.5 %collective-permute-start.7 = (bf16[128,256]{1,0:T(8,128)(2,1)S(1)}, bf16[128,256]{1,0:T(8,128)(2,1)S(1)}, u32[]{:S(2)}, u32[]{:S(2)}) collective-permute-start(bf16[128,256]{1,0:T(8,128)(2,1)S(1)} %get-tuple-element.34), channel_id=1, source_target_pairs={{0,3},{1,2},{2,1},{3,0},{4,7},{5,6},{6,5},{7,4},{8,11},{9,10},{10,... | collective-permute-start | bytes 196616 | tf_op jit(solution)/shard_map/ppermute | solution.py:96
  15.6 0.5 %collective-permute-start.8 = (bf16[128,256]{1,0:T(8,128)(2,1)S(1)}, bf16[128,256]{1,0:T(8,128)(2,1)S(1)}, u32[]{:S(2)}, u32[]{:S(2)}) collective-permute-start(bf16[128,256]{1,0:T(8,128)(2,1)S(1)} %get-tuple-element.35), channel_id=1, source_target_pairs={{0,2},{1,3},{2,0},{3,1},{4,6},{5,7},{6,4},{7,5},{8,10},{9,11},{10,... | collective-permute-start | bytes 196616 | tf_op jit(solution)/shard_map/ppermute | solution.py:96
  16.1 0.5 %collective-permute-start.9 = (bf16[128,256]{1,0:T(8,128)(2,1)S(1)}, bf16[128,256]{1,0:T(8,128)(2,1)S(1)}, u32[]{:S(2)}, u32[]{:S(2)}) collective-permute-start(bf16[128,256]{1,0:T(8,128)(2,1)S(1)} %get-tuple-element.36), channel_id=1, source_target_pairs={{0,1},{1,0},{2,3},{3,2},{4,5},{5,4},{6,7},{7,6},{8,9},{9,8},{10,11... | collective-permute-start | bytes 196616 | tf_op jit(solution)/shard_map/ppermute | solution.py:96
  16.6 1.7 %collective-permute-done.7.refs_1_ = bf16[128,256]{1,0:T(8,128)(2,1)S(1)} collective-permute-done((bf16[128,256]{1,0:T(8,128)(2,1)S(1)}, bf16[128,256]{1,0:T(8,128)(2,1)S(1)}, u32[]{:S(2)}, u32[]{:S(2)}) %collective-permute-start.7) | collective-permute-done | bytes 65568 | tf_op jit(solution)/shard_map/ppermute | solution.py:96
  18.3 1.5 %collective-permute-done.8.refs_2_ = bf16[128,256]{1,0:T(8,128)(2,1)S(1)} collective-permute-done((bf16[128,256]{1,0:T(8,128)(2,1)S(1)}, bf16[128,256]{1,0:T(8,128)(2,1)S(1)}, u32[]{:S(2)}, u32[]{:S(2)}) %collective-permute-start.8) | collective-permute-done | bytes 65568 | tf_op jit(solution)/shard_map/ppermute | solution.py:96
  19.9 0.5 %collective-permute-done.9.refs_3_ = bf16[128,256]{1,0:T(8,128)(2,1)S(1)} collective-permute-done((bf16[128,256]{1,0:T(8,128)(2,1)S(1)}, bf16[128,256]{1,0:T(8,128)(2,1)S(1)}, u32[]{:S(2)}, u32[]{:S(2)}) %collective-permute-start.9) | collective-permute-done | bytes 65568 | tf_op jit(solution)/shard_map/ppermute | solution.py:96
  20.4 0.0 copy-done.3
  20.4 0.4 %dense.1 = (bf16[128,256]{1,0:T(8,128)(2,1)S(1)}, f32[128,256]{1,0:T(8,128)S(1)}, bf16[256,256]{1,0:T(8,128)(2,1)S(1)}) custom-call(bf16[256,256]{1,0:T(8,128)(2,1)S(1)} %copy-done.1, bf16[128,256]{1,0:T(8,128)(2,1)S(1)} %copy-done.3, bf16[256,128]{1,0:T(8,128)(2,1)S(1)} %get-tuple-element.29.placing_ref, bf16[128,256]{1,0:T(8,128)(2,1)S(1)} %get-tuple-element.33.refs_0_, ...), custom_call_target="tpu_custom_call" | custom-call | tf_op jit(solution)/shard_map/dense/pallas_call | solution.py:128
  20.8 0.1 collective-permute-start.10
  20.9 1.3 %collective-permute-done.10.came_ref.refs_1_ = bf16[256,256]{1,0:T(8,128)(2,1)S(1)} collective-permute-done((bf16[256,256]{1,0:T(8,128)(2,1)S(1)}, bf16[256,256]{1,0:T(8,128)(2,1)S(1)}, u32[]{:S(2)}, u32[]{:S(2)}) %collective-permute-start.10) | collective-permute-done | bytes 131104 | tf_op jit(solution)/shard_map/ppermute | solution.py:96
  22.3 1.9 %collective-permute-start.11 = (bf16[192,256]{1,0:T(8,128)(2,1)S(1)}, bf16[192,256]{1,0:T(8,128)(2,1)S(1)}, u32[]{:S(2)}, u32[]{:S(2)}) collective-permute-start(bf16[192,256]{1,0:T(8,128)(2,1)S(1)} %get-tuple-element.41), channel_id=1, source_target_pairs={{0,8},{1,9},{2,10},{3,11},{4,7},{5,6},{6,5},{7,4},{8,16},{9,17},{1... | collective-permute-start | bytes 294920 | tf_op jit(solution)/shard_map/ppermute | solution.py:266
  24.2 2.0 %collective-permute-start.12 = (bf16[192,256]{1,0:T(8,128)(2,1)S(1)}, bf16[192,256]{1,0:T(8,128)(2,1)S(1)}, u32[]{:S(2)}, u32[]{:S(2)}) collective-permute-start(bf16[192,256]{1,0:T(8,128)(2,1)S(1)} %get-tuple-element.42), channel_id=1, source_target_pairs={{0,16},{1,17},{2,18},{3,19},{4,6},{5,7},{6,4},{7,5},{8,24},{9,25},... | collective-permute-start | bytes 294920 | tf_op jit(solution)/shard_map/ppermute | solution.py:266
  26.2 2.2 %collective-permute-start.13 = (bf16[192,256]{1,0:T(8,128)(2,1)S(1)}, bf16[192,256]{1,0:T(8,128)(2,1)S(1)}, u32[]{:S(2)}, u32[]{:S(2)}) collective-permute-start(bf16[192,256]{1,0:T(8,128)(2,1)S(1)} %get-tuple-element.43), channel_id=1, source_target_pairs={{0,24},{1,25},{2,26},{3,27},{4,5},{5,4},{6,7},{7,6},{8,0},{9,1},{1... | collective-permute-start | bytes 294920 | tf_op jit(solution)/shard_map/ppermute | solution.py:266
  28.4 0.4 collective-permute-done.11.refs_0_
  28.7 1.0 %collective-permute-done.12.refs_1_ = bf16[192,256]{1,0:T(8,128)(2,1)S(1)} collective-permute-done((bf16[192,256]{1,0:T(8,128)(2,1)S(1)}, bf16[192,256]{1,0:T(8,128)(2,1)S(1)}, u32[]{:S(2)}, u32[]{:S(2)}) %collective-permute-start.12) | collective-permute-done | bytes 98336 | tf_op jit(solution)/shard_map/ppermute | solution.py:266
  29.8 1.2 %collective-permute-done.13.refs_2_ = bf16[192,256]{1,0:T(8,128)(2,1)S(1)} collective-permute-done((bf16[192,256]{1,0:T(8,128)(2,1)S(1)}, bf16[192,256]{1,0:T(8,128)(2,1)S(1)}, u32[]{:S(2)}, u32[]{:S(2)}) %collective-permute-start.13) | collective-permute-done | bytes 98336 | tf_op jit(solution)/shard_map/ppermute | solution.py:266
  30.9 0.1 second.1
  31.0 1.4 %collective-permute-start.14 = (bf16[192,256]{1,0:T(8,128)(2,1)S(1)}, bf16[192,256]{1,0:T(8,128)(2,1)S(1)}, u32[]{:S(2)}, u32[]{:S(2)}) collective-permute-start(bf16[192,256]{1,0:T(8,128)(2,1)S(1)} %get-tuple-element.45), channel_id=1, source_target_pairs={{0,3},{1,2},{2,1},{3,0},{4,12},{5,13},{6,14},{7,15},{8,11},{9,10},... | collective-permute-start | bytes 294920 | tf_op jit(solution)/shard_map/ppermute | solution.py:266
  32.5 0.9 %collective-permute-start.15 = (bf16[192,256]{1,0:T(8,128)(2,1)S(1)}, bf16[192,256]{1,0:T(8,128)(2,1)S(1)}, u32[]{:S(2)}, u32[]{:S(2)}) collective-permute-start(bf16[192,256]{1,0:T(8,128)(2,1)S(1)} %get-tuple-element.46), channel_id=1, source_target_pairs={{0,2},{1,3},{2,0},{3,1},{4,20},{5,21},{6,22},{7,23},{8,10},{9,11},... | collective-permute-start | bytes 294920 | tf_op jit(solution)/shard_map/ppermute | solution.py:266
  33.3 1.3 %collective-permute-start.16 = (bf16[192,256]{1,0:T(8,128)(2,1)S(1)}, bf16[192,256]{1,0:T(8,128)(2,1)S(1)}, u32[]{:S(2)}, u32[]{:S(2)}) collective-permute-start(bf16[192,256]{1,0:T(8,128)(2,1)S(1)} %get-tuple-element.47), channel_id=1, source_target_pairs={{0,1},{1,0},{2,3},{3,2},{4,28},{5,29},{6,30},{7,31},{8,9},{9,8},{1... | collective-permute-start | bytes 294920 | tf_op jit(solution)/shard_map/ppermute | solution.py:266
  34.6 0.7 %store.2._ = bf16[8,32,256]{2,1,0:T(8,128)(2,1)} custom-call(bf16[128,256]{1,0:T(8,128)(2,1)S(1)} %get-tuple-element.37.same_ref.refs_0_, bf16[256,256]{1,0:T(8,128)(2,1)S(1)} %collective-permute-done.10.came_ref.refs_1_, bf16[192,256]{1,0:T(8,128)(2,1)S(1)} %collective-permute-done.11.refs_0_, bf16[192,256]{1,0:T(8,128)(2,1)S(1)} %collective-permute-done.12.refs_1_, ...), custom_call_target="tpu_custom_call" | custom-call | tf_op jit(solution)/shard_map/store/pallas_call | solution.py:228
  35.3 1.4 %collective-permute-done.14.refs_0_.refs_2_ = bf16[192,256]{1,0:T(8,128)(2,1)S(1)} collective-permute-done((bf16[192,256]{1,0:T(8,128)(2,1)S(1)}, bf16[192,256]{1,0:T(8,128)(2,1)S(1)}, u32[]{:S(2)}, u32[]{:S(2)}) %collective-permute-start.14) | collective-permute-done | bytes 98336 | tf_op jit(solution)/shard_map/ppermute | solution.py:266
  36.7 1.0 %collective-permute-done.15.refs_1_.refs_3_ = bf16[192,256]{1,0:T(8,128)(2,1)S(1)} collective-permute-done((bf16[192,256]{1,0:T(8,128)(2,1)S(1)}, bf16[192,256]{1,0:T(8,128)(2,1)S(1)}, u32[]{:S(2)}, u32[]{:S(2)}) %collective-permute-start.15) | collective-permute-done | bytes 98336 | tf_op jit(solution)/shard_map/ppermute | solution.py:266
  37.7 0.6 %collective-permute-done.16.refs_2_.refs_4_ = bf16[192,256]{1,0:T(8,128)(2,1)S(1)} collective-permute-done((bf16[192,256]{1,0:T(8,128)(2,1)S(1)}, bf16[192,256]{1,0:T(8,128)(2,1)S(1)}, u32[]{:S(2)}, u32[]{:S(2)}) %collective-permute-start.16) | collective-permute-done | bytes 98336 | tf_op jit(solution)/shard_map/ppermute | solution.py:266
  38.3 0.1 third.1.own_ref
  38.4 0.1 collective-permute-start.17
  38.4 1.2 %collective-permute-done.17.came_ref = bf16[128,256]{1,0:T(8,128)(2,1)S(1)} collective-permute-done((bf16[128,256]{1,0:T(8,128)(2,1)S(1)}, bf16[128,256]{1,0:T(8,128)(2,1)S(1)}, u32[]{:S(2)}, u32[]{:S(2)}) %collective-permute-start.17) | collective-permute-done | bytes 65568 | tf_op jit(solution)/shard_map/ppermute | solution.py:96
  39.7 0.7 %finish.1 = f32[2,128,256]{2,1,0:T(8,128)} custom-call(bf16[128,256]{1,0:T(8,128)(2,1)S(1)} %third.1.own_ref, bf16[128,256]{1,0:T(8,128)(2,1)S(1)} %collective-permute-done.17.came_ref), custom_call_target="tpu_custom_call" | custom-call | tf_op jit(solution)/shard_map/finish/pallas_call | solution.py:247
  (9 shorter events, 0.1 us)
Async XLA Ops:
  0.6 9.9 %collective-permute-start = (bf16[128,256]{1,0:T(8,128)(2,1)}, bf16[128,256]{1,0:T(8,128)(2,1)S(1)}, u32[]{:S(2)}, u32[]{:S(2)}) collective-permute-start(bf16[128,256]{1,0:T(8,128)(2,1)} %own_ref.1), channel_id=1, source_target_pairs={{0,8},{4,12},{8,24},{12,28},{16,0},{20,4},{24,16},{28,20},{1,9},{5... | collective-permute-start | bytes 196616 | tf_op jit(solution)/shard_map/ppermute | solution.py:288
  3.7 7.2 %collective-permute-start.1 = (bf16[128,256]{1,0:T(8,128)(2,1)}, bf16[128,256]{1,0:T(8,128)(2,1)S(1)}, u32[]{:S(2)}, u32[]{:S(2)}) collective-permute-start(bf16[128,256]{1,0:T(8,128)(2,1)} %own_ref.1), channel_id=1, source_target_pairs={{0,24},{4,28},{8,16},{12,20},{16,8},{20,12},{24,0},{28,4},{1,25},{... | collective-permute-start | bytes 196616 | tf_op jit(solution)/shard_map/ppermute | solution.py:288
  6.2 5.0 %collective-permute-start.2 = (bf16[128,256]{1,0:T(8,128)(2,1)}, bf16[128,256]{1,0:T(8,128)(2,1)S(1)}, u32[]{:S(2)}, u32[]{:S(2)}) collective-permute-start(bf16[128,256]{1,0:T(8,128)(2,1)} %own_ref.1), channel_id=1, source_target_pairs={{0,16},{4,20},{8,0},{12,4},{16,24},{20,28},{24,8},{28,12},{1,17},{... | collective-permute-start | bytes 196616 | tf_op jit(solution)/shard_map/ppermute | solution.py:288
  7.8 3.9 %collective-permute-start.3 = (bf16[128,256]{1,0:T(8,128)(2,1)}, bf16[128,256]{1,0:T(8,128)(2,1)S(1)}, u32[]{:S(2)}, u32[]{:S(2)}) collective-permute-start(bf16[128,256]{1,0:T(8,128)(2,1)} %own_ref.1), channel_id=1, source_target_pairs={{0,4},{4,0},{8,12},{12,8},{16,20},{20,16},{24,28},{28,24},{1,5},{5... | collective-permute-start | bytes 196616 | tf_op jit(solution)/shard_map/ppermute | solution.py:96
  7.8 0.7 %copy-start.5 = (s32[128,1]{0,1:T(1,128)S(1)}, s32[128,1]{0,1:T(1,128)}, u32[]{:S(2)}) copy-start(s32[128,1]{0,1:T(1,128)} %param.11) | copy-start | bytes 1540
  8.4 1.0 %copy-start = (bf16[4,1,4,128,128]{4,3,2,1,0:T(8,128)(2,1)S(1)}, bf16[4,1,4,128,128]{4,3,2,1,0:T(8,128)(2,1)}, u32[]{:S(2)}) copy-start(bf16[4,1,4,128,128]{4,3,2,1,0:T(8,128)(2,1)} %param.7) | copy-start | bytes 1572868
  9.5 0.8 %copy-start.2 = (bf16[128,256]{1,0:T(8,128)(2,1)S(1)}, bf16[128,256]{1,0:T(8,128)(2,1)}, u32[]{:S(2)}) copy-start(bf16[128,256]{1,0:T(8,128)(2,1)} %own_ref.1) | copy-start | bytes 196612
  10.5 2.1 %copy-start.4 = (s32[4,1,4]{2,1,0:T(1,128)S(1)}, s32[4,1,4]{2,1,0:T(1,128)}, u32[]{:S(2)}) copy-start(s32[4,1,4]{2,1,0:T(1,128)} %param.8) | copy-start | bytes 196
  10.9 1.3 %collective-permute-start.5 = (bf16[128,256]{1,0:T(8,128)(2,1)S(1)}, bf16[128,256]{1,0:T(8,128)(2,1)S(1)}, u32[]{:S(2)}, u32[]{:S(2)}) collective-permute-start(bf16[128,256]{1,0:T(8,128)(2,1)S(1)} %collective-permute-done.1.refs_2_), channel_id=1, source_target_pairs={{0,4},{4,0},{8,12},{12,8},{16,20},{20,16},{24,28},{28,24},{1,5},{5... | collective-permute-start | bytes 196616 | tf_op jit(solution)/shard_map/ppermute | solution.py:96
  11.1 1.3 %collective-permute-start.6 = (bf16[128,256]{1,0:T(8,128)(2,1)S(1)}, bf16[128,256]{1,0:T(8,128)(2,1)S(1)}, u32[]{:S(2)}, u32[]{:S(2)}) collective-permute-start(bf16[128,256]{1,0:T(8,128)(2,1)S(1)} %collective-permute-done.2.refs_3_), channel_id=1, source_target_pairs={{0,4},{4,0},{8,12},{12,8},{16,20},{20,16},{24,28},{28,24},{1,5},{5... | collective-permute-start | bytes 196616 | tf_op jit(solution)/shard_map/ppermute | solution.py:96
  11.4 1.3 %collective-permute-start.4 = (bf16[128,256]{1,0:T(8,128)(2,1)S(1)}, bf16[128,256]{1,0:T(8,128)(2,1)S(1)}, u32[]{:S(2)}, u32[]{:S(2)}) collective-permute-start(bf16[128,256]{1,0:T(8,128)(2,1)S(1)} %collective-permute-done.refs_1_), channel_id=1, source_target_pairs={{0,4},{4,0},{8,12},{12,8},{16,20},{20,16},{24,28},{28,24},{1,5},{5... | collective-permute-start | bytes 196616 | tf_op jit(solution)/shard_map/ppermute | solution.py:96
  12.7 7.7 %copy-start.1 = (bf16[256,256]{1,0:T(8,128)(2,1)S(1)}, bf16[256,256]{1,0:T(8,128)(2,1)}, u32[]{:S(2)}) copy-start(bf16[256,256]{1,0:T(8,128)(2,1)} %weight_ref.1) | copy-start | bytes 393220
  12.7 7.7 %copy-start.3 = (bf16[128,256]{1,0:T(8,128)(2,1)S(1)}, bf16[128,256]{1,0:T(8,128)(2,1)}, u32[]{:S(2)}) copy-start(bf16[128,256]{1,0:T(8,128)(2,1)} %cot_ref.1) | copy-start | bytes 196612
  13.1 5.2 %collective-permute-start.7 = (bf16[128,256]{1,0:T(8,128)(2,1)S(1)}, bf16[128,256]{1,0:T(8,128)(2,1)S(1)}, u32[]{:S(2)}, u32[]{:S(2)}) collective-permute-start(bf16[128,256]{1,0:T(8,128)(2,1)S(1)} %get-tuple-element.34), channel_id=1, source_target_pairs={{0,3},{1,2},{2,1},{3,0},{4,7},{5,6},{6,5},{7,4},{8,11},{9,10},{10,... | collective-permute-start | bytes 196616 | tf_op jit(solution)/shard_map/ppermute | solution.py:96
  15.6 4.3 %collective-permute-start.8 = (bf16[128,256]{1,0:T(8,128)(2,1)S(1)}, bf16[128,256]{1,0:T(8,128)(2,1)S(1)}, u32[]{:S(2)}, u32[]{:S(2)}) collective-permute-start(bf16[128,256]{1,0:T(8,128)(2,1)S(1)} %get-tuple-element.35), channel_id=1, source_target_pairs={{0,2},{1,3},{2,0},{3,1},{4,6},{5,7},{6,4},{7,5},{8,10},{9,11},{10,... | collective-permute-start | bytes 196616 | tf_op jit(solution)/shard_map/ppermute | solution.py:96
  16.1 4.3 %collective-permute-start.9 = (bf16[128,256]{1,0:T(8,128)(2,1)S(1)}, bf16[128,256]{1,0:T(8,128)(2,1)S(1)}, u32[]{:S(2)}, u32[]{:S(2)}) collective-permute-start(bf16[128,256]{1,0:T(8,128)(2,1)S(1)} %get-tuple-element.36), channel_id=1, source_target_pairs={{0,1},{1,0},{2,3},{3,2},{4,5},{5,4},{6,7},{7,6},{8,9},{9,8},{10,11... | collective-permute-start | bytes 196616 | tf_op jit(solution)/shard_map/ppermute | solution.py:96
  20.8 1.4 %collective-permute-start.10 = (bf16[256,256]{1,0:T(8,128)(2,1)S(1)}, bf16[256,256]{1,0:T(8,128)(2,1)S(1)}, u32[]{:S(2)}, u32[]{:S(2)}) collective-permute-start(bf16[256,256]{1,0:T(8,128)(2,1)S(1)} %get-tuple-element.38), channel_id=1, source_target_pairs={{0,4},{4,0},{8,12},{12,8},{16,20},{20,16},{24,28},{28,24},{1,5},{5... | collective-permute-start | bytes 393224 | tf_op jit(solution)/shard_map/ppermute | solution.py:96
  22.3 6.5 %collective-permute-start.11 = (bf16[192,256]{1,0:T(8,128)(2,1)S(1)}, bf16[192,256]{1,0:T(8,128)(2,1)S(1)}, u32[]{:S(2)}, u32[]{:S(2)}) collective-permute-start(bf16[192,256]{1,0:T(8,128)(2,1)S(1)} %get-tuple-element.41), channel_id=1, source_target_pairs={{0,8},{1,9},{2,10},{3,11},{4,7},{5,6},{6,5},{7,4},{8,16},{9,17},{1... | collective-permute-start | bytes 294920 | tf_op jit(solution)/shard_map/ppermute | solution.py:266
  24.2 5.6 %collective-permute-start.12 = (bf16[192,256]{1,0:T(8,128)(2,1)S(1)}, bf16[192,256]{1,0:T(8,128)(2,1)S(1)}, u32[]{:S(2)}, u32[]{:S(2)}) collective-permute-start(bf16[192,256]{1,0:T(8,128)(2,1)S(1)} %get-tuple-element.42), channel_id=1, source_target_pairs={{0,16},{1,17},{2,18},{3,19},{4,6},{5,7},{6,4},{7,5},{8,24},{9,25},... | collective-permute-start | bytes 294920 | tf_op jit(solution)/shard_map/ppermute | solution.py:266
  26.2 4.7 %collective-permute-start.13 = (bf16[192,256]{1,0:T(8,128)(2,1)S(1)}, bf16[192,256]{1,0:T(8,128)(2,1)S(1)}, u32[]{:S(2)}, u32[]{:S(2)}) collective-permute-start(bf16[192,256]{1,0:T(8,128)(2,1)S(1)} %get-tuple-element.43), channel_id=1, source_target_pairs={{0,24},{1,25},{2,26},{3,27},{4,5},{5,4},{6,7},{7,6},{8,0},{9,1},{1... | collective-permute-start | bytes 294920 | tf_op jit(solution)/shard_map/ppermute | solution.py:266
  31.0 5.6 %collective-permute-start.14 = (bf16[192,256]{1,0:T(8,128)(2,1)S(1)}, bf16[192,256]{1,0:T(8,128)(2,1)S(1)}, u32[]{:S(2)}, u32[]{:S(2)}) collective-permute-start(bf16[192,256]{1,0:T(8,128)(2,1)S(1)} %get-tuple-element.45), channel_id=1, source_target_pairs={{0,3},{1,2},{2,1},{3,0},{4,12},{5,13},{6,14},{7,15},{8,11},{9,10},... | collective-permute-start | bytes 294920 | tf_op jit(solution)/shard_map/ppermute | solution.py:266
  32.5 5.2 %collective-permute-start.15 = (bf16[192,256]{1,0:T(8,128)(2,1)S(1)}, bf16[192,256]{1,0:T(8,128)(2,1)S(1)}, u32[]{:S(2)}, u32[]{:S(2)}) collective-permute-start(bf16[192,256]{1,0:T(8,128)(2,1)S(1)} %get-tuple-element.46), channel_id=1, source_target_pairs={{0,2},{1,3},{2,0},{3,1},{4,20},{5,21},{6,22},{7,23},{8,10},{9,11},... | collective-permute-start | bytes 294920 | tf_op jit(solution)/shard_map/ppermute | solution.py:266
  33.3 4.9 %collective-permute-start.16 = (bf16[192,256]{1,0:T(8,128)(2,1)S(1)}, bf16[192,256]{1,0:T(8,128)(2,1)S(1)}, u32[]{:S(2)}, u32[]{:S(2)}) collective-permute-start(bf16[192,256]{1,0:T(8,128)(2,1)S(1)} %get-tuple-element.47), channel_id=1, source_target_pairs={{0,1},{1,0},{2,3},{3,2},{4,28},{5,29},{6,30},{7,31},{8,9},{9,8},{1... | collective-permute-start | bytes 294920 | tf_op jit(solution)/shard_map/ppermute | solution.py:266
  38.4 1.3 %collective-permute-start.17 = (bf16[128,256]{1,0:T(8,128)(2,1)S(1)}, bf16[128,256]{1,0:T(8,128)(2,1)S(1)}, u32[]{:S(2)}, u32[]{:S(2)}) collective-permute-start(bf16[128,256]{1,0:T(8,128)(2,1)S(1)} %third.1.own_ref), channel_id=1, source_target_pairs={{0,4},{4,0},{8,12},{12,8},{16,20},{20,16},{24,28},{28,24},{1,5},{5... | collective-permute-start | bytes 196616 | tf_op jit(solution)/shard_map/ppermute | solution.py:96

commit v25 on v15

--- a/solution.py
+++ b/solution.py
@@ -66,11 +66,13 @@
     block_refs, out_refs, held = refs[:count], refs[count:-1], refs[-1]
     depth = src_ref.shape[1]
     section, rep = lax.axis_index("section"), lax.axis_index("rep")
-    for j in range(count):
-        held[j] = block_refs[j][...]
+    chip, chips = place_of_chip()
+    sources = [chip] + [source_of(route, chip) for route in routes(chips)]
+    for i, ref in enumerate(block_refs):
+        held[2 * sources[i % chips] + ((section + i // chips) & 1)] = ref[...]
     for j, out_ref in zip([0] + across(len(out_refs)), out_refs):
         g = rep ^ j
-        right = jnp.concatenate([held[src_ref[g, k] ^ section] for k in range(depth)], axis=0)
+        right = jnp.concatenate([held[src_ref[g, k]] for k in range(depth)], axis=0)
         out_ref[...] = jnp.dot(wide_ref[g], right, preferred_element_type=jnp.float32).astype(
             jnp.bfloat16
         )
@@ -301,20 +303,30 @@
     return lax.ppermute(value, ("section", "rep"), pairs)
 
 
+def routes(chips):
+    if chips == 4:
+        return [(1, 3, 0, 2), (3, 2, 1, 0), (2, 0, 3, 1)]
+    return [tuple((c + i) % chips for c in range(chips)) for i in range(1, chips)]
+
+
+def source_of(route, place):
+    source = jnp.int32(0)
+    for c, to in enumerate(route):
+        source = jnp.where(place == to, c, source)
+    return source
+
+
+def send_along(value, axis, route):
+    pairs = [(s, 2 * route[s // 2] + s % 2) for s in range(lax.axis_size(axis))]
+    return lax.ppermute(value, axis, pairs)
+
+
 def gather_blocks(features, axis, ready):
-    n = lax.axis_size(axis)
-    blocks = [None] * n
-    blocks[0] = features
-    order = sorted(range(2, n, 2), key=lambda j: (j & 4, -(j & 2)))
-    for j in order:
-        blocks[j] = swap(features, axis, j)
-    blocks[1] = swap(features, axis, 1)
-    came, ready = lax.optimization_barrier(([blocks[j] for j in order], ready))
-    for j, block in zip(order, came):
-        blocks[j] = block
-    for j in range(2, n, 2):
-        blocks[j + 1] = swap(blocks[j], axis, 1)
-    return blocks, ready
+    chips = lax.axis_size(axis) // 2
+    near = [features] + [send_along(features, axis, route) for route in routes(chips)]
+    beside = swap(features, axis, 1)
+    near[1], ready = lax.optimization_barrier((near[1], ready))
+    return near, [beside] + [swap(block, axis, 1) for block in near[1:]], ready
 
 
 def per_device(features, adj_tiles, adj_src, cotangent, weight, destination):
@@ -324,8 +336,8 @@
     slots = max(2, 2 * rows_here // n_section)
     target = destination.reshape(1, rows_here)
     wide, own, placing = prepare(adj_tiles[:, 0], features, target, n_section * slots, slots)
-    blocks, (wide, own, placing) = gather_blocks(features, "section", (wide, own, placing))
-    parts = list(partials(adj_src[:, 0], wide, [own] + blocks[1:]))
+    near, beside, (wide, own, placing) = gather_blocks(features, "section", (wide, own, placing))
+    parts = list(partials(adj_src[:, 0], wide, [own] + near[1:] + beside))
     others = across(n_rep)
     parts = parts[:1] + [swap(part, "rep", j) for part, j in zip(parts[1:], others)]
     same, term, sent = dense(parts, weight, cotangent, placing, slots)

time: 40.6 us -> 40.7 us (level)
  starting transfers between devices: 19.1 us -> 21.2 us
  waiting for transfers between devices: 15.4 us -> 13.4 us
    ppermute x0 -> x3, starting transfers between devices: none -> 7.13 us  [send_along(): return lax.ppermute(value, axis, pairs)]
    ppermute x12 -> x9, starting transfers between devices: 9.89 us -> 4.46 us  [swap(): lax.ppermute(value, axis, [(i, i ^ j) for i in range(lax.axis_size(axis))])]
    ppermute x12 -> x9, waiting for transfers between devices: 9.76 us -> 7.35 us  [swap(): lax.ppermute(value, axis, [(i, i ^ j) for i in range(lax.axis_size(axis))])]
    ppermute x6, starting transfers between devices: 9.2 us -> 9.63 us  [exchange(): return lax.ppermute(value, ('section', 'rep'), pairs)]
  transfers between devices with their start and end apart: 18 -> 18, of which waited for: 16 -> 15; matrix products, arithmetic and copies ran while one was open for 0% -> 0% of each run, Pallas kernels for 2% -> 2%
where the time goes in v25:
time: 40.7 us; the launch traced here: 40.5 us
  starting transfers between devices  21.2 us (52%)
  waiting for transfers between devices  13.4 us (33%)
  Pallas kernels  2.61 us (6%)
  local copies, waits for them, and re-layouts  2.55 us (6%)
  between operations  0.74 us (2%)
    ppermute x6, starting transfers between devices, exchange(): return lax.ppermute(value, ('section', 'rep'), pairs)  9.63 us
    ppermute x9, waiting for transfers between devices, swap(): lax.ppermute(value, axis, [(i, i ^ j) for i in range(lax.axis_size(axis))])  7.35 us
    ppermute x3, starting transfers between devices, send_along(): return lax.ppermute(value, axis, pairs)  7.13 us
    ppermute x6, waiting for transfers between devices, exchange(): return lax.ppermute(value, ('section', 'rep'), pairs)  5.68 us
    ppermute x9, starting transfers between devices, swap(): lax.ppermute(value, axis, [(i, i ^ j) for i in range(lax.axis_size(axis))])  4.46 us
    unnamed x12, local copies, waits for them, and re-layouts  2.55 us
  transfers between devices with their start and end apart: 18, of which 15 were waited for; matrix products, arithmetic and copies ran while one was open for 0% of the time, Pallas kernels for 2%

profile of v25, /device:TPU:0, one launch (start us, length us, event | category | flops | bytes accessed | tf_op | source)
XLA Modules:
  0.0 40.5 jit_solution(14835040288066426599)
XLA Ops:
  0.6 3.1 %collective-permute-start = (bf16[128,256]{1,0:T(8,128)(2,1)}, bf16[128,256]{1,0:T(8,128)(2,1)S(1)}, u32[]{:S(2)}, u32[]{:S(2)}) collective-permute-start(bf16[128,256]{1,0:T(8,128)(2,1)} %own_ref.1), channel_id=1, source_target_pairs={{0,8},{4,12},{8,24},{12,28},{16,0},{20,4},{24,16},{28,20},{1,9},{5... | collective-permute-start | bytes 196616 | tf_op jit(solution)/shard_map/ppermute | solution.py:321
  3.7 2.5 %collective-permute-start.1 = (bf16[128,256]{1,0:T(8,128)(2,1)}, bf16[128,256]{1,0:T(8,128)(2,1)S(1)}, u32[]{:S(2)}, u32[]{:S(2)}) collective-permute-start(bf16[128,256]{1,0:T(8,128)(2,1)} %own_ref.1), channel_id=1, source_target_pairs={{0,24},{4,28},{8,16},{12,20},{16,8},{20,12},{24,0},{28,4},{1,25},{... | collective-permute-start | bytes 196616 | tf_op jit(solution)/shard_map/ppermute | solution.py:321
  6.2 1.6 %collective-permute-start.2 = (bf16[128,256]{1,0:T(8,128)(2,1)}, bf16[128,256]{1,0:T(8,128)(2,1)S(1)}, u32[]{:S(2)}, u32[]{:S(2)}) collective-permute-start(bf16[128,256]{1,0:T(8,128)(2,1)} %own_ref.1), channel_id=1, source_target_pairs={{0,16},{4,20},{8,0},{12,4},{16,24},{20,28},{24,8},{28,12},{1,17},{... | collective-permute-start | bytes 196616 | tf_op jit(solution)/shard_map/ppermute | solution.py:321
  7.8 0.0 collective-permute-start.3
  7.8 0.7 %copy-done.5 = s32[128,1]{0,1:T(1,128)S(1)} copy-done((s32[128,1]{0,1:T(1,128)S(1)}, s32[128,1]{0,1:T(1,128)}, u32[]{:S(2)}) %copy-start.5) | copy-done | bytes 536
  8.4 1.0 %copy-done = bf16[4,1,4,128,128]{4,3,2,1,0:T(8,128)(2,1)S(1)} copy-done((bf16[4,1,4,128,128]{4,3,2,1,0:T(8,128)(2,1)S(1)}, bf16[4,1,4,128,128]{4,3,2,1,0:T(8,128)(2,1)}, u32[]{:S(2)}) %copy-start) | copy-done | bytes 524312
  9.5 0.8 %copy-done.2 = bf16[128,256]{1,0:T(8,128)(2,1)S(1)} copy-done((bf16[128,256]{1,0:T(8,128)(2,1)S(1)}, bf16[128,256]{1,0:T(8,128)(2,1)}, u32[]{:S(2)}) %copy-start.2) | copy-done | bytes 65560
  10.3 0.2 prepare.1
  10.5 0.0 collective-permute-done.refs_1_
  10.5 0.0 copy-start.4
  10.5 0.3 collective-permute-done.1.refs_2_
  10.9 0.3 collective-permute-start.5
  11.1 0.0 collective-permute-done.2.refs_3_
  11.1 0.3 collective-permute-start.6
  11.4 0.3 collective-permute-start.4
  11.6 0.0 collective-permute-done.3.refs_4_
  11.7 0.5 %collective-permute-done.5.refs_6_ = bf16[128,256]{1,0:T(8,128)(2,1)S(1)} collective-permute-done((bf16[128,256]{1,0:T(8,128)(2,1)S(1)}, bf16[128,256]{1,0:T(8,128)(2,1)S(1)}, u32[]{:S(2)}, u32[]{:S(2)}) %collective-permute-start.5) | collective-permute-done | bytes 65568 | tf_op jit(solution)/shard_map/ppermute | solution.py:96
  12.1 0.3 collective-permute-done.6.refs_7_
  12.4 0.3 collective-permute-done.4.refs_5_
  12.6 0.0 copy-done.4
  12.7 0.4 %partials.1 = (bf16[128,256]{1,0:T(8,128)(2,1)S(1)}, bf16[128,256]{1,0:T(8,128)(2,1)S(1)}, bf16[128,256]{1,0:T(8,128)(2,1)S(1)}, bf16[128,256]{1,0:T(8,128)(2,1)S(1)}) custom-call(s32[4,4]{1,0:T(4,128)S(1)} %bitcast.5, bf16[4,128,512]{2,1,0:T(8,128)(2,1)S(1)} %get-tuple-element.30.wide_ref, bf16[128,256]{1,0:T(8,128)(2,1)S(1)} %get-tuple-element.31.refs_0_, ...), custom_call_target="tpu_custom_call" | custom-call | tf_op jit(solution)/shard_map/partials/pallas_call | solution.py:84
  13.1 2.5 %collective-permute-start.7 = (bf16[128,256]{1,0:T(8,128)(2,1)S(1)}, bf16[128,256]{1,0:T(8,128)(2,1)S(1)}, u32[]{:S(2)}, u32[]{:S(2)}) collective-permute-start(bf16[128,256]{1,0:T(8,128)(2,1)S(1)} %get-tuple-element.34), channel_id=1, source_target_pairs={{0,3},{1,2},{2,1},{3,0},{4,7},{5,6},{6,5},{7,4},{8,11},{9,10},{10,... | collective-permute-start | bytes 196616 | tf_op jit(solution)/shard_map/ppermute | solution.py:96
  15.6 0.5 %collective-permute-start.8 = (bf16[128,256]{1,0:T(8,128)(2,1)S(1)}, bf16[128,256]{1,0:T(8,128)(2,1)S(1)}, u32[]{:S(2)}, u32[]{:S(2)}) collective-permute-start(bf16[128,256]{1,0:T(8,128)(2,1)S(1)} %get-tuple-element.35), channel_id=1, source_target_pairs={{0,2},{1,3},{2,0},{3,1},{4,6},{5,7},{6,4},{7,5},{8,10},{9,11},{10,... | collective-permute-start | bytes 196616 | tf_op jit(solution)/shard_map/ppermute | solution.py:96
  16.1 0.5 %collective-permute-start.9 = (bf16[128,256]{1,0:T(8,128)(2,1)S(1)}, bf16[128,256]{1,0:T(8,128)(2,1)S(1)}, u32[]{:S(2)}, u32[]{:S(2)}) collective-permute-start(bf16[128,256]{1,0:T(8,128)(2,1)S(1)} %get-tuple-element.36), channel_id=1, source_target_pairs={{0,1},{1,0},{2,3},{3,2},{4,5},{5,4},{6,7},{7,6},{8,9},{9,8},{10,11... | collective-permute-start | bytes 196616 | tf_op jit(solution)/shard_map/ppermute | solution.py:96
  16.6 1.7 %collective-permute-done.7.refs_1_ = bf16[128,256]{1,0:T(8,128)(2,1)S(1)} collective-permute-done((bf16[128,256]{1,0:T(8,128)(2,1)S(1)}, bf16[128,256]{1,0:T(8,128)(2,1)S(1)}, u32[]{:S(2)}, u32[]{:S(2)}) %collective-permute-start.7) | collective-permute-done | bytes 65568 | tf_op jit(solution)/shard_map/ppermute | solution.py:96
  18.3 1.5 %collective-permute-done.8.refs_2_ = bf16[128,256]{1,0:T(8,128)(2,1)S(1)} collective-permute-done((bf16[128,256]{1,0:T(8,128)(2,1)S(1)}, bf16[128,256]{1,0:T(8,128)(2,1)S(1)}, u32[]{:S(2)}, u32[]{:S(2)}) %collective-permute-start.8) | collective-permute-done | bytes 65568 | tf_op jit(solution)/shard_map/ppermute | solution.py:96
  19.9 0.5 %collective-permute-done.9.refs_3_ = bf16[128,256]{1,0:T(8,128)(2,1)S(1)} collective-permute-done((bf16[128,256]{1,0:T(8,128)(2,1)S(1)}, bf16[128,256]{1,0:T(8,128)(2,1)S(1)}, u32[]{:S(2)}, u32[]{:S(2)}) %collective-permute-start.9) | collective-permute-done | bytes 65568 | tf_op jit(solution)/shard_map/ppermute | solution.py:96
  20.4 0.0 copy-done.1
  20.4 0.4 %dense.1 = (bf16[128,256]{1,0:T(8,128)(2,1)S(1)}, f32[256,256]{1,0:T(8,128)S(1)}, bf16[288,256]{1,0:T(8,128)(2,1)S(1)}) custom-call(bf16[256,256]{1,0:T(8,128)(2,1)S(1)} %copy-done.1, bf16[128,256]{1,0:T(8,128)(2,1)S(1)} %copy-done.3, bf16[256,128]{1,0:T(8,128)(2,1)S(1)} %get-tuple-element.29.placing_ref, bf16[128,256]{1,0:T(8,128)(2,1)S(1)} %get-tuple-element.33.refs_0_, ...), custom_call_target="tpu_custom_call" | custom-call | tf_op jit(solution)/shard_map/dense/pallas_call | solution.py:140
  20.8 0.1 collective-permute-start.10
  20.9 1.4 %collective-permute-done.10.came_ref.refs_1_ = bf16[288,256]{1,0:T(8,128)(2,1)S(1)} collective-permute-done((bf16[288,256]{1,0:T(8,128)(2,1)S(1)}, bf16[288,256]{1,0:T(8,128)(2,1)S(1)}, u32[]{:S(2)}, u32[]{:S(2)}) %collective-permute-start.10) | collective-permute-done | bytes 147488 | tf_op jit(solution)/shard_map/ppermute | solution.py:96
  22.3 1.9 %collective-permute-start.11 = (bf16[160,256]{1,0:T(8,128)(2,1)S(1)}, bf16[160,256]{1,0:T(8,128)(2,1)S(1)}, u32[]{:S(2)}, u32[]{:S(2)}) collective-permute-start(bf16[160,256]{1,0:T(8,128)(2,1)S(1)} %get-tuple-element.41), channel_id=1, source_target_pairs={{0,8},{1,9},{2,10},{3,11},{4,7},{5,6},{6,5},{7,4},{8,16},{9,17},{1... | collective-permute-start | bytes 245768 | tf_op jit(solution)/shard_map/ppermute | solution.py:303
  24.2 2.0 %collective-permute-start.12 = (bf16[160,256]{1,0:T(8,128)(2,1)S(1)}, bf16[160,256]{1,0:T(8,128)(2,1)S(1)}, u32[]{:S(2)}, u32[]{:S(2)}) collective-permute-start(bf16[160,256]{1,0:T(8,128)(2,1)S(1)} %get-tuple-element.42), channel_id=1, source_target_pairs={{0,16},{1,17},{2,18},{3,19},{4,6},{5,7},{6,4},{7,5},{8,24},{9,25},... | collective-permute-start | bytes 245768 | tf_op jit(solution)/shard_map/ppermute | solution.py:303
  26.2 2.2 %collective-permute-start.13 = (bf16[160,256]{1,0:T(8,128)(2,1)S(1)}, bf16[160,256]{1,0:T(8,128)(2,1)S(1)}, u32[]{:S(2)}, u32[]{:S(2)}) collective-permute-start(bf16[160,256]{1,0:T(8,128)(2,1)S(1)} %get-tuple-element.43), channel_id=1, source_target_pairs={{0,24},{1,25},{2,26},{3,27},{4,5},{5,4},{6,7},{7,6},{8,0},{9,1},{1... | collective-permute-start | bytes 245768 | tf_op jit(solution)/shard_map/ppermute | solution.py:303
  28.4 0.2 collective-permute-done.11.refs_0_
  28.6 0.9 %collective-permute-done.12.refs_1_ = bf16[160,256]{1,0:T(8,128)(2,1)S(1)} collective-permute-done((bf16[160,256]{1,0:T(8,128)(2,1)S(1)}, bf16[160,256]{1,0:T(8,128)(2,1)S(1)}, u32[]{:S(2)}, u32[]{:S(2)}) %collective-permute-start.12) | collective-permute-done | bytes 81952 | tf_op jit(solution)/shard_map/ppermute | solution.py:303
  29.5 1.5 %collective-permute-done.13.refs_2_ = bf16[160,256]{1,0:T(8,128)(2,1)S(1)} collective-permute-done((bf16[160,256]{1,0:T(8,128)(2,1)S(1)}, bf16[160,256]{1,0:T(8,128)(2,1)S(1)}, u32[]{:S(2)}, u32[]{:S(2)}) %collective-permute-start.13) | collective-permute-done | bytes 81952 | tf_op jit(solution)/shard_map/ppermute | solution.py:303
  31.0 0.1 second.1
  31.0 1.2 %collective-permute-start.14 = (bf16[224,256]{1,0:T(8,128)(2,1)S(1)}, bf16[224,256]{1,0:T(8,128)(2,1)S(1)}, u32[]{:S(2)}, u32[]{:S(2)}) collective-permute-start(bf16[224,256]{1,0:T(8,128)(2,1)S(1)} %get-tuple-element.45), channel_id=1, source_target_pairs={{0,3},{1,2},{2,1},{3,0},{4,12},{5,13},{6,14},{7,15},{8,11},{9,10},... | collective-permute-start | bytes 344072 | tf_op jit(solution)/shard_map/ppermute | solution.py:303
  32.3 0.8 %collective-permute-start.15 = (bf16[224,256]{1,0:T(8,128)(2,1)S(1)}, bf16[224,256]{1,0:T(8,128)(2,1)S(1)}, u32[]{:S(2)}, u32[]{:S(2)}) collective-permute-start(bf16[224,256]{1,0:T(8,128)(2,1)S(1)} %get-tuple-element.46), channel_id=1, source_target_pairs={{0,2},{1,3},{2,0},{3,1},{4,20},{5,21},{6,22},{7,23},{8,10},{9,11},... | collective-permute-start | bytes 344072 | tf_op jit(solution)/shard_map/ppermute | solution.py:303
  33.1 1.5 %collective-permute-start.16 = (bf16[224,256]{1,0:T(8,128)(2,1)S(1)}, bf16[224,256]{1,0:T(8,128)(2,1)S(1)}, u32[]{:S(2)}, u32[]{:S(2)}) collective-permute-start(bf16[224,256]{1,0:T(8,128)(2,1)S(1)} %get-tuple-element.47), channel_id=1, source_target_pairs={{0,1},{1,0},{2,3},{3,2},{4,28},{5,29},{6,30},{7,31},{8,9},{9,8},{1... | collective-permute-start | bytes 344072 | tf_op jit(solution)/shard_map/ppermute | solution.py:303
  34.6 0.7 %store.2._ = bf16[8,32,256]{2,1,0:T(8,128)(2,1)} custom-call(bf16[128,256]{1,0:T(8,128)(2,1)S(1)} %get-tuple-element.37.same_ref.refs_0_, bf16[288,256]{1,0:T(8,128)(2,1)S(1)} %collective-permute-done.10.came_ref.refs_1_, bf16[160,256]{1,0:T(8,128)(2,1)S(1)} %collective-permute-done.11.refs_0_, bf16[160,256]{1,0:T(8,128)(2,1)S(1)} %collective-permute-done.12.refs_1_, ...), custom_call_target="tpu_custom_call" | custom-call | tf_op jit(solution)/shard_map/store/pallas_call | solution.py:256
  35.3 1.6 %collective-permute-done.14.refs_0_.refs_2_ = bf16[224,256]{1,0:T(8,128)(2,1)S(1)} collective-permute-done((bf16[224,256]{1,0:T(8,128)(2,1)S(1)}, bf16[224,256]{1,0:T(8,128)(2,1)S(1)}, u32[]{:S(2)}, u32[]{:S(2)}) %collective-permute-start.14) | collective-permute-done | bytes 114720 | tf_op jit(solution)/shard_map/ppermute | solution.py:303
  36.9 1.1 %collective-permute-done.15.refs_1_.refs_3_ = bf16[224,256]{1,0:T(8,128)(2,1)S(1)} collective-permute-done((bf16[224,256]{1,0:T(8,128)(2,1)S(1)}, bf16[224,256]{1,0:T(8,128)(2,1)S(1)}, u32[]{:S(2)}, u32[]{:S(2)}) %collective-permute-start.15) | collective-permute-done | bytes 114720 | tf_op jit(solution)/shard_map/ppermute | solution.py:303
  38.0 0.3 collective-permute-done.16.refs_2_.refs_4_
  38.4 0.1 collective-permute-start.17
  38.5 1.3 %collective-permute-done.17.came_ref = bf16[160,256]{1,0:T(8,128)(2,1)S(1)} collective-permute-done((bf16[160,256]{1,0:T(8,128)(2,1)S(1)}, bf16[160,256]{1,0:T(8,128)(2,1)S(1)}, u32[]{:S(2)}, u32[]{:S(2)}) %collective-permute-start.17) | collective-permute-done | bytes 81952 | tf_op jit(solution)/shard_map/ppermute | solution.py:96
  39.8 0.7 %finish.1 = f32[256,256]{1,0:T(8,128)} custom-call(bf16[160,256]{1,0:T(8,128)(2,1)S(1)} %third.1.own_ref, bf16[160,256]{1,0:T(8,128)(2,1)S(1)} %collective-permute-done.17.came_ref), custom_call_target="tpu_custom_call" | custom-call | tf_op jit(solution)/shard_map/finish/pallas_call | solution.py:285
  (9 shorter events, 0.1 us)
Async XLA Ops:
  0.6 9.9 %collective-permute-start = (bf16[128,256]{1,0:T(8,128)(2,1)}, bf16[128,256]{1,0:T(8,128)(2,1)S(1)}, u32[]{:S(2)}, u32[]{:S(2)}) collective-permute-start(bf16[128,256]{1,0:T(8,128)(2,1)} %own_ref.1), channel_id=1, source_target_pairs={{0,8},{4,12},{8,24},{12,28},{16,0},{20,4},{24,16},{28,20},{1,9},{5... | collective-permute-start | bytes 196616 | tf_op jit(solution)/shard_map/ppermute | solution.py:321
  3.7 7.2 %collective-permute-start.1 = (bf16[128,256]{1,0:T(8,128)(2,1)}, bf16[128,256]{1,0:T(8,128)(2,1)S(1)}, u32[]{:S(2)}, u32[]{:S(2)}) collective-permute-start(bf16[128,256]{1,0:T(8,128)(2,1)} %own_ref.1), channel_id=1, source_target_pairs={{0,24},{4,28},{8,16},{12,20},{16,8},{20,12},{24,0},{28,4},{1,25},{... | collective-permute-start | bytes 196616 | tf_op jit(solution)/shard_map/ppermute | solution.py:321
  6.2 5.0 %collective-permute-start.2 = (bf16[128,256]{1,0:T(8,128)(2,1)}, bf16[128,256]{1,0:T(8,128)(2,1)S(1)}, u32[]{:S(2)}, u32[]{:S(2)}) collective-permute-start(bf16[128,256]{1,0:T(8,128)(2,1)} %own_ref.1), channel_id=1, source_target_pairs={{0,16},{4,20},{8,0},{12,4},{16,24},{20,28},{24,8},{28,12},{1,17},{... | collective-permute-start | bytes 196616 | tf_op jit(solution)/shard_map/ppermute | solution.py:321
  7.8 3.9 %collective-permute-start.3 = (bf16[128,256]{1,0:T(8,128)(2,1)}, bf16[128,256]{1,0:T(8,128)(2,1)S(1)}, u32[]{:S(2)}, u32[]{:S(2)}) collective-permute-start(bf16[128,256]{1,0:T(8,128)(2,1)} %own_ref.1), channel_id=1, source_target_pairs={{0,4},{4,0},{8,12},{12,8},{16,20},{20,16},{24,28},{28,24},{1,5},{5... | collective-permute-start | bytes 196616 | tf_op jit(solution)/shard_map/ppermute | solution.py:96
  7.8 0.7 %copy-start.5 = (s32[128,1]{0,1:T(1,128)S(1)}, s32[128,1]{0,1:T(1,128)}, u32[]{:S(2)}) copy-start(s32[128,1]{0,1:T(1,128)} %param.11) | copy-start | bytes 1540
  8.4 1.0 %copy-start = (bf16[4,1,4,128,128]{4,3,2,1,0:T(8,128)(2,1)S(1)}, bf16[4,1,4,128,128]{4,3,2,1,0:T(8,128)(2,1)}, u32[]{:S(2)}) copy-start(bf16[4,1,4,128,128]{4,3,2,1,0:T(8,128)(2,1)} %param.7) | copy-start | bytes 1572868
  9.5 0.8 %copy-start.2 = (bf16[128,256]{1,0:T(8,128)(2,1)S(1)}, bf16[128,256]{1,0:T(8,128)(2,1)}, u32[]{:S(2)}) copy-start(bf16[128,256]{1,0:T(8,128)(2,1)} %own_ref.1) | copy-start | bytes 196612
  10.5 2.1 %copy-start.4 = (s32[4,1,4]{2,1,0:T(1,128)S(1)}, s32[4,1,4]{2,1,0:T(1,128)}, u32[]{:S(2)}) copy-start(s32[4,1,4]{2,1,0:T(1,128)} %param.8) | copy-start | bytes 196
  10.9 1.3 %collective-permute-start.5 = (bf16[128,256]{1,0:T(8,128)(2,1)S(1)}, bf16[128,256]{1,0:T(8,128)(2,1)S(1)}, u32[]{:S(2)}, u32[]{:S(2)}) collective-permute-start(bf16[128,256]{1,0:T(8,128)(2,1)S(1)} %collective-permute-done.1.refs_2_), channel_id=1, source_target_pairs={{0,4},{4,0},{8,12},{12,8},{16,20},{20,16},{24,28},{28,24},{1,5},{5... | collective-permute-start | bytes 196616 | tf_op jit(solution)/shard_map/ppermute | solution.py:96
  11.1 1.3 %collective-permute-start.6 = (bf16[128,256]{1,0:T(8,128)(2,1)S(1)}, bf16[128,256]{1,0:T(8,128)(2,1)S(1)}, u32[]{:S(2)}, u32[]{:S(2)}) collective-permute-start(bf16[128,256]{1,0:T(8,128)(2,1)S(1)} %collective-permute-done.2.refs_3_), channel_id=1, source_target_pairs={{0,4},{4,0},{8,12},{12,8},{16,20},{20,16},{24,28},{28,24},{1,5},{5... | collective-permute-start | bytes 196616 | tf_op jit(solution)/shard_map/ppermute | solution.py:96
  11.4 1.3 %collective-permute-start.4 = (bf16[128,256]{1,0:T(8,128)(2,1)S(1)}, bf16[128,256]{1,0:T(8,128)(2,1)S(1)}, u32[]{:S(2)}, u32[]{:S(2)}) collective-permute-start(bf16[128,256]{1,0:T(8,128)(2,1)S(1)} %collective-permute-done.refs_1_), channel_id=1, source_target_pairs={{0,4},{4,0},{8,12},{12,8},{16,20},{20,16},{24,28},{28,24},{1,5},{5... | collective-permute-start | bytes 196616 | tf_op jit(solution)/shard_map/ppermute | solution.py:96
  12.7 7.7 %copy-start.1 = (bf16[256,256]{1,0:T(8,128)(2,1)S(1)}, bf16[256,256]{1,0:T(8,128)(2,1)}, u32[]{:S(2)}) copy-start(bf16[256,256]{1,0:T(8,128)(2,1)} %weight_ref.1) | copy-start | bytes 393220
  12.7 7.7 %copy-start.3 = (bf16[128,256]{1,0:T(8,128)(2,1)S(1)}, bf16[128,256]{1,0:T(8,128)(2,1)}, u32[]{:S(2)}) copy-start(bf16[128,256]{1,0:T(8,128)(2,1)} %cot_ref.1) | copy-start | bytes 196612
  13.1 5.2 %collective-permute-start.7 = (bf16[128,256]{1,0:T(8,128)(2,1)S(1)}, bf16[128,256]{1,0:T(8,128)(2,1)S(1)}, u32[]{:S(2)}, u32[]{:S(2)}) collective-permute-start(bf16[128,256]{1,0:T(8,128)(2,1)S(1)} %get-tuple-element.34), channel_id=1, source_target_pairs={{0,3},{1,2},{2,1},{3,0},{4,7},{5,6},{6,5},{7,4},{8,11},{9,10},{10,... | collective-permute-start | bytes 196616 | tf_op jit(solution)/shard_map/ppermute | solution.py:96
  15.6 4.3 %collective-permute-start.8 = (bf16[128,256]{1,0:T(8,128)(2,1)S(1)}, bf16[128,256]{1,0:T(8,128)(2,1)S(1)}, u32[]{:S(2)}, u32[]{:S(2)}) collective-permute-start(bf16[128,256]{1,0:T(8,128)(2,1)S(1)} %get-tuple-element.35), channel_id=1, source_target_pairs={{0,2},{1,3},{2,0},{3,1},{4,6},{5,7},{6,4},{7,5},{8,10},{9,11},{10,... | collective-permute-start | bytes 196616 | tf_op jit(solution)/shard_map/ppermute | solution.py:96
  16.1 4.3 %collective-permute-start.9 = (bf16[128,256]{1,0:T(8,128)(2,1)S(1)}, bf16[128,256]{1,0:T(8,128)(2,1)S(1)}, u32[]{:S(2)}, u32[]{:S(2)}) collective-permute-start(bf16[128,256]{1,0:T(8,128)(2,1)S(1)} %get-tuple-element.36), channel_id=1, source_target_pairs={{0,1},{1,0},{2,3},{3,2},{4,5},{5,4},{6,7},{7,6},{8,9},{9,8},{10,11... | collective-permute-start | bytes 196616 | tf_op jit(solution)/shard_map/ppermute | solution.py:96
  20.8 1.4 %collective-permute-start.10 = (bf16[288,256]{1,0:T(8,128)(2,1)S(1)}, bf16[288,256]{1,0:T(8,128)(2,1)S(1)}, u32[]{:S(2)}, u32[]{:S(2)}) collective-permute-start(bf16[288,256]{1,0:T(8,128)(2,1)S(1)} %get-tuple-element.38), channel_id=1, source_target_pairs={{0,4},{4,0},{8,12},{12,8},{16,20},{20,16},{24,28},{28,24},{1,5},{5... | collective-permute-start | bytes 442376 | tf_op jit(solution)/shard_map/ppermute | solution.py:96
  22.3 6.3 %collective-permute-start.11 = (bf16[160,256]{1,0:T(8,128)(2,1)S(1)}, bf16[160,256]{1,0:T(8,128)(2,1)S(1)}, u32[]{:S(2)}, u32[]{:S(2)}) collective-permute-start(bf16[160,256]{1,0:T(8,128)(2,1)S(1)} %get-tuple-element.41), channel_id=1, source_target_pairs={{0,8},{1,9},{2,10},{3,11},{4,7},{5,6},{6,5},{7,4},{8,16},{9,17},{1... | collective-permute-start | bytes 245768 | tf_op jit(solution)/shard_map/ppermute | solution.py:303
  24.2 5.3 %collective-permute-start.12 = (bf16[160,256]{1,0:T(8,128)(2,1)S(1)}, bf16[160,256]{1,0:T(8,128)(2,1)S(1)}, u32[]{:S(2)}, u32[]{:S(2)}) collective-permute-start(bf16[160,256]{1,0:T(8,128)(2,1)S(1)} %get-tuple-element.42), channel_id=1, source_target_pairs={{0,16},{1,17},{2,18},{3,19},{4,6},{5,7},{6,4},{7,5},{8,24},{9,25},... | collective-permute-start | bytes 245768 | tf_op jit(solution)/shard_map/ppermute | solution.py:303
  26.2 4.8 %collective-permute-start.13 = (bf16[160,256]{1,0:T(8,128)(2,1)S(1)}, bf16[160,256]{1,0:T(8,128)(2,1)S(1)}, u32[]{:S(2)}, u32[]{:S(2)}) collective-permute-start(bf16[160,256]{1,0:T(8,128)(2,1)S(1)} %get-tuple-element.43), channel_id=1, source_target_pairs={{0,24},{1,25},{2,26},{3,27},{4,5},{5,4},{6,7},{7,6},{8,0},{9,1},{1... | collective-permute-start | bytes 245768 | tf_op jit(solution)/shard_map/ppermute | solution.py:303
  31.0 5.8 %collective-permute-start.14 = (bf16[224,256]{1,0:T(8,128)(2,1)S(1)}, bf16[224,256]{1,0:T(8,128)(2,1)S(1)}, u32[]{:S(2)}, u32[]{:S(2)}) collective-permute-start(bf16[224,256]{1,0:T(8,128)(2,1)S(1)} %get-tuple-element.45), channel_id=1, source_target_pairs={{0,3},{1,2},{2,1},{3,0},{4,12},{5,13},{6,14},{7,15},{8,11},{9,10},... | collective-permute-start | bytes 344072 | tf_op jit(solution)/shard_map/ppermute | solution.py:303
  32.3 5.7 %collective-permute-start.15 = (bf16[224,256]{1,0:T(8,128)(2,1)S(1)}, bf16[224,256]{1,0:T(8,128)(2,1)S(1)}, u32[]{:S(2)}, u32[]{:S(2)}) collective-permute-start(bf16[224,256]{1,0:T(8,128)(2,1)S(1)} %get-tuple-element.46), channel_id=1, source_target_pairs={{0,2},{1,3},{2,0},{3,1},{4,20},{5,21},{6,22},{7,23},{8,10},{9,11},... | collective-permute-start | bytes 344072 | tf_op jit(solution)/shard_map/ppermute | solution.py:303
  33.1 5.3 %collective-permute-start.16 = (bf16[224,256]{1,0:T(8,128)(2,1)S(1)}, bf16[224,256]{1,0:T(8,128)(2,1)S(1)}, u32[]{:S(2)}, u32[]{:S(2)}) collective-permute-start(bf16[224,256]{1,0:T(8,128)(2,1)S(1)} %get-tuple-element.47), channel_id=1, source_target_pairs={{0,1},{1,0},{2,3},{3,2},{4,28},{5,29},{6,30},{7,31},{8,9},{9,8},{1... | collective-permute-start | bytes 344072 | tf_op jit(solution)/shard_map/ppermute | solution.py:303
  38.4 1.3 %collective-permute-start.17 = (bf16[160,256]{1,0:T(8,128)(2,1)S(1)}, bf16[160,256]{1,0:T(8,128)(2,1)S(1)}, u32[]{:S(2)}, u32[]{:S(2)}) collective-permute-start(bf16[160,256]{1,0:T(8,128)(2,1)S(1)} %third.1.own_ref), channel_id=1, source_target_pairs={{0,4},{4,0},{8,12},{12,8},{16,20},{20,16},{24,28},{28,24},{1,5},{5... | collective-permute-start | bytes 245768 | tf_op jit(solution)/shard_map/ppermute | solution.py:96

commit v26 on v15

--- a/solution.py
+++ b/solution.py
@@ -305,14 +305,12 @@
     n = lax.axis_size(axis)
     blocks = [None] * n
     blocks[0] = features
-    order = sorted(range(2, n, 2), key=lambda j: (j & 4, -(j & 2)))
-    for j in order:
+    far = n // 2 & -2
+    for j in sorted(range(2, n, 2), key=lambda j: (j & 4, -(j & 2))):
         blocks[j] = swap(features, axis, j)
     blocks[1] = swap(features, axis, 1)
-    came, ready = lax.optimization_barrier(([blocks[j] for j in order], ready))
-    for j, block in zip(order, came):
-        blocks[j] = block
-    for j in range(2, n, 2):
+    blocks[far], ready = lax.optimization_barrier((blocks[far], ready))
+    for j in sorted(range(2, n, 2), key=lambda j: -j):
         blocks[j + 1] = swap(blocks[j], axis, 1)
     return blocks, ready
 

time: 40.6 us -> 40.6 us (level)
  no operation moved by 1% of the time
where the time goes in v26:
time: 40.6 us; the launch traced here: 40.4 us
  starting transfers between devices  19.2 us (47%)
  waiting for transfers between devices  15.3 us (38%)
  Pallas kernels  2.62 us (6%)
  local copies, waits for them, and re-layouts  2.55 us (6%)
  between operations  0.74 us (2%)
    ppermute x12, starting transfers between devices, swap(): lax.ppermute(value, axis, [(i, i ^ j) for i in range(lax.axis_size(axis))])  9.89 us
    ppermute x12, waiting for transfers between devices, swap(): lax.ppermute(value, axis, [(i, i ^ j) for i in range(lax.axis_size(axis))])  9.67 us
    ppermute x6, starting transfers between devices, exchange(): return lax.ppermute(value, ('section', 'rep'), pairs)  9.28 us
    ppermute x6, waiting for transfers between devices, exchange(): return lax.ppermute(value, ('section', 'rep'), pairs)  5.65 us
    unnamed x12, local copies, waits for them, and re-layouts  2.55 us
  transfers between devices with their start and end apart: 18, of which 16 were waited for; matrix products, arithmetic and copies ran while one was open for 0% of the time, Pallas kernels for 2%

profile of v26, /device:TPU:0, one launch (start us, length us, event | category | flops | bytes accessed | tf_op | source)
XLA Modules:
  0.0 40.4 jit_solution(6670093219877001766)
XLA Ops:
  0.6 4.1 %collective-permute-start = (bf16[128,256]{1,0:T(8,128)(2,1)}, bf16[128,256]{1,0:T(8,128)(2,1)S(1)}, u32[]{:S(2)}, u32[]{:S(2)}) collective-permute-start(bf16[128,256]{1,0:T(8,128)(2,1)} %own_ref.1), channel_id=1, source_target_pairs={{0,16},{4,20},{8,24},{12,28},{16,0},{20,4},{24,8},{28,12},{1,17},{... | collective-permute-start | bytes 196616 | tf_op jit(solution)/shard_map/ppermute | solution.py:94
  4.7 1.3 %collective-permute-start.5 = (bf16[128,256]{1,0:T(8,128)(2,1)}, bf16[128,256]{1,0:T(8,128)(2,1)S(1)}, u32[]{:S(2)}, u32[]{:S(2)}) collective-permute-start(bf16[128,256]{1,0:T(8,128)(2,1)} %own_ref.1), channel_id=1, source_target_pairs={{0,24},{4,28},{8,16},{12,20},{16,8},{20,12},{24,0},{28,4},{1,25},{... | collective-permute-start | bytes 196616 | tf_op jit(solution)/shard_map/ppermute | solution.py:94
  6.1 0.2 collective-permute-start.2
  6.3 0.0 collective-permute-start.1
  6.3 0.7 %copy-done.5 = s32[128,1]{0,1:T(1,128)S(1)} copy-done((s32[128,1]{0,1:T(1,128)S(1)}, s32[128,1]{0,1:T(1,128)}, u32[]{:S(2)}) %copy-start.5) | copy-done | bytes 536
  7.0 1.0 %copy-done = bf16[4,1,4,128,128]{4,3,2,1,0:T(8,128)(2,1)S(1)} copy-done((bf16[4,1,4,128,128]{4,3,2,1,0:T(8,128)(2,1)S(1)}, bf16[4,1,4,128,128]{4,3,2,1,0:T(8,128)(2,1)}, u32[]{:S(2)}) %copy-start) | copy-done | bytes 524312
  8.0 0.8 %copy-done.2 = bf16[128,256]{1,0:T(8,128)(2,1)S(1)} copy-done((bf16[128,256]{1,0:T(8,128)(2,1)S(1)}, bf16[128,256]{1,0:T(8,128)(2,1)}, u32[]{:S(2)}) %copy-start.2) | copy-done | bytes 65560
  8.9 0.2 prepare.1
  9.1 0.0 collective-permute-done.refs_4_
  9.1 0.0 copy-start.4
  9.1 2.1 %collective-permute-done.5.refs_6_ = bf16[128,256]{1,0:T(8,128)(2,1)S(1)} collective-permute-done((bf16[128,256]{1,0:T(8,128)(2,1)}, bf16[128,256]{1,0:T(8,128)(2,1)S(1)}, u32[]{:S(2)}, u32[]{:S(2)}) %collective-permute-start.5) | collective-permute-done | bytes 65568 | tf_op jit(solution)/shard_map/ppermute | solution.py:94
  11.2 0.0 collective-permute-start.6
  11.2 0.1 collective-permute-done.2.refs_2_
  11.3 0.4 %collective-permute-start.3 = (bf16[128,256]{1,0:T(8,128)(2,1)S(1)}, bf16[128,256]{1,0:T(8,128)(2,1)S(1)}, u32[]{:S(2)}, u32[]{:S(2)}) collective-permute-start(bf16[128,256]{1,0:T(8,128)(2,1)S(1)} %collective-permute-done.2.refs_2_), channel_id=1, source_target_pairs={{0,4},{4,0},{8,12},{12,8},{16,20},{20,16},{24,28},{28,24},{1,5},{5... | collective-permute-start | bytes 196616 | tf_op jit(solution)/shard_map/ppermute | solution.py:94
  11.7 0.1 collective-permute-start.4
  11.8 0.0 collective-permute-done.1.refs_1_
  11.8 0.6 %collective-permute-done.6.refs_7_ = bf16[128,256]{1,0:T(8,128)(2,1)S(1)} collective-permute-done((bf16[128,256]{1,0:T(8,128)(2,1)S(1)}, bf16[128,256]{1,0:T(8,128)(2,1)S(1)}, u32[]{:S(2)}, u32[]{:S(2)}) %collective-permute-start.6) | collective-permute-done | bytes 65568 | tf_op jit(solution)/shard_map/ppermute | solution.py:94
  12.4 0.2 collective-permute-done.3.refs_3_
  12.6 0.4 collective-permute-done.4.refs_5_
  12.9 0.0 copy-done.4
  12.9 0.4 %partials.1 = (bf16[128,256]{1,0:T(8,128)(2,1)S(1)}, bf16[128,256]{1,0:T(8,128)(2,1)S(1)}, bf16[128,256]{1,0:T(8,128)(2,1)S(1)}, bf16[128,256]{1,0:T(8,128)(2,1)S(1)}) custom-call(s32[4,4]{1,0:T(4,128)S(1)} %bitcast.5, bf16[4,128,512]{2,1,0:T(8,128)(2,1)S(1)} %get-tuple-element.30.wide_ref, bf16[128,256]{1,0:T(8,128)(2,1)S(1)} %get-tuple-element.31.refs_0_, ...), custom_call_target="tpu_custom_call" | custom-call | tf_op jit(solution)/shard_map/partials/pallas_call | solution.py:82
  13.4 2.5 %collective-permute-start.7 = (bf16[128,256]{1,0:T(8,128)(2,1)S(1)}, bf16[128,256]{1,0:T(8,128)(2,1)S(1)}, u32[]{:S(2)}, u32[]{:S(2)}) collective-permute-start(bf16[128,256]{1,0:T(8,128)(2,1)S(1)} %get-tuple-element.34), channel_id=1, source_target_pairs={{0,3},{1,2},{2,1},{3,0},{4,7},{5,6},{6,5},{7,4},{8,11},{9,10},{10,... | collective-permute-start | bytes 196616 | tf_op jit(solution)/shard_map/ppermute | solution.py:94
  15.9 0.5 %collective-permute-start.8 = (bf16[128,256]{1,0:T(8,128)(2,1)S(1)}, bf16[128,256]{1,0:T(8,128)(2,1)S(1)}, u32[]{:S(2)}, u32[]{:S(2)}) collective-permute-start(bf16[128,256]{1,0:T(8,128)(2,1)S(1)} %get-tuple-element.35), channel_id=1, source_target_pairs={{0,2},{1,3},{2,0},{3,1},{4,6},{5,7},{6,4},{7,5},{8,10},{9,11},{10,... | collective-permute-start | bytes 196616 | tf_op jit(solution)/shard_map/ppermute | solution.py:94
  16.4 0.5 %collective-permute-start.9 = (bf16[128,256]{1,0:T(8,128)(2,1)S(1)}, bf16[128,256]{1,0:T(8,128)(2,1)S(1)}, u32[]{:S(2)}, u32[]{:S(2)}) collective-permute-start(bf16[128,256]{1,0:T(8,128)(2,1)S(1)} %get-tuple-element.36), channel_id=1, source_target_pairs={{0,1},{1,0},{2,3},{3,2},{4,5},{5,4},{6,7},{7,6},{8,9},{9,8},{10,11... | collective-permute-start | bytes 196616 | tf_op jit(solution)/shard_map/ppermute | solution.py:94
  16.9 1.7 %collective-permute-done.7.refs_1_ = bf16[128,256]{1,0:T(8,128)(2,1)S(1)} collective-permute-done((bf16[128,256]{1,0:T(8,128)(2,1)S(1)}, bf16[128,256]{1,0:T(8,128)(2,1)S(1)}, u32[]{:S(2)}, u32[]{:S(2)}) %collective-permute-start.7) | collective-permute-done | bytes 65568 | tf_op jit(solution)/shard_map/ppermute | solution.py:94
  18.6 1.5 %collective-permute-done.8.refs_2_ = bf16[128,256]{1,0:T(8,128)(2,1)S(1)} collective-permute-done((bf16[128,256]{1,0:T(8,128)(2,1)S(1)}, bf16[128,256]{1,0:T(8,128)(2,1)S(1)}, u32[]{:S(2)}, u32[]{:S(2)}) %collective-permute-start.8) | collective-permute-done | bytes 65568 | tf_op jit(solution)/shard_map/ppermute | solution.py:94
  20.2 0.5 %collective-permute-done.9.refs_3_ = bf16[128,256]{1,0:T(8,128)(2,1)S(1)} collective-permute-done((bf16[128,256]{1,0:T(8,128)(2,1)S(1)}, bf16[128,256]{1,0:T(8,128)(2,1)S(1)}, u32[]{:S(2)}, u32[]{:S(2)}) %collective-permute-start.9) | collective-permute-done | bytes 65568 | tf_op jit(solution)/shard_map/ppermute | solution.py:94
  20.7 0.0 copy-done.1
  20.7 0.4 %dense.1 = (bf16[128,256]{1,0:T(8,128)(2,1)S(1)}, f32[256,256]{1,0:T(8,128)S(1)}, bf16[288,256]{1,0:T(8,128)(2,1)S(1)}) custom-call(bf16[256,256]{1,0:T(8,128)(2,1)S(1)} %copy-done.1, bf16[128,256]{1,0:T(8,128)(2,1)S(1)} %copy-done.3, bf16[256,128]{1,0:T(8,128)(2,1)S(1)} %get-tuple-element.29.placing_ref, bf16[128,256]{1,0:T(8,128)(2,1)S(1)} %get-tuple-element.33.refs_0_, ...), custom_call_target="tpu_custom_call" | custom-call | tf_op jit(solution)/shard_map/dense/pallas_call | solution.py:138
  21.1 0.1 collective-permute-start.10
  21.2 1.4 %collective-permute-done.10.came_ref.refs_1_ = bf16[288,256]{1,0:T(8,128)(2,1)S(1)} collective-permute-done((bf16[288,256]{1,0:T(8,128)(2,1)S(1)}, bf16[288,256]{1,0:T(8,128)(2,1)S(1)}, u32[]{:S(2)}, u32[]{:S(2)}) %collective-permute-start.10) | collective-permute-done | bytes 147488 | tf_op jit(solution)/shard_map/ppermute | solution.py:94
  22.6 1.1 %collective-permute-start.11 = (bf16[160,256]{1,0:T(8,128)(2,1)S(1)}, bf16[160,256]{1,0:T(8,128)(2,1)S(1)}, u32[]{:S(2)}, u32[]{:S(2)}) collective-permute-start(bf16[160,256]{1,0:T(8,128)(2,1)S(1)} %get-tuple-element.41), channel_id=1, source_target_pairs={{0,8},{1,9},{2,10},{3,11},{4,7},{5,6},{6,5},{7,4},{8,16},{9,17},{1... | collective-permute-start | bytes 245768 | tf_op jit(solution)/shard_map/ppermute | solution.py:301
  23.6 2.3 %collective-permute-start.12 = (bf16[160,256]{1,0:T(8,128)(2,1)S(1)}, bf16[160,256]{1,0:T(8,128)(2,1)S(1)}, u32[]{:S(2)}, u32[]{:S(2)}) collective-permute-start(bf16[160,256]{1,0:T(8,128)(2,1)S(1)} %get-tuple-element.42), channel_id=1, source_target_pairs={{0,16},{1,17},{2,18},{3,19},{4,6},{5,7},{6,4},{7,5},{8,24},{9,25},... | collective-permute-start | bytes 245768 | tf_op jit(solution)/shard_map/ppermute | solution.py:301
  25.9 2.4 %collective-permute-start.13 = (bf16[160,256]{1,0:T(8,128)(2,1)S(1)}, bf16[160,256]{1,0:T(8,128)(2,1)S(1)}, u32[]{:S(2)}, u32[]{:S(2)}) collective-permute-start(bf16[160,256]{1,0:T(8,128)(2,1)S(1)} %get-tuple-element.43), channel_id=1, source_target_pairs={{0,24},{1,25},{2,26},{3,27},{4,5},{5,4},{6,7},{7,6},{8,0},{9,1},{1... | collective-permute-start | bytes 245768 | tf_op jit(solution)/shard_map/ppermute | solution.py:301
  28.3 0.6 %collective-permute-done.11.refs_0_ = bf16[160,256]{1,0:T(8,128)(2,1)S(1)} collective-permute-done((bf16[160,256]{1,0:T(8,128)(2,1)S(1)}, bf16[160,256]{1,0:T(8,128)(2,1)S(1)}, u32[]{:S(2)}, u32[]{:S(2)}) %collective-permute-start.11) | collective-permute-done | bytes 81952 | tf_op jit(solution)/shard_map/ppermute | solution.py:301
  29.0 0.8 %collective-permute-done.12.refs_1_ = bf16[160,256]{1,0:T(8,128)(2,1)S(1)} collective-permute-done((bf16[160,256]{1,0:T(8,128)(2,1)S(1)}, bf16[160,256]{1,0:T(8,128)(2,1)S(1)}, u32[]{:S(2)}, u32[]{:S(2)}) %collective-permute-start.12) | collective-permute-done | bytes 81952 | tf_op jit(solution)/shard_map/ppermute | solution.py:301
  29.8 1.4 %collective-permute-done.13.refs_2_ = bf16[160,256]{1,0:T(8,128)(2,1)S(1)} collective-permute-done((bf16[160,256]{1,0:T(8,128)(2,1)S(1)}, bf16[160,256]{1,0:T(8,128)(2,1)S(1)}, u32[]{:S(2)}, u32[]{:S(2)}) %collective-permute-start.13) | collective-permute-done | bytes 81952 | tf_op jit(solution)/shard_map/ppermute | solution.py:301
  31.2 0.1 second.1
  31.2 1.2 %collective-permute-start.14 = (bf16[224,256]{1,0:T(8,128)(2,1)S(1)}, bf16[224,256]{1,0:T(8,128)(2,1)S(1)}, u32[]{:S(2)}, u32[]{:S(2)}) collective-permute-start(bf16[224,256]{1,0:T(8,128)(2,1)S(1)} %get-tuple-element.45), channel_id=1, source_target_pairs={{0,3},{1,2},{2,1},{3,0},{4,12},{5,13},{6,14},{7,15},{8,11},{9,10},... | collective-permute-start | bytes 344072 | tf_op jit(solution)/shard_map/ppermute | solution.py:301
  32.5 1.0 %collective-permute-start.15 = (bf16[224,256]{1,0:T(8,128)(2,1)S(1)}, bf16[224,256]{1,0:T(8,128)(2,1)S(1)}, u32[]{:S(2)}, u32[]{:S(2)}) collective-permute-start(bf16[224,256]{1,0:T(8,128)(2,1)S(1)} %get-tuple-element.46), channel_id=1, source_target_pairs={{0,2},{1,3},{2,0},{3,1},{4,20},{5,21},{6,22},{7,23},{8,10},{9,11},... | collective-permute-start | bytes 344072 | tf_op jit(solution)/shard_map/ppermute | solution.py:301
  33.5 1.3 %collective-permute-start.16 = (bf16[224,256]{1,0:T(8,128)(2,1)S(1)}, bf16[224,256]{1,0:T(8,128)(2,1)S(1)}, u32[]{:S(2)}, u32[]{:S(2)}) collective-permute-start(bf16[224,256]{1,0:T(8,128)(2,1)S(1)} %get-tuple-element.47), channel_id=1, source_target_pairs={{0,1},{1,0},{2,3},{3,2},{4,28},{5,29},{6,30},{7,31},{8,9},{9,8},{1... | collective-permute-start | bytes 344072 | tf_op jit(solution)/shard_map/ppermute | solution.py:301
  34.8 0.7 %store.2._ = bf16[8,32,256]{2,1,0:T(8,128)(2,1)} custom-call(bf16[128,256]{1,0:T(8,128)(2,1)S(1)} %get-tuple-element.37.same_ref.refs_0_, bf16[288,256]{1,0:T(8,128)(2,1)S(1)} %collective-permute-done.10.came_ref.refs_1_, bf16[160,256]{1,0:T(8,128)(2,1)S(1)} %collective-permute-done.11.refs_0_, bf16[160,256]{1,0:T(8,128)(2,1)S(1)} %collective-permute-done.12.refs_1_, ...), custom_call_target="tpu_custom_call" | custom-call | tf_op jit(solution)/shard_map/store/pallas_call | solution.py:254
  35.4 1.6 %collective-permute-done.14.refs_0_.refs_2_ = bf16[224,256]{1,0:T(8,128)(2,1)S(1)} collective-permute-done((bf16[224,256]{1,0:T(8,128)(2,1)S(1)}, bf16[224,256]{1,0:T(8,128)(2,1)S(1)}, u32[]{:S(2)}, u32[]{:S(2)}) %collective-permute-start.14) | collective-permute-done | bytes 114720 | tf_op jit(solution)/shard_map/ppermute | solution.py:301
  37.1 1.1 %collective-permute-done.15.refs_1_.refs_3_ = bf16[224,256]{1,0:T(8,128)(2,1)S(1)} collective-permute-done((bf16[224,256]{1,0:T(8,128)(2,1)S(1)}, bf16[224,256]{1,0:T(8,128)(2,1)S(1)}, u32[]{:S(2)}, u32[]{:S(2)}) %collective-permute-start.15) | collective-permute-done | bytes 114720 | tf_op jit(solution)/shard_map/ppermute | solution.py:301
  38.2 0.1 collective-permute-done.16.refs_2_.refs_4_
  38.3 0.1 collective-permute-start.17
  38.4 1.3 %collective-permute-done.17.came_ref = bf16[160,256]{1,0:T(8,128)(2,1)S(1)} collective-permute-done((bf16[160,256]{1,0:T(8,128)(2,1)S(1)}, bf16[160,256]{1,0:T(8,128)(2,1)S(1)}, u32[]{:S(2)}, u32[]{:S(2)}) %collective-permute-start.17) | collective-permute-done | bytes 81952 | tf_op jit(solution)/shard_map/ppermute | solution.py:94
  39.7 0.7 %finish.1 = f32[256,256]{1,0:T(8,128)} custom-call(bf16[160,256]{1,0:T(8,128)(2,1)S(1)} %third.1.own_ref, bf16[160,256]{1,0:T(8,128)(2,1)S(1)} %collective-permute-done.17.came_ref), custom_call_target="tpu_custom_call" | custom-call | tf_op jit(solution)/shard_map/finish/pallas_call | solution.py:283
  (9 shorter events, 0.1 us)
Async XLA Ops:
  0.6 8.5 %collective-permute-start = (bf16[128,256]{1,0:T(8,128)(2,1)}, bf16[128,256]{1,0:T(8,128)(2,1)S(1)}, u32[]{:S(2)}, u32[]{:S(2)}) collective-permute-start(bf16[128,256]{1,0:T(8,128)(2,1)} %own_ref.1), channel_id=1, source_target_pairs={{0,16},{4,20},{8,24},{12,28},{16,0},{20,4},{24,8},{28,12},{1,17},{... | collective-permute-start | bytes 196616 | tf_op jit(solution)/shard_map/ppermute | solution.py:94
  4.7 6.4 %collective-permute-start.5 = (bf16[128,256]{1,0:T(8,128)(2,1)}, bf16[128,256]{1,0:T(8,128)(2,1)S(1)}, u32[]{:S(2)}, u32[]{:S(2)}) collective-permute-start(bf16[128,256]{1,0:T(8,128)(2,1)} %own_ref.1), channel_id=1, source_target_pairs={{0,24},{4,28},{8,16},{12,20},{16,8},{20,12},{24,0},{28,4},{1,25},{... | collective-permute-start | bytes 196616 | tf_op jit(solution)/shard_map/ppermute | solution.py:94
  6.1 5.2 %collective-permute-start.2 = (bf16[128,256]{1,0:T(8,128)(2,1)}, bf16[128,256]{1,0:T(8,128)(2,1)S(1)}, u32[]{:S(2)}, u32[]{:S(2)}) collective-permute-start(bf16[128,256]{1,0:T(8,128)(2,1)} %own_ref.1), channel_id=1, source_target_pairs={{0,8},{4,12},{8,0},{12,4},{16,24},{20,28},{24,16},{28,20},{1,9},{5... | collective-permute-start | bytes 196616 | tf_op jit(solution)/shard_map/ppermute | solution.py:94
  6.3 5.5 %collective-permute-start.1 = (bf16[128,256]{1,0:T(8,128)(2,1)}, bf16[128,256]{1,0:T(8,128)(2,1)S(1)}, u32[]{:S(2)}, u32[]{:S(2)}) collective-permute-start(bf16[128,256]{1,0:T(8,128)(2,1)} %own_ref.1), channel_id=1, source_target_pairs={{0,4},{4,0},{8,12},{12,8},{16,20},{20,16},{24,28},{28,24},{1,5},{5... | collective-permute-start | bytes 196616 | tf_op jit(solution)/shard_map/ppermute | solution.py:94
  6.3 0.7 %copy-start.5 = (s32[128,1]{0,1:T(1,128)S(1)}, s32[128,1]{0,1:T(1,128)}, u32[]{:S(2)}) copy-start(s32[128,1]{0,1:T(1,128)} %param.11) | copy-start | bytes 1540
  7.0 1.0 %copy-start = (bf16[4,1,4,128,128]{4,3,2,1,0:T(8,128)(2,1)S(1)}, bf16[4,1,4,128,128]{4,3,2,1,0:T(8,128)(2,1)}, u32[]{:S(2)}) copy-start(bf16[4,1,4,128,128]{4,3,2,1,0:T(8,128)(2,1)} %param.7) | copy-start | bytes 1572868
  8.0 0.8 %copy-start.2 = (bf16[128,256]{1,0:T(8,128)(2,1)S(1)}, bf16[128,256]{1,0:T(8,128)(2,1)}, u32[]{:S(2)}) copy-start(bf16[128,256]{1,0:T(8,128)(2,1)} %own_ref.1) | copy-start | bytes 196612
  9.1 3.8 %copy-start.4 = (s32[4,1,4]{2,1,0:T(1,128)S(1)}, s32[4,1,4]{2,1,0:T(1,128)}, u32[]{:S(2)}) copy-start(s32[4,1,4]{2,1,0:T(1,128)} %param.8) | copy-start | bytes 196
  11.2 1.3 %collective-permute-start.6 = (bf16[128,256]{1,0:T(8,128)(2,1)S(1)}, bf16[128,256]{1,0:T(8,128)(2,1)S(1)}, u32[]{:S(2)}, u32[]{:S(2)}) collective-permute-start(bf16[128,256]{1,0:T(8,128)(2,1)S(1)} %collective-permute-done.5.refs_6_), channel_id=1, source_target_pairs={{0,4},{4,0},{8,12},{12,8},{16,20},{20,16},{24,28},{28,24},{1,5},{5... | collective-permute-start | bytes 196616 | tf_op jit(solution)/shard_map/ppermute | solution.py:94
  11.3 1.3 %collective-permute-start.3 = (bf16[128,256]{1,0:T(8,128)(2,1)S(1)}, bf16[128,256]{1,0:T(8,128)(2,1)S(1)}, u32[]{:S(2)}, u32[]{:S(2)}) collective-permute-start(bf16[128,256]{1,0:T(8,128)(2,1)S(1)} %collective-permute-done.2.refs_2_), channel_id=1, source_target_pairs={{0,4},{4,0},{8,12},{12,8},{16,20},{20,16},{24,28},{28,24},{1,5},{5... | collective-permute-start | bytes 196616 | tf_op jit(solution)/shard_map/ppermute | solution.py:94
  11.7 1.3 %collective-permute-start.4 = (bf16[128,256]{1,0:T(8,128)(2,1)S(1)}, bf16[128,256]{1,0:T(8,128)(2,1)S(1)}, u32[]{:S(2)}, u32[]{:S(2)}) collective-permute-start(bf16[128,256]{1,0:T(8,128)(2,1)S(1)} %collective-permute-done.refs_4_), channel_id=1, source_target_pairs={{0,4},{4,0},{8,12},{12,8},{16,20},{20,16},{24,28},{28,24},{1,5},{5... | collective-permute-start | bytes 196616 | tf_op jit(solution)/shard_map/ppermute | solution.py:94
  12.9 7.7 %copy-start.1 = (bf16[256,256]{1,0:T(8,128)(2,1)S(1)}, bf16[256,256]{1,0:T(8,128)(2,1)}, u32[]{:S(2)}) copy-start(bf16[256,256]{1,0:T(8,128)(2,1)} %weight_ref.1) | copy-start | bytes 393220
  12.9 7.7 %copy-start.3 = (bf16[128,256]{1,0:T(8,128)(2,1)S(1)}, bf16[128,256]{1,0:T(8,128)(2,1)}, u32[]{:S(2)}) copy-start(bf16[128,256]{1,0:T(8,128)(2,1)} %cot_ref.1) | copy-start | bytes 196612
  13.4 5.3 %collective-permute-start.7 = (bf16[128,256]{1,0:T(8,128)(2,1)S(1)}, bf16[128,256]{1,0:T(8,128)(2,1)S(1)}, u32[]{:S(2)}, u32[]{:S(2)}) collective-permute-start(bf16[128,256]{1,0:T(8,128)(2,1)S(1)} %get-tuple-element.34), channel_id=1, source_target_pairs={{0,3},{1,2},{2,1},{3,0},{4,7},{5,6},{6,5},{7,4},{8,11},{9,10},{10,... | collective-permute-start | bytes 196616 | tf_op jit(solution)/shard_map/ppermute | solution.py:94
  15.9 4.3 %collective-permute-start.8 = (bf16[128,256]{1,0:T(8,128)(2,1)S(1)}, bf16[128,256]{1,0:T(8,128)(2,1)S(1)}, u32[]{:S(2)}, u32[]{:S(2)}) collective-permute-start(bf16[128,256]{1,0:T(8,128)(2,1)S(1)} %get-tuple-element.35), channel_id=1, source_target_pairs={{0,2},{1,3},{2,0},{3,1},{4,6},{5,7},{6,4},{7,5},{8,10},{9,11},{10,... | collective-permute-start | bytes 196616 | tf_op jit(solution)/shard_map/ppermute | solution.py:94
  16.4 4.3 %collective-permute-start.9 = (bf16[128,256]{1,0:T(8,128)(2,1)S(1)}, bf16[128,256]{1,0:T(8,128)(2,1)S(1)}, u32[]{:S(2)}, u32[]{:S(2)}) collective-permute-start(bf16[128,256]{1,0:T(8,128)(2,1)S(1)} %get-tuple-element.36), channel_id=1, source_target_pairs={{0,1},{1,0},{2,3},{3,2},{4,5},{5,4},{6,7},{7,6},{8,9},{9,8},{10,11... | collective-permute-start | bytes 196616 | tf_op jit(solution)/shard_map/ppermute | solution.py:94
  21.1 1.4 %collective-permute-start.10 = (bf16[288,256]{1,0:T(8,128)(2,1)S(1)}, bf16[288,256]{1,0:T(8,128)(2,1)S(1)}, u32[]{:S(2)}, u32[]{:S(2)}) collective-permute-start(bf16[288,256]{1,0:T(8,128)(2,1)S(1)} %get-tuple-element.38), channel_id=1, source_target_pairs={{0,4},{4,0},{8,12},{12,8},{16,20},{20,16},{24,28},{28,24},{1,5},{5... | collective-permute-start | bytes 442376 | tf_op jit(solution)/shard_map/ppermute | solution.py:94
  22.6 6.4 %collective-permute-start.11 = (bf16[160,256]{1,0:T(8,128)(2,1)S(1)}, bf16[160,256]{1,0:T(8,128)(2,1)S(1)}, u32[]{:S(2)}, u32[]{:S(2)}) collective-permute-start(bf16[160,256]{1,0:T(8,128)(2,1)S(1)} %get-tuple-element.41), channel_id=1, source_target_pairs={{0,8},{1,9},{2,10},{3,11},{4,7},{5,6},{6,5},{7,4},{8,16},{9,17},{1... | collective-permute-start | bytes 245768 | tf_op jit(solution)/shard_map/ppermute | solution.py:301
  23.6 6.1 %collective-permute-start.12 = (bf16[160,256]{1,0:T(8,128)(2,1)S(1)}, bf16[160,256]{1,0:T(8,128)(2,1)S(1)}, u32[]{:S(2)}, u32[]{:S(2)}) collective-permute-start(bf16[160,256]{1,0:T(8,128)(2,1)S(1)} %get-tuple-element.42), channel_id=1, source_target_pairs={{0,16},{1,17},{2,18},{3,19},{4,6},{5,7},{6,4},{7,5},{8,24},{9,25},... | collective-permute-start | bytes 245768 | tf_op jit(solution)/shard_map/ppermute | solution.py:301
  25.9 5.2 %collective-permute-start.13 = (bf16[160,256]{1,0:T(8,128)(2,1)S(1)}, bf16[160,256]{1,0:T(8,128)(2,1)S(1)}, u32[]{:S(2)}, u32[]{:S(2)}) collective-permute-start(bf16[160,256]{1,0:T(8,128)(2,1)S(1)} %get-tuple-element.43), channel_id=1, source_target_pairs={{0,24},{1,25},{2,26},{3,27},{4,5},{5,4},{6,7},{7,6},{8,0},{9,1},{1... | collective-permute-start | bytes 245768 | tf_op jit(solution)/shard_map/ppermute | solution.py:301
  31.2 5.8 %collective-permute-start.14 = (bf16[224,256]{1,0:T(8,128)(2,1)S(1)}, bf16[224,256]{1,0:T(8,128)(2,1)S(1)}, u32[]{:S(2)}, u32[]{:S(2)}) collective-permute-start(bf16[224,256]{1,0:T(8,128)(2,1)S(1)} %get-tuple-element.45), channel_id=1, source_target_pairs={{0,3},{1,2},{2,1},{3,0},{4,12},{5,13},{6,14},{7,15},{8,11},{9,10},... | collective-permute-start | bytes 344072 | tf_op jit(solution)/shard_map/ppermute | solution.py:301
  32.5 5.7 %collective-permute-start.15 = (bf16[224,256]{1,0:T(8,128)(2,1)S(1)}, bf16[224,256]{1,0:T(8,128)(2,1)S(1)}, u32[]{:S(2)}, u32[]{:S(2)}) collective-permute-start(bf16[224,256]{1,0:T(8,128)(2,1)S(1)} %get-tuple-element.46), channel_id=1, source_target_pairs={{0,2},{1,3},{2,0},{3,1},{4,20},{5,21},{6,22},{7,23},{8,10},{9,11},... | collective-permute-start | bytes 344072 | tf_op jit(solution)/shard_map/ppermute | solution.py:301
  33.5 4.8 %collective-permute-start.16 = (bf16[224,256]{1,0:T(8,128)(2,1)S(1)}, bf16[224,256]{1,0:T(8,128)(2,1)S(1)}, u32[]{:S(2)}, u32[]{:S(2)}) collective-permute-start(bf16[224,256]{1,0:T(8,128)(2,1)S(1)} %get-tuple-element.47), channel_id=1, source_target_pairs={{0,1},{1,0},{2,3},{3,2},{4,28},{5,29},{6,30},{7,31},{8,9},{9,8},{1... | collective-permute-start | bytes 344072 | tf_op jit(solution)/shard_map/ppermute | solution.py:301
  38.3 1.3 %collective-permute-start.17 = (bf16[160,256]{1,0:T(8,128)(2,1)S(1)}, bf16[160,256]{1,0:T(8,128)(2,1)S(1)}, u32[]{:S(2)}, u32[]{:S(2)}) collective-permute-start(bf16[160,256]{1,0:T(8,128)(2,1)S(1)} %third.1.own_ref), channel_id=1, source_target_pairs={{0,4},{4,0},{8,12},{12,8},{16,20},{20,16},{24,28},{28,24},{1,5},{5... | collective-permute-start | bytes 245768 | tf_op jit(solution)/shard_map/ppermute | solution.py:94

commit v27 on v26

--- a/solution.py
+++ b/solution.py
@@ -13,7 +13,7 @@
 
 
 def across(n):
-    return list(range(n - 1, 0, -1))
+    return [n - 1] + list(range(1, n - 1))
 
 
 def place_of_chip():
@@ -182,7 +182,9 @@
     @pl.when(core != core_along)
     def _():
         many = rows[1 - core_along]
-        by_xor = [ref[:many].astype(jnp.float32) for ref in [own_ref] + list(message_refs[::-1])]
+        refs = dict(zip(across(len(message_refs) + 1), message_refs))
+        refs = [own_ref] + [refs[j] for j in sorted(refs)]
+        by_xor = [ref[:many].astype(jnp.float32) for ref in refs]
         half_ref[:many] = tree_sum(by_xor[:n_rep]).astype(jnp.bfloat16)
 
 

time: 40.6 us -> 40.6 us (level)
  no operation moved by 1% of the time
where the time goes in v27:
time: 40.6 us; the launch traced here: 40.4 us
  starting transfers between devices  19.2 us (47%)
  waiting for transfers between devices  15.3 us (38%)
  Pallas kernels  2.62 us (6%)
  local copies, waits for them, and re-layouts  2.55 us (6%)
  between operations  0.74 us (2%)
    ppermute x12, starting transfers between devices, swap(): lax.ppermute(value, axis, [(i, i ^ j) for i in range(lax.axis_size(axis))])  9.89 us
    ppermute x12, waiting for transfers between devices, swap(): lax.ppermute(value, axis, [(i, i ^ j) for i in range(lax.axis_size(axis))])  9.69 us
    ppermute x6, starting transfers between devices, exchange(): return lax.ppermute(value, ('section', 'rep'), pairs)  9.28 us
    ppermute x6, waiting for transfers between devices, exchange(): return lax.ppermute(value, ('section', 'rep'), pairs)  5.58 us
    unnamed x12, local copies, waits for them, and re-layouts  2.55 us
  transfers between devices with their start and end apart: 18, of which 16 were waited for; matrix products, arithmetic and copies ran while one was open for 0% of the time, Pallas kernels for 2%

profile of v27, /device:TPU:0, one launch (start us, length us, event | category | flops | bytes accessed | tf_op | source)
XLA Modules:
  0.0 40.4 jit_solution(5862821318812385150)
XLA Ops:
  0.6 4.1 %collective-permute-start = (bf16[128,256]{1,0:T(8,128)(2,1)}, bf16[128,256]{1,0:T(8,128)(2,1)S(1)}, u32[]{:S(2)}, u32[]{:S(2)}) collective-permute-start(bf16[128,256]{1,0:T(8,128)(2,1)} %own_ref.1), channel_id=1, source_target_pairs={{0,16},{4,20},{8,24},{12,28},{16,0},{20,4},{24,8},{28,12},{1,17},{... | collective-permute-start | bytes 196616 | tf_op jit(solution)/shard_map/ppermute | solution.py:94
  4.7 1.3 %collective-permute-start.5 = (bf16[128,256]{1,0:T(8,128)(2,1)}, bf16[128,256]{1,0:T(8,128)(2,1)S(1)}, u32[]{:S(2)}, u32[]{:S(2)}) collective-permute-start(bf16[128,256]{1,0:T(8,128)(2,1)} %own_ref.1), channel_id=1, source_target_pairs={{0,24},{4,28},{8,16},{12,20},{16,8},{20,12},{24,0},{28,4},{1,25},{... | collective-permute-start | bytes 196616 | tf_op jit(solution)/shard_map/ppermute | solution.py:94
  6.1 0.2 collective-permute-start.2
  6.3 0.0 collective-permute-start.1
  6.3 0.7 %copy-done.5 = s32[128,1]{0,1:T(1,128)S(1)} copy-done((s32[128,1]{0,1:T(1,128)S(1)}, s32[128,1]{0,1:T(1,128)}, u32[]{:S(2)}) %copy-start.5) | copy-done | bytes 536
  7.0 1.0 %copy-done = bf16[4,1,4,128,128]{4,3,2,1,0:T(8,128)(2,1)S(1)} copy-done((bf16[4,1,4,128,128]{4,3,2,1,0:T(8,128)(2,1)S(1)}, bf16[4,1,4,128,128]{4,3,2,1,0:T(8,128)(2,1)}, u32[]{:S(2)}) %copy-start) | copy-done | bytes 524312
  8.0 0.8 %copy-done.2 = bf16[128,256]{1,0:T(8,128)(2,1)S(1)} copy-done((bf16[128,256]{1,0:T(8,128)(2,1)S(1)}, bf16[128,256]{1,0:T(8,128)(2,1)}, u32[]{:S(2)}) %copy-start.2) | copy-done | bytes 65560
  8.9 0.2 prepare.1
  9.1 0.0 collective-permute-done.refs_4_
  9.1 0.0 copy-start.4
  9.1 2.1 %collective-permute-done.5.refs_6_ = bf16[128,256]{1,0:T(8,128)(2,1)S(1)} collective-permute-done((bf16[128,256]{1,0:T(8,128)(2,1)}, bf16[128,256]{1,0:T(8,128)(2,1)S(1)}, u32[]{:S(2)}, u32[]{:S(2)}) %collective-permute-start.5) | collective-permute-done | bytes 65568 | tf_op jit(solution)/shard_map/ppermute | solution.py:94
  11.2 0.0 collective-permute-start.6
  11.2 0.1 collective-permute-done.2.refs_2_
  11.3 0.4 %collective-permute-start.3 = (bf16[128,256]{1,0:T(8,128)(2,1)S(1)}, bf16[128,256]{1,0:T(8,128)(2,1)S(1)}, u32[]{:S(2)}, u32[]{:S(2)}) collective-permute-start(bf16[128,256]{1,0:T(8,128)(2,1)S(1)} %collective-permute-done.2.refs_2_), channel_id=1, source_target_pairs={{0,4},{4,0},{8,12},{12,8},{16,20},{20,16},{24,28},{28,24},{1,5},{5... | collective-permute-start | bytes 196616 | tf_op jit(solution)/shard_map/ppermute | solution.py:94
  11.7 0.1 collective-permute-start.4
  11.8 0.0 collective-permute-done.1.refs_1_
  11.8 0.6 %collective-permute-done.6.refs_7_ = bf16[128,256]{1,0:T(8,128)(2,1)S(1)} collective-permute-done((bf16[128,256]{1,0:T(8,128)(2,1)S(1)}, bf16[128,256]{1,0:T(8,128)(2,1)S(1)}, u32[]{:S(2)}, u32[]{:S(2)}) %collective-permute-start.6) | collective-permute-done | bytes 65568 | tf_op jit(solution)/shard_map/ppermute | solution.py:94
  12.4 0.2 collective-permute-done.3.refs_3_
  12.6 0.4 collective-permute-done.4.refs_5_
  12.9 0.0 copy-done.4
  12.9 0.4 %partials.1 = (bf16[128,256]{1,0:T(8,128)(2,1)S(1)}, bf16[128,256]{1,0:T(8,128)(2,1)S(1)}, bf16[128,256]{1,0:T(8,128)(2,1)S(1)}, bf16[128,256]{1,0:T(8,128)(2,1)S(1)}) custom-call(s32[4,4]{1,0:T(4,128)S(1)} %bitcast.5, bf16[4,128,512]{2,1,0:T(8,128)(2,1)S(1)} %get-tuple-element.30.wide_ref, bf16[128,256]{1,0:T(8,128)(2,1)S(1)} %get-tuple-element.31.refs_0_, ...), custom_call_target="tpu_custom_call" | custom-call | tf_op jit(solution)/shard_map/partials/pallas_call | solution.py:82
  13.4 2.5 %collective-permute-start.7 = (bf16[128,256]{1,0:T(8,128)(2,1)S(1)}, bf16[128,256]{1,0:T(8,128)(2,1)S(1)}, u32[]{:S(2)}, u32[]{:S(2)}) collective-permute-start(bf16[128,256]{1,0:T(8,128)(2,1)S(1)} %get-tuple-element.34), channel_id=1, source_target_pairs={{0,3},{1,2},{2,1},{3,0},{4,7},{5,6},{6,5},{7,4},{8,11},{9,10},{10,... | collective-permute-start | bytes 196616 | tf_op jit(solution)/shard_map/ppermute | solution.py:94
  15.9 0.5 %collective-permute-start.8 = (bf16[128,256]{1,0:T(8,128)(2,1)S(1)}, bf16[128,256]{1,0:T(8,128)(2,1)S(1)}, u32[]{:S(2)}, u32[]{:S(2)}) collective-permute-start(bf16[128,256]{1,0:T(8,128)(2,1)S(1)} %get-tuple-element.35), channel_id=1, source_target_pairs={{0,1},{1,0},{2,3},{3,2},{4,5},{5,4},{6,7},{7,6},{8,9},{9,8},{10,11... | collective-permute-start | bytes 196616 | tf_op jit(solution)/shard_map/ppermute | solution.py:94
  16.4 0.5 %collective-permute-start.9 = (bf16[128,256]{1,0:T(8,128)(2,1)S(1)}, bf16[128,256]{1,0:T(8,128)(2,1)S(1)}, u32[]{:S(2)}, u32[]{:S(2)}) collective-permute-start(bf16[128,256]{1,0:T(8,128)(2,1)S(1)} %get-tuple-element.36), channel_id=1, source_target_pairs={{0,2},{1,3},{2,0},{3,1},{4,6},{5,7},{6,4},{7,5},{8,10},{9,11},{10,... | collective-permute-start | bytes 196616 | tf_op jit(solution)/shard_map/ppermute | solution.py:94
  16.9 2.1 %collective-permute-done.7.refs_1_ = bf16[128,256]{1,0:T(8,128)(2,1)S(1)} collective-permute-done((bf16[128,256]{1,0:T(8,128)(2,1)S(1)}, bf16[128,256]{1,0:T(8,128)(2,1)S(1)}, u32[]{:S(2)}, u32[]{:S(2)}) %collective-permute-start.7) | collective-permute-done | bytes 65568 | tf_op jit(solution)/shard_map/ppermute | solution.py:94
  19.0 1.2 %collective-permute-done.8.refs_2_ = bf16[128,256]{1,0:T(8,128)(2,1)S(1)} collective-permute-done((bf16[128,256]{1,0:T(8,128)(2,1)S(1)}, bf16[128,256]{1,0:T(8,128)(2,1)S(1)}, u32[]{:S(2)}, u32[]{:S(2)}) %collective-permute-start.8) | collective-permute-done | bytes 65568 | tf_op jit(solution)/shard_map/ppermute | solution.py:94
  20.2 0.5 %collective-permute-done.9.refs_3_ = bf16[128,256]{1,0:T(8,128)(2,1)S(1)} collective-permute-done((bf16[128,256]{1,0:T(8,128)(2,1)S(1)}, bf16[128,256]{1,0:T(8,128)(2,1)S(1)}, u32[]{:S(2)}, u32[]{:S(2)}) %collective-permute-start.9) | collective-permute-done | bytes 65568 | tf_op jit(solution)/shard_map/ppermute | solution.py:94
  20.7 0.0 copy-done.3
  20.7 0.4 %dense.1 = (bf16[128,256]{1,0:T(8,128)(2,1)S(1)}, f32[256,256]{1,0:T(8,128)S(1)}, bf16[288,256]{1,0:T(8,128)(2,1)S(1)}) custom-call(bf16[256,256]{1,0:T(8,128)(2,1)S(1)} %copy-done.1, bf16[128,256]{1,0:T(8,128)(2,1)S(1)} %copy-done.3, bf16[256,128]{1,0:T(8,128)(2,1)S(1)} %get-tuple-element.29.placing_ref, bf16[128,256]{1,0:T(8,128)(2,1)S(1)} %get-tuple-element.33.refs_0_, ...), custom_call_target="tpu_custom_call" | custom-call | tf_op jit(solution)/shard_map/dense/pallas_call | solution.py:138
  21.1 0.1 collective-permute-start.10
  21.2 1.4 %collective-permute-done.10.came_ref.refs_1_ = bf16[288,256]{1,0:T(8,128)(2,1)S(1)} collective-permute-done((bf16[288,256]{1,0:T(8,128)(2,1)S(1)}, bf16[288,256]{1,0:T(8,128)(2,1)S(1)}, u32[]{:S(2)}, u32[]{:S(2)}) %collective-permute-start.10) | collective-permute-done | bytes 147488 | tf_op jit(solution)/shard_map/ppermute | solution.py:94
  22.6 1.1 %collective-permute-start.11 = (bf16[160,256]{1,0:T(8,128)(2,1)S(1)}, bf16[160,256]{1,0:T(8,128)(2,1)S(1)}, u32[]{:S(2)}, u32[]{:S(2)}) collective-permute-start(bf16[160,256]{1,0:T(8,128)(2,1)S(1)} %get-tuple-element.41), channel_id=1, source_target_pairs={{0,8},{1,9},{2,10},{3,11},{4,7},{5,6},{6,5},{7,4},{8,16},{9,17},{1... | collective-permute-start | bytes 245768 | tf_op jit(solution)/shard_map/ppermute | solution.py:303
  23.7 2.3 %collective-permute-start.12 = (bf16[160,256]{1,0:T(8,128)(2,1)S(1)}, bf16[160,256]{1,0:T(8,128)(2,1)S(1)}, u32[]{:S(2)}, u32[]{:S(2)}) collective-permute-start(bf16[160,256]{1,0:T(8,128)(2,1)S(1)} %get-tuple-element.42), channel_id=1, source_target_pairs={{0,16},{1,17},{2,18},{3,19},{4,5},{5,4},{6,7},{7,6},{8,24},{9,25},... | collective-permute-start | bytes 245768 | tf_op jit(solution)/shard_map/ppermute | solution.py:303
  26.0 2.4 %collective-permute-start.13 = (bf16[160,256]{1,0:T(8,128)(2,1)S(1)}, bf16[160,256]{1,0:T(8,128)(2,1)S(1)}, u32[]{:S(2)}, u32[]{:S(2)}) collective-permute-start(bf16[160,256]{1,0:T(8,128)(2,1)S(1)} %get-tuple-element.43), channel_id=1, source_target_pairs={{0,24},{1,25},{2,26},{3,27},{4,6},{5,7},{6,4},{7,5},{8,0},{9,1},{1... | collective-permute-start | bytes 245768 | tf_op jit(solution)/shard_map/ppermute | solution.py:303
  28.4 0.6 %collective-permute-done.11.refs_0_ = bf16[160,256]{1,0:T(8,128)(2,1)S(1)} collective-permute-done((bf16[160,256]{1,0:T(8,128)(2,1)S(1)}, bf16[160,256]{1,0:T(8,128)(2,1)S(1)}, u32[]{:S(2)}, u32[]{:S(2)}) %collective-permute-start.11) | collective-permute-done | bytes 81952 | tf_op jit(solution)/shard_map/ppermute | solution.py:303
  29.0 0.8 %collective-permute-done.12.refs_1_ = bf16[160,256]{1,0:T(8,128)(2,1)S(1)} collective-permute-done((bf16[160,256]{1,0:T(8,128)(2,1)S(1)}, bf16[160,256]{1,0:T(8,128)(2,1)S(1)}, u32[]{:S(2)}, u32[]{:S(2)}) %collective-permute-start.12) | collective-permute-done | bytes 81952 | tf_op jit(solution)/shard_map/ppermute | solution.py:303
  29.8 1.4 %collective-permute-done.13.refs_2_ = bf16[160,256]{1,0:T(8,128)(2,1)S(1)} collective-permute-done((bf16[160,256]{1,0:T(8,128)(2,1)S(1)}, bf16[160,256]{1,0:T(8,128)(2,1)S(1)}, u32[]{:S(2)}, u32[]{:S(2)}) %collective-permute-start.13) | collective-permute-done | bytes 81952 | tf_op jit(solution)/shard_map/ppermute | solution.py:303
  31.2 0.1 second.1
  31.3 1.6 %collective-permute-start.14 = (bf16[224,256]{1,0:T(8,128)(2,1)S(1)}, bf16[224,256]{1,0:T(8,128)(2,1)S(1)}, u32[]{:S(2)}, u32[]{:S(2)}) collective-permute-start(bf16[224,256]{1,0:T(8,128)(2,1)S(1)} %get-tuple-element.45), channel_id=1, source_target_pairs={{0,3},{1,2},{2,1},{3,0},{4,12},{5,13},{6,14},{7,15},{8,11},{9,10},... | collective-permute-start | bytes 344072 | tf_op jit(solution)/shard_map/ppermute | solution.py:303
  32.9 0.5 %collective-permute-start.15 = (bf16[224,256]{1,0:T(8,128)(2,1)S(1)}, bf16[224,256]{1,0:T(8,128)(2,1)S(1)}, u32[]{:S(2)}, u32[]{:S(2)}) collective-permute-start(bf16[224,256]{1,0:T(8,128)(2,1)S(1)} %get-tuple-element.46), channel_id=1, source_target_pairs={{0,1},{1,0},{2,3},{3,2},{4,20},{5,21},{6,22},{7,23},{8,9},{9,8},{1... | collective-permute-start | bytes 344072 | tf_op jit(solution)/shard_map/ppermute | solution.py:303
  33.4 1.4 %collective-permute-start.16 = (bf16[224,256]{1,0:T(8,128)(2,1)S(1)}, bf16[224,256]{1,0:T(8,128)(2,1)S(1)}, u32[]{:S(2)}, u32[]{:S(2)}) collective-permute-start(bf16[224,256]{1,0:T(8,128)(2,1)S(1)} %get-tuple-element.47), channel_id=1, source_target_pairs={{0,2},{1,3},{2,0},{3,1},{4,28},{5,29},{6,30},{7,31},{8,10},{9,11},... | collective-permute-start | bytes 344072 | tf_op jit(solution)/shard_map/ppermute | solution.py:303
  34.8 0.7 %store.2._ = bf16[8,32,256]{2,1,0:T(8,128)(2,1)} custom-call(bf16[128,256]{1,0:T(8,128)(2,1)S(1)} %get-tuple-element.37.same_ref.refs_0_, bf16[288,256]{1,0:T(8,128)(2,1)S(1)} %collective-permute-done.10.came_ref.refs_1_, bf16[160,256]{1,0:T(8,128)(2,1)S(1)} %collective-permute-done.11.refs_0_, bf16[160,256]{1,0:T(8,128)(2,1)S(1)} %collective-permute-done.12.refs_1_, ...), custom_call_target="tpu_custom_call" | custom-call | tf_op jit(solution)/shard_map/store/pallas_call | solution.py:256
  35.5 1.5 %collective-permute-done.14.refs_0_.refs_2_ = bf16[224,256]{1,0:T(8,128)(2,1)S(1)} collective-permute-done((bf16[224,256]{1,0:T(8,128)(2,1)S(1)}, bf16[224,256]{1,0:T(8,128)(2,1)S(1)}, u32[]{:S(2)}, u32[]{:S(2)}) %collective-permute-start.14) | collective-permute-done | bytes 114720 | tf_op jit(solution)/shard_map/ppermute | solution.py:303
  37.0 0.6 %collective-permute-done.15.refs_1_.refs_3_ = bf16[224,256]{1,0:T(8,128)(2,1)S(1)} collective-permute-done((bf16[224,256]{1,0:T(8,128)(2,1)S(1)}, bf16[224,256]{1,0:T(8,128)(2,1)S(1)}, u32[]{:S(2)}, u32[]{:S(2)}) %collective-permute-start.15) | collective-permute-done | bytes 114720 | tf_op jit(solution)/shard_map/ppermute | solution.py:303
  37.6 0.6 %collective-permute-done.16.refs_2_.refs_4_ = bf16[224,256]{1,0:T(8,128)(2,1)S(1)} collective-permute-done((bf16[224,256]{1,0:T(8,128)(2,1)S(1)}, bf16[224,256]{1,0:T(8,128)(2,1)S(1)}, u32[]{:S(2)}, u32[]{:S(2)}) %collective-permute-start.16) | collective-permute-done | bytes 114720 | tf_op jit(solution)/shard_map/ppermute | solution.py:303
  38.3 0.1 collective-permute-start.17
  38.4 1.3 %collective-permute-done.17.came_ref = bf16[160,256]{1,0:T(8,128)(2,1)S(1)} collective-permute-done((bf16[160,256]{1,0:T(8,128)(2,1)S(1)}, bf16[160,256]{1,0:T(8,128)(2,1)S(1)}, u32[]{:S(2)}, u32[]{:S(2)}) %collective-permute-start.17) | collective-permute-done | bytes 81952 | tf_op jit(solution)/shard_map/ppermute | solution.py:94
  39.6 0.7 %finish.1 = f32[256,256]{1,0:T(8,128)} custom-call(bf16[160,256]{1,0:T(8,128)(2,1)S(1)} %third.1.own_ref, bf16[160,256]{1,0:T(8,128)(2,1)S(1)} %collective-permute-done.17.came_ref), custom_call_target="tpu_custom_call" | custom-call | tf_op jit(solution)/shard_map/finish/pallas_call | solution.py:285
  (9 shorter events, 0.1 us)
Async XLA Ops:
  0.6 8.5 %collective-permute-start = (bf16[128,256]{1,0:T(8,128)(2,1)}, bf16[128,256]{1,0:T(8,128)(2,1)S(1)}, u32[]{:S(2)}, u32[]{:S(2)}) collective-permute-start(bf16[128,256]{1,0:T(8,128)(2,1)} %own_ref.1), channel_id=1, source_target_pairs={{0,16},{4,20},{8,24},{12,28},{16,0},{20,4},{24,8},{28,12},{1,17},{... | collective-permute-start | bytes 196616 | tf_op jit(solution)/shard_map/ppermute | solution.py:94
  4.7 6.4 %collective-permute-start.5 = (bf16[128,256]{1,0:T(8,128)(2,1)}, bf16[128,256]{1,0:T(8,128)(2,1)S(1)}, u32[]{:S(2)}, u32[]{:S(2)}) collective-permute-start(bf16[128,256]{1,0:T(8,128)(2,1)} %own_ref.1), channel_id=1, source_target_pairs={{0,24},{4,28},{8,16},{12,20},{16,8},{20,12},{24,0},{28,4},{1,25},{... | collective-permute-start | bytes 196616 | tf_op jit(solution)/shard_map/ppermute | solution.py:94
  6.1 5.2 %collective-permute-start.2 = (bf16[128,256]{1,0:T(8,128)(2,1)}, bf16[128,256]{1,0:T(8,128)(2,1)S(1)}, u32[]{:S(2)}, u32[]{:S(2)}) collective-permute-start(bf16[128,256]{1,0:T(8,128)(2,1)} %own_ref.1), channel_id=1, source_target_pairs={{0,8},{4,12},{8,0},{12,4},{16,24},{20,28},{24,16},{28,20},{1,9},{5... | collective-permute-start | bytes 196616 | tf_op jit(solution)/shard_map/ppermute | solution.py:94
  6.3 5.5 %collective-permute-start.1 = (bf16[128,256]{1,0:T(8,128)(2,1)}, bf16[128,256]{1,0:T(8,128)(2,1)S(1)}, u32[]{:S(2)}, u32[]{:S(2)}) collective-permute-start(bf16[128,256]{1,0:T(8,128)(2,1)} %own_ref.1), channel_id=1, source_target_pairs={{0,4},{4,0},{8,12},{12,8},{16,20},{20,16},{24,28},{28,24},{1,5},{5... | collective-permute-start | bytes 196616 | tf_op jit(solution)/shard_map/ppermute | solution.py:94
  6.3 0.7 %copy-start.5 = (s32[128,1]{0,1:T(1,128)S(1)}, s32[128,1]{0,1:T(1,128)}, u32[]{:S(2)}) copy-start(s32[128,1]{0,1:T(1,128)} %param.11) | copy-start | bytes 1540
  7.0 1.0 %copy-start = (bf16[4,1,4,128,128]{4,3,2,1,0:T(8,128)(2,1)S(1)}, bf16[4,1,4,128,128]{4,3,2,1,0:T(8,128)(2,1)}, u32[]{:S(2)}) copy-start(bf16[4,1,4,128,128]{4,3,2,1,0:T(8,128)(2,1)} %param.7) | copy-start | bytes 1572868
  8.0 0.8 %copy-start.2 = (bf16[128,256]{1,0:T(8,128)(2,1)S(1)}, bf16[128,256]{1,0:T(8,128)(2,1)}, u32[]{:S(2)}) copy-start(bf16[128,256]{1,0:T(8,128)(2,1)} %own_ref.1) | copy-start | bytes 196612
  9.1 3.8 %copy-start.4 = (s32[4,1,4]{2,1,0:T(1,128)S(1)}, s32[4,1,4]{2,1,0:T(1,128)}, u32[]{:S(2)}) copy-start(s32[4,1,4]{2,1,0:T(1,128)} %param.8) | copy-start | bytes 196
  11.2 1.3 %collective-permute-start.6 = (bf16[128,256]{1,0:T(8,128)(2,1)S(1)}, bf16[128,256]{1,0:T(8,128)(2,1)S(1)}, u32[]{:S(2)}, u32[]{:S(2)}) collective-permute-start(bf16[128,256]{1,0:T(8,128)(2,1)S(1)} %collective-permute-done.5.refs_6_), channel_id=1, source_target_pairs={{0,4},{4,0},{8,12},{12,8},{16,20},{20,16},{24,28},{28,24},{1,5},{5... | collective-permute-start | bytes 196616 | tf_op jit(solution)/shard_map/ppermute | solution.py:94
  11.3 1.3 %collective-permute-start.3 = (bf16[128,256]{1,0:T(8,128)(2,1)S(1)}, bf16[128,256]{1,0:T(8,128)(2,1)S(1)}, u32[]{:S(2)}, u32[]{:S(2)}) collective-permute-start(bf16[128,256]{1,0:T(8,128)(2,1)S(1)} %collective-permute-done.2.refs_2_), channel_id=1, source_target_pairs={{0,4},{4,0},{8,12},{12,8},{16,20},{20,16},{24,28},{28,24},{1,5},{5... | collective-permute-start | bytes 196616 | tf_op jit(solution)/shard_map/ppermute | solution.py:94
  11.7 1.3 %collective-permute-start.4 = (bf16[128,256]{1,0:T(8,128)(2,1)S(1)}, bf16[128,256]{1,0:T(8,128)(2,1)S(1)}, u32[]{:S(2)}, u32[]{:S(2)}) collective-permute-start(bf16[128,256]{1,0:T(8,128)(2,1)S(1)} %collective-permute-done.refs_4_), channel_id=1, source_target_pairs={{0,4},{4,0},{8,12},{12,8},{16,20},{20,16},{24,28},{28,24},{1,5},{5... | collective-permute-start | bytes 196616 | tf_op jit(solution)/shard_map/ppermute | solution.py:94
  12.9 7.7 %copy-start.1 = (bf16[256,256]{1,0:T(8,128)(2,1)S(1)}, bf16[256,256]{1,0:T(8,128)(2,1)}, u32[]{:S(2)}) copy-start(bf16[256,256]{1,0:T(8,128)(2,1)} %weight_ref.1) | copy-start | bytes 393220
  12.9 7.7 %copy-start.3 = (bf16[128,256]{1,0:T(8,128)(2,1)S(1)}, bf16[128,256]{1,0:T(8,128)(2,1)}, u32[]{:S(2)}) copy-start(bf16[128,256]{1,0:T(8,128)(2,1)} %cot_ref.1) | copy-start | bytes 196612
  13.4 5.6 %collective-permute-start.7 = (bf16[128,256]{1,0:T(8,128)(2,1)S(1)}, bf16[128,256]{1,0:T(8,128)(2,1)S(1)}, u32[]{:S(2)}, u32[]{:S(2)}) collective-permute-start(bf16[128,256]{1,0:T(8,128)(2,1)S(1)} %get-tuple-element.34), channel_id=1, source_target_pairs={{0,3},{1,2},{2,1},{3,0},{4,7},{5,6},{6,5},{7,4},{8,11},{9,10},{10,... | collective-permute-start | bytes 196616 | tf_op jit(solution)/shard_map/ppermute | solution.py:94
  15.9 4.3 %collective-permute-start.8 = (bf16[128,256]{1,0:T(8,128)(2,1)S(1)}, bf16[128,256]{1,0:T(8,128)(2,1)S(1)}, u32[]{:S(2)}, u32[]{:S(2)}) collective-permute-start(bf16[128,256]{1,0:T(8,128)(2,1)S(1)} %get-tuple-element.35), channel_id=1, source_target_pairs={{0,1},{1,0},{2,3},{3,2},{4,5},{5,4},{6,7},{7,6},{8,9},{9,8},{10,11... | collective-permute-start | bytes 196616 | tf_op jit(solution)/shard_map/ppermute | solution.py:94
  16.4 4.3 %collective-permute-start.9 = (bf16[128,256]{1,0:T(8,128)(2,1)S(1)}, bf16[128,256]{1,0:T(8,128)(2,1)S(1)}, u32[]{:S(2)}, u32[]{:S(2)}) collective-permute-start(bf16[128,256]{1,0:T(8,128)(2,1)S(1)} %get-tuple-element.36), channel_id=1, source_target_pairs={{0,2},{1,3},{2,0},{3,1},{4,6},{5,7},{6,4},{7,5},{8,10},{9,11},{10,... | collective-permute-start | bytes 196616 | tf_op jit(solution)/shard_map/ppermute | solution.py:94
  21.1 1.4 %collective-permute-start.10 = (bf16[288,256]{1,0:T(8,128)(2,1)S(1)}, bf16[288,256]{1,0:T(8,128)(2,1)S(1)}, u32[]{:S(2)}, u32[]{:S(2)}) collective-permute-start(bf16[288,256]{1,0:T(8,128)(2,1)S(1)} %get-tuple-element.38), channel_id=1, source_target_pairs={{0,4},{4,0},{8,12},{12,8},{16,20},{20,16},{24,28},{28,24},{1,5},{5... | collective-permute-start | bytes 442376 | tf_op jit(solution)/shard_map/ppermute | solution.py:94
  22.6 6.4 %collective-permute-start.11 = (bf16[160,256]{1,0:T(8,128)(2,1)S(1)}, bf16[160,256]{1,0:T(8,128)(2,1)S(1)}, u32[]{:S(2)}, u32[]{:S(2)}) collective-permute-start(bf16[160,256]{1,0:T(8,128)(2,1)S(1)} %get-tuple-element.41), channel_id=1, source_target_pairs={{0,8},{1,9},{2,10},{3,11},{4,7},{5,6},{6,5},{7,4},{8,16},{9,17},{1... | collective-permute-start | bytes 245768 | tf_op jit(solution)/shard_map/ppermute | solution.py:303
  23.7 6.1 %collective-permute-start.12 = (bf16[160,256]{1,0:T(8,128)(2,1)S(1)}, bf16[160,256]{1,0:T(8,128)(2,1)S(1)}, u32[]{:S(2)}, u32[]{:S(2)}) collective-permute-start(bf16[160,256]{1,0:T(8,128)(2,1)S(1)} %get-tuple-element.42), channel_id=1, source_target_pairs={{0,16},{1,17},{2,18},{3,19},{4,5},{5,4},{6,7},{7,6},{8,24},{9,25},... | collective-permute-start | bytes 245768 | tf_op jit(solution)/shard_map/ppermute | solution.py:303
  26.0 5.2 %collective-permute-start.13 = (bf16[160,256]{1,0:T(8,128)(2,1)S(1)}, bf16[160,256]{1,0:T(8,128)(2,1)S(1)}, u32[]{:S(2)}, u32[]{:S(2)}) collective-permute-start(bf16[160,256]{1,0:T(8,128)(2,1)S(1)} %get-tuple-element.43), channel_id=1, source_target_pairs={{0,24},{1,25},{2,26},{3,27},{4,6},{5,7},{6,4},{7,5},{8,0},{9,1},{1... | collective-permute-start | bytes 245768 | tf_op jit(solution)/shard_map/ppermute | solution.py:303
  31.3 5.7 %collective-permute-start.14 = (bf16[224,256]{1,0:T(8,128)(2,1)S(1)}, bf16[224,256]{1,0:T(8,128)(2,1)S(1)}, u32[]{:S(2)}, u32[]{:S(2)}) collective-permute-start(bf16[224,256]{1,0:T(8,128)(2,1)S(1)} %get-tuple-element.45), channel_id=1, source_target_pairs={{0,3},{1,2},{2,1},{3,0},{4,12},{5,13},{6,14},{7,15},{8,11},{9,10},... | collective-permute-start | bytes 344072 | tf_op jit(solution)/shard_map/ppermute | solution.py:303
  32.9 4.8 %collective-permute-start.15 = (bf16[224,256]{1,0:T(8,128)(2,1)S(1)}, bf16[224,256]{1,0:T(8,128)(2,1)S(1)}, u32[]{:S(2)}, u32[]{:S(2)}) collective-permute-start(bf16[224,256]{1,0:T(8,128)(2,1)S(1)} %get-tuple-element.46), channel_id=1, source_target_pairs={{0,1},{1,0},{2,3},{3,2},{4,20},{5,21},{6,22},{7,23},{8,9},{9,8},{1... | collective-permute-start | bytes 344072 | tf_op jit(solution)/shard_map/ppermute | solution.py:303
  33.4 4.8 %collective-permute-start.16 = (bf16[224,256]{1,0:T(8,128)(2,1)S(1)}, bf16[224,256]{1,0:T(8,128)(2,1)S(1)}, u32[]{:S(2)}, u32[]{:S(2)}) collective-permute-start(bf16[224,256]{1,0:T(8,128)(2,1)S(1)} %get-tuple-element.47), channel_id=1, source_target_pairs={{0,2},{1,3},{2,0},{3,1},{4,28},{5,29},{6,30},{7,31},{8,10},{9,11},... | collective-permute-start | bytes 344072 | tf_op jit(solution)/shard_map/ppermute | solution.py:303
  38.3 1.3 %collective-permute-start.17 = (bf16[160,256]{1,0:T(8,128)(2,1)S(1)}, bf16[160,256]{1,0:T(8,128)(2,1)S(1)}, u32[]{:S(2)}, u32[]{:S(2)}) collective-permute-start(bf16[160,256]{1,0:T(8,128)(2,1)S(1)} %third.1.own_ref), channel_id=1, source_target_pairs={{0,4},{4,0},{8,12},{12,8},{16,20},{20,16},{24,28},{28,24},{1,5},{5... | collective-permute-start | bytes 245768 | tf_op jit(solution)/shard_map/ppermute | solution.py:94

commit v28 on v26

--- a/solution.py
+++ b/solution.py
@@ -101,7 +101,7 @@
 
 
 def parts_of(width, slots):
-    low = (width - 2 * slots) // 2 // 16 * 16
+    low = (width - slots) // 2 // 16 * 16
     return low, width - low
 
 

time: 40.6 us -> 40.6 us (level)
  no operation moved by 1% of the time
where the time goes in v28:
time: 40.6 us; the launch traced here: 40.4 us
  starting transfers between devices  19.2 us (47%)
  waiting for transfers between devices  15.3 us (38%)
  Pallas kernels  2.64 us (7%)
  local copies, waits for them, and re-layouts  2.55 us (6%)
  between operations  0.74 us (2%)
    ppermute x12, starting transfers between devices, swap(): lax.ppermute(value, axis, [(i, i ^ j) for i in range(lax.axis_size(axis))])  9.89 us
    ppermute x12, waiting for transfers between devices, swap(): lax.ppermute(value, axis, [(i, i ^ j) for i in range(lax.axis_size(axis))])  9.65 us
    ppermute x6, starting transfers between devices, exchange(): return lax.ppermute(value, ('section', 'rep'), pairs)  9.28 us
    ppermute x6, waiting for transfers between devices, exchange(): return lax.ppermute(value, ('section', 'rep'), pairs)  5.65 us
    unnamed x12, local copies, waits for them, and re-layouts  2.55 us
  transfers between devices with their start and end apart: 18, of which 16 were waited for; matrix products, arithmetic and copies ran while one was open for 0% of the time, Pallas kernels for 2%

profile of v28, /device:TPU:0, one launch (start us, length us, event | category | flops | bytes accessed | tf_op | source)
XLA Modules:
  0.0 40.4 jit_solution(10072172563906003952)
XLA Ops:
  0.6 4.1 %collective-permute-start = (bf16[128,256]{1,0:T(8,128)(2,1)}, bf16[128,256]{1,0:T(8,128)(2,1)S(1)}, u32[]{:S(2)}, u32[]{:S(2)}) collective-permute-start(bf16[128,256]{1,0:T(8,128)(2,1)} %own_ref.1), channel_id=1, source_target_pairs={{0,16},{4,20},{8,24},{12,28},{16,0},{20,4},{24,8},{28,12},{1,17},{... | collective-permute-start | bytes 196616 | tf_op jit(solution)/shard_map/ppermute | solution.py:94
  4.7 1.3 %collective-permute-start.5 = (bf16[128,256]{1,0:T(8,128)(2,1)}, bf16[128,256]{1,0:T(8,128)(2,1)S(1)}, u32[]{:S(2)}, u32[]{:S(2)}) collective-permute-start(bf16[128,256]{1,0:T(8,128)(2,1)} %own_ref.1), channel_id=1, source_target_pairs={{0,24},{4,28},{8,16},{12,20},{16,8},{20,12},{24,0},{28,4},{1,25},{... | collective-permute-start | bytes 196616 | tf_op jit(solution)/shard_map/ppermute | solution.py:94
  6.1 0.2 collective-permute-start.2
  6.3 0.0 collective-permute-start.1
  6.3 0.7 %copy-done.5 = s32[128,1]{0,1:T(1,128)S(1)} copy-done((s32[128,1]{0,1:T(1,128)S(1)}, s32[128,1]{0,1:T(1,128)}, u32[]{:S(2)}) %copy-start.5) | copy-done | bytes 536
  7.0 1.0 %copy-done = bf16[4,1,4,128,128]{4,3,2,1,0:T(8,128)(2,1)S(1)} copy-done((bf16[4,1,4,128,128]{4,3,2,1,0:T(8,128)(2,1)S(1)}, bf16[4,1,4,128,128]{4,3,2,1,0:T(8,128)(2,1)}, u32[]{:S(2)}) %copy-start) | copy-done | bytes 524312
  8.0 0.8 %copy-done.2 = bf16[128,256]{1,0:T(8,128)(2,1)S(1)} copy-done((bf16[128,256]{1,0:T(8,128)(2,1)S(1)}, bf16[128,256]{1,0:T(8,128)(2,1)}, u32[]{:S(2)}) %copy-start.2) | copy-done | bytes 65560
  8.9 0.2 prepare.1
  9.1 0.0 collective-permute-done.refs_4_
  9.1 0.0 copy-start.4
  9.1 2.1 %collective-permute-done.5.refs_6_ = bf16[128,256]{1,0:T(8,128)(2,1)S(1)} collective-permute-done((bf16[128,256]{1,0:T(8,128)(2,1)}, bf16[128,256]{1,0:T(8,128)(2,1)S(1)}, u32[]{:S(2)}, u32[]{:S(2)}) %collective-permute-start.5) | collective-permute-done | bytes 65568 | tf_op jit(solution)/shard_map/ppermute | solution.py:94
  11.2 0.0 collective-permute-start.6
  11.2 0.1 collective-permute-done.2.refs_2_
  11.3 0.4 %collective-permute-start.3 = (bf16[128,256]{1,0:T(8,128)(2,1)S(1)}, bf16[128,256]{1,0:T(8,128)(2,1)S(1)}, u32[]{:S(2)}, u32[]{:S(2)}) collective-permute-start(bf16[128,256]{1,0:T(8,128)(2,1)S(1)} %collective-permute-done.2.refs_2_), channel_id=1, source_target_pairs={{0,4},{4,0},{8,12},{12,8},{16,20},{20,16},{24,28},{28,24},{1,5},{5... | collective-permute-start | bytes 196616 | tf_op jit(solution)/shard_map/ppermute | solution.py:94
  11.7 0.1 collective-permute-start.4
  11.8 0.0 collective-permute-done.1.refs_1_
  11.8 0.6 %collective-permute-done.6.refs_7_ = bf16[128,256]{1,0:T(8,128)(2,1)S(1)} collective-permute-done((bf16[128,256]{1,0:T(8,128)(2,1)S(1)}, bf16[128,256]{1,0:T(8,128)(2,1)S(1)}, u32[]{:S(2)}, u32[]{:S(2)}) %collective-permute-start.6) | collective-permute-done | bytes 65568 | tf_op jit(solution)/shard_map/ppermute | solution.py:94
  12.4 0.2 collective-permute-done.3.refs_3_
  12.6 0.4 collective-permute-done.4.refs_5_
  12.9 0.0 copy-done.4
  12.9 0.4 %partials.1 = (bf16[128,256]{1,0:T(8,128)(2,1)S(1)}, bf16[128,256]{1,0:T(8,128)(2,1)S(1)}, bf16[128,256]{1,0:T(8,128)(2,1)S(1)}, bf16[128,256]{1,0:T(8,128)(2,1)S(1)}) custom-call(s32[4,4]{1,0:T(4,128)S(1)} %bitcast.5, bf16[4,128,512]{2,1,0:T(8,128)(2,1)S(1)} %get-tuple-element.30.wide_ref, bf16[128,256]{1,0:T(8,128)(2,1)S(1)} %get-tuple-element.31.refs_0_, ...), custom_call_target="tpu_custom_call" | custom-call | tf_op jit(solution)/shard_map/partials/pallas_call | solution.py:82
  13.4 2.5 %collective-permute-start.7 = (bf16[128,256]{1,0:T(8,128)(2,1)S(1)}, bf16[128,256]{1,0:T(8,128)(2,1)S(1)}, u32[]{:S(2)}, u32[]{:S(2)}) collective-permute-start(bf16[128,256]{1,0:T(8,128)(2,1)S(1)} %get-tuple-element.34), channel_id=1, source_target_pairs={{0,3},{1,2},{2,1},{3,0},{4,7},{5,6},{6,5},{7,4},{8,11},{9,10},{10,... | collective-permute-start | bytes 196616 | tf_op jit(solution)/shard_map/ppermute | solution.py:94
  15.9 0.5 %collective-permute-start.8 = (bf16[128,256]{1,0:T(8,128)(2,1)S(1)}, bf16[128,256]{1,0:T(8,128)(2,1)S(1)}, u32[]{:S(2)}, u32[]{:S(2)}) collective-permute-start(bf16[128,256]{1,0:T(8,128)(2,1)S(1)} %get-tuple-element.35), channel_id=1, source_target_pairs={{0,2},{1,3},{2,0},{3,1},{4,6},{5,7},{6,4},{7,5},{8,10},{9,11},{10,... | collective-permute-start | bytes 196616 | tf_op jit(solution)/shard_map/ppermute | solution.py:94
  16.4 0.5 %collective-permute-start.9 = (bf16[128,256]{1,0:T(8,128)(2,1)S(1)}, bf16[128,256]{1,0:T(8,128)(2,1)S(1)}, u32[]{:S(2)}, u32[]{:S(2)}) collective-permute-start(bf16[128,256]{1,0:T(8,128)(2,1)S(1)} %get-tuple-element.36), channel_id=1, source_target_pairs={{0,1},{1,0},{2,3},{3,2},{4,5},{5,4},{6,7},{7,6},{8,9},{9,8},{10,11... | collective-permute-start | bytes 196616 | tf_op jit(solution)/shard_map/ppermute | solution.py:94
  16.9 1.7 %collective-permute-done.7.refs_1_ = bf16[128,256]{1,0:T(8,128)(2,1)S(1)} collective-permute-done((bf16[128,256]{1,0:T(8,128)(2,1)S(1)}, bf16[128,256]{1,0:T(8,128)(2,1)S(1)}, u32[]{:S(2)}, u32[]{:S(2)}) %collective-permute-start.7) | collective-permute-done | bytes 65568 | tf_op jit(solution)/shard_map/ppermute | solution.py:94
  18.6 1.5 %collective-permute-done.8.refs_2_ = bf16[128,256]{1,0:T(8,128)(2,1)S(1)} collective-permute-done((bf16[128,256]{1,0:T(8,128)(2,1)S(1)}, bf16[128,256]{1,0:T(8,128)(2,1)S(1)}, u32[]{:S(2)}, u32[]{:S(2)}) %collective-permute-start.8) | collective-permute-done | bytes 65568 | tf_op jit(solution)/shard_map/ppermute | solution.py:94
  20.2 0.5 %collective-permute-done.9.refs_3_ = bf16[128,256]{1,0:T(8,128)(2,1)S(1)} collective-permute-done((bf16[128,256]{1,0:T(8,128)(2,1)S(1)}, bf16[128,256]{1,0:T(8,128)(2,1)S(1)}, u32[]{:S(2)}, u32[]{:S(2)}) %collective-permute-start.9) | collective-permute-done | bytes 65568 | tf_op jit(solution)/shard_map/ppermute | solution.py:94
  20.7 0.0 copy-done.3
  20.7 0.4 %dense.1 = (bf16[128,256]{1,0:T(8,128)(2,1)S(1)}, f32[256,256]{1,0:T(8,128)S(1)}, bf16[272,256]{1,0:T(8,128)(2,1)S(1)}) custom-call(bf16[256,256]{1,0:T(8,128)(2,1)S(1)} %copy-done.1, bf16[128,256]{1,0:T(8,128)(2,1)S(1)} %copy-done.3, bf16[256,128]{1,0:T(8,128)(2,1)S(1)} %get-tuple-element.29.placing_ref, bf16[128,256]{1,0:T(8,128)(2,1)S(1)} %get-tuple-element.33.refs_0_, ...), custom_call_target="tpu_custom_call" | custom-call | tf_op jit(solution)/shard_map/dense/pallas_call | solution.py:138
  21.1 0.1 collective-permute-start.10
  21.2 1.3 %collective-permute-done.10.came_ref.refs_1_ = bf16[272,256]{1,0:T(8,128)(2,1)S(1)} collective-permute-done((bf16[272,256]{1,0:T(8,128)(2,1)S(1)}, bf16[272,256]{1,0:T(8,128)(2,1)S(1)}, u32[]{:S(2)}, u32[]{:S(2)}) %collective-permute-start.10) | collective-permute-done | bytes 139296 | tf_op jit(solution)/shard_map/ppermute | solution.py:94
  22.6 1.1 %collective-permute-start.11 = (bf16[176,256]{1,0:T(8,128)(2,1)S(1)}, bf16[176,256]{1,0:T(8,128)(2,1)S(1)}, u32[]{:S(2)}, u32[]{:S(2)}) collective-permute-start(bf16[176,256]{1,0:T(8,128)(2,1)S(1)} %get-tuple-element.41), channel_id=1, source_target_pairs={{0,8},{1,9},{2,10},{3,11},{4,7},{5,6},{6,5},{7,4},{8,16},{9,17},{1... | collective-permute-start | bytes 270344 | tf_op jit(solution)/shard_map/ppermute | solution.py:301
  23.6 2.3 %collective-permute-start.12 = (bf16[176,256]{1,0:T(8,128)(2,1)S(1)}, bf16[176,256]{1,0:T(8,128)(2,1)S(1)}, u32[]{:S(2)}, u32[]{:S(2)}) collective-permute-start(bf16[176,256]{1,0:T(8,128)(2,1)S(1)} %get-tuple-element.42), channel_id=1, source_target_pairs={{0,16},{1,17},{2,18},{3,19},{4,6},{5,7},{6,4},{7,5},{8,24},{9,25},... | collective-permute-start | bytes 270344 | tf_op jit(solution)/shard_map/ppermute | solution.py:301
  25.9 2.4 %collective-permute-start.13 = (bf16[176,256]{1,0:T(8,128)(2,1)S(1)}, bf16[176,256]{1,0:T(8,128)(2,1)S(1)}, u32[]{:S(2)}, u32[]{:S(2)}) collective-permute-start(bf16[176,256]{1,0:T(8,128)(2,1)S(1)} %get-tuple-element.43), channel_id=1, source_target_pairs={{0,24},{1,25},{2,26},{3,27},{4,5},{5,4},{6,7},{7,6},{8,0},{9,1},{1... | collective-permute-start | bytes 270344 | tf_op jit(solution)/shard_map/ppermute | solution.py:301
  28.3 0.7 %collective-permute-done.11.refs_0_ = bf16[176,256]{1,0:T(8,128)(2,1)S(1)} collective-permute-done((bf16[176,256]{1,0:T(8,128)(2,1)S(1)}, bf16[176,256]{1,0:T(8,128)(2,1)S(1)}, u32[]{:S(2)}, u32[]{:S(2)}) %collective-permute-start.11) | collective-permute-done | bytes 90144 | tf_op jit(solution)/shard_map/ppermute | solution.py:301
  29.0 0.9 %collective-permute-done.12.refs_1_ = bf16[176,256]{1,0:T(8,128)(2,1)S(1)} collective-permute-done((bf16[176,256]{1,0:T(8,128)(2,1)S(1)}, bf16[176,256]{1,0:T(8,128)(2,1)S(1)}, u32[]{:S(2)}, u32[]{:S(2)}) %collective-permute-start.12) | collective-permute-done | bytes 90144 | tf_op jit(solution)/shard_map/ppermute | solution.py:301
  30.0 1.4 %collective-permute-done.13.refs_2_ = bf16[176,256]{1,0:T(8,128)(2,1)S(1)} collective-permute-done((bf16[176,256]{1,0:T(8,128)(2,1)S(1)}, bf16[176,256]{1,0:T(8,128)(2,1)S(1)}, u32[]{:S(2)}, u32[]{:S(2)}) %collective-permute-start.13) | collective-permute-done | bytes 90144 | tf_op jit(solution)/shard_map/ppermute | solution.py:301
  31.3 0.1 second.1
  31.4 1.3 %collective-permute-start.14 = (bf16[208,256]{1,0:T(8,128)(2,1)S(1)}, bf16[208,256]{1,0:T(8,128)(2,1)S(1)}, u32[]{:S(2)}, u32[]{:S(2)}) collective-permute-start(bf16[208,256]{1,0:T(8,128)(2,1)S(1)} %get-tuple-element.45), channel_id=1, source_target_pairs={{0,3},{1,2},{2,1},{3,0},{4,12},{5,13},{6,14},{7,15},{8,11},{9,10},... | collective-permute-start | bytes 319496 | tf_op jit(solution)/shard_map/ppermute | solution.py:301
  32.7 0.9 %collective-permute-start.15 = (bf16[208,256]{1,0:T(8,128)(2,1)S(1)}, bf16[208,256]{1,0:T(8,128)(2,1)S(1)}, u32[]{:S(2)}, u32[]{:S(2)}) collective-permute-start(bf16[208,256]{1,0:T(8,128)(2,1)S(1)} %get-tuple-element.46), channel_id=1, source_target_pairs={{0,2},{1,3},{2,0},{3,1},{4,20},{5,21},{6,22},{7,23},{8,10},{9,11},... | collective-permute-start | bytes 319496 | tf_op jit(solution)/shard_map/ppermute | solution.py:301
  33.6 1.4 %collective-permute-start.16 = (bf16[208,256]{1,0:T(8,128)(2,1)S(1)}, bf16[208,256]{1,0:T(8,128)(2,1)S(1)}, u32[]{:S(2)}, u32[]{:S(2)}) collective-permute-start(bf16[208,256]{1,0:T(8,128)(2,1)S(1)} %get-tuple-element.47), channel_id=1, source_target_pairs={{0,1},{1,0},{2,3},{3,2},{4,28},{5,29},{6,30},{7,31},{8,9},{9,8},{1... | collective-permute-start | bytes 319496 | tf_op jit(solution)/shard_map/ppermute | solution.py:301
  35.0 0.7 %store.2._ = bf16[8,32,256]{2,1,0:T(8,128)(2,1)} custom-call(bf16[128,256]{1,0:T(8,128)(2,1)S(1)} %get-tuple-element.37.same_ref.refs_0_, bf16[272,256]{1,0:T(8,128)(2,1)S(1)} %collective-permute-done.10.came_ref.refs_1_, bf16[176,256]{1,0:T(8,128)(2,1)S(1)} %collective-permute-done.11.refs_0_, bf16[176,256]{1,0:T(8,128)(2,1)S(1)} %collective-permute-done.12.refs_1_, ...), custom_call_target="tpu_custom_call" | custom-call | tf_op jit(solution)/shard_map/store/pallas_call | solution.py:254
  35.6 1.5 %collective-permute-done.14.refs_0_.refs_2_ = bf16[208,256]{1,0:T(8,128)(2,1)S(1)} collective-permute-done((bf16[208,256]{1,0:T(8,128)(2,1)S(1)}, bf16[208,256]{1,0:T(8,128)(2,1)S(1)}, u32[]{:S(2)}, u32[]{:S(2)}) %collective-permute-start.14) | collective-permute-done | bytes 106528 | tf_op jit(solution)/shard_map/ppermute | solution.py:301
  37.2 1.1 %collective-permute-done.15.refs_1_.refs_3_ = bf16[208,256]{1,0:T(8,128)(2,1)S(1)} collective-permute-done((bf16[208,256]{1,0:T(8,128)(2,1)S(1)}, bf16[208,256]{1,0:T(8,128)(2,1)S(1)}, u32[]{:S(2)}, u32[]{:S(2)}) %collective-permute-start.15) | collective-permute-done | bytes 106528 | tf_op jit(solution)/shard_map/ppermute | solution.py:301
  38.2 0.1 collective-permute-done.16.refs_2_.refs_4_
  38.4 0.1 collective-permute-start.17
  38.4 1.3 %collective-permute-done.17.came_ref = bf16[144,256]{1,0:T(8,128)(2,1)S(1)} collective-permute-done((bf16[144,256]{1,0:T(8,128)(2,1)S(1)}, bf16[144,256]{1,0:T(8,128)(2,1)S(1)}, u32[]{:S(2)}, u32[]{:S(2)}) %collective-permute-start.17) | collective-permute-done | bytes 73760 | tf_op jit(solution)/shard_map/ppermute | solution.py:94
  39.7 0.7 %finish.1 = f32[256,256]{1,0:T(8,128)} custom-call(bf16[144,256]{1,0:T(8,128)(2,1)S(1)} %third.1.own_ref, bf16[144,256]{1,0:T(8,128)(2,1)S(1)} %collective-permute-done.17.came_ref), custom_call_target="tpu_custom_call" | custom-call | tf_op jit(solution)/shard_map/finish/pallas_call | solution.py:283
  (9 shorter events, 0.1 us)
Async XLA Ops:
  0.6 8.5 %collective-permute-start = (bf16[128,256]{1,0:T(8,128)(2,1)}, bf16[128,256]{1,0:T(8,128)(2,1)S(1)}, u32[]{:S(2)}, u32[]{:S(2)}) collective-permute-start(bf16[128,256]{1,0:T(8,128)(2,1)} %own_ref.1), channel_id=1, source_target_pairs={{0,16},{4,20},{8,24},{12,28},{16,0},{20,4},{24,8},{28,12},{1,17},{... | collective-permute-start | bytes 196616 | tf_op jit(solution)/shard_map/ppermute | solution.py:94
  4.7 6.4 %collective-permute-start.5 = (bf16[128,256]{1,0:T(8,128)(2,1)}, bf16[128,256]{1,0:T(8,128)(2,1)S(1)}, u32[]{:S(2)}, u32[]{:S(2)}) collective-permute-start(bf16[128,256]{1,0:T(8,128)(2,1)} %own_ref.1), channel_id=1, source_target_pairs={{0,24},{4,28},{8,16},{12,20},{16,8},{20,12},{24,0},{28,4},{1,25},{... | collective-permute-start | bytes 196616 | tf_op jit(solution)/shard_map/ppermute | solution.py:94
  6.1 5.2 %collective-permute-start.2 = (bf16[128,256]{1,0:T(8,128)(2,1)}, bf16[128,256]{1,0:T(8,128)(2,1)S(1)}, u32[]{:S(2)}, u32[]{:S(2)}) collective-permute-start(bf16[128,256]{1,0:T(8,128)(2,1)} %own_ref.1), channel_id=1, source_target_pairs={{0,8},{4,12},{8,0},{12,4},{16,24},{20,28},{24,16},{28,20},{1,9},{5... | collective-permute-start | bytes 196616 | tf_op jit(solution)/shard_map/ppermute | solution.py:94
  6.3 5.5 %collective-permute-start.1 = (bf16[128,256]{1,0:T(8,128)(2,1)}, bf16[128,256]{1,0:T(8,128)(2,1)S(1)}, u32[]{:S(2)}, u32[]{:S(2)}) collective-permute-start(bf16[128,256]{1,0:T(8,128)(2,1)} %own_ref.1), channel_id=1, source_target_pairs={{0,4},{4,0},{8,12},{12,8},{16,20},{20,16},{24,28},{28,24},{1,5},{5... | collective-permute-start | bytes 196616 | tf_op jit(solution)/shard_map/ppermute | solution.py:94
  6.3 0.7 %copy-start.5 = (s32[128,1]{0,1:T(1,128)S(1)}, s32[128,1]{0,1:T(1,128)}, u32[]{:S(2)}) copy-start(s32[128,1]{0,1:T(1,128)} %param.11) | copy-start | bytes 1540
  7.0 1.0 %copy-start = (bf16[4,1,4,128,128]{4,3,2,1,0:T(8,128)(2,1)S(1)}, bf16[4,1,4,128,128]{4,3,2,1,0:T(8,128)(2,1)}, u32[]{:S(2)}) copy-start(bf16[4,1,4,128,128]{4,3,2,1,0:T(8,128)(2,1)} %param.7) | copy-start | bytes 1572868
  8.0 0.8 %copy-start.2 = (bf16[128,256]{1,0:T(8,128)(2,1)S(1)}, bf16[128,256]{1,0:T(8,128)(2,1)}, u32[]{:S(2)}) copy-start(bf16[128,256]{1,0:T(8,128)(2,1)} %own_ref.1) | copy-start | bytes 196612
  9.1 3.8 %copy-start.4 = (s32[4,1,4]{2,1,0:T(1,128)S(1)}, s32[4,1,4]{2,1,0:T(1,128)}, u32[]{:S(2)}) copy-start(s32[4,1,4]{2,1,0:T(1,128)} %param.8) | copy-start | bytes 196
  11.2 1.3 %collective-permute-start.6 = (bf16[128,256]{1,0:T(8,128)(2,1)S(1)}, bf16[128,256]{1,0:T(8,128)(2,1)S(1)}, u32[]{:S(2)}, u32[]{:S(2)}) collective-permute-start(bf16[128,256]{1,0:T(8,128)(2,1)S(1)} %collective-permute-done.5.refs_6_), channel_id=1, source_target_pairs={{0,4},{4,0},{8,12},{12,8},{16,20},{20,16},{24,28},{28,24},{1,5},{5... | collective-permute-start | bytes 196616 | tf_op jit(solution)/shard_map/ppermute | solution.py:94
  11.3 1.3 %collective-permute-start.3 = (bf16[128,256]{1,0:T(8,128)(2,1)S(1)}, bf16[128,256]{1,0:T(8,128)(2,1)S(1)}, u32[]{:S(2)}, u32[]{:S(2)}) collective-permute-start(bf16[128,256]{1,0:T(8,128)(2,1)S(1)} %collective-permute-done.2.refs_2_), channel_id=1, source_target_pairs={{0,4},{4,0},{8,12},{12,8},{16,20},{20,16},{24,28},{28,24},{1,5},{5... | collective-permute-start | bytes 196616 | tf_op jit(solution)/shard_map/ppermute | solution.py:94
  11.7 1.3 %collective-permute-start.4 = (bf16[128,256]{1,0:T(8,128)(2,1)S(1)}, bf16[128,256]{1,0:T(8,128)(2,1)S(1)}, u32[]{:S(2)}, u32[]{:S(2)}) collective-permute-start(bf16[128,256]{1,0:T(8,128)(2,1)S(1)} %collective-permute-done.refs_4_), channel_id=1, source_target_pairs={{0,4},{4,0},{8,12},{12,8},{16,20},{20,16},{24,28},{28,24},{1,5},{5... | collective-permute-start | bytes 196616 | tf_op jit(solution)/shard_map/ppermute | solution.py:94
  12.9 7.7 %copy-start.1 = (bf16[256,256]{1,0:T(8,128)(2,1)S(1)}, bf16[256,256]{1,0:T(8,128)(2,1)}, u32[]{:S(2)}) copy-start(bf16[256,256]{1,0:T(8,128)(2,1)} %weight_ref.1) | copy-start | bytes 393220
  12.9 7.7 %copy-start.3 = (bf16[128,256]{1,0:T(8,128)(2,1)S(1)}, bf16[128,256]{1,0:T(8,128)(2,1)}, u32[]{:S(2)}) copy-start(bf16[128,256]{1,0:T(8,128)(2,1)} %cot_ref.1) | copy-start | bytes 196612
  13.4 5.3 %collective-permute-start.7 = (bf16[128,256]{1,0:T(8,128)(2,1)S(1)}, bf16[128,256]{1,0:T(8,128)(2,1)S(1)}, u32[]{:S(2)}, u32[]{:S(2)}) collective-permute-start(bf16[128,256]{1,0:T(8,128)(2,1)S(1)} %get-tuple-element.34), channel_id=1, source_target_pairs={{0,3},{1,2},{2,1},{3,0},{4,7},{5,6},{6,5},{7,4},{8,11},{9,10},{10,... | collective-permute-start | bytes 196616 | tf_op jit(solution)/shard_map/ppermute | solution.py:94
  15.9 4.3 %collective-permute-start.8 = (bf16[128,256]{1,0:T(8,128)(2,1)S(1)}, bf16[128,256]{1,0:T(8,128)(2,1)S(1)}, u32[]{:S(2)}, u32[]{:S(2)}) collective-permute-start(bf16[128,256]{1,0:T(8,128)(2,1)S(1)} %get-tuple-element.35), channel_id=1, source_target_pairs={{0,2},{1,3},{2,0},{3,1},{4,6},{5,7},{6,4},{7,5},{8,10},{9,11},{10,... | collective-permute-start | bytes 196616 | tf_op jit(solution)/shard_map/ppermute | solution.py:94
  16.4 4.3 %collective-permute-start.9 = (bf16[128,256]{1,0:T(8,128)(2,1)S(1)}, bf16[128,256]{1,0:T(8,128)(2,1)S(1)}, u32[]{:S(2)}, u32[]{:S(2)}) collective-permute-start(bf16[128,256]{1,0:T(8,128)(2,1)S(1)} %get-tuple-element.36), channel_id=1, source_target_pairs={{0,1},{1,0},{2,3},{3,2},{4,5},{5,4},{6,7},{7,6},{8,9},{9,8},{10,11... | collective-permute-start | bytes 196616 | tf_op jit(solution)/shard_map/ppermute | solution.py:94
  21.1 1.4 %collective-permute-start.10 = (bf16[272,256]{1,0:T(8,128)(2,1)S(1)}, bf16[272,256]{1,0:T(8,128)(2,1)S(1)}, u32[]{:S(2)}, u32[]{:S(2)}) collective-permute-start(bf16[272,256]{1,0:T(8,128)(2,1)S(1)} %get-tuple-element.38), channel_id=1, source_target_pairs={{0,4},{4,0},{8,12},{12,8},{16,20},{20,16},{24,28},{28,24},{1,5},{5... | collective-permute-start | bytes 417800 | tf_op jit(solution)/shard_map/ppermute | solution.py:94
  22.6 6.5 %collective-permute-start.11 = (bf16[176,256]{1,0:T(8,128)(2,1)S(1)}, bf16[176,256]{1,0:T(8,128)(2,1)S(1)}, u32[]{:S(2)}, u32[]{:S(2)}) collective-permute-start(bf16[176,256]{1,0:T(8,128)(2,1)S(1)} %get-tuple-element.41), channel_id=1, source_target_pairs={{0,8},{1,9},{2,10},{3,11},{4,7},{5,6},{6,5},{7,4},{8,16},{9,17},{1... | collective-permute-start | bytes 270344 | tf_op jit(solution)/shard_map/ppermute | solution.py:301
  23.6 6.3 %collective-permute-start.12 = (bf16[176,256]{1,0:T(8,128)(2,1)S(1)}, bf16[176,256]{1,0:T(8,128)(2,1)S(1)}, u32[]{:S(2)}, u32[]{:S(2)}) collective-permute-start(bf16[176,256]{1,0:T(8,128)(2,1)S(1)} %get-tuple-element.42), channel_id=1, source_target_pairs={{0,16},{1,17},{2,18},{3,19},{4,6},{5,7},{6,4},{7,5},{8,24},{9,25},... | collective-permute-start | bytes 270344 | tf_op jit(solution)/shard_map/ppermute | solution.py:301
  25.9 5.4 %collective-permute-start.13 = (bf16[176,256]{1,0:T(8,128)(2,1)S(1)}, bf16[176,256]{1,0:T(8,128)(2,1)S(1)}, u32[]{:S(2)}, u32[]{:S(2)}) collective-permute-start(bf16[176,256]{1,0:T(8,128)(2,1)S(1)} %get-tuple-element.43), channel_id=1, source_target_pairs={{0,24},{1,25},{2,26},{3,27},{4,5},{5,4},{6,7},{7,6},{8,0},{9,1},{1... | collective-permute-start | bytes 270344 | tf_op jit(solution)/shard_map/ppermute | solution.py:301
  31.4 5.7 %collective-permute-start.14 = (bf16[208,256]{1,0:T(8,128)(2,1)S(1)}, bf16[208,256]{1,0:T(8,128)(2,1)S(1)}, u32[]{:S(2)}, u32[]{:S(2)}) collective-permute-start(bf16[208,256]{1,0:T(8,128)(2,1)S(1)} %get-tuple-element.45), channel_id=1, source_target_pairs={{0,3},{1,2},{2,1},{3,0},{4,12},{5,13},{6,14},{7,15},{8,11},{9,10},... | collective-permute-start | bytes 319496 | tf_op jit(solution)/shard_map/ppermute | solution.py:301
  32.7 5.5 %collective-permute-start.15 = (bf16[208,256]{1,0:T(8,128)(2,1)S(1)}, bf16[208,256]{1,0:T(8,128)(2,1)S(1)}, u32[]{:S(2)}, u32[]{:S(2)}) collective-permute-start(bf16[208,256]{1,0:T(8,128)(2,1)S(1)} %get-tuple-element.46), channel_id=1, source_target_pairs={{0,2},{1,3},{2,0},{3,1},{4,20},{5,21},{6,22},{7,23},{8,10},{9,11},... | collective-permute-start | bytes 319496 | tf_op jit(solution)/shard_map/ppermute | solution.py:301
  33.6 4.7 %collective-permute-start.16 = (bf16[208,256]{1,0:T(8,128)(2,1)S(1)}, bf16[208,256]{1,0:T(8,128)(2,1)S(1)}, u32[]{:S(2)}, u32[]{:S(2)}) collective-permute-start(bf16[208,256]{1,0:T(8,128)(2,1)S(1)} %get-tuple-element.47), channel_id=1, source_target_pairs={{0,1},{1,0},{2,3},{3,2},{4,28},{5,29},{6,30},{7,31},{8,9},{9,8},{1... | collective-permute-start | bytes 319496 | tf_op jit(solution)/shard_map/ppermute | solution.py:301
  38.4 1.3 %collective-permute-start.17 = (bf16[144,256]{1,0:T(8,128)(2,1)S(1)}, bf16[144,256]{1,0:T(8,128)(2,1)S(1)}, u32[]{:S(2)}, u32[]{:S(2)}) collective-permute-start(bf16[144,256]{1,0:T(8,128)(2,1)S(1)} %third.1.own_ref), channel_id=1, source_target_pairs={{0,4},{4,0},{8,12},{12,8},{16,20},{20,16},{24,28},{28,24},{1,5},{5... | collective-permute-start | bytes 221192 | tf_op jit(solution)/shard_map/ppermute | solution.py:94

commit v29 on v26

--- a/solution.py
+++ b/solution.py
@@ -349,7 +349,6 @@
     third = functools.partial(third_kernel, slots, rows, n_rep)
     (half,) = call_parts(third, "third", [half, *second], part, part, 0, held)
     relaid = store(1, same, came, second, n_section, slots, relaid)
-    half, relaid = lax.optimization_barrier((half, relaid))
     weight_grad = finish(half, swap(half, "section", 1), rows)
     return (relaid.reshape(1, 1, n_section, slots, width), weight_grad)
 

time: 40.6 us -> 40.6 us (level)
    ppermute x12, waiting for transfers between devices: 9.67 us -> 8.93 us  [swap(): lax.ppermute(value, axis, [(i, i ^ j) for i in range(lax.axis_size(axis))])]
    ppermute x6, waiting for transfers between devices: 5.65 us -> 6.34 us  [exchange(): return lax.ppermute(value, ('section', 'rep'), pairs)]
where the time goes in v29:
time: 40.6 us; the launch traced here: 40.4 us
  starting transfers between devices  19.2 us (47%)
  waiting for transfers between devices  15.3 us (38%)
  Pallas kernels  2.64 us (7%)
  local copies, waits for them, and re-layouts  2.55 us (6%)
  between operations  0.74 us (2%)
    ppermute x12, starting transfers between devices, swap(): lax.ppermute(value, axis, [(i, i ^ j) for i in range(lax.axis_size(axis))])  9.89 us
    ppermute x6, starting transfers between devices, exchange(): return lax.ppermute(value, ('section', 'rep'), pairs)  9.28 us
    ppermute x12, waiting for transfers between devices, swap(): lax.ppermute(value, axis, [(i, i ^ j) for i in range(lax.axis_size(axis))])  8.93 us
    ppermute x6, waiting for transfers between devices, exchange(): return lax.ppermute(value, ('section', 'rep'), pairs)  6.34 us
    unnamed x12, local copies, waits for them, and re-layouts  2.55 us
  transfers between devices with their start and end apart: 18, of which 16 were waited for; matrix products, arithmetic and copies ran while one was open for 0% of the time, Pallas kernels for 2%

profile of v29, /device:TPU:0, one launch (start us, length us, event | category | flops | bytes accessed | tf_op | source)
XLA Modules:
  0.0 40.4 jit_solution(18358143527369348389)
XLA Ops:
  0.6 4.1 %collective-permute-start = (bf16[128,256]{1,0:T(8,128)(2,1)}, bf16[128,256]{1,0:T(8,128)(2,1)S(1)}, u32[]{:S(2)}, u32[]{:S(2)}) collective-permute-start(bf16[128,256]{1,0:T(8,128)(2,1)} %own_ref.1), channel_id=1, source_target_pairs={{0,16},{4,20},{8,24},{12,28},{16,0},{20,4},{24,8},{28,12},{1,17},{... | collective-permute-start | bytes 196616 | tf_op jit(solution)/shard_map/ppermute | solution.py:94
  4.7 1.3 %collective-permute-start.5 = (bf16[128,256]{1,0:T(8,128)(2,1)}, bf16[128,256]{1,0:T(8,128)(2,1)S(1)}, u32[]{:S(2)}, u32[]{:S(2)}) collective-permute-start(bf16[128,256]{1,0:T(8,128)(2,1)} %own_ref.1), channel_id=1, source_target_pairs={{0,24},{4,28},{8,16},{12,20},{16,8},{20,12},{24,0},{28,4},{1,25},{... | collective-permute-start | bytes 196616 | tf_op jit(solution)/shard_map/ppermute | solution.py:94
  6.1 0.2 collective-permute-start.2
  6.3 0.0 collective-permute-start.1
  6.3 0.7 %copy-done.5 = s32[128,1]{0,1:T(1,128)S(1)} copy-done((s32[128,1]{0,1:T(1,128)S(1)}, s32[128,1]{0,1:T(1,128)}, u32[]{:S(2)}) %copy-start.5) | copy-done | bytes 536
  7.0 1.0 %copy-done = bf16[4,1,4,128,128]{4,3,2,1,0:T(8,128)(2,1)S(1)} copy-done((bf16[4,1,4,128,128]{4,3,2,1,0:T(8,128)(2,1)S(1)}, bf16[4,1,4,128,128]{4,3,2,1,0:T(8,128)(2,1)}, u32[]{:S(2)}) %copy-start) | copy-done | bytes 524312
  8.0 0.8 %copy-done.2 = bf16[128,256]{1,0:T(8,128)(2,1)S(1)} copy-done((bf16[128,256]{1,0:T(8,128)(2,1)S(1)}, bf16[128,256]{1,0:T(8,128)(2,1)}, u32[]{:S(2)}) %copy-start.2) | copy-done | bytes 65560
  8.9 0.2 prepare.1
  9.1 0.0 collective-permute-done.refs_4_
  9.1 0.0 copy-start.4
  9.1 2.1 %collective-permute-done.5.refs_6_ = bf16[128,256]{1,0:T(8,128)(2,1)S(1)} collective-permute-done((bf16[128,256]{1,0:T(8,128)(2,1)}, bf16[128,256]{1,0:T(8,128)(2,1)S(1)}, u32[]{:S(2)}, u32[]{:S(2)}) %collective-permute-start.5) | collective-permute-done | bytes 65568 | tf_op jit(solution)/shard_map/ppermute | solution.py:94
  11.2 0.0 collective-permute-start.6
  11.2 0.1 collective-permute-done.2.refs_2_
  11.3 0.4 %collective-permute-start.3 = (bf16[128,256]{1,0:T(8,128)(2,1)S(1)}, bf16[128,256]{1,0:T(8,128)(2,1)S(1)}, u32[]{:S(2)}, u32[]{:S(2)}) collective-permute-start(bf16[128,256]{1,0:T(8,128)(2,1)S(1)} %collective-permute-done.2.refs_2_), channel_id=1, source_target_pairs={{0,4},{4,0},{8,12},{12,8},{16,20},{20,16},{24,28},{28,24},{1,5},{5... | collective-permute-start | bytes 196616 | tf_op jit(solution)/shard_map/ppermute | solution.py:94
  11.7 0.1 collective-permute-start.4
  11.8 0.0 collective-permute-done.1.refs_1_
  11.8 0.6 %collective-permute-done.6.refs_7_ = bf16[128,256]{1,0:T(8,128)(2,1)S(1)} collective-permute-done((bf16[128,256]{1,0:T(8,128)(2,1)S(1)}, bf16[128,256]{1,0:T(8,128)(2,1)S(1)}, u32[]{:S(2)}, u32[]{:S(2)}) %collective-permute-start.6) | collective-permute-done | bytes 65568 | tf_op jit(solution)/shard_map/ppermute | solution.py:94
  12.4 0.2 collective-permute-done.3.refs_3_
  12.6 0.4 collective-permute-done.4.refs_5_
  12.9 0.0 copy-done.4
  12.9 0.4 %partials.1 = (bf16[128,256]{1,0:T(8,128)(2,1)S(1)}, bf16[128,256]{1,0:T(8,128)(2,1)S(1)}, bf16[128,256]{1,0:T(8,128)(2,1)S(1)}, bf16[128,256]{1,0:T(8,128)(2,1)S(1)}) custom-call(s32[4,4]{1,0:T(4,128)S(1)} %bitcast.5, bf16[4,128,512]{2,1,0:T(8,128)(2,1)S(1)} %get-tuple-element.28.wide_ref, bf16[128,256]{1,0:T(8,128)(2,1)S(1)} %get-tuple-element.29.refs_0_, ...), custom_call_target="tpu_custom_call" | custom-call | tf_op jit(solution)/shard_map/partials/pallas_call | solution.py:82
  13.4 2.5 %collective-permute-start.7 = (bf16[128,256]{1,0:T(8,128)(2,1)S(1)}, bf16[128,256]{1,0:T(8,128)(2,1)S(1)}, u32[]{:S(2)}, u32[]{:S(2)}) collective-permute-start(bf16[128,256]{1,0:T(8,128)(2,1)S(1)} %get-tuple-element.32), channel_id=1, source_target_pairs={{0,3},{1,2},{2,1},{3,0},{4,7},{5,6},{6,5},{7,4},{8,11},{9,10},{10,... | collective-permute-start | bytes 196616 | tf_op jit(solution)/shard_map/ppermute | solution.py:94
  15.9 0.5 %collective-permute-start.8 = (bf16[128,256]{1,0:T(8,128)(2,1)S(1)}, bf16[128,256]{1,0:T(8,128)(2,1)S(1)}, u32[]{:S(2)}, u32[]{:S(2)}) collective-permute-start(bf16[128,256]{1,0:T(8,128)(2,1)S(1)} %get-tuple-element.33), channel_id=1, source_target_pairs={{0,2},{1,3},{2,0},{3,1},{4,6},{5,7},{6,4},{7,5},{8,10},{9,11},{10,... | collective-permute-start | bytes 196616 | tf_op jit(solution)/shard_map/ppermute | solution.py:94
  16.4 0.5 %collective-permute-start.9 = (bf16[128,256]{1,0:T(8,128)(2,1)S(1)}, bf16[128,256]{1,0:T(8,128)(2,1)S(1)}, u32[]{:S(2)}, u32[]{:S(2)}) collective-permute-start(bf16[128,256]{1,0:T(8,128)(2,1)S(1)} %get-tuple-element.34), channel_id=1, source_target_pairs={{0,1},{1,0},{2,3},{3,2},{4,5},{5,4},{6,7},{7,6},{8,9},{9,8},{10,11... | collective-permute-start | bytes 196616 | tf_op jit(solution)/shard_map/ppermute | solution.py:94
  16.9 1.7 %collective-permute-done.7.refs_1_ = bf16[128,256]{1,0:T(8,128)(2,1)S(1)} collective-permute-done((bf16[128,256]{1,0:T(8,128)(2,1)S(1)}, bf16[128,256]{1,0:T(8,128)(2,1)S(1)}, u32[]{:S(2)}, u32[]{:S(2)}) %collective-permute-start.7) | collective-permute-done | bytes 65568 | tf_op jit(solution)/shard_map/ppermute | solution.py:94
  18.6 1.5 %collective-permute-done.8.refs_2_ = bf16[128,256]{1,0:T(8,128)(2,1)S(1)} collective-permute-done((bf16[128,256]{1,0:T(8,128)(2,1)S(1)}, bf16[128,256]{1,0:T(8,128)(2,1)S(1)}, u32[]{:S(2)}, u32[]{:S(2)}) %collective-permute-start.8) | collective-permute-done | bytes 65568 | tf_op jit(solution)/shard_map/ppermute | solution.py:94
  20.2 0.5 %collective-permute-done.9.refs_3_ = bf16[128,256]{1,0:T(8,128)(2,1)S(1)} collective-permute-done((bf16[128,256]{1,0:T(8,128)(2,1)S(1)}, bf16[128,256]{1,0:T(8,128)(2,1)S(1)}, u32[]{:S(2)}, u32[]{:S(2)}) %collective-permute-start.9) | collective-permute-done | bytes 65568 | tf_op jit(solution)/shard_map/ppermute | solution.py:94
  20.7 0.0 copy-done.1
  20.7 0.4 %dense.1 = (bf16[128,256]{1,0:T(8,128)(2,1)S(1)}, f32[256,256]{1,0:T(8,128)S(1)}, bf16[288,256]{1,0:T(8,128)(2,1)S(1)}) custom-call(bf16[256,256]{1,0:T(8,128)(2,1)S(1)} %copy-done.1, bf16[128,256]{1,0:T(8,128)(2,1)S(1)} %copy-done.3, bf16[256,128]{1,0:T(8,128)(2,1)S(1)} %get-tuple-element.27.placing_ref, bf16[128,256]{1,0:T(8,128)(2,1)S(1)} %get-tuple-element.31.refs_0_, ...), custom_call_target="tpu_custom_call" | custom-call | tf_op jit(solution)/shard_map/dense/pallas_call | solution.py:138
  21.1 0.1 collective-permute-start.10
  21.2 1.4 %collective-permute-done.10.came_ref.refs_1_ = bf16[288,256]{1,0:T(8,128)(2,1)S(1)} collective-permute-done((bf16[288,256]{1,0:T(8,128)(2,1)S(1)}, bf16[288,256]{1,0:T(8,128)(2,1)S(1)}, u32[]{:S(2)}, u32[]{:S(2)}) %collective-permute-start.10) | collective-permute-done | bytes 147488 | tf_op jit(solution)/shard_map/ppermute | solution.py:94
  22.6 1.1 %collective-permute-start.11 = (bf16[160,256]{1,0:T(8,128)(2,1)S(1)}, bf16[160,256]{1,0:T(8,128)(2,1)S(1)}, u32[]{:S(2)}, u32[]{:S(2)}) collective-permute-start(bf16[160,256]{1,0:T(8,128)(2,1)S(1)} %get-tuple-element.38), channel_id=1, source_target_pairs={{0,8},{1,9},{2,10},{3,11},{4,7},{5,6},{6,5},{7,4},{8,16},{9,17},{1... | collective-permute-start | bytes 245768 | tf_op jit(solution)/shard_map/ppermute | solution.py:301
  23.6 2.3 %collective-permute-start.12 = (bf16[160,256]{1,0:T(8,128)(2,1)S(1)}, bf16[160,256]{1,0:T(8,128)(2,1)S(1)}, u32[]{:S(2)}, u32[]{:S(2)}) collective-permute-start(bf16[160,256]{1,0:T(8,128)(2,1)S(1)} %get-tuple-element.39), channel_id=1, source_target_pairs={{0,16},{1,17},{2,18},{3,19},{4,6},{5,7},{6,4},{7,5},{8,24},{9,25},... | collective-permute-start | bytes 245768 | tf_op jit(solution)/shard_map/ppermute | solution.py:301
  25.9 2.4 %collective-permute-start.13 = (bf16[160,256]{1,0:T(8,128)(2,1)S(1)}, bf16[160,256]{1,0:T(8,128)(2,1)S(1)}, u32[]{:S(2)}, u32[]{:S(2)}) collective-permute-start(bf16[160,256]{1,0:T(8,128)(2,1)S(1)} %get-tuple-element.40), channel_id=1, source_target_pairs={{0,24},{1,25},{2,26},{3,27},{4,5},{5,4},{6,7},{7,6},{8,0},{9,1},{1... | collective-permute-start | bytes 245768 | tf_op jit(solution)/shard_map/ppermute | solution.py:301
  28.3 0.6 %collective-permute-done.11.refs_0_ = bf16[160,256]{1,0:T(8,128)(2,1)S(1)} collective-permute-done((bf16[160,256]{1,0:T(8,128)(2,1)S(1)}, bf16[160,256]{1,0:T(8,128)(2,1)S(1)}, u32[]{:S(2)}, u32[]{:S(2)}) %collective-permute-start.11) | collective-permute-done | bytes 81952 | tf_op jit(solution)/shard_map/ppermute | solution.py:301
  29.0 0.8 %collective-permute-done.12.refs_1_ = bf16[160,256]{1,0:T(8,128)(2,1)S(1)} collective-permute-done((bf16[160,256]{1,0:T(8,128)(2,1)S(1)}, bf16[160,256]{1,0:T(8,128)(2,1)S(1)}, u32[]{:S(2)}, u32[]{:S(2)}) %collective-permute-start.12) | collective-permute-done | bytes 81952 | tf_op jit(solution)/shard_map/ppermute | solution.py:301
  29.8 1.4 %collective-permute-done.13.refs_2_ = bf16[160,256]{1,0:T(8,128)(2,1)S(1)} collective-permute-done((bf16[160,256]{1,0:T(8,128)(2,1)S(1)}, bf16[160,256]{1,0:T(8,128)(2,1)S(1)}, u32[]{:S(2)}, u32[]{:S(2)}) %collective-permute-start.13) | collective-permute-done | bytes 81952 | tf_op jit(solution)/shard_map/ppermute | solution.py:301
  31.2 0.1 second.1
  31.2 1.2 %collective-permute-start.14 = (bf16[224,256]{1,0:T(8,128)(2,1)S(1)}, bf16[224,256]{1,0:T(8,128)(2,1)S(1)}, u32[]{:S(2)}, u32[]{:S(2)}) collective-permute-start(bf16[224,256]{1,0:T(8,128)(2,1)S(1)} %get-tuple-element.42), channel_id=1, source_target_pairs={{0,3},{1,2},{2,1},{3,0},{4,12},{5,13},{6,14},{7,15},{8,11},{9,10},... | collective-permute-start | bytes 344072 | tf_op jit(solution)/shard_map/ppermute | solution.py:301
  32.5 1.0 %collective-permute-start.15 = (bf16[224,256]{1,0:T(8,128)(2,1)S(1)}, bf16[224,256]{1,0:T(8,128)(2,1)S(1)}, u32[]{:S(2)}, u32[]{:S(2)}) collective-permute-start(bf16[224,256]{1,0:T(8,128)(2,1)S(1)} %get-tuple-element.43), channel_id=1, source_target_pairs={{0,2},{1,3},{2,0},{3,1},{4,20},{5,21},{6,22},{7,23},{8,10},{9,11},... | collective-permute-start | bytes 344072 | tf_op jit(solution)/shard_map/ppermute | solution.py:301
  33.5 1.3 %collective-permute-start.16 = (bf16[224,256]{1,0:T(8,128)(2,1)S(1)}, bf16[224,256]{1,0:T(8,128)(2,1)S(1)}, u32[]{:S(2)}, u32[]{:S(2)}) collective-permute-start(bf16[224,256]{1,0:T(8,128)(2,1)S(1)} %get-tuple-element.44), channel_id=1, source_target_pairs={{0,1},{1,0},{2,3},{3,2},{4,28},{5,29},{6,30},{7,31},{8,9},{9,8},{1... | collective-permute-start | bytes 344072 | tf_op jit(solution)/shard_map/ppermute | solution.py:301
  34.8 2.3 %collective-permute-done.14.refs_2_.refs_0_ = bf16[224,256]{1,0:T(8,128)(2,1)S(1)} collective-permute-done((bf16[224,256]{1,0:T(8,128)(2,1)S(1)}, bf16[224,256]{1,0:T(8,128)(2,1)S(1)}, u32[]{:S(2)}, u32[]{:S(2)}) %collective-permute-start.14) | collective-permute-done | bytes 114720 | tf_op jit(solution)/shard_map/ppermute | solution.py:301
  37.1 1.1 %collective-permute-done.15.refs_3_.refs_1_ = bf16[224,256]{1,0:T(8,128)(2,1)S(1)} collective-permute-done((bf16[224,256]{1,0:T(8,128)(2,1)S(1)}, bf16[224,256]{1,0:T(8,128)(2,1)S(1)}, u32[]{:S(2)}, u32[]{:S(2)}) %collective-permute-start.15) | collective-permute-done | bytes 114720 | tf_op jit(solution)/shard_map/ppermute | solution.py:301
  38.2 0.1 collective-permute-done.16.refs_4_.refs_2_
  38.3 0.1 collective-permute-start.17
  38.4 0.7 %store.2._ = bf16[8,32,256]{2,1,0:T(8,128)(2,1)} custom-call(bf16[128,256]{1,0:T(8,128)(2,1)S(1)} %get-tuple-element.35.same_ref.refs_0_, bf16[288,256]{1,0:T(8,128)(2,1)S(1)} %collective-permute-done.10.came_ref.refs_1_, bf16[160,256]{1,0:T(8,128)(2,1)S(1)} %collective-permute-done.11.refs_0_, bf16[160,256]{1,0:T(8,128)(2,1)S(1)} %collective-permute-done.12.refs_1_, ...), custom_call_target="tpu_custom_call" | custom-call | tf_op jit(solution)/shard_map/store/pallas_call | solution.py:254
  39.1 0.5 %collective-permute-done.17.came_ref = bf16[160,256]{1,0:T(8,128)(2,1)S(1)} collective-permute-done((bf16[160,256]{1,0:T(8,128)(2,1)S(1)}, bf16[160,256]{1,0:T(8,128)(2,1)S(1)}, u32[]{:S(2)}, u32[]{:S(2)}) %collective-permute-start.17) | collective-permute-done | bytes 81952 | tf_op jit(solution)/shard_map/ppermute | solution.py:94
  39.6 0.7 %finish.1 = f32[256,256]{1,0:T(8,128)} custom-call(bf16[160,256]{1,0:T(8,128)(2,1)S(1)} %third.1.own_ref, bf16[160,256]{1,0:T(8,128)(2,1)S(1)} %collective-permute-done.17.came_ref), custom_call_target="tpu_custom_call" | custom-call | tf_op jit(solution)/shard_map/finish/pallas_call | solution.py:283
  (9 shorter events, 0.1 us)
Async XLA Ops:
  0.6 8.5 %collective-permute-start = (bf16[128,256]{1,0:T(8,128)(2,1)}, bf16[128,256]{1,0:T(8,128)(2,1)S(1)}, u32[]{:S(2)}, u32[]{:S(2)}) collective-permute-start(bf16[128,256]{1,0:T(8,128)(2,1)} %own_ref.1), channel_id=1, source_target_pairs={{0,16},{4,20},{8,24},{12,28},{16,0},{20,4},{24,8},{28,12},{1,17},{... | collective-permute-start | bytes 196616 | tf_op jit(solution)/shard_map/ppermute | solution.py:94
  4.7 6.4 %collective-permute-start.5 = (bf16[128,256]{1,0:T(8,128)(2,1)}, bf16[128,256]{1,0:T(8,128)(2,1)S(1)}, u32[]{:S(2)}, u32[]{:S(2)}) collective-permute-start(bf16[128,256]{1,0:T(8,128)(2,1)} %own_ref.1), channel_id=1, source_target_pairs={{0,24},{4,28},{8,16},{12,20},{16,8},{20,12},{24,0},{28,4},{1,25},{... | collective-permute-start | bytes 196616 | tf_op jit(solution)/shard_map/ppermute | solution.py:94
  6.1 5.2 %collective-permute-start.2 = (bf16[128,256]{1,0:T(8,128)(2,1)}, bf16[128,256]{1,0:T(8,128)(2,1)S(1)}, u32[]{:S(2)}, u32[]{:S(2)}) collective-permute-start(bf16[128,256]{1,0:T(8,128)(2,1)} %own_ref.1), channel_id=1, source_target_pairs={{0,8},{4,12},{8,0},{12,4},{16,24},{20,28},{24,16},{28,20},{1,9},{5... | collective-permute-start | bytes 196616 | tf_op jit(solution)/shard_map/ppermute | solution.py:94
  6.3 5.5 %collective-permute-start.1 = (bf16[128,256]{1,0:T(8,128)(2,1)}, bf16[128,256]{1,0:T(8,128)(2,1)S(1)}, u32[]{:S(2)}, u32[]{:S(2)}) collective-permute-start(bf16[128,256]{1,0:T(8,128)(2,1)} %own_ref.1), channel_id=1, source_target_pairs={{0,4},{4,0},{8,12},{12,8},{16,20},{20,16},{24,28},{28,24},{1,5},{5... | collective-permute-start | bytes 196616 | tf_op jit(solution)/shard_map/ppermute | solution.py:94
  6.3 0.7 %copy-start.5 = (s32[128,1]{0,1:T(1,128)S(1)}, s32[128,1]{0,1:T(1,128)}, u32[]{:S(2)}) copy-start(s32[128,1]{0,1:T(1,128)} %param.11) | copy-start | bytes 1540
  7.0 1.0 %copy-start = (bf16[4,1,4,128,128]{4,3,2,1,0:T(8,128)(2,1)S(1)}, bf16[4,1,4,128,128]{4,3,2,1,0:T(8,128)(2,1)}, u32[]{:S(2)}) copy-start(bf16[4,1,4,128,128]{4,3,2,1,0:T(8,128)(2,1)} %param.7) | copy-start | bytes 1572868
  8.0 0.8 %copy-start.2 = (bf16[128,256]{1,0:T(8,128)(2,1)S(1)}, bf16[128,256]{1,0:T(8,128)(2,1)}, u32[]{:S(2)}) copy-start(bf16[128,256]{1,0:T(8,128)(2,1)} %own_ref.1) | copy-start | bytes 196612
  9.1 3.8 %copy-start.4 = (s32[4,1,4]{2,1,0:T(1,128)S(1)}, s32[4,1,4]{2,1,0:T(1,128)}, u32[]{:S(2)}) copy-start(s32[4,1,4]{2,1,0:T(1,128)} %param.8) | copy-start | bytes 196
  11.2 1.3 %collective-permute-start.6 = (bf16[128,256]{1,0:T(8,128)(2,1)S(1)}, bf16[128,256]{1,0:T(8,128)(2,1)S(1)}, u32[]{:S(2)}, u32[]{:S(2)}) collective-permute-start(bf16[128,256]{1,0:T(8,128)(2,1)S(1)} %collective-permute-done.5.refs_6_), channel_id=1, source_target_pairs={{0,4},{4,0},{8,12},{12,8},{16,20},{20,16},{24,28},{28,24},{1,5},{5... | collective-permute-start | bytes 196616 | tf_op jit(solution)/shard_map/ppermute | solution.py:94
  11.3 1.3 %collective-permute-start.3 = (bf16[128,256]{1,0:T(8,128)(2,1)S(1)}, bf16[128,256]{1,0:T(8,128)(2,1)S(1)}, u32[]{:S(2)}, u32[]{:S(2)}) collective-permute-start(bf16[128,256]{1,0:T(8,128)(2,1)S(1)} %collective-permute-done.2.refs_2_), channel_id=1, source_target_pairs={{0,4},{4,0},{8,12},{12,8},{16,20},{20,16},{24,28},{28,24},{1,5},{5... | collective-permute-start | bytes 196616 | tf_op jit(solution)/shard_map/ppermute | solution.py:94
  11.7 1.3 %collective-permute-start.4 = (bf16[128,256]{1,0:T(8,128)(2,1)S(1)}, bf16[128,256]{1,0:T(8,128)(2,1)S(1)}, u32[]{:S(2)}, u32[]{:S(2)}) collective-permute-start(bf16[128,256]{1,0:T(8,128)(2,1)S(1)} %collective-permute-done.refs_4_), channel_id=1, source_target_pairs={{0,4},{4,0},{8,12},{12,8},{16,20},{20,16},{24,28},{28,24},{1,5},{5... | collective-permute-start | bytes 196616 | tf_op jit(solution)/shard_map/ppermute | solution.py:94
  12.9 7.7 %copy-start.1 = (bf16[256,256]{1,0:T(8,128)(2,1)S(1)}, bf16[256,256]{1,0:T(8,128)(2,1)}, u32[]{:S(2)}) copy-start(bf16[256,256]{1,0:T(8,128)(2,1)} %weight_ref.1) | copy-start | bytes 393220
  12.9 7.7 %copy-start.3 = (bf16[128,256]{1,0:T(8,128)(2,1)S(1)}, bf16[128,256]{1,0:T(8,128)(2,1)}, u32[]{:S(2)}) copy-start(bf16[128,256]{1,0:T(8,128)(2,1)} %cot_ref.1) | copy-start | bytes 196612
  13.4 5.3 %collective-permute-start.7 = (bf16[128,256]{1,0:T(8,128)(2,1)S(1)}, bf16[128,256]{1,0:T(8,128)(2,1)S(1)}, u32[]{:S(2)}, u32[]{:S(2)}) collective-permute-start(bf16[128,256]{1,0:T(8,128)(2,1)S(1)} %get-tuple-element.32), channel_id=1, source_target_pairs={{0,3},{1,2},{2,1},{3,0},{4,7},{5,6},{6,5},{7,4},{8,11},{9,10},{10,... | collective-permute-start | bytes 196616 | tf_op jit(solution)/shard_map/ppermute | solution.py:94
  15.9 4.3 %collective-permute-start.8 = (bf16[128,256]{1,0:T(8,128)(2,1)S(1)}, bf16[128,256]{1,0:T(8,128)(2,1)S(1)}, u32[]{:S(2)}, u32[]{:S(2)}) collective-permute-start(bf16[128,256]{1,0:T(8,128)(2,1)S(1)} %get-tuple-element.33), channel_id=1, source_target_pairs={{0,2},{1,3},{2,0},{3,1},{4,6},{5,7},{6,4},{7,5},{8,10},{9,11},{10,... | collective-permute-start | bytes 196616 | tf_op jit(solution)/shard_map/ppermute | solution.py:94
  16.4 4.3 %collective-permute-start.9 = (bf16[128,256]{1,0:T(8,128)(2,1)S(1)}, bf16[128,256]{1,0:T(8,128)(2,1)S(1)}, u32[]{:S(2)}, u32[]{:S(2)}) collective-permute-start(bf16[128,256]{1,0:T(8,128)(2,1)S(1)} %get-tuple-element.34), channel_id=1, source_target_pairs={{0,1},{1,0},{2,3},{3,2},{4,5},{5,4},{6,7},{7,6},{8,9},{9,8},{10,11... | collective-permute-start | bytes 196616 | tf_op jit(solution)/shard_map/ppermute | solution.py:94
  21.1 1.4 %collective-permute-start.10 = (bf16[288,256]{1,0:T(8,128)(2,1)S(1)}, bf16[288,256]{1,0:T(8,128)(2,1)S(1)}, u32[]{:S(2)}, u32[]{:S(2)}) collective-permute-start(bf16[288,256]{1,0:T(8,128)(2,1)S(1)} %get-tuple-element.36), channel_id=1, source_target_pairs={{0,4},{4,0},{8,12},{12,8},{16,20},{20,16},{24,28},{28,24},{1,5},{5... | collective-permute-start | bytes 442376 | tf_op jit(solution)/shard_map/ppermute | solution.py:94
  22.6 6.4 %collective-permute-start.11 = (bf16[160,256]{1,0:T(8,128)(2,1)S(1)}, bf16[160,256]{1,0:T(8,128)(2,1)S(1)}, u32[]{:S(2)}, u32[]{:S(2)}) collective-permute-start(bf16[160,256]{1,0:T(8,128)(2,1)S(1)} %get-tuple-element.38), channel_id=1, source_target_pairs={{0,8},{1,9},{2,10},{3,11},{4,7},{5,6},{6,5},{7,4},{8,16},{9,17},{1... | collective-permute-start | bytes 245768 | tf_op jit(solution)/shard_map/ppermute | solution.py:301
  23.6 6.1 %collective-permute-start.12 = (bf16[160,256]{1,0:T(8,128)(2,1)S(1)}, bf16[160,256]{1,0:T(8,128)(2,1)S(1)}, u32[]{:S(2)}, u32[]{:S(2)}) collective-permute-start(bf16[160,256]{1,0:T(8,128)(2,1)S(1)} %get-tuple-element.39), channel_id=1, source_target_pairs={{0,16},{1,17},{2,18},{3,19},{4,6},{5,7},{6,4},{7,5},{8,24},{9,25},... | collective-permute-start | bytes 245768 | tf_op jit(solution)/shard_map/ppermute | solution.py:301
  25.9 5.2 %collective-permute-start.13 = (bf16[160,256]{1,0:T(8,128)(2,1)S(1)}, bf16[160,256]{1,0:T(8,128)(2,1)S(1)}, u32[]{:S(2)}, u32[]{:S(2)}) collective-permute-start(bf16[160,256]{1,0:T(8,128)(2,1)S(1)} %get-tuple-element.40), channel_id=1, source_target_pairs={{0,24},{1,25},{2,26},{3,27},{4,5},{5,4},{6,7},{7,6},{8,0},{9,1},{1... | collective-permute-start | bytes 245768 | tf_op jit(solution)/shard_map/ppermute | solution.py:301
  31.2 5.8 %collective-permute-start.14 = (bf16[224,256]{1,0:T(8,128)(2,1)S(1)}, bf16[224,256]{1,0:T(8,128)(2,1)S(1)}, u32[]{:S(2)}, u32[]{:S(2)}) collective-permute-start(bf16[224,256]{1,0:T(8,128)(2,1)S(1)} %get-tuple-element.42), channel_id=1, source_target_pairs={{0,3},{1,2},{2,1},{3,0},{4,12},{5,13},{6,14},{7,15},{8,11},{9,10},... | collective-permute-start | bytes 344072 | tf_op jit(solution)/shard_map/ppermute | solution.py:301
  32.5 5.7 %collective-permute-start.15 = (bf16[224,256]{1,0:T(8,128)(2,1)S(1)}, bf16[224,256]{1,0:T(8,128)(2,1)S(1)}, u32[]{:S(2)}, u32[]{:S(2)}) collective-permute-start(bf16[224,256]{1,0:T(8,128)(2,1)S(1)} %get-tuple-element.43), channel_id=1, source_target_pairs={{0,2},{1,3},{2,0},{3,1},{4,20},{5,21},{6,22},{7,23},{8,10},{9,11},... | collective-permute-start | bytes 344072 | tf_op jit(solution)/shard_map/ppermute | solution.py:301
  33.5 4.8 %collective-permute-start.16 = (bf16[224,256]{1,0:T(8,128)(2,1)S(1)}, bf16[224,256]{1,0:T(8,128)(2,1)S(1)}, u32[]{:S(2)}, u32[]{:S(2)}) collective-permute-start(bf16[224,256]{1,0:T(8,128)(2,1)S(1)} %get-tuple-element.44), channel_id=1, source_target_pairs={{0,1},{1,0},{2,3},{3,2},{4,28},{5,29},{6,30},{7,31},{8,9},{9,8},{1... | collective-permute-start | bytes 344072 | tf_op jit(solution)/shard_map/ppermute | solution.py:301
  38.3 1.3 %collective-permute-start.17 = (bf16[160,256]{1,0:T(8,128)(2,1)S(1)}, bf16[160,256]{1,0:T(8,128)(2,1)S(1)}, u32[]{:S(2)}, u32[]{:S(2)}) collective-permute-start(bf16[160,256]{1,0:T(8,128)(2,1)S(1)} %third.1.own_ref), channel_id=1, source_target_pairs={{0,4},{4,0},{8,12},{12,8},{16,20},{20,16},{24,28},{28,24},{1,5},{5... | collective-permute-start | bytes 245768 | tf_op jit(solution)/shard_map/ppermute | solution.py:94
